TPU v7x, 32 devices: a whole 2x2x4 slice. The times are simulated.
32 devices in a mesh: replica: 4 (over x, core), fsdp: 8 (over z, y).
Axes of the slice: x: 2, y: 2, z: 4, core: 2. Of those that a mesh axis runs over, the one named last changes fastest.
Arguments:
- tokens: bfloat16 [4, 1024, 8192], P('replica', 'fsdp'), may hold values from -6 to 6
- norm_gain: bfloat16 [8192], replicated, may hold values from 0.099609375 to 1.8984375
- cotangent: bfloat16 [4, 1024, 1024], P('replica', 'fsdp'), may hold values from -6 to 6
- layer_weight: bfloat16 [4, 8192, 1024], P('replica', 'fsdp'), may hold values from -0.09375 to 0.09375
- shared_copy: bfloat16 [8192, 1024], P('fsdp'), may hold values from -0.0625 to 0.0625
- master: float32 [8192, 1024], P('fsdp', 'replica'), may hold values from -0.0625 to 0.0625
- momentum: float32 [8192, 1024], P('fsdp', 'replica'), may hold values from -0.078125 to 0.078125
Outputs:
- layer_next: bfloat16 [4, 8192, 1024], P('replica', 'fsdp')
- master_next: float32 [8192, 1024], P('fsdp', 'replica')
- momentum_next: float32 [8192, 1024], P('fsdp', 'replica')
All inputs are finite; a program needn't handle non-finite values.
Results may differ from a plain program's by a relative error of at most 0.013.
Values may be sent and summed in bfloat16 or wider, within the bound.
No kernel may reach another device: no remote copies, remote signals or barrier semaphores. Data moves between devices by JAX's collectives and lax.ppermute only.
A program may use at most 64 MiB of HBM per device.

v0:
```python
import math

import jax
import jax.numpy as jnp
from jax import lax
from jax.sharding import PartitionSpec as P

BLOCK = 64


norm_eps = 1e-05
inner_gain = 0.4
outer_rate = 0.7
outer_beta = 0.9
mix_weight = 0.5
code_range = 448.0


def on_device(tokens, norm_gain, cotangent, layer_weight, shared_copy, master, momentum):
    tok_float = tokens[0].astype(jnp.float32)
    inverse = lax.rsqrt(jnp.mean(tok_float * tok_float, axis=-1, keepdims=True) + norm_eps)
    normed = (tok_float * inverse * norm_gain.astype(jnp.float32)).astype(jnp.bfloat16)
    columns = lax.all_to_all(normed, "fsdp", split_axis=1, concat_axis=0, tiled=True)
    local_rows = columns.shape[1]
    width = cotangent.shape[2]
    inner_rate = inner_gain / math.sqrt(columns.shape[0])
    grad = lax.dot_general(
        columns,
        lax.all_gather(cotangent[0], "fsdp", axis=0, tiled=True),
        (((0,), (0,)), ((), ())),
        preferred_element_type=jnp.float32,
    )
    weight_float = layer_weight[0].astype(jnp.float32)
    delta = (shared_copy.astype(jnp.float32) - weight_float).reshape(
        local_rows, width // BLOCK, BLOCK
    )
    largest = jnp.max(jnp.abs(delta), axis=-1, keepdims=True)
    scale = ((largest + 1e-06) / code_range).astype(jnp.bfloat16)
    coded = (delta / scale.astype(jnp.float32)).astype(jnp.bfloat16)
    groups = lax.axis_size("replica")
    share = width // BLOCK // groups
    decoded = lax.optimization_barrier(coded).astype(jnp.float32) * scale.astype(jnp.float32)
    owned = lax.psum_scatter(
        decoded.astype(jnp.bfloat16), "replica", scatter_dimension=1, tiled=True
    ).astype(jnp.float32)
    average = owned.reshape(local_rows, share * BLOCK) / groups
    momentum_next = outer_beta * momentum + average
    master_next = master - outer_rate * (average + outer_beta * momentum_next)
    shared_next = lax.all_gather(master_next.astype(jnp.bfloat16), "replica", axis=1, tiled=True)
    stepped = weight_float - inner_rate * grad
    layer_next = (
        mix_weight * stepped + (1.0 - mix_weight) * shared_next.astype(jnp.float32)
    ).astype(jnp.bfloat16)
    return (layer_next[None], master_next, momentum_next)


def solution(mesh):
    in_specs = (
        P("replica", "fsdp", None),
        P(),
        P("replica", "fsdp", None),
        P("replica", "fsdp", None),
        P("fsdp", None),
        P("fsdp", "replica"),
        P("fsdp", "replica"),
    )
    out_specs = (P("replica", "fsdp", None), P("fsdp", "replica"), P("fsdp", "replica"))
    return jax.shard_map(
        on_device, mesh=mesh, in_specs=in_specs, out_specs=out_specs, check_vma=False
    )
```

profile of v0, /device:TPU:0, one launch (start us, length us, event | category | flops | bytes accessed | tf_op | source)
XLA Modules:
  0.0 149.5 jit_solution(18023780453712535428)
XLA Ops:
  8.0 0.0 reduce-scatter.2.cloned.1.call-start
  8.0 5.1 %convert_subtract_fusion = f32[1024,1024]{1,0:T(8,128)} fusion(bf16[1024,1024]{1,0:T(8,128)(2,1)} %param.11, bf16[1,1024,1024]{2,1,0:T(8,128)(2,1)} %param.10), kind=kLoop, calls=%fused_computation | loop fusion | flops 3145728 | bytes 8388608 | tf_op jit(solution)/shard_map/sub | solution.py:34
  13.1 5.4 %copy.15 = f32[1024,1024]{0,1:T(8,128)} copy(f32[1024,1024]{1,0:T(8,128)} %convert_subtract_fusion) | data formatting | bytes 8388608 | tf_op jit(solution)/shard_map/sub | solution.py:34
  18.5 0.0 copy-start
  18.5 2.9 %abs_reduce_fusion = f32[1024,16]{0,1:T(8,128)S(1)} fusion(f32[1024,1024]{0,1:T(8,128)} %copy.15), kind=kLoop, calls=%fused_computation.7 | loop fusion | flops 2080768 | bytes 4259840 | tf_op jit(solution)/shard_map/reduce_max | solution.py:37
  21.4 0.5 copy-done
  21.9 0.6 divide_convert_fusion
  22.6 2.0 %multiply_convert_fusion = bf16[1024,16,64]{0,2,1:T(8,128)(2,1)} fusion(bf16[1024,16,64]{0,2,1:T(8,128)(2,1)S(1)} %divide_convert_fusion, f32[1024,16]{0,1:T(8,128)S(1)} %fusion.7), kind=kLoop, calls=%fused_computation.5 | loop fusion | flops 3145728 | bytes 4259840 | tf_op jit(solution)/shard_map/convert_element_type | solution.py:44
  24.6 0.0 copy-start.1
  24.6 0.0 reduce-scatter.2.cloned.1.call-update
  24.6 0.0 all-gather.6.cloned.1.call-start
  24.6 0.5 all-gather.6.cloned.1.call-update
  25.2 3.2 %copy.13 = bf16[1,128,8192]{1,2,0:T(8,128)(2,1)S(1)} copy(bf16[1,128,8192]{2,1,0:T(8,128)(2,1)} %param.7) | data formatting | bytes 4194304 | tf_op args[0]
  28.4 0.0 copy-done.1
  28.4 1.1 multiply_reduce_fusion
  29.5 2.7 %multiply_convert_fusion.1 = bf16[128,8,1024]{0,2,1:T(8,128)(2,1)} fusion(f32[8,1024]{1,0:T(8,128)S(1)} %reshape.55, f32[128]{0:T(128)S(1)} %add_rsqrt_fusion, bf16[128,8,1024]{0,2,1:T(8,128)(2,1)S(1)} %bitcast.22), kind=kLoop, calls=%fused_computation.8 | loop fusion | flops 4194304 | bytes 4227584 | tf_op jit(solution)/shard_map/convert_element_type | solution.py:22
  32.2 7.3 %all-to-all-start = ((bf16[128,8,1024]{0,2,1:T(8,128)(2,1)}), bf16[128,8,1024]{0,2,1:T(8,128)(2,1)S(1)}, u32[]{:S(2)}, u32[]{:S(2)}) async-start(bf16[128,8,1024]{0,2,1:T(8,128)(2,1)} %multiply_convert_fusion.1), calls=%async_computation | async-start | bytes 4194304 | tf_op jit(solution)/shard_map/all_to_all | solution.py:23
  39.5 0.0 all-gather.4.cloned.1.call-start
  39.6 19.3 %reduce-scatter.2.cloned.1.call-done = bf16[1024,4,64]{0,2,1:T(8,128)(2,1)} async-done(((bf16[1024,16,64]{0,2,1:T(8,128)(2,1)}), bf16[1024,4,64]{0,2,1:T(8,128)(2,1)}) %reduce-scatter.2.cloned.1.call-update) | async-done | bytes 524304 | tf_op jit(solution)/shard_map/reduce_scatter | solution.py:43
  58.9 1.1 convert_multiply_fusion
  60.1 1.3 copy.17
  61.4 3.6 %fusion.8 = (bf16[1024,256]{1,0:T(8,128)(2,1)}, f32[1024,256]{1,0:T(8,128)}, f32[1024,256]{1,0:T(8,128)}) fusion(f32[1024,256]{1,0:T(8,128)} %param.12, f32[1024,256]{1,0:T(8,128)} %copy.17, f32[1024,256]{1,0:T(8,128)} %param.13), kind=kLoop, calls=%fused_computation.18 | loop fusion | flops 1835008 | bytes 5767168 | tf_op jit(solution)/shard_map/convert_element_type | solution.py:49
  65.0 0.0 all-gather.4.cloned.1.call-update
  65.0 46.8 %all-to-all-done = bf16[128,8,1024]{0,2,1:T(8,128)(2,1)S(1)} async-done(((bf16[128,8,1024]{0,2,1:T(8,128)(2,1)}), bf16[128,8,1024]{0,2,1:T(8,128)(2,1)S(1)}, u32[]{:S(2)}, u32[]{:S(2)}) %all-to-all-start) | async-done | bytes 2097184 | tf_op jit(solution)/shard_map/all_to_all | solution.py:23
  111.8 2.6 %copy.14 = bf16[8,128,1024]{2,1,0:T(8,128)(2,1)} copy(bf16[8,128,1024]{1,2,0:T(8,128)(2,1)S(1)} %bitcast.23) | data formatting | bytes 4194304 | tf_op jit(solution)/shard_map/all_to_all | solution.py:23
  114.4 0.0 all-gather.6.cloned.1.call-done
  114.4 20.0 %all-gather.4.cloned.1.call-done = bf16[1024,1024]{1,0:T(8,128)(2,1)} async-done(((bf16[1024,256]{1,0:T(8,128)(2,1)}), bf16[1024,1024]{1,0:T(8,128)(2,1)}) %all-gather.4.cloned.1.call-update) | async-done | bytes 2097168 | tf_op jit(solution)/shard_map/all_gather | solution.py:49
  134.3 7.8 %fusion.4 = bf16[1,1024,1024]{2,1,0:T(8,128)(2,1)} fusion(bf16[1024,1024]{1,0:T(8,128)(2,1)} %all-gather.4.cloned.1.call-done, bf16[1024,1024]{1,0:T(8,128)(2,1)} %bitcast.25, bf16[1,1024,1024]{2,1,0:T(8,128)(2,1)} %all-gather.6.cloned.1.call-done, bf16[1,1024,1024]{2,1,0:T(8,128)(2,1)} %param.10), kind=kOutput, calls=%fused_computation.11 | convolution fusion | flops 2154823680 | bytes 10485760 | tf_op jit(solution)/shard_map/dot_general | solution.py:27
  (3 shorter events, 0.0 us)
Async XLA Ops:
  8.0 50.9 %reduce-scatter.2.cloned.1.call-start = ((), (), s32[]{:S(2)}) async-start(), calls=%async_computation.2 | async-start | bytes 2621440 | tf_op jit(solution)/shard_map/reduce_scatter | solution.py:43
  18.5 3.4 %copy-start = (f32[1024,1024]{0,1:T(8,128)S(1)}, f32[1024,1024]{0,1:T(8,128)}, u32[]{:S(2)}) copy-start(f32[1024,1024]{0,1:T(8,128)} %copy.15) | copy-start | bytes 12582916
  24.6 3.8 %copy-start.1 = (bf16[8192]{0:T(1024)(128)(2,1)S(1)}, bf16[8192]{0:T(1024)(128)(2,1)}, u32[]{:S(2)}) copy-start(bf16[8192]{0:T(1024)(128)(2,1)} %param.8) | copy-start | bytes 49156
  24.6 89.8 %all-gather.6.cloned.1.call-start = ((), (), s32[]{:S(2)}) async-start(), calls=%async_computation.4 | async-start | bytes 2359296 | tf_op jit(solution)/shard_map/all_gather | solution.py:29
  32.2 79.6 %all-to-all-start = ((bf16[128,8,1024]{0,2,1:T(8,128)(2,1)}), bf16[128,8,1024]{0,2,1:T(8,128)(2,1)S(1)}, u32[]{:S(2)}, u32[]{:S(2)}) async-start(bf16[128,8,1024]{0,2,1:T(8,128)(2,1)} %multiply_convert_fusion.1), calls=%async_computation | async-start | bytes 4194304 | tf_op jit(solution)/shard_map/all_to_all | solution.py:23
  39.5 94.8 %all-gather.4.cloned.1.call-start = ((), (), s32[]{:S(2)}) async-start(), calls=%async_computation.3 | async-start | bytes 2621440 | tf_op jit(solution)/shard_map/all_gather | solution.py:49
Sparse Core Ops, SparseCore 0:
  24.7 34.1 reduce-scatter.1
Sparse Core Ops, SparseCore 1:
  27.2 83.3 all-gather.5
  112.6 21.7 all-gather.3
where the time goes:
time: 150 us
  waiting for transfers between devices  86.7 us (58%)
  other arithmetic  19.2 us (13%)
  between operations  15.5 us (10%)
  local copies, waits for them, and re-layouts  13 us (9%)
  matrix products  7.75 us (5%)
  starting transfers between devices  7.4 us (5%)
    all_to_all x1, waiting for transfers between devices, on_device(): lax.all_to_all(normed, 'fsdp', split_axis=1, concat_axis=0, tiled=True)  46.8 us
    all_gather x1, waiting for transfers between devices, on_device(): lax.all_gather(master_next.astype(jnp.bfloat16), 'replica', axis=1, tiled...  20 us
    reduce_scatter x1, waiting for transfers between devices, on_device(): lax.psum_scatter(decoded.astype(jnp.bfloat16), 'replica', scatter_dimensi...  19.3 us
    dot_general x1, matrix products, on_device(): lax.dot_general(columns, lax.all_gather(cotangent[0], 'fsdp', axis=0, til...  7.75 us
    all_to_all x1, starting transfers between devices, on_device(): lax.all_to_all(normed, 'fsdp', split_axis=1, concat_axis=0, tiled=True)  7.28 us
    sub x1, local copies, waits for them, and re-layouts, on_device(): shared_copy.astype(jnp.float32) - weight_float  5.38 us
    sub x1, other arithmetic, on_device(): shared_copy.astype(jnp.float32) - weight_float  5.05 us
    unnamed x5, local copies, waits for them, and re-layouts  3.73 us
  transfers between devices with their start and end apart: 4, of which 3 were waited for; matrix products, arithmetic and copies ran while one was open for 10% of the time, Pallas kernels for 0%

commit v1 on v0

v1 whole, which is shorter than its diff:
```python
import functools
import math

import jax
import jax.numpy as jnp
from jax import lax
from jax.experimental import pallas as pl
from jax.experimental.pallas import tpu as pltpu
from jax.sharding import PartitionSpec as P

BLOCK = 64


norm_eps = 1e-05
inner_gain = 0.4
outer_rate = 0.7
outer_beta = 0.9
mix_weight = 0.5
code_range = 448.0


def swap(value, axis, mask):
    size = lax.axis_size(axis)
    return lax.ppermute(value, axis, [(i, i ^ mask) for i in range(size)])


def code_kernel(shared_ref, weight_ref, decoded_ref):
    lanes = 2 * BLOCK
    lane = lax.broadcasted_iota(jnp.int32, (shared_ref.shape[0], lanes), 1)
    low = lane < BLOCK
    for start in range(0, shared_ref.shape[1], lanes):
        columns = slice(start, start + lanes)
        delta = shared_ref[:, columns].astype(jnp.float32) - weight_ref[:, columns].astype(jnp.float32)
        size = jnp.abs(delta)
        largest = jnp.where(
            low,
            jnp.max(jnp.where(low, size, 0.0), axis=-1, keepdims=True),
            jnp.max(jnp.where(low, 0.0, size), axis=-1, keepdims=True),
        )
        scale = ((largest + 1e-06) / code_range).astype(jnp.bfloat16).astype(jnp.float32)
        coded = (delta / scale).astype(jnp.bfloat16)
        decoded_ref[:, columns] = (coded.astype(jnp.float32) * scale).astype(jnp.bfloat16)


def code_and_decode(shared, weight):
    rows, width = shared.shape
    tile = min(rows, 128)
    spec = pl.BlockSpec((tile, width), lambda i: (i, 0))
    return pl.pallas_call(
        code_kernel,
        out_shape=jax.ShapeDtypeStruct((rows, width), jnp.bfloat16),
        grid=(rows // tile,),
        in_specs=[spec, spec],
        out_specs=spec,
        cost_estimate=pl.CostEstimate(flops=20 * rows * width, bytes_accessed=6 * rows * width, transcendentals=0),
        name="code_and_decode",
    )(shared, weight)


def mix_kernel(parts, *refs):
    tokens, cotangents = refs[:parts], refs[parts : 2 * parts]
    gain_ref, weight_ref, shared_ref, out_ref = refs[2 * parts :]
    total = None
    pair = 2 if parts % 2 == 0 else 1
    for first in range(0, parts, pair):
        product = lax.dot_general(
            jnp.concatenate([ref[...] for ref in tokens[first : first + pair]], axis=0),
            jnp.concatenate([ref[...] for ref in cotangents[first : first + pair]], axis=0),
            (((0,), (0,)), ((), ())),
            preferred_element_type=jnp.float32,
        )
        total = product if total is None else total + product
    weight = weight_ref[...].astype(jnp.float32) + shared_ref[...].astype(jnp.float32)
    out_ref[...] = (mix_weight * weight - gain_ref[...] * total).astype(jnp.bfloat16)


def mix(tokens, cotangents, gain, weight, shared):
    parts = len(tokens)
    rows, width = weight.shape
    tile = min(rows, 256)
    depth = tokens[0].shape[0]
    by_row = pl.BlockSpec((tile, width), lambda i: (i, 0))
    return pl.pallas_call(
        functools.partial(mix_kernel, parts),
        out_shape=jax.ShapeDtypeStruct((rows, width), jnp.bfloat16),
        grid=(rows // tile,),
        in_specs=[pl.BlockSpec((depth, tile), lambda i: (0, i))] * parts
        + [pl.BlockSpec((depth, width), lambda i: (0, 0))] * parts
        + [pl.BlockSpec((tile, 1), lambda i: (i, 0)), by_row, by_row],
        out_specs=by_row,
        compiler_params=pltpu.CompilerParams(vmem_limit_bytes=48 * 2**20),
        cost_estimate=pl.CostEstimate(
            flops=2 * parts * depth * rows * width,
            bytes_accessed=2 * parts * depth * (rows + width) + 6 * rows * width,
            transcendentals=0,
        ),
        name="mix",
    )(*tokens, *cotangents, gain, weight, shared)


def on_device(tokens, norm_gain, cotangent, layer_weight, shared_copy, master, momentum):
    tokens, cotangent, weight = tokens[0], cotangent[0], layer_weight[0]
    shards = lax.axis_size("fsdp")
    groups = lax.axis_size("replica")
    mine = lax.axis_index("fsdp")
    own = lax.axis_index("replica")
    rows, width = weight.shape
    share = width // groups
    inner_rate = inner_gain / math.sqrt(tokens.shape[0] * shards)

    blocks = [lax.dynamic_slice_in_dim(tokens, (mine ^ k) * rows, rows, axis=1) for k in range(shards)]
    *blocks, weight, shared_copy, cotangent = lax.optimization_barrier((*blocks, weight, shared_copy, cotangent))
    columns = [swap(block, "fsdp", k) if k else block for k, block in enumerate(blocks)]

    tok_float = tokens.astype(jnp.float32)
    inverse = lax.rsqrt(jnp.mean(tok_float * tok_float, axis=-1, keepdims=True) + norm_eps)
    scaled = (cotangent.astype(jnp.float32) * inverse).astype(jnp.bfloat16)
    cotangents = {0: scaled}
    bit = shards // 2
    while bit:
        held = sorted(cotangents)
        for part in ([k for k in held if k < shards // 2], [k for k in held if k >= shards // 2]):
            if part:
                arrived = swap(jnp.stack([cotangents[k] for k in part]), "fsdp", bit)
                for place, k in enumerate(part):
                    cotangents[k ^ bit] = arrived[place]
        bit //= 2

    total = code_and_decode(shared_copy, weight)
    bit = 1
    while bit < groups:
        side = (own // bit) % 2
        split = total.reshape(rows, groups // bit // 2, 2, share)
        kept = lax.dynamic_index_in_dim(split, side, axis=2, keepdims=False)
        sent = lax.dynamic_index_in_dim(split, 1 - side, axis=2, keepdims=False)
        total = kept.astype(jnp.float32) + swap(sent, "replica", bit).astype(jnp.float32)
        bit *= 2
        if bit < groups:
            total = total.astype(jnp.bfloat16)
    average = total.reshape(rows, share) / groups
    momentum_next = outer_beta * momentum + average
    master_next = master - outer_rate * (average + outer_beta * momentum_next)

    gathered = master_next.astype(jnp.bfloat16).reshape(rows, 1, share)
    bit = groups // 2
    while bit:
        side = (own // bit) % 2
        other = swap(gathered, "replica", bit)
        gathered = jnp.where(
            side == 0, jnp.stack([gathered, other], axis=2), jnp.stack([other, gathered], axis=2)
        ).reshape(rows, -1, share)
        bit //= 2
    shared_next = gathered.reshape(rows, width)

    gain = lax.dynamic_slice_in_dim(norm_gain, mine * rows, rows).astype(jnp.float32)
    gain = (gain * ((1.0 - mix_weight) * inner_rate)).reshape(rows, 1)
    layer_next = mix(columns, [cotangents[k] for k in range(shards)], gain, weight, shared_next)
    return (layer_next[None], master_next, momentum_next)


def solution(mesh):
    in_specs = (
        P("replica", "fsdp", None),
        P(),
        P("replica", "fsdp", None),
        P("replica", "fsdp", None),
        P("fsdp", None),
        P("fsdp", "replica"),
        P("fsdp", "replica"),
    )
    out_specs = (P("replica", "fsdp", None), P("fsdp", "replica"), P("fsdp", "replica"))
    return jax.shard_map(
        on_device, mesh=mesh, in_specs=in_specs, out_specs=out_specs, check_vma=False
    )
```

time: 150 us -> 155 us (1.033)
  the two profiles are of different devices: /device:TPU:0 before, /device:TPU:9 now
where the time goes in v1:
time: 155 us
  waiting for transfers between devices  87.1 us (56%)
  local copies, waits for them, and re-layouts  23 us (15%)
  starting transfers between devices  17.6 us (11%)
  Pallas kernels  13.6 us (9%)
  other arithmetic  12.6 us (8%)
    ppermute x16, waiting for transfers between devices, swap(): return lax.ppermute(value, axis, [(i, i ^ mask) for i in range(size)])  87.1 us
    ppermute x16, starting transfers between devices, swap(): return lax.ppermute(value, axis, [(i, i ^ mask) for i in range(size)])  17.6 us
    select_n x2, local copies, waits for them, and re-layouts, on_device(): jnp.where(side == 0, jnp.stack([gathered, other], axis=2), jnp.stack([oth...  7.91 us
    pallas_call x1, Pallas kernels, code_and_decode(): pl.pallas_call(code_kernel, out_shape=jax.ShapeDtypeStruct((rows, width),...  7.4 us
    pallas_call x1, Pallas kernels, mix(): pl.pallas_call(functools.partial(mix_kernel, parts), out_shape=jax.ShapeD...  6.18 us
    dynamic_slice x1, local copies, waits for them, and re-layouts, on_device(): kept = lax.dynamic_index_in_dim(split, side, axis=2, keepdims=False)  5.64 us
    select_n x3, other arithmetic, on_device(): jnp.where(side == 0, jnp.stack([gathered, other], axis=2), jnp.stack([oth...  4.46 us
    reshape x1, local copies, waits for them, and re-layouts, on_device(): split = total.reshape(rows, groups // bit // 2, 2, share)  3.29 us
  transfers between devices with their start and end apart: 16, of which 10 were waited for; matrix products, arithmetic and copies ran while one was open for 11% of the time, Pallas kernels for 0%

profile of v1, /device:TPU:9, one launch (start us, length us, event | category | flops | bytes accessed | tf_op | source)
XLA Modules:
  0.0 154.5 jit_solution(16759707431851827778)
XLA Ops:
  0.7 2.8 %dynamic-slice_bitcast_fusion = (bf16[128,1024]{1,0:T(8,128)(2,1)}, bf16[128,1024]{1,0:T(8,128)(2,1)}, bf16[128,1024]{1,0:T(8,128)(2,1)}, bf16[128,1024]{1,0:T(8...) fusion(bf16[1,128,8192]{2,1,0:T(8,128)(2,1)} %param.7, ...), kind=kLoop, calls=%fused_computation.22 | loop fusion | bytes 4194336 | tf_op jit(solution)/shard_map/dynamic_slice | solution.py:111
  3.5 7.4 %code_and_decode.1 = bf16[1024,1024]{1,0:T(8,128)(2,1)} custom-call(bf16[1024,1024]{1,0:T(8,128)(2,1)} %shared_ref, bf16[1024,1024]{1,0:T(8,128)(2,1)} %bitcast.59), custom_call_target="tpu_custom_call" | custom-call | flops 20971520 | bytes 6291456 | tf_op jit(solution)/shard_map/code_and_decode/pallas_call | solution.py:49
  10.9 3.3 %reshape.131 = bf16[1024,2,2,256]{3,2,1,0:T(2,128)(2,1)S(1)} reshape(bf16[1024,1024]{1,0:T(8,128)(2,1)} %code_and_decode.1) | data formatting | bytes 4194304 | tf_op jit(solution)/shard_map/reshape | solution.py:133
  14.2 5.6 %constant_dynamic-slice_fusion.2 = (bf16[1024,2,1,256]{3,2,1,0:T(2,128)(2,1)}, bf16[1024,2,1,256]{3,2,1,0:T(2,128)(2,1)S(1)}) fusion(bf16[1024,2,2,256]{3,2,1,0:T(2,128)(2,1)S(1)} %reshape.131, s32[]{:T(128)S(6)} %select_n.108, s32[]{:T(128)S(6)} %select_n.109), kind=kLoop, calls=%fused_computation.33 | loop fusion | bytes 4194312 | tf_op jit(solution)/shard_map/jit(dynamic_index_in_dim)/dynamic_slice | solution.py:134
  20.7 2.3 %collective-permute-done.12 = bf16[1024,2,256]{2,0,1:T(8,128)(2,1)S(1)} collective-permute-done((bf16[1024,2,256]{2,0,1:T(8,128)(2,1)S(1)}, bf16[1024,2,256]{2,0,1:T(8,128)(2,1)S(1)}, u32[]{:S(2)}, u32[]{:S(2)}) %collective-permute-start.12) | collective-permute-done | bytes 1048608 | tf_op jit(solution)/shard_map/ppermute | solution.py:24
  24.0 2.3 %fusion = bf16[1024,2,256]{2,0,1:T(8,128)(2,1)S(1)} fusion(bf16[1024,2,256]{2,0,1:T(8,128)(2,1)} %copy-done.7, bf16[1024,2,1,256]{3,2,1,0:T(2,128)(2,1)} %get-tuple-element.28), kind=kLoop, calls=%fused_computation.3 | loop fusion | flops 2097152 | bytes 3145728 | tf_op jit(solution)/shard_map/convert_element_type | solution.py:139
  27.2 1.2 collective-permute-start.13
  28.9 11.7 %collective-permute-done.13 = bf16[1024,1,256]{2,0,1:T(8,128)(2,1)} collective-permute-done((bf16[1024,1,256]{2,0,1:T(8,128)(2,1)}, bf16[1024,1,256]{2,0,1:T(8,128)(2,1)}, u32[]{:S(2)}, u32[]{:S(2)}) %collective-permute-start.13) | collective-permute-done | bytes 524320 | tf_op jit(solution)/shard_map/ppermute | solution.py:24
  40.6 2.6 %convert_bitcast_fusion.1 = (bf16[1024,1,1,256]{3,0,1,2:T(8,128)(2,1)}, f32[1024,256]{1,0:T(8,128)S(1)}, f32[1024,256]{1,0:T(8,128)}) fusion(f32[1024,256]{1,0:T(8,128)S(1)} %copy-done.5, bf16[1024,1,256]{2,0,1:T(8,128)(2,1)} %collective-permute-done.13, bf16[1024,2,256]{2,0,1:T(8,128)(2,1)S(1)} %fusion, s32[]{:T(128)S(6)} %select_n.110, ...), kind=kLoop, calls=%fused_computation.21 | loop fusion | flops 2883584 | bytes 5767172 | tf_op jit(solution)/shard_map/stack | solution.py:150
  43.3 1.3 collective-permute-start.14
  44.7 2.4 %collective-permute-start.9 = (bf16[1,128,1024]{2,1,0:T(8,128)(2,1)S(1)}, bf16[1,128,1024]{2,1,0:T(8,128)(2,1)S(1)}, u32[]{:S(2)}, u32[]{:S(2)}) collective-permute-start(bf16[1,128,1024]{2,1,0:T(8,128)(2,1)S(1)} %fusion.4), channel_id=1, source_target_pairs={{0,4},{1,5},{2,6},{3,7},{4,0},{5,1},{6,2},{7,3},{8,12},{9,13},{10,... | collective-permute-start | bytes 786440 | tf_op jit(solution)/shard_map/ppermute | solution.py:24
  47.3 11.4 %collective-permute-done.9 = bf16[1,128,1024]{2,1,0:T(8,128)(2,1)S(1)} collective-permute-done((bf16[1,128,1024]{2,1,0:T(8,128)(2,1)S(1)}, bf16[1,128,1024]{2,1,0:T(8,128)(2,1)S(1)}, u32[]{:S(2)}, u32[]{:S(2)}) %collective-permute-start.9) | collective-permute-done | bytes 262176 | tf_op jit(solution)/shard_map/ppermute | solution.py:24
  58.7 1.1 maximum_select_fusion.2
  59.8 1.9 %collective-permute-start.15 = (bf16[1024,2,256]{2,0,1:T(8,128)(2,1)}, bf16[1024,2,256]{2,0,1:T(8,128)(2,1)}, u32[]{:S(2)}, u32[]{:S(2)}) collective-permute-start(bf16[1024,2,256]{2,0,1:T(8,128)(2,1)} %maximum_select_fusion.2), channel_id=1, source_target_pairs={{0,8},{8,0},{16,24},{24,16},{1,9},{9,1},{17,25},{25,17},{2,10},{10... | collective-permute-start | bytes 3145736 | tf_op jit(solution)/shard_map/ppermute | solution.py:24
  62.6 1.2 collective-permute-start.8
  64.3 1.7 %collective-permute-done.10 = bf16[1,128,1024]{2,1,0:T(8,128)(2,1)S(1)} collective-permute-done((bf16[1,128,1024]{2,1,0:T(8,128)(2,1)S(1)}, bf16[1,128,1024]{2,1,0:T(8,128)(2,1)S(1)}, u32[]{:S(2)}, u32[]{:S(2)}) %collective-permute-start.10) | collective-permute-done | bytes 262176 | tf_op jit(solution)/shard_map/ppermute | solution.py:24
  66.9 1.2 collective-permute-start.11
  69.1 7.2 %collective-permute-done.8 = bf16[2,128,1024]{2,1,0:T(8,128)(2,1)S(1)} collective-permute-done((bf16[2,128,1024]{2,1,0:T(8,128)(2,1)}, bf16[2,128,1024]{2,1,0:T(8,128)(2,1)S(1)}, u32[]{:S(2)}, u32[]{:S(2)}) %collective-permute-start.8) | collective-permute-done | bytes 524320 | tf_op jit(solution)/shard_map/ppermute | solution.py:24
  76.4 1.2 collective-permute-start.2
  77.6 21.3 %collective-permute-done.11 = bf16[2,128,1024]{2,1,0:T(8,128)(2,1)} collective-permute-done((bf16[2,128,1024]{2,1,0:T(8,128)(2,1)}, bf16[2,128,1024]{2,1,0:T(8,128)(2,1)}, u32[]{:S(2)}, u32[]{:S(2)}) %collective-permute-start.11) | collective-permute-done | bytes 524320 | tf_op jit(solution)/shard_map/ppermute | solution.py:24
  98.9 1.6 %collective-permute-start.3 = (bf16[128,1024]{1,0:T(8,128)(2,1)}, bf16[128,1024]{1,0:T(8,128)(2,1)}, u32[]{:S(2)}, u32[]{:S(2)}) collective-permute-start(bf16[128,1024]{1,0:T(8,128)(2,1)} %get-tuple-element.18), channel_id=1, source_target_pairs={{0,4},{1,5},{2,6},{3,7},{4,0},{5,1},{6,2},{7,3},{8,12},{9,13},{10,... | collective-permute-start | bytes 786440 | tf_op jit(solution)/shard_map/ppermute | solution.py:24
  101.6 1.8 %collective-permute-start.4 = (bf16[128,1024]{1,0:T(8,128)(2,1)}, bf16[128,1024]{1,0:T(8,128)(2,1)}, u32[]{:S(2)}, u32[]{:S(2)}) collective-permute-start(bf16[128,1024]{1,0:T(8,128)(2,1)} %get-tuple-element.19), channel_id=1, source_target_pairs={{0,5},{1,4},{2,7},{3,6},{4,1},{5,0},{6,3},{7,2},{8,13},{9,12},{10,... | collective-permute-start | bytes 786440 | tf_op jit(solution)/shard_map/ppermute | solution.py:24
  103.4 2.2 %collective-permute-start.5 = (bf16[128,1024]{1,0:T(8,128)(2,1)}, bf16[128,1024]{1,0:T(8,128)(2,1)}, u32[]{:S(2)}, u32[]{:S(2)}) collective-permute-start(bf16[128,1024]{1,0:T(8,128)(2,1)} %get-tuple-element.20), channel_id=1, source_target_pairs={{0,6},{1,7},{2,4},{3,5},{4,2},{5,3},{6,0},{7,1},{8,14},{9,15},{10,... | collective-permute-start | bytes 786440 | tf_op jit(solution)/shard_map/ppermute | solution.py:24
  105.6 1.4 maximum_select_fusion.1
  107.0 1.9 %maximum_select_fusion = bf16[1024,2,2,256]{3,0,1,2:T(8,128)(2,1)S(1)} fusion(bf16[1024,2,1,256]{3,0,1,2:T(8,128)(2,1)} %bitcast.25, bf16[1024,2,1,256]{3,0,1,2:T(8,128)(2,1)S(1)} %maximum_select_fusion.1, pred[]{:T(512)S(6)} %eq.11), kind=kLoop, calls=%fused_computation.1 | loop fusion | flops 3145728 | bytes 4194305 | tf_op jit(solution)/shard_map/jit(_where)/select_n | solution.py:149
  108.9 3.5 %copy.15 = bf16[1024,2,2,256]{3,2,1,0:T(2,128)(2,1)} copy(bf16[1024,2,2,256]{3,0,1,2:T(8,128)(2,1)S(1)} %maximum_select_fusion) | data formatting | bytes 4194304 | tf_op jit(solution)/shard_map/jit(_where)/select_n | solution.py:149
  112.4 4.4 %select_n.116.refs_18_ = bf16[1024,1024]{1,0:T(8,128)(2,1)} reshape(bf16[1024,2,2,256]{3,2,1,0:T(2,128)(2,1)} %copy.15) | data formatting | bytes 4194304 | tf_op jit(solution)/shard_map/jit(_where)/select_n | solution.py:149
  116.9 11.3 %collective-permute-done.3.refs_4_ = bf16[128,1024]{1,0:T(8,128)(2,1)} collective-permute-done((bf16[128,1024]{1,0:T(8,128)(2,1)}, bf16[128,1024]{1,0:T(8,128)(2,1)}, u32[]{:S(2)}, u32[]{:S(2)}) %collective-permute-start.3) | collective-permute-done | bytes 262176 | tf_op jit(solution)/shard_map/ppermute | solution.py:24
  128.2 5.6 %collective-permute-done.4.refs_5_ = bf16[128,1024]{1,0:T(8,128)(2,1)} collective-permute-done((bf16[128,1024]{1,0:T(8,128)(2,1)}, bf16[128,1024]{1,0:T(8,128)(2,1)}, u32[]{:S(2)}, u32[]{:S(2)}) %collective-permute-start.4) | collective-permute-done | bytes 262176 | tf_op jit(solution)/shard_map/ppermute | solution.py:24
  133.8 8.0 %collective-permute-done.5.refs_6_ = bf16[128,1024]{1,0:T(8,128)(2,1)} collective-permute-done((bf16[128,1024]{1,0:T(8,128)(2,1)}, bf16[128,1024]{1,0:T(8,128)(2,1)}, u32[]{:S(2)}, u32[]{:S(2)}) %collective-permute-start.5) | collective-permute-done | bytes 262176 | tf_op jit(solution)/shard_map/ppermute | solution.py:24
  141.8 6.6 %collective-permute-done.6.refs_7_ = bf16[128,1024]{1,0:T(8,128)(2,1)} collective-permute-done((bf16[128,1024]{1,0:T(8,128)(2,1)}, bf16[128,1024]{1,0:T(8,128)(2,1)}, u32[]{:S(2)}, u32[]{:S(2)}) %collective-permute-start.6) | collective-permute-done | bytes 262176 | tf_op jit(solution)/shard_map/ppermute | solution.py:24
  148.3 6.2 %mix.1 = bf16[1024,1024]{1,0:T(8,128)(2,1)} custom-call(bf16[128,1024]{1,0:T(8,128)(2,1)S(1)} %get-tuple-element.14.refs_0_, bf16[128,1024]{1,0:T(8,128)(2,1)S(1)} %collective-permute-done.refs_1_, bf16[128,1024]{1,0:T(8,128)(2,1)S(1)} %collective-permute-done.1.refs_2_, bf16[128,1024]{1,0:T(8,128)(2,1)} %collective-permute-done.2.refs_3_, ...), custom_call_target="tpu_custom_call" | custom-call | flops 2147483648 | bytes 10485760 | tf_op jit(solution)/shard_map/mix/pallas_call | solution.py:83
  (41 shorter events, 8.0 us)
Async XLA Ops:
  20.0 3.0 %collective-permute-start.12 = (bf16[1024,2,256]{2,0,1:T(8,128)(2,1)S(1)}, bf16[1024,2,256]{2,0,1:T(8,128)(2,1)S(1)}, u32[]{:S(2)}, u32[]{:S(2)}) collective-permute-start(bf16[1024,2,256]{2,0,1:T(8,128)(2,1)S(1)} %bitcast.63), channel_id=1, source_target_pairs={{0,8},{8,0},{16,24},{24,16},{1,9},{9,1},{17,25},{25,17},{2,10},{10... | collective-permute-start | bytes 3145736 | tf_op jit(solution)/shard_map/ppermute | solution.py:24
  23.0 1.0 copy-start.7
  24.0 4.4 %copy-start = (bf16[1,128,8192]{2,1,0:T(8,128)(2,1)S(1)}, bf16[1,128,8192]{2,1,0:T(8,128)(2,1)}, u32[]{:S(2)}) copy-start(bf16[1,128,8192]{2,1,0:T(8,128)(2,1)} %param.7) | copy-start | bytes 6291460
  27.2 13.5 %collective-permute-start.13 = (bf16[1024,1,256]{2,0,1:T(8,128)(2,1)}, bf16[1024,1,256]{2,0,1:T(8,128)(2,1)}, u32[]{:S(2)}, u32[]{:S(2)}) collective-permute-start(bf16[1024,1,256]{2,0,1:T(8,128)(2,1)} %constant_dynamic-slice_fusion), channel_id=1, source_target_pairs={{0,16},{8,24},{16,0},{24,8},{1,17},{9,25},{17,1},{25,9},{2,18},{10... | collective-permute-start | bytes 1572872 | tf_op jit(solution)/shard_map/ppermute | solution.py:24
  28.4 12.2 %copy-start.5 = (f32[1024,256]{1,0:T(8,128)S(1)}, f32[1024,256]{1,0:T(8,128)}, u32[]{:S(2)}) copy-start(f32[1024,256]{1,0:T(8,128)} %param.12) | copy-start | bytes 3145732
  28.4 12.2 %copy-start.6 = (f32[1024,256]{1,0:T(8,128)S(1)}, f32[1024,256]{1,0:T(8,128)}, u32[]{:S(2)}) copy-start(f32[1024,256]{1,0:T(8,128)} %param.13) | copy-start | bytes 3145732
  28.9 15.7 %copy-start.4 = (bf16[1,128,1024]{2,1,0:T(8,128)(2,1)S(1)}, bf16[1,128,1024]{2,1,0:T(8,128)(2,1)}, u32[]{:S(2)}) copy-start(bf16[1,128,1024]{2,1,0:T(8,128)(2,1)} %param.9) | copy-start | bytes 786436
  43.3 1.5 copy-start.1
  43.3 15.4 %collective-permute-start.14 = (bf16[1024,1,256]{2,0,1:T(8,128)(2,1)S(1)}, bf16[1024,1,256]{2,0,1:T(8,128)(2,1)S(1)}, u32[]{:S(2)}, u32[]{:S(2)}) collective-permute-start(bf16[1024,1,256]{2,0,1:T(8,128)(2,1)S(1)} %convert_bitcast_fusion), channel_id=1, source_target_pairs={{0,16},{8,24},{16,0},{24,8},{1,17},{9,25},{17,1},{25,9},{2,18},{10... | collective-permute-start | bytes 1572872 | tf_op jit(solution)/shard_map/ppermute | solution.py:24
  44.7 13.9 %collective-permute-start.9 = (bf16[1,128,1024]{2,1,0:T(8,128)(2,1)S(1)}, bf16[1,128,1024]{2,1,0:T(8,128)(2,1)S(1)}, u32[]{:S(2)}, u32[]{:S(2)}) collective-permute-start(bf16[1,128,1024]{2,1,0:T(8,128)(2,1)S(1)} %fusion.4), channel_id=1, source_target_pairs={{0,4},{1,5},{2,6},{3,7},{4,0},{5,1},{6,2},{7,3},{8,12},{9,13},{10,... | collective-permute-start | bytes 786440 | tf_op jit(solution)/shard_map/ppermute | solution.py:24
  47.1 14.6 %collective-permute-start.7 = (bf16[1,128,1024]{2,1,0:T(8,128)(2,1)S(1)}, bf16[1,128,1024]{2,1,0:T(8,128)(2,1)S(1)}, u32[]{:S(2)}, u32[]{:S(2)}) collective-permute-start(bf16[1,128,1024]{2,1,0:T(8,128)(2,1)S(1)} %fusion.4), channel_id=1, source_target_pairs={{0,2},{1,3},{2,0},{3,1},{4,6},{5,7},{6,4},{7,5},{8,10},{9,11},{10,... | collective-permute-start | bytes 786440 | tf_op jit(solution)/shard_map/ppermute | solution.py:24
  58.6 7.4 %collective-permute-start.10 = (bf16[1,128,1024]{2,1,0:T(8,128)(2,1)S(1)}, bf16[1,128,1024]{2,1,0:T(8,128)(2,1)S(1)}, u32[]{:S(2)}, u32[]{:S(2)}) collective-permute-start(bf16[1,128,1024]{2,1,0:T(8,128)(2,1)S(1)} %collective-permute-done.9), channel_id=1, source_target_pairs={{0,2},{1,3},{2,0},{3,1},{4,6},{5,7},{6,4},{7,5},{8,10},{9,11},{10,... | collective-permute-start | bytes 786440 | tf_op jit(solution)/shard_map/ppermute | solution.py:24
  58.7 3.9 %copy-start.2 = (bf16[1024,1,256]{2,0,1:T(8,128)(2,1)}, bf16[1024,1,256]{2,0,1:T(8,128)(2,1)S(1)}, u32[]{:S(2)}) copy-start(bf16[1024,1,256]{2,0,1:T(8,128)(2,1)S(1)} %collective-permute-done.14) | copy-start | bytes 1572868
  59.8 45.8 %collective-permute-start.15 = (bf16[1024,2,256]{2,0,1:T(8,128)(2,1)}, bf16[1024,2,256]{2,0,1:T(8,128)(2,1)}, u32[]{:S(2)}, u32[]{:S(2)}) collective-permute-start(bf16[1024,2,256]{2,0,1:T(8,128)(2,1)} %maximum_select_fusion.2), channel_id=1, source_target_pairs={{0,8},{8,0},{16,24},{24,16},{1,9},{9,1},{17,25},{25,17},{2,10},{10... | collective-permute-start | bytes 3145736 | tf_op jit(solution)/shard_map/ppermute | solution.py:24
  62.6 13.8 %collective-permute-start.8 = (bf16[2,128,1024]{2,1,0:T(8,128)(2,1)}, bf16[2,128,1024]{2,1,0:T(8,128)(2,1)S(1)}, u32[]{:S(2)}, u32[]{:S(2)}) collective-permute-start(bf16[2,128,1024]{2,1,0:T(8,128)(2,1)} %pad_maximum_fusion), channel_id=1, source_target_pairs={{0,1},{1,0},{2,3},{3,2},{4,5},{5,4},{6,7},{7,6},{8,9},{9,8},{10,11... | collective-permute-start | bytes 1572872 | tf_op jit(solution)/shard_map/ppermute | solution.py:24
  63.8 37.8 %collective-permute-start = (bf16[128,1024]{1,0:T(8,128)(2,1)}, bf16[128,1024]{1,0:T(8,128)(2,1)S(1)}, u32[]{:S(2)}, u32[]{:S(2)}) collective-permute-start(bf16[128,1024]{1,0:T(8,128)(2,1)} %get-tuple-element.15), channel_id=1, source_target_pairs={{0,1},{1,0},{2,3},{3,2},{4,5},{5,4},{6,7},{7,6},{8,9},{9,8},{10,11... | collective-permute-start | bytes 786440 | tf_op jit(solution)/shard_map/ppermute | solution.py:24
  64.1 39.3 %collective-permute-start.1 = (bf16[128,1024]{1,0:T(8,128)(2,1)}, bf16[128,1024]{1,0:T(8,128)(2,1)S(1)}, u32[]{:S(2)}, u32[]{:S(2)}) collective-permute-start(bf16[128,1024]{1,0:T(8,128)(2,1)} %get-tuple-element.16), channel_id=1, source_target_pairs={{0,2},{1,3},{2,0},{3,1},{4,6},{5,7},{6,4},{7,5},{8,10},{9,11},{10,... | collective-permute-start | bytes 786440 | tf_op jit(solution)/shard_map/ppermute | solution.py:24
  66.9 32.1 %collective-permute-start.11 = (bf16[2,128,1024]{2,1,0:T(8,128)(2,1)}, bf16[2,128,1024]{2,1,0:T(8,128)(2,1)}, u32[]{:S(2)}, u32[]{:S(2)}) collective-permute-start(bf16[2,128,1024]{2,1,0:T(8,128)(2,1)} %pad_maximum_fusion.1), channel_id=1, source_target_pairs={{0,1},{1,0},{2,3},{3,2},{4,5},{5,4},{6,7},{7,6},{8,9},{9,8},{10,11... | collective-permute-start | bytes 1572872 | tf_op jit(solution)/shard_map/ppermute | solution.py:24
  69.0 36.6 %copy-start.3 = (bf16[1024,1,256]{2,0,1:T(8,128)(2,1)S(1)}, bf16[1024,1,256]{2,0,1:T(8,128)(2,1)}, u32[]{:S(2)}) copy-start(bf16[1024,1,256]{2,0,1:T(8,128)(2,1)} %copy-done.2) | copy-start | bytes 1572868
  76.4 40.5 %collective-permute-start.2 = (bf16[128,1024]{1,0:T(8,128)(2,1)}, bf16[128,1024]{1,0:T(8,128)(2,1)}, u32[]{:S(2)}, u32[]{:S(2)}) collective-permute-start(bf16[128,1024]{1,0:T(8,128)(2,1)} %get-tuple-element.17), channel_id=1, source_target_pairs={{0,3},{1,2},{2,1},{3,0},{4,7},{5,6},{6,5},{7,4},{8,11},{9,10},{10,... | collective-permute-start | bytes 786440 | tf_op jit(solution)/shard_map/ppermute | solution.py:24
  98.9 29.3 %collective-permute-start.3 = (bf16[128,1024]{1,0:T(8,128)(2,1)}, bf16[128,1024]{1,0:T(8,128)(2,1)}, u32[]{:S(2)}, u32[]{:S(2)}) collective-permute-start(bf16[128,1024]{1,0:T(8,128)(2,1)} %get-tuple-element.18), channel_id=1, source_target_pairs={{0,4},{1,5},{2,6},{3,7},{4,0},{5,1},{6,2},{7,3},{8,12},{9,13},{10,... | collective-permute-start | bytes 786440 | tf_op jit(solution)/shard_map/ppermute | solution.py:24
  101.6 32.2 %collective-permute-start.4 = (bf16[128,1024]{1,0:T(8,128)(2,1)}, bf16[128,1024]{1,0:T(8,128)(2,1)}, u32[]{:S(2)}, u32[]{:S(2)}) collective-permute-start(bf16[128,1024]{1,0:T(8,128)(2,1)} %get-tuple-element.19), channel_id=1, source_target_pairs={{0,5},{1,4},{2,7},{3,6},{4,1},{5,0},{6,3},{7,2},{8,13},{9,12},{10,... | collective-permute-start | bytes 786440 | tf_op jit(solution)/shard_map/ppermute | solution.py:24
  103.4 38.4 %collective-permute-start.5 = (bf16[128,1024]{1,0:T(8,128)(2,1)}, bf16[128,1024]{1,0:T(8,128)(2,1)}, u32[]{:S(2)}, u32[]{:S(2)}) collective-permute-start(bf16[128,1024]{1,0:T(8,128)(2,1)} %get-tuple-element.20), channel_id=1, source_target_pairs={{0,6},{1,7},{2,4},{3,5},{4,2},{5,3},{6,0},{7,1},{8,14},{9,15},{10,... | collective-permute-start | bytes 786440 | tf_op jit(solution)/shard_map/ppermute | solution.py:24
  105.6 42.7 %collective-permute-start.6 = (bf16[128,1024]{1,0:T(8,128)(2,1)}, bf16[128,1024]{1,0:T(8,128)(2,1)}, u32[]{:S(2)}, u32[]{:S(2)}) collective-permute-start(bf16[128,1024]{1,0:T(8,128)(2,1)} %get-tuple-element.21), channel_id=1, source_target_pairs={{0,7},{1,6},{2,5},{3,4},{4,3},{5,2},{6,1},{7,0},{8,15},{9,14},{10,... | collective-permute-start | bytes 786440 | tf_op jit(solution)/shard_map/ppermute | solution.py:24

commit v2 on v1

v2 whole, which is shorter than its diff:
```python
import functools
import math

import jax
import jax.numpy as jnp
from jax import lax
from jax.experimental import pallas as pl
from jax.experimental.pallas import tpu as pltpu
from jax.sharding import PartitionSpec as P

BLOCK = 64


norm_eps = 1e-05
inner_gain = 0.4
outer_rate = 0.7
outer_beta = 0.9
mix_weight = 0.5
code_range = 448.0


def swap(value, axis, mask):
    size = lax.axis_size(axis)
    return lax.ppermute(value, axis, [(i, i ^ mask) for i in range(size)])


def prepare_kernel(tokens_ref, cotangent_ref, blocks_ref, scaled_ref):
    shards, _, rows = blocks_ref.shape
    squares = None
    for k in range(shards):
        block = tokens_ref[:, k * rows : (k + 1) * rows]
        blocks_ref[k] = block
        block = block.astype(jnp.float32)
        squares = block * block if squares is None else squares + block * block
    mean = jnp.sum(squares, axis=-1, keepdims=True) / (shards * rows)
    scaled_ref[...] = (cotangent_ref[...].astype(jnp.float32) * lax.rsqrt(mean + norm_eps)).astype(jnp.bfloat16)


def prepare(tokens, cotangent, shards):
    count, features = tokens.shape
    width = cotangent.shape[1]
    rows = features // shards
    tile = min(count, 32)
    return pl.pallas_call(
        prepare_kernel,
        out_shape=(
            jax.ShapeDtypeStruct((shards, count, rows), jnp.bfloat16),
            jax.ShapeDtypeStruct((count, width), jnp.bfloat16),
        ),
        grid=(count // tile,),
        in_specs=[
            pl.BlockSpec((tile, features), lambda i: (i, 0)),
            pl.BlockSpec((tile, width), lambda i: (i, 0)),
        ],
        out_specs=(
            pl.BlockSpec((shards, tile, rows), lambda i: (0, i, 0)),
            pl.BlockSpec((tile, width), lambda i: (i, 0)),
        ),
        cost_estimate=pl.CostEstimate(
            flops=3 * count * features, bytes_accessed=4 * count * (features + width), transcendentals=count
        ),
        name="prepare",
    )(tokens, cotangent)


def code_kernel(side_ref, shared_ref, weight_ref, decoded_ref):
    lanes = 2 * BLOCK
    share = decoded_ref.shape[3]
    lane = lax.broadcasted_iota(jnp.int32, (shared_ref.shape[0], lanes), 1)
    low = lane < BLOCK
    side = side_ref[0]
    for start in range(0, shared_ref.shape[1], lanes):
        columns = slice(start, start + lanes)
        delta = shared_ref[:, columns].astype(jnp.float32) - weight_ref[:, columns].astype(jnp.float32)
        size = jnp.abs(delta)
        largest = jnp.where(
            low,
            jnp.max(jnp.where(low, size, 0.0), axis=-1, keepdims=True),
            jnp.max(jnp.where(low, 0.0, size), axis=-1, keepdims=True),
        )
        scale = ((largest + 1e-06) * (1.0 / code_range)).astype(jnp.bfloat16).astype(jnp.float32)
        coded = (delta / scale).astype(jnp.bfloat16)
        decoded = (coded.astype(jnp.float32) * scale).astype(jnp.bfloat16)
        piece = min(share, lanes)
        for at in range(0, lanes, piece):
            group, offset = divmod(start + at, share)
            decoded_ref[(group % 2) ^ side, group // 2, :, offset : offset + piece] = decoded[:, at : at + piece]


def code_and_decode(shared, weight, groups, side):
    rows, width = shared.shape
    tile = min(rows, 128)
    share = width // groups
    spec = pl.BlockSpec((tile, width), lambda i, side: (i, 0))
    return pl.pallas_call(
        code_kernel,
        out_shape=jax.ShapeDtypeStruct((2, groups // 2, rows, share), jnp.bfloat16),
        grid_spec=pltpu.PrefetchScalarGridSpec(
            num_scalar_prefetch=1,
            grid=(rows // tile,),
            in_specs=[spec, spec],
            out_specs=pl.BlockSpec((2, groups // 2, tile, share), lambda i, side: (0, 0, i, 0)),
        ),
        cost_estimate=pl.CostEstimate(flops=20 * rows * width, bytes_accessed=6 * rows * width, transcendentals=0),
        name="code_and_decode",
    )(side.reshape(1), shared, weight)


def mix_kernel(parts, mine_ref, *refs):
    tokens, cotangents = refs[:parts], refs[parts : 2 * parts]
    gain_ref, weight_ref, shared_ref, out_ref = refs[2 * parts :]
    total = None
    pair = 2 if parts % 2 == 0 else 1
    for first in range(0, parts, pair):
        product = lax.dot_general(
            jnp.concatenate([ref[0] for ref in tokens[first : first + pair]], axis=0),
            jnp.concatenate([ref[...] for ref in cotangents[first : first + pair]], axis=0),
            (((0,), (0,)), ((), ())),
            preferred_element_type=jnp.float32,
        )
        total = product if total is None else total + product
    groups, _, share = shared_ref.shape
    for group in range(groups):
        columns = slice(group * share, (group + 1) * share)
        weight = weight_ref[:, columns].astype(jnp.float32) + shared_ref[group].astype(jnp.float32)
        out_ref[:, columns] = (mix_weight * weight - gain_ref[...] * total[:, columns]).astype(jnp.bfloat16)


def mix(mine, tokens, cotangents, gain, weight, shared):
    parts, depth, rows = tokens.shape
    width = weight.shape[1]
    groups, _, share = shared.shape
    tile = min(rows, 256)

    def token_block(k):
        return pl.BlockSpec((1, depth, tile), lambda i, mine: (mine[0] ^ k, 0, i))

    by_row = pl.BlockSpec((tile, width), lambda i, mine: (i, 0))
    return pl.pallas_call(
        functools.partial(mix_kernel, parts),
        out_shape=jax.ShapeDtypeStruct((rows, width), jnp.bfloat16),
        grid_spec=pltpu.PrefetchScalarGridSpec(
            num_scalar_prefetch=1,
            grid=(rows // tile,),
            in_specs=[token_block(k) for k in range(parts)]
            + [pl.BlockSpec((depth, width), lambda i, mine: (0, 0))] * parts
            + [
                pl.BlockSpec((tile, 1), lambda i, mine: (i, 0)),
                by_row,
                pl.BlockSpec((groups, tile, share), lambda i, mine: (0, i, 0)),
            ],
            out_specs=by_row,
        ),
        compiler_params=pltpu.CompilerParams(vmem_limit_bytes=48 * 2**20),
        cost_estimate=pl.CostEstimate(
            flops=2 * parts * depth * rows * width,
            bytes_accessed=2 * parts * depth * (rows + width) + 6 * rows * width,
            transcendentals=0,
        ),
        name="mix",
    )(mine.reshape(1), *([tokens] * parts), *cotangents, gain, weight, shared)


def on_device(tokens, norm_gain, cotangent, layer_weight, shared_copy, master, momentum):
    tokens, cotangent, weight = tokens[0], cotangent[0], layer_weight[0]
    shards = lax.axis_size("fsdp")
    groups = lax.axis_size("replica")
    mine = lax.axis_index("fsdp")
    own = lax.axis_index("replica")
    rows, width = weight.shape
    share = width // groups
    inner_rate = inner_gain / math.sqrt(tokens.shape[0] * shards)

    blocks, scaled = prepare(tokens, cotangent, shards)
    blocks, scaled, weight, shared_copy = lax.optimization_barrier((blocks, scaled, weight, shared_copy))
    columns = lax.all_to_all(blocks, "fsdp", split_axis=0, concat_axis=0, tiled=True)

    cotangents = {0: scaled}
    bit = shards // 2
    while bit:
        held = sorted(cotangents)
        for part in ([k for k in held if k < shards // 2], [k for k in held if k >= shards // 2]):
            if part:
                arrived = swap(jnp.stack([cotangents[k] for k in part]), "fsdp", bit)
                for place, k in enumerate(part):
                    cotangents[k ^ bit] = arrived[place]
        bit //= 2

    kept, sent = code_and_decode(shared_copy, weight, groups, own % 2)
    total = kept.astype(jnp.float32) + swap(sent, "replica", 1).astype(jnp.float32)
    bit = 2
    while bit < groups:
        side = (own // bit) % 2
        split = total.astype(jnp.bfloat16).reshape(-1, 2, rows, share)
        kept = lax.dynamic_index_in_dim(split, side, axis=1, keepdims=False)
        sent = lax.dynamic_index_in_dim(split, 1 - side, axis=1, keepdims=False)
        total = kept.astype(jnp.float32) + swap(sent, "replica", bit).astype(jnp.float32)
        bit *= 2
    average = total.reshape(rows, share) / groups
    momentum_next = outer_beta * momentum + average
    master_next = master - outer_rate * (average + outer_beta * momentum_next)

    gathered = master_next.astype(jnp.bfloat16).reshape(1, rows, share)
    bit = groups // 2
    while bit:
        side = (own // bit) % 2
        other = swap(gathered, "replica", bit)
        gathered = jnp.where(
            side == 0, jnp.stack([gathered, other], axis=1), jnp.stack([other, gathered], axis=1)
        ).reshape(-1, rows, share)
        bit //= 2

    gain = lax.dynamic_slice_in_dim(norm_gain, mine * rows, rows).astype(jnp.float32)
    gain = (gain * ((1.0 - mix_weight) * inner_rate)).reshape(rows, 1)
    layer_next = mix(mine, columns, [cotangents[k] for k in range(shards)], gain, weight, gathered)
    return (layer_next[None], master_next, momentum_next)


def solution(mesh):
    in_specs = (
        P("replica", "fsdp", None),
        P(),
        P("replica", "fsdp", None),
        P("replica", "fsdp", None),
        P("fsdp", None),
        P("fsdp", "replica"),
        P("fsdp", "replica"),
    )
    out_specs = (P("replica", "fsdp", None), P("fsdp", "replica"), P("fsdp", "replica"))
    return jax.shard_map(
        on_device, mesh=mesh, in_specs=in_specs, out_specs=out_specs, check_vma=False
    )
```

time: 155 us -> 125 us (0.81)
  the two profiles are of different devices: /device:TPU:9 before, /device:TPU:0 now
where the time goes in v2:
time: 125 us; the launch traced here: 124 us
  waiting for transfers between devices  61.6 us (49%)
  Pallas kernels  17.6 us (14%)
  starting transfers between devices  17.4 us (14%)
  other arithmetic  14.4 us (12%)
  local copies, waits for them, and re-layouts  12.3 us (10%)
    ppermute x9, waiting for transfers between devices, swap(): return lax.ppermute(value, axis, [(i, i ^ mask) for i in range(size)])  61.6 us
    ppermute x9, starting transfers between devices, swap(): return lax.ppermute(value, axis, [(i, i ^ mask) for i in range(size)])  10.5 us
    pallas_call x1, Pallas kernels, code_and_decode(): pl.pallas_call(code_kernel, out_shape=jax.ShapeDtypeStruct((2, groups //...  7.42 us
    all_to_all x1, starting transfers between devices, on_device(): lax.all_to_all(blocks, 'fsdp', split_axis=0, concat_axis=0, tiled=True)  6.85 us
    pallas_call x1, Pallas kernels, mix(): pl.pallas_call(functools.partial(mix_kernel, parts), out_shape=jax.ShapeD...  6.07 us
    select_n x3, other arithmetic, on_device(): jnp.where(side == 0, jnp.stack([gathered, other], axis=1), jnp.stack([oth...  6.01 us
    unnamed x18, local copies, waits for them, and re-layouts  4.76 us
    pallas_call x1, Pallas kernels, prepare(): pl.pallas_call(prepare_kernel, out_shape=(jax.ShapeDtypeStruct((shards, c...  4.13 us
  transfers between devices with their start and end apart: 10, of which 5 were waited for; matrix products, arithmetic and copies ran while one was open for 17% of the time, Pallas kernels for 0%

profile of v2, /device:TPU:0, one launch (start us, length us, event | category | flops | bytes accessed | tf_op | source)
XLA Modules:
  0.0 124.0 jit_solution(16710460449309730607)
XLA Ops:
  0.6 4.1 %prepare.1 = (bf16[8,128,1024]{2,1,0:T(8,128)(2,1)}, bf16[128,1024]{1,0:T(8,128)(2,1)}) custom-call(bf16[128,8192]{1,0:T(8,128)(2,1)} %bitcast.51, bf16[128,1024]{1,0:T(8,128)(2,1)} %bitcast.53), custom_call_target="tpu_custom_call" | custom-call | flops 3145728 | bytes 4718592 | tf_op jit(solution)/shard_map/prepare/pallas_call | solution.py:44
  4.8 7.4 %code_and_decode.1 = bf16[2,2,1024,256]{3,2,1,0:T(8,128)(2,1)} custom-call(s32[1]{0:T(128)} %bitcast.13.side_ref, bf16[1024,1024]{1,0:T(8,128)(2,1)} %shared_ref, bf16[1024,1024]{1,0:T(8,128)(2,1)} %bitcast.48), custom_call_target="tpu_custom_call" | custom-call | flops 20971520 | bytes 6291456 | tf_op jit(solution)/shard_map/code_and_decode/pallas_call | solution.py:95
  12.2 1.3 %slice_bitcast_fusion = bf16[2,1024,256]{2,1,0:T(8,128)(2,1)S(1)} fusion(bf16[2,2,1024,256]{3,2,1,0:T(8,128)(2,1)} %code_and_decode.1), kind=kLoop, calls=%fused_computation.3 | loop fusion | bytes 2097152 | tf_op jit(solution)/shard_map/unstack | solution.py:189
  14.0 6.9 %all-to-all-start = ((bf16[8,128,1024]{2,1,0:T(8,128)(2,1)}), bf16[8,128,1024]{2,1,0:T(8,128)(2,1)S(1)}, u32[]{:S(2)}, u32[]{:S(2)}) async-start(bf16[8,128,1024]{2,1,0:T(8,128)(2,1)} %get-tuple-element.11), calls=%async_computation | async-start | bytes 4194304 | tf_op jit(solution)/shard_map/all_to_all | solution.py:176
  20.9 1.8 %fusion = bf16[2,1024,256]{2,1,0:T(8,128)(2,1)S(1)} fusion(bf16[2,1024,256]{2,1,0:T(8,128)(2,1)} %collective-permute-done.5, bf16[2,2,1024,256]{3,2,1,0:T(8,128)(2,1)} %code_and_decode.1), kind=kLoop, calls=%fused_computation.2 | loop fusion | flops 2097152 | bytes 3145728 | tf_op jit(solution)/shard_map/convert_element_type | solution.py:194
  23.5 1.5 %collective-permute-start.6 = (bf16[1,1024,256]{2,1,0:T(8,128)(2,1)}, bf16[1,1024,256]{2,1,0:T(8,128)(2,1)}, u32[]{:S(2)}, u32[]{:S(2)}) collective-permute-start(bf16[1,1024,256]{2,1,0:T(8,128)(2,1)} %constant_dynamic-slice_fusion), channel_id=1, source_target_pairs={{0,16},{8,24},{16,0},{24,8},{1,17},{9,25},{17,1},{25,9},{2,18},{10... | collective-permute-start | bytes 1572872 | tf_op jit(solution)/shard_map/ppermute | solution.py:24
  25.0 12.9 %collective-permute-done.6 = bf16[1,1024,256]{2,1,0:T(8,128)(2,1)} collective-permute-done((bf16[1,1024,256]{2,1,0:T(8,128)(2,1)}, bf16[1,1024,256]{2,1,0:T(8,128)(2,1)}, u32[]{:S(2)}, u32[]{:S(2)}) %collective-permute-start.6) | collective-permute-done | bytes 524320 | tf_op jit(solution)/shard_map/ppermute | solution.py:24
  37.9 3.2 %convert_bitcast_fusion.1 = (bf16[1,1,1024,256]{3,2,0,1:T(8,128)(2,1)}, f32[1024,256]{1,0:T(8,128)S(1)}, f32[1024,256]{1,0:T(8,128)}) fusion(f32[1024,256]{1,0:T(8,128)} %param.12, bf16[1,1024,256]{2,1,0:T(8,128)(2,1)} %collective-permute-done.6, bf16[2,1024,256]{2,1,0:T(8,128)(2,1)S(1)} %fusion, s32[]{:T(128)S(6)} %select_n.71, f32[1024,256]{1,0:T(8,128)} %param.13), kind=kLoop, calls=%fused_computation.19 | loop fusion | flops 2883584 | bytes 5767172 | tf_op jit(solution)/shard_map/stack | solution.py:209
  41.1 1.0 convert_bitcast_fusion
  42.0 1.5 %collective-permute-start.7 = (bf16[1,1024,256]{2,1,0:T(8,128)(2,1)}, bf16[1,1024,256]{2,1,0:T(8,128)(2,1)}, u32[]{:S(2)}, u32[]{:S(2)}) collective-permute-start(bf16[1,1024,256]{2,1,0:T(8,128)(2,1)} %convert_bitcast_fusion), channel_id=1, source_target_pairs={{0,16},{8,24},{16,0},{24,8},{1,17},{9,25},{17,1},{25,9},{2,18},{10... | collective-permute-start | bytes 1572872 | tf_op jit(solution)/shard_map/ppermute | solution.py:24
  43.5 2.6 %collective-permute-start.2 = (bf16[1,128,1024]{2,1,0:T(8,128)(2,1)S(1)}, bf16[1,128,1024]{2,1,0:T(8,128)(2,1)S(1)}, u32[]{:S(2)}, u32[]{:S(2)}) collective-permute-start(bf16[1,128,1024]{2,1,0:T(8,128)(2,1)S(1)} %bitcast.42), channel_id=1, source_target_pairs={{0,4},{1,5},{2,6},{3,7},{4,0},{5,1},{6,2},{7,3},{8,12},{9,13},{10,... | collective-permute-start | bytes 786440 | tf_op jit(solution)/shard_map/ppermute | solution.py:24
  46.2 1.5 %collective-permute-start = (bf16[1,128,1024]{2,1,0:T(8,128)(2,1)S(1)}, bf16[1,128,1024]{2,1,0:T(8,128)(2,1)S(1)}, u32[]{:S(2)}, u32[]{:S(2)}) collective-permute-start(bf16[1,128,1024]{2,1,0:T(8,128)(2,1)S(1)} %bitcast.43), channel_id=1, source_target_pairs={{0,2},{1,3},{2,0},{3,1},{4,6},{5,7},{6,4},{7,5},{8,10},{9,11},{10,... | collective-permute-start | bytes 786440 | tf_op jit(solution)/shard_map/ppermute | solution.py:24
  47.6 33.3 %collective-permute-done.2 = bf16[1,128,1024]{2,1,0:T(8,128)(2,1)S(1)} collective-permute-done((bf16[1,128,1024]{2,1,0:T(8,128)(2,1)S(1)}, bf16[1,128,1024]{2,1,0:T(8,128)(2,1)S(1)}, u32[]{:S(2)}, u32[]{:S(2)}) %collective-permute-start.2) | collective-permute-done | bytes 262176 | tf_op jit(solution)/shard_map/ppermute | solution.py:24
  81.0 0.8 pad_maximum_fusion
  81.8 1.5 %collective-permute-start.1 = (bf16[2,128,1024]{2,1,0:T(8,128)(2,1)}, bf16[2,128,1024]{2,1,0:T(8,128)(2,1)}, u32[]{:S(2)}, u32[]{:S(2)}) collective-permute-start(bf16[2,128,1024]{2,1,0:T(8,128)(2,1)} %pad_maximum_fusion), channel_id=1, source_target_pairs={{0,1},{1,0},{2,3},{3,2},{4,5},{5,4},{6,7},{7,6},{8,9},{9,8},{10,11... | collective-permute-start | bytes 1572872 | tf_op jit(solution)/shard_map/ppermute | solution.py:24
  83.3 2.7 %maximum_select_fusion.2 = bf16[2,1024,256]{2,1,0:T(8,128)(2,1)} fusion(bf16[1,1024,256]{2,1,0:T(8,128)(2,1)} %collective-permute-done.7, bf16[1,1024,256]{2,1,0:T(8,128)(2,1)} %convert_bitcast_fusion, pred[]{:T(512)S(6)} %eq.12), kind=kLoop, calls=%fused_computation.6 | loop fusion | flops 1572864 | bytes 2097153 | tf_op jit(solution)/shard_map/jit(_where)/select_n | solution.py:208
  86.0 2.5 %collective-permute-done.3 = bf16[1,128,1024]{2,1,0:T(8,128)(2,1)S(1)} collective-permute-done((bf16[1,128,1024]{2,1,0:T(8,128)(2,1)S(1)}, bf16[1,128,1024]{2,1,0:T(8,128)(2,1)S(1)}, u32[]{:S(2)}, u32[]{:S(2)}) %collective-permute-start.3) | collective-permute-done | bytes 262176 | tf_op jit(solution)/shard_map/ppermute | solution.py:24
  88.6 0.9 pad_maximum_fusion.1
  89.4 1.5 %collective-permute-start.4 = (bf16[2,128,1024]{2,1,0:T(8,128)(2,1)}, bf16[2,128,1024]{2,1,0:T(8,128)(2,1)}, u32[]{:S(2)}, u32[]{:S(2)}) collective-permute-start(bf16[2,128,1024]{2,1,0:T(8,128)(2,1)} %pad_maximum_fusion.1), channel_id=1, source_target_pairs={{0,1},{1,0},{2,3},{3,2},{4,5},{5,4},{6,7},{7,6},{8,9},{9,8},{10,11... | collective-permute-start | bytes 1572872 | tf_op jit(solution)/shard_map/ppermute | solution.py:24
  91.8 5.2 %collective-permute-done.1 = bf16[2,128,1024]{2,1,0:T(8,128)(2,1)} collective-permute-done((bf16[2,128,1024]{2,1,0:T(8,128)(2,1)}, bf16[2,128,1024]{2,1,0:T(8,128)(2,1)}, u32[]{:S(2)}, u32[]{:S(2)}) %collective-permute-start.1) | collective-permute-done | bytes 524320 | tf_op jit(solution)/shard_map/ppermute | solution.py:24
  97.0 1.9 %slice_bitcast_fusion.4 = (bf16[128,1024]{1,0:T(8,128)(2,1)}, bf16[128,1024]{1,0:T(8,128)(2,1)}) fusion(bf16[2,128,1024]{2,1,0:T(8,128)(2,1)} %collective-permute-done.1), kind=kLoop, calls=%fused_computation.16 | loop fusion | bytes 1048576 | tf_op jit(solution)/shard_map/squeeze | solution.py:186
  98.9 7.7 %collective-permute-done.4 = bf16[2,128,1024]{2,1,0:T(8,128)(2,1)} collective-permute-done((bf16[2,128,1024]{2,1,0:T(8,128)(2,1)}, bf16[2,128,1024]{2,1,0:T(8,128)(2,1)}, u32[]{:S(2)}, u32[]{:S(2)}) %collective-permute-start.4) | collective-permute-done | bytes 524320 | tf_op jit(solution)/shard_map/ppermute | solution.py:24
  106.6 1.8 %slice_bitcast_fusion.2 = (bf16[128,1024]{1,0:T(8,128)(2,1)}, bf16[128,1024]{1,0:T(8,128)(2,1)}) fusion(bf16[2,128,1024]{2,1,0:T(8,128)(2,1)} %collective-permute-done.4), kind=kLoop, calls=%fused_computation.14 | loop fusion | bytes 1048576 | tf_op jit(solution)/shard_map/squeeze | solution.py:186
  108.4 1.4 %maximum_select_fusion.1 = bf16[2,1,1024,256]{3,2,0,1:T(8,128)(2,1)S(1)} fusion(bf16[1,1,1024,256]{3,2,0,1:T(8,128)(2,1)} %bitcast.19, bf16[1,1,1024,256]{3,2,0,1:T(8,128)(2,1)S(1)} %copy-done.8, pred[]{:T(512)S(6)} %eq.12), kind=kLoop, calls=%fused_computation.5 | loop fusion | flops 1572864 | bytes 2097153 | tf_op jit(solution)/shard_map/jit(_where)/select_n | solution.py:208
  109.8 1.9 %maximum_select_fusion = bf16[2,2,1024,256]{3,2,0,1:T(8,128)(2,1)S(1)} fusion(bf16[2,1,1024,256]{3,2,0,1:T(8,128)(2,1)} %bitcast.20, bf16[2,1,1024,256]{3,2,0,1:T(8,128)(2,1)S(1)} %maximum_select_fusion.1, pred[]{:T(512)S(6)} %eq.11), kind=kLoop, calls=%fused_computation | loop fusion | flops 3145728 | bytes 4194305 | tf_op jit(solution)/shard_map/jit(_where)/select_n | solution.py:208
  111.7 1.5 %copy.11 = bf16[2,2,1024,256]{3,2,1,0:T(8,128)(2,1)} copy(bf16[2,2,1024,256]{3,2,0,1:T(8,128)(2,1)S(1)} %maximum_select_fusion) | data formatting | bytes 4194304 | tf_op jit(solution)/shard_map/jit(_where)/select_n | solution.py:208
  113.2 0.9 copy-done.2
  114.1 0.9 copy-done.3
  115.1 0.9 copy-done.4
  116.0 0.9 copy-done.5
  117.0 0.9 copy-done.6
  117.9 6.1 %mix.1 = bf16[1024,1024]{1,0:T(8,128)(2,1)} custom-call(s32[1]{0:T(128)} %bitcast.mine_ref, bf16[8,128,1024]{2,1,0:T(8,128)(2,1)S(1)} %all-to-all-done.refs_0_.refs_1_.refs_2_.refs_3_.refs_4_.refs_5_.refs_6_.refs_7_, bf16[8,128,1024]{2,1,0:T(8,128)(2,1)S(1)} %all-to-all-done.refs_0_.refs_1_.refs_2_.refs_3_.refs_4_.refs_5_.refs_6_.refs_7_, ...), custom_call_target="tpu_custom_call" | custom-call | flops 2147483648 | bytes 10485760 | tf_op jit(solution)/shard_map/mix/pallas_call | solution.py:139
  (24 shorter events, 2.3 us)
Async XLA Ops:
  13.5 7.4 %collective-permute-start.5 = (bf16[2,1024,256]{2,1,0:T(8,128)(2,1)S(1)}, bf16[2,1024,256]{2,1,0:T(8,128)(2,1)}, u32[]{:S(2)}, u32[]{:S(2)}) collective-permute-start(bf16[2,1024,256]{2,1,0:T(8,128)(2,1)S(1)} %slice_bitcast_fusion), channel_id=1, source_target_pairs={{0,8},{8,0},{16,24},{24,16},{1,9},{9,1},{17,25},{25,17},{2,10},{10... | collective-permute-start | bytes 3145736 | tf_op jit(solution)/shard_map/ppermute | solution.py:24
  14.0 99.2 %all-to-all-start = ((bf16[8,128,1024]{2,1,0:T(8,128)(2,1)}), bf16[8,128,1024]{2,1,0:T(8,128)(2,1)S(1)}, u32[]{:S(2)}, u32[]{:S(2)}) async-start(bf16[8,128,1024]{2,1,0:T(8,128)(2,1)} %get-tuple-element.11), calls=%async_computation | async-start | bytes 4194304 | tf_op jit(solution)/shard_map/all_to_all | solution.py:176
  23.5 14.3 %collective-permute-start.6 = (bf16[1,1024,256]{2,1,0:T(8,128)(2,1)}, bf16[1,1024,256]{2,1,0:T(8,128)(2,1)}, u32[]{:S(2)}, u32[]{:S(2)}) collective-permute-start(bf16[1,1024,256]{2,1,0:T(8,128)(2,1)} %constant_dynamic-slice_fusion), channel_id=1, source_target_pairs={{0,16},{8,24},{16,0},{24,8},{1,17},{9,25},{17,1},{25,9},{2,18},{10... | collective-permute-start | bytes 1572872 | tf_op jit(solution)/shard_map/ppermute | solution.py:24
  25.0 18.5 %copy-start = (bf16[128,1024]{1,0:T(8,128)(2,1)S(1)}, bf16[128,1024]{1,0:T(8,128)(2,1)}, u32[]{:S(2)}) copy-start(bf16[128,1024]{1,0:T(8,128)(2,1)} %get-tuple-element.12.refs_8_) | copy-start | bytes 786436
  41.1 2.5 %copy-start.7 = (f32[1024,256]{1,0:T(8,128)}, f32[1024,256]{1,0:T(8,128)S(1)}, u32[]{:S(2)}) copy-start(f32[1024,256]{1,0:T(8,128)S(1)} %get-tuple-element.16) | copy-start | bytes 3145732
  42.0 41.3 %collective-permute-start.7 = (bf16[1,1024,256]{2,1,0:T(8,128)(2,1)}, bf16[1,1024,256]{2,1,0:T(8,128)(2,1)}, u32[]{:S(2)}, u32[]{:S(2)}) collective-permute-start(bf16[1,1024,256]{2,1,0:T(8,128)(2,1)} %convert_bitcast_fusion), channel_id=1, source_target_pairs={{0,16},{8,24},{16,0},{24,8},{1,17},{9,25},{17,1},{25,9},{2,18},{10... | collective-permute-start | bytes 1572872 | tf_op jit(solution)/shard_map/ppermute | solution.py:24
  43.5 37.4 %collective-permute-start.2 = (bf16[1,128,1024]{2,1,0:T(8,128)(2,1)S(1)}, bf16[1,128,1024]{2,1,0:T(8,128)(2,1)S(1)}, u32[]{:S(2)}, u32[]{:S(2)}) collective-permute-start(bf16[1,128,1024]{2,1,0:T(8,128)(2,1)S(1)} %bitcast.42), channel_id=1, source_target_pairs={{0,4},{1,5},{2,6},{3,7},{4,0},{5,1},{6,2},{7,3},{8,12},{9,13},{10,... | collective-permute-start | bytes 786440 | tf_op jit(solution)/shard_map/ppermute | solution.py:24
  46.2 34.8 %collective-permute-start = (bf16[1,128,1024]{2,1,0:T(8,128)(2,1)S(1)}, bf16[1,128,1024]{2,1,0:T(8,128)(2,1)S(1)}, u32[]{:S(2)}, u32[]{:S(2)}) collective-permute-start(bf16[1,128,1024]{2,1,0:T(8,128)(2,1)S(1)} %bitcast.43), channel_id=1, source_target_pairs={{0,2},{1,3},{2,0},{3,1},{4,6},{5,7},{6,4},{7,5},{8,10},{9,11},{10,... | collective-permute-start | bytes 786440 | tf_op jit(solution)/shard_map/ppermute | solution.py:24
  81.0 7.6 %collective-permute-start.3 = (bf16[1,128,1024]{2,1,0:T(8,128)(2,1)S(1)}, bf16[1,128,1024]{2,1,0:T(8,128)(2,1)S(1)}, u32[]{:S(2)}, u32[]{:S(2)}) collective-permute-start(bf16[1,128,1024]{2,1,0:T(8,128)(2,1)S(1)} %collective-permute-done.2), channel_id=1, source_target_pairs={{0,2},{1,3},{2,0},{3,1},{4,6},{5,7},{6,4},{7,5},{8,10},{9,11},{10,... | collective-permute-start | bytes 786440 | tf_op jit(solution)/shard_map/ppermute | solution.py:24
  81.8 15.2 %collective-permute-start.1 = (bf16[2,128,1024]{2,1,0:T(8,128)(2,1)}, bf16[2,128,1024]{2,1,0:T(8,128)(2,1)}, u32[]{:S(2)}, u32[]{:S(2)}) collective-permute-start(bf16[2,128,1024]{2,1,0:T(8,128)(2,1)} %pad_maximum_fusion), channel_id=1, source_target_pairs={{0,1},{1,0},{2,3},{3,2},{4,5},{5,4},{6,7},{7,6},{8,9},{9,8},{10,11... | collective-permute-start | bytes 1572872 | tf_op jit(solution)/shard_map/ppermute | solution.py:24
  86.0 23.8 %collective-permute-start.8 = (bf16[2,1024,256]{2,1,0:T(8,128)(2,1)}, bf16[2,1024,256]{2,1,0:T(8,128)(2,1)}, u32[]{:S(2)}, u32[]{:S(2)}) collective-permute-start(bf16[2,1024,256]{2,1,0:T(8,128)(2,1)} %maximum_select_fusion.2), channel_id=1, source_target_pairs={{0,8},{8,0},{16,24},{24,16},{1,9},{9,1},{17,25},{25,17},{2,10},{10... | collective-permute-start | bytes 3145736 | tf_op jit(solution)/shard_map/ppermute | solution.py:24
  88.6 3.0 %copy-start.1 = (bf16[1,128,1024]{2,1,0:T(8,128)(2,1)}, bf16[1,128,1024]{2,1,0:T(8,128)(2,1)S(1)}, u32[]{:S(2)}) copy-start(bf16[1,128,1024]{2,1,0:T(8,128)(2,1)S(1)} %collective-permute-done.3) | copy-start | bytes 786436
  89.4 17.1 %collective-permute-start.4 = (bf16[2,128,1024]{2,1,0:T(8,128)(2,1)}, bf16[2,128,1024]{2,1,0:T(8,128)(2,1)}, u32[]{:S(2)}, u32[]{:S(2)}) collective-permute-start(bf16[2,128,1024]{2,1,0:T(8,128)(2,1)} %pad_maximum_fusion.1), channel_id=1, source_target_pairs={{0,1},{1,0},{2,3},{3,2},{4,5},{5,4},{6,7},{7,6},{8,9},{9,8},{10,11... | collective-permute-start | bytes 1572872 | tf_op jit(solution)/shard_map/ppermute | solution.py:24
  91.8 16.6 %copy-start.8 = (bf16[1,1,1024,256]{3,2,0,1:T(8,128)(2,1)S(1)}, bf16[1,1,1024,256]{3,2,0,1:T(8,128)(2,1)}, u32[]{:S(2)}) copy-start(bf16[1,1,1024,256]{3,2,0,1:T(8,128)(2,1)} %get-tuple-element.15) | copy-start | bytes 1572868
  113.2 1.0 copy-start.2
  114.1 0.9 copy-start.3
  115.1 0.9 copy-start.4
  116.0 0.9 copy-start.5
  117.0 0.9 copy-start.6

commit v3 on v2

v3 whole, which is shorter than its diff:
```python
import functools
import math

import jax
import jax.numpy as jnp
from jax import lax
from jax.experimental import pallas as pl
from jax.experimental.pallas import tpu as pltpu
from jax.sharding import PartitionSpec as P

BLOCK = 64


norm_eps = 1e-05
inner_gain = 0.4
outer_rate = 0.7
outer_beta = 0.9
mix_weight = 0.5
code_range = 448.0


def swap(value, axis, mask):
    size = lax.axis_size(axis)
    return lax.ppermute(value, axis, [(i, i ^ mask) for i in range(size)])


def prepare_kernel(tokens_ref, cotangent_ref, blocks_ref, scaled_ref):
    shards, _, rows = blocks_ref.shape
    squares = None
    for k in range(shards):
        block = tokens_ref[:, k * rows : (k + 1) * rows]
        blocks_ref[k] = block
        block = block.astype(jnp.float32)
        squares = block * block if squares is None else squares + block * block
    mean = jnp.sum(squares, axis=-1, keepdims=True) / (shards * rows)
    scaled_ref[...] = (cotangent_ref[...].astype(jnp.float32) * lax.rsqrt(mean + norm_eps)).astype(jnp.bfloat16)


def prepare(tokens, cotangent, shards):
    count, features = tokens.shape
    width = cotangent.shape[1]
    rows = features // shards
    tile = min(count, 32)
    return pl.pallas_call(
        prepare_kernel,
        out_shape=(
            jax.ShapeDtypeStruct((shards, count, rows), jnp.bfloat16),
            jax.ShapeDtypeStruct((count, width), jnp.bfloat16),
        ),
        grid=(count // tile,),
        in_specs=[
            pl.BlockSpec((tile, features), lambda i: (i, 0)),
            pl.BlockSpec((tile, width), lambda i: (i, 0)),
        ],
        out_specs=(
            pl.BlockSpec((shards, tile, rows), lambda i: (0, i, 0)),
            pl.BlockSpec((tile, width), lambda i: (i, 0)),
        ),
        cost_estimate=pl.CostEstimate(
            flops=3 * count * features, bytes_accessed=4 * count * (features + width), transcendentals=count
        ),
        name="prepare",
    )(tokens, cotangent)


def code_kernel(own_ref, shared_ref, weight_ref, kept_ref, sent_ref, decoded_ref):
    lanes = 2 * BLOCK
    groups, rows, share = decoded_ref.shape
    low = lax.broadcasted_iota(jnp.int32, (rows, lanes), 1) < BLOCK
    for start in range(0, groups * share, lanes):
        columns = slice(start, start + lanes)
        delta = shared_ref[:, columns].astype(jnp.float32) - weight_ref[:, columns].astype(jnp.float32)
        size = jnp.abs(delta)
        largest = jnp.where(
            low,
            jnp.max(jnp.where(low, size, 0.0), axis=-1, keepdims=True),
            jnp.max(jnp.where(low, 0.0, size), axis=-1, keepdims=True),
        )
        scale = ((largest + 1e-06) * (1.0 / code_range)).astype(jnp.bfloat16).astype(jnp.float32)
        coded = (delta / scale).astype(jnp.bfloat16)
        decoded = (coded.astype(jnp.float32) * scale).astype(jnp.bfloat16)
        piece = min(share, lanes)
        for at in range(0, lanes, piece):
            group, offset = divmod(start + at, share)
            decoded_ref[group, :, offset : offset + piece] = decoded[:, at : at + piece]
    own = own_ref[0]
    for k in range(0, groups, 2):
        kept_ref[k // 2] = decoded_ref[own ^ k]
        sent_ref[k // 2] = decoded_ref[own ^ (k + 1)]


def code_and_decode(own, shared, weight, groups):
    rows, width = shared.shape
    tile = min(rows, 128)
    share = width // groups
    spec = pl.BlockSpec((tile, width), lambda i, own: (i, 0))
    half = jax.ShapeDtypeStruct((groups // 2, rows, share), jnp.bfloat16)
    half_spec = pl.BlockSpec((groups // 2, tile, share), lambda i, own: (0, i, 0))
    return pl.pallas_call(
        code_kernel,
        out_shape=(half, half),
        grid_spec=pltpu.PrefetchScalarGridSpec(
            num_scalar_prefetch=1,
            grid=(rows // tile,),
            in_specs=[spec, spec],
            out_specs=(half_spec, half_spec),
            scratch_shapes=[pltpu.VMEM((groups, tile, share), jnp.bfloat16)],
        ),
        cost_estimate=pl.CostEstimate(flops=20 * rows * width, bytes_accessed=6 * rows * width, transcendentals=0),
        name="code_and_decode",
    )(own.reshape(1), shared, weight)


def mix_kernel(parts, groups, place_ref, *refs):
    tokens, refs = refs[:parts], refs[parts:]
    cotangents, refs = refs[:parts], refs[parts:]
    pieces, refs = refs[:groups], refs[groups:]
    gain_ref, weight_ref, out_ref, shared_ref = refs
    total = None
    pair = 2 if parts % 2 == 0 else 1
    for first in range(0, parts, pair):
        product = lax.dot_general(
            jnp.concatenate([ref[0] for ref in tokens[first : first + pair]], axis=0),
            jnp.concatenate([ref[...] for ref in cotangents[first : first + pair]], axis=0),
            (((0,), (0,)), ((), ())),
            preferred_element_type=jnp.float32,
        )
        total = product if total is None else total + product
    own = place_ref[1]
    for k, piece in enumerate(pieces):
        shared_ref[own ^ k] = piece[...]
    share = shared_ref.shape[2]
    for group in range(groups):
        columns = slice(group * share, (group + 1) * share)
        weight = weight_ref[:, columns].astype(jnp.float32) + shared_ref[group].astype(jnp.float32)
        out_ref[:, columns] = (mix_weight * weight - gain_ref[...] * total[:, columns]).astype(jnp.bfloat16)


def mix(mine, own, tokens, cotangents, pieces, gain, weight):
    parts, depth, rows = tokens.shape
    width = weight.shape[1]
    groups = len(pieces)
    share = width // groups
    tile = min(rows, 256)

    def token_block(k):
        return pl.BlockSpec((1, depth, tile), lambda i, place: (place[0] ^ k, 0, i))

    by_row = pl.BlockSpec((tile, width), lambda i, place: (i, 0))
    return pl.pallas_call(
        functools.partial(mix_kernel, parts, groups),
        out_shape=jax.ShapeDtypeStruct((rows, width), jnp.bfloat16),
        grid_spec=pltpu.PrefetchScalarGridSpec(
            num_scalar_prefetch=1,
            grid=(rows // tile,),
            in_specs=[token_block(k) for k in range(parts)]
            + [pl.BlockSpec((depth, width), lambda i, place: (0, 0))] * parts
            + [pl.BlockSpec((tile, share), lambda i, place: (i, 0))] * groups
            + [pl.BlockSpec((tile, 1), lambda i, place: (i, 0)), by_row],
            out_specs=by_row,
            scratch_shapes=[pltpu.VMEM((groups, tile, share), jnp.bfloat16)],
        ),
        compiler_params=pltpu.CompilerParams(vmem_limit_bytes=48 * 2**20),
        cost_estimate=pl.CostEstimate(
            flops=2 * parts * depth * rows * width,
            bytes_accessed=2 * parts * depth * (rows + width) + 6 * rows * width,
            transcendentals=0,
        ),
        name="mix",
    )(jnp.stack([mine, own]), *([tokens] * parts), *cotangents, *pieces, gain, weight)


def gather(piece, axis):
    size = lax.axis_size(axis)
    pieces = {0: piece}
    bit = size // 2
    while bit:
        for k in sorted(pieces):
            pieces[k ^ bit] = swap(pieces[k], axis, bit)
        bit //= 2
    return [pieces[k] for k in range(size)]


def on_device(tokens, norm_gain, cotangent, layer_weight, shared_copy, master, momentum):
    tokens, cotangent, weight = tokens[0], cotangent[0], layer_weight[0]
    shards = lax.axis_size("fsdp")
    groups = lax.axis_size("replica")
    mine = lax.axis_index("fsdp")
    own = lax.axis_index("replica")
    rows, width = weight.shape
    inner_rate = inner_gain / math.sqrt(tokens.shape[0] * shards)

    blocks, scaled = prepare(tokens, cotangent, shards)
    cotangents = gather(scaled, "fsdp")
    columns = lax.all_to_all(blocks, "fsdp", split_axis=0, concat_axis=0, tiled=True)

    _, coded_weight, coded_shared = lax.optimization_barrier((cotangents[shards // 2], weight, shared_copy))
    kept, sent = code_and_decode(own, coded_shared, coded_weight, groups)
    total = kept.astype(jnp.float32) + swap(sent, "replica", 1).astype(jnp.float32)
    bit = 2
    while bit < groups:
        sent = swap(total[1::2].astype(jnp.bfloat16), "replica", bit)
        total = total[0::2] + sent.astype(jnp.float32)
        bit *= 2
    average = total[0] / groups
    momentum_next = outer_beta * momentum + average
    master_next = master - outer_rate * (average + outer_beta * momentum_next)
    pieces = gather(master_next.astype(jnp.bfloat16), "replica")

    gain = lax.dynamic_slice_in_dim(norm_gain, mine * rows, rows).astype(jnp.float32)
    gain = (gain * ((1.0 - mix_weight) * inner_rate)).reshape(rows, 1)
    layer_next = mix(mine, own, columns, cotangents, pieces, gain, weight)
    return (layer_next[None], master_next, momentum_next)


def solution(mesh):
    in_specs = (
        P("replica", "fsdp", None),
        P(),
        P("replica", "fsdp", None),
        P("replica", "fsdp", None),
        P("fsdp", None),
        P("fsdp", "replica"),
        P("fsdp", "replica"),
    )
    out_specs = (P("replica", "fsdp", None), P("fsdp", "replica"), P("fsdp", "replica"))
    return jax.shard_map(
        on_device, mesh=mesh, in_specs=in_specs, out_specs=out_specs, check_vma=False
    )
```

time: 125 us -> 141 us (1.13)
  waiting for transfers between devices: 61.6 us -> 94.9 us
  local copies, waits for them, and re-layouts: 12.3 us -> 1.92 us
  other arithmetic: 14.4 us -> 4.06 us
  starting transfers between devices: 17.4 us -> 20.4 us
    ppermute x9 -> x12, waiting for transfers between devices: 61.6 us -> 94.9 us  [swap(): return lax.ppermute(value, axis, [(i, i ^ mask) for i in range(size)])]
    select_n x3 -> x0, other arithmetic: 6.01 us -> none  [on_device(): jnp.where(side == 0, jnp.stack([gathered, other], axis=1), jnp.stack([oth...]
    another operation x3 -> x1, other arithmetic: 4.93 us -> 0.08 us  [mix(): jnp.stack([mine, own])]
    squeeze x3 -> x0, local copies, waits for them, and re-layouts: 4.53 us -> none  [the longest x2 3.7 us: on_device(): cotangents[k ^ bit] = arrived[place]]
    unnamed x18 -> x10, local copies, waits for them, and re-layouts: 4.76 us -> 1.64 us
    ppermute x9 -> x12, starting transfers between devices: 10.5 us -> 13 us  [swap(): return lax.ppermute(value, axis, [(i, i ^ mask) for i in range(size)])]
    add x0 -> x1, other arithmetic: none -> 1.64 us  [on_device(): kept.astype(jnp.float32) + swap(sent, 'replica', 1).astype(jnp.float32)]
    select_n x1 -> x0, local copies, waits for them, and re-layouts: 1.46 us -> none  [on_device(): jnp.where(side == 0, jnp.stack([gathered, other], axis=1), jnp.stack([oth...]
  transfers between devices with their start and end apart: 10 -> 13, of which waited for: 5 -> 7; matrix products, arithmetic and copies ran while one was open for 17% -> 3% of each run, Pallas kernels for 0% -> 5%
where the time goes in v3:
time: 141 us
  waiting for transfers between devices  94.9 us (67%)
  starting transfers between devices  20.4 us (14%)
  Pallas kernels  18.6 us (13%)
  other arithmetic  4.06 us (3%)
  local copies, waits for them, and re-layouts  1.92 us (1%)
    ppermute x12, waiting for transfers between devices, swap(): return lax.ppermute(value, axis, [(i, i ^ mask) for i in range(size)])  94.9 us
    ppermute x12, starting transfers between devices, swap(): return lax.ppermute(value, axis, [(i, i ^ mask) for i in range(size)])  13 us
    pallas_call x1, Pallas kernels, code_and_decode(): pl.pallas_call(code_kernel, out_shape=(half, half), grid_spec=pltpu.Prefe...  7.45 us
    all_to_all x1, starting transfers between devices, on_device(): lax.all_to_all(blocks, 'fsdp', split_axis=0, concat_axis=0, tiled=True)  7.41 us
    pallas_call x1, Pallas kernels, mix(): pl.pallas_call(functools.partial(mix_kernel, parts, groups), out_shape=ja...  7.04 us
    pallas_call x1, Pallas kernels, prepare(): pl.pallas_call(prepare_kernel, out_shape=(jax.ShapeDtypeStruct((shards, c...  4.14 us
  transfers between devices with their start and end apart: 13, of which 7 were waited for; matrix products, arithmetic and copies ran while one was open for 3% of the time, Pallas kernels for 5%

profile of v3, /device:TPU:0, one launch (start us, length us, event | category | flops | bytes accessed | tf_op | source)
XLA Modules:
  0.0 140.6 jit_solution(13098969815622223257)
XLA Ops:
  0.6 4.1 %prepare.1 = (bf16[8,128,1024]{2,1,0:T(8,128)(2,1)}, bf16[128,1024]{1,0:T(8,128)(2,1)}) custom-call(bf16[128,8192]{1,0:T(8,128)(2,1)} %bitcast.17, bf16[128,1024]{1,0:T(8,128)(2,1)} %bitcast.19), custom_call_target="tpu_custom_call" | custom-call | flops 3145728 | bytes 4718592 | tf_op jit(solution)/shard_map/prepare/pallas_call | solution.py:44
  4.8 7.4 %all-to-all-start = ((bf16[8,128,1024]{2,1,0:T(8,128)(2,1)}), bf16[8,128,1024]{2,1,0:T(8,128)(2,1)}, u32[]{:S(2)}, u32[]{:S(2)}) async-start(bf16[8,128,1024]{2,1,0:T(8,128)(2,1)} %get-tuple-element.9), calls=%async_computation | async-start | bytes 4194304 | tf_op jit(solution)/shard_map/all_to_all | solution.py:195
  12.2 2.9 %collective-permute-start.3 = (bf16[128,1024]{1,0:T(8,128)(2,1)S(1)}, bf16[128,1024]{1,0:T(8,128)(2,1)S(1)}, u32[]{:S(2)}, u32[]{:S(2)}) collective-permute-start(bf16[128,1024]{1,0:T(8,128)(2,1)S(1)} %copy-done), channel_id=1, source_target_pairs={{0,4},{1,5},{2,6},{3,7},{4,0},{5,1},{6,2},{7,3},{8,12},{9,13},{10,... | collective-permute-start | bytes 786440 | tf_op jit(solution)/shard_map/ppermute | solution.py:24
  15.1 56.5 %collective-permute-done.3.refs_12_ = bf16[128,1024]{1,0:T(8,128)(2,1)S(1)} collective-permute-done((bf16[128,1024]{1,0:T(8,128)(2,1)S(1)}, bf16[128,1024]{1,0:T(8,128)(2,1)S(1)}, u32[]{:S(2)}, u32[]{:S(2)}) %collective-permute-start.3) | collective-permute-done | bytes 262176 | tf_op jit(solution)/shard_map/ppermute | solution.py:24
  71.7 7.5 %code_and_decode.1 = (bf16[2,1024,256]{2,1,0:T(8,128)(2,1)}, bf16[2,1024,256]{2,1,0:T(8,128)(2,1)}) custom-call(s32[1]{0:T(128)} %bitcast.1.own_ref, bf16[1024,1024]{1,0:T(8,128)(2,1)} %shared_ref, bf16[1024,1024]{1,0:T(8,128)(2,1)} %bitcast.15), custom_call_target="tpu_custom_call" | custom-call | flops 20971520 | bytes 6291456 | tf_op jit(solution)/shard_map/code_and_decode/pallas_call | solution.py:99
  79.1 0.0 collective-permute-start.7
  79.1 2.9 %collective-permute-done.7 = bf16[2,1024,256]{2,1,0:T(8,128)(2,1)S(1)} collective-permute-done((bf16[2,1024,256]{2,1,0:T(8,128)(2,1)}, bf16[2,1024,256]{2,1,0:T(8,128)(2,1)S(1)}, u32[]{:S(2)}, u32[]{:S(2)}) %collective-permute-start.7) | collective-permute-done | bytes 1048608 | tf_op jit(solution)/shard_map/ppermute | solution.py:24
  82.0 1.6 %convert_add_fusion = f32[2,1024,256]{2,1,0:T(8,128)S(1)} fusion(bf16[2,1024,256]{2,1,0:T(8,128)(2,1)S(1)} %collective-permute-done.7, bf16[2,1024,256]{2,1,0:T(8,128)(2,1)} %get-tuple-element.13), kind=kLoop, calls=%fused_computation | loop fusion | flops 1572864 | bytes 4194304 | tf_op jit(solution)/shard_map/add | solution.py:199
  83.6 0.1 slice.23
  83.7 1.6 %collective-permute-start.8 = (bf16[1,1024,256]{2,1,0:T(8,128)(2,1)S(1)}, bf16[1,1024,256]{2,1,0:T(8,128)(2,1)S(1)}, u32[]{:S(2)}, u32[]{:S(2)}) collective-permute-start(bf16[1,1024,256]{2,1,0:T(8,128)(2,1)S(1)} %slice.23), channel_id=1, source_target_pairs={{0,16},{8,24},{16,0},{24,8},{1,17},{9,25},{17,1},{25,9},{2,18},{10... | collective-permute-start | bytes 1572872 | tf_op jit(solution)/shard_map/ppermute | solution.py:24
  85.2 12.5 %collective-permute-done.8 = bf16[1,1024,256]{2,1,0:T(8,128)(2,1)S(1)} collective-permute-done((bf16[1,1024,256]{2,1,0:T(8,128)(2,1)S(1)}, bf16[1,1024,256]{2,1,0:T(8,128)(2,1)S(1)}, u32[]{:S(2)}, u32[]{:S(2)}) %collective-permute-start.8) | collective-permute-done | bytes 524320 | tf_op jit(solution)/shard_map/ppermute | solution.py:24
  97.7 1.7 %fusion.2 = (bf16[1024,256]{1,0:T(8,128)(2,1)S(1)}, f32[1024,256]{1,0:T(8,128)}, f32[1024,256]{1,0:T(8,128)}) fusion(f32[1024,256]{1,0:T(8,128)S(1)} %copy-done.3, bf16[1,1024,256]{2,1,0:T(8,128)(2,1)S(1)} %collective-permute-done.8, f32[2,1024,256]{2,1,0:T(8,128)S(1)} %convert_add_fusion, f32[1024,256]{1,0:T(8,128)S(1)} %copy-done.4), kind=kLoop, calls=%fused_computation.9 | loop fusion | flops 2621440 | bytes 6291456 | tf_op jit(solution)/shard_map/convert_element_type | solution.py:208
  99.4 1.5 %collective-permute-start.10 = (bf16[1024,256]{1,0:T(8,128)(2,1)S(1)}, bf16[1024,256]{1,0:T(8,128)(2,1)S(1)}, u32[]{:S(2)}, u32[]{:S(2)}) collective-permute-start(bf16[1024,256]{1,0:T(8,128)(2,1)S(1)} %get-tuple-element.15.refs_16_), channel_id=1, source_target_pairs={{0,16},{8,24},{16,0},{24,8},{1,17},{9,25},{17,1},{25,9},{2,18},{10... | collective-permute-start | bytes 1572872 | tf_op jit(solution)/shard_map/ppermute | solution.py:24
  100.9 0.0 collective-permute-start.1
  100.9 1.5 %collective-permute-start = (bf16[128,1024]{1,0:T(8,128)(2,1)S(1)}, bf16[128,1024]{1,0:T(8,128)(2,1)S(1)}, u32[]{:S(2)}, u32[]{:S(2)}) collective-permute-start(bf16[128,1024]{1,0:T(8,128)(2,1)S(1)} %copy-done), channel_id=1, source_target_pairs={{0,1},{1,0},{2,3},{3,2},{4,5},{5,4},{6,7},{7,6},{8,9},{9,8},{10,11... | collective-permute-start | bytes 786440 | tf_op jit(solution)/shard_map/ppermute | solution.py:24
  102.3 2.0 %collective-permute-start.5 = (bf16[128,1024]{1,0:T(8,128)(2,1)S(1)}, bf16[128,1024]{1,0:T(8,128)(2,1)}, u32[]{:S(2)}, u32[]{:S(2)}) collective-permute-start(bf16[128,1024]{1,0:T(8,128)(2,1)S(1)} %collective-permute-done.3.refs_12_), channel_id=1, source_target_pairs={{0,2},{1,3},{2,0},{3,1},{4,6},{5,7},{6,4},{7,5},{8,10},{9,11},{10,... | collective-permute-start | bytes 786440 | tf_op jit(solution)/shard_map/ppermute | solution.py:24
  104.4 8.2 %collective-permute-done.10.refs_18_ = bf16[1024,256]{1,0:T(8,128)(2,1)S(1)} collective-permute-done((bf16[1024,256]{1,0:T(8,128)(2,1)S(1)}, bf16[1024,256]{1,0:T(8,128)(2,1)S(1)}, u32[]{:S(2)}, u32[]{:S(2)}) %collective-permute-start.10) | collective-permute-done | bytes 524320 | tf_op jit(solution)/shard_map/ppermute | solution.py:24
  112.5 0.0 collective-permute-start.11
  112.5 1.5 %collective-permute-start.4 = (bf16[128,1024]{1,0:T(8,128)(2,1)S(1)}, bf16[128,1024]{1,0:T(8,128)(2,1)}, u32[]{:S(2)}, u32[]{:S(2)}) collective-permute-start(bf16[128,1024]{1,0:T(8,128)(2,1)S(1)} %collective-permute-done.3.refs_12_), channel_id=1, source_target_pairs={{0,1},{1,0},{2,3},{3,2},{4,5},{5,4},{6,7},{7,6},{8,9},{9,8},{10,11... | collective-permute-start | bytes 786440 | tf_op jit(solution)/shard_map/ppermute | solution.py:24
  114.0 0.0 collective-permute-done.refs_9_
  114.0 0.7 copy-done.1
  114.7 0.6 collective-permute-start.2
  115.2 0.0 collective-permute-done.5.refs_14_
  115.3 1.5 %collective-permute-start.6 = (bf16[128,1024]{1,0:T(8,128)(2,1)}, bf16[128,1024]{1,0:T(8,128)(2,1)}, u32[]{:S(2)}, u32[]{:S(2)}) collective-permute-start(bf16[128,1024]{1,0:T(8,128)(2,1)} %collective-permute-done.5.refs_14_), channel_id=1, source_target_pairs={{0,1},{1,0},{2,3},{3,2},{4,5},{5,4},{6,7},{7,6},{8,9},{9,8},{10,11... | collective-permute-start | bytes 786440 | tf_op jit(solution)/shard_map/ppermute | solution.py:24
  116.7 0.7 convert_multiply_fusion
  117.4 0.2 copy.10.refs_20_
  117.6 0.1 pad_add_fusion.place_ref
  117.7 4.0 %collective-permute-done.4.refs_13_ = bf16[128,1024]{1,0:T(8,128)(2,1)} collective-permute-done((bf16[128,1024]{1,0:T(8,128)(2,1)S(1)}, bf16[128,1024]{1,0:T(8,128)(2,1)}, u32[]{:S(2)}, u32[]{:S(2)}) %collective-permute-start.4) | collective-permute-done | bytes 262176 | tf_op jit(solution)/shard_map/ppermute | solution.py:24
  121.7 5.6 %collective-permute-done.2.refs_11_ = bf16[128,1024]{1,0:T(8,128)(2,1)} collective-permute-done((bf16[128,1024]{1,0:T(8,128)(2,1)S(1)}, bf16[128,1024]{1,0:T(8,128)(2,1)}, u32[]{:S(2)}, u32[]{:S(2)}) %collective-permute-start.2) | collective-permute-done | bytes 262176 | tf_op jit(solution)/shard_map/ppermute | solution.py:24
  127.4 5.2 %collective-permute-done.6.refs_15_ = bf16[128,1024]{1,0:T(8,128)(2,1)} collective-permute-done((bf16[128,1024]{1,0:T(8,128)(2,1)}, bf16[128,1024]{1,0:T(8,128)(2,1)}, u32[]{:S(2)}, u32[]{:S(2)}) %collective-permute-start.6) | collective-permute-done | bytes 262176 | tf_op jit(solution)/shard_map/ppermute | solution.py:24
  132.6 0.9 copy-done.2
  133.6 7.0 %mix.1 = bf16[1024,1024]{1,0:T(8,128)(2,1)} custom-call(s32[2]{0:T(128)S(1)} %pad_add_fusion.place_ref, bf16[8,128,1024]{2,1,0:T(8,128)(2,1)} %all-to-all-done.refs_0_.refs_1_.refs_2_.refs_3_.refs_4_.refs_5_.refs_6_.refs_7_, bf16[8,128,1024]{2,1,0:T(8,128)(2,1)} %all-to-all-done.refs_0_.refs_1_.refs_2_.refs_3_.refs_4_.refs_5_.refs_6_.refs_7_, ...), custom_call_target="tpu_custom_call" | custom-call | flops 2147483648 | bytes 10485760 | tf_op jit(solution)/shard_map/mix/pallas_call | solution.py:150
  (13 shorter events, 0.0 us)
Async XLA Ops:
  4.8 7.4 %copy-start = (bf16[128,1024]{1,0:T(8,128)(2,1)S(1)}, bf16[128,1024]{1,0:T(8,128)(2,1)}, u32[]{:S(2)}) copy-start(bf16[128,1024]{1,0:T(8,128)(2,1)} %get-tuple-element.10.refs_8_) | copy-start | bytes 786436
  4.8 127.8 %all-to-all-start = ((bf16[8,128,1024]{2,1,0:T(8,128)(2,1)}), bf16[8,128,1024]{2,1,0:T(8,128)(2,1)}, u32[]{:S(2)}, u32[]{:S(2)}) async-start(bf16[8,128,1024]{2,1,0:T(8,128)(2,1)} %get-tuple-element.9), calls=%async_computation | async-start | bytes 4194304 | tf_op jit(solution)/shard_map/all_to_all | solution.py:195
  12.2 59.5 %collective-permute-start.3 = (bf16[128,1024]{1,0:T(8,128)(2,1)S(1)}, bf16[128,1024]{1,0:T(8,128)(2,1)S(1)}, u32[]{:S(2)}, u32[]{:S(2)}) collective-permute-start(bf16[128,1024]{1,0:T(8,128)(2,1)S(1)} %copy-done), channel_id=1, source_target_pairs={{0,4},{1,5},{2,6},{3,7},{4,0},{5,1},{6,2},{7,3},{8,12},{9,13},{10,... | collective-permute-start | bytes 786440 | tf_op jit(solution)/shard_map/ppermute | solution.py:24
  79.1 2.9 %collective-permute-start.7 = (bf16[2,1024,256]{2,1,0:T(8,128)(2,1)}, bf16[2,1024,256]{2,1,0:T(8,128)(2,1)S(1)}, u32[]{:S(2)}, u32[]{:S(2)}) collective-permute-start(bf16[2,1024,256]{2,1,0:T(8,128)(2,1)} %get-tuple-element.14), channel_id=1, source_target_pairs={{0,8},{8,0},{16,24},{24,16},{1,9},{9,1},{17,25},{25,17},{2,10},{10... | collective-permute-start | bytes 3145736 | tf_op jit(solution)/shard_map/ppermute | solution.py:24
  82.0 15.7 %copy-start.3 = (f32[1024,256]{1,0:T(8,128)S(1)}, f32[1024,256]{1,0:T(8,128)}, u32[]{:S(2)}) copy-start(f32[1024,256]{1,0:T(8,128)} %param.12) | copy-start | bytes 3145732
  82.0 15.7 %copy-start.4 = (f32[1024,256]{1,0:T(8,128)S(1)}, f32[1024,256]{1,0:T(8,128)}, u32[]{:S(2)}) copy-start(f32[1024,256]{1,0:T(8,128)} %param.13) | copy-start | bytes 3145732
  83.7 14.0 %collective-permute-start.8 = (bf16[1,1024,256]{2,1,0:T(8,128)(2,1)S(1)}, bf16[1,1024,256]{2,1,0:T(8,128)(2,1)S(1)}, u32[]{:S(2)}, u32[]{:S(2)}) collective-permute-start(bf16[1,1024,256]{2,1,0:T(8,128)(2,1)S(1)} %slice.23), channel_id=1, source_target_pairs={{0,16},{8,24},{16,0},{24,8},{1,17},{9,25},{17,1},{25,9},{2,18},{10... | collective-permute-start | bytes 1572872 | tf_op jit(solution)/shard_map/ppermute | solution.py:24
  99.4 13.1 %collective-permute-start.10 = (bf16[1024,256]{1,0:T(8,128)(2,1)S(1)}, bf16[1024,256]{1,0:T(8,128)(2,1)S(1)}, u32[]{:S(2)}, u32[]{:S(2)}) collective-permute-start(bf16[1024,256]{1,0:T(8,128)(2,1)S(1)} %get-tuple-element.15.refs_16_), channel_id=1, source_target_pairs={{0,16},{8,24},{16,0},{24,8},{1,17},{9,25},{17,1},{25,9},{2,18},{10... | collective-permute-start | bytes 1572872 | tf_op jit(solution)/shard_map/ppermute | solution.py:24
  100.9 11.7 %collective-permute-start.1 = (bf16[128,1024]{1,0:T(8,128)(2,1)S(1)}, bf16[128,1024]{1,0:T(8,128)(2,1)S(1)}, u32[]{:S(2)}, u32[]{:S(2)}) collective-permute-start(bf16[128,1024]{1,0:T(8,128)(2,1)S(1)} %copy-done), channel_id=1, source_target_pairs={{0,2},{1,3},{2,0},{3,1},{4,6},{5,7},{6,4},{7,5},{8,10},{9,11},{10,... | collective-permute-start | bytes 786440 | tf_op jit(solution)/shard_map/ppermute | solution.py:24
  100.9 13.1 %collective-permute-start = (bf16[128,1024]{1,0:T(8,128)(2,1)S(1)}, bf16[128,1024]{1,0:T(8,128)(2,1)S(1)}, u32[]{:S(2)}, u32[]{:S(2)}) collective-permute-start(bf16[128,1024]{1,0:T(8,128)(2,1)S(1)} %copy-done), channel_id=1, source_target_pairs={{0,1},{1,0},{2,3},{3,2},{4,5},{5,4},{6,7},{7,6},{8,9},{9,8},{10,11... | collective-permute-start | bytes 786440 | tf_op jit(solution)/shard_map/ppermute | solution.py:24
  102.3 12.9 %collective-permute-start.5 = (bf16[128,1024]{1,0:T(8,128)(2,1)S(1)}, bf16[128,1024]{1,0:T(8,128)(2,1)}, u32[]{:S(2)}, u32[]{:S(2)}) collective-permute-start(bf16[128,1024]{1,0:T(8,128)(2,1)S(1)} %collective-permute-done.3.refs_12_), channel_id=1, source_target_pairs={{0,2},{1,3},{2,0},{3,1},{4,6},{5,7},{6,4},{7,5},{8,10},{9,11},{10,... | collective-permute-start | bytes 786440 | tf_op jit(solution)/shard_map/ppermute | solution.py:24
  104.4 28.2 %collective-permute-start.9 = (bf16[1024,256]{1,0:T(8,128)(2,1)S(1)}, bf16[1024,256]{1,0:T(8,128)(2,1)S(1)}, u32[]{:S(2)}, u32[]{:S(2)}) collective-permute-start(bf16[1024,256]{1,0:T(8,128)(2,1)S(1)} %get-tuple-element.15.refs_16_), channel_id=1, source_target_pairs={{0,8},{8,0},{16,24},{24,16},{1,9},{9,1},{17,25},{25,17},{2,10},{10... | collective-permute-start | bytes 1572872 | tf_op jit(solution)/shard_map/ppermute | solution.py:24
  112.5 20.1 %collective-permute-start.11 = (bf16[1024,256]{1,0:T(8,128)(2,1)S(1)}, bf16[1024,256]{1,0:T(8,128)(2,1)S(1)}, u32[]{:S(2)}, u32[]{:S(2)}) collective-permute-start(bf16[1024,256]{1,0:T(8,128)(2,1)S(1)} %collective-permute-done.10.refs_18_), channel_id=1, source_target_pairs={{0,8},{8,0},{16,24},{24,16},{1,9},{9,1},{17,25},{25,17},{2,10},{10... | collective-permute-start | bytes 1572872 | tf_op jit(solution)/shard_map/ppermute | solution.py:24
  112.5 9.2 %collective-permute-start.4 = (bf16[128,1024]{1,0:T(8,128)(2,1)S(1)}, bf16[128,1024]{1,0:T(8,128)(2,1)}, u32[]{:S(2)}, u32[]{:S(2)}) collective-permute-start(bf16[128,1024]{1,0:T(8,128)(2,1)S(1)} %collective-permute-done.3.refs_12_), channel_id=1, source_target_pairs={{0,1},{1,0},{2,3},{3,2},{4,5},{5,4},{6,7},{7,6},{8,9},{9,8},{10,11... | collective-permute-start | bytes 786440 | tf_op jit(solution)/shard_map/ppermute | solution.py:24
  114.0 0.7 copy-start.1
  114.7 12.7 %collective-permute-start.2 = (bf16[128,1024]{1,0:T(8,128)(2,1)S(1)}, bf16[128,1024]{1,0:T(8,128)(2,1)}, u32[]{:S(2)}, u32[]{:S(2)}) collective-permute-start(bf16[128,1024]{1,0:T(8,128)(2,1)S(1)} %collective-permute-done.1.refs_10_), channel_id=1, source_target_pairs={{0,1},{1,0},{2,3},{3,2},{4,5},{5,4},{6,7},{7,6},{8,9},{9,8},{10,11... | collective-permute-start | bytes 786440 | tf_op jit(solution)/shard_map/ppermute | solution.py:24
  115.3 17.3 %collective-permute-start.6 = (bf16[128,1024]{1,0:T(8,128)(2,1)}, bf16[128,1024]{1,0:T(8,128)(2,1)}, u32[]{:S(2)}, u32[]{:S(2)}) collective-permute-start(bf16[128,1024]{1,0:T(8,128)(2,1)} %collective-permute-done.5.refs_14_), channel_id=1, source_target_pairs={{0,1},{1,0},{2,3},{3,2},{4,5},{5,4},{6,7},{7,6},{8,9},{9,8},{10,11... | collective-permute-start | bytes 786440 | tf_op jit(solution)/shard_map/ppermute | solution.py:24
  132.6 1.0 copy-start.2

commit v4 on v3

--- a/solution.py
+++ b/solution.py
@@ -192,9 +192,10 @@
 
     blocks, scaled = prepare(tokens, cotangent, shards)
     cotangents = gather(scaled, "fsdp")
+    first = [cotangents[1 << bit] for bit in range(shards.bit_length() - 1)]
+    *_, blocks, coded_weight, coded_shared = lax.optimization_barrier((*first, blocks, weight, shared_copy))
     columns = lax.all_to_all(blocks, "fsdp", split_axis=0, concat_axis=0, tiled=True)
 
-    _, coded_weight, coded_shared = lax.optimization_barrier((cotangents[shards // 2], weight, shared_copy))
     kept, sent = code_and_decode(own, coded_shared, coded_weight, groups)
     total = kept.astype(jnp.float32) + swap(sent, "replica", 1).astype(jnp.float32)
     bit = 2

time: 141 us -> 97.2 us (0.69)
  waiting for transfers between devices: 94.9 us -> 49.7 us
    ppermute x12, waiting for transfers between devices: 94.9 us -> 49.7 us  [swap(): return lax.ppermute(value, axis, [(i, i ^ mask) for i in range(size)])]
    ppermute x12, starting transfers between devices: 13 us -> 16.1 us  [swap(): return lax.ppermute(value, axis, [(i, i ^ mask) for i in range(size)])]
    all_to_all x1, starting transfers between devices: 7.41 us -> 5.48 us  [on_device(): lax.all_to_all(blocks, 'fsdp', split_axis=0, concat_axis=0, tiled=True)]
  transfers between devices with their start and end apart: 13 -> 13, of which waited for: 7 -> 8; matrix products, arithmetic and copies ran while one was open for 3% -> 4% of each run, Pallas kernels for 5% -> 8%
where the time goes in v4:
time: 97.2 us; the launch traced here: 96.6 us
  waiting for transfers between devices  49.7 us (51%)
  starting transfers between devices  21.6 us (22%)
  Pallas kernels  18.6 us (19%)
  other arithmetic  4.06 us (4%)
  local copies, waits for them, and re-layouts  1.93 us (2%)
    ppermute x12, waiting for transfers between devices, swap(): return lax.ppermute(value, axis, [(i, i ^ mask) for i in range(size)])  49.7 us
    ppermute x12, starting transfers between devices, swap(): return lax.ppermute(value, axis, [(i, i ^ mask) for i in range(size)])  16.1 us
    pallas_call x1, Pallas kernels, code_and_decode(): pl.pallas_call(code_kernel, out_shape=(half, half), grid_spec=pltpu.Prefe...  7.46 us
    pallas_call x1, Pallas kernels, mix(): pl.pallas_call(functools.partial(mix_kernel, parts, groups), out_shape=ja...  7.04 us
    all_to_all x1, starting transfers between devices, on_device(): lax.all_to_all(blocks, 'fsdp', split_axis=0, concat_axis=0, tiled=True)  5.48 us
    pallas_call x1, Pallas kernels, prepare(): pl.pallas_call(prepare_kernel, out_shape=(jax.ShapeDtypeStruct((shards, c...  4.13 us
  transfers between devices with their start and end apart: 13, of which 8 were waited for; matrix products, arithmetic and copies ran while one was open for 4% of the time, Pallas kernels for 8%

profile of v4, /device:TPU:0, one launch (start us, length us, event | category | flops | bytes accessed | tf_op | source)
XLA Modules:
  0.0 96.6 jit_solution(18127171877073566771)
XLA Ops:
  0.6 4.1 %prepare.1 = (bf16[8,128,1024]{2,1,0:T(8,128)(2,1)}, bf16[128,1024]{1,0:T(8,128)(2,1)}) custom-call(bf16[128,8192]{1,0:T(8,128)(2,1)} %bitcast.17, bf16[128,1024]{1,0:T(8,128)(2,1)} %bitcast.19), custom_call_target="tpu_custom_call" | custom-call | flops 3145728 | bytes 4718592 | tf_op jit(solution)/shard_map/prepare/pallas_call | solution.py:44
  4.8 4.0 %collective-permute-start.2 = (bf16[128,1024]{1,0:T(8,128)(2,1)}, bf16[128,1024]{1,0:T(8,128)(2,1)S(1)}, u32[]{:S(2)}, u32[]{:S(2)}) collective-permute-start(bf16[128,1024]{1,0:T(8,128)(2,1)} %get-tuple-element.10.refs_8_), channel_id=1, source_target_pairs={{0,4},{1,5},{2,6},{3,7},{4,0},{5,1},{6,2},{7,3},{8,12},{9,13},{10,... | collective-permute-start | bytes 786440 | tf_op jit(solution)/shard_map/ppermute | solution.py:24
  8.8 1.6 %collective-permute-start.1 = (bf16[128,1024]{1,0:T(8,128)(2,1)}, bf16[128,1024]{1,0:T(8,128)(2,1)S(1)}, u32[]{:S(2)}, u32[]{:S(2)}) collective-permute-start(bf16[128,1024]{1,0:T(8,128)(2,1)} %get-tuple-element.10.refs_8_), channel_id=1, source_target_pairs={{0,2},{1,3},{2,0},{3,1},{4,6},{5,7},{6,4},{7,5},{8,10},{9,11},{10,... | collective-permute-start | bytes 786440 | tf_op jit(solution)/shard_map/ppermute | solution.py:24
  10.4 1.5 %collective-permute-start = (bf16[128,1024]{1,0:T(8,128)(2,1)}, bf16[128,1024]{1,0:T(8,128)(2,1)S(1)}, u32[]{:S(2)}, u32[]{:S(2)}) collective-permute-start(bf16[128,1024]{1,0:T(8,128)(2,1)} %get-tuple-element.10.refs_8_), channel_id=1, source_target_pairs={{0,1},{1,0},{2,3},{3,2},{4,5},{5,4},{6,7},{7,6},{8,9},{9,8},{10,11... | collective-permute-start | bytes 786440 | tf_op jit(solution)/shard_map/ppermute | solution.py:24
  11.9 9.1 %collective-permute-done.2.refs_12_ = bf16[128,1024]{1,0:T(8,128)(2,1)S(1)} collective-permute-done((bf16[128,1024]{1,0:T(8,128)(2,1)}, bf16[128,1024]{1,0:T(8,128)(2,1)S(1)}, u32[]{:S(2)}, u32[]{:S(2)}) %collective-permute-start.2) | collective-permute-done | bytes 262176 | tf_op jit(solution)/shard_map/ppermute | solution.py:24
  21.0 0.2 collective-permute-done.1.refs_10_
  21.2 0.7 copy-done.1
  21.9 5.5 %all-to-all-start = ((bf16[8,128,1024]{2,1,0:T(8,128)(2,1)}), bf16[8,128,1024]{2,1,0:T(8,128)(2,1)}, u32[]{:S(2)}, u32[]{:S(2)}) async-start(bf16[8,128,1024]{2,1,0:T(8,128)(2,1)} %get-tuple-element.12), calls=%async_computation | async-start | bytes 4194304 | tf_op jit(solution)/shard_map/all_to_all | solution.py:197
  27.4 7.5 %code_and_decode.1 = (bf16[2,1024,256]{2,1,0:T(8,128)(2,1)}, bf16[2,1024,256]{2,1,0:T(8,128)(2,1)}) custom-call(s32[1]{0:T(128)} %bitcast.1.own_ref, bf16[1024,1024]{1,0:T(8,128)(2,1)} %shared_ref, bf16[1024,1024]{1,0:T(8,128)(2,1)} %bitcast.15), custom_call_target="tpu_custom_call" | custom-call | flops 20971520 | bytes 6291456 | tf_op jit(solution)/shard_map/code_and_decode/pallas_call | solution.py:99
  34.9 0.0 collective-permute-start.7
  34.9 2.9 %collective-permute-done.7 = bf16[2,1024,256]{2,1,0:T(8,128)(2,1)S(1)} collective-permute-done((bf16[2,1024,256]{2,1,0:T(8,128)(2,1)}, bf16[2,1024,256]{2,1,0:T(8,128)(2,1)S(1)}, u32[]{:S(2)}, u32[]{:S(2)}) %collective-permute-start.7) | collective-permute-done | bytes 1048608 | tf_op jit(solution)/shard_map/ppermute | solution.py:24
  37.7 1.6 %convert_add_fusion = f32[2,1024,256]{2,1,0:T(8,128)S(1)} fusion(bf16[2,1024,256]{2,1,0:T(8,128)(2,1)S(1)} %collective-permute-done.7, bf16[2,1024,256]{2,1,0:T(8,128)(2,1)} %get-tuple-element.15), kind=kLoop, calls=%fused_computation | loop fusion | flops 1572864 | bytes 4194304 | tf_op jit(solution)/shard_map/add | solution.py:200
  39.4 0.1 slice.23
  39.5 1.6 %collective-permute-start.8 = (bf16[1,1024,256]{2,1,0:T(8,128)(2,1)S(1)}, bf16[1,1024,256]{2,1,0:T(8,128)(2,1)S(1)}, u32[]{:S(2)}, u32[]{:S(2)}) collective-permute-start(bf16[1,1024,256]{2,1,0:T(8,128)(2,1)S(1)} %slice.23), channel_id=1, source_target_pairs={{0,16},{8,24},{16,0},{24,8},{1,17},{9,25},{17,1},{25,9},{2,18},{10... | collective-permute-start | bytes 1572872 | tf_op jit(solution)/shard_map/ppermute | solution.py:24
  41.0 12.5 %collective-permute-done.8 = bf16[1,1024,256]{2,1,0:T(8,128)(2,1)S(1)} collective-permute-done((bf16[1,1024,256]{2,1,0:T(8,128)(2,1)S(1)}, bf16[1,1024,256]{2,1,0:T(8,128)(2,1)S(1)}, u32[]{:S(2)}, u32[]{:S(2)}) %collective-permute-start.8) | collective-permute-done | bytes 524320 | tf_op jit(solution)/shard_map/ppermute | solution.py:24
  53.5 1.7 %fusion.2 = (bf16[1024,256]{1,0:T(8,128)(2,1)S(1)}, f32[1024,256]{1,0:T(8,128)}, f32[1024,256]{1,0:T(8,128)}) fusion(f32[1024,256]{1,0:T(8,128)S(1)} %copy-done.3, bf16[1,1024,256]{2,1,0:T(8,128)(2,1)S(1)} %collective-permute-done.8, f32[2,1024,256]{2,1,0:T(8,128)S(1)} %convert_add_fusion, f32[1024,256]{1,0:T(8,128)S(1)} %copy-done.4), kind=kLoop, calls=%fused_computation.9 | loop fusion | flops 2621440 | bytes 6291456 | tf_op jit(solution)/shard_map/convert_element_type | solution.py:209
  55.1 1.5 %collective-permute-start.10 = (bf16[1024,256]{1,0:T(8,128)(2,1)S(1)}, bf16[1024,256]{1,0:T(8,128)(2,1)S(1)}, u32[]{:S(2)}, u32[]{:S(2)}) collective-permute-start(bf16[1024,256]{1,0:T(8,128)(2,1)S(1)} %get-tuple-element.17.refs_16_), channel_id=1, source_target_pairs={{0,16},{8,24},{16,0},{24,8},{1,17},{9,25},{17,1},{25,9},{2,18},{10... | collective-permute-start | bytes 1572872 | tf_op jit(solution)/shard_map/ppermute | solution.py:24
  56.6 2.0 %collective-permute-start.5 = (bf16[128,1024]{1,0:T(8,128)(2,1)S(1)}, bf16[128,1024]{1,0:T(8,128)(2,1)}, u32[]{:S(2)}, u32[]{:S(2)}) collective-permute-start(bf16[128,1024]{1,0:T(8,128)(2,1)S(1)} %collective-permute-done.2.refs_12_), channel_id=1, source_target_pairs={{0,2},{1,3},{2,0},{3,1},{4,6},{5,7},{6,4},{7,5},{8,10},{9,11},{10,... | collective-permute-start | bytes 786440 | tf_op jit(solution)/shard_map/ppermute | solution.py:24
  58.7 9.7 %collective-permute-done.10.refs_18_ = bf16[1024,256]{1,0:T(8,128)(2,1)S(1)} collective-permute-done((bf16[1024,256]{1,0:T(8,128)(2,1)S(1)}, bf16[1024,256]{1,0:T(8,128)(2,1)S(1)}, u32[]{:S(2)}, u32[]{:S(2)}) %collective-permute-start.10) | collective-permute-done | bytes 524320 | tf_op jit(solution)/shard_map/ppermute | solution.py:24
  68.4 0.0 collective-permute-start.11
  68.4 1.9 %collective-permute-start.4 = (bf16[128,1024]{1,0:T(8,128)(2,1)S(1)}, bf16[128,1024]{1,0:T(8,128)(2,1)}, u32[]{:S(2)}, u32[]{:S(2)}) collective-permute-start(bf16[128,1024]{1,0:T(8,128)(2,1)S(1)} %collective-permute-done.2.refs_12_), channel_id=1, source_target_pairs={{0,1},{1,0},{2,3},{3,2},{4,5},{5,4},{6,7},{7,6},{8,9},{9,8},{10,11... | collective-permute-start | bytes 786440 | tf_op jit(solution)/shard_map/ppermute | solution.py:24
  70.3 0.2 collective-permute-start.3
  70.5 1.9 %collective-permute-start.6 = (bf16[128,1024]{1,0:T(8,128)(2,1)}, bf16[128,1024]{1,0:T(8,128)(2,1)}, u32[]{:S(2)}, u32[]{:S(2)}) collective-permute-start(bf16[128,1024]{1,0:T(8,128)(2,1)} %collective-permute-done.5.refs_14_), channel_id=1, source_target_pairs={{0,1},{1,0},{2,3},{3,2},{4,5},{5,4},{6,7},{7,6},{8,9},{9,8},{10,11... | collective-permute-start | bytes 786440 | tf_op jit(solution)/shard_map/ppermute | solution.py:24
  72.3 0.7 convert_multiply_fusion
  73.0 0.2 copy.10.refs_20_
  73.3 0.1 pad_add_fusion.place_ref
  73.3 4.3 %collective-permute-done.4.refs_13_ = bf16[128,1024]{1,0:T(8,128)(2,1)} collective-permute-done((bf16[128,1024]{1,0:T(8,128)(2,1)S(1)}, bf16[128,1024]{1,0:T(8,128)(2,1)}, u32[]{:S(2)}, u32[]{:S(2)}) %collective-permute-start.4) | collective-permute-done | bytes 262176 | tf_op jit(solution)/shard_map/ppermute | solution.py:24
  77.7 5.6 %collective-permute-done.3.refs_11_ = bf16[128,1024]{1,0:T(8,128)(2,1)} collective-permute-done((bf16[128,1024]{1,0:T(8,128)(2,1)S(1)}, bf16[128,1024]{1,0:T(8,128)(2,1)}, u32[]{:S(2)}, u32[]{:S(2)}) %collective-permute-start.3) | collective-permute-done | bytes 262176 | tf_op jit(solution)/shard_map/ppermute | solution.py:24
  83.3 5.3 %collective-permute-done.6.refs_15_ = bf16[128,1024]{1,0:T(8,128)(2,1)} collective-permute-done((bf16[128,1024]{1,0:T(8,128)(2,1)}, bf16[128,1024]{1,0:T(8,128)(2,1)}, u32[]{:S(2)}, u32[]{:S(2)}) %collective-permute-start.6) | collective-permute-done | bytes 262176 | tf_op jit(solution)/shard_map/ppermute | solution.py:24
  88.6 0.0 collective-permute-done.9.refs_17_
  88.7 0.9 copy-done.2
  89.6 7.0 %mix.1 = bf16[1024,1024]{1,0:T(8,128)(2,1)} custom-call(s32[2]{0:T(128)S(1)} %pad_add_fusion.place_ref, bf16[8,128,1024]{2,1,0:T(8,128)(2,1)} %all-to-all-done.refs_0_.refs_1_.refs_2_.refs_3_.refs_4_.refs_5_.refs_6_.refs_7_, bf16[8,128,1024]{2,1,0:T(8,128)(2,1)} %all-to-all-done.refs_0_.refs_1_.refs_2_.refs_3_.refs_4_.refs_5_.refs_6_.refs_7_, ...), custom_call_target="tpu_custom_call" | custom-call | flops 2147483648 | bytes 10485760 | tf_op jit(solution)/shard_map/mix/pallas_call | solution.py:150
  (13 shorter events, 0.0 us)
Async XLA Ops:
  4.8 16.3 %collective-permute-start.2 = (bf16[128,1024]{1,0:T(8,128)(2,1)}, bf16[128,1024]{1,0:T(8,128)(2,1)S(1)}, u32[]{:S(2)}, u32[]{:S(2)}) collective-permute-start(bf16[128,1024]{1,0:T(8,128)(2,1)} %get-tuple-element.10.refs_8_), channel_id=1, source_target_pairs={{0,4},{1,5},{2,6},{3,7},{4,0},{5,1},{6,2},{7,3},{8,12},{9,13},{10,... | collective-permute-start | bytes 786440 | tf_op jit(solution)/shard_map/ppermute | solution.py:24
  8.8 12.4 %collective-permute-start.1 = (bf16[128,1024]{1,0:T(8,128)(2,1)}, bf16[128,1024]{1,0:T(8,128)(2,1)S(1)}, u32[]{:S(2)}, u32[]{:S(2)}) collective-permute-start(bf16[128,1024]{1,0:T(8,128)(2,1)} %get-tuple-element.10.refs_8_), channel_id=1, source_target_pairs={{0,2},{1,3},{2,0},{3,1},{4,6},{5,7},{6,4},{7,5},{8,10},{9,11},{10,... | collective-permute-start | bytes 786440 | tf_op jit(solution)/shard_map/ppermute | solution.py:24
  10.4 10.9 %collective-permute-start = (bf16[128,1024]{1,0:T(8,128)(2,1)}, bf16[128,1024]{1,0:T(8,128)(2,1)S(1)}, u32[]{:S(2)}, u32[]{:S(2)}) collective-permute-start(bf16[128,1024]{1,0:T(8,128)(2,1)} %get-tuple-element.10.refs_8_), channel_id=1, source_target_pairs={{0,1},{1,0},{2,3},{3,2},{4,5},{5,4},{6,7},{7,6},{8,9},{9,8},{10,11... | collective-permute-start | bytes 786440 | tf_op jit(solution)/shard_map/ppermute | solution.py:24
  21.2 0.7 copy-start.1
  21.9 66.7 %all-to-all-start = ((bf16[8,128,1024]{2,1,0:T(8,128)(2,1)}), bf16[8,128,1024]{2,1,0:T(8,128)(2,1)}, u32[]{:S(2)}, u32[]{:S(2)}) async-start(bf16[8,128,1024]{2,1,0:T(8,128)(2,1)} %get-tuple-element.12), calls=%async_computation | async-start | bytes 4194304 | tf_op jit(solution)/shard_map/all_to_all | solution.py:197
  34.9 2.9 %collective-permute-start.7 = (bf16[2,1024,256]{2,1,0:T(8,128)(2,1)}, bf16[2,1024,256]{2,1,0:T(8,128)(2,1)S(1)}, u32[]{:S(2)}, u32[]{:S(2)}) collective-permute-start(bf16[2,1024,256]{2,1,0:T(8,128)(2,1)} %get-tuple-element.16), channel_id=1, source_target_pairs={{0,8},{8,0},{16,24},{24,16},{1,9},{9,1},{17,25},{25,17},{2,10},{10... | collective-permute-start | bytes 3145736 | tf_op jit(solution)/shard_map/ppermute | solution.py:24
  37.7 15.8 %copy-start.3 = (f32[1024,256]{1,0:T(8,128)S(1)}, f32[1024,256]{1,0:T(8,128)}, u32[]{:S(2)}) copy-start(f32[1024,256]{1,0:T(8,128)} %param.12) | copy-start | bytes 3145732
  37.7 15.8 %copy-start.4 = (f32[1024,256]{1,0:T(8,128)S(1)}, f32[1024,256]{1,0:T(8,128)}, u32[]{:S(2)}) copy-start(f32[1024,256]{1,0:T(8,128)} %param.13) | copy-start | bytes 3145732
  39.4 49.2 %copy-start = (bf16[128,1024]{1,0:T(8,128)(2,1)S(1)}, bf16[128,1024]{1,0:T(8,128)(2,1)}, u32[]{:S(2)}) copy-start(bf16[128,1024]{1,0:T(8,128)(2,1)} %get-tuple-element.10.refs_8_) | copy-start | bytes 786436
  39.5 14.0 %collective-permute-start.8 = (bf16[1,1024,256]{2,1,0:T(8,128)(2,1)S(1)}, bf16[1,1024,256]{2,1,0:T(8,128)(2,1)S(1)}, u32[]{:S(2)}, u32[]{:S(2)}) collective-permute-start(bf16[1,1024,256]{2,1,0:T(8,128)(2,1)S(1)} %slice.23), channel_id=1, source_target_pairs={{0,16},{8,24},{16,0},{24,8},{1,17},{9,25},{17,1},{25,9},{2,18},{10... | collective-permute-start | bytes 1572872 | tf_op jit(solution)/shard_map/ppermute | solution.py:24
  55.1 13.2 %collective-permute-start.10 = (bf16[1024,256]{1,0:T(8,128)(2,1)S(1)}, bf16[1024,256]{1,0:T(8,128)(2,1)S(1)}, u32[]{:S(2)}, u32[]{:S(2)}) collective-permute-start(bf16[1024,256]{1,0:T(8,128)(2,1)S(1)} %get-tuple-element.17.refs_16_), channel_id=1, source_target_pairs={{0,16},{8,24},{16,0},{24,8},{1,17},{9,25},{17,1},{25,9},{2,18},{10... | collective-permute-start | bytes 1572872 | tf_op jit(solution)/shard_map/ppermute | solution.py:24
  56.6 13.8 %collective-permute-start.5 = (bf16[128,1024]{1,0:T(8,128)(2,1)S(1)}, bf16[128,1024]{1,0:T(8,128)(2,1)}, u32[]{:S(2)}, u32[]{:S(2)}) collective-permute-start(bf16[128,1024]{1,0:T(8,128)(2,1)S(1)} %collective-permute-done.2.refs_12_), channel_id=1, source_target_pairs={{0,2},{1,3},{2,0},{3,1},{4,6},{5,7},{6,4},{7,5},{8,10},{9,11},{10,... | collective-permute-start | bytes 786440 | tf_op jit(solution)/shard_map/ppermute | solution.py:24
  58.7 30.0 %collective-permute-start.9 = (bf16[1024,256]{1,0:T(8,128)(2,1)S(1)}, bf16[1024,256]{1,0:T(8,128)(2,1)S(1)}, u32[]{:S(2)}, u32[]{:S(2)}) collective-permute-start(bf16[1024,256]{1,0:T(8,128)(2,1)S(1)} %get-tuple-element.17.refs_16_), channel_id=1, source_target_pairs={{0,8},{8,0},{16,24},{24,16},{1,9},{9,1},{17,25},{25,17},{2,10},{10... | collective-permute-start | bytes 1572872 | tf_op jit(solution)/shard_map/ppermute | solution.py:24
  68.4 20.2 %collective-permute-start.11 = (bf16[1024,256]{1,0:T(8,128)(2,1)S(1)}, bf16[1024,256]{1,0:T(8,128)(2,1)S(1)}, u32[]{:S(2)}, u32[]{:S(2)}) collective-permute-start(bf16[1024,256]{1,0:T(8,128)(2,1)S(1)} %collective-permute-done.10.refs_18_), channel_id=1, source_target_pairs={{0,8},{8,0},{16,24},{24,16},{1,9},{9,1},{17,25},{25,17},{2,10},{10... | collective-permute-start | bytes 1572872 | tf_op jit(solution)/shard_map/ppermute | solution.py:24
  68.4 9.3 %collective-permute-start.4 = (bf16[128,1024]{1,0:T(8,128)(2,1)S(1)}, bf16[128,1024]{1,0:T(8,128)(2,1)}, u32[]{:S(2)}, u32[]{:S(2)}) collective-permute-start(bf16[128,1024]{1,0:T(8,128)(2,1)S(1)} %collective-permute-done.2.refs_12_), channel_id=1, source_target_pairs={{0,1},{1,0},{2,3},{3,2},{4,5},{5,4},{6,7},{7,6},{8,9},{9,8},{10,11... | collective-permute-start | bytes 786440 | tf_op jit(solution)/shard_map/ppermute | solution.py:24
  70.3 13.0 %collective-permute-start.3 = (bf16[128,1024]{1,0:T(8,128)(2,1)S(1)}, bf16[128,1024]{1,0:T(8,128)(2,1)}, u32[]{:S(2)}, u32[]{:S(2)}) collective-permute-start(bf16[128,1024]{1,0:T(8,128)(2,1)S(1)} %collective-permute-done.1.refs_10_), channel_id=1, source_target_pairs={{0,1},{1,0},{2,3},{3,2},{4,5},{5,4},{6,7},{7,6},{8,9},{9,8},{10,11... | collective-permute-start | bytes 786440 | tf_op jit(solution)/shard_map/ppermute | solution.py:24
  70.5 18.1 %collective-permute-start.6 = (bf16[128,1024]{1,0:T(8,128)(2,1)}, bf16[128,1024]{1,0:T(8,128)(2,1)}, u32[]{:S(2)}, u32[]{:S(2)}) collective-permute-start(bf16[128,1024]{1,0:T(8,128)(2,1)} %collective-permute-done.5.refs_14_), channel_id=1, source_target_pairs={{0,1},{1,0},{2,3},{3,2},{4,5},{5,4},{6,7},{7,6},{8,9},{9,8},{10,11... | collective-permute-start | bytes 786440 | tf_op jit(solution)/shard_map/ppermute | solution.py:24
  88.6 1.0 copy-start.2

commit v5 on v4

--- a/solution.py
+++ b/solution.py
@@ -24,43 +24,65 @@
     return lax.ppermute(value, axis, [(i, i ^ mask) for i in range(size)])
 
 
-def prepare_kernel(tokens_ref, cotangent_ref, blocks_ref, scaled_ref):
-    shards, _, rows = blocks_ref.shape
-    squares = None
-    for k in range(shards):
-        block = tokens_ref[:, k * rows : (k + 1) * rows]
-        blocks_ref[k] = block
-        block = block.astype(jnp.float32)
-        squares = block * block if squares is None else squares + block * block
-    mean = jnp.sum(squares, axis=-1, keepdims=True) / (shards * rows)
+def scale_kernel(tokens_ref, cotangent_ref, scaled_ref):
+    count, features = tokens_ref.shape
+    lanes = min(features, 1024)
+    squares = jnp.zeros((count, lanes), jnp.float32)
+    for start in range(0, features, lanes):
+        block = tokens_ref[:, start : start + lanes].astype(jnp.float32)
+        squares = squares + block * block
+    mean = jnp.sum(squares, axis=-1, keepdims=True) / features
     scaled_ref[...] = (cotangent_ref[...].astype(jnp.float32) * lax.rsqrt(mean + norm_eps)).astype(jnp.bfloat16)
 
 
-def prepare(tokens, cotangent, shards):
+def scale_cotangent(tokens, cotangent):
     count, features = tokens.shape
     width = cotangent.shape[1]
-    rows = features // shards
     tile = min(count, 32)
     return pl.pallas_call(
-        prepare_kernel,
-        out_shape=(
-            jax.ShapeDtypeStruct((shards, count, rows), jnp.bfloat16),
-            jax.ShapeDtypeStruct((count, width), jnp.bfloat16),
-        ),
+        scale_kernel,
+        out_shape=jax.ShapeDtypeStruct((count, width), jnp.bfloat16),
         grid=(count // tile,),
         in_specs=[
             pl.BlockSpec((tile, features), lambda i: (i, 0)),
             pl.BlockSpec((tile, width), lambda i: (i, 0)),
         ],
-        out_specs=(
-            pl.BlockSpec((shards, tile, rows), lambda i: (0, i, 0)),
-            pl.BlockSpec((tile, width), lambda i: (i, 0)),
-        ),
+        out_specs=pl.BlockSpec((tile, width), lambda i: (i, 0)),
         cost_estimate=pl.CostEstimate(
-            flops=3 * count * features, bytes_accessed=4 * count * (features + width), transcendentals=count
-        ),
-        name="prepare",
+            flops=3 * count * features, bytes_accessed=2 * count * (features + 2 * width), transcendentals=count
+        ),
+        name="scale_cotangent",
     )(tokens, cotangent)
+
+
+def cut_kernel(tokens_ref, *refs):
+    *out_refs, sems = refs
+    shards, count, rows = out_refs[0].shape
+    copies = [
+        pltpu.make_async_copy(
+            tokens_ref.at[pl.ds(part * count, count), pl.ds(k * rows, rows)], out_ref.at[k], sems.at[part, k]
+        )
+        for part, out_ref in enumerate(out_refs)
+        for k in range(shards)
+    ]
+    for copy in copies:
+        copy.start()
+    for copy in copies:
+        copy.wait()
+
+
+def cut(tokens, shards, parts):
+    count, features = tokens.shape
+    part = jax.ShapeDtypeStruct((shards, count // parts, features // shards), jnp.bfloat16)
+    return pl.pallas_call(
+        cut_kernel,
+        out_shape=(part,) * parts,
+        in_specs=[pl.BlockSpec(memory_space=pl.ANY)],
+        out_specs=(pl.BlockSpec(memory_space=pl.ANY),) * parts,
+        scratch_shapes=[pltpu.SemaphoreType.DMA((parts, shards))],
+        cost_estimate=pl.CostEstimate(flops=0, bytes_accessed=4 * count * features, transcendentals=0),
+        name="cut",
+    )(tokens)
 
 
 def code_kernel(own_ref, shared_ref, weight_ref, kept_ref, sent_ref, decoded_ref):
@@ -77,7 +99,7 @@
             jnp.max(jnp.where(low, 0.0, size), axis=-1, keepdims=True),
         )
         scale = ((largest + 1e-06) * (1.0 / code_range)).astype(jnp.bfloat16).astype(jnp.float32)
-        coded = (delta / scale).astype(jnp.bfloat16)
+        coded = (delta * pl.reciprocal(scale)).astype(jnp.bfloat16)
         decoded = (coded.astype(jnp.float32) * scale).astype(jnp.bfloat16)
         piece = min(share, lanes)
         for at in range(0, lanes, piece):
@@ -111,16 +133,16 @@
     )(own.reshape(1), shared, weight)
 
 
-def mix_kernel(parts, groups, place_ref, *refs):
-    tokens, refs = refs[:parts], refs[parts:]
-    cotangents, refs = refs[:parts], refs[parts:]
+def mix_kernel(shards, parts, groups, place_ref, *refs):
+    tokens, refs = refs[: shards * parts], refs[shards * parts :]
+    cotangents, refs = refs[:shards], refs[shards:]
     pieces, refs = refs[:groups], refs[groups:]
     gain_ref, weight_ref, out_ref, shared_ref = refs
     total = None
-    pair = 2 if parts % 2 == 0 else 1
-    for first in range(0, parts, pair):
+    pair = 2
+    for first in range(0, shards, pair):
         product = lax.dot_general(
-            jnp.concatenate([ref[0] for ref in tokens[first : first + pair]], axis=0),
+            jnp.concatenate([ref[0] for ref in tokens[first * parts : (first + pair) * parts]], axis=0),
             jnp.concatenate([ref[...] for ref in cotangents[first : first + pair]], axis=0),
             (((0,), (0,)), ((), ())),
             preferred_element_type=jnp.float32,
@@ -137,7 +159,8 @@
 
 
 def mix(mine, own, tokens, cotangents, pieces, gain, weight):
-    parts, depth, rows = tokens.shape
+    parts = len(tokens)
+    shards, depth, rows = tokens[0].shape
     width = weight.shape[1]
     groups = len(pieces)
     share = width // groups
@@ -148,13 +171,13 @@
 
     by_row = pl.BlockSpec((tile, width), lambda i, place: (i, 0))
     return pl.pallas_call(
-        functools.partial(mix_kernel, parts, groups),
+        functools.partial(mix_kernel, shards, parts, groups),
         out_shape=jax.ShapeDtypeStruct((rows, width), jnp.bfloat16),
         grid_spec=pltpu.PrefetchScalarGridSpec(
             num_scalar_prefetch=1,
             grid=(rows // tile,),
-            in_specs=[token_block(k) for k in range(parts)]
-            + [pl.BlockSpec((depth, width), lambda i, place: (0, 0))] * parts
+            in_specs=[token_block(k) for k in range(shards) for _ in range(parts)]
+            + [pl.BlockSpec((parts * depth, width), lambda i, place: (0, 0))] * shards
             + [pl.BlockSpec((tile, share), lambda i, place: (i, 0))] * groups
             + [pl.BlockSpec((tile, 1), lambda i, place: (i, 0)), by_row],
             out_specs=by_row,
@@ -162,12 +185,12 @@
         ),
         compiler_params=pltpu.CompilerParams(vmem_limit_bytes=48 * 2**20),
         cost_estimate=pl.CostEstimate(
-            flops=2 * parts * depth * rows * width,
-            bytes_accessed=2 * parts * depth * (rows + width) + 6 * rows * width,
+            flops=2 * parts * depth * shards * rows * width,
+            bytes_accessed=2 * parts * depth * shards * (rows + width) + 6 * rows * width,
             transcendentals=0,
         ),
         name="mix",
-    )(jnp.stack([mine, own]), *([tokens] * parts), *cotangents, *pieces, gain, weight)
+    )(jnp.stack([mine, own]), *(list(tokens) * shards), *cotangents, *pieces, gain, weight)
 
 
 def gather(piece, axis):
@@ -190,11 +213,13 @@
     rows, width = weight.shape
     inner_rate = inner_gain / math.sqrt(tokens.shape[0] * shards)
 
-    blocks, scaled = prepare(tokens, cotangent, shards)
+    scaled = scale_cotangent(tokens, cotangent)
     cotangents = gather(scaled, "fsdp")
+    early, late = cut(tokens, shards, 2)
+    early = lax.all_to_all(early, "fsdp", split_axis=0, concat_axis=0, tiled=True)
     first = [cotangents[1 << bit] for bit in range(shards.bit_length() - 1)]
-    *_, blocks, coded_weight, coded_shared = lax.optimization_barrier((*first, blocks, weight, shared_copy))
-    columns = lax.all_to_all(blocks, "fsdp", split_axis=0, concat_axis=0, tiled=True)
+    *_, late, coded_shared, coded_weight = lax.optimization_barrier((*first, late, shared_copy, weight))
+    late = lax.all_to_all(late, "fsdp", split_axis=0, concat_axis=0, tiled=True)
 
     kept, sent = code_and_decode(own, coded_shared, coded_weight, groups)
     total = kept.astype(jnp.float32) + swap(sent, "replica", 1).astype(jnp.float32)
@@ -210,7 +235,7 @@
 
     gain = lax.dynamic_slice_in_dim(norm_gain, mine * rows, rows).astype(jnp.float32)
     gain = (gain * ((1.0 - mix_weight) * inner_rate)).reshape(rows, 1)
-    layer_next = mix(mine, own, columns, cotangents, pieces, gain, weight)
+    layer_next = mix(mine, own, (early, late), cotangents, pieces, gain, weight)
     return (layer_next[None], master_next, momentum_next)
 
 

time: 97.2 us -> 183 us (1.88)
  Pallas kernels: 18.6 us -> 83.4 us
  waiting for transfers between devices: 49.7 us -> 66.2 us
  starting transfers between devices: 21.6 us -> 23.8 us
    pallas_call x2 -> x3, Pallas kernels: 11.2 us -> 75.8 us  [the longest x1 64.8 us: cut(): pl.pallas_call(cut_kernel, out_shape=(part,) * parts, in_specs=[pl.BlockS...]
    ppermute x12, waiting for transfers between devices: 49.7 us -> 66.2 us  [swap(): return lax.ppermute(value, axis, [(i, i ^ mask) for i in range(size)])]
    all_to_all x1 -> x2, starting transfers between devices: 5.48 us -> 11.5 us  [the longest x1 7.29 us: on_device(): lax.all_to_all(early, 'fsdp', split_axis=0, concat_axis=0, tiled=True)]
    ppermute x12, starting transfers between devices: 16.1 us -> 12.3 us  [swap(): return lax.ppermute(value, axis, [(i, i ^ mask) for i in range(size)])]
  transfers between devices with their start and end apart: 13 -> 14, of which waited for: 8 -> 7; matrix products, arithmetic and copies ran while one was open for 4% -> 3% of each run, Pallas kernels for 8% -> 6%
where the time goes in v5:
time: 183 us; the launch traced here: 182 us
  Pallas kernels  83.4 us (46%)
  waiting for transfers between devices  66.2 us (36%)
  starting transfers between devices  23.8 us (13%)
  other arithmetic  5.43 us (3%)
  local copies, waits for them, and re-layouts  2.47 us (1%)
    ppermute x12, waiting for transfers between devices, swap(): return lax.ppermute(value, axis, [(i, i ^ mask) for i in range(size)])  66.2 us
    pallas_call x1, Pallas kernels, cut(): pl.pallas_call(cut_kernel, out_shape=(part,) * parts, in_specs=[pl.BlockS...  64.8 us
    ppermute x12, starting transfers between devices, swap(): return lax.ppermute(value, axis, [(i, i ^ mask) for i in range(size)])  12.3 us
    pallas_call x1, Pallas kernels, code_and_decode(): pl.pallas_call(code_kernel, out_shape=(half, half), grid_spec=pltpu.Prefe...  7.56 us
    pallas_call x1, Pallas kernels, mix(): pl.pallas_call(functools.partial(mix_kernel, shards, parts, groups), out_...  7.31 us
    all_to_all x1, starting transfers between devices, on_device(): lax.all_to_all(early, 'fsdp', split_axis=0, concat_axis=0, tiled=True)  7.29 us
    all_to_all x1, starting transfers between devices, on_device(): late = lax.all_to_all(late, 'fsdp', split_axis=0, concat_axis=0, tiled=True)  4.25 us
    pallas_call x1, Pallas kernels, scale_cotangent(): pl.pallas_call(scale_kernel, out_shape=jax.ShapeDtypeStruct((count, width...  3.71 us
  transfers between devices with their start and end apart: 14, of which 7 were waited for; matrix products, arithmetic and copies ran while one was open for 3% of the time, Pallas kernels for 6%

profile of v5, /device:TPU:0, one launch (start us, length us, event | category | flops | bytes accessed | tf_op | source)
XLA Modules:
  0.0 182.0 jit_solution(15131635443194240)
XLA Ops:
  0.6 64.8 %cut.1 = (bf16[8,64,1024]{2,1,0:T(8,128)(2,1)}, bf16[8,64,1024]{2,1,0:T(8,128)(2,1)}) custom-call(bf16[128,8192]{1,0:T(8,128)(2,1)} %bitcast.15), custom_call_target="tpu_custom_call" | custom-call | bytes 4194304 | tf_op jit(solution)/shard_map/cut/pallas_call | solution.py:77
  65.4 7.3 %all-to-all-start = ((bf16[8,64,1024]{2,1,0:T(8,128)(2,1)}), bf16[8,64,1024]{2,1,0:T(8,128)(2,1)S(1)}, u32[]{:S(2)}, u32[]{:S(2)}) async-start(bf16[8,64,1024]{2,1,0:T(8,128)(2,1)} %get-tuple-element.10), calls=%async_computation | async-start | bytes 2097152 | tf_op jit(solution)/shard_map/all_to_all | solution.py:219
  72.7 3.7 %scale_cotangent.1.refs_16_ = bf16[128,1024]{1,0:T(8,128)(2,1)} custom-call(bf16[128,8192]{1,0:T(8,128)(2,1)} %bitcast.16, bf16[128,1024]{1,0:T(8,128)(2,1)} %bitcast.20), custom_call_target="tpu_custom_call" | custom-call | flops 3145728 | bytes 2621440 | tf_op jit(solution)/shard_map/scale_cotangent/pallas_call | solution.py:42
  76.4 2.9 %collective-permute-start.2 = (bf16[128,1024]{1,0:T(8,128)(2,1)}, bf16[128,1024]{1,0:T(8,128)(2,1)}, u32[]{:S(2)}, u32[]{:S(2)}) collective-permute-start(bf16[128,1024]{1,0:T(8,128)(2,1)} %scale_cotangent.1.refs_16_), channel_id=1, source_target_pairs={{0,4},{1,5},{2,6},{3,7},{4,0},{5,1},{6,2},{7,3},{8,12},{9,13},{10,... | collective-permute-start | bytes 786440 | tf_op jit(solution)/shard_map/ppermute | solution.py:24
  79.3 1.5 collective-permute-start.1
  80.8 1.5 collective-permute-start
  82.3 27.6 %collective-permute-done.2.refs_20_ = bf16[128,1024]{1,0:T(8,128)(2,1)} collective-permute-done((bf16[128,1024]{1,0:T(8,128)(2,1)}, bf16[128,1024]{1,0:T(8,128)(2,1)}, u32[]{:S(2)}, u32[]{:S(2)}) %collective-permute-start.2) | collective-permute-done | bytes 262176 | tf_op jit(solution)/shard_map/ppermute | solution.py:24
  109.8 0.0 collective-permute-done.1.refs_18_
  109.8 7.6 %code_and_decode.1 = (bf16[2,1024,256]{2,1,0:T(8,128)(2,1)}, bf16[2,1024,256]{2,1,0:T(8,128)(2,1)}) custom-call(s32[1]{0:T(128)} %bitcast.1.own_ref, bf16[1024,1024]{1,0:T(8,128)(2,1)} %shared_ref, bf16[1024,1024]{1,0:T(8,128)(2,1)} %bitcast.17), custom_call_target="tpu_custom_call" | custom-call | flops 20971520 | bytes 6291456 | tf_op jit(solution)/shard_map/code_and_decode/pallas_call | solution.py:121
  117.4 2.9 %collective-permute-done.7 = bf16[2,1024,256]{2,1,0:T(8,128)(2,1)S(1)} collective-permute-done((bf16[2,1024,256]{2,1,0:T(8,128)(2,1)}, bf16[2,1024,256]{2,1,0:T(8,128)(2,1)S(1)}, u32[]{:S(2)}, u32[]{:S(2)}) %collective-permute-start.7) | collective-permute-done | bytes 1048608 | tf_op jit(solution)/shard_map/ppermute | solution.py:24
  120.3 1.5 convert_add_fusion
  121.8 0.0 copy-start.3
  121.8 0.0 copy-start.4
  121.8 0.1 slice.23
  121.8 1.2 copy-done.3
  123.1 1.5 collective-permute-start.8
  124.6 4.2 %all-to-all-start.1 = ((bf16[8,64,1024]{2,1,0:T(8,128)(2,1)}), bf16[8,64,1024]{2,1,0:T(8,128)(2,1)}, u32[]{:S(2)}, u32[]{:S(2)}) async-start(bf16[8,64,1024]{2,1,0:T(8,128)(2,1)} %get-tuple-element.12), calls=%async_computation.1 | async-start | bytes 2097152 | tf_op jit(solution)/shard_map/all_to_all | solution.py:222
  128.8 8.2 %collective-permute-done.8 = bf16[1,1024,256]{2,1,0:T(8,128)(2,1)S(1)} collective-permute-done((bf16[1,1024,256]{2,1,0:T(8,128)(2,1)S(1)}, bf16[1,1024,256]{2,1,0:T(8,128)(2,1)S(1)}, u32[]{:S(2)}, u32[]{:S(2)}) %collective-permute-start.8) | collective-permute-done | bytes 524320 | tf_op jit(solution)/shard_map/ppermute | solution.py:24
  137.0 3.2 %fusion.2 = (bf16[1024,256]{1,0:T(8,128)(2,1)S(1)}, f32[1024,256]{1,0:T(8,128)}, f32[1024,256]{1,0:T(8,128)}) fusion(f32[1024,256]{1,0:T(8,128)S(1)} %copy-done.4, bf16[1,1024,256]{2,1,0:T(8,128)(2,1)S(1)} %collective-permute-done.8, f32[2,1024,256]{2,1,0:T(8,128)} %copy-done.3, f32[1024,256]{1,0:T(8,128)} %param.13), kind=kLoop, calls=%fused_computation.9 | loop fusion | flops 2621440 | bytes 6291456 | tf_op jit(solution)/shard_map/convert_element_type | solution.py:234
  140.2 1.5 collective-permute-start.10
  141.7 11.7 %collective-permute-done.10.refs_26_ = bf16[1024,256]{1,0:T(8,128)(2,1)S(1)} collective-permute-done((bf16[1024,256]{1,0:T(8,128)(2,1)S(1)}, bf16[1024,256]{1,0:T(8,128)(2,1)S(1)}, u32[]{:S(2)}, u32[]{:S(2)}) %collective-permute-start.10) | collective-permute-done | bytes 524320 | tf_op jit(solution)/shard_map/ppermute | solution.py:24
  153.5 1.4 collective-permute-start.4
  154.9 0.6 collective-permute-start.3
  155.5 1.4 collective-permute-start.6
  156.9 0.7 convert_multiply_fusion
  157.6 0.2 copy.10.refs_28_
  157.8 0.1 pad_add_fusion.place_ref
  157.9 5.0 %collective-permute-done.4.refs_21_ = bf16[128,1024]{1,0:T(8,128)(2,1)} collective-permute-done((bf16[128,1024]{1,0:T(8,128)(2,1)}, bf16[128,1024]{1,0:T(8,128)(2,1)}, u32[]{:S(2)}, u32[]{:S(2)}) %collective-permute-start.4) | collective-permute-done | bytes 262176 | tf_op jit(solution)/shard_map/ppermute | solution.py:24
  162.9 5.6 %collective-permute-done.3.refs_19_ = bf16[128,1024]{1,0:T(8,128)(2,1)} collective-permute-done((bf16[128,1024]{1,0:T(8,128)(2,1)}, bf16[128,1024]{1,0:T(8,128)(2,1)}, u32[]{:S(2)}, u32[]{:S(2)}) %collective-permute-start.3) | collective-permute-done | bytes 262176 | tf_op jit(solution)/shard_map/ppermute | solution.py:24
  168.5 5.2 %collective-permute-done.6.refs_23_ = bf16[128,1024]{1,0:T(8,128)(2,1)} collective-permute-done((bf16[128,1024]{1,0:T(8,128)(2,1)}, bf16[128,1024]{1,0:T(8,128)(2,1)}, u32[]{:S(2)}, u32[]{:S(2)}) %collective-permute-start.6) | collective-permute-done | bytes 262176 | tf_op jit(solution)/shard_map/ppermute | solution.py:24
  173.8 0.9 copy-done.2
  174.7 7.3 %mix.1 = bf16[1024,1024]{1,0:T(8,128)(2,1)} custom-call(s32[2]{0:T(128)S(1)} %pad_add_fusion.place_ref, bf16[8,64,1024]{2,1,0:T(8,128)(2,1)S(1)} %all-to-all-done.refs_0_.refs_2_.refs_4_.refs_6_.refs_8_.refs_10_.refs_12_.refs_14_, bf16[8,64,1024]{2,1,0:T(8,128)(2,1)} %all-to-all-done.1.refs_1_.refs_3_.refs_5_.refs_7_.refs_9_.refs_11_.refs_13_.refs_15_, ...), custom_call_target="tpu_custom_call" | custom-call | flops 2147483648 | bytes 10485760 | tf_op jit(solution)/shard_map/mix/pallas_call | solution.py:173
  (16 shorter events, 0.0 us)
Async XLA Ops:
  65.4 59.2 %all-to-all-start = ((bf16[8,64,1024]{2,1,0:T(8,128)(2,1)}), bf16[8,64,1024]{2,1,0:T(8,128)(2,1)S(1)}, u32[]{:S(2)}, u32[]{:S(2)}) async-start(bf16[8,64,1024]{2,1,0:T(8,128)(2,1)} %get-tuple-element.10), calls=%async_computation | async-start | bytes 2097152 | tf_op jit(solution)/shard_map/all_to_all | solution.py:219
  76.4 33.4 %collective-permute-start.2 = (bf16[128,1024]{1,0:T(8,128)(2,1)}, bf16[128,1024]{1,0:T(8,128)(2,1)}, u32[]{:S(2)}, u32[]{:S(2)}) collective-permute-start(bf16[128,1024]{1,0:T(8,128)(2,1)} %scale_cotangent.1.refs_16_), channel_id=1, source_target_pairs={{0,4},{1,5},{2,6},{3,7},{4,0},{5,1},{6,2},{7,3},{8,12},{9,13},{10,... | collective-permute-start | bytes 786440 | tf_op jit(solution)/shard_map/ppermute | solution.py:24
  79.3 30.5 %collective-permute-start.1 = (bf16[128,1024]{1,0:T(8,128)(2,1)}, bf16[128,1024]{1,0:T(8,128)(2,1)}, u32[]{:S(2)}, u32[]{:S(2)}) collective-permute-start(bf16[128,1024]{1,0:T(8,128)(2,1)} %scale_cotangent.1.refs_16_), channel_id=1, source_target_pairs={{0,2},{1,3},{2,0},{3,1},{4,6},{5,7},{6,4},{7,5},{8,10},{9,11},{10,... | collective-permute-start | bytes 786440 | tf_op jit(solution)/shard_map/ppermute | solution.py:24
  80.8 29.0 %collective-permute-start = (bf16[128,1024]{1,0:T(8,128)(2,1)}, bf16[128,1024]{1,0:T(8,128)(2,1)S(1)}, u32[]{:S(2)}, u32[]{:S(2)}) collective-permute-start(bf16[128,1024]{1,0:T(8,128)(2,1)} %scale_cotangent.1.refs_16_), channel_id=1, source_target_pairs={{0,1},{1,0},{2,3},{3,2},{4,5},{5,4},{6,7},{7,6},{8,9},{9,8},{10,11... | collective-permute-start | bytes 786440 | tf_op jit(solution)/shard_map/ppermute | solution.py:24
  109.8 7.6 %copy-start.1 = (bf16[128,1024]{1,0:T(8,128)(2,1)}, bf16[128,1024]{1,0:T(8,128)(2,1)S(1)}, u32[]{:S(2)}) copy-start(bf16[128,1024]{1,0:T(8,128)(2,1)S(1)} %collective-permute-done.refs_17_) | copy-start | bytes 786436
  117.4 2.9 %collective-permute-start.7 = (bf16[2,1024,256]{2,1,0:T(8,128)(2,1)}, bf16[2,1024,256]{2,1,0:T(8,128)(2,1)S(1)}, u32[]{:S(2)}, u32[]{:S(2)}) collective-permute-start(bf16[2,1024,256]{2,1,0:T(8,128)(2,1)} %get-tuple-element.16), channel_id=1, source_target_pairs={{0,8},{8,0},{16,24},{24,16},{1,9},{9,1},{17,25},{25,17},{2,10},{10... | collective-permute-start | bytes 3145736 | tf_op jit(solution)/shard_map/ppermute | solution.py:24
  121.8 1.3 copy-start.3
  121.8 15.3 %copy-start.4 = (f32[1024,256]{1,0:T(8,128)S(1)}, f32[1024,256]{1,0:T(8,128)}, u32[]{:S(2)}) copy-start(f32[1024,256]{1,0:T(8,128)} %param.12) | copy-start | bytes 3145732
  123.1 14.0 %collective-permute-start.8 = (bf16[1,1024,256]{2,1,0:T(8,128)(2,1)S(1)}, bf16[1,1024,256]{2,1,0:T(8,128)(2,1)S(1)}, u32[]{:S(2)}, u32[]{:S(2)}) collective-permute-start(bf16[1,1024,256]{2,1,0:T(8,128)(2,1)S(1)} %slice.23), channel_id=1, source_target_pairs={{0,16},{8,24},{16,0},{24,8},{1,17},{9,25},{17,1},{25,9},{2,18},{10... | collective-permute-start | bytes 1572872 | tf_op jit(solution)/shard_map/ppermute | solution.py:24
  124.6 49.2 %all-to-all-start.1 = ((bf16[8,64,1024]{2,1,0:T(8,128)(2,1)}), bf16[8,64,1024]{2,1,0:T(8,128)(2,1)}, u32[]{:S(2)}, u32[]{:S(2)}) async-start(bf16[8,64,1024]{2,1,0:T(8,128)(2,1)} %get-tuple-element.12), calls=%async_computation.1 | async-start | bytes 2097152 | tf_op jit(solution)/shard_map/all_to_all | solution.py:222
  128.8 44.9 %copy-start = (bf16[128,1024]{1,0:T(8,128)(2,1)S(1)}, bf16[128,1024]{1,0:T(8,128)(2,1)}, u32[]{:S(2)}) copy-start(bf16[128,1024]{1,0:T(8,128)(2,1)} %scale_cotangent.1.refs_16_) | copy-start | bytes 786436
  140.2 13.2 %collective-permute-start.10 = (bf16[1024,256]{1,0:T(8,128)(2,1)S(1)}, bf16[1024,256]{1,0:T(8,128)(2,1)S(1)}, u32[]{:S(2)}, u32[]{:S(2)}) collective-permute-start(bf16[1024,256]{1,0:T(8,128)(2,1)S(1)} %get-tuple-element.17.refs_24_), channel_id=1, source_target_pairs={{0,16},{8,24},{16,0},{24,8},{1,17},{9,25},{17,1},{25,9},{2,18},{10... | collective-permute-start | bytes 1572872 | tf_op jit(solution)/shard_map/ppermute | solution.py:24
  141.7 13.8 %collective-permute-start.5 = (bf16[128,1024]{1,0:T(8,128)(2,1)}, bf16[128,1024]{1,0:T(8,128)(2,1)}, u32[]{:S(2)}, u32[]{:S(2)}) collective-permute-start(bf16[128,1024]{1,0:T(8,128)(2,1)} %collective-permute-done.2.refs_20_), channel_id=1, source_target_pairs={{0,2},{1,3},{2,0},{3,1},{4,6},{5,7},{6,4},{7,5},{8,10},{9,11},{10,... | collective-permute-start | bytes 786440 | tf_op jit(solution)/shard_map/ppermute | solution.py:24
  141.7 32.0 %collective-permute-start.9 = (bf16[1024,256]{1,0:T(8,128)(2,1)S(1)}, bf16[1024,256]{1,0:T(8,128)(2,1)S(1)}, u32[]{:S(2)}, u32[]{:S(2)}) collective-permute-start(bf16[1024,256]{1,0:T(8,128)(2,1)S(1)} %get-tuple-element.17.refs_24_), channel_id=1, source_target_pairs={{0,8},{8,0},{16,24},{24,16},{1,9},{9,1},{17,25},{25,17},{2,10},{10... | collective-permute-start | bytes 1572872 | tf_op jit(solution)/shard_map/ppermute | solution.py:24
  153.5 20.3 %collective-permute-start.11 = (bf16[1024,256]{1,0:T(8,128)(2,1)S(1)}, bf16[1024,256]{1,0:T(8,128)(2,1)}, u32[]{:S(2)}, u32[]{:S(2)}) collective-permute-start(bf16[1024,256]{1,0:T(8,128)(2,1)S(1)} %collective-permute-done.10.refs_26_), channel_id=1, source_target_pairs={{0,8},{8,0},{16,24},{24,16},{1,9},{9,1},{17,25},{25,17},{2,10},{10... | collective-permute-start | bytes 1572872 | tf_op jit(solution)/shard_map/ppermute | solution.py:24
  153.5 9.4 %collective-permute-start.4 = (bf16[128,1024]{1,0:T(8,128)(2,1)}, bf16[128,1024]{1,0:T(8,128)(2,1)}, u32[]{:S(2)}, u32[]{:S(2)}) collective-permute-start(bf16[128,1024]{1,0:T(8,128)(2,1)} %collective-permute-done.2.refs_20_), channel_id=1, source_target_pairs={{0,1},{1,0},{2,3},{3,2},{4,5},{5,4},{6,7},{7,6},{8,9},{9,8},{10,11... | collective-permute-start | bytes 786440 | tf_op jit(solution)/shard_map/ppermute | solution.py:24
  154.9 13.6 %collective-permute-start.3 = (bf16[128,1024]{1,0:T(8,128)(2,1)}, bf16[128,1024]{1,0:T(8,128)(2,1)}, u32[]{:S(2)}, u32[]{:S(2)}) collective-permute-start(bf16[128,1024]{1,0:T(8,128)(2,1)} %collective-permute-done.1.refs_18_), channel_id=1, source_target_pairs={{0,1},{1,0},{2,3},{3,2},{4,5},{5,4},{6,7},{7,6},{8,9},{9,8},{10,11... | collective-permute-start | bytes 786440 | tf_op jit(solution)/shard_map/ppermute | solution.py:24
  155.5 18.2 %collective-permute-start.6 = (bf16[128,1024]{1,0:T(8,128)(2,1)}, bf16[128,1024]{1,0:T(8,128)(2,1)}, u32[]{:S(2)}, u32[]{:S(2)}) collective-permute-start(bf16[128,1024]{1,0:T(8,128)(2,1)} %collective-permute-done.5.refs_22_), channel_id=1, source_target_pairs={{0,1},{1,0},{2,3},{3,2},{4,5},{5,4},{6,7},{7,6},{8,9},{9,8},{10,11... | collective-permute-start | bytes 786440 | tf_op jit(solution)/shard_map/ppermute | solution.py:24
  173.8 1.0 copy-start.2

commit v6 on v3

--- a/solution.py
+++ b/solution.py
@@ -24,41 +24,58 @@
     return lax.ppermute(value, axis, [(i, i ^ mask) for i in range(size)])
 
 
-def prepare_kernel(tokens_ref, cotangent_ref, blocks_ref, scaled_ref):
-    shards, _, rows = blocks_ref.shape
-    squares = None
-    for k in range(shards):
-        block = tokens_ref[:, k * rows : (k + 1) * rows]
-        blocks_ref[k] = block
-        block = block.astype(jnp.float32)
-        squares = block * block if squares is None else squares + block * block
-    mean = jnp.sum(squares, axis=-1, keepdims=True) / (shards * rows)
-    scaled_ref[...] = (cotangent_ref[...].astype(jnp.float32) * lax.rsqrt(mean + norm_eps)).astype(jnp.bfloat16)
+def prepare_kernel(tokens_ref, cotangent_ref, blocks_ref, scaled_ref, inverse_ref, squares_ref):
+    step, steps = pl.program_id(0), pl.num_programs(0)
+    count, rows = tokens_ref.shape
+    lanes = squares_ref.shape[1]
+    blocks_ref[0] = tokens_ref[...]
+    squares = jnp.zeros((count, lanes), jnp.float32)
+    for start in range(0, rows, lanes):
+        block = tokens_ref[:, start : start + lanes].astype(jnp.float32)
+        squares = squares + block * block
+
+    @pl.when(step == 0)
+    def _():
+        squares_ref[...] = squares
+
+    @pl.when(step > 0)
+    def _():
+        squares_ref[...] += squares
+
+    @pl.when(step == steps - 1)
+    def _():
+        mean = jnp.sum(squares_ref[...], axis=-1, keepdims=True) / (steps * rows)
+        inverse = lax.rsqrt(mean + norm_eps)
+        scaled_ref[...] = (cotangent_ref[...].astype(jnp.float32) * inverse).astype(jnp.bfloat16)
+        inverse_ref[...] = jnp.transpose(jnp.broadcast_to(inverse, (count, lanes)))[: inverse_ref.shape[0]]
 
 
 def prepare(tokens, cotangent, shards):
     count, features = tokens.shape
     width = cotangent.shape[1]
     rows = features // shards
-    tile = min(count, 32)
     return pl.pallas_call(
         prepare_kernel,
         out_shape=(
             jax.ShapeDtypeStruct((shards, count, rows), jnp.bfloat16),
             jax.ShapeDtypeStruct((count, width), jnp.bfloat16),
-        ),
-        grid=(count // tile,),
+            jax.ShapeDtypeStruct((8, count), jnp.float32),
+        ),
+        grid=(shards,),
         in_specs=[
-            pl.BlockSpec((tile, features), lambda i: (i, 0)),
-            pl.BlockSpec((tile, width), lambda i: (i, 0)),
+            pl.BlockSpec((count, rows), lambda k: (0, k)),
+            pl.BlockSpec((count, width), lambda k: (0, 0)),
         ],
         out_specs=(
-            pl.BlockSpec((shards, tile, rows), lambda i: (0, i, 0)),
-            pl.BlockSpec((tile, width), lambda i: (i, 0)),
-        ),
+            pl.BlockSpec((1, count, rows), lambda k: (k, 0, 0)),
+            pl.BlockSpec((count, width), lambda k: (0, 0)),
+            pl.BlockSpec((8, count), lambda k: (0, 0)),
+        ),
+        scratch_shapes=[pltpu.VMEM((count, 128), jnp.float32)],
         cost_estimate=pl.CostEstimate(
             flops=3 * count * features, bytes_accessed=4 * count * (features + width), transcendentals=count
         ),
+        compiler_params=pltpu.CompilerParams(vmem_limit_bytes=12 * 2**20),
         name="prepare",
     )(tokens, cotangent)
 
@@ -77,7 +94,7 @@
             jnp.max(jnp.where(low, 0.0, size), axis=-1, keepdims=True),
         )
         scale = ((largest + 1e-06) * (1.0 / code_range)).astype(jnp.bfloat16).astype(jnp.float32)
-        coded = (delta / scale).astype(jnp.bfloat16)
+        coded = (delta * pl.reciprocal(scale)).astype(jnp.bfloat16)
         decoded = (coded.astype(jnp.float32) * scale).astype(jnp.bfloat16)
         piece = min(share, lanes)
         for at in range(0, lanes, piece):
@@ -107,6 +124,7 @@
             scratch_shapes=[pltpu.VMEM((groups, tile, share), jnp.bfloat16)],
         ),
         cost_estimate=pl.CostEstimate(flops=20 * rows * width, bytes_accessed=6 * rows * width, transcendentals=0),
+        compiler_params=pltpu.CompilerParams(vmem_limit_bytes=12 * 2**20),
         name="code_and_decode",
     )(own.reshape(1), shared, weight)
 
@@ -160,7 +178,7 @@
             out_specs=by_row,
             scratch_shapes=[pltpu.VMEM((groups, tile, share), jnp.bfloat16)],
         ),
-        compiler_params=pltpu.CompilerParams(vmem_limit_bytes=48 * 2**20),
+        compiler_params=pltpu.CompilerParams(vmem_limit_bytes=20 * 2**20),
         cost_estimate=pl.CostEstimate(
             flops=2 * parts * depth * rows * width,
             bytes_accessed=2 * parts * depth * (rows + width) + 6 * rows * width,
@@ -170,11 +188,13 @@
     )(jnp.stack([mine, own]), *([tokens] * parts), *cotangents, *pieces, gain, weight)
 
 
-def gather(piece, axis):
-    size = lax.axis_size(axis)
+def gather(piece, axis, size, after=()):
     pieces = {0: piece}
     bit = size // 2
     while bit:
+        if bit == 1 and after:
+            (*held, _) = lax.optimization_barrier((*(pieces[k] for k in sorted(pieces)[1:]), after))
+            pieces.update(zip(sorted(pieces)[1:], held))
         for k in sorted(pieces):
             pieces[k ^ bit] = swap(pieces[k], axis, bit)
         bit //= 2
@@ -190,11 +210,18 @@
     rows, width = weight.shape
     inner_rate = inner_gain / math.sqrt(tokens.shape[0] * shards)
 
-    blocks, scaled = prepare(tokens, cotangent, shards)
-    cotangents = gather(scaled, "fsdp")
+    half = shards // 2
+    far = swap(cotangent, "fsdp", half)
+    blocks, scaled, inverse = prepare(tokens, cotangent, shards)
+    inverse = swap(inverse, "fsdp", half)
+    near = gather(scaled, "fsdp", half)
+    far, *near[1:3], blocks, coded_shared, coded_weight = lax.optimization_barrier(
+        (far, *near[1:3], blocks, shared_copy, weight)
+    )
     columns = lax.all_to_all(blocks, "fsdp", split_axis=0, concat_axis=0, tiled=True)
-
-    _, coded_weight, coded_shared = lax.optimization_barrier((cotangents[shards // 2], weight, shared_copy))
+    far = (far.astype(jnp.float32) * inverse[0][:, None]).astype(jnp.bfloat16)
+    cotangents = near + gather(far, "fsdp", half)
+
     kept, sent = code_and_decode(own, coded_shared, coded_weight, groups)
     total = kept.astype(jnp.float32) + swap(sent, "replica", 1).astype(jnp.float32)
     bit = 2
@@ -205,7 +232,7 @@
     average = total[0] / groups
     momentum_next = outer_beta * momentum + average
     master_next = master - outer_rate * (average + outer_beta * momentum_next)
-    pieces = gather(master_next.astype(jnp.bfloat16), "replica")
+    pieces = gather(master_next.astype(jnp.bfloat16), "replica", groups, after=cotangents[:-1])
 
     gain = lax.dynamic_slice_in_dim(norm_gain, mine * rows, rows).astype(jnp.float32)
     gain = (gain * ((1.0 - mix_weight) * inner_rate)).reshape(rows, 1)

time: 141 us -> 110 us (0.78)
  waiting for transfers between devices: 94.9 us -> 57.1 us
  local copies, waits for them, and re-layouts: 1.92 us -> 16.5 us
  Pallas kernels: 18.6 us -> 11 us
    ppermute x12 -> x13, waiting for transfers between devices: 94.9 us -> 57.1 us  [swap(): return lax.ppermute(value, axis, [(i, i ^ mask) for i in range(size)])]
    unnamed x10 -> x40, local copies, waits for them, and re-layouts: 1.64 us -> 16.2 us
    ppermute x12 -> x13, starting transfers between devices: 13 us -> 17.1 us  [swap(): return lax.ppermute(value, axis, [(i, i ^ mask) for i in range(size)])]
    pallas_call x1, Pallas kernels: 7.45 us -> 3.44 us  [code_and_decode(): pl.pallas_call(code_kernel, out_shape=(half, half), grid_spec=pltpu.Prefe...]
    pallas_call x1, Pallas kernels: 4.14 us -> 1.04 us  [prepare(): pl.pallas_call(prepare_kernel, out_shape=(jax.ShapeDtypeStruct((shards, c...]
    all_to_all x1, starting transfers between devices: 7.41 us -> 4.69 us  [on_device(): lax.all_to_all(blocks, 'fsdp', split_axis=0, concat_axis=0, tiled=True)]
    add x1, other arithmetic: 1.64 us -> 0.23 us  [on_device(): kept.astype(jnp.float32) + swap(sent, 'replica', 1).astype(jnp.float32)]
  transfers between devices with their start and end apart: 13 -> 14, of which waited for: 7 -> 8; matrix products, arithmetic and copies ran while one was open for 3% -> 3% of each run, Pallas kernels for 5% -> 4%
where the time goes in v6:
time: 110 us
  waiting for transfers between devices  57.1 us (52%)
  starting transfers between devices  21.8 us (20%)
  local copies, waits for them, and re-layouts  16.5 us (15%)
  Pallas kernels  11 us (10%)
  other arithmetic  2.76 us (3%)
    ppermute x13, waiting for transfers between devices, swap(): return lax.ppermute(value, axis, [(i, i ^ mask) for i in range(size)])  57.1 us
    ppermute x13, starting transfers between devices, swap(): return lax.ppermute(value, axis, [(i, i ^ mask) for i in range(size)])  17.1 us
    unnamed x40, local copies, waits for them, and re-layouts  16.2 us
    pallas_call x1, Pallas kernels, mix(): pl.pallas_call(functools.partial(mix_kernel, parts, groups), out_shape=ja...  6.52 us
    all_to_all x1, starting transfers between devices, on_device(): lax.all_to_all(blocks, 'fsdp', split_axis=0, concat_axis=0, tiled=True)  4.69 us
    pallas_call x1, Pallas kernels, code_and_decode(): pl.pallas_call(code_kernel, out_shape=(half, half), grid_spec=pltpu.Prefe...  3.44 us
  transfers between devices with their start and end apart: 14, of which 8 were waited for; matrix products, arithmetic and copies ran while one was open for 3% of the time, Pallas kernels for 4%

profile of v6, /device:TPU:0, one launch (start us, length us, event | category | flops | bytes accessed | tf_op | source)
XLA Modules:
  0.0 109.9 jit_solution(16230546497307216636)
XLA Ops:
  0.6 4.1 %collective-permute-start = (bf16[128,1024]{1,0:T(8,128)(2,1)}, bf16[128,1024]{1,0:T(8,128)(2,1)S(1)}, u32[]{:S(2)}, u32[]{:S(2)}) collective-permute-start(bf16[128,1024]{1,0:T(8,128)(2,1)} %bitcast.20), channel_id=1, source_target_pairs={{0,4},{1,5},{2,6},{3,7},{4,0},{5,1},{6,2},{7,3},{8,12},{9,13},{10,... | collective-permute-start | bytes 786440 | tf_op jit(solution)/shard_map/ppermute | solution.py:24
  4.7 1.6 %copy-done.2 = bf16[1,128,8192]{2,1,0:T(8,128)(2,1)S(1)} copy-done((bf16[1,128,8192]{2,1,0:T(8,128)(2,1)S(1)}, bf16[1,128,8192]{2,1,0:T(8,128)(2,1)}, u32[]{:S(2)}) %copy-start.2) | copy-done | bytes 2097176
  6.3 0.9 copy-done.15
  7.3 1.0 prepare.1
  8.3 1.3 %copy-done.4 = bf16[8,128,1024]{2,1,0:T(8,128)(2,1)} copy-done((bf16[8,128,1024]{2,1,0:T(8,128)(2,1)}, bf16[8,128,1024]{2,1,0:T(8,128)(2,1)S(1)}, u32[]{:S(2)}) %copy-start.4) | copy-done | bytes 2097176
  9.6 1.6 %collective-permute-start.2 = (bf16[128,1024]{1,0:T(8,128)(2,1)S(1)}, bf16[128,1024]{1,0:T(8,128)(2,1)S(1)}, u32[]{:S(2)}, u32[]{:S(2)}) collective-permute-start(bf16[128,1024]{1,0:T(8,128)(2,1)S(1)} %get-tuple-element.15.refs_8_), channel_id=1, source_target_pairs={{0,2},{1,3},{2,0},{3,1},{4,6},{5,7},{6,4},{7,5},{8,10},{9,11},{10,... | collective-permute-start | bytes 786440 | tf_op jit(solution)/shard_map/ppermute | solution.py:24
  11.2 1.5 %collective-permute-start.1 = (bf16[128,1024]{1,0:T(8,128)(2,1)S(1)}, bf16[128,1024]{1,0:T(8,128)(2,1)S(1)}, u32[]{:S(2)}, u32[]{:S(2)}) collective-permute-start(bf16[128,1024]{1,0:T(8,128)(2,1)S(1)} %get-tuple-element.15.refs_8_), channel_id=1, source_target_pairs={{0,1},{1,0},{2,3},{3,2},{4,5},{5,4},{6,7},{7,6},{8,9},{9,8},{10,11... | collective-permute-start | bytes 786440 | tf_op jit(solution)/shard_map/ppermute | solution.py:24
  13.4 3.5 %collective-permute-done = bf16[128,1024]{1,0:T(8,128)(2,1)S(1)} collective-permute-done((bf16[128,1024]{1,0:T(8,128)(2,1)}, bf16[128,1024]{1,0:T(8,128)(2,1)S(1)}, u32[]{:S(2)}, u32[]{:S(2)}) %collective-permute-start) | collective-permute-done | bytes 262176 | tf_op jit(solution)/shard_map/ppermute | solution.py:24
  17.0 4.8 %collective-permute-done.2.refs_10_ = bf16[128,1024]{1,0:T(8,128)(2,1)S(1)} collective-permute-done((bf16[128,1024]{1,0:T(8,128)(2,1)S(1)}, bf16[128,1024]{1,0:T(8,128)(2,1)S(1)}, u32[]{:S(2)}, u32[]{:S(2)}) %collective-permute-start.2) | collective-permute-done | bytes 262176 | tf_op jit(solution)/shard_map/ppermute | solution.py:24
  22.6 4.7 %all-to-all-start = ((bf16[8,128,1024]{2,1,0:T(8,128)(2,1)}), bf16[8,128,1024]{2,1,0:T(8,128)(2,1)S(1)}, u32[]{:S(2)}, u32[]{:S(2)}) async-start(bf16[8,128,1024]{2,1,0:T(8,128)(2,1)} %copy-done.4), calls=%async_computation | async-start | bytes 4194304 | tf_op jit(solution)/shard_map/all_to_all | solution.py:221
  27.3 1.6 %copy-done = bf16[1,1024,1024]{2,1,0:T(8,128)(2,1)S(1)} copy-done((bf16[1,1024,1024]{2,1,0:T(8,128)(2,1)S(1)}, bf16[1,1024,1024]{2,1,0:T(8,128)(2,1)}, u32[]{:S(2)}) %copy-start) | copy-done | bytes 2097176
  28.8 1.6 %copy-done.3 = bf16[1024,1024]{1,0:T(8,128)(2,1)S(1)} copy-done((bf16[1024,1024]{1,0:T(8,128)(2,1)S(1)}, bf16[1024,1024]{1,0:T(8,128)(2,1)}, u32[]{:S(2)}) %copy-start.3) | copy-done | bytes 2097176
  30.4 3.4 %code_and_decode.1 = (bf16[2,1024,256]{2,1,0:T(8,128)(2,1)S(1)}, bf16[2,1024,256]{2,1,0:T(8,128)(2,1)S(1)}) custom-call(s32[1]{0:T(128)} %bitcast.1.own_ref, bf16[1024,1024]{1,0:T(8,128)(2,1)S(1)} %copy-done.3, bf16[1024,1024]{1,0:T(8,128)(2,1)S(1)} %bitcast.17), custom_call_target="tpu_custom_call" | custom-call | flops 20971520 | bytes 6291456 | tf_op jit(solution)/shard_map/code_and_decode/pallas_call | solution.py:116
  34.0 2.6 %collective-permute-done.8 = bf16[2,1024,256]{2,1,0:T(8,128)(2,1)S(1)} collective-permute-done((bf16[2,1024,256]{2,1,0:T(8,128)(2,1)S(1)}, bf16[2,1024,256]{2,1,0:T(8,128)(2,1)S(1)}, u32[]{:S(2)}, u32[]{:S(2)}) %collective-permute-start.8) | collective-permute-done | bytes 1048608 | tf_op jit(solution)/shard_map/ppermute | solution.py:24
  36.9 1.6 %collective-permute-start.9 = (bf16[1,1024,256]{2,1,0:T(8,128)(2,1)S(1)}, bf16[1,1024,256]{2,1,0:T(8,128)(2,1)S(1)}, u32[]{:S(2)}, u32[]{:S(2)}) collective-permute-start(bf16[1,1024,256]{2,1,0:T(8,128)(2,1)S(1)} %slice.28), channel_id=1, source_target_pairs={{0,16},{8,24},{16,0},{24,8},{1,17},{9,25},{17,1},{25,9},{2,18},{10... | collective-permute-start | bytes 1572872 | tf_op jit(solution)/shard_map/ppermute | solution.py:24
  38.5 2.9 %collective-permute-start.4 = (f32[8,128]{1,0:T(8,128)S(1)}, f32[8,128]{1,0:T(8,128)S(1)}, u32[]{:S(2)}, u32[]{:S(2)}) collective-permute-start(f32[8,128]{1,0:T(8,128)S(1)} %get-tuple-element.21), channel_id=1, source_target_pairs={{0,4},{1,5},{2,6},{3,7},{4,0},{5,1},{6,2},{7,3},{8,12},{9,13},{10,... | collective-permute-start | bytes 12296 | tf_op jit(solution)/shard_map/ppermute | solution.py:24
  41.4 9.5 %collective-permute-done.9 = bf16[1,1024,256]{2,1,0:T(8,128)(2,1)S(1)} collective-permute-done((bf16[1,1024,256]{2,1,0:T(8,128)(2,1)S(1)}, bf16[1,1024,256]{2,1,0:T(8,128)(2,1)S(1)}, u32[]{:S(2)}, u32[]{:S(2)}) %collective-permute-start.9) | collective-permute-done | bytes 524320 | tf_op jit(solution)/shard_map/ppermute | solution.py:24
  50.9 1.7 %fusion.2 = (bf16[1024,256]{1,0:T(8,128)(2,1)S(1)}, f32[1024,256]{1,0:T(8,128)}, f32[1024,256]{1,0:T(8,128)}) fusion(f32[1024,256]{1,0:T(8,128)S(1)} %copy-done.16, bf16[1,1024,256]{2,1,0:T(8,128)(2,1)S(1)} %collective-permute-done.9, f32[2,1024,256]{2,1,0:T(8,128)S(1)} %convert_add_fusion, f32[1024,256]{1,0:T(8,128)S(1)} %copy-done.17), kind=kLoop, calls=%fused_computation.11 | loop fusion | flops 2621440 | bytes 6291456 | tf_op jit(solution)/shard_map/convert_element_type | solution.py:235
  52.6 1.5 %collective-permute-start.11 = (bf16[1024,256]{1,0:T(8,128)(2,1)S(1)}, bf16[1024,256]{1,0:T(8,128)(2,1)}, u32[]{:S(2)}, u32[]{:S(2)}) collective-permute-start(bf16[1024,256]{1,0:T(8,128)(2,1)S(1)} %get-tuple-element.27.refs_16_), channel_id=1, source_target_pairs={{0,16},{8,24},{16,0},{24,8},{1,17},{9,25},{17,1},{25,9},{2,18},{10... | collective-permute-start | bytes 1572872 | tf_op jit(solution)/shard_map/ppermute | solution.py:24
  54.1 20.4 %collective-permute-done.4 = f32[8,128]{1,0:T(8,128)S(1)} collective-permute-done((f32[8,128]{1,0:T(8,128)S(1)}, f32[8,128]{1,0:T(8,128)S(1)}, u32[]{:S(2)}, u32[]{:S(2)}) %collective-permute-start.4) | collective-permute-done | bytes 4128 | tf_op jit(solution)/shard_map/ppermute | solution.py:24
  74.6 1.5 %collective-permute-start.3 = (bf16[128,1024]{1,0:T(8,128)(2,1)S(1)}, bf16[128,1024]{1,0:T(8,128)(2,1)S(1)}, u32[]{:S(2)}, u32[]{:S(2)}) collective-permute-start(bf16[128,1024]{1,0:T(8,128)(2,1)S(1)} %collective-permute-done.2.refs_10_), channel_id=1, source_target_pairs={{0,1},{1,0},{2,3},{3,2},{4,5},{5,4},{6,7},{7,6},{8,9},{9,8},{10,11... | collective-permute-start | bytes 786440 | tf_op jit(solution)/shard_map/ppermute | solution.py:24
  76.7 7.2 %collective-permute-done.3.refs_11_ = bf16[128,1024]{1,0:T(8,128)(2,1)S(1)} collective-permute-done((bf16[128,1024]{1,0:T(8,128)(2,1)S(1)}, bf16[128,1024]{1,0:T(8,128)(2,1)S(1)}, u32[]{:S(2)}, u32[]{:S(2)}) %collective-permute-start.3) | collective-permute-done | bytes 262176 | tf_op jit(solution)/shard_map/ppermute | solution.py:24
  84.6 2.7 %collective-permute-done.5.refs_13_ = bf16[128,1024]{1,0:T(8,128)(2,1)S(1)} collective-permute-done((bf16[128,1024]{1,0:T(8,128)(2,1)S(1)}, bf16[128,1024]{1,0:T(8,128)(2,1)S(1)}, u32[]{:S(2)}, u32[]{:S(2)}) %collective-permute-start.5) | collective-permute-done | bytes 262176 | tf_op jit(solution)/shard_map/ppermute | solution.py:24
  88.0 1.7 %collective-permute-start.7 = (bf16[128,1024]{1,0:T(8,128)(2,1)}, bf16[128,1024]{1,0:T(8,128)(2,1)}, u32[]{:S(2)}, u32[]{:S(2)}) collective-permute-start(bf16[128,1024]{1,0:T(8,128)(2,1)} %collective-permute-done.6.refs_14_), channel_id=1, source_target_pairs={{0,1},{1,0},{2,3},{3,2},{4,5},{5,4},{6,7},{7,6},{8,9},{9,8},{10,11... | collective-permute-start | bytes 786440 | tf_op jit(solution)/shard_map/ppermute | solution.py:24
  90.7 6.3 %collective-permute-done.7.refs_15_ = bf16[128,1024]{1,0:T(8,128)(2,1)} collective-permute-done((bf16[128,1024]{1,0:T(8,128)(2,1)}, bf16[128,1024]{1,0:T(8,128)(2,1)}, u32[]{:S(2)}, u32[]{:S(2)}) %collective-permute-start.7) | collective-permute-done | bytes 262176 | tf_op jit(solution)/shard_map/ppermute | solution.py:24
  97.0 1.6 %copy-done.1 = bf16[1,1024,1024]{2,1,0:T(8,128)(2,1)S(1)} copy-done((bf16[1,1024,1024]{2,1,0:T(8,128)(2,1)S(1)}, bf16[1,1024,1024]{2,1,0:T(8,128)(2,1)}, u32[]{:S(2)}) %copy-start.1) | copy-done | bytes 2097176
  98.6 0.9 copy-done.6
  99.6 0.9 copy-done.8
  100.5 0.9 copy-done.10
  101.5 0.9 copy-done.12
  102.4 0.9 copy-done.14
  103.4 6.5 %mix.1 = bf16[1024,1024]{1,0:T(8,128)(2,1)} custom-call(s32[2]{0:T(128)S(1)} %pad_add_fusion.place_ref, bf16[8,128,1024]{2,1,0:T(8,128)(2,1)S(1)} %all-to-all-done.refs_0_.refs_1_.refs_2_.refs_3_.refs_4_.refs_5_.refs_6_.refs_7_, bf16[8,128,1024]{2,1,0:T(8,128)(2,1)S(1)} %all-to-all-done.refs_0_.refs_1_.refs_2_.refs_3_.refs_4_.refs_5_.refs_6_.refs_7_, ...), custom_call_target="tpu_custom_call" | custom-call | flops 2147483648 | bytes 10485760 | tf_op jit(solution)/shard_map/mix/pallas_call | solution.py:168
  (47 shorter events, 4.9 us)
Async XLA Ops:
  0.6 16.3 %collective-permute-start = (bf16[128,1024]{1,0:T(8,128)(2,1)}, bf16[128,1024]{1,0:T(8,128)(2,1)S(1)}, u32[]{:S(2)}, u32[]{:S(2)}) collective-permute-start(bf16[128,1024]{1,0:T(8,128)(2,1)} %bitcast.20), channel_id=1, source_target_pairs={{0,4},{1,5},{2,6},{3,7},{4,0},{5,1},{6,2},{7,3},{8,12},{9,13},{10,... | collective-permute-start | bytes 786440 | tf_op jit(solution)/shard_map/ppermute | solution.py:24
  4.7 1.6 %copy-start.2 = (bf16[1,128,8192]{2,1,0:T(8,128)(2,1)S(1)}, bf16[1,128,8192]{2,1,0:T(8,128)(2,1)}, u32[]{:S(2)}) copy-start(bf16[1,128,8192]{2,1,0:T(8,128)(2,1)} %param.7) | copy-start | bytes 6291460
  6.3 0.9 copy-start.15
  8.3 1.3 %copy-start.4 = (bf16[8,128,1024]{2,1,0:T(8,128)(2,1)}, bf16[8,128,1024]{2,1,0:T(8,128)(2,1)S(1)}, u32[]{:S(2)}) copy-start(bf16[8,128,1024]{2,1,0:T(8,128)(2,1)S(1)} %get-tuple-element.17) | copy-start | bytes 6291460
  9.6 12.2 %collective-permute-start.2 = (bf16[128,1024]{1,0:T(8,128)(2,1)S(1)}, bf16[128,1024]{1,0:T(8,128)(2,1)S(1)}, u32[]{:S(2)}, u32[]{:S(2)}) collective-permute-start(bf16[128,1024]{1,0:T(8,128)(2,1)S(1)} %get-tuple-element.15.refs_8_), channel_id=1, source_target_pairs={{0,2},{1,3},{2,0},{3,1},{4,6},{5,7},{6,4},{7,5},{8,10},{9,11},{10,... | collective-permute-start | bytes 786440 | tf_op jit(solution)/shard_map/ppermute | solution.py:24
  11.2 10.6 %collective-permute-start.1 = (bf16[128,1024]{1,0:T(8,128)(2,1)S(1)}, bf16[128,1024]{1,0:T(8,128)(2,1)S(1)}, u32[]{:S(2)}, u32[]{:S(2)}) collective-permute-start(bf16[128,1024]{1,0:T(8,128)(2,1)S(1)} %get-tuple-element.15.refs_8_), channel_id=1, source_target_pairs={{0,1},{1,0},{2,3},{3,2},{4,5},{5,4},{6,7},{7,6},{8,9},{9,8},{10,11... | collective-permute-start | bytes 786440 | tf_op jit(solution)/shard_map/ppermute | solution.py:24
  12.7 0.7 copy-start.5
  17.0 4.9 %copy-start.18 = (bf16[128,1024]{1,0:T(8,128)(2,1)}, bf16[128,1024]{1,0:T(8,128)(2,1)S(1)}, u32[]{:S(2)}) copy-start(bf16[128,1024]{1,0:T(8,128)(2,1)S(1)} %collective-permute-done) | copy-start | bytes 786436
  21.8 52.8 %copy-start.7 = (bf16[128,1024]{1,0:T(8,128)(2,1)}, bf16[128,1024]{1,0:T(8,128)(2,1)S(1)}, u32[]{:S(2)}) copy-start(bf16[128,1024]{1,0:T(8,128)(2,1)S(1)} %collective-permute-done.2.refs_10_) | copy-start | bytes 786436
  21.8 0.7 copy-start.9
  22.6 74.4 %all-to-all-start = ((bf16[8,128,1024]{2,1,0:T(8,128)(2,1)}), bf16[8,128,1024]{2,1,0:T(8,128)(2,1)S(1)}, u32[]{:S(2)}, u32[]{:S(2)}) async-start(bf16[8,128,1024]{2,1,0:T(8,128)(2,1)} %copy-done.4), calls=%async_computation | async-start | bytes 4194304 | tf_op jit(solution)/shard_map/all_to_all | solution.py:221
  27.3 1.6 %copy-start = (bf16[1,1024,1024]{2,1,0:T(8,128)(2,1)S(1)}, bf16[1,1024,1024]{2,1,0:T(8,128)(2,1)}, u32[]{:S(2)}) copy-start(bf16[1,1024,1024]{2,1,0:T(8,128)(2,1)} %param.10) | copy-start | bytes 6291460
  28.8 1.6 %copy-start.3 = (bf16[1024,1024]{1,0:T(8,128)(2,1)S(1)}, bf16[1024,1024]{1,0:T(8,128)(2,1)}, u32[]{:S(2)}) copy-start(bf16[1024,1024]{1,0:T(8,128)(2,1)} %shared_ref) | copy-start | bytes 6291460
  33.9 2.7 %collective-permute-start.8 = (bf16[2,1024,256]{2,1,0:T(8,128)(2,1)S(1)}, bf16[2,1024,256]{2,1,0:T(8,128)(2,1)S(1)}, u32[]{:S(2)}, u32[]{:S(2)}) collective-permute-start(bf16[2,1024,256]{2,1,0:T(8,128)(2,1)S(1)} %get-tuple-element.25), channel_id=1, source_target_pairs={{0,8},{8,0},{16,24},{24,16},{1,9},{9,1},{17,25},{25,17},{2,10},{10... | collective-permute-start | bytes 3145736 | tf_op jit(solution)/shard_map/ppermute | solution.py:24
  36.6 14.3 %copy-start.16 = (f32[1024,256]{1,0:T(8,128)S(1)}, f32[1024,256]{1,0:T(8,128)}, u32[]{:S(2)}) copy-start(f32[1024,256]{1,0:T(8,128)} %param.12) | copy-start | bytes 3145732
  36.6 14.3 %copy-start.17 = (f32[1024,256]{1,0:T(8,128)S(1)}, f32[1024,256]{1,0:T(8,128)}, u32[]{:S(2)}) copy-start(f32[1024,256]{1,0:T(8,128)} %param.13) | copy-start | bytes 3145732
  36.9 14.0 %collective-permute-start.9 = (bf16[1,1024,256]{2,1,0:T(8,128)(2,1)S(1)}, bf16[1,1024,256]{2,1,0:T(8,128)(2,1)S(1)}, u32[]{:S(2)}, u32[]{:S(2)}) collective-permute-start(bf16[1,1024,256]{2,1,0:T(8,128)(2,1)S(1)} %slice.28), channel_id=1, source_target_pairs={{0,16},{8,24},{16,0},{24,8},{1,17},{9,25},{17,1},{25,9},{2,18},{10... | collective-permute-start | bytes 1572872 | tf_op jit(solution)/shard_map/ppermute | solution.py:24
  38.5 36.0 %copy-start.19 = (bf16[128,1024]{1,0:T(8,128)(2,1)S(1)}, bf16[128,1024]{1,0:T(8,128)(2,1)}, u32[]{:S(2)}) copy-start(bf16[128,1024]{1,0:T(8,128)(2,1)} %copy-done.18) | copy-start | bytes 786436
  38.5 36.0 %collective-permute-start.4 = (f32[8,128]{1,0:T(8,128)S(1)}, f32[8,128]{1,0:T(8,128)S(1)}, u32[]{:S(2)}, u32[]{:S(2)}) collective-permute-start(f32[8,128]{1,0:T(8,128)S(1)} %get-tuple-element.21), channel_id=1, source_target_pairs={{0,4},{1,5},{2,6},{3,7},{4,0},{5,1},{6,2},{7,3},{8,12},{9,13},{10,... | collective-permute-start | bytes 12296 | tf_op jit(solution)/shard_map/ppermute | solution.py:24
  52.6 35.4 %collective-permute-start.11 = (bf16[1024,256]{1,0:T(8,128)(2,1)S(1)}, bf16[1024,256]{1,0:T(8,128)(2,1)}, u32[]{:S(2)}, u32[]{:S(2)}) collective-permute-start(bf16[1024,256]{1,0:T(8,128)(2,1)S(1)} %get-tuple-element.27.refs_16_), channel_id=1, source_target_pairs={{0,16},{8,24},{16,0},{24,8},{1,17},{9,25},{17,1},{25,9},{2,18},{10... | collective-permute-start | bytes 1572872 | tf_op jit(solution)/shard_map/ppermute | solution.py:24
  74.6 9.3 %collective-permute-start.3 = (bf16[128,1024]{1,0:T(8,128)(2,1)S(1)}, bf16[128,1024]{1,0:T(8,128)(2,1)S(1)}, u32[]{:S(2)}, u32[]{:S(2)}) collective-permute-start(bf16[128,1024]{1,0:T(8,128)(2,1)S(1)} %collective-permute-done.2.refs_10_), channel_id=1, source_target_pairs={{0,1},{1,0},{2,3},{3,2},{4,5},{5,4},{6,7},{7,6},{8,9},{9,8},{10,11... | collective-permute-start | bytes 786440 | tf_op jit(solution)/shard_map/ppermute | solution.py:24
  76.1 8.5 %collective-permute-start.6 = (bf16[128,1024]{1,0:T(8,128)(2,1)S(1)}, bf16[128,1024]{1,0:T(8,128)(2,1)}, u32[]{:S(2)}, u32[]{:S(2)}) collective-permute-start(bf16[128,1024]{1,0:T(8,128)(2,1)S(1)} %multiply_convert_fusion.refs_12_), channel_id=1, source_target_pairs={{0,2},{1,3},{2,0},{3,1},{4,6},{5,7},{6,4},{7,5},{8,10},{9,11},{10,... | collective-permute-start | bytes 786440 | tf_op jit(solution)/shard_map/ppermute | solution.py:24
  76.1 11.1 %collective-permute-start.5 = (bf16[128,1024]{1,0:T(8,128)(2,1)S(1)}, bf16[128,1024]{1,0:T(8,128)(2,1)S(1)}, u32[]{:S(2)}, u32[]{:S(2)}) collective-permute-start(bf16[128,1024]{1,0:T(8,128)(2,1)S(1)} %multiply_convert_fusion.refs_12_), channel_id=1, source_target_pairs={{0,1},{1,0},{2,3},{3,2},{4,5},{5,4},{6,7},{7,6},{8,9},{9,8},{10,11... | collective-permute-start | bytes 786440 | tf_op jit(solution)/shard_map/ppermute | solution.py:24
  76.7 20.3 %collective-permute-start.10 = (bf16[1024,256]{1,0:T(8,128)(2,1)S(1)}, bf16[1024,256]{1,0:T(8,128)(2,1)}, u32[]{:S(2)}, u32[]{:S(2)}) collective-permute-start(bf16[1024,256]{1,0:T(8,128)(2,1)S(1)} %get-tuple-element.27.refs_16_), channel_id=1, source_target_pairs={{0,8},{8,0},{16,24},{24,16},{1,9},{9,1},{17,25},{25,17},{2,10},{10... | collective-permute-start | bytes 1572872 | tf_op jit(solution)/shard_map/ppermute | solution.py:24
  88.0 9.0 %collective-permute-start.12 = (bf16[1024,256]{1,0:T(8,128)(2,1)}, bf16[1024,256]{1,0:T(8,128)(2,1)}, u32[]{:S(2)}, u32[]{:S(2)}) collective-permute-start(bf16[1024,256]{1,0:T(8,128)(2,1)} %collective-permute-done.11.refs_18_), channel_id=1, source_target_pairs={{0,8},{8,0},{16,24},{24,16},{1,9},{9,1},{17,25},{25,17},{2,10},{10... | collective-permute-start | bytes 1572872 | tf_op jit(solution)/shard_map/ppermute | solution.py:24
  88.0 9.0 %collective-permute-start.7 = (bf16[128,1024]{1,0:T(8,128)(2,1)}, bf16[128,1024]{1,0:T(8,128)(2,1)}, u32[]{:S(2)}, u32[]{:S(2)}) collective-permute-start(bf16[128,1024]{1,0:T(8,128)(2,1)} %collective-permute-done.6.refs_14_), channel_id=1, source_target_pairs={{0,1},{1,0},{2,3},{3,2},{4,5},{5,4},{6,7},{7,6},{8,9},{9,8},{10,11... | collective-permute-start | bytes 786440 | tf_op jit(solution)/shard_map/ppermute | solution.py:24
  97.0 1.6 %copy-start.1 = (bf16[1,1024,1024]{2,1,0:T(8,128)(2,1)S(1)}, bf16[1,1024,1024]{2,1,0:T(8,128)(2,1)}, u32[]{:S(2)}) copy-start(bf16[1,1024,1024]{2,1,0:T(8,128)(2,1)} %param.10) | copy-start | bytes 6291460
  98.6 0.9 copy-start.6
  99.6 0.9 copy-start.8
  100.5 0.9 copy-start.10
  101.5 0.9 copy-start.12
  102.4 0.9 copy-start.14
  (2 other events, 1.4 us)

commit v7 on v3

v7 whole, which is shorter than its diff:
```python
import functools
import math

import jax
import jax.numpy as jnp
from jax import lax
from jax.experimental import pallas as pl
from jax.experimental.pallas import tpu as pltpu
from jax.sharding import PartitionSpec as P

BLOCK = 64


norm_eps = 1e-05
inner_gain = 0.4
outer_rate = 0.7
outer_beta = 0.9
mix_weight = 0.5
code_range = 448.0


def swap(value, axis, mask):
    size = lax.axis_size(axis)
    return lax.ppermute(value, axis, [(i, i ^ mask) for i in range(size)])


def prepare_kernel(tokens_ref, gain_ref, blocks_ref, inverse_ref):
    lanes = 128
    count, features = tokens_ref.shape
    rows = blocks_ref.shape[1]

    @pl.when(pl.program_id(0) == 0)
    def _():
        squares = jnp.zeros((count, lanes), jnp.float32)
        for start in range(0, features, lanes):
            block = tokens_ref[:, start : start + lanes].astype(jnp.float32)
            squares = squares + block * block
        mean = jnp.sum(squares, axis=-1, keepdims=True) / features
        inverse_ref[...] = jnp.broadcast_to(lax.rsqrt(mean + norm_eps), inverse_ref.shape)

    first = pl.program_id(0) * rows
    for start in range(0, rows, lanes):
        columns = pl.ds(pl.multiple_of(first + start, lanes), lanes)
        normed = tokens_ref[:, columns].astype(jnp.float32) * inverse_ref[...] * gain_ref[:, columns]
        blocks_ref[0, start : start + lanes] = jnp.transpose(normed).astype(jnp.bfloat16)


def prepare(tokens, gain, shards):
    count, features = tokens.shape
    rows = features // shards
    return pl.pallas_call(
        prepare_kernel,
        out_shape=jax.ShapeDtypeStruct((shards, rows, count), jnp.bfloat16),
        grid=(shards,),
        in_specs=[
            pl.BlockSpec((count, features), lambda k: (0, 0)),
            pl.BlockSpec((1, features), lambda k: (0, 0)),
        ],
        out_specs=pl.BlockSpec((1, rows, count), lambda k: (k, 0, 0)),
        scratch_shapes=[pltpu.VMEM((count, 128), jnp.float32)],
        cost_estimate=pl.CostEstimate(
            flops=5 * count * features, bytes_accessed=4 * count * features, transcendentals=count
        ),
        name="prepare",
    )(tokens, gain.astype(jnp.float32).reshape(1, features))


def code_kernel(own_ref, shared_ref, weight_ref, kept_ref, sent_ref, decoded_ref):
    lanes = 2 * BLOCK
    groups, rows, share = decoded_ref.shape
    low = lax.broadcasted_iota(jnp.int32, (rows, lanes), 1) < BLOCK
    for start in range(0, groups * share, lanes):
        columns = slice(start, start + lanes)
        delta = shared_ref[:, columns].astype(jnp.float32) - weight_ref[:, columns].astype(jnp.float32)
        size = jnp.abs(delta)
        largest = jnp.where(
            low,
            jnp.max(jnp.where(low, size, 0.0), axis=-1, keepdims=True),
            jnp.max(jnp.where(low, 0.0, size), axis=-1, keepdims=True),
        )
        scale = ((largest + 1e-06) * (1.0 / code_range)).astype(jnp.bfloat16).astype(jnp.float32)
        coded = (delta * pl.reciprocal(scale)).astype(jnp.bfloat16)
        decoded = (coded.astype(jnp.float32) * scale).astype(jnp.bfloat16)
        piece = min(share, lanes)
        for at in range(0, lanes, piece):
            group, offset = divmod(start + at, share)
            decoded_ref[group, :, offset : offset + piece] = decoded[:, at : at + piece]
    own = own_ref[0]
    for k in range(0, groups, 2):
        kept_ref[k // 2] = decoded_ref[own ^ k]
        sent_ref[k // 2] = decoded_ref[own ^ (k + 1)]


def code_and_decode(own, shared, weight, groups):
    rows, width = shared.shape
    tile = min(rows, 128)
    share = width // groups
    spec = pl.BlockSpec((tile, width), lambda i, own: (i, 0))
    half = jax.ShapeDtypeStruct((groups // 2, rows, share), jnp.bfloat16)
    half_spec = pl.BlockSpec((groups // 2, tile, share), lambda i, own: (0, i, 0))
    return pl.pallas_call(
        code_kernel,
        out_shape=(half, half),
        grid_spec=pltpu.PrefetchScalarGridSpec(
            num_scalar_prefetch=1,
            grid=(rows // tile,),
            in_specs=[spec, spec],
            out_specs=(half_spec, half_spec),
            scratch_shapes=[pltpu.VMEM((groups, tile, share), jnp.bfloat16)],
        ),
        cost_estimate=pl.CostEstimate(flops=20 * rows * width, bytes_accessed=6 * rows * width, transcendentals=0),
        name="code_and_decode",
    )(own.reshape(1), shared, weight)


def mix_kernel(shards, groups, rate, place_ref, *refs):
    tokens_ref, refs = refs[0], refs[1:]
    cotangent_refs, refs = refs[:shards], refs[shards:]
    piece_refs, refs = refs[:groups], refs[groups:]
    weight_ref, out_ref, refs = refs[0], refs[1], refs[2:]
    tokens, cotangents, pieces, weights, outs, token_sem, cotangent_sems, piece_sems, weight_sem, out_sems = refs
    mine, own = place_ref[0], place_ref[1]
    depth, width = cotangent_refs[0].shape
    share = pieces.shape[2]
    tile = outs.shape[2]

    def own_row(k):
        return pl.ds(pl.multiple_of((mine ^ k) * depth, depth), depth)

    loads = [pltpu.make_async_copy(tokens_ref, tokens, token_sem)]
    for k, ref in enumerate(cotangent_refs):
        loads.append(pltpu.make_async_copy(ref, cotangents.at[own_row(k)], cotangent_sems.at[k]))
    loads.append(pltpu.make_async_copy(weight_ref, weights, weight_sem))
    for k, ref in enumerate(piece_refs):
        loads.append(pltpu.make_async_copy(ref, pieces.at[own ^ k], piece_sems.at[k]))
    for load in loads:
        load.start()
    for load in loads[: 1 + shards]:
        load.wait()
    left = jnp.concatenate([tokens[k] for k in range(shards)], axis=1)
    stores = []
    for step in range(width // tile):
        columns = slice(step * tile, (step + 1) * tile)
        total = jnp.dot(left, cotangents[:, columns], preferred_element_type=jnp.float32)
        if step == 0:
            for load in loads[1 + shards :]:
                load.wait()
        for group in range(step * tile // share, (step + 1) * tile // share):
            place = slice(group * share, (group + 1) * share)
            part = slice(group * share - step * tile, (group + 1) * share - step * tile)
            mixed = weights[:, place].astype(jnp.float32) + pieces[group].astype(jnp.float32)
            outs[step, :, part] = (mix_weight * mixed - rate * total[:, part]).astype(jnp.bfloat16)
        stores.append(pltpu.make_async_copy(outs.at[step], out_ref.at[:, pl.ds(step * tile, tile)], out_sems.at[step]))
        stores[-1].start()
    for store in stores:
        store.wait()


def mix(mine, own, tokens, cotangents, pieces, weight, rate):
    shards, rows, depth = tokens.shape
    width = weight.shape[1]
    groups = len(pieces)
    share = width // groups
    tile = max(share, 256)
    return pl.pallas_call(
        functools.partial(mix_kernel, shards, groups, rate),
        out_shape=jax.ShapeDtypeStruct((rows, width), jnp.bfloat16),
        in_specs=[pl.BlockSpec(memory_space=pltpu.SMEM)]
        + [pl.BlockSpec(memory_space=pltpu.HBM)] * (2 + shards + groups),
        out_specs=pl.BlockSpec(memory_space=pltpu.HBM),
        scratch_shapes=[
            pltpu.VMEM((shards, rows, depth), jnp.bfloat16),
            pltpu.VMEM((shards * depth, width), jnp.bfloat16),
            pltpu.VMEM((groups, rows, share), jnp.bfloat16),
            pltpu.VMEM((rows, width), jnp.bfloat16),
            pltpu.VMEM((width // tile, rows, tile), jnp.bfloat16),
            pltpu.SemaphoreType.DMA,
            pltpu.SemaphoreType.DMA((shards,)),
            pltpu.SemaphoreType.DMA((groups,)),
            pltpu.SemaphoreType.DMA,
            pltpu.SemaphoreType.DMA((width // tile,)),
        ],
        compiler_params=pltpu.CompilerParams(vmem_limit_bytes=48 * 2**20),
        cost_estimate=pl.CostEstimate(
            flops=2 * depth * shards * rows * width,
            bytes_accessed=2 * depth * shards * (rows + width) + 6 * rows * width,
            transcendentals=0,
        ),
        name="mix",
    )(jnp.stack([mine, own]), tokens, *cotangents, *pieces, weight)


def gather(piece, axis, size, after=()):
    pieces = {0: piece}
    bit = size // 2
    while bit:
        if bit == 1 and after:
            (*held, _) = lax.optimization_barrier((*(pieces[k] for k in sorted(pieces)[1:]), after))
            pieces.update(zip(sorted(pieces)[1:], held))
        for k in sorted(pieces):
            pieces[k ^ bit] = swap(pieces[k], axis, bit)
        bit //= 2
    return [pieces[k] for k in range(size)]


def on_device(tokens, norm_gain, cotangent, layer_weight, shared_copy, master, momentum):
    tokens, cotangent, weight = tokens[0], cotangent[0], layer_weight[0]
    shards = lax.axis_size("fsdp")
    groups = lax.axis_size("replica")
    mine = lax.axis_index("fsdp")
    own = lax.axis_index("replica")
    rows, width = weight.shape
    inner_rate = inner_gain / math.sqrt(tokens.shape[0] * shards)

    own_exchanges = [1 << bit for bit in range(shards.bit_length() - 1)]
    cotangents = gather(cotangent, "fsdp", shards)
    blocks = prepare(tokens, norm_gain, shards)
    *_, blocks, coded_shared, coded_weight = lax.optimization_barrier(
        (*(cotangents[k] for k in own_exchanges), blocks, shared_copy, weight)
    )
    columns = lax.all_to_all(blocks, "fsdp", split_axis=0, concat_axis=0, tiled=True)

    kept, sent = code_and_decode(own, coded_shared, coded_weight, groups)
    total = kept.astype(jnp.float32) + swap(sent, "replica", 1).astype(jnp.float32)
    bit = 2
    while bit < groups:
        sent = swap(total[1::2].astype(jnp.bfloat16), "replica", bit)
        total = total[0::2] + sent.astype(jnp.float32)
        bit *= 2
    average = total[0] / groups
    momentum_next = outer_beta * momentum + average
    master_next = master - outer_rate * (average + outer_beta * momentum_next)
    pieces = gather(master_next.astype(jnp.bfloat16), "replica", groups, after=cotangents[:-1])

    layer_next = mix(mine, own, columns, cotangents, pieces, weight, (1.0 - mix_weight) * inner_rate)
    return (layer_next[None], master_next, momentum_next)


def solution(mesh):
    in_specs = (
        P("replica", "fsdp", None),
        P(),
        P("replica", "fsdp", None),
        P("replica", "fsdp", None),
        P("fsdp", None),
        P("fsdp", "replica"),
        P("fsdp", "replica"),
    )
    out_specs = (P("replica", "fsdp", None), P("fsdp", "replica"), P("fsdp", "replica"))
    return jax.shard_map(
        on_device, mesh=mesh, in_specs=in_specs, out_specs=out_specs, check_vma=False
    )
```

time: 141 us -> 89.7 us (0.64)
  waiting for transfers between devices: 94.9 us -> 38.1 us
  starting transfers between devices: 20.4 us -> 22.3 us
  Pallas kernels: 18.6 us -> 20.2 us
  local copies, waits for them, and re-layouts: 1.92 us -> 3.38 us
    ppermute x12, waiting for transfers between devices: 94.9 us -> 38.1 us  [swap(): return lax.ppermute(value, axis, [(i, i ^ mask) for i in range(size)])]
    ppermute x12, starting transfers between devices: 13 us -> 16.8 us  [swap(): return lax.ppermute(value, axis, [(i, i ^ mask) for i in range(size)])]
    all_to_all x1, starting transfers between devices: 7.41 us -> 5.48 us  [on_device(): lax.all_to_all(blocks, 'fsdp', split_axis=0, concat_axis=0, tiled=True)]
    unnamed x10 -> x14, local copies, waits for them, and re-layouts: 1.64 us -> 3.33 us
    pallas_call x2, Pallas kernels: 11.2 us -> 12.7 us  [the longest x1 7.03 us: mix(): pl.pallas_call(functools.partial(mix_kernel, shards, groups, rate), out_s...]
  transfers between devices with their start and end apart: 13 -> 13, of which waited for: 7 -> 8; matrix products, arithmetic and copies ran while one was open for 3% -> 5% of each run, Pallas kernels for 5% -> 15%
where the time goes in v7:
time: 89.7 us; the launch traced here: 89.3 us
  waiting for transfers between devices  38.1 us (42%)
  starting transfers between devices  22.3 us (25%)
  Pallas kernels  20.2 us (23%)
  other arithmetic  4.7 us (5%)
  local copies, waits for them, and re-layouts  3.38 us (4%)
    ppermute x12, waiting for transfers between devices, swap(): return lax.ppermute(value, axis, [(i, i ^ mask) for i in range(size)])  38.1 us
    ppermute x12, starting transfers between devices, swap(): return lax.ppermute(value, axis, [(i, i ^ mask) for i in range(size)])  16.8 us
    pallas_call x1, Pallas kernels, code_and_decode(): pl.pallas_call(code_kernel, out_shape=(half, half), grid_spec=pltpu.Prefe...  7.46 us
    pallas_call x1, Pallas kernels, mix(): pl.pallas_call(functools.partial(mix_kernel, shards, groups, rate), out_s...  7.03 us
    pallas_call x1, Pallas kernels, prepare(): pl.pallas_call(prepare_kernel, out_shape=jax.ShapeDtypeStruct((shards, ro...  5.69 us
    all_to_all x1, starting transfers between devices, on_device(): lax.all_to_all(blocks, 'fsdp', split_axis=0, concat_axis=0, tiled=True)  5.48 us
    unnamed x14, local copies, waits for them, and re-layouts  3.33 us
  transfers between devices with their start and end apart: 13, of which 8 were waited for; matrix products, arithmetic and copies ran while one was open for 5% of the time, Pallas kernels for 15%

profile of v7, /device:TPU:0, one launch (start us, length us, event | category | flops | bytes accessed | tf_op | source)
XLA Modules:
  0.0 89.3 jit_solution(15328401690985952193)
XLA Ops:
  0.6 4.1 %collective-permute-start.2 = (bf16[128,1024]{1,0:T(8,128)(2,1)}, bf16[128,1024]{1,0:T(8,128)(2,1)S(1)}, u32[]{:S(2)}, u32[]{:S(2)}) collective-permute-start(bf16[128,1024]{1,0:T(8,128)(2,1)} %bitcast.15), channel_id=1, source_target_pairs={{0,4},{1,5},{2,6},{3,7},{4,0},{5,1},{6,2},{7,3},{8,12},{9,13},{10,... | collective-permute-start | bytes 786440 | tf_op jit(solution)/shard_map/ppermute | solution.py:24
  4.7 1.6 %collective-permute-start.1 = (bf16[128,1024]{1,0:T(8,128)(2,1)}, bf16[128,1024]{1,0:T(8,128)(2,1)S(1)}, u32[]{:S(2)}, u32[]{:S(2)}) collective-permute-start(bf16[128,1024]{1,0:T(8,128)(2,1)} %bitcast.16), channel_id=1, source_target_pairs={{0,2},{1,3},{2,0},{3,1},{4,6},{5,7},{6,4},{7,5},{8,10},{9,11},{10,... | collective-permute-start | bytes 786440 | tf_op jit(solution)/shard_map/ppermute | solution.py:24
  6.3 1.5 %collective-permute-start = (bf16[128,1024]{1,0:T(8,128)(2,1)}, bf16[128,1024]{1,0:T(8,128)(2,1)S(1)}, u32[]{:S(2)}, u32[]{:S(2)}) collective-permute-start(bf16[128,1024]{1,0:T(8,128)(2,1)} %bitcast.17), channel_id=1, source_target_pairs={{0,1},{1,0},{2,3},{3,2},{4,5},{5,4},{6,7},{7,6},{8,9},{9,8},{10,11... | collective-permute-start | bytes 786440 | tf_op jit(solution)/shard_map/ppermute | solution.py:24
  7.8 1.3 %reshape.16 = f32[8192]{0:T(1024)} convert(bf16[8192]{0:T(1024)(128)(2,1)} %param.8) | non-fusion elementwise | flops 8192 | bytes 49152 | tf_op jit(solution)/shard_map/reshape | solution.py:65
  9.2 5.7 %prepare.1 = bf16[8,1024,128]{2,1,0:T(8,128)(2,1)} custom-call(bf16[128,8192]{1,0:T(8,128)(2,1)} %bitcast.21, f32[1,8192]{1,0:T(1,128)} %bitcast.23), custom_call_target="tpu_custom_call" | custom-call | flops 5242880 | bytes 4194304 | tf_op jit(solution)/shard_map/prepare/pallas_call | solution.py:51
  14.9 2.1 %collective-permute-done.2.refs_5_ = bf16[128,1024]{1,0:T(8,128)(2,1)S(1)} collective-permute-done((bf16[128,1024]{1,0:T(8,128)(2,1)}, bf16[128,1024]{1,0:T(8,128)(2,1)S(1)}, u32[]{:S(2)}, u32[]{:S(2)}) %collective-permute-start.2) | collective-permute-done | bytes 262176 | tf_op jit(solution)/shard_map/ppermute | solution.py:24
  17.0 0.2 collective-permute-done.1.refs_3_
  17.2 0.0 collective-permute-done.refs_2_
  17.2 5.5 %all-to-all-start = ((bf16[8,1024,128]{2,1,0:T(8,128)(2,1)}), bf16[8,1024,128]{2,1,0:T(8,128)(2,1)}, u32[]{:S(2)}, u32[]{:S(2)}) async-start(bf16[8,1024,128]{2,1,0:T(8,128)(2,1)} %prepare.1), calls=%async_computation | async-start | bytes 4194304 | tf_op jit(solution)/shard_map/all_to_all | solution.py:221
  22.6 7.5 %code_and_decode.1 = (bf16[2,1024,256]{2,1,0:T(8,128)(2,1)}, bf16[2,1024,256]{2,1,0:T(8,128)(2,1)}) custom-call(s32[1]{0:T(128)} %bitcast.1.own_ref, bf16[1024,1024]{1,0:T(8,128)(2,1)} %shared_ref, bf16[1024,1024]{1,0:T(8,128)(2,1)} %bitcast.19), custom_call_target="tpu_custom_call" | custom-call | flops 20971520 | bytes 6291456 | tf_op jit(solution)/shard_map/code_and_decode/pallas_call | solution.py:101
  30.1 2.9 %collective-permute-done.7 = bf16[2,1024,256]{2,1,0:T(8,128)(2,1)S(1)} collective-permute-done((bf16[2,1024,256]{2,1,0:T(8,128)(2,1)}, bf16[2,1024,256]{2,1,0:T(8,128)(2,1)S(1)}, u32[]{:S(2)}, u32[]{:S(2)}) %collective-permute-start.7) | collective-permute-done | bytes 1048608 | tf_op jit(solution)/shard_map/ppermute | solution.py:24
  33.0 1.6 %convert_add_fusion = f32[2,1024,256]{2,1,0:T(8,128)S(1)} fusion(bf16[2,1024,256]{2,1,0:T(8,128)(2,1)S(1)} %collective-permute-done.7, bf16[2,1024,256]{2,1,0:T(8,128)(2,1)} %get-tuple-element.12), kind=kLoop, calls=%fused_computation | loop fusion | flops 1572864 | bytes 4194304 | tf_op jit(solution)/shard_map/add | solution.py:224
  34.6 0.1 slice.23
  34.7 0.0 copy-start
  34.7 1.6 %collective-permute-start.8 = (bf16[1,1024,256]{2,1,0:T(8,128)(2,1)S(1)}, bf16[1,1024,256]{2,1,0:T(8,128)(2,1)S(1)}, u32[]{:S(2)}, u32[]{:S(2)}) collective-permute-start(bf16[1,1024,256]{2,1,0:T(8,128)(2,1)S(1)} %slice.23), channel_id=1, source_target_pairs={{0,16},{8,24},{16,0},{24,8},{1,17},{9,25},{17,1},{25,9},{2,18},{10... | collective-permute-start | bytes 1572872 | tf_op jit(solution)/shard_map/ppermute | solution.py:24
  36.2 12.5 %collective-permute-done.8 = bf16[1,1024,256]{2,1,0:T(8,128)(2,1)S(1)} collective-permute-done((bf16[1,1024,256]{2,1,0:T(8,128)(2,1)S(1)}, bf16[1,1024,256]{2,1,0:T(8,128)(2,1)S(1)}, u32[]{:S(2)}, u32[]{:S(2)}) %collective-permute-start.8) | collective-permute-done | bytes 524320 | tf_op jit(solution)/shard_map/ppermute | solution.py:24
  48.7 1.7 %fusion.2 = (bf16[1024,256]{1,0:T(8,128)(2,1)S(1)}, f32[1024,256]{1,0:T(8,128)}, f32[1024,256]{1,0:T(8,128)}) fusion(f32[1024,256]{1,0:T(8,128)S(1)} %copy-done.5, bf16[1,1024,256]{2,1,0:T(8,128)(2,1)S(1)} %collective-permute-done.8, f32[2,1024,256]{2,1,0:T(8,128)S(1)} %convert_add_fusion, f32[1024,256]{1,0:T(8,128)S(1)} %copy-done.6), kind=kLoop, calls=%fused_computation.8 | loop fusion | flops 2621440 | bytes 6291456 | tf_op jit(solution)/shard_map/convert_element_type | solution.py:233
  50.4 1.5 %collective-permute-start.10 = (bf16[1024,256]{1,0:T(8,128)(2,1)S(1)}, bf16[1024,256]{1,0:T(8,128)(2,1)S(1)}, u32[]{:S(2)}, u32[]{:S(2)}) collective-permute-start(bf16[1024,256]{1,0:T(8,128)(2,1)S(1)} %get-tuple-element.15.refs_9_), channel_id=1, source_target_pairs={{0,16},{8,24},{16,0},{24,8},{1,17},{9,25},{17,1},{25,9},{2,18},{10... | collective-permute-start | bytes 1572872 | tf_op jit(solution)/shard_map/ppermute | solution.py:24
  51.9 2.0 %collective-permute-start.5 = (bf16[128,1024]{1,0:T(8,128)(2,1)S(1)}, bf16[128,1024]{1,0:T(8,128)(2,1)S(1)}, u32[]{:S(2)}, u32[]{:S(2)}) collective-permute-start(bf16[128,1024]{1,0:T(8,128)(2,1)S(1)} %collective-permute-done.2.refs_5_), channel_id=1, source_target_pairs={{0,2},{1,3},{2,0},{3,1},{4,6},{5,7},{6,4},{7,5},{8,10},{9,11},{10,... | collective-permute-start | bytes 786440 | tf_op jit(solution)/shard_map/ppermute | solution.py:24
  53.9 1.5 %collective-permute-start.4 = (bf16[128,1024]{1,0:T(8,128)(2,1)S(1)}, bf16[128,1024]{1,0:T(8,128)(2,1)S(1)}, u32[]{:S(2)}, u32[]{:S(2)}) collective-permute-start(bf16[128,1024]{1,0:T(8,128)(2,1)S(1)} %collective-permute-done.2.refs_5_), channel_id=1, source_target_pairs={{0,1},{1,0},{2,3},{3,2},{4,5},{5,4},{6,7},{7,6},{8,9},{9,8},{10,11... | collective-permute-start | bytes 786440 | tf_op jit(solution)/shard_map/ppermute | solution.py:24
  55.4 0.6 collective-permute-start.3
  55.9 7.6 %collective-permute-done.5.refs_7_ = bf16[128,1024]{1,0:T(8,128)(2,1)S(1)} collective-permute-done((bf16[128,1024]{1,0:T(8,128)(2,1)S(1)}, bf16[128,1024]{1,0:T(8,128)(2,1)S(1)}, u32[]{:S(2)}, u32[]{:S(2)}) %collective-permute-start.5) | collective-permute-done | bytes 262176 | tf_op jit(solution)/shard_map/ppermute | solution.py:24
  63.5 3.1 %collective-permute-done.4.refs_6_ = bf16[128,1024]{1,0:T(8,128)(2,1)S(1)} collective-permute-done((bf16[128,1024]{1,0:T(8,128)(2,1)S(1)}, bf16[128,1024]{1,0:T(8,128)(2,1)S(1)}, u32[]{:S(2)}, u32[]{:S(2)}) %collective-permute-start.4) | collective-permute-done | bytes 262176 | tf_op jit(solution)/shard_map/ppermute | solution.py:24
  66.6 0.7 copy-done.1
  67.3 2.7 %collective-permute-done.3.refs_4_ = bf16[128,1024]{1,0:T(8,128)(2,1)S(1)} collective-permute-done((bf16[128,1024]{1,0:T(8,128)(2,1)S(1)}, bf16[128,1024]{1,0:T(8,128)(2,1)S(1)}, u32[]{:S(2)}, u32[]{:S(2)}) %collective-permute-start.3) | collective-permute-done | bytes 262176 | tf_op jit(solution)/shard_map/ppermute | solution.py:24
  70.0 0.7 copy-done.3
  70.7 2.5 %collective-permute-start.6 = (bf16[128,1024]{1,0:T(8,128)(2,1)S(1)}, bf16[128,1024]{1,0:T(8,128)(2,1)}, u32[]{:S(2)}, u32[]{:S(2)}) collective-permute-start(bf16[128,1024]{1,0:T(8,128)(2,1)S(1)} %collective-permute-done.5.refs_7_), channel_id=1, source_target_pairs={{0,1},{1,0},{2,3},{3,2},{4,5},{5,4},{6,7},{7,6},{8,9},{9,8},{10,11... | collective-permute-start | bytes 786440 | tf_op jit(solution)/shard_map/ppermute | solution.py:24
  73.2 0.1 pad_add_fusion.place_ref
  73.3 7.0 %collective-permute-done.6.refs_8_ = bf16[128,1024]{1,0:T(8,128)(2,1)} collective-permute-done((bf16[128,1024]{1,0:T(8,128)(2,1)S(1)}, bf16[128,1024]{1,0:T(8,128)(2,1)}, u32[]{:S(2)}, u32[]{:S(2)}) %collective-permute-start.6) | collective-permute-done | bytes 262176 | tf_op jit(solution)/shard_map/ppermute | solution.py:24
  80.3 0.9 %copy-done.2 = bf16[128,1024]{1,0:T(8,128)(2,1)S(1)} copy-done((bf16[128,1024]{1,0:T(8,128)(2,1)S(1)}, bf16[128,1024]{1,0:T(8,128)(2,1)}, u32[]{:S(2)}) %copy-start.2) | copy-done | bytes 262168
  81.3 0.9 %copy-done.4 = bf16[128,1024]{1,0:T(8,128)(2,1)S(1)} copy-done((bf16[128,1024]{1,0:T(8,128)(2,1)S(1)}, bf16[128,1024]{1,0:T(8,128)(2,1)}, u32[]{:S(2)}) %copy-start.4) | copy-done | bytes 262168
  82.2 7.0 %mix.1 = bf16[1024,1024]{1,0:T(8,128)(2,1)} custom-call(s32[2]{0:T(128)S(1)} %pad_add_fusion.place_ref, bf16[8,1024,128]{2,1,0:T(8,128)(2,1)} %all-to-all-done.refs_0_, bf16[128,1024]{1,0:T(8,128)(2,1)S(1)} %bitcast.18, bf16[128,1024]{1,0:T(8,128)(2,1)S(1)} %collective-permute-done.refs_2_, bf16[128,1024]{1,0:T(8,128)(2,1)S(1)} %collective-permute-done.1.refs_3_, ...), custom_call_target="tpu_custom_call" | custom-call | flops 2147483648 | bytes 10485760 | tf_op jit(solution)/shard_map/mix/pallas_call | solution.py:165
  (16 shorter events, 0.0 us)
Async XLA Ops:
  0.6 16.3 %collective-permute-start.2 = (bf16[128,1024]{1,0:T(8,128)(2,1)}, bf16[128,1024]{1,0:T(8,128)(2,1)S(1)}, u32[]{:S(2)}, u32[]{:S(2)}) collective-permute-start(bf16[128,1024]{1,0:T(8,128)(2,1)} %bitcast.15), channel_id=1, source_target_pairs={{0,4},{1,5},{2,6},{3,7},{4,0},{5,1},{6,2},{7,3},{8,12},{9,13},{10,... | collective-permute-start | bytes 786440 | tf_op jit(solution)/shard_map/ppermute | solution.py:24
  4.7 12.4 %collective-permute-start.1 = (bf16[128,1024]{1,0:T(8,128)(2,1)}, bf16[128,1024]{1,0:T(8,128)(2,1)S(1)}, u32[]{:S(2)}, u32[]{:S(2)}) collective-permute-start(bf16[128,1024]{1,0:T(8,128)(2,1)} %bitcast.16), channel_id=1, source_target_pairs={{0,2},{1,3},{2,0},{3,1},{4,6},{5,7},{6,4},{7,5},{8,10},{9,11},{10,... | collective-permute-start | bytes 786440 | tf_op jit(solution)/shard_map/ppermute | solution.py:24
  6.3 10.9 %collective-permute-start = (bf16[128,1024]{1,0:T(8,128)(2,1)}, bf16[128,1024]{1,0:T(8,128)(2,1)S(1)}, u32[]{:S(2)}, u32[]{:S(2)}) collective-permute-start(bf16[128,1024]{1,0:T(8,128)(2,1)} %bitcast.17), channel_id=1, source_target_pairs={{0,1},{1,0},{2,3},{3,2},{4,5},{5,4},{6,7},{7,6},{8,9},{9,8},{10,11... | collective-permute-start | bytes 786440 | tf_op jit(solution)/shard_map/ppermute | solution.py:24
  17.2 63.1 %all-to-all-start = ((bf16[8,1024,128]{2,1,0:T(8,128)(2,1)}), bf16[8,1024,128]{2,1,0:T(8,128)(2,1)}, u32[]{:S(2)}, u32[]{:S(2)}) async-start(bf16[8,1024,128]{2,1,0:T(8,128)(2,1)} %prepare.1), calls=%async_computation | async-start | bytes 4194304 | tf_op jit(solution)/shard_map/all_to_all | solution.py:221
  30.1 2.9 %collective-permute-start.7 = (bf16[2,1024,256]{2,1,0:T(8,128)(2,1)}, bf16[2,1024,256]{2,1,0:T(8,128)(2,1)S(1)}, u32[]{:S(2)}, u32[]{:S(2)}) collective-permute-start(bf16[2,1024,256]{2,1,0:T(8,128)(2,1)} %get-tuple-element.13), channel_id=1, source_target_pairs={{0,8},{8,0},{16,24},{24,16},{1,9},{9,1},{17,25},{25,17},{2,10},{10... | collective-permute-start | bytes 3145736 | tf_op jit(solution)/shard_map/ppermute | solution.py:24
  33.0 15.8 %copy-start.5 = (f32[1024,256]{1,0:T(8,128)S(1)}, f32[1024,256]{1,0:T(8,128)}, u32[]{:S(2)}) copy-start(f32[1024,256]{1,0:T(8,128)} %param.12) | copy-start | bytes 3145732
  33.0 15.8 %copy-start.6 = (f32[1024,256]{1,0:T(8,128)S(1)}, f32[1024,256]{1,0:T(8,128)}, u32[]{:S(2)}) copy-start(f32[1024,256]{1,0:T(8,128)} %param.13) | copy-start | bytes 3145732
  34.7 45.6 %copy-start = (bf16[1,128,1024]{2,1,0:T(8,128)(2,1)S(1)}, bf16[1,128,1024]{2,1,0:T(8,128)(2,1)}, u32[]{:S(2)}) copy-start(bf16[1,128,1024]{2,1,0:T(8,128)(2,1)} %param.9) | copy-start | bytes 786436
  34.7 14.0 %collective-permute-start.8 = (bf16[1,1024,256]{2,1,0:T(8,128)(2,1)S(1)}, bf16[1,1024,256]{2,1,0:T(8,128)(2,1)S(1)}, u32[]{:S(2)}, u32[]{:S(2)}) collective-permute-start(bf16[1,1024,256]{2,1,0:T(8,128)(2,1)S(1)} %slice.23), channel_id=1, source_target_pairs={{0,16},{8,24},{16,0},{24,8},{1,17},{9,25},{17,1},{25,9},{2,18},{10... | collective-permute-start | bytes 1572872 | tf_op jit(solution)/shard_map/ppermute | solution.py:24
  50.4 20.4 %collective-permute-start.10 = (bf16[1024,256]{1,0:T(8,128)(2,1)S(1)}, bf16[1024,256]{1,0:T(8,128)(2,1)S(1)}, u32[]{:S(2)}, u32[]{:S(2)}) collective-permute-start(bf16[1024,256]{1,0:T(8,128)(2,1)S(1)} %get-tuple-element.15.refs_9_), channel_id=1, source_target_pairs={{0,16},{8,24},{16,0},{24,8},{1,17},{9,25},{17,1},{25,9},{2,18},{10... | collective-permute-start | bytes 1572872 | tf_op jit(solution)/shard_map/ppermute | solution.py:24
  51.9 11.6 %collective-permute-start.5 = (bf16[128,1024]{1,0:T(8,128)(2,1)S(1)}, bf16[128,1024]{1,0:T(8,128)(2,1)S(1)}, u32[]{:S(2)}, u32[]{:S(2)}) collective-permute-start(bf16[128,1024]{1,0:T(8,128)(2,1)S(1)} %collective-permute-done.2.refs_5_), channel_id=1, source_target_pairs={{0,2},{1,3},{2,0},{3,1},{4,6},{5,7},{6,4},{7,5},{8,10},{9,11},{10,... | collective-permute-start | bytes 786440 | tf_op jit(solution)/shard_map/ppermute | solution.py:24
  53.9 12.7 %collective-permute-start.4 = (bf16[128,1024]{1,0:T(8,128)(2,1)S(1)}, bf16[128,1024]{1,0:T(8,128)(2,1)S(1)}, u32[]{:S(2)}, u32[]{:S(2)}) collective-permute-start(bf16[128,1024]{1,0:T(8,128)(2,1)S(1)} %collective-permute-done.2.refs_5_), channel_id=1, source_target_pairs={{0,1},{1,0},{2,3},{3,2},{4,5},{5,4},{6,7},{7,6},{8,9},{9,8},{10,11... | collective-permute-start | bytes 786440 | tf_op jit(solution)/shard_map/ppermute | solution.py:24
  55.4 14.7 %collective-permute-start.3 = (bf16[128,1024]{1,0:T(8,128)(2,1)S(1)}, bf16[128,1024]{1,0:T(8,128)(2,1)S(1)}, u32[]{:S(2)}, u32[]{:S(2)}) collective-permute-start(bf16[128,1024]{1,0:T(8,128)(2,1)S(1)} %collective-permute-done.1.refs_3_), channel_id=1, source_target_pairs={{0,1},{1,0},{2,3},{3,2},{4,5},{5,4},{6,7},{7,6},{8,9},{9,8},{10,11... | collective-permute-start | bytes 786440 | tf_op jit(solution)/shard_map/ppermute | solution.py:24
  55.9 24.4 %collective-permute-start.9 = (bf16[1024,256]{1,0:T(8,128)(2,1)S(1)}, bf16[1024,256]{1,0:T(8,128)(2,1)S(1)}, u32[]{:S(2)}, u32[]{:S(2)}) collective-permute-start(bf16[1024,256]{1,0:T(8,128)(2,1)S(1)} %get-tuple-element.15.refs_9_), channel_id=1, source_target_pairs={{0,8},{8,0},{16,24},{24,16},{1,9},{9,1},{17,25},{25,17},{2,10},{10... | collective-permute-start | bytes 1572872 | tf_op jit(solution)/shard_map/ppermute | solution.py:24
  66.6 0.7 copy-start.1
  70.0 0.7 copy-start.3
  70.7 9.6 %collective-permute-start.11 = (bf16[1024,256]{1,0:T(8,128)(2,1)S(1)}, bf16[1024,256]{1,0:T(8,128)(2,1)S(1)}, u32[]{:S(2)}, u32[]{:S(2)}) collective-permute-start(bf16[1024,256]{1,0:T(8,128)(2,1)S(1)} %collective-permute-done.10.refs_11_), channel_id=1, source_target_pairs={{0,8},{8,0},{16,24},{24,16},{1,9},{9,1},{17,25},{25,17},{2,10},{10... | collective-permute-start | bytes 1572872 | tf_op jit(solution)/shard_map/ppermute | solution.py:24
  70.7 9.6 %collective-permute-start.6 = (bf16[128,1024]{1,0:T(8,128)(2,1)S(1)}, bf16[128,1024]{1,0:T(8,128)(2,1)}, u32[]{:S(2)}, u32[]{:S(2)}) collective-permute-start(bf16[128,1024]{1,0:T(8,128)(2,1)S(1)} %collective-permute-done.5.refs_7_), channel_id=1, source_target_pairs={{0,1},{1,0},{2,3},{3,2},{4,5},{5,4},{6,7},{7,6},{8,9},{9,8},{10,11... | collective-permute-start | bytes 786440 | tf_op jit(solution)/shard_map/ppermute | solution.py:24
  80.3 1.0 %copy-start.2 = (bf16[128,1024]{1,0:T(8,128)(2,1)S(1)}, bf16[128,1024]{1,0:T(8,128)(2,1)}, u32[]{:S(2)}) copy-start(bf16[128,1024]{1,0:T(8,128)(2,1)} %copy-done.1) | copy-start | bytes 786436
  81.3 0.9 %copy-start.4 = (bf16[128,1024]{1,0:T(8,128)(2,1)S(1)}, bf16[128,1024]{1,0:T(8,128)(2,1)}, u32[]{:S(2)}) copy-start(bf16[128,1024]{1,0:T(8,128)(2,1)} %copy-done.3) | copy-start | bytes 786436

commit v8 on v7

v8 whole, which is shorter than its diff:
```python
import functools
import math

import jax
import jax.numpy as jnp
from jax import lax
from jax.experimental import pallas as pl
from jax.experimental.pallas import tpu as pltpu
from jax.sharding import PartitionSpec as P

BLOCK = 64


norm_eps = 1e-05
inner_gain = 0.4
outer_rate = 0.7
outer_beta = 0.9
mix_weight = 0.5
code_range = 448.0


def swap(value, axis, mask):
    size = lax.axis_size(axis)
    return lax.ppermute(value, axis, [(i, i ^ mask) for i in range(size)])


def prepare_kernel(tokens_ref, gain_ref, blocks_ref, tokens, blocks, load_sems, store_sems):
    lanes = 128
    shards, rows, count = blocks.shape
    features = shards * rows
    loads, stores = [], []
    for k in range(shards):
        columns = pl.ds(k * rows, rows)
        loads.append(pltpu.make_async_copy(tokens_ref.at[:, columns], tokens.at[:, columns], load_sems.at[k]))
        loads[k].start()
        stores.append(pltpu.make_async_copy(blocks.at[k], blocks_ref.at[k], store_sems.at[k]))
    squares = jnp.zeros((count, lanes), jnp.float32)
    for k in range(shards):
        loads[k].wait()
        for start in range(k * rows, (k + 1) * rows, lanes):
            block = tokens[:, start : start + lanes].astype(jnp.float32)
            squares = squares + block * block
    mean = jnp.sum(squares, axis=-1, keepdims=True) / features
    inverse = jnp.broadcast_to(lax.rsqrt(mean + norm_eps), (count, lanes))
    for k in range(shards):
        for start in range(0, rows, lanes):
            columns = slice(k * rows + start, k * rows + start + lanes)
            normed = tokens[:, columns].astype(jnp.float32) * inverse * gain_ref[:, columns]
            blocks[k, start : start + lanes] = jnp.transpose(normed).astype(jnp.bfloat16)
        stores[k].start()
    for store in stores:
        store.wait()


def prepare(tokens, gain, shards):
    count, features = tokens.shape
    rows = features // shards
    return pl.pallas_call(
        prepare_kernel,
        out_shape=jax.ShapeDtypeStruct((shards, rows, count), jnp.bfloat16),
        in_specs=[pl.BlockSpec(memory_space=pltpu.HBM), pl.BlockSpec(memory_space=pltpu.VMEM)],
        out_specs=pl.BlockSpec(memory_space=pltpu.HBM),
        scratch_shapes=[
            pltpu.VMEM((count, features), jnp.bfloat16),
            pltpu.VMEM((shards, rows, count), jnp.bfloat16),
            pltpu.SemaphoreType.DMA((shards,)),
            pltpu.SemaphoreType.DMA((shards,)),
        ],
        compiler_params=pltpu.CompilerParams(vmem_limit_bytes=16 * 2**20),
        cost_estimate=pl.CostEstimate(
            flops=5 * count * features, bytes_accessed=4 * count * features, transcendentals=count
        ),
        name="prepare",
    )(tokens, gain.astype(jnp.float32).reshape(1, features))


def code_kernel(own_ref, shared_ref, weight_ref, kept_ref, sent_ref, shared, weight, decoded, sems):
    lanes = 2 * BLOCK
    groups, tile, share = decoded.shape
    rows, width = shared.shape
    own = own_ref[0]
    low = lax.broadcasted_iota(jnp.int32, (tile, lanes), 1) < BLOCK

    def loads(i):
        part = pl.ds(pl.multiple_of(i * tile, tile), tile)
        return (
            pltpu.make_async_copy(shared_ref.at[part], shared.at[part], sems.at[0, i]),
            pltpu.make_async_copy(weight_ref.at[part], weight.at[part], sems.at[1, i]),
        )

    for i in range(rows // tile):
        for load in loads(i):
            load.start()

    def step(i, _):
        for load in loads(i):
            load.wait()
        part = pl.ds(pl.multiple_of(i * tile, tile), tile)
        for start in range(0, width, lanes):
            columns = slice(start, start + lanes)
            delta = shared[part, columns].astype(jnp.float32) - weight[part, columns].astype(jnp.float32)
            size = jnp.abs(delta)
            largest = jnp.where(
                low,
                jnp.max(jnp.where(low, size, 0.0), axis=-1, keepdims=True),
                jnp.max(jnp.where(low, 0.0, size), axis=-1, keepdims=True),
            )
            scale = ((largest + 1e-06) * (1.0 / code_range)).astype(jnp.bfloat16).astype(jnp.float32)
            coded = (delta * pl.reciprocal(scale)).astype(jnp.bfloat16)
            value = (coded.astype(jnp.float32) * scale).astype(jnp.bfloat16)
            piece = min(share, lanes)
            for at in range(0, lanes, piece):
                group, offset = divmod(start + at, share)
                decoded[group, :, offset : offset + piece] = value[:, at : at + piece]
        for k in range(0, groups, 2):
            kept_ref[k // 2, part] = decoded[own ^ k]
            sent_ref[k // 2, part] = decoded[own ^ (k + 1)]
        return 0

    lax.fori_loop(0, rows // tile, step, 0)


def code_and_decode(own, shared, weight, groups):
    rows, width = shared.shape
    tile = min(rows, 128)
    share = width // groups
    half = jax.ShapeDtypeStruct((groups // 2, rows, share), jnp.bfloat16)
    return pl.pallas_call(
        code_kernel,
        out_shape=(half, half),
        in_specs=[pl.BlockSpec(memory_space=pltpu.SMEM)] + [pl.BlockSpec(memory_space=pltpu.HBM)] * 2,
        out_specs=(pl.BlockSpec(memory_space=pltpu.VMEM),) * 2,
        scratch_shapes=[
            pltpu.VMEM((rows, width), jnp.bfloat16),
            pltpu.VMEM((rows, width), jnp.bfloat16),
            pltpu.VMEM((groups, tile, share), jnp.bfloat16),
            pltpu.SemaphoreType.DMA((2, rows // tile)),
        ],
        compiler_params=pltpu.CompilerParams(vmem_limit_bytes=16 * 2**20),
        cost_estimate=pl.CostEstimate(flops=20 * rows * width, bytes_accessed=6 * rows * width, transcendentals=0),
        name="code_and_decode",
    )(own.reshape(1), shared, weight)


def mix_kernel(shards, groups, rate, place_ref, *refs):
    tokens_ref, refs = refs[0], refs[1:]
    cotangent_refs, refs = refs[:shards], refs[shards:]
    piece_refs, refs = refs[:groups], refs[groups:]
    weight_ref, out_ref, cotangents, pieces, outs, out_sems = refs
    mine, own = place_ref[0], place_ref[1]
    depth, width = cotangent_refs[0].shape
    share = pieces.shape[2]
    tile = outs.shape[2]
    for k, ref in enumerate(cotangent_refs):
        cotangents[mine ^ k] = ref[...]
    for k, ref in enumerate(piece_refs):
        pieces[own ^ k] = ref[...]
    left = jnp.concatenate([tokens_ref[k] for k in range(shards)], axis=1)
    stores = []
    for step in range(width // tile):
        columns = slice(step * tile, (step + 1) * tile)
        right = jnp.concatenate([cotangents[k, :, columns] for k in range(shards)], axis=0)
        total = jnp.dot(left, right, preferred_element_type=jnp.float32)
        for group in range(step * tile // share, (step + 1) * tile // share):
            place = slice(group * share, (group + 1) * share)
            part = slice(group * share - step * tile, (group + 1) * share - step * tile)
            mixed = weight_ref[:, place].astype(jnp.float32) + pieces[group].astype(jnp.float32)
            outs[step, :, part] = (mix_weight * mixed - rate * total[:, part]).astype(jnp.bfloat16)
        stores.append(pltpu.make_async_copy(outs.at[step], out_ref.at[:, pl.ds(step * tile, tile)], out_sems.at[step]))
        stores[-1].start()
    for store in stores:
        store.wait()


def mix(mine, own, tokens, cotangents, pieces, weight, rate):
    shards, rows, depth = tokens.shape
    width = weight.shape[1]
    groups = len(pieces)
    share = width // groups
    tile = max(share, 256)
    return pl.pallas_call(
        functools.partial(mix_kernel, shards, groups, rate),
        out_shape=jax.ShapeDtypeStruct((rows, width), jnp.bfloat16),
        in_specs=[pl.BlockSpec(memory_space=pltpu.SMEM)]
        + [pl.BlockSpec(memory_space=pltpu.VMEM)] * (2 + shards + groups),
        out_specs=pl.BlockSpec(memory_space=pltpu.HBM),
        scratch_shapes=[
            pltpu.VMEM((shards, depth, width), jnp.bfloat16),
            pltpu.VMEM((groups, rows, share), jnp.bfloat16),
            pltpu.VMEM((width // tile, rows, tile), jnp.bfloat16),
            pltpu.SemaphoreType.DMA((width // tile,)),
        ],
        compiler_params=pltpu.CompilerParams(vmem_limit_bytes=24 * 2**20),
        cost_estimate=pl.CostEstimate(
            flops=2 * depth * shards * rows * width,
            bytes_accessed=2 * depth * shards * (rows + width) + 6 * rows * width,
            transcendentals=0,
        ),
        name="mix",
    )(jnp.stack([mine, own]), tokens, *cotangents, *pieces, weight)


def gather(piece, axis, size, after=()):
    pieces = {0: piece}
    bit = size // 2
    while bit:
        if bit == 1 and after:
            (*held, _) = lax.optimization_barrier((*(pieces[k] for k in sorted(pieces)[1:]), after))
            pieces.update(zip(sorted(pieces)[1:], held))
        for k in sorted(pieces):
            pieces[k ^ bit] = swap(pieces[k], axis, bit)
        bit //= 2
    return [pieces[k] for k in range(size)]


def on_device(tokens, norm_gain, cotangent, layer_weight, shared_copy, master, momentum):
    tokens, cotangent, weight = tokens[0], cotangent[0], layer_weight[0]
    shards = lax.axis_size("fsdp")
    groups = lax.axis_size("replica")
    mine = lax.axis_index("fsdp")
    own = lax.axis_index("replica")
    rows, width = weight.shape
    inner_rate = inner_gain / math.sqrt(tokens.shape[0] * shards)

    own_exchanges = [1 << bit for bit in range(shards.bit_length() - 1)]
    cotangents = gather(cotangent, "fsdp", shards)
    blocks = prepare(tokens, norm_gain, shards)
    *_, blocks, coded_shared, coded_weight = lax.optimization_barrier(
        (*(cotangents[k] for k in own_exchanges), blocks, shared_copy, weight)
    )
    columns = lax.all_to_all(blocks, "fsdp", split_axis=0, concat_axis=0, tiled=True)

    kept, sent = code_and_decode(own, coded_shared, coded_weight, groups)
    total = kept.astype(jnp.float32) + swap(sent, "replica", 1).astype(jnp.float32)
    bit = 2
    while bit < groups:
        sent = swap(total[1::2].astype(jnp.bfloat16), "replica", bit)
        bit *= 2
        if bit >= groups:
            *_, sent = lax.optimization_barrier((*cotangents[: shards // 2 + 2], sent))
        total = total[0::2] + sent.astype(jnp.float32)
    average = total[0] / groups
    momentum_next = outer_beta * momentum + average
    master_next = master - outer_rate * (average + outer_beta * momentum_next)
    pieces = gather(master_next.astype(jnp.bfloat16), "replica", groups, after=cotangents)

    layer_next = mix(mine, own, columns, cotangents, pieces, weight, (1.0 - mix_weight) * inner_rate)
    return (layer_next[None], master_next, momentum_next)


def solution(mesh):
    in_specs = (
        P("replica", "fsdp", None),
        P(),
        P("replica", "fsdp", None),
        P("replica", "fsdp", None),
        P("fsdp", None),
        P("fsdp", "replica"),
        P("fsdp", "replica"),
    )
    out_specs = (P("replica", "fsdp", None), P("fsdp", "replica"), P("fsdp", "replica"))
    return jax.shard_map(
        on_device, mesh=mesh, in_specs=in_specs, out_specs=out_specs, check_vma=False
    )
```

time: 89.7 us -> 91.5 us (1.020); the launches traced: 89.3 us -> 89.8 us
  Pallas kernels: 20.2 us -> 11.6 us
  local copies, waits for them, and re-layouts: 3.38 us -> 11.8 us
  waiting for transfers between devices: 38.1 us -> 41.8 us
  other arithmetic: 4.7 us -> 2.68 us
  starting transfers between devices: 22.3 us -> 21.2 us
    unnamed x14 -> x36, local copies, waits for them, and re-layouts: 3.33 us -> 11.7 us
    pallas_call x1, Pallas kernels: 7.46 us -> 3.69 us  [code_and_decode(): pl.pallas_call(code_kernel, out_shape=(half, half), in_specs=[pl.BlockSpe...]
    ppermute x12, waiting for transfers between devices: 38.1 us -> 41.8 us  [swap(): return lax.ppermute(value, axis, [(i, i ^ mask) for i in range(size)])]
    pallas_call x1, Pallas kernels: 5.69 us -> 2.21 us  [prepare(): pl.pallas_call(prepare_kernel, out_shape=jax.ShapeDtypeStruct((shards, ro...]
    add x1, other arithmetic: 1.64 us -> 0.23 us  [on_device(): kept.astype(jnp.float32) + swap(sent, 'replica', 1).astype(jnp.float32)]
    ppermute x12, starting transfers between devices: 16.8 us -> 15.4 us  [swap(): return lax.ppermute(value, axis, [(i, i ^ mask) for i in range(size)])]
    pallas_call x1, Pallas kernels: 7.03 us -> 5.73 us  [mix(): pl.pallas_call(functools.partial(mix_kernel, shards, groups, rate), out_s...]
  transfers between devices with their start and end apart: 13 -> 13, of which waited for: 8 -> 9; matrix products, arithmetic and copies ran while one was open for 5% -> 3% of each run, Pallas kernels for 15% -> 7%
where the time goes in v8:
time: 91.5 us; the launch traced here: 89.8 us
  waiting for transfers between devices  41.8 us (46%)
  starting transfers between devices  21.2 us (23%)
  local copies, waits for them, and re-layouts  11.8 us (13%)
  Pallas kernels  11.6 us (13%)
  other arithmetic  2.68 us (3%)
    ppermute x12, waiting for transfers between devices, swap(): return lax.ppermute(value, axis, [(i, i ^ mask) for i in range(size)])  41.8 us
    ppermute x12, starting transfers between devices, swap(): return lax.ppermute(value, axis, [(i, i ^ mask) for i in range(size)])  15.4 us
    unnamed x36, local copies, waits for them, and re-layouts  11.7 us
    pallas_call x1, Pallas kernels, mix(): pl.pallas_call(functools.partial(mix_kernel, shards, groups, rate), out_s...  5.73 us
    all_to_all x1, starting transfers between devices, on_device(): lax.all_to_all(blocks, 'fsdp', split_axis=0, concat_axis=0, tiled=True)  5.71 us
    pallas_call x1, Pallas kernels, code_and_decode(): pl.pallas_call(code_kernel, out_shape=(half, half), in_specs=[pl.BlockSpe...  3.69 us
    pallas_call x1, Pallas kernels, prepare(): pl.pallas_call(prepare_kernel, out_shape=jax.ShapeDtypeStruct((shards, ro...  2.21 us
  transfers between devices with their start and end apart: 13, of which 9 were waited for; matrix products, arithmetic and copies ran while one was open for 3% of the time, Pallas kernels for 7%

profile of v8, /device:TPU:0, one launch (start us, length us, event | category | flops | bytes accessed | tf_op | source)
XLA Modules:
  0.0 89.8 jit_solution(5986759978280186971)
XLA Ops:
  0.6 4.1 %collective-permute-start.2 = (bf16[128,1024]{1,0:T(8,128)(2,1)}, bf16[128,1024]{1,0:T(8,128)(2,1)}, u32[]{:S(2)}, u32[]{:S(2)}) collective-permute-start(bf16[128,1024]{1,0:T(8,128)(2,1)} %bitcast.18), channel_id=1, source_target_pairs={{0,4},{1,5},{2,6},{3,7},{4,0},{5,1},{6,2},{7,3},{8,12},{9,13},{10,... | collective-permute-start | bytes 786440 | tf_op jit(solution)/shard_map/ppermute | solution.py:24
  4.7 1.6 %collective-permute-start.1 = (bf16[128,1024]{1,0:T(8,128)(2,1)}, bf16[128,1024]{1,0:T(8,128)(2,1)S(1)}, u32[]{:S(2)}, u32[]{:S(2)}) collective-permute-start(bf16[128,1024]{1,0:T(8,128)(2,1)} %bitcast.19), channel_id=1, source_target_pairs={{0,2},{1,3},{2,0},{3,1},{4,6},{5,7},{6,4},{7,5},{8,10},{9,11},{10,... | collective-permute-start | bytes 786440 | tf_op jit(solution)/shard_map/ppermute | solution.py:24
  6.3 1.5 %collective-permute-start = (bf16[128,1024]{1,0:T(8,128)(2,1)}, bf16[128,1024]{1,0:T(8,128)(2,1)S(1)}, u32[]{:S(2)}, u32[]{:S(2)}) collective-permute-start(bf16[128,1024]{1,0:T(8,128)(2,1)} %bitcast.20), channel_id=1, source_target_pairs={{0,1},{1,0},{2,3},{3,2},{4,5},{5,4},{6,7},{7,6},{8,9},{9,8},{10,11... | collective-permute-start | bytes 786440 | tf_op jit(solution)/shard_map/ppermute | solution.py:24
  7.8 0.7 reshape.16
  8.6 1.6 %copy-done.1 = bf16[1,128,8192]{2,1,0:T(8,128)(2,1)S(1)} copy-done((bf16[1,128,8192]{2,1,0:T(8,128)(2,1)S(1)}, bf16[1,128,8192]{2,1,0:T(8,128)(2,1)}, u32[]{:S(2)}) %copy-start.1) | copy-done | bytes 2097176
  10.1 2.2 %prepare.1 = bf16[8,1024,128]{2,1,0:T(8,128)(2,1)} custom-call(bf16[128,8192]{1,0:T(8,128)(2,1)S(1)} %bitcast.17, f32[1,8192]{1,0:T(1,128)S(1)} %bitcast.22), custom_call_target="tpu_custom_call" | custom-call | flops 5242880 | bytes 4194304 | tf_op jit(solution)/shard_map/prepare/pallas_call | solution.py:58
  12.4 4.7 %collective-permute-done.2.refs_5_ = bf16[128,1024]{1,0:T(8,128)(2,1)} collective-permute-done((bf16[128,1024]{1,0:T(8,128)(2,1)}, bf16[128,1024]{1,0:T(8,128)(2,1)}, u32[]{:S(2)}, u32[]{:S(2)}) %collective-permute-start.2) | collective-permute-done | bytes 262176 | tf_op jit(solution)/shard_map/ppermute | solution.py:24
  17.2 0.7 copy-done.6
  17.9 5.7 %all-to-all-start = ((bf16[8,1024,128]{2,1,0:T(8,128)(2,1)}), bf16[8,1024,128]{2,1,0:T(8,128)(2,1)}, u32[]{:S(2)}, u32[]{:S(2)}) async-start(bf16[8,1024,128]{2,1,0:T(8,128)(2,1)} %prepare.1), calls=%async_computation | async-start | bytes 4194304 | tf_op jit(solution)/shard_map/all_to_all | solution.py:231
  23.6 1.6 %copy-done.2 = bf16[1024,1024]{1,0:T(8,128)(2,1)S(1)} copy-done((bf16[1024,1024]{1,0:T(8,128)(2,1)S(1)}, bf16[1024,1024]{1,0:T(8,128)(2,1)}, u32[]{:S(2)}) %copy-start.2) | copy-done | bytes 2097176
  25.2 3.7 %code_and_decode.1 = (bf16[2,1024,256]{2,1,0:T(8,128)(2,1)S(1)}, bf16[2,1024,256]{2,1,0:T(8,128)(2,1)S(1)}) custom-call(s32[1]{0:T(128)} %bitcast.1.own_ref, bf16[1024,1024]{1,0:T(8,128)(2,1)S(1)} %copy-done.2, bf16[1024,1024]{1,0:T(8,128)(2,1)S(1)} %bitcast.15), custom_call_target="tpu_custom_call" | custom-call | flops 20971520 | bytes 6291456 | tf_op jit(solution)/shard_map/code_and_decode/pallas_call | solution.py:128
  29.0 2.6 %collective-permute-done.7 = bf16[2,1024,256]{2,1,0:T(8,128)(2,1)S(1)} collective-permute-done((bf16[2,1024,256]{2,1,0:T(8,128)(2,1)S(1)}, bf16[2,1024,256]{2,1,0:T(8,128)(2,1)S(1)}, u32[]{:S(2)}, u32[]{:S(2)}) %collective-permute-start.7) | collective-permute-done | bytes 1048608 | tf_op jit(solution)/shard_map/ppermute | solution.py:24
  31.9 1.6 %collective-permute-start.8 = (bf16[1,1024,256]{2,1,0:T(8,128)(2,1)S(1)}, bf16[1,1024,256]{2,1,0:T(8,128)(2,1)S(1)}, u32[]{:S(2)}, u32[]{:S(2)}) collective-permute-start(bf16[1,1024,256]{2,1,0:T(8,128)(2,1)S(1)} %slice.23), channel_id=1, source_target_pairs={{0,16},{8,24},{16,0},{24,8},{1,17},{9,25},{17,1},{25,9},{2,18},{10... | collective-permute-start | bytes 1572872 | tf_op jit(solution)/shard_map/ppermute | solution.py:24
  33.5 2.0 %collective-permute-start.4 = (bf16[128,1024]{1,0:T(8,128)(2,1)}, bf16[128,1024]{1,0:T(8,128)(2,1)S(1)}, u32[]{:S(2)}, u32[]{:S(2)}) collective-permute-start(bf16[128,1024]{1,0:T(8,128)(2,1)} %collective-permute-done.2.refs_5_), channel_id=1, source_target_pairs={{0,1},{1,0},{2,3},{3,2},{4,5},{5,4},{6,7},{7,6},{8,9},{9,8},{10,11... | collective-permute-start | bytes 786440 | tf_op jit(solution)/shard_map/ppermute | solution.py:24
  35.6 2.0 %collective-permute-start.5 = (bf16[128,1024]{1,0:T(8,128)(2,1)}, bf16[128,1024]{1,0:T(8,128)(2,1)S(1)}, u32[]{:S(2)}, u32[]{:S(2)}) collective-permute-start(bf16[128,1024]{1,0:T(8,128)(2,1)} %collective-permute-done.2.refs_5_), channel_id=1, source_target_pairs={{0,2},{1,3},{2,0},{3,1},{4,6},{5,7},{6,4},{7,5},{8,10},{9,11},{10,... | collective-permute-start | bytes 786440 | tf_op jit(solution)/shard_map/ppermute | solution.py:24
  37.5 11.1 %collective-permute-done.4.refs_6_ = bf16[128,1024]{1,0:T(8,128)(2,1)S(1)} collective-permute-done((bf16[128,1024]{1,0:T(8,128)(2,1)}, bf16[128,1024]{1,0:T(8,128)(2,1)S(1)}, u32[]{:S(2)}, u32[]{:S(2)}) %collective-permute-start.4) | collective-permute-done | bytes 262176 | tf_op jit(solution)/shard_map/ppermute | solution.py:24
  49.3 11.4 %collective-permute-done.3.refs_4_ = bf16[128,1024]{1,0:T(8,128)(2,1)S(1)} collective-permute-done((bf16[128,1024]{1,0:T(8,128)(2,1)S(1)}, bf16[128,1024]{1,0:T(8,128)(2,1)S(1)}, u32[]{:S(2)}, u32[]{:S(2)}) %collective-permute-start.3) | collective-permute-done | bytes 262176 | tf_op jit(solution)/shard_map/ppermute | solution.py:24
  60.8 1.7 %fusion.2 = (bf16[1024,256]{1,0:T(8,128)(2,1)S(1)}, f32[1024,256]{1,0:T(8,128)}, f32[1024,256]{1,0:T(8,128)}) fusion(f32[1024,256]{1,0:T(8,128)S(1)} %copy-done.16, bf16[1,1024,256]{2,1,0:T(8,128)(2,1)S(1)} %collective-permute-done.8, f32[2,1024,256]{2,1,0:T(8,128)S(1)} %convert_add_fusion, f32[1024,256]{1,0:T(8,128)S(1)} %copy-done.17), kind=kLoop, calls=%fused_computation.8 | loop fusion | flops 2621440 | bytes 6291456 | tf_op jit(solution)/shard_map/convert_element_type | solution.py:245
  62.4 1.4 %collective-permute-start.10 = (bf16[1024,256]{1,0:T(8,128)(2,1)S(1)}, bf16[1024,256]{1,0:T(8,128)(2,1)S(1)}, u32[]{:S(2)}, u32[]{:S(2)}) collective-permute-start(bf16[1024,256]{1,0:T(8,128)(2,1)S(1)} %get-tuple-element.17.refs_9_), channel_id=1, source_target_pairs={{0,16},{8,24},{16,0},{24,8},{1,17},{9,25},{17,1},{25,9},{2,18},{10... | collective-permute-start | bytes 1572872 | tf_op jit(solution)/shard_map/ppermute | solution.py:24
  63.8 0.8 collective-permute-done.5.refs_7_
  64.6 1.2 %collective-permute-start.6 = (bf16[128,1024]{1,0:T(8,128)(2,1)S(1)}, bf16[128,1024]{1,0:T(8,128)(2,1)S(1)}, u32[]{:S(2)}, u32[]{:S(2)}) collective-permute-start(bf16[128,1024]{1,0:T(8,128)(2,1)S(1)} %collective-permute-done.5.refs_7_), channel_id=1, source_target_pairs={{0,1},{1,0},{2,3},{3,2},{4,5},{5,4},{6,7},{7,6},{8,9},{9,8},{10,11... | collective-permute-start | bytes 786440 | tf_op jit(solution)/shard_map/ppermute | solution.py:24
  66.5 5.5 %collective-permute-done.6.refs_8_ = bf16[128,1024]{1,0:T(8,128)(2,1)S(1)} collective-permute-done((bf16[128,1024]{1,0:T(8,128)(2,1)S(1)}, bf16[128,1024]{1,0:T(8,128)(2,1)S(1)}, u32[]{:S(2)}, u32[]{:S(2)}) %collective-permute-start.6) | collective-permute-done | bytes 262176 | tf_op jit(solution)/shard_map/ppermute | solution.py:24
  72.0 0.7 copy-done.14
  72.7 3.6 %collective-permute-done.10.refs_11_ = bf16[1024,256]{1,0:T(8,128)(2,1)S(1)} collective-permute-done((bf16[1024,256]{1,0:T(8,128)(2,1)S(1)}, bf16[1024,256]{1,0:T(8,128)(2,1)S(1)}, u32[]{:S(2)}, u32[]{:S(2)}) %collective-permute-start.10) | collective-permute-done | bytes 524320 | tf_op jit(solution)/shard_map/ppermute | solution.py:24
  76.4 2.0 %collective-permute-done.11.refs_12_ = bf16[1024,256]{1,0:T(8,128)(2,1)} collective-permute-done((bf16[1024,256]{1,0:T(8,128)(2,1)S(1)}, bf16[1024,256]{1,0:T(8,128)(2,1)}, u32[]{:S(2)}, u32[]{:S(2)}) %collective-permute-start.11) | collective-permute-done | bytes 524320 | tf_op jit(solution)/shard_map/ppermute | solution.py:24
  78.3 0.9 %copy-done.5 = bf16[128,1024]{1,0:T(8,128)(2,1)S(1)} copy-done((bf16[128,1024]{1,0:T(8,128)(2,1)S(1)}, bf16[128,1024]{1,0:T(8,128)(2,1)}, u32[]{:S(2)}) %copy-start.5) | copy-done | bytes 262168
  79.3 0.9 %copy-done.7 = bf16[128,1024]{1,0:T(8,128)(2,1)S(1)} copy-done((bf16[128,1024]{1,0:T(8,128)(2,1)S(1)}, bf16[128,1024]{1,0:T(8,128)(2,1)}, u32[]{:S(2)}) %copy-start.7) | copy-done | bytes 262168
  80.2 0.9 %copy-done.9 = bf16[128,1024]{1,0:T(8,128)(2,1)S(1)} copy-done((bf16[128,1024]{1,0:T(8,128)(2,1)S(1)}, bf16[128,1024]{1,0:T(8,128)(2,1)}, u32[]{:S(2)}) %copy-start.9) | copy-done | bytes 262168
  81.2 0.9 %copy-done.11 = bf16[128,1024]{1,0:T(8,128)(2,1)S(1)} copy-done((bf16[128,1024]{1,0:T(8,128)(2,1)S(1)}, bf16[128,1024]{1,0:T(8,128)(2,1)}, u32[]{:S(2)}) %copy-start.11) | copy-done | bytes 262168
  82.1 0.9 %copy-done.13 = bf16[128,1024]{1,0:T(8,128)(2,1)S(1)} copy-done((bf16[128,1024]{1,0:T(8,128)(2,1)S(1)}, bf16[128,1024]{1,0:T(8,128)(2,1)}, u32[]{:S(2)}) %copy-start.13) | copy-done | bytes 262168
  83.1 0.9 %copy-done.15 = bf16[128,1024]{1,0:T(8,128)(2,1)S(1)} copy-done((bf16[128,1024]{1,0:T(8,128)(2,1)S(1)}, bf16[128,1024]{1,0:T(8,128)(2,1)}, u32[]{:S(2)}) %copy-start.15) | copy-done | bytes 262168
  84.0 5.7 %mix.1 = bf16[1024,1024]{1,0:T(8,128)(2,1)} custom-call(s32[2]{0:T(128)S(1)} %pad_add_fusion.place_ref, bf16[8,1024,128]{2,1,0:T(8,128)(2,1)} %all-to-all-done.refs_0_, bf16[128,1024]{1,0:T(8,128)(2,1)S(1)} %bitcast.21, bf16[128,1024]{1,0:T(8,128)(2,1)S(1)} %copy-done.7, bf16[128,1024]{1,0:T(8,128)(2,1)S(1)} %copy-done.5, bf16[128,1024]{1,0:T(8,128)(2,1)S(1)} %copy-done.11, ...), custom_call_target="tpu_custom_call" | custom-call | flops 2147483648 | bytes 10485760 | tf_op jit(solution)/shard_map/mix/pallas_call | solution.py:181
  (38 shorter events, 2.0 us)
Async XLA Ops:
  0.6 16.5 %collective-permute-start.2 = (bf16[128,1024]{1,0:T(8,128)(2,1)}, bf16[128,1024]{1,0:T(8,128)(2,1)}, u32[]{:S(2)}, u32[]{:S(2)}) collective-permute-start(bf16[128,1024]{1,0:T(8,128)(2,1)} %bitcast.18), channel_id=1, source_target_pairs={{0,4},{1,5},{2,6},{3,7},{4,0},{5,1},{6,2},{7,3},{8,12},{9,13},{10,... | collective-permute-start | bytes 786440 | tf_op jit(solution)/shard_map/ppermute | solution.py:24
  4.7 12.4 %collective-permute-start.1 = (bf16[128,1024]{1,0:T(8,128)(2,1)}, bf16[128,1024]{1,0:T(8,128)(2,1)S(1)}, u32[]{:S(2)}, u32[]{:S(2)}) collective-permute-start(bf16[128,1024]{1,0:T(8,128)(2,1)} %bitcast.19), channel_id=1, source_target_pairs={{0,2},{1,3},{2,0},{3,1},{4,6},{5,7},{6,4},{7,5},{8,10},{9,11},{10,... | collective-permute-start | bytes 786440 | tf_op jit(solution)/shard_map/ppermute | solution.py:24
  6.3 10.9 %collective-permute-start = (bf16[128,1024]{1,0:T(8,128)(2,1)}, bf16[128,1024]{1,0:T(8,128)(2,1)S(1)}, u32[]{:S(2)}, u32[]{:S(2)}) collective-permute-start(bf16[128,1024]{1,0:T(8,128)(2,1)} %bitcast.20), channel_id=1, source_target_pairs={{0,1},{1,0},{2,3},{3,2},{4,5},{5,4},{6,7},{7,6},{8,9},{9,8},{10,11... | collective-permute-start | bytes 786440 | tf_op jit(solution)/shard_map/ppermute | solution.py:24
  8.5 1.6 %copy-start.1 = (bf16[1,128,8192]{2,1,0:T(8,128)(2,1)S(1)}, bf16[1,128,8192]{2,1,0:T(8,128)(2,1)}, u32[]{:S(2)}) copy-start(bf16[1,128,8192]{2,1,0:T(8,128)(2,1)} %param.7) | copy-start | bytes 6291460
  17.2 18.4 %copy-start.4 = (bf16[128,1024]{1,0:T(8,128)(2,1)}, bf16[128,1024]{1,0:T(8,128)(2,1)S(1)}, u32[]{:S(2)}) copy-start(bf16[128,1024]{1,0:T(8,128)(2,1)S(1)} %collective-permute-done.1.refs_3_) | copy-start | bytes 786436
  17.2 0.7 copy-start.6
  17.9 5.7 %copy-start = (bf16[1,1024,1024]{2,1,0:T(8,128)(2,1)S(1)}, bf16[1,1024,1024]{2,1,0:T(8,128)(2,1)}, u32[]{:S(2)}) copy-start(bf16[1,1024,1024]{2,1,0:T(8,128)(2,1)} %param.10) | copy-start | bytes 6291460
  17.9 60.4 %all-to-all-start = ((bf16[8,1024,128]{2,1,0:T(8,128)(2,1)}), bf16[8,1024,128]{2,1,0:T(8,128)(2,1)}, u32[]{:S(2)}, u32[]{:S(2)}) async-start(bf16[8,1024,128]{2,1,0:T(8,128)(2,1)} %prepare.1), calls=%async_computation | async-start | bytes 4194304 | tf_op jit(solution)/shard_map/all_to_all | solution.py:231
  23.6 1.6 %copy-start.2 = (bf16[1024,1024]{1,0:T(8,128)(2,1)S(1)}, bf16[1024,1024]{1,0:T(8,128)(2,1)}, u32[]{:S(2)}) copy-start(bf16[1024,1024]{1,0:T(8,128)(2,1)} %shared_ref) | copy-start | bytes 6291460
  28.9 2.7 %collective-permute-start.7 = (bf16[2,1024,256]{2,1,0:T(8,128)(2,1)S(1)}, bf16[2,1024,256]{2,1,0:T(8,128)(2,1)S(1)}, u32[]{:S(2)}, u32[]{:S(2)}) collective-permute-start(bf16[2,1024,256]{2,1,0:T(8,128)(2,1)S(1)} %get-tuple-element.14), channel_id=1, source_target_pairs={{0,8},{8,0},{16,24},{24,16},{1,9},{9,1},{17,25},{25,17},{2,10},{10... | collective-permute-start | bytes 3145736 | tf_op jit(solution)/shard_map/ppermute | solution.py:24
  31.6 29.1 %copy-start.16 = (f32[1024,256]{1,0:T(8,128)S(1)}, f32[1024,256]{1,0:T(8,128)}, u32[]{:S(2)}) copy-start(f32[1024,256]{1,0:T(8,128)} %param.12) | copy-start | bytes 3145732
  31.6 29.1 %copy-start.17 = (f32[1024,256]{1,0:T(8,128)S(1)}, f32[1024,256]{1,0:T(8,128)}, u32[]{:S(2)}) copy-start(f32[1024,256]{1,0:T(8,128)} %param.13) | copy-start | bytes 3145732
  31.9 46.4 %copy-start.3 = (bf16[1,128,1024]{2,1,0:T(8,128)(2,1)S(1)}, bf16[1,128,1024]{2,1,0:T(8,128)(2,1)}, u32[]{:S(2)}) copy-start(bf16[1,128,1024]{2,1,0:T(8,128)(2,1)} %param.9) | copy-start | bytes 786436
  31.9 28.8 %collective-permute-start.8 = (bf16[1,1024,256]{2,1,0:T(8,128)(2,1)S(1)}, bf16[1,1024,256]{2,1,0:T(8,128)(2,1)S(1)}, u32[]{:S(2)}, u32[]{:S(2)}) collective-permute-start(bf16[1,1024,256]{2,1,0:T(8,128)(2,1)S(1)} %slice.23), channel_id=1, source_target_pairs={{0,16},{8,24},{16,0},{24,8},{1,17},{9,25},{17,1},{25,9},{2,18},{10... | collective-permute-start | bytes 1572872 | tf_op jit(solution)/shard_map/ppermute | solution.py:24
  33.5 15.1 %collective-permute-start.4 = (bf16[128,1024]{1,0:T(8,128)(2,1)}, bf16[128,1024]{1,0:T(8,128)(2,1)S(1)}, u32[]{:S(2)}, u32[]{:S(2)}) collective-permute-start(bf16[128,1024]{1,0:T(8,128)(2,1)} %collective-permute-done.2.refs_5_), channel_id=1, source_target_pairs={{0,1},{1,0},{2,3},{3,2},{4,5},{5,4},{6,7},{7,6},{8,9},{9,8},{10,11... | collective-permute-start | bytes 786440 | tf_op jit(solution)/shard_map/ppermute | solution.py:24
  35.5 25.2 %collective-permute-start.3 = (bf16[128,1024]{1,0:T(8,128)(2,1)S(1)}, bf16[128,1024]{1,0:T(8,128)(2,1)S(1)}, u32[]{:S(2)}, u32[]{:S(2)}) collective-permute-start(bf16[128,1024]{1,0:T(8,128)(2,1)S(1)} %collective-permute-done.1.refs_3_), channel_id=1, source_target_pairs={{0,1},{1,0},{2,3},{3,2},{4,5},{5,4},{6,7},{7,6},{8,9},{9,8},{10,11... | collective-permute-start | bytes 786440 | tf_op jit(solution)/shard_map/ppermute | solution.py:24
  35.6 29.0 %collective-permute-start.5 = (bf16[128,1024]{1,0:T(8,128)(2,1)}, bf16[128,1024]{1,0:T(8,128)(2,1)S(1)}, u32[]{:S(2)}, u32[]{:S(2)}) collective-permute-start(bf16[128,1024]{1,0:T(8,128)(2,1)} %collective-permute-done.2.refs_5_), channel_id=1, source_target_pairs={{0,2},{1,3},{2,0},{3,1},{4,6},{5,7},{6,4},{7,5},{8,10},{9,11},{10,... | collective-permute-start | bytes 786440 | tf_op jit(solution)/shard_map/ppermute | solution.py:24
  48.6 0.7 copy-start.8
  60.7 1.7 %copy-start.10 = (bf16[128,1024]{1,0:T(8,128)(2,1)}, bf16[128,1024]{1,0:T(8,128)(2,1)S(1)}, u32[]{:S(2)}) copy-start(bf16[128,1024]{1,0:T(8,128)(2,1)S(1)} %collective-permute-done.3.refs_4_) | copy-start | bytes 786436
  62.4 13.9 %collective-permute-start.10 = (bf16[1024,256]{1,0:T(8,128)(2,1)S(1)}, bf16[1024,256]{1,0:T(8,128)(2,1)S(1)}, u32[]{:S(2)}, u32[]{:S(2)}) collective-permute-start(bf16[1024,256]{1,0:T(8,128)(2,1)S(1)} %get-tuple-element.17.refs_9_), channel_id=1, source_target_pairs={{0,16},{8,24},{16,0},{24,8},{1,17},{9,25},{17,1},{25,9},{2,18},{10... | collective-permute-start | bytes 1572872 | tf_op jit(solution)/shard_map/ppermute | solution.py:24
  64.6 7.4 %collective-permute-start.6 = (bf16[128,1024]{1,0:T(8,128)(2,1)S(1)}, bf16[128,1024]{1,0:T(8,128)(2,1)S(1)}, u32[]{:S(2)}, u32[]{:S(2)}) collective-permute-start(bf16[128,1024]{1,0:T(8,128)(2,1)S(1)} %collective-permute-done.5.refs_7_), channel_id=1, source_target_pairs={{0,1},{1,0},{2,3},{3,2},{4,5},{5,4},{6,7},{7,6},{8,9},{9,8},{10,11... | collective-permute-start | bytes 786440 | tf_op jit(solution)/shard_map/ppermute | solution.py:24
  65.8 0.7 copy-start.12
  66.5 9.9 %collective-permute-start.9 = (bf16[1024,256]{1,0:T(8,128)(2,1)S(1)}, bf16[1024,256]{1,0:T(8,128)(2,1)}, u32[]{:S(2)}, u32[]{:S(2)}) collective-permute-start(bf16[1024,256]{1,0:T(8,128)(2,1)S(1)} %get-tuple-element.17.refs_9_), channel_id=1, source_target_pairs={{0,8},{8,0},{16,24},{24,16},{1,9},{9,1},{17,25},{25,17},{2,10},{10... | collective-permute-start | bytes 1572872 | tf_op jit(solution)/shard_map/ppermute | solution.py:24
  72.0 0.7 copy-start.14
  76.3 2.0 %collective-permute-start.11 = (bf16[1024,256]{1,0:T(8,128)(2,1)S(1)}, bf16[1024,256]{1,0:T(8,128)(2,1)}, u32[]{:S(2)}, u32[]{:S(2)}) collective-permute-start(bf16[1024,256]{1,0:T(8,128)(2,1)S(1)} %collective-permute-done.10.refs_11_), channel_id=1, source_target_pairs={{0,8},{8,0},{16,24},{24,16},{1,9},{9,1},{17,25},{25,17},{2,10},{10... | collective-permute-start | bytes 1572872 | tf_op jit(solution)/shard_map/ppermute | solution.py:24
  78.3 1.0 %copy-start.5 = (bf16[128,1024]{1,0:T(8,128)(2,1)S(1)}, bf16[128,1024]{1,0:T(8,128)(2,1)}, u32[]{:S(2)}) copy-start(bf16[128,1024]{1,0:T(8,128)(2,1)} %copy-done.4) | copy-start | bytes 786436
  79.3 0.9 %copy-start.7 = (bf16[128,1024]{1,0:T(8,128)(2,1)S(1)}, bf16[128,1024]{1,0:T(8,128)(2,1)}, u32[]{:S(2)}) copy-start(bf16[128,1024]{1,0:T(8,128)(2,1)} %copy-done.6) | copy-start | bytes 786436
  80.2 0.9 %copy-start.9 = (bf16[128,1024]{1,0:T(8,128)(2,1)S(1)}, bf16[128,1024]{1,0:T(8,128)(2,1)}, u32[]{:S(2)}) copy-start(bf16[128,1024]{1,0:T(8,128)(2,1)} %copy-done.8) | copy-start | bytes 786436
  81.2 0.9 %copy-start.11 = (bf16[128,1024]{1,0:T(8,128)(2,1)S(1)}, bf16[128,1024]{1,0:T(8,128)(2,1)}, u32[]{:S(2)}) copy-start(bf16[128,1024]{1,0:T(8,128)(2,1)} %copy-done.10) | copy-start | bytes 786436
  82.1 0.9 %copy-start.13 = (bf16[128,1024]{1,0:T(8,128)(2,1)S(1)}, bf16[128,1024]{1,0:T(8,128)(2,1)}, u32[]{:S(2)}) copy-start(bf16[128,1024]{1,0:T(8,128)(2,1)} %copy-done.12) | copy-start | bytes 786436
  83.1 0.9 %copy-start.15 = (bf16[128,1024]{1,0:T(8,128)(2,1)S(1)}, bf16[128,1024]{1,0:T(8,128)(2,1)}, u32[]{:S(2)}) copy-start(bf16[128,1024]{1,0:T(8,128)(2,1)} %copy-done.14) | copy-start | bytes 786436

commit v9 on v8

--- a/solution.py
+++ b/solution.py
@@ -146,28 +146,48 @@
     tokens_ref, refs = refs[0], refs[1:]
     cotangent_refs, refs = refs[:shards], refs[shards:]
     piece_refs, refs = refs[:groups], refs[groups:]
-    weight_ref, out_ref, cotangents, pieces, outs, out_sems = refs
+    weight_ref, out_ref, refs = refs[0], refs[1], refs[2:]
+    tokens, cotangents, pieces, weights, totals, outs, token_sems, cotangent_sems, piece_sems, weight_sem, out_sems = refs
     mine, own = place_ref[0], place_ref[1]
     depth, width = cotangent_refs[0].shape
     share = pieces.shape[2]
-    tile = outs.shape[2]
+    steps, _, tile = outs.shape
+
+    first = [pltpu.make_async_copy(tokens_ref.at[k], tokens.at[k], token_sems.at[k]) for k in range(shards)]
     for k, ref in enumerate(cotangent_refs):
-        cotangents[mine ^ k] = ref[...]
+        row = pl.ds(pl.multiple_of((mine ^ k) * depth, depth), depth)
+        first.append(pltpu.make_async_copy(ref, cotangents.at[row], cotangent_sems.at[k]))
+    second = [pltpu.make_async_copy(weight_ref, weights, weight_sem)]
     for k, ref in enumerate(piece_refs):
-        pieces[own ^ k] = ref[...]
-    left = jnp.concatenate([tokens_ref[k] for k in range(shards)], axis=1)
-    stores = []
-    for step in range(width // tile):
-        columns = slice(step * tile, (step + 1) * tile)
-        right = jnp.concatenate([cotangents[k, :, columns] for k in range(shards)], axis=0)
-        total = jnp.dot(left, right, preferred_element_type=jnp.float32)
-        for group in range(step * tile // share, (step + 1) * tile // share):
+        second.append(pltpu.make_async_copy(ref, pieces.at[own ^ k], piece_sems.at[k]))
+    for load in first:
+        load.start()
+    for load in first:
+        load.wait()
+    for load in second:
+        load.start()
+    left = jnp.concatenate([tokens[k] for k in range(shards)], axis=1)
+    stores = [
+        pltpu.make_async_copy(outs.at[step], out_ref.at[:, pl.ds(step * tile, tile)], out_sems.at[step])
+        for step in range(steps)
+    ]
+    ahead = min(2, steps)
+    for step in range(steps + ahead):
+        if step < steps:
+            columns = slice(step * tile, (step + 1) * tile)
+            totals[step] = jnp.dot(left, cotangents[:, columns], preferred_element_type=jnp.float32)
+        done = step - ahead
+        if done < 0:
+            continue
+        if done == 0:
+            for load in second:
+                load.wait()
+        for group in range(done * tile // share, (done + 1) * tile // share):
             place = slice(group * share, (group + 1) * share)
-            part = slice(group * share - step * tile, (group + 1) * share - step * tile)
-            mixed = weight_ref[:, place].astype(jnp.float32) + pieces[group].astype(jnp.float32)
-            outs[step, :, part] = (mix_weight * mixed - rate * total[:, part]).astype(jnp.bfloat16)
-        stores.append(pltpu.make_async_copy(outs.at[step], out_ref.at[:, pl.ds(step * tile, tile)], out_sems.at[step]))
-        stores[-1].start()
+            part = slice(group * share - done * tile, (group + 1) * share - done * tile)
+            mixed = weights[:, place].astype(jnp.float32) + pieces[group].astype(jnp.float32)
+            outs[done, :, part] = (mix_weight * mixed - rate * totals[done, :, part]).astype(jnp.bfloat16)
+        stores[done].start()
     for store in stores:
         store.wait()
 
@@ -182,15 +202,22 @@
         functools.partial(mix_kernel, shards, groups, rate),
         out_shape=jax.ShapeDtypeStruct((rows, width), jnp.bfloat16),
         in_specs=[pl.BlockSpec(memory_space=pltpu.SMEM)]
-        + [pl.BlockSpec(memory_space=pltpu.VMEM)] * (2 + shards + groups),
+        + [pl.BlockSpec(memory_space=pltpu.HBM)] * (2 + shards + groups),
         out_specs=pl.BlockSpec(memory_space=pltpu.HBM),
         scratch_shapes=[
-            pltpu.VMEM((shards, depth, width), jnp.bfloat16),
+            pltpu.VMEM((shards, rows, depth), jnp.bfloat16),
+            pltpu.VMEM((shards * depth, width), jnp.bfloat16),
             pltpu.VMEM((groups, rows, share), jnp.bfloat16),
+            pltpu.VMEM((rows, width), jnp.bfloat16),
+            pltpu.VMEM((width // tile, rows, tile), jnp.float32),
             pltpu.VMEM((width // tile, rows, tile), jnp.bfloat16),
+            pltpu.SemaphoreType.DMA((shards,)),
+            pltpu.SemaphoreType.DMA((shards,)),
+            pltpu.SemaphoreType.DMA((groups,)),
+            pltpu.SemaphoreType.DMA,
             pltpu.SemaphoreType.DMA((width // tile,)),
         ],
-        compiler_params=pltpu.CompilerParams(vmem_limit_bytes=24 * 2**20),
+        compiler_params=pltpu.CompilerParams(vmem_limit_bytes=44 * 2**20),
         cost_estimate=pl.CostEstimate(
             flops=2 * depth * shards * rows * width,
             bytes_accessed=2 * depth * shards * (rows + width) + 6 * rows * width,
@@ -222,11 +249,10 @@
     rows, width = weight.shape
     inner_rate = inner_gain / math.sqrt(tokens.shape[0] * shards)
 
-    own_exchanges = [1 << bit for bit in range(shards.bit_length() - 1)]
     cotangents = gather(cotangent, "fsdp", shards)
     blocks = prepare(tokens, norm_gain, shards)
     *_, blocks, coded_shared, coded_weight = lax.optimization_barrier(
-        (*(cotangents[k] for k in own_exchanges), blocks, shared_copy, weight)
+        (*cotangents[: shards // 2 + 1], blocks, shared_copy, weight)
     )
     columns = lax.all_to_all(blocks, "fsdp", split_axis=0, concat_axis=0, tiled=True)
 
@@ -236,13 +262,11 @@
     while bit < groups:
         sent = swap(total[1::2].astype(jnp.bfloat16), "replica", bit)
         bit *= 2
-        if bit >= groups:
-            *_, sent = lax.optimization_barrier((*cotangents[: shards // 2 + 2], sent))
         total = total[0::2] + sent.astype(jnp.float32)
     average = total[0] / groups
     momentum_next = outer_beta * momentum + average
     master_next = master - outer_rate * (average + outer_beta * momentum_next)
-    pieces = gather(master_next.astype(jnp.bfloat16), "replica", groups, after=cotangents)
+    pieces = gather(master_next.astype(jnp.bfloat16), "replica", groups, after=cotangents[:-1])
 
     layer_next = mix(mine, own, columns, cotangents, pieces, weight, (1.0 - mix_weight) * inner_rate)
     return (layer_next[None], master_next, momentum_next)

time: 91.5 us -> 90.5 us (0.989)
  Pallas kernels: 11.6 us -> 14.1 us
  waiting for transfers between devices: 41.8 us -> 39.8 us
  local copies, waits for them, and re-layouts: 11.8 us -> 10.1 us
    pallas_call x1, Pallas kernels: 5.73 us -> 8.2 us  [mix(): pl.pallas_call(functools.partial(mix_kernel, shards, groups, rate), out_s...]
    ppermute x12, waiting for transfers between devices: 41.8 us -> 39.8 us  [swap(): return lax.ppermute(value, axis, [(i, i ^ mask) for i in range(size)])]
    ppermute x12, starting transfers between devices: 15.4 us -> 17.2 us  [swap(): return lax.ppermute(value, axis, [(i, i ^ mask) for i in range(size)])]
    unnamed x36 -> x34, local copies, waits for them, and re-layouts: 11.7 us -> 10.1 us
    all_to_all x1, starting transfers between devices: 5.71 us -> 4.71 us  [on_device(): lax.all_to_all(blocks, 'fsdp', split_axis=0, concat_axis=0, tiled=True)]
  transfers between devices with their start and end apart: 13 -> 13, of which waited for: 9 -> 6; matrix products, arithmetic and copies ran while one was open for 3% -> 3% of each run, Pallas kernels for 7% -> 7%
where the time goes in v9:
time: 90.5 us; the launch traced here: 89.5 us
  waiting for transfers between devices  39.8 us (44%)
  starting transfers between devices  21.9 us (24%)
  Pallas kernels  14.1 us (16%)
  local copies, waits for them, and re-layouts  10.1 us (11%)
  other arithmetic  2.73 us (3%)
    ppermute x12, waiting for transfers between devices, swap(): return lax.ppermute(value, axis, [(i, i ^ mask) for i in range(size)])  39.8 us
    ppermute x12, starting transfers between devices, swap(): return lax.ppermute(value, axis, [(i, i ^ mask) for i in range(size)])  17.2 us
    unnamed x34, local copies, waits for them, and re-layouts  10.1 us
    pallas_call x1, Pallas kernels, mix(): pl.pallas_call(functools.partial(mix_kernel, shards, groups, rate), out_s...  8.2 us
    all_to_all x1, starting transfers between devices, on_device(): lax.all_to_all(blocks, 'fsdp', split_axis=0, concat_axis=0, tiled=True)  4.71 us
    pallas_call x1, Pallas kernels, code_and_decode(): pl.pallas_call(code_kernel, out_shape=(half, half), in_specs=[pl.BlockSpe...  3.69 us
    pallas_call x1, Pallas kernels, prepare(): pl.pallas_call(prepare_kernel, out_shape=jax.ShapeDtypeStruct((shards, ro...  2.21 us
  transfers between devices with their start and end apart: 13, of which 6 were waited for; matrix products, arithmetic and copies ran while one was open for 3% of the time, Pallas kernels for 7%

profile of v9, /device:TPU:0, one launch (start us, length us, event | category | flops | bytes accessed | tf_op | source)
XLA Modules:
  0.0 89.5 jit_solution(14326236391484168884)
XLA Ops:
  0.6 3.1 %collective-permute-start.1 = (bf16[128,1024]{1,0:T(8,128)(2,1)}, bf16[128,1024]{1,0:T(8,128)(2,1)S(1)}, u32[]{:S(2)}, u32[]{:S(2)}) collective-permute-start(bf16[128,1024]{1,0:T(8,128)(2,1)} %bitcast.18), channel_id=1, source_target_pairs={{0,2},{1,3},{2,0},{3,1},{4,6},{5,7},{6,4},{7,5},{8,10},{9,11},{10,... | collective-permute-start | bytes 786440 | tf_op jit(solution)/shard_map/ppermute | solution.py:24
  3.7 2.6 %collective-permute-start.3 = (bf16[128,1024]{1,0:T(8,128)(2,1)}, bf16[128,1024]{1,0:T(8,128)(2,1)S(1)}, u32[]{:S(2)}, u32[]{:S(2)}) collective-permute-start(bf16[128,1024]{1,0:T(8,128)(2,1)} %bitcast.19), channel_id=1, source_target_pairs={{0,4},{1,5},{2,6},{3,7},{4,0},{5,1},{6,2},{7,3},{8,12},{9,13},{10,... | collective-permute-start | bytes 786440 | tf_op jit(solution)/shard_map/ppermute | solution.py:24
  6.3 1.5 %collective-permute-start = (bf16[128,1024]{1,0:T(8,128)(2,1)}, bf16[128,1024]{1,0:T(8,128)(2,1)S(1)}, u32[]{:S(2)}, u32[]{:S(2)}) collective-permute-start(bf16[128,1024]{1,0:T(8,128)(2,1)} %bitcast.20), channel_id=1, source_target_pairs={{0,1},{1,0},{2,3},{3,2},{4,5},{5,4},{6,7},{7,6},{8,9},{9,8},{10,11... | collective-permute-start | bytes 786440 | tf_op jit(solution)/shard_map/ppermute | solution.py:24
  7.8 7.9 %collective-permute-done.1.refs_3_ = bf16[128,1024]{1,0:T(8,128)(2,1)S(1)} collective-permute-done((bf16[128,1024]{1,0:T(8,128)(2,1)}, bf16[128,1024]{1,0:T(8,128)(2,1)S(1)}, u32[]{:S(2)}, u32[]{:S(2)}) %collective-permute-start.1) | collective-permute-done | bytes 262176 | tf_op jit(solution)/shard_map/ppermute | solution.py:24
  15.7 1.7 %collective-permute-start.2 = (bf16[128,1024]{1,0:T(8,128)(2,1)S(1)}, bf16[128,1024]{1,0:T(8,128)(2,1)S(1)}, u32[]{:S(2)}, u32[]{:S(2)}) collective-permute-start(bf16[128,1024]{1,0:T(8,128)(2,1)S(1)} %collective-permute-done.1.refs_3_), channel_id=1, source_target_pairs={{0,1},{1,0},{2,3},{3,2},{4,5},{5,4},{6,7},{7,6},{8,9},{9,8},{10,11... | collective-permute-start | bytes 786440 | tf_op jit(solution)/shard_map/ppermute | solution.py:24
  17.4 0.7 reshape.16
  18.1 1.6 %copy-done.1 = bf16[1,128,8192]{2,1,0:T(8,128)(2,1)S(1)} copy-done((bf16[1,128,8192]{2,1,0:T(8,128)(2,1)S(1)}, bf16[1,128,8192]{2,1,0:T(8,128)(2,1)}, u32[]{:S(2)}) %copy-start.1) | copy-done | bytes 2097176
  19.7 2.2 %prepare.1 = bf16[8,1024,128]{2,1,0:T(8,128)(2,1)} custom-call(bf16[128,8192]{1,0:T(8,128)(2,1)S(1)} %bitcast.17, f32[1,8192]{1,0:T(1,128)S(1)} %bitcast.22), custom_call_target="tpu_custom_call" | custom-call | flops 5242880 | bytes 4194304 | tf_op jit(solution)/shard_map/prepare/pallas_call | solution.py:58
  22.0 0.7 copy-done.9
  22.7 0.5 collective-permute-done.2.refs_4_
  23.2 0.7 copy-done.11
  23.9 4.7 %all-to-all-start = ((bf16[8,1024,128]{2,1,0:T(8,128)(2,1)}), bf16[8,1024,128]{2,1,0:T(8,128)(2,1)}, u32[]{:S(2)}, u32[]{:S(2)}) async-start(bf16[8,1024,128]{2,1,0:T(8,128)(2,1)} %prepare.1), calls=%async_computation | async-start | bytes 4194304 | tf_op jit(solution)/shard_map/all_to_all | solution.py:257
  28.6 1.6 %copy-done.2 = bf16[1024,1024]{1,0:T(8,128)(2,1)S(1)} copy-done((bf16[1024,1024]{1,0:T(8,128)(2,1)S(1)}, bf16[1024,1024]{1,0:T(8,128)(2,1)}, u32[]{:S(2)}) %copy-start.2) | copy-done | bytes 2097176
  30.2 3.7 %code_and_decode.1 = (bf16[2,1024,256]{2,1,0:T(8,128)(2,1)S(1)}, bf16[2,1024,256]{2,1,0:T(8,128)(2,1)S(1)}) custom-call(s32[1]{0:T(128)} %bitcast.1.own_ref, bf16[1024,1024]{1,0:T(8,128)(2,1)S(1)} %copy-done.2, bf16[1024,1024]{1,0:T(8,128)(2,1)S(1)} %bitcast.15), custom_call_target="tpu_custom_call" | custom-call | flops 20971520 | bytes 6291456 | tf_op jit(solution)/shard_map/code_and_decode/pallas_call | solution.py:128
  34.0 2.6 %collective-permute-done.7 = bf16[2,1024,256]{2,1,0:T(8,128)(2,1)S(1)} collective-permute-done((bf16[2,1024,256]{2,1,0:T(8,128)(2,1)S(1)}, bf16[2,1024,256]{2,1,0:T(8,128)(2,1)S(1)}, u32[]{:S(2)}, u32[]{:S(2)}) %collective-permute-start.7) | collective-permute-done | bytes 1048608 | tf_op jit(solution)/shard_map/ppermute | solution.py:24
  36.7 0.2 convert_add_fusion
  37.0 1.6 %collective-permute-start.8 = (bf16[1,1024,256]{2,1,0:T(8,128)(2,1)S(1)}, bf16[1,1024,256]{2,1,0:T(8,128)(2,1)S(1)}, u32[]{:S(2)}, u32[]{:S(2)}) collective-permute-start(bf16[1,1024,256]{2,1,0:T(8,128)(2,1)S(1)} %slice.23), channel_id=1, source_target_pairs={{0,16},{8,24},{16,0},{24,8},{1,17},{9,25},{17,1},{25,9},{2,18},{10... | collective-permute-start | bytes 1572872 | tf_op jit(solution)/shard_map/ppermute | solution.py:24
  38.5 12.5 %collective-permute-done.8 = bf16[1,1024,256]{2,1,0:T(8,128)(2,1)S(1)} collective-permute-done((bf16[1,1024,256]{2,1,0:T(8,128)(2,1)S(1)}, bf16[1,1024,256]{2,1,0:T(8,128)(2,1)S(1)}, u32[]{:S(2)}, u32[]{:S(2)}) %collective-permute-start.8) | collective-permute-done | bytes 524320 | tf_op jit(solution)/shard_map/ppermute | solution.py:24
  51.0 1.7 %fusion.2 = (bf16[1024,256]{1,0:T(8,128)(2,1)S(1)}, f32[1024,256]{1,0:T(8,128)}, f32[1024,256]{1,0:T(8,128)}) fusion(f32[1024,256]{1,0:T(8,128)S(1)} %copy-done.15, bf16[1,1024,256]{2,1,0:T(8,128)(2,1)S(1)} %collective-permute-done.8, f32[2,1024,256]{2,1,0:T(8,128)S(1)} %convert_add_fusion, f32[1024,256]{1,0:T(8,128)S(1)} %copy-done.16), kind=kLoop, calls=%fused_computation.8 | loop fusion | flops 2621440 | bytes 6291456 | tf_op jit(solution)/shard_map/convert_element_type | solution.py:269
  52.7 1.5 %collective-permute-start.10 = (bf16[1024,256]{1,0:T(8,128)(2,1)S(1)}, bf16[1024,256]{1,0:T(8,128)(2,1)S(1)}, u32[]{:S(2)}, u32[]{:S(2)}) collective-permute-start(bf16[1024,256]{1,0:T(8,128)(2,1)S(1)} %get-tuple-element.15.refs_9_), channel_id=1, source_target_pairs={{0,16},{8,24},{16,0},{24,8},{1,17},{9,25},{17,1},{25,9},{2,18},{10... | collective-permute-start | bytes 1572872 | tf_op jit(solution)/shard_map/ppermute | solution.py:24
  54.2 2.0 %collective-permute-start.5 = (bf16[128,1024]{1,0:T(8,128)(2,1)S(1)}, bf16[128,1024]{1,0:T(8,128)(2,1)}, u32[]{:S(2)}, u32[]{:S(2)}) collective-permute-start(bf16[128,1024]{1,0:T(8,128)(2,1)S(1)} %copy-done.7), channel_id=1, source_target_pairs={{0,2},{1,3},{2,0},{3,1},{4,6},{5,7},{6,4},{7,5},{8,10},{9,11},{10,... | collective-permute-start | bytes 786440 | tf_op jit(solution)/shard_map/ppermute | solution.py:24
  56.2 1.5 %collective-permute-start.4 = (bf16[128,1024]{1,0:T(8,128)(2,1)S(1)}, bf16[128,1024]{1,0:T(8,128)(2,1)S(1)}, u32[]{:S(2)}, u32[]{:S(2)}) collective-permute-start(bf16[128,1024]{1,0:T(8,128)(2,1)S(1)} %copy-done.7), channel_id=1, source_target_pairs={{0,1},{1,0},{2,3},{3,2},{4,5},{5,4},{6,7},{7,6},{8,9},{9,8},{10,11... | collective-permute-start | bytes 786440 | tf_op jit(solution)/shard_map/ppermute | solution.py:24
  57.7 9.0 %collective-permute-done.5.refs_7_ = bf16[128,1024]{1,0:T(8,128)(2,1)} collective-permute-done((bf16[128,1024]{1,0:T(8,128)(2,1)S(1)}, bf16[128,1024]{1,0:T(8,128)(2,1)}, u32[]{:S(2)}, u32[]{:S(2)}) %collective-permute-start.5) | collective-permute-done | bytes 262176 | tf_op jit(solution)/shard_map/ppermute | solution.py:24
  66.7 0.7 copy-done.13
  67.4 1.7 %collective-permute-start.6 = (bf16[128,1024]{1,0:T(8,128)(2,1)}, bf16[128,1024]{1,0:T(8,128)(2,1)}, u32[]{:S(2)}, u32[]{:S(2)}) collective-permute-start(bf16[128,1024]{1,0:T(8,128)(2,1)} %collective-permute-done.5.refs_7_), channel_id=1, source_target_pairs={{0,1},{1,0},{2,3},{3,2},{4,5},{5,4},{6,7},{7,6},{8,9},{9,8},{10,11... | collective-permute-start | bytes 786440 | tf_op jit(solution)/shard_map/ppermute | solution.py:24
  69.1 7.4 %collective-permute-done.6.refs_8_ = bf16[128,1024]{1,0:T(8,128)(2,1)} collective-permute-done((bf16[128,1024]{1,0:T(8,128)(2,1)}, bf16[128,1024]{1,0:T(8,128)(2,1)}, u32[]{:S(2)}, u32[]{:S(2)}) %collective-permute-start.6) | collective-permute-done | bytes 262176 | tf_op jit(solution)/shard_map/ppermute | solution.py:24
  76.5 0.9 %copy-done.5 = bf16[128,1024]{1,0:T(8,128)(2,1)S(1)} copy-done((bf16[128,1024]{1,0:T(8,128)(2,1)S(1)}, bf16[128,1024]{1,0:T(8,128)(2,1)}, u32[]{:S(2)}) %copy-start.5) | copy-done | bytes 262168
  77.5 0.9 %copy-done.8 = bf16[128,1024]{1,0:T(8,128)(2,1)S(1)} copy-done((bf16[128,1024]{1,0:T(8,128)(2,1)S(1)}, bf16[128,1024]{1,0:T(8,128)(2,1)}, u32[]{:S(2)}) %copy-start.8) | copy-done | bytes 262168
  78.4 0.9 %copy-done.10 = bf16[128,1024]{1,0:T(8,128)(2,1)S(1)} copy-done((bf16[128,1024]{1,0:T(8,128)(2,1)S(1)}, bf16[128,1024]{1,0:T(8,128)(2,1)}, u32[]{:S(2)}) %copy-start.10) | copy-done | bytes 262168
  79.4 0.9 %copy-done.12 = bf16[128,1024]{1,0:T(8,128)(2,1)S(1)} copy-done((bf16[128,1024]{1,0:T(8,128)(2,1)S(1)}, bf16[128,1024]{1,0:T(8,128)(2,1)}, u32[]{:S(2)}) %copy-start.12) | copy-done | bytes 262168
  80.3 0.9 %copy-done.14 = bf16[128,1024]{1,0:T(8,128)(2,1)S(1)} copy-done((bf16[128,1024]{1,0:T(8,128)(2,1)S(1)}, bf16[128,1024]{1,0:T(8,128)(2,1)}, u32[]{:S(2)}) %copy-start.14) | copy-done | bytes 262168
  81.3 8.2 %mix.1 = bf16[1024,1024]{1,0:T(8,128)(2,1)} custom-call(s32[2]{0:T(128)S(1)} %pad_add_fusion.place_ref, bf16[8,1024,128]{2,1,0:T(8,128)(2,1)} %all-to-all-done.refs_0_, bf16[128,1024]{1,0:T(8,128)(2,1)S(1)} %bitcast.21, bf16[128,1024]{1,0:T(8,128)(2,1)S(1)} %copy-done.10, bf16[128,1024]{1,0:T(8,128)(2,1)S(1)} %copy-done.5, bf16[128,1024]{1,0:T(8,128)(2,1)S(1)} %copy-done.12, ...), custom_call_target="tpu_custom_call" | custom-call | flops 2147483648 | bytes 10485760 | tf_op jit(solution)/shard_map/mix/pallas_call | solution.py:201
  (36 shorter events, 0.3 us)
Async XLA Ops:
  0.6 15.1 %collective-permute-start.1 = (bf16[128,1024]{1,0:T(8,128)(2,1)}, bf16[128,1024]{1,0:T(8,128)(2,1)S(1)}, u32[]{:S(2)}, u32[]{:S(2)}) collective-permute-start(bf16[128,1024]{1,0:T(8,128)(2,1)} %bitcast.18), channel_id=1, source_target_pairs={{0,2},{1,3},{2,0},{3,1},{4,6},{5,7},{6,4},{7,5},{8,10},{9,11},{10,... | collective-permute-start | bytes 786440 | tf_op jit(solution)/shard_map/ppermute | solution.py:24
  3.7 18.2 %collective-permute-start.3 = (bf16[128,1024]{1,0:T(8,128)(2,1)}, bf16[128,1024]{1,0:T(8,128)(2,1)S(1)}, u32[]{:S(2)}, u32[]{:S(2)}) collective-permute-start(bf16[128,1024]{1,0:T(8,128)(2,1)} %bitcast.19), channel_id=1, source_target_pairs={{0,4},{1,5},{2,6},{3,7},{4,0},{5,1},{6,2},{7,3},{8,12},{9,13},{10,... | collective-permute-start | bytes 786440 | tf_op jit(solution)/shard_map/ppermute | solution.py:24
  6.3 15.7 %collective-permute-start = (bf16[128,1024]{1,0:T(8,128)(2,1)}, bf16[128,1024]{1,0:T(8,128)(2,1)S(1)}, u32[]{:S(2)}, u32[]{:S(2)}) collective-permute-start(bf16[128,1024]{1,0:T(8,128)(2,1)} %bitcast.20), channel_id=1, source_target_pairs={{0,1},{1,0},{2,3},{3,2},{4,5},{5,4},{6,7},{7,6},{8,9},{9,8},{10,11... | collective-permute-start | bytes 786440 | tf_op jit(solution)/shard_map/ppermute | solution.py:24
  15.7 6.2 %copy-start.4 = (bf16[128,1024]{1,0:T(8,128)(2,1)}, bf16[128,1024]{1,0:T(8,128)(2,1)S(1)}, u32[]{:S(2)}) copy-start(bf16[128,1024]{1,0:T(8,128)(2,1)S(1)} %collective-permute-done.1.refs_3_) | copy-start | bytes 786436
  15.7 7.5 %collective-permute-start.2 = (bf16[128,1024]{1,0:T(8,128)(2,1)S(1)}, bf16[128,1024]{1,0:T(8,128)(2,1)S(1)}, u32[]{:S(2)}, u32[]{:S(2)}) collective-permute-start(bf16[128,1024]{1,0:T(8,128)(2,1)S(1)} %collective-permute-done.1.refs_3_), channel_id=1, source_target_pairs={{0,1},{1,0},{2,3},{3,2},{4,5},{5,4},{6,7},{7,6},{8,9},{9,8},{10,11... | collective-permute-start | bytes 786440 | tf_op jit(solution)/shard_map/ppermute | solution.py:24
  18.1 1.6 %copy-start.1 = (bf16[1,128,8192]{2,1,0:T(8,128)(2,1)S(1)}, bf16[1,128,8192]{2,1,0:T(8,128)(2,1)}, u32[]{:S(2)}) copy-start(bf16[1,128,8192]{2,1,0:T(8,128)(2,1)} %param.7) | copy-start | bytes 6291460
  22.0 1.3 %copy-start.6 = (bf16[128,1024]{1,0:T(8,128)(2,1)}, bf16[128,1024]{1,0:T(8,128)(2,1)S(1)}, u32[]{:S(2)}) copy-start(bf16[128,1024]{1,0:T(8,128)(2,1)S(1)} %collective-permute-done.3.refs_5_) | copy-start | bytes 786436
  22.0 0.7 copy-start.9
  23.2 0.7 copy-start.11
  23.9 4.7 %copy-start = (bf16[1,1024,1024]{2,1,0:T(8,128)(2,1)S(1)}, bf16[1,1024,1024]{2,1,0:T(8,128)(2,1)}, u32[]{:S(2)}) copy-start(bf16[1,1024,1024]{2,1,0:T(8,128)(2,1)} %param.10) | copy-start | bytes 6291460
  23.9 52.6 %all-to-all-start = ((bf16[8,1024,128]{2,1,0:T(8,128)(2,1)}), bf16[8,1024,128]{2,1,0:T(8,128)(2,1)}, u32[]{:S(2)}, u32[]{:S(2)}) async-start(bf16[8,1024,128]{2,1,0:T(8,128)(2,1)} %prepare.1), calls=%async_computation | async-start | bytes 4194304 | tf_op jit(solution)/shard_map/all_to_all | solution.py:257
  28.6 1.6 %copy-start.2 = (bf16[1024,1024]{1,0:T(8,128)(2,1)S(1)}, bf16[1024,1024]{1,0:T(8,128)(2,1)}, u32[]{:S(2)}) copy-start(bf16[1024,1024]{1,0:T(8,128)(2,1)} %shared_ref) | copy-start | bytes 6291460
  33.9 2.7 %collective-permute-start.7 = (bf16[2,1024,256]{2,1,0:T(8,128)(2,1)S(1)}, bf16[2,1024,256]{2,1,0:T(8,128)(2,1)S(1)}, u32[]{:S(2)}, u32[]{:S(2)}) collective-permute-start(bf16[2,1024,256]{2,1,0:T(8,128)(2,1)S(1)} %get-tuple-element.13), channel_id=1, source_target_pairs={{0,8},{8,0},{16,24},{24,16},{1,9},{9,1},{17,25},{25,17},{2,10},{10... | collective-permute-start | bytes 3145736 | tf_op jit(solution)/shard_map/ppermute | solution.py:24
  36.6 14.4 %copy-start.15 = (f32[1024,256]{1,0:T(8,128)S(1)}, f32[1024,256]{1,0:T(8,128)}, u32[]{:S(2)}) copy-start(f32[1024,256]{1,0:T(8,128)} %param.12) | copy-start | bytes 3145732
  36.7 14.4 %copy-start.16 = (f32[1024,256]{1,0:T(8,128)S(1)}, f32[1024,256]{1,0:T(8,128)}, u32[]{:S(2)}) copy-start(f32[1024,256]{1,0:T(8,128)} %param.13) | copy-start | bytes 3145732
  37.0 17.3 %copy-start.7 = (bf16[128,1024]{1,0:T(8,128)(2,1)S(1)}, bf16[128,1024]{1,0:T(8,128)(2,1)}, u32[]{:S(2)}) copy-start(bf16[128,1024]{1,0:T(8,128)(2,1)} %copy-done.6) | copy-start | bytes 786436
  37.0 39.6 %copy-start.3 = (bf16[1,128,1024]{2,1,0:T(8,128)(2,1)S(1)}, bf16[1,128,1024]{2,1,0:T(8,128)(2,1)}, u32[]{:S(2)}) copy-start(bf16[1,128,1024]{2,1,0:T(8,128)(2,1)} %param.9) | copy-start | bytes 786436
  37.0 14.0 %collective-permute-start.8 = (bf16[1,1024,256]{2,1,0:T(8,128)(2,1)S(1)}, bf16[1,1024,256]{2,1,0:T(8,128)(2,1)S(1)}, u32[]{:S(2)}, u32[]{:S(2)}) collective-permute-start(bf16[1,1024,256]{2,1,0:T(8,128)(2,1)S(1)} %slice.23), channel_id=1, source_target_pairs={{0,16},{8,24},{16,0},{24,8},{1,17},{9,25},{17,1},{25,9},{2,18},{10... | collective-permute-start | bytes 1572872 | tf_op jit(solution)/shard_map/ppermute | solution.py:24
  52.7 14.7 %collective-permute-start.10 = (bf16[1024,256]{1,0:T(8,128)(2,1)S(1)}, bf16[1024,256]{1,0:T(8,128)(2,1)S(1)}, u32[]{:S(2)}, u32[]{:S(2)}) collective-permute-start(bf16[1024,256]{1,0:T(8,128)(2,1)S(1)} %get-tuple-element.15.refs_9_), channel_id=1, source_target_pairs={{0,16},{8,24},{16,0},{24,8},{1,17},{9,25},{17,1},{25,9},{2,18},{10... | collective-permute-start | bytes 1572872 | tf_op jit(solution)/shard_map/ppermute | solution.py:24
  54.2 12.4 %collective-permute-start.5 = (bf16[128,1024]{1,0:T(8,128)(2,1)S(1)}, bf16[128,1024]{1,0:T(8,128)(2,1)}, u32[]{:S(2)}, u32[]{:S(2)}) collective-permute-start(bf16[128,1024]{1,0:T(8,128)(2,1)S(1)} %copy-done.7), channel_id=1, source_target_pairs={{0,2},{1,3},{2,0},{3,1},{4,6},{5,7},{6,4},{7,5},{8,10},{9,11},{10,... | collective-permute-start | bytes 786440 | tf_op jit(solution)/shard_map/ppermute | solution.py:24
  56.2 10.4 %collective-permute-start.4 = (bf16[128,1024]{1,0:T(8,128)(2,1)S(1)}, bf16[128,1024]{1,0:T(8,128)(2,1)S(1)}, u32[]{:S(2)}, u32[]{:S(2)}) collective-permute-start(bf16[128,1024]{1,0:T(8,128)(2,1)S(1)} %copy-done.7), channel_id=1, source_target_pairs={{0,1},{1,0},{2,3},{3,2},{4,5},{5,4},{6,7},{7,6},{8,9},{9,8},{10,11... | collective-permute-start | bytes 786440 | tf_op jit(solution)/shard_map/ppermute | solution.py:24
  57.7 18.8 %collective-permute-start.9 = (bf16[1024,256]{1,0:T(8,128)(2,1)S(1)}, bf16[1024,256]{1,0:T(8,128)(2,1)}, u32[]{:S(2)}, u32[]{:S(2)}) collective-permute-start(bf16[1024,256]{1,0:T(8,128)(2,1)S(1)} %get-tuple-element.15.refs_9_), channel_id=1, source_target_pairs={{0,8},{8,0},{16,24},{24,16},{1,9},{9,1},{17,25},{25,17},{2,10},{10... | collective-permute-start | bytes 1572872 | tf_op jit(solution)/shard_map/ppermute | solution.py:24
  66.7 0.7 copy-start.13
  67.4 9.1 %collective-permute-start.11 = (bf16[1024,256]{1,0:T(8,128)(2,1)S(1)}, bf16[1024,256]{1,0:T(8,128)(2,1)}, u32[]{:S(2)}, u32[]{:S(2)}) collective-permute-start(bf16[1024,256]{1,0:T(8,128)(2,1)S(1)} %collective-permute-done.10.refs_11_), channel_id=1, source_target_pairs={{0,8},{8,0},{16,24},{24,16},{1,9},{9,1},{17,25},{25,17},{2,10},{10... | collective-permute-start | bytes 1572872 | tf_op jit(solution)/shard_map/ppermute | solution.py:24
  67.4 9.1 %collective-permute-start.6 = (bf16[128,1024]{1,0:T(8,128)(2,1)}, bf16[128,1024]{1,0:T(8,128)(2,1)}, u32[]{:S(2)}, u32[]{:S(2)}) collective-permute-start(bf16[128,1024]{1,0:T(8,128)(2,1)} %collective-permute-done.5.refs_7_), channel_id=1, source_target_pairs={{0,1},{1,0},{2,3},{3,2},{4,5},{5,4},{6,7},{7,6},{8,9},{9,8},{10,11... | collective-permute-start | bytes 786440 | tf_op jit(solution)/shard_map/ppermute | solution.py:24
  76.5 1.0 %copy-start.5 = (bf16[128,1024]{1,0:T(8,128)(2,1)S(1)}, bf16[128,1024]{1,0:T(8,128)(2,1)}, u32[]{:S(2)}) copy-start(bf16[128,1024]{1,0:T(8,128)(2,1)} %copy-done.4) | copy-start | bytes 786436
  77.5 0.9 %copy-start.8 = (bf16[128,1024]{1,0:T(8,128)(2,1)S(1)}, bf16[128,1024]{1,0:T(8,128)(2,1)}, u32[]{:S(2)}) copy-start(bf16[128,1024]{1,0:T(8,128)(2,1)} %copy-done.6) | copy-start | bytes 786436
  78.4 0.9 %copy-start.10 = (bf16[128,1024]{1,0:T(8,128)(2,1)S(1)}, bf16[128,1024]{1,0:T(8,128)(2,1)}, u32[]{:S(2)}) copy-start(bf16[128,1024]{1,0:T(8,128)(2,1)} %copy-done.9) | copy-start | bytes 786436
  79.4 0.9 %copy-start.12 = (bf16[128,1024]{1,0:T(8,128)(2,1)S(1)}, bf16[128,1024]{1,0:T(8,128)(2,1)}, u32[]{:S(2)}) copy-start(bf16[128,1024]{1,0:T(8,128)(2,1)} %copy-done.11) | copy-start | bytes 786436
  80.3 0.9 %copy-start.14 = (bf16[128,1024]{1,0:T(8,128)(2,1)S(1)}, bf16[128,1024]{1,0:T(8,128)(2,1)}, u32[]{:S(2)}) copy-start(bf16[128,1024]{1,0:T(8,128)(2,1)} %copy-done.13) | copy-start | bytes 786436

commit v10 on v8

--- a/solution.py
+++ b/solution.py
@@ -137,76 +137,132 @@
             pltpu.SemaphoreType.DMA((2, rows // tile)),
         ],
         compiler_params=pltpu.CompilerParams(vmem_limit_bytes=16 * 2**20),
-        cost_estimate=pl.CostEstimate(flops=20 * rows * width, bytes_accessed=6 * rows * width, transcendentals=0),
+        cost_estimate=pl.CostEstimate(flops=20 * rows * width, bytes_accessed=360 * rows * width, transcendentals=0),
         name="code_and_decode",
     )(own.reshape(1), shared, weight)
 
 
-def mix_kernel(shards, groups, rate, place_ref, *refs):
-    tokens_ref, refs = refs[0], refs[1:]
-    cotangent_refs, refs = refs[:shards], refs[shards:]
+def stage_kernel(*refs):
+    *part_refs, out_ref, sems = refs
+    depth = part_refs[0].shape[0]
+    loads = [
+        pltpu.make_async_copy(ref, out_ref.at[pl.ds(k * depth, depth)], sems.at[k]) for k, ref in enumerate(part_refs)
+    ]
+    for load in loads:
+        load.start()
+    for load in loads:
+        load.wait()
+
+
+def stage(parts):
+    depth, width = parts[0].shape
+    return pl.pallas_call(
+        stage_kernel,
+        out_shape=jax.ShapeDtypeStruct((len(parts) * depth, width), parts[0].dtype),
+        in_specs=[pl.BlockSpec(memory_space=pltpu.HBM)] * len(parts),
+        out_specs=pl.BlockSpec(memory_space=pltpu.VMEM),
+        scratch_shapes=[pltpu.SemaphoreType.DMA((len(parts),))],
+        compiler_params=pltpu.CompilerParams(vmem_limit_bytes=16 * 2**20),
+        cost_estimate=pl.CostEstimate(flops=0, bytes_accessed=4 * len(parts) * depth * width, transcendentals=0),
+        name="stage",
+    )(*parts)
+
+
+def accumulate_kernel(groups, rate, place_ref, cotangent_ref, tokens_ref, weight_ref, *refs):
     piece_refs, refs = refs[:groups], refs[groups:]
-    weight_ref, out_ref, cotangents, pieces, outs, out_sems = refs
+    total_ref, last_ref, tokens, weight, pieces, token_sems, weight_sem, piece_sems, last_sem = refs
     mine, own = place_ref[0], place_ref[1]
-    depth, width = cotangent_refs[0].shape
+    parts, rows, depth = tokens.shape
+    width = total_ref.shape[1]
     share = pieces.shape[2]
-    tile = outs.shape[2]
-    for k, ref in enumerate(cotangent_refs):
-        cotangents[mine ^ k] = ref[...]
+    tile = max(share, 256)
+    loads = [pltpu.make_async_copy(tokens_ref.at[mine ^ k], tokens.at[k], token_sems.at[k]) for k in range(parts)]
+    rest = [pltpu.make_async_copy(weight_ref, weight, weight_sem)]
     for k, ref in enumerate(piece_refs):
-        pieces[own ^ k] = ref[...]
-    left = jnp.concatenate([tokens_ref[k] for k in range(shards)], axis=1)
-    stores = []
-    for step in range(width // tile):
-        columns = slice(step * tile, (step + 1) * tile)
-        right = jnp.concatenate([cotangents[k, :, columns] for k in range(shards)], axis=0)
-        total = jnp.dot(left, right, preferred_element_type=jnp.float32)
-        for group in range(step * tile // share, (step + 1) * tile // share):
-            place = slice(group * share, (group + 1) * share)
-            part = slice(group * share - step * tile, (group + 1) * share - step * tile)
-            mixed = weight_ref[:, place].astype(jnp.float32) + pieces[group].astype(jnp.float32)
-            outs[step, :, part] = (mix_weight * mixed - rate * total[:, part]).astype(jnp.bfloat16)
-        stores.append(pltpu.make_async_copy(outs.at[step], out_ref.at[:, pl.ds(step * tile, tile)], out_sems.at[step]))
-        stores[-1].start()
-    for store in stores:
-        store.wait()
-
-
-def mix(mine, own, tokens, cotangents, pieces, weight, rate):
+        rest.append(pltpu.make_async_copy(ref, pieces.at[own ^ k], piece_sems.at[k]))
+    rest.append(pltpu.make_async_copy(tokens_ref.at[mine ^ parts], last_ref, last_sem))
+    for load in loads + rest:
+        load.start()
+    for load in loads:
+        load.wait()
+    left = jnp.concatenate([tokens[k] for k in range(parts)], axis=1)
+    for start in range(0, width, tile):
+        product = jnp.dot(left, cotangent_ref[:, start : start + tile], preferred_element_type=jnp.float32)
+        if start == 0:
+            for load in rest:
+                load.wait()
+        for group in range(start // share, (start + tile) // share):
+            columns = slice(group * share, (group + 1) * share)
+            mixed = weight[:, columns].astype(jnp.float32) + pieces[group].astype(jnp.float32)
+            part = slice(group * share - start, (group + 1) * share - start)
+            total_ref[:, columns] = mix_weight * mixed - rate * product[:, part]
+
+
+def accumulate(mine, own, cotangents, tokens, weight, pieces, rate):
     shards, rows, depth = tokens.shape
     width = weight.shape[1]
     groups = len(pieces)
-    share = width // groups
-    tile = max(share, 256)
-    return pl.pallas_call(
-        functools.partial(mix_kernel, shards, groups, rate),
-        out_shape=jax.ShapeDtypeStruct((rows, width), jnp.bfloat16),
-        in_specs=[pl.BlockSpec(memory_space=pltpu.SMEM)]
-        + [pl.BlockSpec(memory_space=pltpu.VMEM)] * (2 + shards + groups),
-        out_specs=pl.BlockSpec(memory_space=pltpu.HBM),
+    parts = shards - 1
+    return pl.pallas_call(
+        functools.partial(accumulate_kernel, groups, rate),
+        out_shape=(jax.ShapeDtypeStruct((rows, width), jnp.float32), jax.ShapeDtypeStruct((rows, depth), jnp.bfloat16)),
+        in_specs=[pl.BlockSpec(memory_space=pltpu.SMEM), pl.BlockSpec(memory_space=pltpu.VMEM)]
+        + [pl.BlockSpec(memory_space=pltpu.HBM)] * (2 + groups),
+        out_specs=(pl.BlockSpec(memory_space=pltpu.VMEM),) * 2,
         scratch_shapes=[
-            pltpu.VMEM((shards, depth, width), jnp.bfloat16),
-            pltpu.VMEM((groups, rows, share), jnp.bfloat16),
-            pltpu.VMEM((width // tile, rows, tile), jnp.bfloat16),
-            pltpu.SemaphoreType.DMA((width // tile,)),
+            pltpu.VMEM((parts, rows, depth), jnp.bfloat16),
+            pltpu.VMEM((rows, width), jnp.bfloat16),
+            pltpu.VMEM((groups, rows, width // groups), jnp.bfloat16),
+            pltpu.SemaphoreType.DMA((parts,)),
+            pltpu.SemaphoreType.DMA,
+            pltpu.SemaphoreType.DMA((groups,)),
+            pltpu.SemaphoreType.DMA,
         ],
-        compiler_params=pltpu.CompilerParams(vmem_limit_bytes=24 * 2**20),
+        compiler_params=pltpu.CompilerParams(vmem_limit_bytes=36 * 2**20),
         cost_estimate=pl.CostEstimate(
-            flops=2 * depth * shards * rows * width,
-            bytes_accessed=2 * depth * shards * (rows + width) + 6 * rows * width,
+            flops=2 * parts * depth * rows * width,
+            bytes_accessed=2 * parts * depth * (rows + width) + 8 * rows * width,
             transcendentals=0,
         ),
-        name="mix",
-    )(jnp.stack([mine, own]), tokens, *cotangents, *pieces, weight)
-
-
-def gather(piece, axis, size, after=()):
+        name="accumulate",
+    )(jnp.stack([mine, own]), cotangents, tokens, weight, *pieces)
+
+
+def finish_kernel(rate, tokens_ref, cotangent_ref, total_ref, out_ref, outs, sems):
+    steps, _, tile = outs.shape
+    stores = []
+    for step in range(steps):
+        columns = slice(step * tile, (step + 1) * tile)
+        product = jnp.dot(tokens_ref[...], cotangent_ref[:, columns], preferred_element_type=jnp.float32)
+        outs[step] = (total_ref[:, columns] - rate * product).astype(jnp.bfloat16)
+        stores.append(pltpu.make_async_copy(outs.at[step], out_ref.at[:, pl.ds(step * tile, tile)], sems.at[step]))
+        stores[step].start()
+    for store in stores:
+        store.wait()
+
+
+def finish(tokens, cotangent, total, rate):
+    rows, width = total.shape
+    depth = tokens.shape[1]
+    tile = min(width, 256)
+    return pl.pallas_call(
+        functools.partial(finish_kernel, rate),
+        out_shape=jax.ShapeDtypeStruct((rows, width), jnp.bfloat16),
+        in_specs=[pl.BlockSpec(memory_space=pltpu.VMEM)] * 3,
+        out_specs=pl.BlockSpec(memory_space=pltpu.HBM),
+        scratch_shapes=[pltpu.VMEM((width // tile, rows, tile), jnp.bfloat16), pltpu.SemaphoreType.DMA((width // tile,))],
+        compiler_params=pltpu.CompilerParams(vmem_limit_bytes=16 * 2**20),
+        cost_estimate=pl.CostEstimate(
+            flops=2 * depth * rows * width, bytes_accessed=2 * depth * (rows + width) + 6 * rows * width, transcendentals=0
+        ),
+        name="finish",
+    )(tokens, cotangent, total)
+
+
+def gather(piece, axis, size):
     pieces = {0: piece}
     bit = size // 2
     while bit:
-        if bit == 1 and after:
-            (*held, _) = lax.optimization_barrier((*(pieces[k] for k in sorted(pieces)[1:]), after))
-            pieces.update(zip(sorted(pieces)[1:], held))
         for k in sorted(pieces):
             pieces[k ^ bit] = swap(pieces[k], axis, bit)
         bit //= 2
@@ -222,13 +278,13 @@
     rows, width = weight.shape
     inner_rate = inner_gain / math.sqrt(tokens.shape[0] * shards)
 
-    own_exchanges = [1 << bit for bit in range(shards.bit_length() - 1)]
+    rate = (1.0 - mix_weight) * inner_rate
+
     cotangents = gather(cotangent, "fsdp", shards)
     blocks = prepare(tokens, norm_gain, shards)
-    *_, blocks, coded_shared, coded_weight = lax.optimization_barrier(
-        (*(cotangents[k] for k in own_exchanges), blocks, shared_copy, weight)
-    )
     columns = lax.all_to_all(blocks, "fsdp", split_axis=0, concat_axis=0, tiled=True)
+    first = [cotangents[1 << bit] for bit in range(shards.bit_length() - 1)]
+    *_, coded_shared, coded_weight = lax.optimization_barrier((*first, blocks, shared_copy, weight))
 
     kept, sent = code_and_decode(own, coded_shared, coded_weight, groups)
     total = kept.astype(jnp.float32) + swap(sent, "replica", 1).astype(jnp.float32)
@@ -236,15 +292,14 @@
     while bit < groups:
         sent = swap(total[1::2].astype(jnp.bfloat16), "replica", bit)
         bit *= 2
-        if bit >= groups:
-            *_, sent = lax.optimization_barrier((*cotangents[: shards // 2 + 2], sent))
         total = total[0::2] + sent.astype(jnp.float32)
     average = total[0] / groups
     momentum_next = outer_beta * momentum + average
     master_next = master - outer_rate * (average + outer_beta * momentum_next)
-    pieces = gather(master_next.astype(jnp.bfloat16), "replica", groups, after=cotangents)
-
-    layer_next = mix(mine, own, columns, cotangents, pieces, weight, (1.0 - mix_weight) * inner_rate)
+    pieces = gather(master_next.astype(jnp.bfloat16), "replica", groups)
+
+    total, last = accumulate(mine, own, stage(cotangents[:-1]), columns, weight, pieces, rate)
+    layer_next = finish(last, cotangents[-1], total, rate)
     return (layer_next[None], master_next, momentum_next)
 
 

time: 91.5 us -> 139 us (1.52)
  waiting for transfers between devices: 41.8 us -> 92 us
  local copies, waits for them, and re-layouts: 11.8 us -> 7.03 us
  Pallas kernels: 11.6 us -> 16 us
    ppermute x12, waiting for transfers between devices: 41.8 us -> 92 us  [swap(): return lax.ppermute(value, axis, [(i, i ^ mask) for i in range(size)])]
    unnamed x36 -> x20, local copies, waits for them, and re-layouts: 11.7 us -> 6.97 us
    pallas_call x1 -> x3, Pallas kernels: 5.73 us -> 10.1 us  [the longest x1 6 us: accumulate(): pl.pallas_call(functools.partial(accumulate_kernel, groups, rate), out_sh...]
    ppermute x12, starting transfers between devices: 15.4 us -> 12.5 us  [swap(): return lax.ppermute(value, axis, [(i, i ^ mask) for i in range(size)])]
    all_to_all x1, starting transfers between devices: 5.71 us -> 7.42 us  [on_device(): lax.all_to_all(blocks, 'fsdp', split_axis=0, concat_axis=0, tiled=True)]
  transfers between devices with their start and end apart: 13 -> 13, of which waited for: 9 -> 6; matrix products, arithmetic and copies ran while one was open for 3% -> 2% of each run, Pallas kernels for 7% -> 8%
where the time goes in v10:
time: 139 us; the launch traced here: 138 us
  waiting for transfers between devices  92 us (66%)
  starting transfers between devices  19.9 us (14%)
  Pallas kernels  16 us (12%)
  local copies, waits for them, and re-layouts  7.03 us (5%)
  other arithmetic  2.76 us (2%)
    ppermute x12, waiting for transfers between devices, swap(): return lax.ppermute(value, axis, [(i, i ^ mask) for i in range(size)])  92 us
    ppermute x12, starting transfers between devices, swap(): return lax.ppermute(value, axis, [(i, i ^ mask) for i in range(size)])  12.5 us
    all_to_all x1, starting transfers between devices, on_device(): lax.all_to_all(blocks, 'fsdp', split_axis=0, concat_axis=0, tiled=True)  7.42 us
    unnamed x20, local copies, waits for them, and re-layouts  6.97 us
    pallas_call x1, Pallas kernels, accumulate(): pl.pallas_call(functools.partial(accumulate_kernel, groups, rate), out_sh...  6 us
    pallas_call x1, Pallas kernels, code_and_decode(): pl.pallas_call(code_kernel, out_shape=(half, half), in_specs=[pl.BlockSpe...  3.69 us
  transfers between devices with their start and end apart: 13, of which 6 were waited for; matrix products, arithmetic and copies ran while one was open for 2% of the time, Pallas kernels for 8%

profile of v10, /device:TPU:0, one launch (start us, length us, event | category | flops | bytes accessed | tf_op | source)
XLA Modules:
  0.0 138.4 jit_solution(7458672455696696643)
XLA Ops:
  0.6 0.7 reshape.16
  1.4 1.6 %copy-done.3 = bf16[1,128,8192]{2,1,0:T(8,128)(2,1)S(1)} copy-done((bf16[1,128,8192]{2,1,0:T(8,128)(2,1)S(1)}, bf16[1,128,8192]{2,1,0:T(8,128)(2,1)}, u32[]{:S(2)}) %copy-start.3) | copy-done | bytes 2097176
  2.9 2.2 %prepare.1 = bf16[8,1024,128]{2,1,0:T(8,128)(2,1)} custom-call(bf16[128,8192]{1,0:T(8,128)(2,1)S(1)} %bitcast.17, f32[1,8192]{1,0:T(1,128)S(1)} %bitcast.22), custom_call_target="tpu_custom_call" | custom-call | flops 5242880 | bytes 4194304 | tf_op jit(solution)/shard_map/prepare/pallas_call | solution.py:58
  5.2 0.0 copy-start.5
  5.2 7.4 %all-to-all-start = ((bf16[8,1024,128]{2,1,0:T(8,128)(2,1)}), bf16[8,1024,128]{2,1,0:T(8,128)(2,1)}, u32[]{:S(2)}, u32[]{:S(2)}) async-start(bf16[8,1024,128]{2,1,0:T(8,128)(2,1)} %prepare.1), calls=%async_computation | async-start | bytes 4194304 | tf_op jit(solution)/shard_map/all_to_all | solution.py:285
  12.6 2.9 %collective-permute-start.3 = (bf16[128,1024]{1,0:T(8,128)(2,1)S(1)}, bf16[128,1024]{1,0:T(8,128)(2,1)}, u32[]{:S(2)}, u32[]{:S(2)}) collective-permute-start(bf16[128,1024]{1,0:T(8,128)(2,1)S(1)} %bitcast.18), channel_id=1, source_target_pairs={{0,4},{1,5},{2,6},{3,7},{4,0},{5,1},{6,2},{7,3},{8,12},{9,13},{10,... | collective-permute-start | bytes 786440 | tf_op jit(solution)/shard_map/ppermute | solution.py:24
  15.5 1.5 %collective-permute-start.1 = (bf16[128,1024]{1,0:T(8,128)(2,1)S(1)}, bf16[128,1024]{1,0:T(8,128)(2,1)}, u32[]{:S(2)}, u32[]{:S(2)}) collective-permute-start(bf16[128,1024]{1,0:T(8,128)(2,1)S(1)} %bitcast.19), channel_id=1, source_target_pairs={{0,2},{1,3},{2,0},{3,1},{4,6},{5,7},{6,4},{7,5},{8,10},{9,11},{10,... | collective-permute-start | bytes 786440 | tf_op jit(solution)/shard_map/ppermute | solution.py:24
  17.0 1.5 %collective-permute-start = (bf16[128,1024]{1,0:T(8,128)(2,1)S(1)}, bf16[128,1024]{1,0:T(8,128)(2,1)S(1)}, u32[]{:S(2)}, u32[]{:S(2)}) collective-permute-start(bf16[128,1024]{1,0:T(8,128)(2,1)S(1)} %bitcast.20), channel_id=1, source_target_pairs={{0,1},{1,0},{2,3},{3,2},{4,5},{5,4},{6,7},{7,6},{8,9},{9,8},{10,11... | collective-permute-start | bytes 786440 | tf_op jit(solution)/shard_map/ppermute | solution.py:24
  18.5 53.7 %collective-permute-done.3.refs_4_ = bf16[128,1024]{1,0:T(8,128)(2,1)} collective-permute-done((bf16[128,1024]{1,0:T(8,128)(2,1)S(1)}, bf16[128,1024]{1,0:T(8,128)(2,1)}, u32[]{:S(2)}, u32[]{:S(2)}) %collective-permute-start.3) | collective-permute-done | bytes 262176 | tf_op jit(solution)/shard_map/ppermute | solution.py:24
  72.2 1.7 %copy-done.4 = bf16[1024,1024]{1,0:T(8,128)(2,1)S(1)} copy-done((bf16[1024,1024]{1,0:T(8,128)(2,1)S(1)}, bf16[1024,1024]{1,0:T(8,128)(2,1)}, u32[]{:S(2)}) %copy-start.4) | copy-done | bytes 2097176
  73.9 3.7 %code_and_decode.1 = (bf16[2,1024,256]{2,1,0:T(8,128)(2,1)S(1)}, bf16[2,1024,256]{2,1,0:T(8,128)(2,1)S(1)}) custom-call(s32[1]{0:T(128)} %bitcast.1.own_ref, bf16[1024,1024]{1,0:T(8,128)(2,1)S(1)} %copy-done.4, bf16[1024,1024]{1,0:T(8,128)(2,1)S(1)} %bitcast.15), custom_call_target="tpu_custom_call" | custom-call | flops 20971520 | bytes 377487360 | tf_op jit(solution)/shard_map/code_and_decode/pallas_call | solution.py:128
  77.6 0.1 collective-permute-start.6
  77.7 2.6 %collective-permute-done.6 = bf16[2,1024,256]{2,1,0:T(8,128)(2,1)S(1)} collective-permute-done((bf16[2,1024,256]{2,1,0:T(8,128)(2,1)S(1)}, bf16[2,1024,256]{2,1,0:T(8,128)(2,1)S(1)}, u32[]{:S(2)}, u32[]{:S(2)}) %collective-permute-start.6) | collective-permute-done | bytes 1048608 | tf_op jit(solution)/shard_map/ppermute | solution.py:24
  80.3 0.3 convert_add_fusion
  80.6 0.1 slice.23
  80.7 1.6 %collective-permute-start.7 = (bf16[1,1024,256]{2,1,0:T(8,128)(2,1)S(1)}, bf16[1,1024,256]{2,1,0:T(8,128)(2,1)S(1)}, u32[]{:S(2)}, u32[]{:S(2)}) collective-permute-start(bf16[1,1024,256]{2,1,0:T(8,128)(2,1)S(1)} %slice.23), channel_id=1, source_target_pairs={{0,16},{8,24},{16,0},{24,8},{1,17},{9,25},{17,1},{25,9},{2,18},{10... | collective-permute-start | bytes 1572872 | tf_op jit(solution)/shard_map/ppermute | solution.py:24
  82.2 12.5 %collective-permute-done.7 = bf16[1,1024,256]{2,1,0:T(8,128)(2,1)S(1)} collective-permute-done((bf16[1,1024,256]{2,1,0:T(8,128)(2,1)S(1)}, bf16[1,1024,256]{2,1,0:T(8,128)(2,1)S(1)}, u32[]{:S(2)}, u32[]{:S(2)}) %collective-permute-start.7) | collective-permute-done | bytes 524320 | tf_op jit(solution)/shard_map/ppermute | solution.py:24
  94.7 1.7 %fusion.2 = (bf16[1024,256]{1,0:T(8,128)(2,1)S(1)}, f32[1024,256]{1,0:T(8,128)}, f32[1024,256]{1,0:T(8,128)}) fusion(f32[1024,256]{1,0:T(8,128)S(1)} %copy-done.8, bf16[1,1024,256]{2,1,0:T(8,128)(2,1)S(1)} %collective-permute-done.7, f32[2,1024,256]{2,1,0:T(8,128)S(1)} %convert_add_fusion, f32[1024,256]{1,0:T(8,128)S(1)} %copy-done.9), kind=kLoop, calls=%fused_computation.8 | loop fusion | flops 2621440 | bytes 6291456 | tf_op jit(solution)/shard_map/convert_element_type | solution.py:299
  96.4 1.5 %collective-permute-start.9 = (bf16[1024,256]{1,0:T(8,128)(2,1)S(1)}, bf16[1024,256]{1,0:T(8,128)(2,1)S(1)}, u32[]{:S(2)}, u32[]{:S(2)}) collective-permute-start(bf16[1024,256]{1,0:T(8,128)(2,1)S(1)} %get-tuple-element.15.refs_0_), channel_id=1, source_target_pairs={{0,16},{8,24},{16,0},{24,8},{1,17},{9,25},{17,1},{25,9},{2,18},{10... | collective-permute-start | bytes 1572872 | tf_op jit(solution)/shard_map/ppermute | solution.py:24
  97.9 11.6 %collective-permute-done.9.refs_2_ = bf16[1024,256]{1,0:T(8,128)(2,1)S(1)} collective-permute-done((bf16[1024,256]{1,0:T(8,128)(2,1)S(1)}, bf16[1024,256]{1,0:T(8,128)(2,1)S(1)}, u32[]{:S(2)}, u32[]{:S(2)}) %collective-permute-start.9) | collective-permute-done | bytes 524320 | tf_op jit(solution)/shard_map/ppermute | solution.py:24
  109.5 1.5 %collective-permute-start.4 = (bf16[128,1024]{1,0:T(8,128)(2,1)}, bf16[128,1024]{1,0:T(8,128)(2,1)}, u32[]{:S(2)}, u32[]{:S(2)}) collective-permute-start(bf16[128,1024]{1,0:T(8,128)(2,1)} %collective-permute-done.3.refs_4_), channel_id=1, source_target_pairs={{0,1},{1,0},{2,3},{3,2},{4,5},{5,4},{6,7},{7,6},{8,9},{9,8},{10,11... | collective-permute-start | bytes 786440 | tf_op jit(solution)/shard_map/ppermute | solution.py:24
  111.0 0.6 collective-permute-start.2
  111.6 7.0 %collective-permute-done.5.refs_6_ = bf16[128,1024]{1,0:T(8,128)(2,1)} collective-permute-done((bf16[128,1024]{1,0:T(8,128)(2,1)}, bf16[128,1024]{1,0:T(8,128)(2,1)}, u32[]{:S(2)}, u32[]{:S(2)}) %collective-permute-start.5) | collective-permute-done | bytes 262176 | tf_op jit(solution)/shard_map/ppermute | solution.py:24
  118.6 1.5 %collective-permute-start.11 = (bf16[128,1024]{1,0:T(8,128)(2,1)}, bf16[128,1024]{1,0:T(8,128)(2,1)}, u32[]{:S(2)}, u32[]{:S(2)}) collective-permute-start(bf16[128,1024]{1,0:T(8,128)(2,1)} %collective-permute-done.5.refs_6_), channel_id=1, source_target_pairs={{0,1},{1,0},{2,3},{3,2},{4,5},{5,4},{6,7},{7,6},{8,9},{9,8},{10,11... | collective-permute-start | bytes 786440 | tf_op jit(solution)/shard_map/ppermute | solution.py:24
  120.0 0.1 pad_add_fusion.place_ref
  120.1 4.5 %collective-permute-done.2.refs_3_ = bf16[128,1024]{1,0:T(8,128)(2,1)} collective-permute-done((bf16[128,1024]{1,0:T(8,128)(2,1)}, bf16[128,1024]{1,0:T(8,128)(2,1)}, u32[]{:S(2)}, u32[]{:S(2)}) %collective-permute-start.2) | collective-permute-done | bytes 262176 | tf_op jit(solution)/shard_map/ppermute | solution.py:24
  124.6 0.9 copy-done.7
  125.5 1.4 stage.1.cotangent_ref
  126.9 1.2 copy-done.1
  128.2 1.5 %copy-done.2 = bf16[896,1024]{1,0:T(8,128)(2,1)S(1)} copy-done((bf16[896,1024]{1,0:T(8,128)(2,1)S(1)}, bf16[896,1024]{1,0:T(8,128)(2,1)}, u32[]{:S(2)}) %copy-start.2) | copy-done | bytes 1835032
  129.7 6.0 %accumulate.1 = (f32[1024,1024]{1,0:T(8,128)S(1)}, bf16[1024,128]{1,0:T(8,128)(2,1)S(1)}) custom-call(s32[2]{0:T(128)S(1)} %pad_add_fusion.place_ref, bf16[896,1024]{1,0:T(8,128)(2,1)S(1)} %copy-done.2, bf16[8,1024,128]{2,1,0:T(8,128)(2,1)} %all-to-all-done.tokens_ref, bf16[1024,1024]{1,0:T(8,128)(2,1)S(1)} %bitcast.16, ...), custom_call_target="tpu_custom_call" | custom-call | flops 1879048192 | bytes 12058624 | tf_op jit(solution)/shard_map/accumulate/pallas_call | solution.py:206
  135.7 2.7 %finish.1 = bf16[1024,1024]{1,0:T(8,128)(2,1)} custom-call(bf16[1024,128]{1,0:T(8,128)(2,1)S(1)} %get-tuple-element.13.tokens_ref, bf16[128,1024]{1,0:T(8,128)(2,1)} %collective-permute-done.11.cotangent_ref, f32[1024,1024]{1,0:T(8,128)S(1)} %get-tuple-element.14.total_ref), custom_call_target="tpu_custom_call" | custom-call | flops 268435456 | bytes 6815744 | tf_op jit(solution)/shard_map/finish/pallas_call | solution.py:248
  (24 shorter events, 0.1 us)
Async XLA Ops:
  1.4 1.6 %copy-start.3 = (bf16[1,128,8192]{2,1,0:T(8,128)(2,1)S(1)}, bf16[1,128,8192]{2,1,0:T(8,128)(2,1)}, u32[]{:S(2)}) copy-start(bf16[1,128,8192]{2,1,0:T(8,128)(2,1)} %param.7) | copy-start | bytes 6291460
  5.2 7.5 %copy-start.5 = (bf16[1,128,1024]{2,1,0:T(8,128)(2,1)S(1)}, bf16[1,128,1024]{2,1,0:T(8,128)(2,1)}, u32[]{:S(2)}) copy-start(bf16[1,128,1024]{2,1,0:T(8,128)(2,1)} %param.9) | copy-start | bytes 786436
  5.2 67.0 %copy-start = (bf16[1,1024,1024]{2,1,0:T(8,128)(2,1)S(1)}, bf16[1,1024,1024]{2,1,0:T(8,128)(2,1)}, u32[]{:S(2)}) copy-start(bf16[1,1024,1024]{2,1,0:T(8,128)(2,1)} %param.10) | copy-start | bytes 6291460
  5.2 123.0 %all-to-all-start = ((bf16[8,1024,128]{2,1,0:T(8,128)(2,1)}), bf16[8,1024,128]{2,1,0:T(8,128)(2,1)}, u32[]{:S(2)}, u32[]{:S(2)}) async-start(bf16[8,1024,128]{2,1,0:T(8,128)(2,1)} %prepare.1), calls=%async_computation | async-start | bytes 4194304 | tf_op jit(solution)/shard_map/all_to_all | solution.py:285
  12.6 59.6 %collective-permute-start.3 = (bf16[128,1024]{1,0:T(8,128)(2,1)S(1)}, bf16[128,1024]{1,0:T(8,128)(2,1)}, u32[]{:S(2)}, u32[]{:S(2)}) collective-permute-start(bf16[128,1024]{1,0:T(8,128)(2,1)S(1)} %bitcast.18), channel_id=1, source_target_pairs={{0,4},{1,5},{2,6},{3,7},{4,0},{5,1},{6,2},{7,3},{8,12},{9,13},{10,... | collective-permute-start | bytes 786440 | tf_op jit(solution)/shard_map/ppermute | solution.py:24
  15.5 56.7 %collective-permute-start.1 = (bf16[128,1024]{1,0:T(8,128)(2,1)S(1)}, bf16[128,1024]{1,0:T(8,128)(2,1)}, u32[]{:S(2)}, u32[]{:S(2)}) collective-permute-start(bf16[128,1024]{1,0:T(8,128)(2,1)S(1)} %bitcast.19), channel_id=1, source_target_pairs={{0,2},{1,3},{2,0},{3,1},{4,6},{5,7},{6,4},{7,5},{8,10},{9,11},{10,... | collective-permute-start | bytes 786440 | tf_op jit(solution)/shard_map/ppermute | solution.py:24
  17.0 55.2 %collective-permute-start = (bf16[128,1024]{1,0:T(8,128)(2,1)S(1)}, bf16[128,1024]{1,0:T(8,128)(2,1)S(1)}, u32[]{:S(2)}, u32[]{:S(2)}) collective-permute-start(bf16[128,1024]{1,0:T(8,128)(2,1)S(1)} %bitcast.20), channel_id=1, source_target_pairs={{0,1},{1,0},{2,3},{3,2},{4,5},{5,4},{6,7},{7,6},{8,9},{9,8},{10,11... | collective-permute-start | bytes 786440 | tf_op jit(solution)/shard_map/ppermute | solution.py:24
  72.2 5.4 %copy-start.6 = (bf16[128,1024]{1,0:T(8,128)(2,1)}, bf16[128,1024]{1,0:T(8,128)(2,1)S(1)}, u32[]{:S(2)}) copy-start(bf16[128,1024]{1,0:T(8,128)(2,1)S(1)} %collective-permute-done.refs_1_) | copy-start | bytes 786436
  72.2 1.7 %copy-start.4 = (bf16[1024,1024]{1,0:T(8,128)(2,1)S(1)}, bf16[1024,1024]{1,0:T(8,128)(2,1)}, u32[]{:S(2)}) copy-start(bf16[1024,1024]{1,0:T(8,128)(2,1)} %shared_ref) | copy-start | bytes 6291460
  77.6 2.7 %collective-permute-start.6 = (bf16[2,1024,256]{2,1,0:T(8,128)(2,1)S(1)}, bf16[2,1024,256]{2,1,0:T(8,128)(2,1)S(1)}, u32[]{:S(2)}, u32[]{:S(2)}) collective-permute-start(bf16[2,1024,256]{2,1,0:T(8,128)(2,1)S(1)} %get-tuple-element.12), channel_id=1, source_target_pairs={{0,8},{8,0},{16,24},{24,16},{1,9},{9,1},{17,25},{25,17},{2,10},{10... | collective-permute-start | bytes 3145736 | tf_op jit(solution)/shard_map/ppermute | solution.py:24
  80.3 14.4 %copy-start.8 = (f32[1024,256]{1,0:T(8,128)S(1)}, f32[1024,256]{1,0:T(8,128)}, u32[]{:S(2)}) copy-start(f32[1024,256]{1,0:T(8,128)} %param.12) | copy-start | bytes 3145732
  80.3 14.4 %copy-start.9 = (f32[1024,256]{1,0:T(8,128)S(1)}, f32[1024,256]{1,0:T(8,128)}, u32[]{:S(2)}) copy-start(f32[1024,256]{1,0:T(8,128)} %param.13) | copy-start | bytes 3145732
  80.7 14.0 %collective-permute-start.7 = (bf16[1,1024,256]{2,1,0:T(8,128)(2,1)S(1)}, bf16[1,1024,256]{2,1,0:T(8,128)(2,1)S(1)}, u32[]{:S(2)}, u32[]{:S(2)}) collective-permute-start(bf16[1,1024,256]{2,1,0:T(8,128)(2,1)S(1)} %slice.23), channel_id=1, source_target_pairs={{0,16},{8,24},{16,0},{24,8},{1,17},{9,25},{17,1},{25,9},{2,18},{10... | collective-permute-start | bytes 1572872 | tf_op jit(solution)/shard_map/ppermute | solution.py:24
  96.4 13.1 %collective-permute-start.9 = (bf16[1024,256]{1,0:T(8,128)(2,1)S(1)}, bf16[1024,256]{1,0:T(8,128)(2,1)S(1)}, u32[]{:S(2)}, u32[]{:S(2)}) collective-permute-start(bf16[1024,256]{1,0:T(8,128)(2,1)S(1)} %get-tuple-element.15.refs_0_), channel_id=1, source_target_pairs={{0,16},{8,24},{16,0},{24,8},{1,17},{9,25},{17,1},{25,9},{2,18},{10... | collective-permute-start | bytes 1572872 | tf_op jit(solution)/shard_map/ppermute | solution.py:24
  97.9 30.3 %collective-permute-start.8 = (bf16[1024,256]{1,0:T(8,128)(2,1)S(1)}, bf16[1024,256]{1,0:T(8,128)(2,1)}, u32[]{:S(2)}, u32[]{:S(2)}) collective-permute-start(bf16[1024,256]{1,0:T(8,128)(2,1)S(1)} %get-tuple-element.15.refs_0_), channel_id=1, source_target_pairs={{0,8},{8,0},{16,24},{24,16},{1,9},{9,1},{17,25},{25,17},{2,10},{10... | collective-permute-start | bytes 1572872 | tf_op jit(solution)/shard_map/ppermute | solution.py:24
  109.5 18.6 %collective-permute-start.10 = (bf16[1024,256]{1,0:T(8,128)(2,1)S(1)}, bf16[1024,256]{1,0:T(8,128)(2,1)}, u32[]{:S(2)}, u32[]{:S(2)}) collective-permute-start(bf16[1024,256]{1,0:T(8,128)(2,1)S(1)} %collective-permute-done.9.refs_2_), channel_id=1, source_target_pairs={{0,8},{8,0},{16,24},{24,16},{1,9},{9,1},{17,25},{25,17},{2,10},{10... | collective-permute-start | bytes 1572872 | tf_op jit(solution)/shard_map/ppermute | solution.py:24
  109.5 9.0 %collective-permute-start.5 = (bf16[128,1024]{1,0:T(8,128)(2,1)}, bf16[128,1024]{1,0:T(8,128)(2,1)}, u32[]{:S(2)}, u32[]{:S(2)}) collective-permute-start(bf16[128,1024]{1,0:T(8,128)(2,1)} %collective-permute-done.3.refs_4_), channel_id=1, source_target_pairs={{0,2},{1,3},{2,0},{3,1},{4,6},{5,7},{6,4},{7,5},{8,10},{9,11},{10,... | collective-permute-start | bytes 786440 | tf_op jit(solution)/shard_map/ppermute | solution.py:24
  109.5 10.6 %collective-permute-start.4 = (bf16[128,1024]{1,0:T(8,128)(2,1)}, bf16[128,1024]{1,0:T(8,128)(2,1)}, u32[]{:S(2)}, u32[]{:S(2)}) collective-permute-start(bf16[128,1024]{1,0:T(8,128)(2,1)} %collective-permute-done.3.refs_4_), channel_id=1, source_target_pairs={{0,1},{1,0},{2,3},{3,2},{4,5},{5,4},{6,7},{7,6},{8,9},{9,8},{10,11... | collective-permute-start | bytes 786440 | tf_op jit(solution)/shard_map/ppermute | solution.py:24
  111.0 13.6 %collective-permute-start.2 = (bf16[128,1024]{1,0:T(8,128)(2,1)}, bf16[128,1024]{1,0:T(8,128)(2,1)}, u32[]{:S(2)}, u32[]{:S(2)}) collective-permute-start(bf16[128,1024]{1,0:T(8,128)(2,1)} %collective-permute-done.1.refs_2_), channel_id=1, source_target_pairs={{0,1},{1,0},{2,3},{3,2},{4,5},{5,4},{6,7},{7,6},{8,9},{9,8},{10,11... | collective-permute-start | bytes 786440 | tf_op jit(solution)/shard_map/ppermute | solution.py:24
  118.6 17.1 %collective-permute-start.11 = (bf16[128,1024]{1,0:T(8,128)(2,1)}, bf16[128,1024]{1,0:T(8,128)(2,1)}, u32[]{:S(2)}, u32[]{:S(2)}) collective-permute-start(bf16[128,1024]{1,0:T(8,128)(2,1)} %collective-permute-done.5.refs_6_), channel_id=1, source_target_pairs={{0,1},{1,0},{2,3},{3,2},{4,5},{5,4},{6,7},{7,6},{8,9},{9,8},{10,11... | collective-permute-start | bytes 786440 | tf_op jit(solution)/shard_map/ppermute | solution.py:24
  124.6 1.0 copy-start.7
  126.9 1.2 copy-start.1
  128.2 1.5 %copy-start.2 = (bf16[896,1024]{1,0:T(8,128)(2,1)S(1)}, bf16[896,1024]{1,0:T(8,128)(2,1)}, u32[]{:S(2)}) copy-start(bf16[896,1024]{1,0:T(8,128)(2,1)} %copy-done.1) | copy-start | bytes 5505028

commit v11 on v8

v11 whole, which is shorter than its diff:
```python
import functools
import math

import jax
import jax.numpy as jnp
from jax import lax
from jax.experimental import pallas as pl
from jax.experimental.pallas import tpu as pltpu
from jax.sharding import PartitionSpec as P

BLOCK = 64


norm_eps = 1e-05
inner_gain = 0.4
outer_rate = 0.7
outer_beta = 0.9
mix_weight = 0.5
code_range = 448.0


def swap(value, axis, mask):
    size = lax.axis_size(axis)
    return lax.ppermute(value, axis, [(i, i ^ mask) for i in range(size)])


def prepare_kernel(shards, skip, mine_ref, tokens_ref, gain_ref, group_ref, *refs):
    other_refs, (tokens, group, load_sems, store_sems) = refs[: shards // 2], refs[shards // 2 :]
    lanes = 128
    rows, count = other_refs[0].shape
    features = shards * rows
    mine = mine_ref[0]
    loads = []
    for k in range(shards):
        columns = pl.ds(k * rows, rows)
        loads.append(pltpu.make_async_copy(tokens_ref.at[:, columns], tokens.at[:, columns], load_sems.at[k]))
        loads[k].start()
    squares = jnp.zeros((count, lanes), jnp.float32)
    for k in range(shards):
        loads[k].wait()
        for start in range(k * rows, (k + 1) * rows, lanes):
            block = tokens[:, start : start + lanes].astype(jnp.float32)
            squares = squares + block * block
    mean = jnp.sum(squares, axis=-1, keepdims=True) / features
    inverse = jnp.broadcast_to(lax.rsqrt(mean + norm_eps), (count, lanes))

    def write(ref, shard):
        for start in range(0, rows, lanes):
            columns = pl.ds(pl.multiple_of(shard * rows + start, lanes), lanes)
            normed = tokens[:, columns].astype(jnp.float32) * inverse * gain_ref[:, columns]
            ref[start : start + lanes] = jnp.transpose(normed).astype(jnp.bfloat16)

    stores = []
    for place, k in enumerate(without(skip, shards)):
        write(group.at[place], k + mine % (2 * skip) // skip * skip)
        stores.append(pltpu.make_async_copy(group.at[place], group_ref.at[place], store_sems.at[place]))
        stores[place].start()
    for ref, k in zip(other_refs, without(skip, shards)):
        write(ref, mine ^ (k + skip))
    for store in stores:
        store.wait()


def prepare(mine, tokens, gain, shards, skip):
    count, features = tokens.shape
    rows = features // shards
    half = shards // 2
    block = jax.ShapeDtypeStruct((rows, count), jnp.bfloat16)
    group, *others = pl.pallas_call(
        functools.partial(prepare_kernel, shards, skip),
        out_shape=(jax.ShapeDtypeStruct((half, rows, count), jnp.bfloat16),) + (block,) * half,
        in_specs=[
            pl.BlockSpec(memory_space=pltpu.SMEM),
            pl.BlockSpec(memory_space=pltpu.HBM),
            pl.BlockSpec(memory_space=pltpu.VMEM),
        ],
        out_specs=(pl.BlockSpec(memory_space=pltpu.HBM),) + (pl.BlockSpec(memory_space=pltpu.VMEM),) * half,
        scratch_shapes=[
            pltpu.VMEM((count, features), jnp.bfloat16),
            pltpu.VMEM((half, rows, count), jnp.bfloat16),
            pltpu.SemaphoreType.DMA((shards,)),
            pltpu.SemaphoreType.DMA((half,)),
        ],
        compiler_params=pltpu.CompilerParams(vmem_limit_bytes=16 * 2**20),
        cost_estimate=pl.CostEstimate(
            flops=5 * count * features, bytes_accessed=4 * count * features, transcendentals=count
        ),
        name="prepare",
    )(mine.reshape(1), tokens, gain.astype(jnp.float32).reshape(1, features))
    return group, others


def code_kernel(own_ref, shared_ref, weight_ref, kept_ref, sent_ref, shared, weight, decoded, sems):
    lanes = 2 * BLOCK
    groups, tile, share = decoded.shape
    rows, width = shared.shape
    own = own_ref[0]
    low = lax.broadcasted_iota(jnp.int32, (tile, lanes), 1) < BLOCK

    def loads(i):
        part = pl.ds(pl.multiple_of(i * tile, tile), tile)
        return (
            pltpu.make_async_copy(shared_ref.at[part], shared.at[part], sems.at[0, i]),
            pltpu.make_async_copy(weight_ref.at[part], weight.at[part], sems.at[1, i]),
        )

    for i in range(rows // tile):
        for load in loads(i):
            load.start()

    def step(i, _):
        for load in loads(i):
            load.wait()
        part = pl.ds(pl.multiple_of(i * tile, tile), tile)
        for start in range(0, width, lanes):
            columns = slice(start, start + lanes)
            delta = shared[part, columns].astype(jnp.float32) - weight[part, columns].astype(jnp.float32)
            size = jnp.abs(delta)
            largest = jnp.where(
                low,
                jnp.max(jnp.where(low, size, 0.0), axis=-1, keepdims=True),
                jnp.max(jnp.where(low, 0.0, size), axis=-1, keepdims=True),
            )
            scale = ((largest + 1e-06) * (1.0 / code_range)).astype(jnp.bfloat16).astype(jnp.float32)
            coded = (delta * pl.reciprocal(scale)).astype(jnp.bfloat16)
            value = (coded.astype(jnp.float32) * scale).astype(jnp.bfloat16)
            piece = min(share, lanes)
            for at in range(0, lanes, piece):
                group, offset = divmod(start + at, share)
                decoded[group, :, offset : offset + piece] = value[:, at : at + piece]
        for k in range(0, groups, 2):
            kept_ref[k // 2, part] = decoded[own ^ k]
            sent_ref[k // 2, part] = decoded[own ^ (k + 1)]
        return 0

    lax.fori_loop(0, rows // tile, step, 0)


def code_and_decode(own, shared, weight, groups):
    rows, width = shared.shape
    tile = min(rows, 128)
    share = width // groups
    half = jax.ShapeDtypeStruct((groups // 2, rows, share), jnp.bfloat16)
    return pl.pallas_call(
        code_kernel,
        out_shape=(half, half),
        in_specs=[pl.BlockSpec(memory_space=pltpu.SMEM)] + [pl.BlockSpec(memory_space=pltpu.HBM)] * 2,
        out_specs=(pl.BlockSpec(memory_space=pltpu.VMEM),) * 2,
        scratch_shapes=[
            pltpu.VMEM((rows, width), jnp.bfloat16),
            pltpu.VMEM((rows, width), jnp.bfloat16),
            pltpu.VMEM((groups, tile, share), jnp.bfloat16),
            pltpu.SemaphoreType.DMA((2, rows // tile)),
        ],
        compiler_params=pltpu.CompilerParams(vmem_limit_bytes=16 * 2**20),
        cost_estimate=pl.CostEstimate(flops=20 * rows * width, bytes_accessed=6 * rows * width, transcendentals=0),
        name="code_and_decode",
    )(own.reshape(1), shared, weight)


def accumulate_kernel(offsets, others, rate, place_ref, tokens_ref, weight_ref, *refs):
    parts = len(offsets)
    group_refs, refs = refs[:parts], refs[parts:]
    other_refs, refs = refs[:others], refs[others : 2 * others] + refs[2 * others :]
    cotangent_refs, refs = refs[:others], refs[others:]
    total_ref, tokens, weight, token_sems, weight_sem = refs
    loads = [
        pltpu.make_async_copy(tokens_ref.at[place_ref[0] ^ place], tokens.at[place], token_sems.at[place])
        for place in range(parts)
    ]
    loads.append(pltpu.make_async_copy(weight_ref, weight, weight_sem))
    for load in loads:
        load.start()
    width = total_ref.shape[1]
    tile = min(width, 256)
    for load in loads[:-1]:
        load.wait()
    left = jnp.concatenate([tokens[place] for place in range(parts)] + [ref[...] for ref in other_refs], axis=1)
    for start in range(0, width, tile):
        columns = slice(start, start + tile)
        right = jnp.concatenate([ref[:, columns] for ref in group_refs + cotangent_refs], axis=0)
        product = jnp.dot(left, right, preferred_element_type=jnp.float32)
        if start == 0:
            loads[-1].wait()
        total_ref[:, columns] = mix_weight * weight[:, columns].astype(jnp.float32) - rate * product


def accumulate(place, offsets, tokens, group, other_tokens, others, weight, rate):
    parts, rows, depth = tokens.shape
    width = weight.shape[1]
    whole = pl.BlockSpec(memory_space=pltpu.VMEM)
    remote = pl.BlockSpec(memory_space=pltpu.HBM)
    return pl.pallas_call(
        functools.partial(accumulate_kernel, offsets, len(others), rate),
        out_shape=jax.ShapeDtypeStruct((rows, width), jnp.float32),
        in_specs=[pl.BlockSpec(memory_space=pltpu.SMEM), remote, remote] + [whole] * (parts + 2 * len(others)),
        out_specs=whole,
        scratch_shapes=[
            pltpu.VMEM((parts, rows, depth), jnp.bfloat16),
            pltpu.VMEM((rows, width), jnp.bfloat16),
            pltpu.SemaphoreType.DMA((parts,)),
            pltpu.SemaphoreType.DMA,
        ],
        compiler_params=pltpu.CompilerParams(vmem_limit_bytes=20 * 2**20),
        cost_estimate=pl.CostEstimate(
            flops=2 * (parts + len(others)) * depth * rows * width,
            bytes_accessed=2 * (parts + len(others)) * depth * (rows + width) + 6 * rows * width,
            transcendentals=0,
        ),
        name="accumulate",
    )(place.reshape(1), tokens, weight, *group, *other_tokens, *others)


def place_kernel(own_ref, *refs):
    *piece_refs, out_ref = refs
    for k, ref in enumerate(piece_refs):
        out_ref[own_ref[0] ^ k] = ref[...]


def put_in_place(own, pieces):
    rows, share = pieces[0].shape
    return pl.pallas_call(
        place_kernel,
        out_shape=jax.ShapeDtypeStruct((len(pieces), rows, share), jnp.bfloat16),
        in_specs=[pl.BlockSpec(memory_space=pltpu.SMEM)] + [pl.BlockSpec(memory_space=pltpu.VMEM)] * len(pieces),
        out_specs=pl.BlockSpec(memory_space=pltpu.VMEM),
        compiler_params=pltpu.CompilerParams(vmem_limit_bytes=16 * 2**20),
        cost_estimate=pl.CostEstimate(flops=0, bytes_accessed=4 * len(pieces) * rows * share, transcendentals=0),
        name="put_in_place",
    )(own.reshape(1), *pieces)


def finish_kernel(parts, rate, *refs):
    token_refs, refs = refs[:parts], refs[parts:]
    cotangent_refs, refs = refs[:parts], refs[parts:]
    total_ref, shared_ref, out_ref, outs, sems = refs
    share = shared_ref.shape[2]
    steps, _, tile = outs.shape
    left = jnp.concatenate([ref[...] for ref in token_refs], axis=1)
    stores = []
    for step in range(steps):
        columns = slice(step * tile, (step + 1) * tile)
        right = jnp.concatenate([ref[:, columns] for ref in cotangent_refs], axis=0)
        total = total_ref[:, columns] - rate * jnp.dot(left, right, preferred_element_type=jnp.float32)
        for group in range(step * tile // share, (step + 1) * tile // share):
            part = slice(group * share - step * tile, (group + 1) * share - step * tile)
            shared = shared_ref[group].astype(jnp.float32)
            outs[step, :, part] = (total[:, part] + (1.0 - mix_weight) * shared).astype(jnp.bfloat16)
        stores.append(pltpu.make_async_copy(outs.at[step], out_ref.at[:, pl.ds(step * tile, tile)], sems.at[step]))
        stores[step].start()
    for store in stores:
        store.wait()


def finish(tokens, cotangents, total, shared, rate):
    parts = len(tokens)
    rows, width = total.shape
    depth = tokens[0].shape[1]
    tile = max(shared.shape[2], 256)
    return pl.pallas_call(
        functools.partial(finish_kernel, parts, rate),
        out_shape=jax.ShapeDtypeStruct((rows, width), jnp.bfloat16),
        in_specs=[pl.BlockSpec(memory_space=pltpu.VMEM)] * (2 * parts + 2),
        out_specs=pl.BlockSpec(memory_space=pltpu.HBM),
        scratch_shapes=[pltpu.VMEM((width // tile, rows, tile), jnp.bfloat16), pltpu.SemaphoreType.DMA((width // tile,))],
        compiler_params=pltpu.CompilerParams(vmem_limit_bytes=20 * 2**20),
        cost_estimate=pl.CostEstimate(
            flops=2 * parts * depth * rows * width,
            bytes_accessed=2 * parts * depth * (rows + width) + 8 * rows * width,
            transcendentals=0,
        ),
        name="finish",
    )(*tokens, *cotangents, total, shared)


def without(bit, size):
    return [k for k in range(size) if not k & bit]


def after(value, *others):
    return lax.optimization_barrier((value, *others))[0]


def gather(piece, axis, size, gates={}):
    pieces = {0: piece}
    bit = size // 2
    while bit:
        for k in sorted(pieces):
            pieces[k ^ bit] = swap(after(pieces[k], *gates.get(k ^ bit, ())), axis, bit)
        bit //= 2
    return [pieces[k] for k in range(size)]


def on_device(tokens, norm_gain, cotangent, layer_weight, shared_copy, master, momentum):
    tokens, cotangent, weight = tokens[0], cotangent[0], layer_weight[0]
    shards = lax.axis_size("fsdp")
    groups = lax.axis_size("replica")
    mine = lax.axis_index("fsdp")
    own = lax.axis_index("replica")
    rows, width = weight.shape
    inner_rate = inner_gain / math.sqrt(tokens.shape[0] * shards)

    rate = (1.0 - mix_weight) * inner_rate
    half, skip = shards // 2, shards // 4

    cotangents = gather(cotangent, "fsdp", shards)
    first = [cotangents[1 << bit] for bit in range(shards.bit_length() - 1)]
    group, others = prepare(mine, tokens, norm_gain, shards, skip)
    coded_shared, coded_weight, *_ = lax.optimization_barrier((shared_copy, weight, group))
    kept, sent = code_and_decode(own, coded_shared, coded_weight, groups)

    inside = without(skip, shards)
    group = after(group, *first, sent)
    members = [inside, [k + skip for k in inside]]
    columns = lax.all_to_all(group, "fsdp", split_axis=0, concat_axis=0, axis_index_groups=members, tiled=True)
    arrived = {}
    for k, block in zip(members[1], others):
        gate = [arrived[k - 1]] if k - 1 in arrived and k > half else [cotangents[half]]
        arrived[k] = swap(after(block, *gate), "fsdp", k)

    total = kept.astype(jnp.float32) + swap(sent, "replica", 1).astype(jnp.float32)
    bit = 2
    while bit < groups:
        sent = swap(total[1::2].astype(jnp.bfloat16), "replica", bit)
        bit *= 2
        total = total[0::2] + sent.astype(jnp.float32)
    average = total[0] / groups
    momentum_next = outer_beta * momentum + average
    master_next = master - outer_rate * (average + outer_beta * momentum_next)
    pieces = gather(master_next.astype(jnp.bfloat16), "replica", groups)

    near = [k for k in members[1] if k < half]
    far = [k for k in members[1] if k > half]
    place = mine // (2 * skip) * skip + mine % skip
    total = accumulate(
        place,
        inside,
        columns,
        [cotangents[k] for k in inside],
        [arrived[k] for k in near],
        [cotangents[k] for k in near],
        weight,
        rate,
    )
    shared = put_in_place(own, pieces)
    layer_next = finish([arrived[k] for k in far], [cotangents[k] for k in far], total, shared, rate)
    return (layer_next[None], master_next, momentum_next)


def solution(mesh):
    in_specs = (
        P("replica", "fsdp", None),
        P(),
        P("replica", "fsdp", None),
        P("replica", "fsdp", None),
        P("fsdp", None),
        P("fsdp", "replica"),
        P("fsdp", "replica"),
    )
    out_specs = (P("replica", "fsdp", None), P("fsdp", "replica"), P("fsdp", "replica"))
    return jax.shard_map(
        on_device, mesh=mesh, in_specs=in_specs, out_specs=out_specs, check_vma=False
    )
```

time: 91.5 us -> 106 us (1.16); the launches traced: 89.8 us -> 106 us
  starting transfers between devices: 21.2 us -> 29.9 us
  Pallas kernels: 11.6 us -> 15.2 us
  local copies, waits for them, and re-layouts: 11.8 us -> 14.5 us
  other arithmetic: 2.68 us -> 4.93 us
  waiting for transfers between devices: 41.8 us -> 40.3 us
    ppermute x12 -> x16, starting transfers between devices: 15.4 us -> 26.4 us  [swap(): return lax.ppermute(value, axis, [(i, i ^ mask) for i in range(size)])]
    pallas_call x2 -> x4, Pallas kernels: 7.94 us -> 11.6 us  [the longest x1 4.24 us: accumulate(): pl.pallas_call(functools.partial(accumulate_kernel, offsets, len(others),...]
    all_to_all x1, starting transfers between devices: 5.71 us -> 3.52 us  [on_device(): lax.all_to_all(group, 'fsdp', split_axis=0, concat_axis=0, axis_index_gro...]
    convert_element_type x1, other arithmetic: 1.66 us -> 3.84 us  [on_device(): pieces = gather(master_next.astype(jnp.bfloat16), 'replica', groups)]
    unnamed x36 -> x50, local copies, waits for them, and re-layouts: 11.7 us -> 13.5 us
    ppermute x12 -> x16, waiting for transfers between devices: 41.8 us -> 40.3 us  [swap(): return lax.ppermute(value, axis, [(i, i ^ mask) for i in range(size)])]
  transfers between devices with their start and end apart: 13 -> 17, of which waited for: 9 -> 8; matrix products, arithmetic and copies ran while one was open for 3% -> 5% of each run, Pallas kernels for 7% -> 6%
where the time goes in v11:
time: 106 us
  waiting for transfers between devices  40.3 us (38%)
  starting transfers between devices  29.9 us (28%)
  Pallas kernels  15.2 us (14%)
  local copies, waits for them, and re-layouts  14.5 us (14%)
  other arithmetic  4.93 us (5%)
    ppermute x16, waiting for transfers between devices, swap(): return lax.ppermute(value, axis, [(i, i ^ mask) for i in range(size)])  40.3 us
    ppermute x16, starting transfers between devices, swap(): return lax.ppermute(value, axis, [(i, i ^ mask) for i in range(size)])  26.4 us
    unnamed x50, local copies, waits for them, and re-layouts  13.5 us
    pallas_call x1, Pallas kernels, accumulate(): pl.pallas_call(functools.partial(accumulate_kernel, offsets, len(others),...  4.24 us
    convert_element_type x1, other arithmetic, on_device(): pieces = gather(master_next.astype(jnp.bfloat16), 'replica', groups)  3.84 us
    pallas_call x1, Pallas kernels, code_and_decode(): pl.pallas_call(code_kernel, out_shape=(half, half), in_specs=[pl.BlockSpe...  3.69 us
    all_to_all x1, starting transfers between devices, on_device(): lax.all_to_all(group, 'fsdp', split_axis=0, concat_axis=0, axis_index_gro...  3.52 us
    pallas_call x1, Pallas kernels, finish(): pl.pallas_call(functools.partial(finish_kernel, parts, rate), out_shape=j...  3.09 us
  transfers between devices with their start and end apart: 17, of which 8 were waited for; matrix products, arithmetic and copies ran while one was open for 5% of the time, Pallas kernels for 6%

profile of v11, /device:TPU:0, one launch (start us, length us, event | category | flops | bytes accessed | tf_op | source)
XLA Modules:
  0.0 105.7 jit_solution(2111988528772978727)
XLA Ops:
  1.5 1.6 %copy-done.1 = bf16[1,128,8192]{2,1,0:T(8,128)(2,1)S(1)} copy-done((bf16[1,128,8192]{2,1,0:T(8,128)(2,1)S(1)}, bf16[1,128,8192]{2,1,0:T(8,128)(2,1)}, u32[]{:S(2)}) %copy-start.1) | copy-done | bytes 2097176
  3.1 2.5 %prepare.1 = (bf16[4,1024,128]{2,1,0:T(8,128)(2,1)S(1)}, bf16[1024,128]{1,0:T(8,128)(2,1)S(1)}, bf16[1024,128]{1,0:T(8,128)(2,1)S(1)}, bf16[1024,128]{1,0:T(8,128)(2,1)S(1)}, bf16[1024,128]{1,0:T(8,128)(2,1)}) custom-call(s32[1]{0:T(128)} %bitcast.mine_ref, bf16[128,8192]{1,0:T(8,128)(2,1)S(1)} %bitcast.18, f32[1,8192]{1,0:T(1,128)S(1)} %bitcast.23), custom_call_target="tpu_custom_call" | custom-call | flops 5242880 | bytes 4194304 | tf_op jit(solution)/shard_map/prepare/pallas_call | solution.py:69
  5.7 1.0 copy-done.3
  6.7 1.9 %copy-done.2 = bf16[1024,1024]{1,0:T(8,128)(2,1)S(1)} copy-done((bf16[1024,1024]{1,0:T(8,128)(2,1)S(1)}, bf16[1024,1024]{1,0:T(8,128)(2,1)}, u32[]{:S(2)}) %copy-start.2) | copy-done | bytes 2097176
  8.5 3.7 %code_and_decode.1 = (bf16[2,1024,256]{2,1,0:T(8,128)(2,1)S(1)}, bf16[2,1024,256]{2,1,0:T(8,128)(2,1)S(1)}) custom-call(s32[1]{0:T(128)} %bitcast.5.own_ref, bf16[1024,1024]{1,0:T(8,128)(2,1)S(1)} %copy-done.2, bf16[1024,1024]{1,0:T(8,128)(2,1)S(1)} %bitcast.16), custom_call_target="tpu_custom_call" | custom-call | flops 20971520 | bytes 6291456 | tf_op jit(solution)/shard_map/code_and_decode/pallas_call | solution.py:144
  12.8 3.7 %collective-permute-start = (bf16[128,1024]{1,0:T(8,128)(2,1)S(1)}, bf16[128,1024]{1,0:T(8,128)(2,1)S(1)}, u32[]{:S(2)}, u32[]{:S(2)}) collective-permute-start(bf16[128,1024]{1,0:T(8,128)(2,1)S(1)} %bitcast.19), channel_id=1, source_target_pairs={{0,4},{1,5},{2,6},{3,7},{4,0},{5,1},{6,2},{7,3},{8,12},{9,13},{10,... | collective-permute-start | bytes 786440 | tf_op jit(solution)/shard_map/ppermute | solution.py:24
  16.5 1.5 %collective-permute-start.5 = (bf16[128,1024]{1,0:T(8,128)(2,1)S(1)}, bf16[128,1024]{1,0:T(8,128)(2,1)S(1)}, u32[]{:S(2)}, u32[]{:S(2)}) collective-permute-start(bf16[128,1024]{1,0:T(8,128)(2,1)S(1)} %bitcast.20), channel_id=1, source_target_pairs={{0,1},{1,0},{2,3},{3,2},{4,5},{5,4},{6,7},{7,6},{8,9},{9,8},{10,11... | collective-permute-start | bytes 786440 | tf_op jit(solution)/shard_map/ppermute | solution.py:24
  18.0 1.6 %collective-permute-start.6 = (bf16[128,1024]{1,0:T(8,128)(2,1)S(1)}, bf16[128,1024]{1,0:T(8,128)(2,1)}, u32[]{:S(2)}, u32[]{:S(2)}) collective-permute-start(bf16[128,1024]{1,0:T(8,128)(2,1)S(1)} %bitcast.21), channel_id=1, source_target_pairs={{0,2},{1,3},{2,0},{3,1},{4,6},{5,7},{6,4},{7,5},{8,10},{9,11},{10,... | collective-permute-start | bytes 786440 | tf_op jit(solution)/shard_map/ppermute | solution.py:24
  19.8 1.0 slice.23
  20.8 1.5 %collective-permute-start.12 = (bf16[1,1024,256]{2,1,0:T(8,128)(2,1)}, bf16[1,1024,256]{2,1,0:T(8,128)(2,1)}, u32[]{:S(2)}, u32[]{:S(2)}) collective-permute-start(bf16[1,1024,256]{2,1,0:T(8,128)(2,1)} %slice.23), channel_id=1, source_target_pairs={{0,16},{8,24},{16,0},{24,8},{1,17},{9,25},{17,1},{25,9},{2,18},{10... | collective-permute-start | bytes 1572872 | tf_op jit(solution)/shard_map/ppermute | solution.py:24
  22.3 6.8 %collective-permute-done.refs_2_ = bf16[128,1024]{1,0:T(8,128)(2,1)S(1)} collective-permute-done((bf16[128,1024]{1,0:T(8,128)(2,1)S(1)}, bf16[128,1024]{1,0:T(8,128)(2,1)S(1)}, u32[]{:S(2)}, u32[]{:S(2)}) %collective-permute-start) | collective-permute-done | bytes 262176 | tf_op jit(solution)/shard_map/ppermute | solution.py:24
  30.6 3.5 %all-to-all-start = ((bf16[4,1024,128]{2,1,0:T(8,128)(2,1)}), bf16[4,1024,128]{2,1,0:T(8,128)(2,1)S(1)}, u32[]{:S(2)}, u32[]{:S(2)}) async-start(bf16[4,1024,128]{2,1,0:T(8,128)(2,1)} %copy-done.3), calls=%async_computation | async-start | bytes 2097152 | tf_op jit(solution)/shard_map/all_to_all | solution.py:315
  34.5 3.8 %fusion.2 = (bf16[1024,256]{1,0:T(8,128)(2,1)}, f32[1024,256]{1,0:T(8,128)}, f32[1024,256]{1,0:T(8,128)}) fusion(f32[1024,256]{1,0:T(8,128)} %param.12, bf16[1,1024,256]{2,1,0:T(8,128)(2,1)} %collective-permute-done.12, f32[2,1024,256]{2,1,0:T(8,128)} %copy-done.24, f32[1024,256]{1,0:T(8,128)} %param.13), kind=kLoop, calls=%fused_computation.7 | loop fusion | flops 2621440 | bytes 6291456 | tf_op jit(solution)/shard_map/convert_element_type | solution.py:330
  38.4 1.5 %collective-permute-start.14 = (bf16[1024,256]{1,0:T(8,128)(2,1)}, bf16[1024,256]{1,0:T(8,128)(2,1)}, u32[]{:S(2)}, u32[]{:S(2)}) collective-permute-start(bf16[1024,256]{1,0:T(8,128)(2,1)} %get-tuple-element.31.refs_0_), channel_id=1, source_target_pairs={{0,16},{8,24},{16,0},{24,8},{1,17},{9,25},{17,1},{25,9},{2,18},{10... | collective-permute-start | bytes 1572872 | tf_op jit(solution)/shard_map/ppermute | solution.py:24
  39.9 4.7 %collective-permute-start.1 = (bf16[1024,128]{1,0:T(8,128)(2,1)S(1)}, bf16[1024,128]{1,0:T(8,128)(2,1)S(1)}, u32[]{:S(2)}, u32[]{:S(2)}) collective-permute-start(bf16[1024,128]{1,0:T(8,128)(2,1)S(1)} %copy-done.23), channel_id=1, source_target_pairs={{0,6},{1,7},{2,4},{3,5},{4,2},{5,3},{6,0},{7,1},{8,14},{9,15},{10,... | collective-permute-start | bytes 786440 | tf_op jit(solution)/shard_map/ppermute | solution.py:24
  44.5 1.5 %collective-permute-start.7 = (bf16[128,1024]{1,0:T(8,128)(2,1)S(1)}, bf16[128,1024]{1,0:T(8,128)(2,1)S(1)}, u32[]{:S(2)}, u32[]{:S(2)}) collective-permute-start(bf16[128,1024]{1,0:T(8,128)(2,1)S(1)} %copy-done.6), channel_id=1, source_target_pairs={{0,1},{1,0},{2,3},{3,2},{4,5},{5,4},{6,7},{7,6},{8,9},{9,8},{10,11... | collective-permute-start | bytes 786440 | tf_op jit(solution)/shard_map/ppermute | solution.py:24
  46.0 2.0 %collective-permute-start.8 = (bf16[1024,128]{1,0:T(8,128)(2,1)S(1)}, bf16[1024,128]{1,0:T(8,128)(2,1)S(1)}, u32[]{:S(2)}, u32[]{:S(2)}) collective-permute-start(bf16[1024,128]{1,0:T(8,128)(2,1)S(1)} %copy-done.21), channel_id=1, source_target_pairs={{0,2},{1,3},{2,0},{3,1},{4,6},{5,7},{6,4},{7,5},{8,10},{9,11},{10,... | collective-permute-start | bytes 786440 | tf_op jit(solution)/shard_map/ppermute | solution.py:24
  48.0 3.9 %collective-permute-done.14.refs_2_ = bf16[1024,256]{1,0:T(8,128)(2,1)} collective-permute-done((bf16[1024,256]{1,0:T(8,128)(2,1)}, bf16[1024,256]{1,0:T(8,128)(2,1)}, u32[]{:S(2)}, u32[]{:S(2)}) %collective-permute-start.14) | collective-permute-done | bytes 524320 | tf_op jit(solution)/shard_map/ppermute | solution.py:24
  51.9 5.9 %collective-permute-done.1.refs_0_ = bf16[1024,128]{1,0:T(8,128)(2,1)S(1)} collective-permute-done((bf16[1024,128]{1,0:T(8,128)(2,1)S(1)}, bf16[1024,128]{1,0:T(8,128)(2,1)S(1)}, u32[]{:S(2)}, u32[]{:S(2)}) %collective-permute-start.1) | collective-permute-done | bytes 262176 | tf_op jit(solution)/shard_map/ppermute | solution.py:24
  58.5 9.9 %collective-permute-done.3.refs_2_ = bf16[128,1024]{1,0:T(8,128)(2,1)} collective-permute-done((bf16[128,1024]{1,0:T(8,128)(2,1)S(1)}, bf16[128,1024]{1,0:T(8,128)(2,1)}, u32[]{:S(2)}, u32[]{:S(2)}) %collective-permute-start.3) | collective-permute-done | bytes 262176 | tf_op jit(solution)/shard_map/ppermute | solution.py:24
  68.5 5.0 %collective-permute-start.9 = (bf16[1024,128]{1,0:T(8,128)(2,1)S(1)}, bf16[1024,128]{1,0:T(8,128)(2,1)S(1)}, u32[]{:S(2)}, u32[]{:S(2)}) collective-permute-start(bf16[1024,128]{1,0:T(8,128)(2,1)S(1)} %copy-done.19), channel_id=1, source_target_pairs={{0,3},{1,2},{2,1},{3,0},{4,7},{5,6},{6,5},{7,4},{8,11},{9,10},{10,... | collective-permute-start | bytes 786440 | tf_op jit(solution)/shard_map/ppermute | solution.py:24
  75.5 2.4 %collective-permute-start.2 = (bf16[1024,128]{1,0:T(8,128)(2,1)}, bf16[1024,128]{1,0:T(8,128)(2,1)}, u32[]{:S(2)}, u32[]{:S(2)}) collective-permute-start(bf16[1024,128]{1,0:T(8,128)(2,1)} %get-tuple-element.20), channel_id=1, source_target_pairs={{0,7},{1,6},{2,5},{3,4},{4,3},{5,2},{6,1},{7,0},{8,15},{9,14},{10,... | collective-permute-start | bytes 786440 | tf_op jit(solution)/shard_map/ppermute | solution.py:24
  77.8 4.6 %collective-permute-done.9.refs_5_ = bf16[1024,128]{1,0:T(8,128)(2,1)S(1)} collective-permute-done((bf16[1024,128]{1,0:T(8,128)(2,1)S(1)}, bf16[1024,128]{1,0:T(8,128)(2,1)S(1)}, u32[]{:S(2)}, u32[]{:S(2)}) %collective-permute-start.9) | collective-permute-done | bytes 262176 | tf_op jit(solution)/shard_map/ppermute | solution.py:24
  83.2 8.6 %collective-permute-done.10.refs_7_ = bf16[128,1024]{1,0:T(8,128)(2,1)} collective-permute-done((bf16[128,1024]{1,0:T(8,128)(2,1)}, bf16[128,1024]{1,0:T(8,128)(2,1)}, u32[]{:S(2)}, u32[]{:S(2)}) %collective-permute-start.10) | collective-permute-done | bytes 262176 | tf_op jit(solution)/shard_map/ppermute | solution.py:24
  91.8 0.9 copy-done.7
  92.8 0.9 copy-done.9
  93.7 0.9 copy-done.13
  94.7 0.9 copy-done.15
  95.6 0.9 copy-done.17
  96.6 4.2 %accumulate.1.refs_4_ = f32[1024,1024]{1,0:T(8,128)S(1)} custom-call(s32[1]{0:T(128)} %bitcast.4.place_ref, bf16[4,1024,128]{2,1,0:T(8,128)(2,1)S(1)} %all-to-all-done.tokens_ref, bf16[1024,1024]{1,0:T(8,128)(2,1)S(1)} %bitcast.17, bf16[128,1024]{1,0:T(8,128)(2,1)S(1)} %bitcast.22, bf16[128,1024]{1,0:T(8,128)(2,1)S(1)} %copy-done.9, ...), custom_call_target="tpu_custom_call" | custom-call | flops 1610612736 | bytes 9437184 | tf_op jit(solution)/shard_map/accumulate/pallas_call | solution.py:193
  100.8 1.7 %put_in_place.1.refs_5_ = bf16[4,1024,256]{2,1,0:T(8,128)(2,1)S(1)} custom-call(s32[1]{0:T(128)} %bitcast.5.own_ref, bf16[1024,256]{1,0:T(8,128)(2,1)} %get-tuple-element.31.refs_0_, bf16[1024,256]{1,0:T(8,128)(2,1)} %collective-permute-done.13.refs_1_, bf16[1024,256]{1,0:T(8,128)(2,1)} %collective-permute-done.14.refs_2_, ...), custom_call_target="tpu_custom_call" | custom-call | bytes 4194304 | tf_op jit(solution)/shard_map/put_in_place/pallas_call | solution.py:222
  102.6 3.1 %finish.1 = bf16[1024,1024]{1,0:T(8,128)(2,1)} custom-call(bf16[1024,128]{1,0:T(8,128)(2,1)S(1)} %copy-done.11, bf16[1024,128]{1,0:T(8,128)(2,1)} %collective-permute-done.2.refs_1_, bf16[128,1024]{1,0:T(8,128)(2,1)} %collective-permute-done.3.refs_2_, bf16[128,1024]{1,0:T(8,128)(2,1)} %collective-permute-done.4.refs_3_, ...), custom_call_target="tpu_custom_call" | custom-call | flops 536870912 | bytes 9437184 | tf_op jit(solution)/shard_map/finish/pallas_call | solution.py:260
  (61 shorter events, 7.0 us)
Async XLA Ops:
  0.6 6.0 %copy-start = (bf16[1,1024,1024]{2,1,0:T(8,128)(2,1)S(1)}, bf16[1,1024,1024]{2,1,0:T(8,128)(2,1)}, u32[]{:S(2)}) copy-start(bf16[1,1024,1024]{2,1,0:T(8,128)(2,1)} %param.10) | copy-start | bytes 6291460
  1.5 1.6 %copy-start.1 = (bf16[1,128,8192]{2,1,0:T(8,128)(2,1)S(1)}, bf16[1,128,8192]{2,1,0:T(8,128)(2,1)}, u32[]{:S(2)}) copy-start(bf16[1,128,8192]{2,1,0:T(8,128)(2,1)} %param.7) | copy-start | bytes 6291460
  5.7 1.0 copy-start.3
  6.7 5.6 %copy-start.18 = (bf16[1024,128]{1,0:T(8,128)(2,1)}, bf16[1024,128]{1,0:T(8,128)(2,1)S(1)}, u32[]{:S(2)}) copy-start(bf16[1024,128]{1,0:T(8,128)(2,1)S(1)} %get-tuple-element.29) | copy-start | bytes 786436
  6.7 5.6 %copy-start.20 = (bf16[1024,128]{1,0:T(8,128)(2,1)}, bf16[1024,128]{1,0:T(8,128)(2,1)S(1)}, u32[]{:S(2)}) copy-start(bf16[1024,128]{1,0:T(8,128)(2,1)S(1)} %get-tuple-element.27) | copy-start | bytes 786436
  6.7 5.6 %copy-start.22 = (bf16[1024,128]{1,0:T(8,128)(2,1)}, bf16[1024,128]{1,0:T(8,128)(2,1)S(1)}, u32[]{:S(2)}) copy-start(bf16[1024,128]{1,0:T(8,128)(2,1)S(1)} %get-tuple-element.18) | copy-start | bytes 786436
  6.7 1.9 %copy-start.2 = (bf16[1024,1024]{1,0:T(8,128)(2,1)S(1)}, bf16[1024,1024]{1,0:T(8,128)(2,1)}, u32[]{:S(2)}) copy-start(bf16[1024,1024]{1,0:T(8,128)(2,1)} %shared_ref) | copy-start | bytes 6291460
  8.5 4.2 %copy-start.4 = (bf16[1,128,1024]{2,1,0:T(8,128)(2,1)S(1)}, bf16[1,128,1024]{2,1,0:T(8,128)(2,1)}, u32[]{:S(2)}) copy-start(bf16[1,128,1024]{2,1,0:T(8,128)(2,1)} %param.9) | copy-start | bytes 786436
  12.3 7.3 %collective-permute-start.11 = (bf16[2,1024,256]{2,1,0:T(8,128)(2,1)S(1)}, bf16[2,1024,256]{2,1,0:T(8,128)(2,1)S(1)}, u32[]{:S(2)}, u32[]{:S(2)}) collective-permute-start(bf16[2,1024,256]{2,1,0:T(8,128)(2,1)S(1)} %get-tuple-element.24), channel_id=1, source_target_pairs={{0,8},{8,0},{16,24},{24,16},{1,9},{9,1},{17,25},{25,17},{2,10},{10... | collective-permute-start | bytes 3145736 | tf_op jit(solution)/shard_map/ppermute | solution.py:24
  12.8 16.3 %collective-permute-start = (bf16[128,1024]{1,0:T(8,128)(2,1)S(1)}, bf16[128,1024]{1,0:T(8,128)(2,1)S(1)}, u32[]{:S(2)}, u32[]{:S(2)}) collective-permute-start(bf16[128,1024]{1,0:T(8,128)(2,1)S(1)} %bitcast.19), channel_id=1, source_target_pairs={{0,4},{1,5},{2,6},{3,7},{4,0},{5,1},{6,2},{7,3},{8,12},{9,13},{10,... | collective-permute-start | bytes 786440 | tf_op jit(solution)/shard_map/ppermute | solution.py:24
  16.5 12.6 %collective-permute-start.5 = (bf16[128,1024]{1,0:T(8,128)(2,1)S(1)}, bf16[128,1024]{1,0:T(8,128)(2,1)S(1)}, u32[]{:S(2)}, u32[]{:S(2)}) collective-permute-start(bf16[128,1024]{1,0:T(8,128)(2,1)S(1)} %bitcast.20), channel_id=1, source_target_pairs={{0,1},{1,0},{2,3},{3,2},{4,5},{5,4},{6,7},{7,6},{8,9},{9,8},{10,11... | collective-permute-start | bytes 786440 | tf_op jit(solution)/shard_map/ppermute | solution.py:24
  18.0 12.6 %collective-permute-start.6 = (bf16[128,1024]{1,0:T(8,128)(2,1)S(1)}, bf16[128,1024]{1,0:T(8,128)(2,1)}, u32[]{:S(2)}, u32[]{:S(2)}) collective-permute-start(bf16[128,1024]{1,0:T(8,128)(2,1)S(1)} %bitcast.21), channel_id=1, source_target_pairs={{0,2},{1,3},{2,0},{3,1},{4,6},{5,7},{6,4},{7,5},{8,10},{9,11},{10,... | collective-permute-start | bytes 786440 | tf_op jit(solution)/shard_map/ppermute | solution.py:24
  19.8 9.3 %copy-start.24 = (f32[2,1024,256]{2,1,0:T(8,128)}, f32[2,1024,256]{2,1,0:T(8,128)S(1)}, u32[]{:S(2)}) copy-start(f32[2,1024,256]{2,1,0:T(8,128)S(1)} %convert_add_fusion) | copy-start | bytes 6291460
  20.8 13.7 %collective-permute-start.12 = (bf16[1,1024,256]{2,1,0:T(8,128)(2,1)}, bf16[1,1024,256]{2,1,0:T(8,128)(2,1)}, u32[]{:S(2)}, u32[]{:S(2)}) collective-permute-start(bf16[1,1024,256]{2,1,0:T(8,128)(2,1)} %slice.23), channel_id=1, source_target_pairs={{0,16},{8,24},{16,0},{24,8},{1,17},{9,25},{17,1},{25,9},{2,18},{10... | collective-permute-start | bytes 1572872 | tf_op jit(solution)/shard_map/ppermute | solution.py:24
  30.6 61.2 %all-to-all-start = ((bf16[4,1024,128]{2,1,0:T(8,128)(2,1)}), bf16[4,1024,128]{2,1,0:T(8,128)(2,1)S(1)}, u32[]{:S(2)}, u32[]{:S(2)}) async-start(bf16[4,1024,128]{2,1,0:T(8,128)(2,1)} %copy-done.3), calls=%async_computation | async-start | bytes 2097152 | tf_op jit(solution)/shard_map/all_to_all | solution.py:315
  34.1 5.7 %copy-start.23 = (bf16[1024,128]{1,0:T(8,128)(2,1)S(1)}, bf16[1024,128]{1,0:T(8,128)(2,1)}, u32[]{:S(2)}) copy-start(bf16[1024,128]{1,0:T(8,128)(2,1)} %copy-done.22) | copy-start | bytes 786436
  34.1 10.4 %copy-start.6 = (bf16[128,1024]{1,0:T(8,128)(2,1)S(1)}, bf16[128,1024]{1,0:T(8,128)(2,1)}, u32[]{:S(2)}) copy-start(bf16[128,1024]{1,0:T(8,128)(2,1)} %copy-done.5) | copy-start | bytes 786436
  34.2 11.9 %copy-start.21 = (bf16[1024,128]{1,0:T(8,128)(2,1)S(1)}, bf16[1024,128]{1,0:T(8,128)(2,1)}, u32[]{:S(2)}) copy-start(bf16[1024,128]{1,0:T(8,128)(2,1)} %copy-done.20) | copy-start | bytes 786436
  34.2 34.3 %copy-start.19 = (bf16[1024,128]{1,0:T(8,128)(2,1)S(1)}, bf16[1024,128]{1,0:T(8,128)(2,1)}, u32[]{:S(2)}) copy-start(bf16[1024,128]{1,0:T(8,128)(2,1)} %copy-done.18) | copy-start | bytes 786436
  38.4 13.6 %collective-permute-start.14 = (bf16[1024,256]{1,0:T(8,128)(2,1)}, bf16[1024,256]{1,0:T(8,128)(2,1)}, u32[]{:S(2)}, u32[]{:S(2)}) collective-permute-start(bf16[1024,256]{1,0:T(8,128)(2,1)} %get-tuple-element.31.refs_0_), channel_id=1, source_target_pairs={{0,16},{8,24},{16,0},{24,8},{1,17},{9,25},{17,1},{25,9},{2,18},{10... | collective-permute-start | bytes 1572872 | tf_op jit(solution)/shard_map/ppermute | solution.py:24
  39.9 18.0 %collective-permute-start.1 = (bf16[1024,128]{1,0:T(8,128)(2,1)S(1)}, bf16[1024,128]{1,0:T(8,128)(2,1)S(1)}, u32[]{:S(2)}, u32[]{:S(2)}) collective-permute-start(bf16[1024,128]{1,0:T(8,128)(2,1)S(1)} %copy-done.23), channel_id=1, source_target_pairs={{0,6},{1,7},{2,4},{3,5},{4,2},{5,3},{6,0},{7,1},{8,14},{9,15},{10,... | collective-permute-start | bytes 786440 | tf_op jit(solution)/shard_map/ppermute | solution.py:24
  44.5 23.9 %collective-permute-start.3 = (bf16[128,1024]{1,0:T(8,128)(2,1)S(1)}, bf16[128,1024]{1,0:T(8,128)(2,1)}, u32[]{:S(2)}, u32[]{:S(2)}) collective-permute-start(bf16[128,1024]{1,0:T(8,128)(2,1)S(1)} %copy-done.6), channel_id=1, source_target_pairs={{0,2},{1,3},{2,0},{3,1},{4,6},{5,7},{6,4},{7,5},{8,10},{9,11},{10,... | collective-permute-start | bytes 786440 | tf_op jit(solution)/shard_map/ppermute | solution.py:24
  44.5 28.9 %collective-permute-start.7 = (bf16[128,1024]{1,0:T(8,128)(2,1)S(1)}, bf16[128,1024]{1,0:T(8,128)(2,1)S(1)}, u32[]{:S(2)}, u32[]{:S(2)}) collective-permute-start(bf16[128,1024]{1,0:T(8,128)(2,1)S(1)} %copy-done.6), channel_id=1, source_target_pairs={{0,1},{1,0},{2,3},{3,2},{4,5},{5,4},{6,7},{7,6},{8,9},{9,8},{10,11... | collective-permute-start | bytes 786440 | tf_op jit(solution)/shard_map/ppermute | solution.py:24
  46.0 28.7 %collective-permute-start.8 = (bf16[1024,128]{1,0:T(8,128)(2,1)S(1)}, bf16[1024,128]{1,0:T(8,128)(2,1)S(1)}, u32[]{:S(2)}, u32[]{:S(2)}) collective-permute-start(bf16[1024,128]{1,0:T(8,128)(2,1)S(1)} %copy-done.21), channel_id=1, source_target_pairs={{0,2},{1,3},{2,0},{3,1},{4,6},{5,7},{6,4},{7,5},{8,10},{9,11},{10,... | collective-permute-start | bytes 786440 | tf_op jit(solution)/shard_map/ppermute | solution.py:24
  51.9 48.9 %collective-permute-start.13 = (bf16[1024,256]{1,0:T(8,128)(2,1)}, bf16[1024,256]{1,0:T(8,128)(2,1)}, u32[]{:S(2)}, u32[]{:S(2)}) collective-permute-start(bf16[1024,256]{1,0:T(8,128)(2,1)} %get-tuple-element.31.refs_0_), channel_id=1, source_target_pairs={{0,8},{8,0},{16,24},{24,16},{1,9},{9,1},{17,25},{25,17},{2,10},{10... | collective-permute-start | bytes 1572872 | tf_op jit(solution)/shard_map/ppermute | solution.py:24
  58.5 42.3 %collective-permute-start.15 = (bf16[1024,256]{1,0:T(8,128)(2,1)}, bf16[1024,256]{1,0:T(8,128)(2,1)}, u32[]{:S(2)}, u32[]{:S(2)}) collective-permute-start(bf16[1024,256]{1,0:T(8,128)(2,1)} %collective-permute-done.14.refs_2_), channel_id=1, source_target_pairs={{0,8},{8,0},{16,24},{24,16},{1,9},{9,1},{17,25},{25,17},{2,10},{10... | collective-permute-start | bytes 1572872 | tf_op jit(solution)/shard_map/ppermute | solution.py:24
  68.5 14.0 %collective-permute-start.9 = (bf16[1024,128]{1,0:T(8,128)(2,1)S(1)}, bf16[1024,128]{1,0:T(8,128)(2,1)S(1)}, u32[]{:S(2)}, u32[]{:S(2)}) collective-permute-start(bf16[1024,128]{1,0:T(8,128)(2,1)S(1)} %copy-done.19), channel_id=1, source_target_pairs={{0,3},{1,2},{2,1},{3,0},{4,7},{5,6},{6,5},{7,4},{8,11},{9,10},{10,... | collective-permute-start | bytes 786440 | tf_op jit(solution)/shard_map/ppermute | solution.py:24
  74.2 17.6 %collective-permute-start.10 = (bf16[128,1024]{1,0:T(8,128)(2,1)}, bf16[128,1024]{1,0:T(8,128)(2,1)}, u32[]{:S(2)}, u32[]{:S(2)}) collective-permute-start(bf16[128,1024]{1,0:T(8,128)(2,1)} %collective-permute-done.6.refs_6_), channel_id=1, source_target_pairs={{0,1},{1,0},{2,3},{3,2},{4,5},{5,4},{6,7},{7,6},{8,9},{9,8},{10,11... | collective-permute-start | bytes 786440 | tf_op jit(solution)/shard_map/ppermute | solution.py:24
  75.5 27.1 %collective-permute-start.2 = (bf16[1024,128]{1,0:T(8,128)(2,1)}, bf16[1024,128]{1,0:T(8,128)(2,1)}, u32[]{:S(2)}, u32[]{:S(2)}) collective-permute-start(bf16[1024,128]{1,0:T(8,128)(2,1)} %get-tuple-element.20), channel_id=1, source_target_pairs={{0,7},{1,6},{2,5},{3,4},{4,3},{5,2},{6,1},{7,0},{8,15},{9,14},{10,... | collective-permute-start | bytes 786440 | tf_op jit(solution)/shard_map/ppermute | solution.py:24
  83.2 19.4 %collective-permute-start.4 = (bf16[128,1024]{1,0:T(8,128)(2,1)}, bf16[128,1024]{1,0:T(8,128)(2,1)}, u32[]{:S(2)}, u32[]{:S(2)}) collective-permute-start(bf16[128,1024]{1,0:T(8,128)(2,1)} %collective-permute-done.3.refs_2_), channel_id=1, source_target_pairs={{0,1},{1,0},{2,3},{3,2},{4,5},{5,4},{6,7},{7,6},{8,9},{9,8},{10,11... | collective-permute-start | bytes 786440 | tf_op jit(solution)/shard_map/ppermute | solution.py:24
  91.8 1.0 copy-start.7
  100.8 1.8 %copy-start.11 = (bf16[1024,128]{1,0:T(8,128)(2,1)S(1)}, bf16[1024,128]{1,0:T(8,128)(2,1)}, u32[]{:S(2)}) copy-start(bf16[1024,128]{1,0:T(8,128)(2,1)} %copy-done.10) | copy-start | bytes 786436
  (10 other events, 8.0 us)

commit v12 on v8

--- a/solution.py
+++ b/solution.py
@@ -146,25 +146,38 @@
     tokens_ref, refs = refs[0], refs[1:]
     cotangent_refs, refs = refs[:shards], refs[shards:]
     piece_refs, refs = refs[:groups], refs[groups:]
-    weight_ref, out_ref, cotangents, pieces, outs, out_sems = refs
+    weight_ref, out_ref, refs = refs[0], refs[1], refs[2:]
+    tokens, cotangents, pieces, weights, outs, token_sem, cotangent_sems, piece_sems, weight_sem, out_sems = refs
     mine, own = place_ref[0], place_ref[1]
     depth, width = cotangent_refs[0].shape
     share = pieces.shape[2]
     tile = outs.shape[2]
+
+    def own_row(k):
+        return pl.ds(pl.multiple_of((mine ^ k) * depth, depth), depth)
+
+    loads = [pltpu.make_async_copy(tokens_ref, tokens, token_sem)]
     for k, ref in enumerate(cotangent_refs):
-        cotangents[mine ^ k] = ref[...]
+        loads.append(pltpu.make_async_copy(ref, cotangents.at[own_row(k)], cotangent_sems.at[k]))
+    loads.append(pltpu.make_async_copy(weight_ref, weights, weight_sem))
     for k, ref in enumerate(piece_refs):
-        pieces[own ^ k] = ref[...]
-    left = jnp.concatenate([tokens_ref[k] for k in range(shards)], axis=1)
+        loads.append(pltpu.make_async_copy(ref, pieces.at[own ^ k], piece_sems.at[k]))
+    for load in loads:
+        load.start()
+    for load in loads[: 1 + shards]:
+        load.wait()
+    left = jnp.concatenate([tokens[k] for k in range(shards)], axis=1)
     stores = []
     for step in range(width // tile):
         columns = slice(step * tile, (step + 1) * tile)
-        right = jnp.concatenate([cotangents[k, :, columns] for k in range(shards)], axis=0)
-        total = jnp.dot(left, right, preferred_element_type=jnp.float32)
+        total = jnp.dot(left, cotangents[:, columns], preferred_element_type=jnp.float32)
+        if step == 0:
+            for load in loads[1 + shards :]:
+                load.wait()
         for group in range(step * tile // share, (step + 1) * tile // share):
             place = slice(group * share, (group + 1) * share)
             part = slice(group * share - step * tile, (group + 1) * share - step * tile)
-            mixed = weight_ref[:, place].astype(jnp.float32) + pieces[group].astype(jnp.float32)
+            mixed = weights[:, place].astype(jnp.float32) + pieces[group].astype(jnp.float32)
             outs[step, :, part] = (mix_weight * mixed - rate * total[:, part]).astype(jnp.bfloat16)
         stores.append(pltpu.make_async_copy(outs.at[step], out_ref.at[:, pl.ds(step * tile, tile)], out_sems.at[step]))
         stores[-1].start()
@@ -182,15 +195,21 @@
         functools.partial(mix_kernel, shards, groups, rate),
         out_shape=jax.ShapeDtypeStruct((rows, width), jnp.bfloat16),
         in_specs=[pl.BlockSpec(memory_space=pltpu.SMEM)]
-        + [pl.BlockSpec(memory_space=pltpu.VMEM)] * (2 + shards + groups),
+        + [pl.BlockSpec(memory_space=pltpu.HBM)] * (2 + shards + groups),
         out_specs=pl.BlockSpec(memory_space=pltpu.HBM),
         scratch_shapes=[
-            pltpu.VMEM((shards, depth, width), jnp.bfloat16),
+            pltpu.VMEM((shards, rows, depth), jnp.bfloat16),
+            pltpu.VMEM((shards * depth, width), jnp.bfloat16),
             pltpu.VMEM((groups, rows, share), jnp.bfloat16),
+            pltpu.VMEM((rows, width), jnp.bfloat16),
             pltpu.VMEM((width // tile, rows, tile), jnp.bfloat16),
+            pltpu.SemaphoreType.DMA,
+            pltpu.SemaphoreType.DMA((shards,)),
+            pltpu.SemaphoreType.DMA((groups,)),
+            pltpu.SemaphoreType.DMA,
             pltpu.SemaphoreType.DMA((width // tile,)),
         ],
-        compiler_params=pltpu.CompilerParams(vmem_limit_bytes=24 * 2**20),
+        compiler_params=pltpu.CompilerParams(vmem_limit_bytes=50 * 2**20),
         cost_estimate=pl.CostEstimate(
             flops=2 * depth * shards * rows * width,
             bytes_accessed=2 * depth * shards * (rows + width) + 6 * rows * width,
@@ -237,12 +256,12 @@
         sent = swap(total[1::2].astype(jnp.bfloat16), "replica", bit)
         bit *= 2
         if bit >= groups:
-            *_, sent = lax.optimization_barrier((*cotangents[: shards // 2 + 2], sent))
+            *_, sent = lax.optimization_barrier((cotangents[shards // 2 + 1], sent))
         total = total[0::2] + sent.astype(jnp.float32)
     average = total[0] / groups
     momentum_next = outer_beta * momentum + average
     master_next = master - outer_rate * (average + outer_beta * momentum_next)
-    pieces = gather(master_next.astype(jnp.bfloat16), "replica", groups, after=cotangents)
+    pieces = gather(master_next.astype(jnp.bfloat16), "replica", groups, after=cotangents[-2:-1])
 
     layer_next = mix(mine, own, columns, cotangents, pieces, weight, (1.0 - mix_weight) * inner_rate)
     return (layer_next[None], master_next, momentum_next)

time: 91.5 us -> 95.9 us (1.048)
  the two profiles are of different devices: /device:TPU:0 before, /device:TPU:26 now
where the time goes in v12:
time: 95.9 us; the launch traced here: 95.6 us
  waiting for transfers between devices  61.8 us (64%)
  starting transfers between devices  14.2 us (15%)
  Pallas kernels  12.9 us (13%)
  local copies, waits for them, and re-layouts  3.25 us (3%)
  other arithmetic  2.74 us (3%)
    ppermute x12, waiting for transfers between devices, swap(): return lax.ppermute(value, axis, [(i, i ^ mask) for i in range(size)])  61.8 us
    ppermute x12, starting transfers between devices, swap(): return lax.ppermute(value, axis, [(i, i ^ mask) for i in range(size)])  7.97 us
    pallas_call x1, Pallas kernels, mix(): pl.pallas_call(functools.partial(mix_kernel, shards, groups, rate), out_s...  7.04 us
    all_to_all x1, starting transfers between devices, on_device(): lax.all_to_all(blocks, 'fsdp', split_axis=0, concat_axis=0, tiled=True)  6.2 us
    pallas_call x1, Pallas kernels, code_and_decode(): pl.pallas_call(code_kernel, out_shape=(half, half), in_specs=[pl.BlockSpe...  3.69 us
    unnamed x12, local copies, waits for them, and re-layouts  3.2 us
    pallas_call x1, Pallas kernels, prepare(): pl.pallas_call(prepare_kernel, out_shape=jax.ShapeDtypeStruct((shards, ro...  2.21 us
  transfers between devices with their start and end apart: 13, of which 6 were waited for; matrix products, arithmetic and copies ran while one was open for 3% of the time, Pallas kernels for 6%

profile of v12, /device:TPU:26, one launch (start us, length us, event | category | flops | bytes accessed | tf_op | source)
XLA Modules:
  0.0 95.6 jit_solution(10176031248510270278)
XLA Ops:
  0.6 0.4 collective-permute-start.2
  1.0 0.4 collective-permute-start.1
  1.5 1.5 %collective-permute-start = (bf16[128,1024]{1,0:T(8,128)(2,1)}, bf16[128,1024]{1,0:T(8,128)(2,1)S(1)}, u32[]{:S(2)}, u32[]{:S(2)}) collective-permute-start(bf16[128,1024]{1,0:T(8,128)(2,1)} %bitcast.20), channel_id=1, source_target_pairs={{0,1},{1,0},{2,3},{3,2},{4,5},{5,4},{6,7},{7,6},{8,9},{9,8},{10,11... | collective-permute-start | bytes 786440 | tf_op jit(solution)/shard_map/ppermute | solution.py:24
  3.0 0.7 reshape.16
  3.7 1.6 %copy-done.1 = bf16[1,128,8192]{2,1,0:T(8,128)(2,1)S(1)} copy-done((bf16[1,128,8192]{2,1,0:T(8,128)(2,1)S(1)}, bf16[1,128,8192]{2,1,0:T(8,128)(2,1)}, u32[]{:S(2)}) %copy-start.1) | copy-done | bytes 2097176
  5.3 2.2 %prepare.1 = bf16[8,1024,128]{2,1,0:T(8,128)(2,1)} custom-call(bf16[128,8192]{1,0:T(8,128)(2,1)S(1)} %bitcast.17, f32[1,8192]{1,0:T(1,128)S(1)} %bitcast.22), custom_call_target="tpu_custom_call" | custom-call | flops 5242880 | bytes 4194304 | tf_op jit(solution)/shard_map/prepare/pallas_call | solution.py:58
  7.5 7.8 %collective-permute-done.2.refs_5_ = bf16[128,1024]{1,0:T(8,128)(2,1)S(1)} collective-permute-done((bf16[128,1024]{1,0:T(8,128)(2,1)}, bf16[128,1024]{1,0:T(8,128)(2,1)S(1)}, u32[]{:S(2)}, u32[]{:S(2)}) %collective-permute-start.2) | collective-permute-done | bytes 262176 | tf_op jit(solution)/shard_map/ppermute | solution.py:24
  15.4 0.0 collective-permute-done.refs_2_
  15.4 6.2 %all-to-all-start = ((bf16[8,1024,128]{2,1,0:T(8,128)(2,1)}), bf16[8,1024,128]{2,1,0:T(8,128)(2,1)}, u32[]{:S(2)}, u32[]{:S(2)}) async-start(bf16[8,1024,128]{2,1,0:T(8,128)(2,1)} %prepare.1), calls=%async_computation | async-start | bytes 4194304 | tf_op jit(solution)/shard_map/all_to_all | solution.py:250
  21.6 1.6 %copy-done.2 = bf16[1024,1024]{1,0:T(8,128)(2,1)S(1)} copy-done((bf16[1024,1024]{1,0:T(8,128)(2,1)S(1)}, bf16[1024,1024]{1,0:T(8,128)(2,1)}, u32[]{:S(2)}) %copy-start.2) | copy-done | bytes 2097176
  23.2 3.7 %code_and_decode.1 = (bf16[2,1024,256]{2,1,0:T(8,128)(2,1)S(1)}, bf16[2,1024,256]{2,1,0:T(8,128)(2,1)S(1)}) custom-call(s32[1]{0:T(128)} %bitcast.1.own_ref, bf16[1024,1024]{1,0:T(8,128)(2,1)S(1)} %copy-done.2, bf16[1024,1024]{1,0:T(8,128)(2,1)S(1)} %bitcast.16), custom_call_target="tpu_custom_call" | custom-call | flops 20971520 | bytes 6291456 | tf_op jit(solution)/shard_map/code_and_decode/pallas_call | solution.py:128
  26.9 0.1 collective-permute-start.7
  26.9 2.6 %collective-permute-done.7 = bf16[2,1024,256]{2,1,0:T(8,128)(2,1)S(1)} collective-permute-done((bf16[2,1024,256]{2,1,0:T(8,128)(2,1)S(1)}, bf16[2,1024,256]{2,1,0:T(8,128)(2,1)S(1)}, u32[]{:S(2)}, u32[]{:S(2)}) %collective-permute-start.7) | collective-permute-done | bytes 1048608 | tf_op jit(solution)/shard_map/ppermute | solution.py:24
  29.6 0.2 convert_add_fusion
  29.8 0.1 slice.23
  29.9 0.0 copy-start.3
  29.9 0.6 collective-permute-start.8
  30.5 1.5 %collective-permute-start.4 = (bf16[128,1024]{1,0:T(8,128)(2,1)S(1)}, bf16[128,1024]{1,0:T(8,128)(2,1)S(1)}, u32[]{:S(2)}, u32[]{:S(2)}) collective-permute-start(bf16[128,1024]{1,0:T(8,128)(2,1)S(1)} %collective-permute-done.2.refs_5_), channel_id=1, source_target_pairs={{0,1},{1,0},{2,3},{3,2},{4,5},{5,4},{6,7},{7,6},{8,9},{9,8},{10,11... | collective-permute-start | bytes 786440 | tf_op jit(solution)/shard_map/ppermute | solution.py:24
  32.0 22.7 %collective-permute-done.4.refs_6_ = bf16[128,1024]{1,0:T(8,128)(2,1)S(1)} collective-permute-done((bf16[128,1024]{1,0:T(8,128)(2,1)S(1)}, bf16[128,1024]{1,0:T(8,128)(2,1)S(1)}, u32[]{:S(2)}, u32[]{:S(2)}) %collective-permute-start.4) | collective-permute-done | bytes 262176 | tf_op jit(solution)/shard_map/ppermute | solution.py:24
  54.7 0.0 collective-permute-done.8
  54.7 1.7 %fusion.2 = (bf16[1024,256]{1,0:T(8,128)(2,1)S(1)}, f32[1024,256]{1,0:T(8,128)}, f32[1024,256]{1,0:T(8,128)}) fusion(f32[1024,256]{1,0:T(8,128)S(1)} %copy-done.4, bf16[1,1024,256]{2,1,0:T(8,128)(2,1)S(1)} %collective-permute-done.8, f32[2,1024,256]{2,1,0:T(8,128)S(1)} %convert_add_fusion, f32[1024,256]{1,0:T(8,128)S(1)} %copy-done.5), kind=kLoop, calls=%fused_computation.8 | loop fusion | flops 2621440 | bytes 6291456 | tf_op jit(solution)/shard_map/convert_element_type | solution.py:264
  56.4 1.4 %collective-permute-start.10 = (bf16[1024,256]{1,0:T(8,128)(2,1)S(1)}, bf16[1024,256]{1,0:T(8,128)(2,1)S(1)}, u32[]{:S(2)}, u32[]{:S(2)}) collective-permute-start(bf16[1024,256]{1,0:T(8,128)(2,1)S(1)} %get-tuple-element.17.refs_9_), channel_id=1, source_target_pairs={{0,16},{8,24},{16,0},{24,8},{1,17},{9,25},{17,1},{25,9},{2,18},{10... | collective-permute-start | bytes 1572872 | tf_op jit(solution)/shard_map/ppermute | solution.py:24
  57.8 0.0 collective-permute-start.9
  57.8 16.2 %collective-permute-done.5.refs_7_ = bf16[128,1024]{1,0:T(8,128)(2,1)S(1)} collective-permute-done((bf16[128,1024]{1,0:T(8,128)(2,1)S(1)}, bf16[128,1024]{1,0:T(8,128)(2,1)S(1)}, u32[]{:S(2)}, u32[]{:S(2)}) %collective-permute-start.5) | collective-permute-done | bytes 262176 | tf_op jit(solution)/shard_map/ppermute | solution.py:24
  74.1 0.0 collective-permute-done.10.refs_11_
  74.1 0.0 collective-permute-start.11
  74.1 2.0 %collective-permute-start.6 = (bf16[128,1024]{1,0:T(8,128)(2,1)S(1)}, bf16[128,1024]{1,0:T(8,128)(2,1)}, u32[]{:S(2)}, u32[]{:S(2)}) collective-permute-start(bf16[128,1024]{1,0:T(8,128)(2,1)S(1)} %collective-permute-done.5.refs_7_), channel_id=1, source_target_pairs={{0,1},{1,0},{2,3},{3,2},{4,5},{5,4},{6,7},{7,6},{8,9},{9,8},{10,11... | collective-permute-start | bytes 786440 | tf_op jit(solution)/shard_map/ppermute | solution.py:24
  76.1 0.1 pad_add_fusion.place_ref
  76.2 7.0 %collective-permute-done.3.refs_4_ = bf16[128,1024]{1,0:T(8,128)(2,1)S(1)} collective-permute-done((bf16[128,1024]{1,0:T(8,128)(2,1)S(1)}, bf16[128,1024]{1,0:T(8,128)(2,1)S(1)}, u32[]{:S(2)}, u32[]{:S(2)}) %collective-permute-start.3) | collective-permute-done | bytes 262176 | tf_op jit(solution)/shard_map/ppermute | solution.py:24
  83.2 5.3 %collective-permute-done.6.refs_8_ = bf16[128,1024]{1,0:T(8,128)(2,1)} collective-permute-done((bf16[128,1024]{1,0:T(8,128)(2,1)S(1)}, bf16[128,1024]{1,0:T(8,128)(2,1)}, u32[]{:S(2)}, u32[]{:S(2)}) %collective-permute-start.6) | collective-permute-done | bytes 262176 | tf_op jit(solution)/shard_map/ppermute | solution.py:24
  88.5 0.0 collective-permute-done.9.refs_10_
  88.5 7.0 %mix.1 = bf16[1024,1024]{1,0:T(8,128)(2,1)} custom-call(s32[2]{0:T(128)S(1)} %pad_add_fusion.place_ref, bf16[8,1024,128]{2,1,0:T(8,128)(2,1)} %all-to-all-done.refs_0_, bf16[128,1024]{1,0:T(8,128)(2,1)S(1)} %bitcast.21, bf16[128,1024]{1,0:T(8,128)(2,1)S(1)} %collective-permute-done.refs_2_, bf16[128,1024]{1,0:T(8,128)(2,1)S(1)} %collective-permute-done.1.refs_3_, ...), custom_call_target="tpu_custom_call" | custom-call | flops 2147483648 | bytes 10485760 | tf_op jit(solution)/shard_map/mix/pallas_call | solution.py:194
  (14 shorter events, 0.0 us)
Async XLA Ops:
  0.6 14.7 %collective-permute-start.2 = (bf16[128,1024]{1,0:T(8,128)(2,1)}, bf16[128,1024]{1,0:T(8,128)(2,1)S(1)}, u32[]{:S(2)}, u32[]{:S(2)}) collective-permute-start(bf16[128,1024]{1,0:T(8,128)(2,1)} %bitcast.18), channel_id=1, source_target_pairs={{0,4},{1,5},{2,6},{3,7},{4,0},{5,1},{6,2},{7,3},{8,12},{9,13},{10,... | collective-permute-start | bytes 786440 | tf_op jit(solution)/shard_map/ppermute | solution.py:24
  1.0 14.3 %collective-permute-start.1 = (bf16[128,1024]{1,0:T(8,128)(2,1)}, bf16[128,1024]{1,0:T(8,128)(2,1)S(1)}, u32[]{:S(2)}, u32[]{:S(2)}) collective-permute-start(bf16[128,1024]{1,0:T(8,128)(2,1)} %bitcast.19), channel_id=1, source_target_pairs={{0,2},{1,3},{2,0},{3,1},{4,6},{5,7},{6,4},{7,5},{8,10},{9,11},{10,... | collective-permute-start | bytes 786440 | tf_op jit(solution)/shard_map/ppermute | solution.py:24
  1.5 13.9 %collective-permute-start = (bf16[128,1024]{1,0:T(8,128)(2,1)}, bf16[128,1024]{1,0:T(8,128)(2,1)S(1)}, u32[]{:S(2)}, u32[]{:S(2)}) collective-permute-start(bf16[128,1024]{1,0:T(8,128)(2,1)} %bitcast.20), channel_id=1, source_target_pairs={{0,1},{1,0},{2,3},{3,2},{4,5},{5,4},{6,7},{7,6},{8,9},{9,8},{10,11... | collective-permute-start | bytes 786440 | tf_op jit(solution)/shard_map/ppermute | solution.py:24
  3.7 1.6 %copy-start.1 = (bf16[1,128,8192]{2,1,0:T(8,128)(2,1)S(1)}, bf16[1,128,8192]{2,1,0:T(8,128)(2,1)}, u32[]{:S(2)}) copy-start(bf16[1,128,8192]{2,1,0:T(8,128)(2,1)} %param.7) | copy-start | bytes 6291460
  15.4 6.2 %copy-start = (bf16[1,1024,1024]{2,1,0:T(8,128)(2,1)S(1)}, bf16[1,1024,1024]{2,1,0:T(8,128)(2,1)}, u32[]{:S(2)}) copy-start(bf16[1,1024,1024]{2,1,0:T(8,128)(2,1)} %param.10) | copy-start | bytes 6291460
  15.4 73.2 %all-to-all-start = ((bf16[8,1024,128]{2,1,0:T(8,128)(2,1)}), bf16[8,1024,128]{2,1,0:T(8,128)(2,1)}, u32[]{:S(2)}, u32[]{:S(2)}) async-start(bf16[8,1024,128]{2,1,0:T(8,128)(2,1)} %prepare.1), calls=%async_computation | async-start | bytes 4194304 | tf_op jit(solution)/shard_map/all_to_all | solution.py:250
  21.6 1.6 %copy-start.2 = (bf16[1024,1024]{1,0:T(8,128)(2,1)S(1)}, bf16[1024,1024]{1,0:T(8,128)(2,1)}, u32[]{:S(2)}) copy-start(bf16[1024,1024]{1,0:T(8,128)(2,1)} %shared_ref) | copy-start | bytes 6291460
  26.9 2.7 %collective-permute-start.7 = (bf16[2,1024,256]{2,1,0:T(8,128)(2,1)S(1)}, bf16[2,1024,256]{2,1,0:T(8,128)(2,1)S(1)}, u32[]{:S(2)}, u32[]{:S(2)}) collective-permute-start(bf16[2,1024,256]{2,1,0:T(8,128)(2,1)S(1)} %get-tuple-element.14), channel_id=1, source_target_pairs={{0,8},{8,0},{16,24},{24,16},{1,9},{9,1},{17,25},{25,17},{2,10},{10... | collective-permute-start | bytes 3145736 | tf_op jit(solution)/shard_map/ppermute | solution.py:24
  29.6 25.1 %copy-start.4 = (f32[1024,256]{1,0:T(8,128)S(1)}, f32[1024,256]{1,0:T(8,128)}, u32[]{:S(2)}) copy-start(f32[1024,256]{1,0:T(8,128)} %param.12) | copy-start | bytes 3145732
  29.6 25.1 %copy-start.5 = (f32[1024,256]{1,0:T(8,128)S(1)}, f32[1024,256]{1,0:T(8,128)}, u32[]{:S(2)}) copy-start(f32[1024,256]{1,0:T(8,128)} %param.13) | copy-start | bytes 3145732
  29.9 58.6 %copy-start.3 = (bf16[1,128,1024]{2,1,0:T(8,128)(2,1)S(1)}, bf16[1,128,1024]{2,1,0:T(8,128)(2,1)}, u32[]{:S(2)}) copy-start(bf16[1,128,1024]{2,1,0:T(8,128)(2,1)} %param.9) | copy-start | bytes 786436
  29.9 24.8 %collective-permute-start.8 = (bf16[1,1024,256]{2,1,0:T(8,128)(2,1)S(1)}, bf16[1,1024,256]{2,1,0:T(8,128)(2,1)S(1)}, u32[]{:S(2)}, u32[]{:S(2)}) collective-permute-start(bf16[1,1024,256]{2,1,0:T(8,128)(2,1)S(1)} %slice.23), channel_id=1, source_target_pairs={{0,16},{8,24},{16,0},{24,8},{1,17},{9,25},{17,1},{25,9},{2,18},{10... | collective-permute-start | bytes 1572872 | tf_op jit(solution)/shard_map/ppermute | solution.py:24
  30.5 24.2 %collective-permute-start.4 = (bf16[128,1024]{1,0:T(8,128)(2,1)S(1)}, bf16[128,1024]{1,0:T(8,128)(2,1)S(1)}, u32[]{:S(2)}, u32[]{:S(2)}) collective-permute-start(bf16[128,1024]{1,0:T(8,128)(2,1)S(1)} %collective-permute-done.2.refs_5_), channel_id=1, source_target_pairs={{0,1},{1,0},{2,3},{3,2},{4,5},{5,4},{6,7},{7,6},{8,9},{9,8},{10,11... | collective-permute-start | bytes 786440 | tf_op jit(solution)/shard_map/ppermute | solution.py:24
  56.4 17.6 %collective-permute-start.10 = (bf16[1024,256]{1,0:T(8,128)(2,1)S(1)}, bf16[1024,256]{1,0:T(8,128)(2,1)S(1)}, u32[]{:S(2)}, u32[]{:S(2)}) collective-permute-start(bf16[1024,256]{1,0:T(8,128)(2,1)S(1)} %get-tuple-element.17.refs_9_), channel_id=1, source_target_pairs={{0,16},{8,24},{16,0},{24,8},{1,17},{9,25},{17,1},{25,9},{2,18},{10... | collective-permute-start | bytes 1572872 | tf_op jit(solution)/shard_map/ppermute | solution.py:24
  57.8 16.2 %collective-permute-start.5 = (bf16[128,1024]{1,0:T(8,128)(2,1)S(1)}, bf16[128,1024]{1,0:T(8,128)(2,1)S(1)}, u32[]{:S(2)}, u32[]{:S(2)}) collective-permute-start(bf16[128,1024]{1,0:T(8,128)(2,1)S(1)} %collective-permute-done.2.refs_5_), channel_id=1, source_target_pairs={{0,2},{1,3},{2,0},{3,1},{4,6},{5,7},{6,4},{7,5},{8,10},{9,11},{10,... | collective-permute-start | bytes 786440 | tf_op jit(solution)/shard_map/ppermute | solution.py:24
  57.8 30.7 %collective-permute-start.9 = (bf16[1024,256]{1,0:T(8,128)(2,1)S(1)}, bf16[1024,256]{1,0:T(8,128)(2,1)S(1)}, u32[]{:S(2)}, u32[]{:S(2)}) collective-permute-start(bf16[1024,256]{1,0:T(8,128)(2,1)S(1)} %get-tuple-element.17.refs_9_), channel_id=1, source_target_pairs={{0,8},{8,0},{16,24},{24,16},{1,9},{9,1},{17,25},{25,17},{2,10},{10... | collective-permute-start | bytes 1572872 | tf_op jit(solution)/shard_map/ppermute | solution.py:24
  74.1 14.5 %collective-permute-start.11 = (bf16[1024,256]{1,0:T(8,128)(2,1)S(1)}, bf16[1024,256]{1,0:T(8,128)(2,1)}, u32[]{:S(2)}, u32[]{:S(2)}) collective-permute-start(bf16[1024,256]{1,0:T(8,128)(2,1)S(1)} %collective-permute-done.10.refs_11_), channel_id=1, source_target_pairs={{0,8},{8,0},{16,24},{24,16},{1,9},{9,1},{17,25},{25,17},{2,10},{10... | collective-permute-start | bytes 1572872 | tf_op jit(solution)/shard_map/ppermute | solution.py:24
  74.1 9.1 %collective-permute-start.3 = (bf16[128,1024]{1,0:T(8,128)(2,1)S(1)}, bf16[128,1024]{1,0:T(8,128)(2,1)S(1)}, u32[]{:S(2)}, u32[]{:S(2)}) collective-permute-start(bf16[128,1024]{1,0:T(8,128)(2,1)S(1)} %collective-permute-done.1.refs_3_), channel_id=1, source_target_pairs={{0,1},{1,0},{2,3},{3,2},{4,5},{5,4},{6,7},{7,6},{8,9},{9,8},{10,11... | collective-permute-start | bytes 786440 | tf_op jit(solution)/shard_map/ppermute | solution.py:24
  74.1 14.4 %collective-permute-start.6 = (bf16[128,1024]{1,0:T(8,128)(2,1)S(1)}, bf16[128,1024]{1,0:T(8,128)(2,1)}, u32[]{:S(2)}, u32[]{:S(2)}) collective-permute-start(bf16[128,1024]{1,0:T(8,128)(2,1)S(1)} %collective-permute-done.5.refs_7_), channel_id=1, source_target_pairs={{0,1},{1,0},{2,3},{3,2},{4,5},{5,4},{6,7},{7,6},{8,9},{9,8},{10,11... | collective-permute-start | bytes 786440 | tf_op jit(solution)/shard_map/ppermute | solution.py:24

commit v13 on v12

--- a/solution.py
+++ b/solution.py
@@ -142,92 +142,141 @@
     )(own.reshape(1), shared, weight)
 
 
-def mix_kernel(shards, groups, rate, place_ref, *refs):
-    tokens_ref, refs = refs[0], refs[1:]
-    cotangent_refs, refs = refs[:shards], refs[shards:]
-    piece_refs, refs = refs[:groups], refs[groups:]
-    weight_ref, out_ref, refs = refs[0], refs[1], refs[2:]
-    tokens, cotangents, pieces, weights, outs, token_sem, cotangent_sems, piece_sems, weight_sem, out_sems = refs
-    mine, own = place_ref[0], place_ref[1]
-    depth, width = cotangent_refs[0].shape
-    share = pieces.shape[2]
-    tile = outs.shape[2]
-
-    def own_row(k):
-        return pl.ds(pl.multiple_of((mine ^ k) * depth, depth), depth)
-
-    loads = [pltpu.make_async_copy(tokens_ref, tokens, token_sem)]
-    for k, ref in enumerate(cotangent_refs):
-        loads.append(pltpu.make_async_copy(ref, cotangents.at[own_row(k)], cotangent_sems.at[k]))
-    loads.append(pltpu.make_async_copy(weight_ref, weights, weight_sem))
+def base_kernel(own_ref, weight_ref, *refs):
+    piece_refs, (base_ref, weight, pieces, base, load_sem, piece_sems, store_sem) = refs[:-7], refs[-7:]
+    own = own_ref[0]
+    groups, rows, share = pieces.shape
+    loads = [pltpu.make_async_copy(weight_ref, weight, load_sem)]
     for k, ref in enumerate(piece_refs):
         loads.append(pltpu.make_async_copy(ref, pieces.at[own ^ k], piece_sems.at[k]))
     for load in loads:
         load.start()
-    for load in loads[: 1 + shards]:
+    for load in loads:
         load.wait()
-    left = jnp.concatenate([tokens[k] for k in range(shards)], axis=1)
+    for group in range(groups):
+        columns = slice(group * share, (group + 1) * share)
+        mixed = mix_weight * weight[:, columns].astype(jnp.float32)
+        mixed = mixed + (1.0 - mix_weight) * pieces[group].astype(jnp.float32)
+        base[:, columns] = mixed.astype(jnp.bfloat16)
+    store = pltpu.make_async_copy(base, base_ref, store_sem)
+    store.start()
+    store.wait()
+
+
+def base_of(own, weight, pieces):
+    rows, width = weight.shape
+    groups = len(pieces)
+    return pl.pallas_call(
+        base_kernel,
+        out_shape=jax.ShapeDtypeStruct((rows, width), jnp.bfloat16),
+        in_specs=[pl.BlockSpec(memory_space=pltpu.SMEM)] + [pl.BlockSpec(memory_space=pltpu.HBM)] * (1 + groups),
+        out_specs=pl.BlockSpec(memory_space=pltpu.HBM),
+        scratch_shapes=[
+            pltpu.VMEM((rows, width), jnp.bfloat16),
+            pltpu.VMEM((groups, rows, width // groups), jnp.bfloat16),
+            pltpu.VMEM((rows, width), jnp.bfloat16),
+            pltpu.SemaphoreType.DMA,
+            pltpu.SemaphoreType.DMA((groups,)),
+            pltpu.SemaphoreType.DMA,
+        ],
+        compiler_params=pltpu.CompilerParams(vmem_limit_bytes=16 * 2**20),
+        cost_estimate=pl.CostEstimate(flops=3 * rows * width, bytes_accessed=6 * rows * width, transcendentals=0),
+        name="base",
+    )(own.reshape(1), weight, *pieces)
+
+
+def mix_kernel(shards, rate, mine_ref, tokens_ref, base_ref, *refs):
+    cotangent_refs, out_ref, refs = refs[:shards], refs[shards], refs[shards + 1 :]
+    tokens, cotangents, base, totals, outs, token_sems, cotangent_sems, base_sem, out_sems = refs
+    mine = mine_ref[0]
+    depth, width = cotangent_refs[0].shape
+    steps, _, tile = outs.shape
+
+    loads = []
+    for k, ref in enumerate(cotangent_refs):
+        loads.append(pltpu.make_async_copy(tokens_ref.at[mine ^ k], tokens.at[k], token_sems.at[k]))
+        loads.append(pltpu.make_async_copy(ref, cotangents.at[pl.ds(k * depth, depth)], cotangent_sems.at[k]))
+    loads.append(pltpu.make_async_copy(base_ref, base, base_sem))
+    for load in loads:
+        load.start()
     stores = []
-    for step in range(width // tile):
-        columns = slice(step * tile, (step + 1) * tile)
-        total = jnp.dot(left, cotangents[:, columns], preferred_element_type=jnp.float32)
-        if step == 0:
-            for load in loads[1 + shards :]:
-                load.wait()
-        for group in range(step * tile // share, (step + 1) * tile // share):
-            place = slice(group * share, (group + 1) * share)
-            part = slice(group * share - step * tile, (group + 1) * share - step * tile)
-            mixed = weights[:, place].astype(jnp.float32) + pieces[group].astype(jnp.float32)
-            outs[step, :, part] = (mix_weight * mixed - rate * total[:, part]).astype(jnp.bfloat16)
-        stores.append(pltpu.make_async_copy(outs.at[step], out_ref.at[:, pl.ds(step * tile, tile)], out_sems.at[step]))
-        stores[-1].start()
+    some = 2
+    for first in range(0, shards, some):
+        for load in loads[2 * first : 2 * (first + some)]:
+            load.wait()
+        last = first + some == shards
+        if last:
+            loads[-1].wait()
+        left = jnp.concatenate([tokens[k] for k in range(first, first + some)], axis=1)
+        for step in range(steps):
+            columns = slice(step * tile, (step + 1) * tile)
+            right = cotangents[first * depth : (first + some) * depth, columns]
+            total = jnp.dot(left, right, preferred_element_type=jnp.float32)
+            if first:
+                total = totals[step] + total
+            if not last:
+                totals[step] = total
+                continue
+            outs[step] = (base[:, columns].astype(jnp.float32) - rate * total).astype(jnp.bfloat16)
+            place = pl.ds(step * tile, tile)
+            stores.append(pltpu.make_async_copy(outs.at[step], out_ref.at[:, place], out_sems.at[step]))
+            stores[step].start()
     for store in stores:
         store.wait()
 
 
-def mix(mine, own, tokens, cotangents, pieces, weight, rate):
+def mix(mine, tokens, cotangents, base, rate):
     shards, rows, depth = tokens.shape
-    width = weight.shape[1]
-    groups = len(pieces)
-    share = width // groups
-    tile = max(share, 256)
+    width = base.shape[1]
+    tile = min(width, 256)
     return pl.pallas_call(
-        functools.partial(mix_kernel, shards, groups, rate),
+        functools.partial(mix_kernel, shards, rate),
         out_shape=jax.ShapeDtypeStruct((rows, width), jnp.bfloat16),
-        in_specs=[pl.BlockSpec(memory_space=pltpu.SMEM)]
-        + [pl.BlockSpec(memory_space=pltpu.HBM)] * (2 + shards + groups),
+        in_specs=[pl.BlockSpec(memory_space=pltpu.SMEM)] + [pl.BlockSpec(memory_space=pltpu.HBM)] * (2 + shards),
         out_specs=pl.BlockSpec(memory_space=pltpu.HBM),
         scratch_shapes=[
             pltpu.VMEM((shards, rows, depth), jnp.bfloat16),
             pltpu.VMEM((shards * depth, width), jnp.bfloat16),
-            pltpu.VMEM((groups, rows, share), jnp.bfloat16),
-            pltpu.VMEM((rows, width), jnp.bfloat16),
+            pltpu.VMEM((rows, width), jnp.bfloat16),
+            pltpu.VMEM((width // tile, rows, tile), jnp.float32),
             pltpu.VMEM((width // tile, rows, tile), jnp.bfloat16),
-            pltpu.SemaphoreType.DMA,
             pltpu.SemaphoreType.DMA((shards,)),
-            pltpu.SemaphoreType.DMA((groups,)),
+            pltpu.SemaphoreType.DMA((shards,)),
             pltpu.SemaphoreType.DMA,
             pltpu.SemaphoreType.DMA((width // tile,)),
         ],
         compiler_params=pltpu.CompilerParams(vmem_limit_bytes=50 * 2**20),
         cost_estimate=pl.CostEstimate(
             flops=2 * depth * shards * rows * width,
-            bytes_accessed=2 * depth * shards * (rows + width) + 6 * rows * width,
+            bytes_accessed=2 * depth * shards * (rows + width) + 4 * rows * width,
             transcendentals=0,
         ),
         name="mix",
-    )(jnp.stack([mine, own]), tokens, *cotangents, *pieces, weight)
+    )(mine.reshape(1), tokens, base, *cotangents)
+
+
+def later(value, *others):
+    return lax.optimization_barrier((value, *others))[0]
 
 
 def gather(piece, axis, size, after=()):
     pieces = {0: piece}
     bit = size // 2
     while bit:
-        if bit == 1 and after:
-            (*held, _) = lax.optimization_barrier((*(pieces[k] for k in sorted(pieces)[1:]), after))
-            pieces.update(zip(sorted(pieces)[1:], held))
         for k in sorted(pieces):
-            pieces[k ^ bit] = swap(pieces[k], axis, bit)
+            value = later(pieces[k], *after) if bit == 1 and k else pieces[k]
+            pieces[k ^ bit] = swap(value, axis, bit)
+        bit //= 2
+    return [pieces[k] for k in range(size)]
+
+
+def gather_far(piece, axis, size):
+    pieces = {0: swap(piece, axis, size)}
+    pieces[1] = swap(pieces[0], axis, 1)
+    bit = size // 2
+    while bit:
+        for k in [k for k in sorted(pieces) if k ^ bit not in pieces and not k % (2 * bit) % bit and not (bit > 1 and k % 2)]:
+            pieces[k ^ bit] = swap(later(pieces[k], pieces[1]), axis, bit)
         bit //= 2
     return [pieces[k] for k in range(size)]
 
@@ -242,7 +291,8 @@
     inner_rate = inner_gain / math.sqrt(tokens.shape[0] * shards)
 
     own_exchanges = [1 << bit for bit in range(shards.bit_length() - 1)]
-    cotangents = gather(cotangent, "fsdp", shards)
+    half = shards // 2
+    cotangents = gather(cotangent, "fsdp", half) + gather_far(cotangent, "fsdp", half)
     blocks = prepare(tokens, norm_gain, shards)
     *_, blocks, coded_shared, coded_weight = lax.optimization_barrier(
         (*(cotangents[k] for k in own_exchanges), blocks, shared_copy, weight)
@@ -255,15 +305,14 @@
     while bit < groups:
         sent = swap(total[1::2].astype(jnp.bfloat16), "replica", bit)
         bit *= 2
-        if bit >= groups:
-            *_, sent = lax.optimization_barrier((cotangents[shards // 2 + 1], sent))
         total = total[0::2] + sent.astype(jnp.float32)
     average = total[0] / groups
     momentum_next = outer_beta * momentum + average
     master_next = master - outer_rate * (average + outer_beta * momentum_next)
     pieces = gather(master_next.astype(jnp.bfloat16), "replica", groups, after=cotangents[-2:-1])
 
-    layer_next = mix(mine, own, columns, cotangents, pieces, weight, (1.0 - mix_weight) * inner_rate)
+    base = base_of(own, weight, pieces)
+    layer_next = mix(mine, columns, cotangents, base, (1.0 - mix_weight) * inner_rate)
     return (layer_next[None], master_next, momentum_next)
 
 

time: 95.9 us -> 98 us (1.022)
  the two profiles are of different devices: /device:TPU:26 before, /device:TPU:24 now
where the time goes in v13:
time: 98 us; the launch traced here: 97.6 us
  waiting for transfers between devices  55.6 us (57%)
  starting transfers between devices  15.2 us (16%)
  Pallas kernels  13.2 us (13%)
  local copies, waits for them, and re-layouts  10.2 us (10%)
  other arithmetic  2.69 us (3%)
    ppermute x12, waiting for transfers between devices, swap(): return lax.ppermute(value, axis, [(i, i ^ mask) for i in range(size)])  55.6 us
    unnamed x28, local copies, waits for them, and re-layouts  10.1 us
    ppermute x12, starting transfers between devices, swap(): return lax.ppermute(value, axis, [(i, i ^ mask) for i in range(size)])  9 us
    all_to_all x1, starting transfers between devices, on_device(): lax.all_to_all(blocks, 'fsdp', split_axis=0, concat_axis=0, tiled=True)  6.19 us
    pallas_call x1, Pallas kernels, mix(): pl.pallas_call(functools.partial(mix_kernel, shards, rate), out_shape=jax...  5.16 us
    pallas_call x1, Pallas kernels, code_and_decode(): pl.pallas_call(code_kernel, out_shape=(half, half), in_specs=[pl.BlockSpe...  3.69 us
    pallas_call x1, Pallas kernels, base_of(): pl.pallas_call(base_kernel, out_shape=jax.ShapeDtypeStruct((rows, width),...  2.35 us
    pallas_call x1, Pallas kernels, prepare(): pl.pallas_call(prepare_kernel, out_shape=jax.ShapeDtypeStruct((shards, ro...  2.04 us
  transfers between devices with their start and end apart: 13, of which 7 were waited for; matrix products, arithmetic and copies ran while one was open for 3% of the time, Pallas kernels for 8%

profile of v13, /device:TPU:24, one launch (start us, length us, event | category | flops | bytes accessed | tf_op | source)
XLA Modules:
  0.0 97.6 jit_solution(9904201595497720473)
XLA Ops:
  0.6 0.4 collective-permute-start.2
  1.0 0.2 collective-permute-start.1
  1.2 1.8 %collective-permute-start = (bf16[128,1024]{1,0:T(8,128)(2,1)}, bf16[128,1024]{1,0:T(8,128)(2,1)S(1)}, u32[]{:S(2)}, u32[]{:S(2)}) collective-permute-start(bf16[128,1024]{1,0:T(8,128)(2,1)} %bitcast.20), channel_id=1, source_target_pairs={{0,1},{1,0},{2,3},{3,2},{4,5},{5,4},{6,7},{7,6},{8,9},{9,8},{10,11... | collective-permute-start | bytes 786440 | tf_op jit(solution)/shard_map/ppermute | solution.py:24
  3.0 0.7 reshape.24
  3.7 1.6 %copy-done.3 = bf16[1,128,8192]{2,1,0:T(8,128)(2,1)S(1)} copy-done((bf16[1,128,8192]{2,1,0:T(8,128)(2,1)S(1)}, bf16[1,128,8192]{2,1,0:T(8,128)(2,1)}, u32[]{:S(2)}) %copy-start.3) | copy-done | bytes 2097176
  5.3 2.0 %prepare.1 = bf16[8,1024,128]{2,1,0:T(8,128)(2,1)S(1)} custom-call(bf16[128,8192]{1,0:T(8,128)(2,1)S(1)} %bitcast.17, f32[1,8192]{1,0:T(1,128)S(1)} %bitcast.22), custom_call_target="tpu_custom_call" | custom-call | flops 5242880 | bytes 4194304 | tf_op jit(solution)/shard_map/prepare/pallas_call | solution.py:58
  7.4 1.3 %copy-done.1 = bf16[8,1024,128]{2,1,0:T(8,128)(2,1)} copy-done((bf16[8,1024,128]{2,1,0:T(8,128)(2,1)}, bf16[8,1024,128]{2,1,0:T(8,128)(2,1)S(1)}, u32[]{:S(2)}) %copy-start.1) | copy-done | bytes 2097176
  8.7 6.7 %collective-permute-done.2.refs_4_ = bf16[128,1024]{1,0:T(8,128)(2,1)S(1)} collective-permute-done((bf16[128,1024]{1,0:T(8,128)(2,1)}, bf16[128,1024]{1,0:T(8,128)(2,1)S(1)}, u32[]{:S(2)}, u32[]{:S(2)}) %collective-permute-start.2) | collective-permute-done | bytes 262176 | tf_op jit(solution)/shard_map/ppermute | solution.py:24
  15.4 0.7 copy-done.8
  16.1 6.2 %all-to-all-start = ((bf16[8,1024,128]{2,1,0:T(8,128)(2,1)}), bf16[8,1024,128]{2,1,0:T(8,128)(2,1)}, u32[]{:S(2)}, u32[]{:S(2)}) async-start(bf16[8,1024,128]{2,1,0:T(8,128)(2,1)} %copy-done.1), calls=%async_computation | async-start | bytes 4194304 | tf_op jit(solution)/shard_map/all_to_all | solution.py:300
  22.3 1.6 %copy-done.4 = bf16[1024,1024]{1,0:T(8,128)(2,1)S(1)} copy-done((bf16[1024,1024]{1,0:T(8,128)(2,1)S(1)}, bf16[1024,1024]{1,0:T(8,128)(2,1)}, u32[]{:S(2)}) %copy-start.4) | copy-done | bytes 2097176
  23.9 3.7 %code_and_decode.1 = (bf16[2,1024,256]{2,1,0:T(8,128)(2,1)S(1)}, bf16[2,1024,256]{2,1,0:T(8,128)(2,1)S(1)}) custom-call(s32[1]{0:T(128)} %bitcast.5.own_ref, bf16[1024,1024]{1,0:T(8,128)(2,1)S(1)} %copy-done.4, bf16[1024,1024]{1,0:T(8,128)(2,1)S(1)} %bitcast.15), custom_call_target="tpu_custom_call" | custom-call | flops 20971520 | bytes 6291456 | tf_op jit(solution)/shard_map/code_and_decode/pallas_call | solution.py:128
  27.6 0.1 collective-permute-start.3
  27.7 2.6 %collective-permute-done.3 = bf16[2,1024,256]{2,1,0:T(8,128)(2,1)S(1)} collective-permute-done((bf16[2,1024,256]{2,1,0:T(8,128)(2,1)S(1)}, bf16[2,1024,256]{2,1,0:T(8,128)(2,1)S(1)}, u32[]{:S(2)}, u32[]{:S(2)}) %collective-permute-start.3) | collective-permute-done | bytes 1048608 | tf_op jit(solution)/shard_map/ppermute | solution.py:24
  30.3 0.3 convert_add_fusion
  30.6 1.6 %collective-permute-start.4 = (bf16[1,1024,256]{2,1,0:T(8,128)(2,1)S(1)}, bf16[1,1024,256]{2,1,0:T(8,128)(2,1)S(1)}, u32[]{:S(2)}, u32[]{:S(2)}) collective-permute-start(bf16[1,1024,256]{2,1,0:T(8,128)(2,1)S(1)} %slice.23), channel_id=1, source_target_pairs={{0,16},{8,24},{16,0},{24,8},{1,17},{9,25},{17,1},{25,9},{2,18},{10... | collective-permute-start | bytes 1572872 | tf_op jit(solution)/shard_map/ppermute | solution.py:24
  32.2 1.5 %collective-permute-start.7 = (bf16[128,1024]{1,0:T(8,128)(2,1)S(1)}, bf16[128,1024]{1,0:T(8,128)(2,1)S(1)}, u32[]{:S(2)}, u32[]{:S(2)}) collective-permute-start(bf16[128,1024]{1,0:T(8,128)(2,1)S(1)} %collective-permute-done.2.refs_4_), channel_id=1, source_target_pairs={{0,1},{1,0},{2,3},{3,2},{4,5},{5,4},{6,7},{7,6},{8,9},{9,8},{10,11... | collective-permute-start | bytes 786440 | tf_op jit(solution)/shard_map/ppermute | solution.py:24
  33.7 11.0 %collective-permute-done.4 = bf16[1,1024,256]{2,1,0:T(8,128)(2,1)S(1)} collective-permute-done((bf16[1,1024,256]{2,1,0:T(8,128)(2,1)S(1)}, bf16[1,1024,256]{2,1,0:T(8,128)(2,1)S(1)}, u32[]{:S(2)}, u32[]{:S(2)}) %collective-permute-start.4) | collective-permute-done | bytes 524320 | tf_op jit(solution)/shard_map/ppermute | solution.py:24
  44.7 1.7 %fusion.2 = (bf16[1024,256]{1,0:T(8,128)(2,1)S(1)}, f32[1024,256]{1,0:T(8,128)}, f32[1024,256]{1,0:T(8,128)}) fusion(f32[1024,256]{1,0:T(8,128)S(1)} %copy-done.12, bf16[1,1024,256]{2,1,0:T(8,128)(2,1)S(1)} %collective-permute-done.4, f32[2,1024,256]{2,1,0:T(8,128)S(1)} %convert_add_fusion, f32[1024,256]{1,0:T(8,128)S(1)} %copy-done.13), kind=kLoop, calls=%fused_computation.7 | loop fusion | flops 2621440 | bytes 6291456 | tf_op jit(solution)/shard_map/convert_element_type | solution.py:312
  46.4 1.5 %collective-permute-start.6 = (bf16[1024,256]{1,0:T(8,128)(2,1)S(1)}, bf16[1024,256]{1,0:T(8,128)(2,1)S(1)}, u32[]{:S(2)}, u32[]{:S(2)}) collective-permute-start(bf16[1024,256]{1,0:T(8,128)(2,1)S(1)} %get-tuple-element.19.refs_0_), channel_id=1, source_target_pairs={{0,16},{8,24},{16,0},{24,8},{1,17},{9,25},{17,1},{25,9},{2,18},{10... | collective-permute-start | bytes 1572872 | tf_op jit(solution)/shard_map/ppermute | solution.py:24
  47.9 8.4 %collective-permute-done.7.refs_5_ = bf16[128,1024]{1,0:T(8,128)(2,1)S(1)} collective-permute-done((bf16[128,1024]{1,0:T(8,128)(2,1)S(1)}, bf16[128,1024]{1,0:T(8,128)(2,1)S(1)}, u32[]{:S(2)}, u32[]{:S(2)}) %collective-permute-start.7) | collective-permute-done | bytes 262176 | tf_op jit(solution)/shard_map/ppermute | solution.py:24
  56.3 0.7 copy-done.10
  57.0 17.8 %collective-permute-done.8.refs_6_ = bf16[128,1024]{1,0:T(8,128)(2,1)} collective-permute-done((bf16[128,1024]{1,0:T(8,128)(2,1)S(1)}, bf16[128,1024]{1,0:T(8,128)(2,1)}, u32[]{:S(2)}, u32[]{:S(2)}) %collective-permute-start.8) | collective-permute-done | bytes 262176 | tf_op jit(solution)/shard_map/ppermute | solution.py:24
  74.9 2.0 %collective-permute-start.11 = (bf16[128,1024]{1,0:T(8,128)(2,1)}, bf16[128,1024]{1,0:T(8,128)(2,1)}, u32[]{:S(2)}, u32[]{:S(2)}) collective-permute-start(bf16[128,1024]{1,0:T(8,128)(2,1)} %collective-permute-done.8.refs_6_), channel_id=1, source_target_pairs={{0,1},{1,0},{2,3},{3,2},{4,5},{5,4},{6,7},{7,6},{8,9},{9,8},{10,11... | collective-permute-start | bytes 786440 | tf_op jit(solution)/shard_map/ppermute | solution.py:24
  77.0 2.4 %base.1.base_ref = bf16[1024,1024]{1,0:T(8,128)(2,1)S(1)} custom-call(s32[1]{0:T(128)} %bitcast.5.own_ref, bf16[1024,1024]{1,0:T(8,128)(2,1)S(1)} %bitcast.16, bf16[1024,256]{1,0:T(8,128)(2,1)S(1)} %get-tuple-element.19.refs_0_, bf16[1024,256]{1,0:T(8,128)(2,1)} %collective-permute-done.5.refs_1_, bf16[1024,256]{1,0:T(8,128)(2,1)S(1)} %collective-permute-done.6.refs_2_, ...), custom_call_target="tpu_custom_call" | custom-call | flops 3145728 | bytes 6291456 | tf_op jit(solution)/shard_map/base/pallas_call | solution.py:169
  79.3 1.3 %copy-done.2 = bf16[1024,1024]{1,0:T(8,128)(2,1)} copy-done((bf16[1024,1024]{1,0:T(8,128)(2,1)}, bf16[1024,1024]{1,0:T(8,128)(2,1)S(1)}, u32[]{:S(2)}) %copy-start.2) | copy-done | bytes 2097176
  80.6 3.7 %collective-permute-done.10.refs_3_ = bf16[128,1024]{1,0:T(8,128)(2,1)} collective-permute-done((bf16[128,1024]{1,0:T(8,128)(2,1)}, bf16[128,1024]{1,0:T(8,128)(2,1)}, u32[]{:S(2)}, u32[]{:S(2)}) %collective-permute-start.10) | collective-permute-done | bytes 262176 | tf_op jit(solution)/shard_map/ppermute | solution.py:24
  84.3 5.2 %collective-permute-done.11.refs_7_ = bf16[128,1024]{1,0:T(8,128)(2,1)} collective-permute-done((bf16[128,1024]{1,0:T(8,128)(2,1)}, bf16[128,1024]{1,0:T(8,128)(2,1)}, u32[]{:S(2)}, u32[]{:S(2)}) %collective-permute-start.11) | collective-permute-done | bytes 262176 | tf_op jit(solution)/shard_map/ppermute | solution.py:24
  89.6 0.9 copy-done.7
  90.5 0.9 copy-done.9
  91.5 0.9 copy-done.11
  92.4 5.2 %mix.1 = bf16[1024,1024]{1,0:T(8,128)(2,1)} custom-call(s32[1]{0:T(128)} %bitcast.mine_ref, bf16[8,1024,128]{2,1,0:T(8,128)(2,1)} %all-to-all-done.tokens_ref, bf16[1024,1024]{1,0:T(8,128)(2,1)} %copy-done.2, bf16[128,1024]{1,0:T(8,128)(2,1)S(1)} %bitcast.21, bf16[128,1024]{1,0:T(8,128)(2,1)S(1)} %copy-done.9, ...), custom_call_target="tpu_custom_call" | custom-call | flops 2147483648 | bytes 8388608 | tf_op jit(solution)/shard_map/mix/pallas_call | solution.py:232
  (30 shorter events, 0.1 us)
Async XLA Ops:
  0.6 14.7 %collective-permute-start.2 = (bf16[128,1024]{1,0:T(8,128)(2,1)}, bf16[128,1024]{1,0:T(8,128)(2,1)S(1)}, u32[]{:S(2)}, u32[]{:S(2)}) collective-permute-start(bf16[128,1024]{1,0:T(8,128)(2,1)} %bitcast.18), channel_id=1, source_target_pairs={{0,4},{1,5},{2,6},{3,7},{4,0},{5,1},{6,2},{7,3},{8,12},{9,13},{10,... | collective-permute-start | bytes 786440 | tf_op jit(solution)/shard_map/ppermute | solution.py:24
  1.0 14.3 %collective-permute-start.1 = (bf16[128,1024]{1,0:T(8,128)(2,1)}, bf16[128,1024]{1,0:T(8,128)(2,1)}, u32[]{:S(2)}, u32[]{:S(2)}) collective-permute-start(bf16[128,1024]{1,0:T(8,128)(2,1)} %bitcast.19), channel_id=1, source_target_pairs={{0,2},{1,3},{2,0},{3,1},{4,6},{5,7},{6,4},{7,5},{8,10},{9,11},{10,... | collective-permute-start | bytes 786440 | tf_op jit(solution)/shard_map/ppermute | solution.py:24
  1.2 14.1 %collective-permute-start = (bf16[128,1024]{1,0:T(8,128)(2,1)}, bf16[128,1024]{1,0:T(8,128)(2,1)S(1)}, u32[]{:S(2)}, u32[]{:S(2)}) collective-permute-start(bf16[128,1024]{1,0:T(8,128)(2,1)} %bitcast.20), channel_id=1, source_target_pairs={{0,1},{1,0},{2,3},{3,2},{4,5},{5,4},{6,7},{7,6},{8,9},{9,8},{10,11... | collective-permute-start | bytes 786440 | tf_op jit(solution)/shard_map/ppermute | solution.py:24
  3.7 1.6 %copy-start.3 = (bf16[1,128,8192]{2,1,0:T(8,128)(2,1)S(1)}, bf16[1,128,8192]{2,1,0:T(8,128)(2,1)}, u32[]{:S(2)}) copy-start(bf16[1,128,8192]{2,1,0:T(8,128)(2,1)} %param.7) | copy-start | bytes 6291460
  7.4 1.3 %copy-start.1 = (bf16[8,1024,128]{2,1,0:T(8,128)(2,1)}, bf16[8,1024,128]{2,1,0:T(8,128)(2,1)S(1)}, u32[]{:S(2)}) copy-start(bf16[8,1024,128]{2,1,0:T(8,128)(2,1)S(1)} %prepare.1) | copy-start | bytes 6291460
  15.4 41.0 %copy-start.6 = (bf16[128,1024]{1,0:T(8,128)(2,1)}, bf16[128,1024]{1,0:T(8,128)(2,1)S(1)}, u32[]{:S(2)}) copy-start(bf16[128,1024]{1,0:T(8,128)(2,1)S(1)} %collective-permute-done.2.refs_4_) | copy-start | bytes 786436
  15.4 0.7 copy-start.8
  16.1 6.2 %copy-start = (bf16[1,1024,1024]{2,1,0:T(8,128)(2,1)S(1)}, bf16[1,1024,1024]{2,1,0:T(8,128)(2,1)}, u32[]{:S(2)}) copy-start(bf16[1,1024,1024]{2,1,0:T(8,128)(2,1)} %param.10) | copy-start | bytes 6291460
  16.1 73.5 %all-to-all-start = ((bf16[8,1024,128]{2,1,0:T(8,128)(2,1)}), bf16[8,1024,128]{2,1,0:T(8,128)(2,1)}, u32[]{:S(2)}, u32[]{:S(2)}) async-start(bf16[8,1024,128]{2,1,0:T(8,128)(2,1)} %copy-done.1), calls=%async_computation | async-start | bytes 4194304 | tf_op jit(solution)/shard_map/all_to_all | solution.py:300
  22.3 1.6 %copy-start.4 = (bf16[1024,1024]{1,0:T(8,128)(2,1)S(1)}, bf16[1024,1024]{1,0:T(8,128)(2,1)}, u32[]{:S(2)}) copy-start(bf16[1024,1024]{1,0:T(8,128)(2,1)} %shared_ref) | copy-start | bytes 6291460
  27.6 2.7 %collective-permute-start.3 = (bf16[2,1024,256]{2,1,0:T(8,128)(2,1)S(1)}, bf16[2,1024,256]{2,1,0:T(8,128)(2,1)S(1)}, u32[]{:S(2)}, u32[]{:S(2)}) collective-permute-start(bf16[2,1024,256]{2,1,0:T(8,128)(2,1)S(1)} %get-tuple-element.15), channel_id=1, source_target_pairs={{0,8},{8,0},{16,24},{24,16},{1,9},{9,1},{17,25},{25,17},{2,10},{10... | collective-permute-start | bytes 3145736 | tf_op jit(solution)/shard_map/ppermute | solution.py:24
  30.3 14.4 %copy-start.12 = (f32[1024,256]{1,0:T(8,128)S(1)}, f32[1024,256]{1,0:T(8,128)}, u32[]{:S(2)}) copy-start(f32[1024,256]{1,0:T(8,128)} %param.12) | copy-start | bytes 3145732
  30.3 14.4 %copy-start.13 = (f32[1024,256]{1,0:T(8,128)S(1)}, f32[1024,256]{1,0:T(8,128)}, u32[]{:S(2)}) copy-start(f32[1024,256]{1,0:T(8,128)} %param.13) | copy-start | bytes 3145732
  30.6 14.0 %collective-permute-start.4 = (bf16[1,1024,256]{2,1,0:T(8,128)(2,1)S(1)}, bf16[1,1024,256]{2,1,0:T(8,128)(2,1)S(1)}, u32[]{:S(2)}, u32[]{:S(2)}) collective-permute-start(bf16[1,1024,256]{2,1,0:T(8,128)(2,1)S(1)} %slice.23), channel_id=1, source_target_pairs={{0,16},{8,24},{16,0},{24,8},{1,17},{9,25},{17,1},{25,9},{2,18},{10... | collective-permute-start | bytes 1572872 | tf_op jit(solution)/shard_map/ppermute | solution.py:24
  32.2 24.1 %collective-permute-start.7 = (bf16[128,1024]{1,0:T(8,128)(2,1)S(1)}, bf16[128,1024]{1,0:T(8,128)(2,1)S(1)}, u32[]{:S(2)}, u32[]{:S(2)}) collective-permute-start(bf16[128,1024]{1,0:T(8,128)(2,1)S(1)} %collective-permute-done.2.refs_4_), channel_id=1, source_target_pairs={{0,1},{1,0},{2,3},{3,2},{4,5},{5,4},{6,7},{7,6},{8,9},{9,8},{10,11... | collective-permute-start | bytes 786440 | tf_op jit(solution)/shard_map/ppermute | solution.py:24
  46.4 28.5 %collective-permute-start.6 = (bf16[1024,256]{1,0:T(8,128)(2,1)S(1)}, bf16[1024,256]{1,0:T(8,128)(2,1)S(1)}, u32[]{:S(2)}, u32[]{:S(2)}) collective-permute-start(bf16[1024,256]{1,0:T(8,128)(2,1)S(1)} %get-tuple-element.19.refs_0_), channel_id=1, source_target_pairs={{0,16},{8,24},{16,0},{24,8},{1,17},{9,25},{17,1},{25,9},{2,18},{10... | collective-permute-start | bytes 1572872 | tf_op jit(solution)/shard_map/ppermute | solution.py:24
  56.3 0.7 copy-start.10
  57.0 17.9 %collective-permute-start.8 = (bf16[128,1024]{1,0:T(8,128)(2,1)S(1)}, bf16[128,1024]{1,0:T(8,128)(2,1)}, u32[]{:S(2)}, u32[]{:S(2)}) collective-permute-start(bf16[128,1024]{1,0:T(8,128)(2,1)S(1)} %collective-permute-done.2.refs_4_), channel_id=1, source_target_pairs={{0,2},{1,3},{2,0},{3,1},{4,6},{5,7},{6,4},{7,5},{8,10},{9,11},{10,... | collective-permute-start | bytes 786440 | tf_op jit(solution)/shard_map/ppermute | solution.py:24
  57.0 19.9 %collective-permute-start.5 = (bf16[1024,256]{1,0:T(8,128)(2,1)S(1)}, bf16[1024,256]{1,0:T(8,128)(2,1)}, u32[]{:S(2)}, u32[]{:S(2)}) collective-permute-start(bf16[1024,256]{1,0:T(8,128)(2,1)S(1)} %get-tuple-element.19.refs_0_), channel_id=1, source_target_pairs={{0,8},{8,0},{16,24},{24,16},{1,9},{9,1},{17,25},{25,17},{2,10},{10... | collective-permute-start | bytes 1572872 | tf_op jit(solution)/shard_map/ppermute | solution.py:24
  74.9 2.1 %collective-permute-start.9 = (bf16[1024,256]{1,0:T(8,128)(2,1)S(1)}, bf16[1024,256]{1,0:T(8,128)(2,1)}, u32[]{:S(2)}, u32[]{:S(2)}) collective-permute-start(bf16[1024,256]{1,0:T(8,128)(2,1)S(1)} %collective-permute-done.6.refs_2_), channel_id=1, source_target_pairs={{0,8},{8,0},{16,24},{24,16},{1,9},{9,1},{17,25},{25,17},{2,10},{10... | collective-permute-start | bytes 1572872 | tf_op jit(solution)/shard_map/ppermute | solution.py:24
  74.9 9.4 %collective-permute-start.10 = (bf16[128,1024]{1,0:T(8,128)(2,1)}, bf16[128,1024]{1,0:T(8,128)(2,1)}, u32[]{:S(2)}, u32[]{:S(2)}) collective-permute-start(bf16[128,1024]{1,0:T(8,128)(2,1)} %collective-permute-done.1.refs_2_), channel_id=1, source_target_pairs={{0,1},{1,0},{2,3},{3,2},{4,5},{5,4},{6,7},{7,6},{8,9},{9,8},{10,11... | collective-permute-start | bytes 786440 | tf_op jit(solution)/shard_map/ppermute | solution.py:24
  74.9 14.6 %collective-permute-start.11 = (bf16[128,1024]{1,0:T(8,128)(2,1)}, bf16[128,1024]{1,0:T(8,128)(2,1)}, u32[]{:S(2)}, u32[]{:S(2)}) collective-permute-start(bf16[128,1024]{1,0:T(8,128)(2,1)} %collective-permute-done.8.refs_6_), channel_id=1, source_target_pairs={{0,1},{1,0},{2,3},{3,2},{4,5},{5,4},{6,7},{7,6},{8,9},{9,8},{10,11... | collective-permute-start | bytes 786440 | tf_op jit(solution)/shard_map/ppermute | solution.py:24
  76.9 12.6 %copy-start.5 = (bf16[1,128,1024]{2,1,0:T(8,128)(2,1)S(1)}, bf16[1,128,1024]{2,1,0:T(8,128)(2,1)}, u32[]{:S(2)}) copy-start(bf16[1,128,1024]{2,1,0:T(8,128)(2,1)} %param.9) | copy-start | bytes 786436
  79.3 1.3 %copy-start.2 = (bf16[1024,1024]{1,0:T(8,128)(2,1)}, bf16[1024,1024]{1,0:T(8,128)(2,1)S(1)}, u32[]{:S(2)}) copy-start(bf16[1024,1024]{1,0:T(8,128)(2,1)S(1)} %base.1.base_ref) | copy-start | bytes 6291460
  89.6 1.0 copy-start.7
  90.5 0.9 copy-start.9
  91.5 0.9 copy-start.11

commit v14 on v10

--- a/solution.py
+++ b/solution.py
@@ -137,126 +137,133 @@
             pltpu.SemaphoreType.DMA((2, rows // tile)),
         ],
         compiler_params=pltpu.CompilerParams(vmem_limit_bytes=16 * 2**20),
-        cost_estimate=pl.CostEstimate(flops=20 * rows * width, bytes_accessed=360 * rows * width, transcendentals=0),
+        cost_estimate=pl.CostEstimate(flops=20 * rows * width, bytes_accessed=6 * rows * width, transcendentals=0),
         name="code_and_decode",
     )(own.reshape(1), shared, weight)
 
 
-def stage_kernel(*refs):
-    *part_refs, out_ref, sems = refs
-    depth = part_refs[0].shape[0]
-    loads = [
-        pltpu.make_async_copy(ref, out_ref.at[pl.ds(k * depth, depth)], sems.at[k]) for k, ref in enumerate(part_refs)
-    ]
+def base_kernel(own_ref, weight_ref, *refs):
+    piece_refs, (base_ref, weight, pieces, load_sem, piece_sems) = refs[:-5], refs[-5:]
+    own = own_ref[0]
+    groups, rows, share = pieces.shape
+    loads = [pltpu.make_async_copy(weight_ref, weight, load_sem)]
+    for k, ref in enumerate(piece_refs):
+        loads.append(pltpu.make_async_copy(ref, pieces.at[own ^ k], piece_sems.at[k]))
     for load in loads:
         load.start()
     for load in loads:
         load.wait()
-
-
-def stage(parts):
-    depth, width = parts[0].shape
-    return pl.pallas_call(
-        stage_kernel,
-        out_shape=jax.ShapeDtypeStruct((len(parts) * depth, width), parts[0].dtype),
-        in_specs=[pl.BlockSpec(memory_space=pltpu.HBM)] * len(parts),
+    for group in range(groups):
+        columns = slice(group * share, (group + 1) * share)
+        mixed = mix_weight * weight[:, columns].astype(jnp.float32)
+        mixed = mixed + (1.0 - mix_weight) * pieces[group].astype(jnp.float32)
+        base_ref[:, columns] = mixed.astype(jnp.bfloat16)
+
+
+def base_of(own, weight, pieces):
+    rows, width = weight.shape
+    groups = len(pieces)
+    return pl.pallas_call(
+        base_kernel,
+        out_shape=jax.ShapeDtypeStruct((rows, width), jnp.bfloat16),
+        in_specs=[pl.BlockSpec(memory_space=pltpu.SMEM)] + [pl.BlockSpec(memory_space=pltpu.HBM)] * (1 + groups),
         out_specs=pl.BlockSpec(memory_space=pltpu.VMEM),
-        scratch_shapes=[pltpu.SemaphoreType.DMA((len(parts),))],
+        scratch_shapes=[
+            pltpu.VMEM((rows, width), jnp.bfloat16),
+            pltpu.VMEM((groups, rows, width // groups), jnp.bfloat16),
+            pltpu.SemaphoreType.DMA,
+            pltpu.SemaphoreType.DMA((groups,)),
+        ],
         compiler_params=pltpu.CompilerParams(vmem_limit_bytes=16 * 2**20),
-        cost_estimate=pl.CostEstimate(flops=0, bytes_accessed=4 * len(parts) * depth * width, transcendentals=0),
-        name="stage",
-    )(*parts)
-
-
-def accumulate_kernel(groups, rate, place_ref, cotangent_ref, tokens_ref, weight_ref, *refs):
-    piece_refs, refs = refs[:groups], refs[groups:]
-    total_ref, last_ref, tokens, weight, pieces, token_sems, weight_sem, piece_sems, last_sem = refs
-    mine, own = place_ref[0], place_ref[1]
-    parts, rows, depth = tokens.shape
-    width = total_ref.shape[1]
-    share = pieces.shape[2]
-    tile = max(share, 256)
-    loads = [pltpu.make_async_copy(tokens_ref.at[mine ^ k], tokens.at[k], token_sems.at[k]) for k in range(parts)]
-    rest = [pltpu.make_async_copy(weight_ref, weight, weight_sem)]
-    for k, ref in enumerate(piece_refs):
-        rest.append(pltpu.make_async_copy(ref, pieces.at[own ^ k], piece_sems.at[k]))
-    rest.append(pltpu.make_async_copy(tokens_ref.at[mine ^ parts], last_ref, last_sem))
-    for load in loads + rest:
+        cost_estimate=pl.CostEstimate(flops=3 * rows * width, bytes_accessed=6 * rows * width, transcendentals=0),
+        name="base",
+    )(own.reshape(1), weight, *pieces)
+
+
+def accumulate_kernel(parts, mine_ref, tokens_ref, *refs):
+    cotangent_refs, refs = refs[:parts], refs[parts:]
+    total_ref, last_ref, tokens, cotangents, token_sems, cotangent_sems, last_sem = refs
+    mine = mine_ref[0]
+    depth, width = cotangent_refs[0].shape
+    tile = min(width, 256)
+
+    loads = []
+    for k, ref in enumerate(cotangent_refs):
+        loads.append(pltpu.make_async_copy(tokens_ref.at[mine ^ k], tokens.at[k], token_sems.at[k]))
+        loads.append(pltpu.make_async_copy(ref, cotangents.at[pl.ds(k * depth, depth)], cotangent_sems.at[k]))
+    loads.append(pltpu.make_async_copy(tokens_ref.at[mine ^ parts], last_ref, last_sem))
+    for load in loads:
         load.start()
-    for load in loads:
-        load.wait()
-    left = jnp.concatenate([tokens[k] for k in range(parts)], axis=1)
-    for start in range(0, width, tile):
-        product = jnp.dot(left, cotangent_ref[:, start : start + tile], preferred_element_type=jnp.float32)
-        if start == 0:
-            for load in rest:
-                load.wait()
-        for group in range(start // share, (start + tile) // share):
-            columns = slice(group * share, (group + 1) * share)
-            mixed = weight[:, columns].astype(jnp.float32) + pieces[group].astype(jnp.float32)
-            part = slice(group * share - start, (group + 1) * share - start)
-            total_ref[:, columns] = mix_weight * mixed - rate * product[:, part]
-
-
-def accumulate(mine, own, cotangents, tokens, weight, pieces, rate):
+    some = 2
+    for first in range(0, parts, some):
+        end = min(first + some, parts)
+        for load in loads[2 * first : 2 * end]:
+            load.wait()
+        left = jnp.concatenate([tokens[k] for k in range(first, end)], axis=1)
+        for start in range(0, width, tile):
+            columns = slice(start, start + tile)
+            right = cotangents[first * depth : end * depth, columns]
+            total = jnp.dot(left, right, preferred_element_type=jnp.float32)
+            total_ref[:, columns] = total_ref[:, columns] + total if first else total
+    loads[-1].wait()
+
+
+def accumulate(mine, tokens, cotangents):
     shards, rows, depth = tokens.shape
-    width = weight.shape[1]
-    groups = len(pieces)
     parts = shards - 1
-    return pl.pallas_call(
-        functools.partial(accumulate_kernel, groups, rate),
+    width = cotangents[0].shape[1]
+    return pl.pallas_call(
+        functools.partial(accumulate_kernel, parts),
         out_shape=(jax.ShapeDtypeStruct((rows, width), jnp.float32), jax.ShapeDtypeStruct((rows, depth), jnp.bfloat16)),
-        in_specs=[pl.BlockSpec(memory_space=pltpu.SMEM), pl.BlockSpec(memory_space=pltpu.VMEM)]
-        + [pl.BlockSpec(memory_space=pltpu.HBM)] * (2 + groups),
+        in_specs=[pl.BlockSpec(memory_space=pltpu.SMEM)] + [pl.BlockSpec(memory_space=pltpu.HBM)] * (1 + parts),
         out_specs=(pl.BlockSpec(memory_space=pltpu.VMEM),) * 2,
         scratch_shapes=[
             pltpu.VMEM((parts, rows, depth), jnp.bfloat16),
-            pltpu.VMEM((rows, width), jnp.bfloat16),
-            pltpu.VMEM((groups, rows, width // groups), jnp.bfloat16),
+            pltpu.VMEM((parts * depth, width), jnp.bfloat16),
+            pltpu.SemaphoreType.DMA((parts,)),
             pltpu.SemaphoreType.DMA((parts,)),
             pltpu.SemaphoreType.DMA,
-            pltpu.SemaphoreType.DMA((groups,)),
-            pltpu.SemaphoreType.DMA,
         ],
-        compiler_params=pltpu.CompilerParams(vmem_limit_bytes=36 * 2**20),
+        compiler_params=pltpu.CompilerParams(vmem_limit_bytes=44 * 2**20),
         cost_estimate=pl.CostEstimate(
-            flops=2 * parts * depth * rows * width,
-            bytes_accessed=2 * parts * depth * (rows + width) + 8 * rows * width,
+            flops=2 * depth * parts * rows * width,
+            bytes_accessed=2 * depth * shards * (rows + width) + 4 * rows * width,
             transcendentals=0,
         ),
         name="accumulate",
-    )(jnp.stack([mine, own]), cotangents, tokens, weight, *pieces)
-
-
-def finish_kernel(rate, tokens_ref, cotangent_ref, total_ref, out_ref, outs, sems):
+    )(mine.reshape(1), tokens, *cotangents)
+
+
+def finish_kernel(rate, tokens_ref, cotangent_ref, total_ref, base_ref, out_ref, outs, sems):
     steps, _, tile = outs.shape
     stores = []
     for step in range(steps):
         columns = slice(step * tile, (step + 1) * tile)
         product = jnp.dot(tokens_ref[...], cotangent_ref[:, columns], preferred_element_type=jnp.float32)
-        outs[step] = (total_ref[:, columns] - rate * product).astype(jnp.bfloat16)
+        total = total_ref[:, columns] + product
+        outs[step] = (base_ref[:, columns].astype(jnp.float32) - rate * total).astype(jnp.bfloat16)
         stores.append(pltpu.make_async_copy(outs.at[step], out_ref.at[:, pl.ds(step * tile, tile)], sems.at[step]))
         stores[step].start()
     for store in stores:
         store.wait()
 
 
-def finish(tokens, cotangent, total, rate):
+def finish(tokens, cotangent, total, base, rate):
     rows, width = total.shape
     depth = tokens.shape[1]
     tile = min(width, 256)
     return pl.pallas_call(
         functools.partial(finish_kernel, rate),
         out_shape=jax.ShapeDtypeStruct((rows, width), jnp.bfloat16),
-        in_specs=[pl.BlockSpec(memory_space=pltpu.VMEM)] * 3,
+        in_specs=[pl.BlockSpec(memory_space=pltpu.VMEM)] * 4,
         out_specs=pl.BlockSpec(memory_space=pltpu.HBM),
         scratch_shapes=[pltpu.VMEM((width // tile, rows, tile), jnp.bfloat16), pltpu.SemaphoreType.DMA((width // tile,))],
         compiler_params=pltpu.CompilerParams(vmem_limit_bytes=16 * 2**20),
         cost_estimate=pl.CostEstimate(
-            flops=2 * depth * rows * width, bytes_accessed=2 * depth * (rows + width) + 6 * rows * width, transcendentals=0
+            flops=2 * depth * rows * width, bytes_accessed=2 * depth * (rows + width) + 8 * rows * width, transcendentals=0
         ),
         name="finish",
-    )(tokens, cotangent, total)
+    )(tokens, cotangent, total, base)
 
 
 def gather(piece, axis, size):
@@ -278,13 +285,13 @@
     rows, width = weight.shape
     inner_rate = inner_gain / math.sqrt(tokens.shape[0] * shards)
 
-    rate = (1.0 - mix_weight) * inner_rate
-
+    own_exchanges = [1 << bit for bit in range(shards.bit_length() - 1)]
     cotangents = gather(cotangent, "fsdp", shards)
     blocks = prepare(tokens, norm_gain, shards)
+    *_, blocks, coded_shared, coded_weight = lax.optimization_barrier(
+        (*(cotangents[k] for k in own_exchanges), blocks, shared_copy, weight)
+    )
     columns = lax.all_to_all(blocks, "fsdp", split_axis=0, concat_axis=0, tiled=True)
-    first = [cotangents[1 << bit] for bit in range(shards.bit_length() - 1)]
-    *_, coded_shared, coded_weight = lax.optimization_barrier((*first, blocks, shared_copy, weight))
 
     kept, sent = code_and_decode(own, coded_shared, coded_weight, groups)
     total = kept.astype(jnp.float32) + swap(sent, "replica", 1).astype(jnp.float32)
@@ -298,8 +305,8 @@
     master_next = master - outer_rate * (average + outer_beta * momentum_next)
     pieces = gather(master_next.astype(jnp.bfloat16), "replica", groups)
 
-    total, last = accumulate(mine, own, stage(cotangents[:-1]), columns, weight, pieces, rate)
-    layer_next = finish(last, cotangents[-1], total, rate)
+    total, last = accumulate(mine, columns, cotangents[:-1])
+    layer_next = finish(last, cotangents[-1], total, base_of(own, weight, pieces), (1.0 - mix_weight) * inner_rate)
     return (layer_next[None], master_next, momentum_next)
 
 

time: 139 us -> 92.3 us (0.66)
  waiting for transfers between devices: 92 us -> 43.4 us
  local copies, waits for them, and re-layouts: 7.03 us -> 12.4 us
  Pallas kernels: 16 us -> 12.5 us
    ppermute x12, waiting for transfers between devices: 92 us -> 43.4 us  [swap(): return lax.ppermute(value, axis, [(i, i ^ mask) for i in range(size)])]
    unnamed x20 -> x28, local copies, waits for them, and re-layouts: 6.97 us -> 12.4 us
    pallas_call x2, Pallas kernels: 7.36 us -> 4.96 us  [the longest x1 3.89 us: accumulate(): pl.pallas_call(functools.partial(accumulate_kernel, parts), out_shape=(ja...]
    ppermute x12, starting transfers between devices: 12.5 us -> 14.4 us  [swap(): return lax.ppermute(value, axis, [(i, i ^ mask) for i in range(size)])]
    all_to_all x1, starting transfers between devices: 7.42 us -> 5.61 us  [on_device(): lax.all_to_all(blocks, 'fsdp', split_axis=0, concat_axis=0, tiled=True)]
  transfers between devices with their start and end apart: 13 -> 13, of which waited for: 6 -> 6; matrix products, arithmetic and copies ran while one was open for 2% -> 3% of each run, Pallas kernels for 8% -> 12%
where the time goes in v14:
time: 92.3 us; the launch traced here: 91.8 us
  waiting for transfers between devices  43.4 us (47%)
  starting transfers between devices  20 us (22%)
  Pallas kernels  12.5 us (14%)
  local copies, waits for them, and re-layouts  12.4 us (13%)
  other arithmetic  2.64 us (3%)
    ppermute x12, waiting for transfers between devices, swap(): return lax.ppermute(value, axis, [(i, i ^ mask) for i in range(size)])  43.4 us
    ppermute x12, starting transfers between devices, swap(): return lax.ppermute(value, axis, [(i, i ^ mask) for i in range(size)])  14.4 us
    unnamed x28, local copies, waits for them, and re-layouts  12.4 us
    all_to_all x1, starting transfers between devices, on_device(): lax.all_to_all(blocks, 'fsdp', split_axis=0, concat_axis=0, tiled=True)  5.61 us
    pallas_call x1, Pallas kernels, accumulate(): pl.pallas_call(functools.partial(accumulate_kernel, parts), out_shape=(ja...  3.89 us
    pallas_call x1, Pallas kernels, code_and_decode(): pl.pallas_call(code_kernel, out_shape=(half, half), in_specs=[pl.BlockSpe...  3.69 us
    pallas_call x1, Pallas kernels, prepare(): pl.pallas_call(prepare_kernel, out_shape=jax.ShapeDtypeStruct((shards, ro...  2.04 us
  transfers between devices with their start and end apart: 13, of which 6 were waited for; matrix products, arithmetic and copies ran while one was open for 3% of the time, Pallas kernels for 12%

profile of v14, /device:TPU:0, one launch (start us, length us, event | category | flops | bytes accessed | tf_op | source)
XLA Modules:
  0.0 91.8 jit_solution(18268062700441820120)
XLA Ops:
  0.6 4.1 %collective-permute-start.2 = (bf16[128,1024]{1,0:T(8,128)(2,1)}, bf16[128,1024]{1,0:T(8,128)(2,1)}, u32[]{:S(2)}, u32[]{:S(2)}) collective-permute-start(bf16[128,1024]{1,0:T(8,128)(2,1)} %bitcast.19), channel_id=1, source_target_pairs={{0,4},{1,5},{2,6},{3,7},{4,0},{5,1},{6,2},{7,3},{8,12},{9,13},{10,... | collective-permute-start | bytes 786440 | tf_op jit(solution)/shard_map/ppermute | solution.py:24
  4.7 1.6 %collective-permute-start.1 = (bf16[128,1024]{1,0:T(8,128)(2,1)}, bf16[128,1024]{1,0:T(8,128)(2,1)}, u32[]{:S(2)}, u32[]{:S(2)}) collective-permute-start(bf16[128,1024]{1,0:T(8,128)(2,1)} %bitcast.20), channel_id=1, source_target_pairs={{0,2},{1,3},{2,0},{3,1},{4,6},{5,7},{6,4},{7,5},{8,10},{9,11},{10,... | collective-permute-start | bytes 786440 | tf_op jit(solution)/shard_map/ppermute | solution.py:24
  6.3 1.5 %collective-permute-start = (bf16[128,1024]{1,0:T(8,128)(2,1)}, bf16[128,1024]{1,0:T(8,128)(2,1)S(1)}, u32[]{:S(2)}, u32[]{:S(2)}) collective-permute-start(bf16[128,1024]{1,0:T(8,128)(2,1)} %bitcast.21), channel_id=1, source_target_pairs={{0,1},{1,0},{2,3},{3,2},{4,5},{5,4},{6,7},{7,6},{8,9},{9,8},{10,11... | collective-permute-start | bytes 786440 | tf_op jit(solution)/shard_map/ppermute | solution.py:24
  7.8 0.7 reshape.24
  8.6 1.6 %copy-done.3 = bf16[1,128,8192]{2,1,0:T(8,128)(2,1)S(1)} copy-done((bf16[1,128,8192]{2,1,0:T(8,128)(2,1)S(1)}, bf16[1,128,8192]{2,1,0:T(8,128)(2,1)}, u32[]{:S(2)}) %copy-start.3) | copy-done | bytes 2097176
  10.1 2.0 %prepare.1 = bf16[8,1024,128]{2,1,0:T(8,128)(2,1)S(1)} custom-call(bf16[128,8192]{1,0:T(8,128)(2,1)S(1)} %bitcast.17, f32[1,8192]{1,0:T(1,128)S(1)} %bitcast.18), custom_call_target="tpu_custom_call" | custom-call | flops 5242880 | bytes 4194304 | tf_op jit(solution)/shard_map/prepare/pallas_call | solution.py:58
  12.2 1.3 %copy-done.2 = bf16[8,1024,128]{2,1,0:T(8,128)(2,1)} copy-done((bf16[8,1024,128]{2,1,0:T(8,128)(2,1)}, bf16[8,1024,128]{2,1,0:T(8,128)(2,1)S(1)}, u32[]{:S(2)}) %copy-start.2) | copy-done | bytes 2097176
  13.5 3.6 %collective-permute-done.2.refs_4_ = bf16[128,1024]{1,0:T(8,128)(2,1)} collective-permute-done((bf16[128,1024]{1,0:T(8,128)(2,1)}, bf16[128,1024]{1,0:T(8,128)(2,1)}, u32[]{:S(2)}, u32[]{:S(2)}) %collective-permute-start.2) | collective-permute-done | bytes 262176 | tf_op jit(solution)/shard_map/ppermute | solution.py:24
  17.3 0.7 copy-done.10
  18.0 5.6 %all-to-all-start = ((bf16[8,1024,128]{2,1,0:T(8,128)(2,1)}), bf16[8,1024,128]{2,1,0:T(8,128)(2,1)}, u32[]{:S(2)}, u32[]{:S(2)}) async-start(bf16[8,1024,128]{2,1,0:T(8,128)(2,1)} %copy-done.2), calls=%async_computation | async-start | bytes 4194304 | tf_op jit(solution)/shard_map/all_to_all | solution.py:294
  23.6 1.6 %copy-done.4 = bf16[1024,1024]{1,0:T(8,128)(2,1)S(1)} copy-done((bf16[1024,1024]{1,0:T(8,128)(2,1)S(1)}, bf16[1024,1024]{1,0:T(8,128)(2,1)}, u32[]{:S(2)}) %copy-start.4) | copy-done | bytes 2097176
  25.2 3.7 %code_and_decode.1 = (bf16[2,1024,256]{2,1,0:T(8,128)(2,1)S(1)}, bf16[2,1024,256]{2,1,0:T(8,128)(2,1)S(1)}) custom-call(s32[1]{0:T(128)} %bitcast.5.own_ref, bf16[1024,1024]{1,0:T(8,128)(2,1)S(1)} %copy-done.4, bf16[1024,1024]{1,0:T(8,128)(2,1)S(1)} %bitcast.15), custom_call_target="tpu_custom_call" | custom-call | flops 20971520 | bytes 6291456 | tf_op jit(solution)/shard_map/code_and_decode/pallas_call | solution.py:128
  29.0 2.6 %collective-permute-done.7 = bf16[2,1024,256]{2,1,0:T(8,128)(2,1)S(1)} collective-permute-done((bf16[2,1024,256]{2,1,0:T(8,128)(2,1)S(1)}, bf16[2,1024,256]{2,1,0:T(8,128)(2,1)S(1)}, u32[]{:S(2)}, u32[]{:S(2)}) %collective-permute-start.7) | collective-permute-done | bytes 1048608 | tf_op jit(solution)/shard_map/ppermute | solution.py:24
  32.0 1.6 %collective-permute-start.8 = (bf16[1,1024,256]{2,1,0:T(8,128)(2,1)S(1)}, bf16[1,1024,256]{2,1,0:T(8,128)(2,1)S(1)}, u32[]{:S(2)}, u32[]{:S(2)}) collective-permute-start(bf16[1,1024,256]{2,1,0:T(8,128)(2,1)S(1)} %slice.23), channel_id=1, source_target_pairs={{0,16},{8,24},{16,0},{24,8},{1,17},{9,25},{17,1},{25,9},{2,18},{10... | collective-permute-start | bytes 1572872 | tf_op jit(solution)/shard_map/ppermute | solution.py:24
  33.5 12.5 %collective-permute-done.8 = bf16[1,1024,256]{2,1,0:T(8,128)(2,1)S(1)} collective-permute-done((bf16[1,1024,256]{2,1,0:T(8,128)(2,1)S(1)}, bf16[1,1024,256]{2,1,0:T(8,128)(2,1)S(1)}, u32[]{:S(2)}, u32[]{:S(2)}) %collective-permute-start.8) | collective-permute-done | bytes 524320 | tf_op jit(solution)/shard_map/ppermute | solution.py:24
  46.0 1.7 %fusion.2 = (bf16[1024,256]{1,0:T(8,128)(2,1)S(1)}, f32[1024,256]{1,0:T(8,128)}, f32[1024,256]{1,0:T(8,128)}) fusion(f32[1024,256]{1,0:T(8,128)S(1)} %copy-done.12, bf16[1,1024,256]{2,1,0:T(8,128)(2,1)S(1)} %collective-permute-done.8, f32[2,1024,256]{2,1,0:T(8,128)S(1)} %convert_add_fusion, f32[1024,256]{1,0:T(8,128)S(1)} %copy-done.13), kind=kLoop, calls=%fused_computation.7 | loop fusion | flops 2621440 | bytes 6291456 | tf_op jit(solution)/shard_map/convert_element_type | solution.py:306
  47.6 1.5 %collective-permute-start.10 = (bf16[1024,256]{1,0:T(8,128)(2,1)S(1)}, bf16[1024,256]{1,0:T(8,128)(2,1)S(1)}, u32[]{:S(2)}, u32[]{:S(2)}) collective-permute-start(bf16[1024,256]{1,0:T(8,128)(2,1)S(1)} %get-tuple-element.17.refs_0_), channel_id=1, source_target_pairs={{0,16},{8,24},{16,0},{24,8},{1,17},{9,25},{17,1},{25,9},{2,18},{10... | collective-permute-start | bytes 1572872 | tf_op jit(solution)/shard_map/ppermute | solution.py:24
  49.1 11.7 %collective-permute-done.10.refs_2_ = bf16[1024,256]{1,0:T(8,128)(2,1)S(1)} collective-permute-done((bf16[1024,256]{1,0:T(8,128)(2,1)S(1)}, bf16[1024,256]{1,0:T(8,128)(2,1)S(1)}, u32[]{:S(2)}, u32[]{:S(2)}) %collective-permute-start.10) | collective-permute-done | bytes 524320 | tf_op jit(solution)/shard_map/ppermute | solution.py:24
  60.9 2.0 %collective-permute-start.5 = (bf16[128,1024]{1,0:T(8,128)(2,1)}, bf16[128,1024]{1,0:T(8,128)(2,1)}, u32[]{:S(2)}, u32[]{:S(2)}) collective-permute-start(bf16[128,1024]{1,0:T(8,128)(2,1)} %collective-permute-done.2.refs_4_), channel_id=1, source_target_pairs={{0,2},{1,3},{2,0},{3,1},{4,6},{5,7},{6,4},{7,5},{8,10},{9,11},{10,... | collective-permute-start | bytes 786440 | tf_op jit(solution)/shard_map/ppermute | solution.py:24
  62.9 1.5 %collective-permute-start.4 = (bf16[128,1024]{1,0:T(8,128)(2,1)}, bf16[128,1024]{1,0:T(8,128)(2,1)}, u32[]{:S(2)}, u32[]{:S(2)}) collective-permute-start(bf16[128,1024]{1,0:T(8,128)(2,1)} %collective-permute-done.2.refs_4_), channel_id=1, source_target_pairs={{0,1},{1,0},{2,3},{3,2},{4,5},{5,4},{6,7},{7,6},{8,9},{9,8},{10,11... | collective-permute-start | bytes 786440 | tf_op jit(solution)/shard_map/ppermute | solution.py:24
  64.4 0.6 collective-permute-start.3
  64.9 12.8 %collective-permute-done.5.refs_6_ = bf16[128,1024]{1,0:T(8,128)(2,1)} collective-permute-done((bf16[128,1024]{1,0:T(8,128)(2,1)}, bf16[128,1024]{1,0:T(8,128)(2,1)}, u32[]{:S(2)}, u32[]{:S(2)}) %collective-permute-start.5) | collective-permute-done | bytes 262176 | tf_op jit(solution)/shard_map/ppermute | solution.py:24
  77.7 0.8 copy-done.5
  78.6 0.8 copy-done.7
  79.4 1.6 %copy-done.1 = bf16[1,1024,1024]{2,1,0:T(8,128)(2,1)S(1)} copy-done((bf16[1,1024,1024]{2,1,0:T(8,128)(2,1)S(1)}, bf16[1,1024,1024]{2,1,0:T(8,128)(2,1)}, u32[]{:S(2)}) %copy-start.1) | copy-done | bytes 2097176
  81.0 1.0 %copy-done.6 = bf16[1024,256]{1,0:T(8,128)(2,1)S(1)} copy-done((bf16[1024,256]{1,0:T(8,128)(2,1)S(1)}, bf16[1024,256]{1,0:T(8,128)(2,1)}, u32[]{:S(2)}) %copy-start.6) | copy-done | bytes 524312
  82.0 1.0 %copy-done.8 = bf16[1024,256]{1,0:T(8,128)(2,1)S(1)} copy-done((bf16[1024,256]{1,0:T(8,128)(2,1)S(1)}, bf16[1024,256]{1,0:T(8,128)(2,1)}, u32[]{:S(2)}) %copy-start.8) | copy-done | bytes 524312
  83.0 1.1 %base.1.base_ref = bf16[1024,1024]{1,0:T(8,128)(2,1)S(1)} custom-call(s32[1]{0:T(128)} %bitcast.5.own_ref, bf16[1024,1024]{1,0:T(8,128)(2,1)S(1)} %bitcast.16, bf16[1024,256]{1,0:T(8,128)(2,1)S(1)} %get-tuple-element.17.refs_0_, bf16[1024,256]{1,0:T(8,128)(2,1)S(1)} %copy-done.6, bf16[1024,256]{1,0:T(8,128)(2,1)S(1)} %collective-permute-done.10.refs_2_, ...), custom_call_target="tpu_custom_call" | custom-call | flops 3145728 | bytes 6291456 | tf_op jit(solution)/shard_map/base/pallas_call | solution.py:166
  84.2 0.9 %copy-done.9 = bf16[1,128,1024]{2,1,0:T(8,128)(2,1)S(1)} copy-done((bf16[1,128,1024]{2,1,0:T(8,128)(2,1)S(1)}, bf16[1,128,1024]{2,1,0:T(8,128)(2,1)}, u32[]{:S(2)}) %copy-start.9) | copy-done | bytes 262168
  85.1 0.9 %copy-done.11 = bf16[128,1024]{1,0:T(8,128)(2,1)S(1)} copy-done((bf16[128,1024]{1,0:T(8,128)(2,1)S(1)}, bf16[128,1024]{1,0:T(8,128)(2,1)}, u32[]{:S(2)}) %copy-start.11) | copy-done | bytes 262168
  86.1 3.9 %accumulate.1 = (f32[1024,1024]{1,0:T(8,128)S(1)}, bf16[1024,128]{1,0:T(8,128)(2,1)S(1)}) custom-call(s32[1]{0:T(128)} %bitcast.mine_ref, bf16[8,1024,128]{2,1,0:T(8,128)(2,1)} %all-to-all-done.tokens_ref, bf16[128,1024]{1,0:T(8,128)(2,1)S(1)} %bitcast.22, bf16[128,1024]{1,0:T(8,128)(2,1)S(1)} %copy-done.11, ...), custom_call_target="tpu_custom_call" | custom-call | flops 1879048192 | bytes 8388608 | tf_op jit(solution)/shard_map/accumulate/pallas_call | solution.py:215
  90.0 1.8 %finish.1 = bf16[1024,1024]{1,0:T(8,128)(2,1)} custom-call(bf16[1024,128]{1,0:T(8,128)(2,1)S(1)} %get-tuple-element.11.tokens_ref, bf16[128,1024]{1,0:T(8,128)(2,1)S(1)} %collective-permute-done.6.cotangent_ref, f32[1024,1024]{1,0:T(8,128)S(1)} %get-tuple-element.12.total_ref, bf16[1024,1024]{1,0:T(8,128)(2,1)S(1)} %base.1.base_ref), custom_call_target="tpu_custom_call" | custom-call | flops 268435456 | bytes 8912896 | tf_op jit(solution)/shard_map/finish/pallas_call | solution.py:255
  (31 shorter events, 0.6 us)
Async XLA Ops:
  0.6 16.5 %collective-permute-start.2 = (bf16[128,1024]{1,0:T(8,128)(2,1)}, bf16[128,1024]{1,0:T(8,128)(2,1)}, u32[]{:S(2)}, u32[]{:S(2)}) collective-permute-start(bf16[128,1024]{1,0:T(8,128)(2,1)} %bitcast.19), channel_id=1, source_target_pairs={{0,4},{1,5},{2,6},{3,7},{4,0},{5,1},{6,2},{7,3},{8,12},{9,13},{10,... | collective-permute-start | bytes 786440 | tf_op jit(solution)/shard_map/ppermute | solution.py:24
  4.7 12.5 %collective-permute-start.1 = (bf16[128,1024]{1,0:T(8,128)(2,1)}, bf16[128,1024]{1,0:T(8,128)(2,1)}, u32[]{:S(2)}, u32[]{:S(2)}) collective-permute-start(bf16[128,1024]{1,0:T(8,128)(2,1)} %bitcast.20), channel_id=1, source_target_pairs={{0,2},{1,3},{2,0},{3,1},{4,6},{5,7},{6,4},{7,5},{8,10},{9,11},{10,... | collective-permute-start | bytes 786440 | tf_op jit(solution)/shard_map/ppermute | solution.py:24
  6.3 11.0 %collective-permute-start = (bf16[128,1024]{1,0:T(8,128)(2,1)}, bf16[128,1024]{1,0:T(8,128)(2,1)S(1)}, u32[]{:S(2)}, u32[]{:S(2)}) collective-permute-start(bf16[128,1024]{1,0:T(8,128)(2,1)} %bitcast.21), channel_id=1, source_target_pairs={{0,1},{1,0},{2,3},{3,2},{4,5},{5,4},{6,7},{7,6},{8,9},{9,8},{10,11... | collective-permute-start | bytes 786440 | tf_op jit(solution)/shard_map/ppermute | solution.py:24
  8.5 1.6 %copy-start.3 = (bf16[1,128,8192]{2,1,0:T(8,128)(2,1)S(1)}, bf16[1,128,8192]{2,1,0:T(8,128)(2,1)}, u32[]{:S(2)}) copy-start(bf16[1,128,8192]{2,1,0:T(8,128)(2,1)} %param.7) | copy-start | bytes 6291460
  12.2 1.3 %copy-start.2 = (bf16[8,1024,128]{2,1,0:T(8,128)(2,1)}, bf16[8,1024,128]{2,1,0:T(8,128)(2,1)S(1)}, u32[]{:S(2)}) copy-start(bf16[8,1024,128]{2,1,0:T(8,128)(2,1)S(1)} %prepare.1) | copy-start | bytes 6291460
  17.3 0.7 copy-start.10
  18.0 5.6 %copy-start = (bf16[1,1024,1024]{2,1,0:T(8,128)(2,1)S(1)}, bf16[1,1024,1024]{2,1,0:T(8,128)(2,1)}, u32[]{:S(2)}) copy-start(bf16[1,1024,1024]{2,1,0:T(8,128)(2,1)} %param.10) | copy-start | bytes 6291460
  18.0 66.2 %all-to-all-start = ((bf16[8,1024,128]{2,1,0:T(8,128)(2,1)}), bf16[8,1024,128]{2,1,0:T(8,128)(2,1)}, u32[]{:S(2)}, u32[]{:S(2)}) async-start(bf16[8,1024,128]{2,1,0:T(8,128)(2,1)} %copy-done.2), calls=%async_computation | async-start | bytes 4194304 | tf_op jit(solution)/shard_map/all_to_all | solution.py:294
  23.6 1.6 %copy-start.4 = (bf16[1024,1024]{1,0:T(8,128)(2,1)S(1)}, bf16[1024,1024]{1,0:T(8,128)(2,1)}, u32[]{:S(2)}) copy-start(bf16[1024,1024]{1,0:T(8,128)(2,1)} %shared_ref) | copy-start | bytes 6291460
  28.9 2.7 %collective-permute-start.7 = (bf16[2,1024,256]{2,1,0:T(8,128)(2,1)S(1)}, bf16[2,1024,256]{2,1,0:T(8,128)(2,1)S(1)}, u32[]{:S(2)}, u32[]{:S(2)}) collective-permute-start(bf16[2,1024,256]{2,1,0:T(8,128)(2,1)S(1)} %get-tuple-element.16), channel_id=1, source_target_pairs={{0,8},{8,0},{16,24},{24,16},{1,9},{9,1},{17,25},{25,17},{2,10},{10... | collective-permute-start | bytes 3145736 | tf_op jit(solution)/shard_map/ppermute | solution.py:24
  31.6 14.4 %copy-start.12 = (f32[1024,256]{1,0:T(8,128)S(1)}, f32[1024,256]{1,0:T(8,128)}, u32[]{:S(2)}) copy-start(f32[1024,256]{1,0:T(8,128)} %param.12) | copy-start | bytes 3145732
  31.6 14.4 %copy-start.13 = (f32[1024,256]{1,0:T(8,128)S(1)}, f32[1024,256]{1,0:T(8,128)}, u32[]{:S(2)}) copy-start(f32[1024,256]{1,0:T(8,128)} %param.13) | copy-start | bytes 3145732
  32.0 14.0 %collective-permute-start.8 = (bf16[1,1024,256]{2,1,0:T(8,128)(2,1)S(1)}, bf16[1,1024,256]{2,1,0:T(8,128)(2,1)S(1)}, u32[]{:S(2)}, u32[]{:S(2)}) collective-permute-start(bf16[1,1024,256]{2,1,0:T(8,128)(2,1)S(1)} %slice.23), channel_id=1, source_target_pairs={{0,16},{8,24},{16,0},{24,8},{1,17},{9,25},{17,1},{25,9},{2,18},{10... | collective-permute-start | bytes 1572872 | tf_op jit(solution)/shard_map/ppermute | solution.py:24
  47.6 13.2 %collective-permute-start.10 = (bf16[1024,256]{1,0:T(8,128)(2,1)S(1)}, bf16[1024,256]{1,0:T(8,128)(2,1)S(1)}, u32[]{:S(2)}, u32[]{:S(2)}) collective-permute-start(bf16[1024,256]{1,0:T(8,128)(2,1)S(1)} %get-tuple-element.17.refs_0_), channel_id=1, source_target_pairs={{0,16},{8,24},{16,0},{24,8},{1,17},{9,25},{17,1},{25,9},{2,18},{10... | collective-permute-start | bytes 1572872 | tf_op jit(solution)/shard_map/ppermute | solution.py:24
  49.1 28.6 %collective-permute-start.9 = (bf16[1024,256]{1,0:T(8,128)(2,1)S(1)}, bf16[1024,256]{1,0:T(8,128)(2,1)S(1)}, u32[]{:S(2)}, u32[]{:S(2)}) collective-permute-start(bf16[1024,256]{1,0:T(8,128)(2,1)S(1)} %get-tuple-element.17.refs_0_), channel_id=1, source_target_pairs={{0,8},{8,0},{16,24},{24,16},{1,9},{9,1},{17,25},{25,17},{2,10},{10... | collective-permute-start | bytes 1572872 | tf_op jit(solution)/shard_map/ppermute | solution.py:24
  60.9 17.7 %collective-permute-start.11 = (bf16[1024,256]{1,0:T(8,128)(2,1)S(1)}, bf16[1024,256]{1,0:T(8,128)(2,1)S(1)}, u32[]{:S(2)}, u32[]{:S(2)}) collective-permute-start(bf16[1024,256]{1,0:T(8,128)(2,1)S(1)} %collective-permute-done.10.refs_2_), channel_id=1, source_target_pairs={{0,8},{8,0},{16,24},{24,16},{1,9},{9,1},{17,25},{25,17},{2,10},{10... | collective-permute-start | bytes 1572872 | tf_op jit(solution)/shard_map/ppermute | solution.py:24
  60.9 16.8 %collective-permute-start.5 = (bf16[128,1024]{1,0:T(8,128)(2,1)}, bf16[128,1024]{1,0:T(8,128)(2,1)}, u32[]{:S(2)}, u32[]{:S(2)}) collective-permute-start(bf16[128,1024]{1,0:T(8,128)(2,1)} %collective-permute-done.2.refs_4_), channel_id=1, source_target_pairs={{0,2},{1,3},{2,0},{3,1},{4,6},{5,7},{6,4},{7,5},{8,10},{9,11},{10,... | collective-permute-start | bytes 786440 | tf_op jit(solution)/shard_map/ppermute | solution.py:24
  62.9 21.2 %collective-permute-start.4 = (bf16[128,1024]{1,0:T(8,128)(2,1)}, bf16[128,1024]{1,0:T(8,128)(2,1)}, u32[]{:S(2)}, u32[]{:S(2)}) collective-permute-start(bf16[128,1024]{1,0:T(8,128)(2,1)} %collective-permute-done.2.refs_4_), channel_id=1, source_target_pairs={{0,1},{1,0},{2,3},{3,2},{4,5},{5,4},{6,7},{7,6},{8,9},{9,8},{10,11... | collective-permute-start | bytes 786440 | tf_op jit(solution)/shard_map/ppermute | solution.py:24
  64.4 19.8 %collective-permute-start.3 = (bf16[128,1024]{1,0:T(8,128)(2,1)}, bf16[128,1024]{1,0:T(8,128)(2,1)}, u32[]{:S(2)}, u32[]{:S(2)}) collective-permute-start(bf16[128,1024]{1,0:T(8,128)(2,1)} %collective-permute-done.1.refs_2_), channel_id=1, source_target_pairs={{0,1},{1,0},{2,3},{3,2},{4,5},{5,4},{6,7},{7,6},{8,9},{9,8},{10,11... | collective-permute-start | bytes 786440 | tf_op jit(solution)/shard_map/ppermute | solution.py:24
  77.7 12.2 %collective-permute-start.6 = (bf16[128,1024]{1,0:T(8,128)(2,1)}, bf16[128,1024]{1,0:T(8,128)(2,1)S(1)}, u32[]{:S(2)}, u32[]{:S(2)}) collective-permute-start(bf16[128,1024]{1,0:T(8,128)(2,1)} %collective-permute-done.5.refs_6_), channel_id=1, source_target_pairs={{0,1},{1,0},{2,3},{3,2},{4,5},{5,4},{6,7},{7,6},{8,9},{9,8},{10,11... | collective-permute-start | bytes 786440 | tf_op jit(solution)/shard_map/ppermute | solution.py:24
  77.7 0.8 copy-start.5
  78.6 0.8 copy-start.7
  79.4 1.6 %copy-start.1 = (bf16[1,1024,1024]{2,1,0:T(8,128)(2,1)S(1)}, bf16[1,1024,1024]{2,1,0:T(8,128)(2,1)}, u32[]{:S(2)}) copy-start(bf16[1,1024,1024]{2,1,0:T(8,128)(2,1)} %param.10) | copy-start | bytes 6291460
  80.9 1.0 %copy-start.6 = (bf16[1024,256]{1,0:T(8,128)(2,1)S(1)}, bf16[1024,256]{1,0:T(8,128)(2,1)}, u32[]{:S(2)}) copy-start(bf16[1024,256]{1,0:T(8,128)(2,1)} %copy-done.5) | copy-start | bytes 1572868
  82.0 1.0 %copy-start.8 = (bf16[1024,256]{1,0:T(8,128)(2,1)S(1)}, bf16[1024,256]{1,0:T(8,128)(2,1)}, u32[]{:S(2)}) copy-start(bf16[1024,256]{1,0:T(8,128)(2,1)} %copy-done.7) | copy-start | bytes 1572868
  84.1 1.0 %copy-start.9 = (bf16[1,128,1024]{2,1,0:T(8,128)(2,1)S(1)}, bf16[1,128,1024]{2,1,0:T(8,128)(2,1)}, u32[]{:S(2)}) copy-start(bf16[1,128,1024]{2,1,0:T(8,128)(2,1)} %param.9) | copy-start | bytes 786436
  85.1 0.9 %copy-start.11 = (bf16[128,1024]{1,0:T(8,128)(2,1)S(1)}, bf16[128,1024]{1,0:T(8,128)(2,1)}, u32[]{:S(2)}) copy-start(bf16[128,1024]{1,0:T(8,128)(2,1)} %copy-done.10) | copy-start | bytes 786436

commit v15 on v14

--- a/solution.py
+++ b/solution.py
@@ -142,47 +142,9 @@
     )(own.reshape(1), shared, weight)
 
 
-def base_kernel(own_ref, weight_ref, *refs):
-    piece_refs, (base_ref, weight, pieces, load_sem, piece_sems) = refs[:-5], refs[-5:]
-    own = own_ref[0]
-    groups, rows, share = pieces.shape
-    loads = [pltpu.make_async_copy(weight_ref, weight, load_sem)]
-    for k, ref in enumerate(piece_refs):
-        loads.append(pltpu.make_async_copy(ref, pieces.at[own ^ k], piece_sems.at[k]))
-    for load in loads:
-        load.start()
-    for load in loads:
-        load.wait()
-    for group in range(groups):
-        columns = slice(group * share, (group + 1) * share)
-        mixed = mix_weight * weight[:, columns].astype(jnp.float32)
-        mixed = mixed + (1.0 - mix_weight) * pieces[group].astype(jnp.float32)
-        base_ref[:, columns] = mixed.astype(jnp.bfloat16)
-
-
-def base_of(own, weight, pieces):
-    rows, width = weight.shape
-    groups = len(pieces)
-    return pl.pallas_call(
-        base_kernel,
-        out_shape=jax.ShapeDtypeStruct((rows, width), jnp.bfloat16),
-        in_specs=[pl.BlockSpec(memory_space=pltpu.SMEM)] + [pl.BlockSpec(memory_space=pltpu.HBM)] * (1 + groups),
-        out_specs=pl.BlockSpec(memory_space=pltpu.VMEM),
-        scratch_shapes=[
-            pltpu.VMEM((rows, width), jnp.bfloat16),
-            pltpu.VMEM((groups, rows, width // groups), jnp.bfloat16),
-            pltpu.SemaphoreType.DMA,
-            pltpu.SemaphoreType.DMA((groups,)),
-        ],
-        compiler_params=pltpu.CompilerParams(vmem_limit_bytes=16 * 2**20),
-        cost_estimate=pl.CostEstimate(flops=3 * rows * width, bytes_accessed=6 * rows * width, transcendentals=0),
-        name="base",
-    )(own.reshape(1), weight, *pieces)
-
-
-def accumulate_kernel(parts, mine_ref, tokens_ref, *refs):
+def accumulate_kernel(parts, rate, mine_ref, tokens_ref, weight_ref, *refs):
     cotangent_refs, refs = refs[:parts], refs[parts:]
-    total_ref, last_ref, tokens, cotangents, token_sems, cotangent_sems, last_sem = refs
+    total_ref, last_ref, tokens, cotangents, weight, token_sems, cotangent_sems, last_sem, weight_sem = refs
     mine = mine_ref[0]
     depth, width = cotangent_refs[0].shape
     tile = min(width, 256)
@@ -191,6 +153,7 @@
     for k, ref in enumerate(cotangent_refs):
         loads.append(pltpu.make_async_copy(tokens_ref.at[mine ^ k], tokens.at[k], token_sems.at[k]))
         loads.append(pltpu.make_async_copy(ref, cotangents.at[pl.ds(k * depth, depth)], cotangent_sems.at[k]))
+    loads.append(pltpu.make_async_copy(weight_ref, weight, weight_sem))
     loads.append(pltpu.make_async_copy(tokens_ref.at[mine ^ parts], last_ref, last_sem))
     for load in loads:
         load.start()
@@ -204,66 +167,87 @@
             columns = slice(start, start + tile)
             right = cotangents[first * depth : end * depth, columns]
             total = jnp.dot(left, right, preferred_element_type=jnp.float32)
-            total_ref[:, columns] = total_ref[:, columns] + total if first else total
+            if first:
+                total = total_ref[:, columns] + total
+            if end == parts:
+                if start == 0:
+                    loads[-2].wait()
+                total = mix_weight * weight[:, columns].astype(jnp.float32) - rate * total
+            total_ref[:, columns] = total
     loads[-1].wait()
 
 
-def accumulate(mine, tokens, cotangents):
+def accumulate(mine, tokens, cotangents, weight, rate):
     shards, rows, depth = tokens.shape
     parts = shards - 1
     width = cotangents[0].shape[1]
     return pl.pallas_call(
-        functools.partial(accumulate_kernel, parts),
+        functools.partial(accumulate_kernel, parts, rate),
         out_shape=(jax.ShapeDtypeStruct((rows, width), jnp.float32), jax.ShapeDtypeStruct((rows, depth), jnp.bfloat16)),
-        in_specs=[pl.BlockSpec(memory_space=pltpu.SMEM)] + [pl.BlockSpec(memory_space=pltpu.HBM)] * (1 + parts),
+        in_specs=[pl.BlockSpec(memory_space=pltpu.SMEM)] + [pl.BlockSpec(memory_space=pltpu.HBM)] * (2 + parts),
         out_specs=(pl.BlockSpec(memory_space=pltpu.VMEM),) * 2,
         scratch_shapes=[
             pltpu.VMEM((parts, rows, depth), jnp.bfloat16),
             pltpu.VMEM((parts * depth, width), jnp.bfloat16),
+            pltpu.VMEM((rows, width), jnp.bfloat16),
             pltpu.SemaphoreType.DMA((parts,)),
             pltpu.SemaphoreType.DMA((parts,)),
             pltpu.SemaphoreType.DMA,
+            pltpu.SemaphoreType.DMA,
         ],
-        compiler_params=pltpu.CompilerParams(vmem_limit_bytes=44 * 2**20),
+        compiler_params=pltpu.CompilerParams(vmem_limit_bytes=40 * 2**20),
         cost_estimate=pl.CostEstimate(
             flops=2 * depth * parts * rows * width,
             bytes_accessed=2 * depth * shards * (rows + width) + 4 * rows * width,
             transcendentals=0,
         ),
         name="accumulate",
-    )(mine.reshape(1), tokens, *cotangents)
-
-
-def finish_kernel(rate, tokens_ref, cotangent_ref, total_ref, base_ref, out_ref, outs, sems):
+    )(mine.reshape(1), tokens, weight, *cotangents)
+
+
+def finish_kernel(groups, rate, own_ref, tokens_ref, cotangent_ref, total_ref, *refs):
+    piece_refs, (out_ref, pieces, outs, sems) = refs[:groups], refs[groups:]
+    share = pieces.shape[2]
     steps, _, tile = outs.shape
+    for k, ref in enumerate(piece_refs):
+        pieces[own_ref[0] ^ k] = ref[...]
     stores = []
     for step in range(steps):
         columns = slice(step * tile, (step + 1) * tile)
         product = jnp.dot(tokens_ref[...], cotangent_ref[:, columns], preferred_element_type=jnp.float32)
-        total = total_ref[:, columns] + product
-        outs[step] = (base_ref[:, columns].astype(jnp.float32) - rate * total).astype(jnp.bfloat16)
+        total = total_ref[:, columns] - rate * product
+        for group in range(step * tile // share, (step + 1) * tile // share):
+            part = slice(group * share - step * tile, (group + 1) * share - step * tile)
+            shared = pieces[group].astype(jnp.float32)
+            outs[step, :, part] = (total[:, part] + (1.0 - mix_weight) * shared).astype(jnp.bfloat16)
         stores.append(pltpu.make_async_copy(outs.at[step], out_ref.at[:, pl.ds(step * tile, tile)], sems.at[step]))
         stores[step].start()
     for store in stores:
         store.wait()
 
 
-def finish(tokens, cotangent, total, base, rate):
+def finish(own, tokens, cotangent, total, pieces, rate):
     rows, width = total.shape
     depth = tokens.shape[1]
-    tile = min(width, 256)
+    groups = len(pieces)
+    share = width // groups
+    tile = max(share, 256)
     return pl.pallas_call(
-        functools.partial(finish_kernel, rate),
+        functools.partial(finish_kernel, groups, rate),
         out_shape=jax.ShapeDtypeStruct((rows, width), jnp.bfloat16),
-        in_specs=[pl.BlockSpec(memory_space=pltpu.VMEM)] * 4,
+        in_specs=[pl.BlockSpec(memory_space=pltpu.SMEM)] + [pl.BlockSpec(memory_space=pltpu.VMEM)] * (3 + groups),
         out_specs=pl.BlockSpec(memory_space=pltpu.HBM),
-        scratch_shapes=[pltpu.VMEM((width // tile, rows, tile), jnp.bfloat16), pltpu.SemaphoreType.DMA((width // tile,))],
+        scratch_shapes=[
+            pltpu.VMEM((groups, rows, share), jnp.bfloat16),
+            pltpu.VMEM((width // tile, rows, tile), jnp.bfloat16),
+            pltpu.SemaphoreType.DMA((width // tile,)),
+        ],
         compiler_params=pltpu.CompilerParams(vmem_limit_bytes=16 * 2**20),
         cost_estimate=pl.CostEstimate(
             flops=2 * depth * rows * width, bytes_accessed=2 * depth * (rows + width) + 8 * rows * width, transcendentals=0
         ),
         name="finish",
-    )(tokens, cotangent, total, base)
+    )(own.reshape(1), tokens, cotangent, total, *pieces)
 
 
 def gather(piece, axis, size):
@@ -305,8 +289,9 @@
     master_next = master - outer_rate * (average + outer_beta * momentum_next)
     pieces = gather(master_next.astype(jnp.bfloat16), "replica", groups)
 
-    total, last = accumulate(mine, columns, cotangents[:-1])
-    layer_next = finish(last, cotangents[-1], total, base_of(own, weight, pieces), (1.0 - mix_weight) * inner_rate)
+    rate = (1.0 - mix_weight) * inner_rate
+    total, last = accumulate(mine, columns, cotangents[:-1], weight, rate)
+    layer_next = finish(own, last, cotangents[-1], total, pieces, rate)
     return (layer_next[None], master_next, momentum_next)
 
 

time: 92.3 us -> 87.1 us (0.944)
  local copies, waits for them, and re-layouts: 12.4 us -> 5.85 us
  Pallas kernels: 12.5 us -> 13.9 us
  starting transfers between devices: 20 us -> 21.1 us
    unnamed x28 -> x18, local copies, waits for them, and re-layouts: 12.4 us -> 5.79 us
    pallas_call x3 -> x2, Pallas kernels: 6.79 us -> 7.96 us  [the longest x1 4.6 us: accumulate(): pl.pallas_call(functools.partial(accumulate_kernel, parts, rate), out_sha...]
    ppermute x12, starting transfers between devices: 14.4 us -> 15.5 us  [swap(): return lax.ppermute(value, axis, [(i, i ^ mask) for i in range(size)])]
    ppermute x12, waiting for transfers between devices: 43.4 us -> 42.5 us  [swap(): return lax.ppermute(value, axis, [(i, i ^ mask) for i in range(size)])]
  transfers between devices with their start and end apart: 13 -> 13, of which waited for: 6 -> 8; matrix products, arithmetic and copies ran while one was open for 3% -> 3% of each run, Pallas kernels for 12% -> 12%
where the time goes in v15:
time: 87.1 us; the launch traced here: 86.7 us
  waiting for transfers between devices  42.5 us (49%)
  starting transfers between devices  21.1 us (24%)
  Pallas kernels  13.9 us (16%)
  local copies, waits for them, and re-layouts  5.85 us (7%)
  other arithmetic  2.6 us (3%)
    ppermute x12, waiting for transfers between devices, swap(): return lax.ppermute(value, axis, [(i, i ^ mask) for i in range(size)])  42.5 us
    ppermute x12, starting transfers between devices, swap(): return lax.ppermute(value, axis, [(i, i ^ mask) for i in range(size)])  15.5 us
    unnamed x18, local copies, waits for them, and re-layouts  5.79 us
    all_to_all x1, starting transfers between devices, on_device(): lax.all_to_all(blocks, 'fsdp', split_axis=0, concat_axis=0, tiled=True)  5.61 us
    pallas_call x1, Pallas kernels, accumulate(): pl.pallas_call(functools.partial(accumulate_kernel, parts, rate), out_sha...  4.6 us
    pallas_call x1, Pallas kernels, code_and_decode(): pl.pallas_call(code_kernel, out_shape=(half, half), in_specs=[pl.BlockSpe...  3.69 us
    pallas_call x1, Pallas kernels, finish(): pl.pallas_call(functools.partial(finish_kernel, groups, rate), out_shape=...  3.36 us
    pallas_call x1, Pallas kernels, prepare(): pl.pallas_call(prepare_kernel, out_shape=jax.ShapeDtypeStruct((shards, ro...  2.21 us
  transfers between devices with their start and end apart: 13, of which 8 were waited for; matrix products, arithmetic and copies ran while one was open for 3% of the time, Pallas kernels for 12%

profile of v15, /device:TPU:0, one launch (start us, length us, event | category | flops | bytes accessed | tf_op | source)
XLA Modules:
  0.0 86.7 jit_solution(14147254688260651527)
XLA Ops:
  0.6 4.1 %collective-permute-start.2 = (bf16[128,1024]{1,0:T(8,128)(2,1)}, bf16[128,1024]{1,0:T(8,128)(2,1)}, u32[]{:S(2)}, u32[]{:S(2)}) collective-permute-start(bf16[128,1024]{1,0:T(8,128)(2,1)} %bitcast.19), channel_id=1, source_target_pairs={{0,4},{1,5},{2,6},{3,7},{4,0},{5,1},{6,2},{7,3},{8,12},{9,13},{10,... | collective-permute-start | bytes 786440 | tf_op jit(solution)/shard_map/ppermute | solution.py:24
  4.7 1.6 %collective-permute-start.1 = (bf16[128,1024]{1,0:T(8,128)(2,1)}, bf16[128,1024]{1,0:T(8,128)(2,1)}, u32[]{:S(2)}, u32[]{:S(2)}) collective-permute-start(bf16[128,1024]{1,0:T(8,128)(2,1)} %bitcast.20), channel_id=1, source_target_pairs={{0,2},{1,3},{2,0},{3,1},{4,6},{5,7},{6,4},{7,5},{8,10},{9,11},{10,... | collective-permute-start | bytes 786440 | tf_op jit(solution)/shard_map/ppermute | solution.py:24
  6.3 1.5 %collective-permute-start = (bf16[128,1024]{1,0:T(8,128)(2,1)}, bf16[128,1024]{1,0:T(8,128)(2,1)S(1)}, u32[]{:S(2)}, u32[]{:S(2)}) collective-permute-start(bf16[128,1024]{1,0:T(8,128)(2,1)} %bitcast.21), channel_id=1, source_target_pairs={{0,1},{1,0},{2,3},{3,2},{4,5},{5,4},{6,7},{7,6},{8,9},{9,8},{10,11... | collective-permute-start | bytes 786440 | tf_op jit(solution)/shard_map/ppermute | solution.py:24
  7.8 0.7 reshape.24
  8.6 1.6 %copy-done = bf16[1,128,8192]{2,1,0:T(8,128)(2,1)S(1)} copy-done((bf16[1,128,8192]{2,1,0:T(8,128)(2,1)S(1)}, bf16[1,128,8192]{2,1,0:T(8,128)(2,1)}, u32[]{:S(2)}) %copy-start) | copy-done | bytes 2097176
  10.1 2.2 %prepare.1 = bf16[8,1024,128]{2,1,0:T(8,128)(2,1)} custom-call(bf16[128,8192]{1,0:T(8,128)(2,1)S(1)} %bitcast.15, f32[1,8192]{1,0:T(1,128)S(1)} %bitcast.18), custom_call_target="tpu_custom_call" | custom-call | flops 5242880 | bytes 4194304 | tf_op jit(solution)/shard_map/prepare/pallas_call | solution.py:58
  12.4 4.7 %collective-permute-done.2.refs_4_ = bf16[128,1024]{1,0:T(8,128)(2,1)} collective-permute-done((bf16[128,1024]{1,0:T(8,128)(2,1)}, bf16[128,1024]{1,0:T(8,128)(2,1)}, u32[]{:S(2)}, u32[]{:S(2)}) %collective-permute-start.2) | collective-permute-done | bytes 262176 | tf_op jit(solution)/shard_map/ppermute | solution.py:24
  17.1 0.2 collective-permute-done.1.refs_2_
  17.3 0.7 copy-done.5
  18.0 5.6 %all-to-all-start = ((bf16[8,1024,128]{2,1,0:T(8,128)(2,1)}), bf16[8,1024,128]{2,1,0:T(8,128)(2,1)}, u32[]{:S(2)}, u32[]{:S(2)}) async-start(bf16[8,1024,128]{2,1,0:T(8,128)(2,1)} %prepare.1), calls=%async_computation | async-start | bytes 4194304 | tf_op jit(solution)/shard_map/all_to_all | solution.py:278
  23.6 1.6 %copy-done.2 = bf16[1,1024,1024]{2,1,0:T(8,128)(2,1)S(1)} copy-done((bf16[1,1024,1024]{2,1,0:T(8,128)(2,1)S(1)}, bf16[1,1024,1024]{2,1,0:T(8,128)(2,1)}, u32[]{:S(2)}) %copy-start.2) | copy-done | bytes 2097176
  25.2 3.7 %code_and_decode.1 = (bf16[2,1024,256]{2,1,0:T(8,128)(2,1)S(1)}, bf16[2,1024,256]{2,1,0:T(8,128)(2,1)S(1)}) custom-call(s32[1]{0:T(128)} %bitcast.own_ref, bf16[1024,1024]{1,0:T(8,128)(2,1)S(1)} %copy-done.1, bf16[1024,1024]{1,0:T(8,128)(2,1)S(1)} %bitcast.16), custom_call_target="tpu_custom_call" | custom-call | flops 20971520 | bytes 6291456 | tf_op jit(solution)/shard_map/code_and_decode/pallas_call | solution.py:128
  28.9 0.1 collective-permute-start.7
  29.0 2.6 %collective-permute-done.7 = bf16[2,1024,256]{2,1,0:T(8,128)(2,1)S(1)} collective-permute-done((bf16[2,1024,256]{2,1,0:T(8,128)(2,1)S(1)}, bf16[2,1024,256]{2,1,0:T(8,128)(2,1)S(1)}, u32[]{:S(2)}, u32[]{:S(2)}) %collective-permute-start.7) | collective-permute-done | bytes 1048608 | tf_op jit(solution)/shard_map/ppermute | solution.py:24
  31.6 0.2 convert_add_fusion
  31.8 0.1 slice.23
  31.9 1.6 %collective-permute-start.8 = (bf16[1,1024,256]{2,1,0:T(8,128)(2,1)S(1)}, bf16[1,1024,256]{2,1,0:T(8,128)(2,1)S(1)}, u32[]{:S(2)}, u32[]{:S(2)}) collective-permute-start(bf16[1,1024,256]{2,1,0:T(8,128)(2,1)S(1)} %slice.23), channel_id=1, source_target_pairs={{0,16},{8,24},{16,0},{24,8},{1,17},{9,25},{17,1},{25,9},{2,18},{10... | collective-permute-start | bytes 1572872 | tf_op jit(solution)/shard_map/ppermute | solution.py:24
  33.5 12.5 %collective-permute-done.8 = bf16[1,1024,256]{2,1,0:T(8,128)(2,1)S(1)} collective-permute-done((bf16[1,1024,256]{2,1,0:T(8,128)(2,1)S(1)}, bf16[1,1024,256]{2,1,0:T(8,128)(2,1)S(1)}, u32[]{:S(2)}, u32[]{:S(2)}) %collective-permute-start.8) | collective-permute-done | bytes 524320 | tf_op jit(solution)/shard_map/ppermute | solution.py:24
  46.0 1.7 %fusion.2 = (bf16[1024,256]{1,0:T(8,128)(2,1)S(1)}, f32[1024,256]{1,0:T(8,128)}, f32[1024,256]{1,0:T(8,128)}) fusion(f32[1024,256]{1,0:T(8,128)S(1)} %copy-done.7, bf16[1,1024,256]{2,1,0:T(8,128)(2,1)S(1)} %collective-permute-done.8, f32[2,1024,256]{2,1,0:T(8,128)S(1)} %convert_add_fusion, f32[1024,256]{1,0:T(8,128)S(1)} %copy-done.8), kind=kLoop, calls=%fused_computation.7 | loop fusion | flops 2621440 | bytes 6291456 | tf_op jit(solution)/shard_map/convert_element_type | solution.py:290
  47.6 1.5 %collective-permute-start.10 = (bf16[1024,256]{1,0:T(8,128)(2,1)S(1)}, bf16[1024,256]{1,0:T(8,128)(2,1)S(1)}, u32[]{:S(2)}, u32[]{:S(2)}) collective-permute-start(bf16[1024,256]{1,0:T(8,128)(2,1)S(1)} %get-tuple-element.17.refs_0_), channel_id=1, source_target_pairs={{0,16},{8,24},{16,0},{24,8},{1,17},{9,25},{17,1},{25,9},{2,18},{10... | collective-permute-start | bytes 1572872 | tf_op jit(solution)/shard_map/ppermute | solution.py:24
  49.1 2.0 %collective-permute-start.5 = (bf16[128,1024]{1,0:T(8,128)(2,1)}, bf16[128,1024]{1,0:T(8,128)(2,1)}, u32[]{:S(2)}, u32[]{:S(2)}) collective-permute-start(bf16[128,1024]{1,0:T(8,128)(2,1)} %collective-permute-done.2.refs_4_), channel_id=1, source_target_pairs={{0,2},{1,3},{2,0},{3,1},{4,6},{5,7},{6,4},{7,5},{8,10},{9,11},{10,... | collective-permute-start | bytes 786440 | tf_op jit(solution)/shard_map/ppermute | solution.py:24
  51.1 9.7 %collective-permute-done.10.refs_2_ = bf16[1024,256]{1,0:T(8,128)(2,1)S(1)} collective-permute-done((bf16[1024,256]{1,0:T(8,128)(2,1)S(1)}, bf16[1024,256]{1,0:T(8,128)(2,1)S(1)}, u32[]{:S(2)}, u32[]{:S(2)}) %collective-permute-start.10) | collective-permute-done | bytes 524320 | tf_op jit(solution)/shard_map/ppermute | solution.py:24
  60.9 2.0 %collective-permute-start.4 = (bf16[128,1024]{1,0:T(8,128)(2,1)}, bf16[128,1024]{1,0:T(8,128)(2,1)}, u32[]{:S(2)}, u32[]{:S(2)}) collective-permute-start(bf16[128,1024]{1,0:T(8,128)(2,1)} %collective-permute-done.2.refs_4_), channel_id=1, source_target_pairs={{0,1},{1,0},{2,3},{3,2},{4,5},{5,4},{6,7},{7,6},{8,9},{9,8},{10,11... | collective-permute-start | bytes 786440 | tf_op jit(solution)/shard_map/ppermute | solution.py:24
  62.9 0.0 collective-permute-start.3
  62.9 1.6 %collective-permute-done.5.refs_6_ = bf16[128,1024]{1,0:T(8,128)(2,1)} collective-permute-done((bf16[128,1024]{1,0:T(8,128)(2,1)}, bf16[128,1024]{1,0:T(8,128)(2,1)}, u32[]{:S(2)}, u32[]{:S(2)}) %collective-permute-start.5) | collective-permute-done | bytes 262176 | tf_op jit(solution)/shard_map/ppermute | solution.py:24
  64.6 1.1 %collective-permute-start.6 = (bf16[128,1024]{1,0:T(8,128)(2,1)}, bf16[128,1024]{1,0:T(8,128)(2,1)S(1)}, u32[]{:S(2)}, u32[]{:S(2)}) collective-permute-start(bf16[128,1024]{1,0:T(8,128)(2,1)} %collective-permute-done.5.refs_6_), channel_id=1, source_target_pairs={{0,1},{1,0},{2,3},{3,2},{4,5},{5,4},{6,7},{7,6},{8,9},{9,8},{10,11... | collective-permute-start | bytes 786440 | tf_op jit(solution)/shard_map/ppermute | solution.py:24
  65.7 5.4 %collective-permute-done.4.refs_5_ = bf16[128,1024]{1,0:T(8,128)(2,1)} collective-permute-done((bf16[128,1024]{1,0:T(8,128)(2,1)}, bf16[128,1024]{1,0:T(8,128)(2,1)}, u32[]{:S(2)}, u32[]{:S(2)}) %collective-permute-start.4) | collective-permute-done | bytes 262176 | tf_op jit(solution)/shard_map/ppermute | solution.py:24
  71.1 5.6 %collective-permute-done.3.refs_3_ = bf16[128,1024]{1,0:T(8,128)(2,1)} collective-permute-done((bf16[128,1024]{1,0:T(8,128)(2,1)}, bf16[128,1024]{1,0:T(8,128)(2,1)}, u32[]{:S(2)}, u32[]{:S(2)}) %collective-permute-start.3) | collective-permute-done | bytes 262176 | tf_op jit(solution)/shard_map/ppermute | solution.py:24
  76.8 0.9 %copy-done.4 = bf16[1,128,1024]{2,1,0:T(8,128)(2,1)S(1)} copy-done((bf16[1,128,1024]{2,1,0:T(8,128)(2,1)S(1)}, bf16[1,128,1024]{2,1,0:T(8,128)(2,1)}, u32[]{:S(2)}) %copy-start.4) | copy-done | bytes 262168
  77.7 0.9 %copy-done.6 = bf16[128,1024]{1,0:T(8,128)(2,1)S(1)} copy-done((bf16[128,1024]{1,0:T(8,128)(2,1)S(1)}, bf16[128,1024]{1,0:T(8,128)(2,1)}, u32[]{:S(2)}) %copy-start.6) | copy-done | bytes 262168
  78.7 4.6 %accumulate.1 = (f32[1024,1024]{1,0:T(8,128)S(1)}, bf16[1024,128]{1,0:T(8,128)(2,1)S(1)}) custom-call(s32[1]{0:T(128)} %bitcast.1.mine_ref, bf16[8,1024,128]{2,1,0:T(8,128)(2,1)} %all-to-all-done.tokens_ref, bf16[1024,1024]{1,0:T(8,128)(2,1)S(1)} %bitcast.17, bf16[128,1024]{1,0:T(8,128)(2,1)S(1)} %bitcast.22, bf16[128,1024]{1,0:T(8,128)(2,1)S(1)} %copy-done.6, ...), custom_call_target="tpu_custom_call" | custom-call | flops 1879048192 | bytes 8388608 | tf_op jit(solution)/shard_map/accumulate/pallas_call | solution.py:184
  83.3 3.4 %finish.1 = bf16[1024,1024]{1,0:T(8,128)(2,1)} custom-call(s32[1]{0:T(128)} %bitcast.own_ref, bf16[1024,128]{1,0:T(8,128)(2,1)S(1)} %get-tuple-element.11.tokens_ref, bf16[128,1024]{1,0:T(8,128)(2,1)S(1)} %collective-permute-done.6.cotangent_ref, f32[1024,1024]{1,0:T(8,128)S(1)} %get-tuple-element.12.total_ref, ...), custom_call_target="tpu_custom_call" | custom-call | flops 268435456 | bytes 8912896 | tf_op jit(solution)/shard_map/finish/pallas_call | solution.py:235
  (20 shorter events, 0.0 us)
Async XLA Ops:
  0.6 16.5 %collective-permute-start.2 = (bf16[128,1024]{1,0:T(8,128)(2,1)}, bf16[128,1024]{1,0:T(8,128)(2,1)}, u32[]{:S(2)}, u32[]{:S(2)}) collective-permute-start(bf16[128,1024]{1,0:T(8,128)(2,1)} %bitcast.19), channel_id=1, source_target_pairs={{0,4},{1,5},{2,6},{3,7},{4,0},{5,1},{6,2},{7,3},{8,12},{9,13},{10,... | collective-permute-start | bytes 786440 | tf_op jit(solution)/shard_map/ppermute | solution.py:24
  4.7 12.5 %collective-permute-start.1 = (bf16[128,1024]{1,0:T(8,128)(2,1)}, bf16[128,1024]{1,0:T(8,128)(2,1)}, u32[]{:S(2)}, u32[]{:S(2)}) collective-permute-start(bf16[128,1024]{1,0:T(8,128)(2,1)} %bitcast.20), channel_id=1, source_target_pairs={{0,2},{1,3},{2,0},{3,1},{4,6},{5,7},{6,4},{7,5},{8,10},{9,11},{10,... | collective-permute-start | bytes 786440 | tf_op jit(solution)/shard_map/ppermute | solution.py:24
  6.3 11.0 %collective-permute-start = (bf16[128,1024]{1,0:T(8,128)(2,1)}, bf16[128,1024]{1,0:T(8,128)(2,1)S(1)}, u32[]{:S(2)}, u32[]{:S(2)}) collective-permute-start(bf16[128,1024]{1,0:T(8,128)(2,1)} %bitcast.21), channel_id=1, source_target_pairs={{0,1},{1,0},{2,3},{3,2},{4,5},{5,4},{6,7},{7,6},{8,9},{9,8},{10,11... | collective-permute-start | bytes 786440 | tf_op jit(solution)/shard_map/ppermute | solution.py:24
  8.5 1.6 %copy-start = (bf16[1,128,8192]{2,1,0:T(8,128)(2,1)S(1)}, bf16[1,128,8192]{2,1,0:T(8,128)(2,1)}, u32[]{:S(2)}) copy-start(bf16[1,128,8192]{2,1,0:T(8,128)(2,1)} %param.7) | copy-start | bytes 6291460
  17.3 0.7 copy-start.5
  18.0 5.6 %copy-start.1 = (bf16[1024,1024]{1,0:T(8,128)(2,1)S(1)}, bf16[1024,1024]{1,0:T(8,128)(2,1)}, u32[]{:S(2)}) copy-start(bf16[1024,1024]{1,0:T(8,128)(2,1)} %shared_ref) | copy-start | bytes 6291460
  18.0 58.8 %all-to-all-start = ((bf16[8,1024,128]{2,1,0:T(8,128)(2,1)}), bf16[8,1024,128]{2,1,0:T(8,128)(2,1)}, u32[]{:S(2)}, u32[]{:S(2)}) async-start(bf16[8,1024,128]{2,1,0:T(8,128)(2,1)} %prepare.1), calls=%async_computation | async-start | bytes 4194304 | tf_op jit(solution)/shard_map/all_to_all | solution.py:278
  23.6 1.6 %copy-start.2 = (bf16[1,1024,1024]{2,1,0:T(8,128)(2,1)S(1)}, bf16[1,1024,1024]{2,1,0:T(8,128)(2,1)}, u32[]{:S(2)}) copy-start(bf16[1,1024,1024]{2,1,0:T(8,128)(2,1)} %param.10) | copy-start | bytes 6291460
  28.9 2.7 %collective-permute-start.7 = (bf16[2,1024,256]{2,1,0:T(8,128)(2,1)S(1)}, bf16[2,1024,256]{2,1,0:T(8,128)(2,1)S(1)}, u32[]{:S(2)}, u32[]{:S(2)}) collective-permute-start(bf16[2,1024,256]{2,1,0:T(8,128)(2,1)S(1)} %get-tuple-element.16), channel_id=1, source_target_pairs={{0,8},{8,0},{16,24},{24,16},{1,9},{9,1},{17,25},{25,17},{2,10},{10... | collective-permute-start | bytes 3145736 | tf_op jit(solution)/shard_map/ppermute | solution.py:24
  31.6 14.3 %copy-start.7 = (f32[1024,256]{1,0:T(8,128)S(1)}, f32[1024,256]{1,0:T(8,128)}, u32[]{:S(2)}) copy-start(f32[1024,256]{1,0:T(8,128)} %param.12) | copy-start | bytes 3145732
  31.6 14.3 %copy-start.8 = (f32[1024,256]{1,0:T(8,128)S(1)}, f32[1024,256]{1,0:T(8,128)}, u32[]{:S(2)}) copy-start(f32[1024,256]{1,0:T(8,128)} %param.13) | copy-start | bytes 3145732
  31.9 44.8 %copy-start.3 = (bf16[1,1024,1024]{2,1,0:T(8,128)(2,1)S(1)}, bf16[1,1024,1024]{2,1,0:T(8,128)(2,1)}, u32[]{:S(2)}) copy-start(bf16[1,1024,1024]{2,1,0:T(8,128)(2,1)} %param.10) | copy-start | bytes 6291460
  31.9 14.0 %collective-permute-start.8 = (bf16[1,1024,256]{2,1,0:T(8,128)(2,1)S(1)}, bf16[1,1024,256]{2,1,0:T(8,128)(2,1)S(1)}, u32[]{:S(2)}, u32[]{:S(2)}) collective-permute-start(bf16[1,1024,256]{2,1,0:T(8,128)(2,1)S(1)} %slice.23), channel_id=1, source_target_pairs={{0,16},{8,24},{16,0},{24,8},{1,17},{9,25},{17,1},{25,9},{2,18},{10... | collective-permute-start | bytes 1572872 | tf_op jit(solution)/shard_map/ppermute | solution.py:24
  47.6 13.2 %collective-permute-start.10 = (bf16[1024,256]{1,0:T(8,128)(2,1)S(1)}, bf16[1024,256]{1,0:T(8,128)(2,1)S(1)}, u32[]{:S(2)}, u32[]{:S(2)}) collective-permute-start(bf16[1024,256]{1,0:T(8,128)(2,1)S(1)} %get-tuple-element.17.refs_0_), channel_id=1, source_target_pairs={{0,16},{8,24},{16,0},{24,8},{1,17},{9,25},{17,1},{25,9},{2,18},{10... | collective-permute-start | bytes 1572872 | tf_op jit(solution)/shard_map/ppermute | solution.py:24
  49.1 15.5 %collective-permute-start.5 = (bf16[128,1024]{1,0:T(8,128)(2,1)}, bf16[128,1024]{1,0:T(8,128)(2,1)}, u32[]{:S(2)}, u32[]{:S(2)}) collective-permute-start(bf16[128,1024]{1,0:T(8,128)(2,1)} %collective-permute-done.2.refs_4_), channel_id=1, source_target_pairs={{0,2},{1,3},{2,0},{3,1},{4,6},{5,7},{6,4},{7,5},{8,10},{9,11},{10,... | collective-permute-start | bytes 786440 | tf_op jit(solution)/shard_map/ppermute | solution.py:24
  51.1 32.2 %collective-permute-start.9 = (bf16[1024,256]{1,0:T(8,128)(2,1)S(1)}, bf16[1024,256]{1,0:T(8,128)(2,1)}, u32[]{:S(2)}, u32[]{:S(2)}) collective-permute-start(bf16[1024,256]{1,0:T(8,128)(2,1)S(1)} %get-tuple-element.17.refs_0_), channel_id=1, source_target_pairs={{0,8},{8,0},{16,24},{24,16},{1,9},{9,1},{17,25},{25,17},{2,10},{10... | collective-permute-start | bytes 1572872 | tf_op jit(solution)/shard_map/ppermute | solution.py:24
  60.9 22.4 %collective-permute-start.11 = (bf16[1024,256]{1,0:T(8,128)(2,1)S(1)}, bf16[1024,256]{1,0:T(8,128)(2,1)}, u32[]{:S(2)}, u32[]{:S(2)}) collective-permute-start(bf16[1024,256]{1,0:T(8,128)(2,1)S(1)} %collective-permute-done.10.refs_2_), channel_id=1, source_target_pairs={{0,8},{8,0},{16,24},{24,16},{1,9},{9,1},{17,25},{25,17},{2,10},{10... | collective-permute-start | bytes 1572872 | tf_op jit(solution)/shard_map/ppermute | solution.py:24
  60.9 10.3 %collective-permute-start.4 = (bf16[128,1024]{1,0:T(8,128)(2,1)}, bf16[128,1024]{1,0:T(8,128)(2,1)}, u32[]{:S(2)}, u32[]{:S(2)}) collective-permute-start(bf16[128,1024]{1,0:T(8,128)(2,1)} %collective-permute-done.2.refs_4_), channel_id=1, source_target_pairs={{0,1},{1,0},{2,3},{3,2},{4,5},{5,4},{6,7},{7,6},{8,9},{9,8},{10,11... | collective-permute-start | bytes 786440 | tf_op jit(solution)/shard_map/ppermute | solution.py:24
  62.9 13.9 %collective-permute-start.3 = (bf16[128,1024]{1,0:T(8,128)(2,1)}, bf16[128,1024]{1,0:T(8,128)(2,1)}, u32[]{:S(2)}, u32[]{:S(2)}) collective-permute-start(bf16[128,1024]{1,0:T(8,128)(2,1)} %collective-permute-done.1.refs_2_), channel_id=1, source_target_pairs={{0,1},{1,0},{2,3},{3,2},{4,5},{5,4},{6,7},{7,6},{8,9},{9,8},{10,11... | collective-permute-start | bytes 786440 | tf_op jit(solution)/shard_map/ppermute | solution.py:24
  64.6 18.7 %collective-permute-start.6 = (bf16[128,1024]{1,0:T(8,128)(2,1)}, bf16[128,1024]{1,0:T(8,128)(2,1)S(1)}, u32[]{:S(2)}, u32[]{:S(2)}) collective-permute-start(bf16[128,1024]{1,0:T(8,128)(2,1)} %collective-permute-done.5.refs_6_), channel_id=1, source_target_pairs={{0,1},{1,0},{2,3},{3,2},{4,5},{5,4},{6,7},{7,6},{8,9},{9,8},{10,11... | collective-permute-start | bytes 786440 | tf_op jit(solution)/shard_map/ppermute | solution.py:24
  76.7 1.0 %copy-start.4 = (bf16[1,128,1024]{2,1,0:T(8,128)(2,1)S(1)}, bf16[1,128,1024]{2,1,0:T(8,128)(2,1)}, u32[]{:S(2)}) copy-start(bf16[1,128,1024]{2,1,0:T(8,128)(2,1)} %param.9) | copy-start | bytes 786436
  77.7 0.9 %copy-start.6 = (bf16[128,1024]{1,0:T(8,128)(2,1)S(1)}, bf16[128,1024]{1,0:T(8,128)(2,1)}, u32[]{:S(2)}) copy-start(bf16[128,1024]{1,0:T(8,128)(2,1)} %copy-done.5) | copy-start | bytes 786436

commit v16 on v15

--- a/solution.py
+++ b/solution.py
@@ -209,21 +209,35 @@
     piece_refs, (out_ref, pieces, outs, sems) = refs[:groups], refs[groups:]
     share = pieces.shape[2]
     steps, _, tile = outs.shape
-    for k, ref in enumerate(piece_refs):
-        pieces[own_ref[0] ^ k] = ref[...]
-    stores = []
+    own = own_ref[0]
+
+    def store(step, columns):
+        return pltpu.make_async_copy(outs.at[step], out_ref.at[:, columns], sems.at[step])
+
+    def total_of(columns):
+        product = jnp.dot(tokens_ref[...], cotangent_ref[:, columns], preferred_element_type=jnp.float32)
+        return total_ref[:, columns] - rate * product
+
+    places = []
+    if share == tile:
+        for k, ref in enumerate(piece_refs):
+            places.append(pl.ds(pl.multiple_of((own ^ k) * share, share), share))
+            shared = ref[...].astype(jnp.float32)
+            outs[k] = (total_of(places[k]) + (1.0 - mix_weight) * shared).astype(jnp.bfloat16)
+            store(k, places[k]).start()
+    else:
+        for k, ref in enumerate(piece_refs):
+            pieces[own ^ k] = ref[...]
+        for step in range(steps):
+            places.append(pl.ds(step * tile, tile))
+            total = total_of(slice(step * tile, (step + 1) * tile))
+            for group in range(step * tile // share, (step + 1) * tile // share):
+                part = slice(group * share - step * tile, (group + 1) * share - step * tile)
+                shared = pieces[group].astype(jnp.float32)
+                outs[step, :, part] = (total[:, part] + (1.0 - mix_weight) * shared).astype(jnp.bfloat16)
+            store(step, places[step]).start()
     for step in range(steps):
-        columns = slice(step * tile, (step + 1) * tile)
-        product = jnp.dot(tokens_ref[...], cotangent_ref[:, columns], preferred_element_type=jnp.float32)
-        total = total_ref[:, columns] - rate * product
-        for group in range(step * tile // share, (step + 1) * tile // share):
-            part = slice(group * share - step * tile, (group + 1) * share - step * tile)
-            shared = pieces[group].astype(jnp.float32)
-            outs[step, :, part] = (total[:, part] + (1.0 - mix_weight) * shared).astype(jnp.bfloat16)
-        stores.append(pltpu.make_async_copy(outs.at[step], out_ref.at[:, pl.ds(step * tile, tile)], sems.at[step]))
-        stores[step].start()
-    for store in stores:
-        store.wait()
+        store(step, places[step]).wait()
 
 
 def finish(own, tokens, cotangent, total, pieces, rate):
@@ -250,12 +264,13 @@
     )(own.reshape(1), tokens, cotangent, total, *pieces)
 
 
-def gather(piece, axis, size):
+def gather(piece, axis, size, after=()):
     pieces = {0: piece}
     bit = size // 2
     while bit:
         for k in sorted(pieces):
-            pieces[k ^ bit] = swap(pieces[k], axis, bit)
+            value = lax.optimization_barrier((pieces[k], *after))[0] if k and bit == 1 else pieces[k]
+            pieces[k ^ bit] = swap(value, axis, bit)
         bit //= 2
     return [pieces[k] for k in range(size)]
 
@@ -287,7 +302,7 @@
     average = total[0] / groups
     momentum_next = outer_beta * momentum + average
     master_next = master - outer_rate * (average + outer_beta * momentum_next)
-    pieces = gather(master_next.astype(jnp.bfloat16), "replica", groups)
+    pieces = gather(master_next.astype(jnp.bfloat16), "replica", groups, after=cotangents[:-1])
 
     rate = (1.0 - mix_weight) * inner_rate
     total, last = accumulate(mine, columns, cotangents[:-1], weight, rate)

time: 87.1 us -> 84.2 us (0.967)
  waiting for transfers between devices: 42.5 us -> 35.2 us
  local copies, waits for them, and re-layouts: 5.85 us -> 11.8 us
  starting transfers between devices: 21.1 us -> 19.3 us
    ppermute x12, waiting for transfers between devices: 42.5 us -> 32.9 us  [swap(): return lax.ppermute(value, axis, [(i, i ^ mask) for i in range(size)])]
    unnamed x18 -> x36, local copies, waits for them, and re-layouts: 5.79 us -> 11.7 us
    all_to_all x1, waiting for transfers between devices: 0.01 us -> 2.37 us  [on_device(): lax.all_to_all(blocks, 'fsdp', split_axis=0, concat_axis=0, tiled=True)]
    all_to_all x1, starting transfers between devices: 5.61 us -> 4.47 us  [on_device(): lax.all_to_all(blocks, 'fsdp', split_axis=0, concat_axis=0, tiled=True)]
  transfers between devices with their start and end apart: 13 -> 13, of which waited for: 8 -> 7; matrix products, arithmetic and copies ran while one was open for 3% -> 3% of each run, Pallas kernels for 12% -> 13%
where the time goes in v16:
time: 84.2 us; the launch traced here: 83.5 us
  waiting for transfers between devices  35.2 us (42%)
  starting transfers between devices  19.3 us (23%)
  Pallas kernels  13.7 us (16%)
  local copies, waits for them, and re-layouts  11.8 us (14%)
  other arithmetic  2.65 us (3%)
    ppermute x12, waiting for transfers between devices, swap(): return lax.ppermute(value, axis, [(i, i ^ mask) for i in range(size)])  32.9 us
    ppermute x12, starting transfers between devices, swap(): return lax.ppermute(value, axis, [(i, i ^ mask) for i in range(size)])  14.8 us
    unnamed x36, local copies, waits for them, and re-layouts  11.7 us
    pallas_call x1, Pallas kernels, accumulate(): pl.pallas_call(functools.partial(accumulate_kernel, parts, rate), out_sha...  4.6 us
    all_to_all x1, starting transfers between devices, on_device(): lax.all_to_all(blocks, 'fsdp', split_axis=0, concat_axis=0, tiled=True)  4.47 us
    pallas_call x1, Pallas kernels, code_and_decode(): pl.pallas_call(code_kernel, out_shape=(half, half), in_specs=[pl.BlockSpe...  3.69 us
    pallas_call x1, Pallas kernels, finish(): pl.pallas_call(functools.partial(finish_kernel, groups, rate), out_shape=...  3.23 us
    all_to_all x1, waiting for transfers between devices, on_device(): lax.all_to_all(blocks, 'fsdp', split_axis=0, concat_axis=0, tiled=True)  2.37 us
  transfers between devices with their start and end apart: 13, of which 7 were waited for; matrix products, arithmetic and copies ran while one was open for 3% of the time, Pallas kernels for 13%

profile of v16, /device:TPU:0, one launch (start us, length us, event | category | flops | bytes accessed | tf_op | source)
XLA Modules:
  0.0 83.5 jit_solution(1323491009839972134)
XLA Ops:
  0.6 3.0 %collective-permute-start = (bf16[128,1024]{1,0:T(8,128)(2,1)}, bf16[128,1024]{1,0:T(8,128)(2,1)S(1)}, u32[]{:S(2)}, u32[]{:S(2)}) collective-permute-start(bf16[128,1024]{1,0:T(8,128)(2,1)} %bitcast.19), channel_id=1, source_target_pairs={{0,1},{1,0},{2,3},{3,2},{4,5},{5,4},{6,7},{7,6},{8,9},{9,8},{10,11... | collective-permute-start | bytes 786440 | tf_op jit(solution)/shard_map/ppermute | solution.py:24
  3.7 1.6 %collective-permute-start.1 = (bf16[128,1024]{1,0:T(8,128)(2,1)}, bf16[128,1024]{1,0:T(8,128)(2,1)S(1)}, u32[]{:S(2)}, u32[]{:S(2)}) collective-permute-start(bf16[128,1024]{1,0:T(8,128)(2,1)} %bitcast.20), channel_id=1, source_target_pairs={{0,2},{1,3},{2,0},{3,1},{4,6},{5,7},{6,4},{7,5},{8,10},{9,11},{10,... | collective-permute-start | bytes 786440 | tf_op jit(solution)/shard_map/ppermute | solution.py:24
  5.2 2.6 %collective-permute-start.2 = (bf16[128,1024]{1,0:T(8,128)(2,1)}, bf16[128,1024]{1,0:T(8,128)(2,1)S(1)}, u32[]{:S(2)}, u32[]{:S(2)}) collective-permute-start(bf16[128,1024]{1,0:T(8,128)(2,1)} %bitcast.21), channel_id=1, source_target_pairs={{0,4},{1,5},{2,6},{3,7},{4,0},{5,1},{6,2},{7,3},{8,12},{9,13},{10,... | collective-permute-start | bytes 786440 | tf_op jit(solution)/shard_map/ppermute | solution.py:24
  7.8 0.7 reshape.24
  8.6 1.6 %copy-done = bf16[1,128,8192]{2,1,0:T(8,128)(2,1)S(1)} copy-done((bf16[1,128,8192]{2,1,0:T(8,128)(2,1)S(1)}, bf16[1,128,8192]{2,1,0:T(8,128)(2,1)}, u32[]{:S(2)}) %copy-start) | copy-done | bytes 2097176
  10.1 2.2 %prepare.1 = bf16[8,1024,128]{2,1,0:T(8,128)(2,1)} custom-call(bf16[128,8192]{1,0:T(8,128)(2,1)S(1)} %bitcast.15, f32[1,8192]{1,0:T(1,128)S(1)} %bitcast.18), custom_call_target="tpu_custom_call" | custom-call | flops 5242880 | bytes 4194304 | tf_op jit(solution)/shard_map/prepare/pallas_call | solution.py:58
  12.4 0.7 copy-done.5
  13.1 4.0 %collective-permute-done.1.refs_2_ = bf16[128,1024]{1,0:T(8,128)(2,1)S(1)} collective-permute-done((bf16[128,1024]{1,0:T(8,128)(2,1)}, bf16[128,1024]{1,0:T(8,128)(2,1)S(1)}, u32[]{:S(2)}, u32[]{:S(2)}) %collective-permute-start.1) | collective-permute-done | bytes 262176 | tf_op jit(solution)/shard_map/ppermute | solution.py:24
  17.1 2.4 %collective-permute-done.2.refs_4_ = bf16[128,1024]{1,0:T(8,128)(2,1)S(1)} collective-permute-done((bf16[128,1024]{1,0:T(8,128)(2,1)}, bf16[128,1024]{1,0:T(8,128)(2,1)S(1)}, u32[]{:S(2)}, u32[]{:S(2)}) %collective-permute-start.2) | collective-permute-done | bytes 262176 | tf_op jit(solution)/shard_map/ppermute | solution.py:24
  19.5 0.7 copy-done.9
  20.2 4.5 %all-to-all-start = ((bf16[8,1024,128]{2,1,0:T(8,128)(2,1)}), bf16[8,1024,128]{2,1,0:T(8,128)(2,1)}, u32[]{:S(2)}, u32[]{:S(2)}) async-start(bf16[8,1024,128]{2,1,0:T(8,128)(2,1)} %prepare.1), calls=%async_computation | async-start | bytes 4194304 | tf_op jit(solution)/shard_map/all_to_all | solution.py:293
  24.7 1.6 %copy-done.2 = bf16[1,1024,1024]{2,1,0:T(8,128)(2,1)S(1)} copy-done((bf16[1,1024,1024]{2,1,0:T(8,128)(2,1)S(1)}, bf16[1,1024,1024]{2,1,0:T(8,128)(2,1)}, u32[]{:S(2)}) %copy-start.2) | copy-done | bytes 2097176
  26.3 3.7 %code_and_decode.1 = (bf16[2,1024,256]{2,1,0:T(8,128)(2,1)S(1)}, bf16[2,1024,256]{2,1,0:T(8,128)(2,1)S(1)}) custom-call(s32[1]{0:T(128)} %bitcast.own_ref, bf16[1024,1024]{1,0:T(8,128)(2,1)S(1)} %copy-done.1, bf16[1024,1024]{1,0:T(8,128)(2,1)S(1)} %bitcast.16), custom_call_target="tpu_custom_call" | custom-call | flops 20971520 | bytes 6291456 | tf_op jit(solution)/shard_map/code_and_decode/pallas_call | solution.py:128
  30.1 2.6 %collective-permute-done.7 = bf16[2,1024,256]{2,1,0:T(8,128)(2,1)S(1)} collective-permute-done((bf16[2,1024,256]{2,1,0:T(8,128)(2,1)S(1)}, bf16[2,1024,256]{2,1,0:T(8,128)(2,1)S(1)}, u32[]{:S(2)}, u32[]{:S(2)}) %collective-permute-start.7) | collective-permute-done | bytes 1048608 | tf_op jit(solution)/shard_map/ppermute | solution.py:24
  33.1 1.6 %collective-permute-start.8 = (bf16[1,1024,256]{2,1,0:T(8,128)(2,1)S(1)}, bf16[1,1024,256]{2,1,0:T(8,128)(2,1)S(1)}, u32[]{:S(2)}, u32[]{:S(2)}) collective-permute-start(bf16[1,1024,256]{2,1,0:T(8,128)(2,1)S(1)} %slice.23), channel_id=1, source_target_pairs={{0,16},{8,24},{16,0},{24,8},{1,17},{9,25},{17,1},{25,9},{2,18},{10... | collective-permute-start | bytes 1572872 | tf_op jit(solution)/shard_map/ppermute | solution.py:24
  34.6 12.5 %collective-permute-done.8 = bf16[1,1024,256]{2,1,0:T(8,128)(2,1)S(1)} collective-permute-done((bf16[1,1024,256]{2,1,0:T(8,128)(2,1)S(1)}, bf16[1,1024,256]{2,1,0:T(8,128)(2,1)S(1)}, u32[]{:S(2)}, u32[]{:S(2)}) %collective-permute-start.8) | collective-permute-done | bytes 524320 | tf_op jit(solution)/shard_map/ppermute | solution.py:24
  47.1 1.7 %fusion.2 = (bf16[1024,256]{1,0:T(8,128)(2,1)S(1)}, f32[1024,256]{1,0:T(8,128)}, f32[1024,256]{1,0:T(8,128)}) fusion(f32[1024,256]{1,0:T(8,128)S(1)} %copy-done.16, bf16[1,1024,256]{2,1,0:T(8,128)(2,1)S(1)} %collective-permute-done.8, f32[2,1024,256]{2,1,0:T(8,128)S(1)} %convert_add_fusion, f32[1024,256]{1,0:T(8,128)S(1)} %copy-done.17), kind=kLoop, calls=%fused_computation.7 | loop fusion | flops 2621440 | bytes 6291456 | tf_op jit(solution)/shard_map/convert_element_type | solution.py:305
  48.8 1.5 %collective-permute-start.10 = (bf16[1024,256]{1,0:T(8,128)(2,1)S(1)}, bf16[1024,256]{1,0:T(8,128)(2,1)S(1)}, u32[]{:S(2)}, u32[]{:S(2)}) collective-permute-start(bf16[1024,256]{1,0:T(8,128)(2,1)S(1)} %get-tuple-element.19.refs_0_), channel_id=1, source_target_pairs={{0,16},{8,24},{16,0},{24,8},{1,17},{9,25},{17,1},{25,9},{2,18},{10... | collective-permute-start | bytes 1572872 | tf_op jit(solution)/shard_map/ppermute | solution.py:24
  50.3 1.9 %collective-permute-start.3 = (bf16[128,1024]{1,0:T(8,128)(2,1)S(1)}, bf16[128,1024]{1,0:T(8,128)(2,1)S(1)}, u32[]{:S(2)}, u32[]{:S(2)}) collective-permute-start(bf16[128,1024]{1,0:T(8,128)(2,1)S(1)} %collective-permute-done.1.refs_2_), channel_id=1, source_target_pairs={{0,1},{1,0},{2,3},{3,2},{4,5},{5,4},{6,7},{7,6},{8,9},{9,8},{10,11... | collective-permute-start | bytes 786440 | tf_op jit(solution)/shard_map/ppermute | solution.py:24
  52.3 1.9 %collective-permute-start.5 = (bf16[128,1024]{1,0:T(8,128)(2,1)S(1)}, bf16[128,1024]{1,0:T(8,128)(2,1)}, u32[]{:S(2)}, u32[]{:S(2)}) collective-permute-start(bf16[128,1024]{1,0:T(8,128)(2,1)S(1)} %copy-done.10), channel_id=1, source_target_pairs={{0,2},{1,3},{2,0},{3,1},{4,6},{5,7},{6,4},{7,5},{8,10},{9,11},{10,... | collective-permute-start | bytes 786440 | tf_op jit(solution)/shard_map/ppermute | solution.py:24
  54.2 8.1 %collective-permute-done.3.refs_3_ = bf16[128,1024]{1,0:T(8,128)(2,1)S(1)} collective-permute-done((bf16[128,1024]{1,0:T(8,128)(2,1)S(1)}, bf16[128,1024]{1,0:T(8,128)(2,1)S(1)}, u32[]{:S(2)}, u32[]{:S(2)}) %collective-permute-start.3) | collective-permute-done | bytes 262176 | tf_op jit(solution)/shard_map/ppermute | solution.py:24
  63.0 3.2 %collective-permute-done.4.refs_5_ = bf16[128,1024]{1,0:T(8,128)(2,1)S(1)} collective-permute-done((bf16[128,1024]{1,0:T(8,128)(2,1)S(1)}, bf16[128,1024]{1,0:T(8,128)(2,1)S(1)}, u32[]{:S(2)}, u32[]{:S(2)}) %collective-permute-start.4) | collective-permute-done | bytes 262176 | tf_op jit(solution)/shard_map/ppermute | solution.py:24
  66.2 0.7 copy-done.14
  67.5 2.4 %all-to-all-done.tokens_ref = bf16[8,1024,128]{2,1,0:T(8,128)(2,1)} async-done(((bf16[8,1024,128]{2,1,0:T(8,128)(2,1)}), bf16[8,1024,128]{2,1,0:T(8,128)(2,1)}, u32[]{:S(2)}, u32[]{:S(2)}) %all-to-all-start) | async-done | bytes 2097184 | tf_op jit(solution)/shard_map/all_to_all | solution.py:293
  69.9 0.9 %copy-done.4 = bf16[1,128,1024]{2,1,0:T(8,128)(2,1)S(1)} copy-done((bf16[1,128,1024]{2,1,0:T(8,128)(2,1)S(1)}, bf16[1,128,1024]{2,1,0:T(8,128)(2,1)}, u32[]{:S(2)}) %copy-start.4) | copy-done | bytes 262168
  70.8 0.9 %copy-done.6 = bf16[128,1024]{1,0:T(8,128)(2,1)S(1)} copy-done((bf16[128,1024]{1,0:T(8,128)(2,1)S(1)}, bf16[128,1024]{1,0:T(8,128)(2,1)}, u32[]{:S(2)}) %copy-start.6) | copy-done | bytes 262168
  71.8 0.9 %copy-done.8 = bf16[128,1024]{1,0:T(8,128)(2,1)S(1)} copy-done((bf16[128,1024]{1,0:T(8,128)(2,1)S(1)}, bf16[128,1024]{1,0:T(8,128)(2,1)}, u32[]{:S(2)}) %copy-start.8) | copy-done | bytes 262168
  72.7 0.9 %copy-done.11 = bf16[128,1024]{1,0:T(8,128)(2,1)S(1)} copy-done((bf16[128,1024]{1,0:T(8,128)(2,1)S(1)}, bf16[128,1024]{1,0:T(8,128)(2,1)}, u32[]{:S(2)}) %copy-start.11) | copy-done | bytes 262168
  73.7 0.9 %copy-done.13 = bf16[128,1024]{1,0:T(8,128)(2,1)S(1)} copy-done((bf16[128,1024]{1,0:T(8,128)(2,1)S(1)}, bf16[128,1024]{1,0:T(8,128)(2,1)}, u32[]{:S(2)}) %copy-start.13) | copy-done | bytes 262168
  74.6 0.9 %copy-done.15 = bf16[128,1024]{1,0:T(8,128)(2,1)S(1)} copy-done((bf16[128,1024]{1,0:T(8,128)(2,1)S(1)}, bf16[128,1024]{1,0:T(8,128)(2,1)}, u32[]{:S(2)}) %copy-start.15) | copy-done | bytes 262168
  75.6 4.6 %accumulate.1 = (f32[1024,1024]{1,0:T(8,128)S(1)}, bf16[1024,128]{1,0:T(8,128)(2,1)S(1)}) custom-call(s32[1]{0:T(128)} %bitcast.1.mine_ref, bf16[8,1024,128]{2,1,0:T(8,128)(2,1)} %all-to-all-done.tokens_ref, bf16[1024,1024]{1,0:T(8,128)(2,1)S(1)} %bitcast.17, bf16[128,1024]{1,0:T(8,128)(2,1)S(1)} %bitcast.22, bf16[128,1024]{1,0:T(8,128)(2,1)S(1)} %copy-done.6, ...), custom_call_target="tpu_custom_call" | custom-call | flops 1879048192 | bytes 8388608 | tf_op jit(solution)/shard_map/accumulate/pallas_call | solution.py:184
  80.2 3.2 %finish.1 = bf16[1024,1024]{1,0:T(8,128)(2,1)} custom-call(s32[1]{0:T(128)} %bitcast.own_ref, bf16[1024,128]{1,0:T(8,128)(2,1)S(1)} %get-tuple-element.12.tokens_ref, bf16[128,1024]{1,0:T(8,128)(2,1)S(1)} %collective-permute-done.6.cotangent_ref, f32[1024,1024]{1,0:T(8,128)S(1)} %get-tuple-element.13.total_ref, ...), custom_call_target="tpu_custom_call" | custom-call | flops 268435456 | bytes 8912896 | tf_op jit(solution)/shard_map/finish/pallas_call | solution.py:249
  (38 shorter events, 1.9 us)
Async XLA Ops:
  0.6 11.7 %collective-permute-start = (bf16[128,1024]{1,0:T(8,128)(2,1)}, bf16[128,1024]{1,0:T(8,128)(2,1)S(1)}, u32[]{:S(2)}, u32[]{:S(2)}) collective-permute-start(bf16[128,1024]{1,0:T(8,128)(2,1)} %bitcast.19), channel_id=1, source_target_pairs={{0,1},{1,0},{2,3},{3,2},{4,5},{5,4},{6,7},{7,6},{8,9},{9,8},{10,11... | collective-permute-start | bytes 786440 | tf_op jit(solution)/shard_map/ppermute | solution.py:24
  3.7 13.5 %collective-permute-start.1 = (bf16[128,1024]{1,0:T(8,128)(2,1)}, bf16[128,1024]{1,0:T(8,128)(2,1)S(1)}, u32[]{:S(2)}, u32[]{:S(2)}) collective-permute-start(bf16[128,1024]{1,0:T(8,128)(2,1)} %bitcast.20), channel_id=1, source_target_pairs={{0,2},{1,3},{2,0},{3,1},{4,6},{5,7},{6,4},{7,5},{8,10},{9,11},{10,... | collective-permute-start | bytes 786440 | tf_op jit(solution)/shard_map/ppermute | solution.py:24
  5.2 14.3 %collective-permute-start.2 = (bf16[128,1024]{1,0:T(8,128)(2,1)}, bf16[128,1024]{1,0:T(8,128)(2,1)S(1)}, u32[]{:S(2)}, u32[]{:S(2)}) collective-permute-start(bf16[128,1024]{1,0:T(8,128)(2,1)} %bitcast.21), channel_id=1, source_target_pairs={{0,4},{1,5},{2,6},{3,7},{4,0},{5,1},{6,2},{7,3},{8,12},{9,13},{10,... | collective-permute-start | bytes 786440 | tf_op jit(solution)/shard_map/ppermute | solution.py:24
  8.5 1.6 %copy-start = (bf16[1,128,8192]{2,1,0:T(8,128)(2,1)S(1)}, bf16[1,128,8192]{2,1,0:T(8,128)(2,1)}, u32[]{:S(2)}) copy-start(bf16[1,128,8192]{2,1,0:T(8,128)(2,1)} %param.7) | copy-start | bytes 6291460
  12.4 0.7 copy-start.5
  17.1 33.2 %copy-start.7 = (bf16[128,1024]{1,0:T(8,128)(2,1)}, bf16[128,1024]{1,0:T(8,128)(2,1)S(1)}, u32[]{:S(2)}) copy-start(bf16[128,1024]{1,0:T(8,128)(2,1)S(1)} %collective-permute-done.1.refs_2_) | copy-start | bytes 786436
  19.5 0.7 copy-start.9
  20.2 4.5 %copy-start.1 = (bf16[1024,1024]{1,0:T(8,128)(2,1)S(1)}, bf16[1024,1024]{1,0:T(8,128)(2,1)}, u32[]{:S(2)}) copy-start(bf16[1024,1024]{1,0:T(8,128)(2,1)} %shared_ref) | copy-start | bytes 6291460
  20.2 49.7 %all-to-all-start = ((bf16[8,1024,128]{2,1,0:T(8,128)(2,1)}), bf16[8,1024,128]{2,1,0:T(8,128)(2,1)}, u32[]{:S(2)}, u32[]{:S(2)}) async-start(bf16[8,1024,128]{2,1,0:T(8,128)(2,1)} %prepare.1), calls=%async_computation | async-start | bytes 4194304 | tf_op jit(solution)/shard_map/all_to_all | solution.py:293
  24.7 1.6 %copy-start.2 = (bf16[1,1024,1024]{2,1,0:T(8,128)(2,1)S(1)}, bf16[1,1024,1024]{2,1,0:T(8,128)(2,1)}, u32[]{:S(2)}) copy-start(bf16[1,1024,1024]{2,1,0:T(8,128)(2,1)} %param.10) | copy-start | bytes 6291460
  30.0 2.7 %collective-permute-start.7 = (bf16[2,1024,256]{2,1,0:T(8,128)(2,1)S(1)}, bf16[2,1024,256]{2,1,0:T(8,128)(2,1)S(1)}, u32[]{:S(2)}, u32[]{:S(2)}) collective-permute-start(bf16[2,1024,256]{2,1,0:T(8,128)(2,1)S(1)} %get-tuple-element.17), channel_id=1, source_target_pairs={{0,8},{8,0},{16,24},{24,16},{1,9},{9,1},{17,25},{25,17},{2,10},{10... | collective-permute-start | bytes 3145736 | tf_op jit(solution)/shard_map/ppermute | solution.py:24
  32.7 14.4 %copy-start.16 = (f32[1024,256]{1,0:T(8,128)S(1)}, f32[1024,256]{1,0:T(8,128)}, u32[]{:S(2)}) copy-start(f32[1024,256]{1,0:T(8,128)} %param.12) | copy-start | bytes 3145732
  32.7 14.4 %copy-start.17 = (f32[1024,256]{1,0:T(8,128)S(1)}, f32[1024,256]{1,0:T(8,128)}, u32[]{:S(2)}) copy-start(f32[1024,256]{1,0:T(8,128)} %param.13) | copy-start | bytes 3145732
  33.0 19.1 %copy-start.10 = (bf16[128,1024]{1,0:T(8,128)(2,1)S(1)}, bf16[128,1024]{1,0:T(8,128)(2,1)}, u32[]{:S(2)}) copy-start(bf16[128,1024]{1,0:T(8,128)(2,1)} %copy-done.9) | copy-start | bytes 786436
  33.1 36.8 %copy-start.3 = (bf16[1,1024,1024]{2,1,0:T(8,128)(2,1)S(1)}, bf16[1,1024,1024]{2,1,0:T(8,128)(2,1)}, u32[]{:S(2)}) copy-start(bf16[1,1024,1024]{2,1,0:T(8,128)(2,1)} %param.10) | copy-start | bytes 6291460
  33.1 14.0 %collective-permute-start.8 = (bf16[1,1024,256]{2,1,0:T(8,128)(2,1)S(1)}, bf16[1,1024,256]{2,1,0:T(8,128)(2,1)S(1)}, u32[]{:S(2)}, u32[]{:S(2)}) collective-permute-start(bf16[1,1024,256]{2,1,0:T(8,128)(2,1)S(1)} %slice.23), channel_id=1, source_target_pairs={{0,16},{8,24},{16,0},{24,8},{1,17},{9,25},{17,1},{25,9},{2,18},{10... | collective-permute-start | bytes 1572872 | tf_op jit(solution)/shard_map/ppermute | solution.py:24
  48.8 18.1 %collective-permute-start.10 = (bf16[1024,256]{1,0:T(8,128)(2,1)S(1)}, bf16[1024,256]{1,0:T(8,128)(2,1)S(1)}, u32[]{:S(2)}, u32[]{:S(2)}) collective-permute-start(bf16[1024,256]{1,0:T(8,128)(2,1)S(1)} %get-tuple-element.19.refs_0_), channel_id=1, source_target_pairs={{0,16},{8,24},{16,0},{24,8},{1,17},{9,25},{17,1},{25,9},{2,18},{10... | collective-permute-start | bytes 1572872 | tf_op jit(solution)/shard_map/ppermute | solution.py:24
  50.3 12.0 %collective-permute-start.3 = (bf16[128,1024]{1,0:T(8,128)(2,1)S(1)}, bf16[128,1024]{1,0:T(8,128)(2,1)S(1)}, u32[]{:S(2)}, u32[]{:S(2)}) collective-permute-start(bf16[128,1024]{1,0:T(8,128)(2,1)S(1)} %collective-permute-done.1.refs_2_), channel_id=1, source_target_pairs={{0,1},{1,0},{2,3},{3,2},{4,5},{5,4},{6,7},{7,6},{8,9},{9,8},{10,11... | collective-permute-start | bytes 786440 | tf_op jit(solution)/shard_map/ppermute | solution.py:24
  52.2 14.0 %collective-permute-start.4 = (bf16[128,1024]{1,0:T(8,128)(2,1)S(1)}, bf16[128,1024]{1,0:T(8,128)(2,1)S(1)}, u32[]{:S(2)}, u32[]{:S(2)}) collective-permute-start(bf16[128,1024]{1,0:T(8,128)(2,1)S(1)} %copy-done.10), channel_id=1, source_target_pairs={{0,1},{1,0},{2,3},{3,2},{4,5},{5,4},{6,7},{7,6},{8,9},{9,8},{10,11... | collective-permute-start | bytes 786440 | tf_op jit(solution)/shard_map/ppermute | solution.py:24
  52.3 14.6 %collective-permute-start.5 = (bf16[128,1024]{1,0:T(8,128)(2,1)S(1)}, bf16[128,1024]{1,0:T(8,128)(2,1)}, u32[]{:S(2)}, u32[]{:S(2)}) collective-permute-start(bf16[128,1024]{1,0:T(8,128)(2,1)S(1)} %copy-done.10), channel_id=1, source_target_pairs={{0,2},{1,3},{2,0},{3,1},{4,6},{5,7},{6,4},{7,5},{8,10},{9,11},{10,... | collective-permute-start | bytes 786440 | tf_op jit(solution)/shard_map/ppermute | solution.py:24
  54.2 26.0 %collective-permute-start.9 = (bf16[1024,256]{1,0:T(8,128)(2,1)S(1)}, bf16[1024,256]{1,0:T(8,128)(2,1)}, u32[]{:S(2)}, u32[]{:S(2)}) collective-permute-start(bf16[1024,256]{1,0:T(8,128)(2,1)S(1)} %get-tuple-element.19.refs_0_), channel_id=1, source_target_pairs={{0,8},{8,0},{16,24},{24,16},{1,9},{9,1},{17,25},{25,17},{2,10},{10... | collective-permute-start | bytes 1572872 | tf_op jit(solution)/shard_map/ppermute | solution.py:24
  62.3 0.7 copy-start.12
  66.2 0.7 copy-start.14
  66.9 13.3 %collective-permute-start.11 = (bf16[1024,256]{1,0:T(8,128)(2,1)S(1)}, bf16[1024,256]{1,0:T(8,128)(2,1)}, u32[]{:S(2)}, u32[]{:S(2)}) collective-permute-start(bf16[1024,256]{1,0:T(8,128)(2,1)S(1)} %collective-permute-done.10.refs_2_), channel_id=1, source_target_pairs={{0,8},{8,0},{16,24},{24,16},{1,9},{9,1},{17,25},{25,17},{2,10},{10... | collective-permute-start | bytes 1572872 | tf_op jit(solution)/shard_map/ppermute | solution.py:24
  66.9 13.3 %collective-permute-start.6 = (bf16[128,1024]{1,0:T(8,128)(2,1)}, bf16[128,1024]{1,0:T(8,128)(2,1)S(1)}, u32[]{:S(2)}, u32[]{:S(2)}) collective-permute-start(bf16[128,1024]{1,0:T(8,128)(2,1)} %collective-permute-done.5.refs_6_), channel_id=1, source_target_pairs={{0,1},{1,0},{2,3},{3,2},{4,5},{5,4},{6,7},{7,6},{8,9},{9,8},{10,11... | collective-permute-start | bytes 786440 | tf_op jit(solution)/shard_map/ppermute | solution.py:24
  69.9 1.0 %copy-start.4 = (bf16[1,128,1024]{2,1,0:T(8,128)(2,1)S(1)}, bf16[1,128,1024]{2,1,0:T(8,128)(2,1)}, u32[]{:S(2)}) copy-start(bf16[1,128,1024]{2,1,0:T(8,128)(2,1)} %param.9) | copy-start | bytes 786436
  70.8 0.9 %copy-start.6 = (bf16[128,1024]{1,0:T(8,128)(2,1)S(1)}, bf16[128,1024]{1,0:T(8,128)(2,1)}, u32[]{:S(2)}) copy-start(bf16[128,1024]{1,0:T(8,128)(2,1)} %copy-done.5) | copy-start | bytes 786436
  71.8 0.9 %copy-start.8 = (bf16[128,1024]{1,0:T(8,128)(2,1)S(1)}, bf16[128,1024]{1,0:T(8,128)(2,1)}, u32[]{:S(2)}) copy-start(bf16[128,1024]{1,0:T(8,128)(2,1)} %copy-done.7) | copy-start | bytes 786436
  72.7 0.9 %copy-start.11 = (bf16[128,1024]{1,0:T(8,128)(2,1)S(1)}, bf16[128,1024]{1,0:T(8,128)(2,1)}, u32[]{:S(2)}) copy-start(bf16[128,1024]{1,0:T(8,128)(2,1)} %copy-done.9) | copy-start | bytes 786436
  73.7 0.9 %copy-start.13 = (bf16[128,1024]{1,0:T(8,128)(2,1)S(1)}, bf16[128,1024]{1,0:T(8,128)(2,1)}, u32[]{:S(2)}) copy-start(bf16[128,1024]{1,0:T(8,128)(2,1)} %copy-done.12) | copy-start | bytes 786436
  74.6 0.9 %copy-start.15 = (bf16[128,1024]{1,0:T(8,128)(2,1)S(1)}, bf16[128,1024]{1,0:T(8,128)(2,1)}, u32[]{:S(2)}) copy-start(bf16[128,1024]{1,0:T(8,128)(2,1)} %copy-done.14) | copy-start | bytes 786436

commit v17 on v15

--- a/solution.py
+++ b/solution.py
@@ -142,21 +142,26 @@
     )(own.reshape(1), shared, weight)
 
 
-def accumulate_kernel(parts, rate, mine_ref, tokens_ref, weight_ref, *refs):
+def accumulate_kernel(parts, groups, rate, place_ref, tokens_ref, weight_ref, *refs):
     cotangent_refs, refs = refs[:parts], refs[parts:]
-    total_ref, last_ref, tokens, cotangents, weight, token_sems, cotangent_sems, last_sem, weight_sem = refs
-    mine = mine_ref[0]
+    piece_refs, refs = refs[: groups - 1], refs[groups - 1 :]
+    total_ref, last_ref, tokens, cotangents, weight, pieces, token_sems, cotangent_sems, piece_sems, sems = refs
+    mine, own = place_ref[0], place_ref[1]
     depth, width = cotangent_refs[0].shape
-    tile = min(width, 256)
-
-    loads = []
+    share = pieces.shape[2]
+    tile = max(share, 256)
+
+    loads, rest = [], []
     for k, ref in enumerate(cotangent_refs):
         loads.append(pltpu.make_async_copy(tokens_ref.at[mine ^ k], tokens.at[k], token_sems.at[k]))
         loads.append(pltpu.make_async_copy(ref, cotangents.at[pl.ds(k * depth, depth)], cotangent_sems.at[k]))
-    loads.append(pltpu.make_async_copy(weight_ref, weight, weight_sem))
-    loads.append(pltpu.make_async_copy(tokens_ref.at[mine ^ parts], last_ref, last_sem))
-    for load in loads:
+    rest.append(pltpu.make_async_copy(weight_ref, weight, sems.at[0]))
+    for k, ref in enumerate(piece_refs):
+        rest.append(pltpu.make_async_copy(ref, pieces.at[own ^ k], piece_sems.at[k]))
+    rest.append(pltpu.make_async_copy(tokens_ref.at[mine ^ parts], last_ref, sems.at[1]))
+    for load in loads + rest:
         load.start()
+    pieces[own ^ (groups - 1)] = jnp.zeros(pieces.shape[1:], pieces.dtype)
     some = 2
     for first in range(0, parts, some):
         end = min(first + some, parts)
@@ -169,48 +174,54 @@
             total = jnp.dot(left, right, preferred_element_type=jnp.float32)
             if first:
                 total = total_ref[:, columns] + total
-            if end == parts:
-                if start == 0:
-                    loads[-2].wait()
-                total = mix_weight * weight[:, columns].astype(jnp.float32) - rate * total
-            total_ref[:, columns] = total
-    loads[-1].wait()
-
-
-def accumulate(mine, tokens, cotangents, weight, rate):
+            if end < parts:
+                total_ref[:, columns] = total
+                continue
+            if start == 0:
+                for load in rest:
+                    load.wait()
+            for group in range(start // share, (start + tile) // share):
+                place = slice(group * share, (group + 1) * share)
+                part = slice(group * share - start, (group + 1) * share - start)
+                mixed = mix_weight * weight[:, place].astype(jnp.float32)
+                mixed = mixed + (1.0 - mix_weight) * pieces[group].astype(jnp.float32)
+                total_ref[:, place] = mixed - rate * total[:, part]
+
+
+def accumulate(mine, own, tokens, cotangents, weight, pieces, rate):
     shards, rows, depth = tokens.shape
     parts = shards - 1
+    groups = len(pieces) + 1
     width = cotangents[0].shape[1]
     return pl.pallas_call(
-        functools.partial(accumulate_kernel, parts, rate),
+        functools.partial(accumulate_kernel, parts, groups, rate),
         out_shape=(jax.ShapeDtypeStruct((rows, width), jnp.float32), jax.ShapeDtypeStruct((rows, depth), jnp.bfloat16)),
-        in_specs=[pl.BlockSpec(memory_space=pltpu.SMEM)] + [pl.BlockSpec(memory_space=pltpu.HBM)] * (2 + parts),
+        in_specs=[pl.BlockSpec(memory_space=pltpu.SMEM)]
+        + [pl.BlockSpec(memory_space=pltpu.HBM)] * (1 + parts + groups),
         out_specs=(pl.BlockSpec(memory_space=pltpu.VMEM),) * 2,
         scratch_shapes=[
             pltpu.VMEM((parts, rows, depth), jnp.bfloat16),
             pltpu.VMEM((parts * depth, width), jnp.bfloat16),
             pltpu.VMEM((rows, width), jnp.bfloat16),
+            pltpu.VMEM((groups, rows, width // groups), jnp.bfloat16),
             pltpu.SemaphoreType.DMA((parts,)),
             pltpu.SemaphoreType.DMA((parts,)),
-            pltpu.SemaphoreType.DMA,
-            pltpu.SemaphoreType.DMA,
+            pltpu.SemaphoreType.DMA((groups,)),
+            pltpu.SemaphoreType.DMA((2,)),
         ],
-        compiler_params=pltpu.CompilerParams(vmem_limit_bytes=40 * 2**20),
+        compiler_params=pltpu.CompilerParams(vmem_limit_bytes=58 * 2**20),
         cost_estimate=pl.CostEstimate(
             flops=2 * depth * parts * rows * width,
-            bytes_accessed=2 * depth * shards * (rows + width) + 4 * rows * width,
+            bytes_accessed=2 * depth * shards * (rows + width) + 8 * rows * width,
             transcendentals=0,
         ),
         name="accumulate",
-    )(mine.reshape(1), tokens, weight, *cotangents)
-
-
-def finish_kernel(groups, rate, own_ref, tokens_ref, cotangent_ref, total_ref, *refs):
-    piece_refs, (out_ref, pieces, outs, sems) = refs[:groups], refs[groups:]
-    share = pieces.shape[2]
+    )(jnp.stack([mine, own]), tokens, weight, *cotangents, *pieces)
+
+
+def finish_kernel(groups, rate, own_ref, tokens_ref, cotangent_ref, total_ref, piece_ref, out_ref, outs, sems):
+    share = piece_ref.shape[1]
     steps, _, tile = outs.shape
-    for k, ref in enumerate(piece_refs):
-        pieces[own_ref[0] ^ k] = ref[...]
     stores = []
     for step in range(steps):
         columns = slice(step * tile, (step + 1) * tile)
@@ -218,44 +229,40 @@
         total = total_ref[:, columns] - rate * product
         for group in range(step * tile // share, (step + 1) * tile // share):
             part = slice(group * share - step * tile, (group + 1) * share - step * tile)
-            shared = pieces[group].astype(jnp.float32)
-            outs[step, :, part] = (total[:, part] + (1.0 - mix_weight) * shared).astype(jnp.bfloat16)
+            factor = jnp.where((own_ref[0] ^ (groups - 1)) == group, 1.0 - mix_weight, 0.0)
+            outs[step, :, part] = (total[:, part] + factor * piece_ref[...].astype(jnp.float32)).astype(jnp.bfloat16)
         stores.append(pltpu.make_async_copy(outs.at[step], out_ref.at[:, pl.ds(step * tile, tile)], sems.at[step]))
         stores[step].start()
     for store in stores:
         store.wait()
 
 
-def finish(own, tokens, cotangent, total, pieces, rate):
+def finish(own, tokens, cotangent, total, piece, rate):
     rows, width = total.shape
     depth = tokens.shape[1]
-    groups = len(pieces)
-    share = width // groups
+    share = piece.shape[1]
     tile = max(share, 256)
     return pl.pallas_call(
-        functools.partial(finish_kernel, groups, rate),
+        functools.partial(finish_kernel, width // share, rate),
         out_shape=jax.ShapeDtypeStruct((rows, width), jnp.bfloat16),
-        in_specs=[pl.BlockSpec(memory_space=pltpu.SMEM)] + [pl.BlockSpec(memory_space=pltpu.VMEM)] * (3 + groups),
+        in_specs=[pl.BlockSpec(memory_space=pltpu.SMEM)] + [pl.BlockSpec(memory_space=pltpu.VMEM)] * 4,
         out_specs=pl.BlockSpec(memory_space=pltpu.HBM),
-        scratch_shapes=[
-            pltpu.VMEM((groups, rows, share), jnp.bfloat16),
-            pltpu.VMEM((width // tile, rows, tile), jnp.bfloat16),
-            pltpu.SemaphoreType.DMA((width // tile,)),
-        ],
+        scratch_shapes=[pltpu.VMEM((width // tile, rows, tile), jnp.bfloat16), pltpu.SemaphoreType.DMA((width // tile,))],
         compiler_params=pltpu.CompilerParams(vmem_limit_bytes=16 * 2**20),
         cost_estimate=pl.CostEstimate(
-            flops=2 * depth * rows * width, bytes_accessed=2 * depth * (rows + width) + 8 * rows * width, transcendentals=0
+            flops=2 * depth * rows * width, bytes_accessed=2 * depth * (rows + width) + 7 * rows * width, transcendentals=0
         ),
         name="finish",
-    )(own.reshape(1), tokens, cotangent, total, *pieces)
-
-
-def gather(piece, axis, size):
+    )(own.reshape(1), tokens, cotangent, total, piece)
+
+
+def gather(piece, axis, size, after=()):
     pieces = {0: piece}
     bit = size // 2
     while bit:
         for k in sorted(pieces):
-            pieces[k ^ bit] = swap(pieces[k], axis, bit)
+            value = lax.optimization_barrier((pieces[k], *after))[0] if k and bit == 1 else pieces[k]
+            pieces[k ^ bit] = swap(value, axis, bit)
         bit //= 2
     return [pieces[k] for k in range(size)]
 
@@ -287,11 +294,11 @@
     average = total[0] / groups
     momentum_next = outer_beta * momentum + average
     master_next = master - outer_rate * (average + outer_beta * momentum_next)
-    pieces = gather(master_next.astype(jnp.bfloat16), "replica", groups)
+    pieces = gather(master_next.astype(jnp.bfloat16), "replica", groups, after=cotangents[:-1])
 
     rate = (1.0 - mix_weight) * inner_rate
-    total, last = accumulate(mine, columns, cotangents[:-1], weight, rate)
-    layer_next = finish(own, last, cotangents[-1], total, pieces, rate)
+    total, last = accumulate(mine, own, columns, cotangents[:-1], weight, pieces[:-1], rate)
+    layer_next = finish(own, last, cotangents[-1], total, pieces[-1], rate)
     return (layer_next[None], master_next, momentum_next)
 
 

time: 87.1 us -> 85.4 us (0.980)
  waiting for transfers between devices: 42.5 us -> 37 us
  local copies, waits for them, and re-layouts: 5.85 us -> 7.87 us
  Pallas kernels: 13.9 us -> 15.6 us
    ppermute x12, waiting for transfers between devices: 42.5 us -> 34.3 us  [swap(): return lax.ppermute(value, axis, [(i, i ^ mask) for i in range(size)])]
    all_to_all x1, waiting for transfers between devices: 0.01 us -> 2.78 us  [on_device(): lax.all_to_all(blocks, 'fsdp', split_axis=0, concat_axis=0, tiled=True)]
    unnamed x18 -> x32, local copies, waits for them, and re-layouts: 5.79 us -> 7.82 us
    pallas_call x2, Pallas kernels: 7.96 us -> 9.67 us  [the longest x1 7.72 us: accumulate(): pl.pallas_call(functools.partial(accumulate_kernel, parts, groups, rate),...]
  transfers between devices with their start and end apart: 13 -> 13, of which waited for: 8 -> 7; matrix products, arithmetic and copies ran while one was open for 3% -> 4% of each run, Pallas kernels for 12% -> 16%
where the time goes in v17:
time: 85.4 us; the launch traced here: 85 us
  waiting for transfers between devices  37 us (43%)
  starting transfers between devices  20.5 us (24%)
  Pallas kernels  15.6 us (18%)
  local copies, waits for them, and re-layouts  7.87 us (9%)
  other arithmetic  3.27 us (4%)
    ppermute x12, waiting for transfers between devices, swap(): return lax.ppermute(value, axis, [(i, i ^ mask) for i in range(size)])  34.3 us
    ppermute x12, starting transfers between devices, swap(): return lax.ppermute(value, axis, [(i, i ^ mask) for i in range(size)])  14.9 us
    unnamed x32, local copies, waits for them, and re-layouts  7.82 us
    pallas_call x1, Pallas kernels, accumulate(): pl.pallas_call(functools.partial(accumulate_kernel, parts, groups, rate),...  7.72 us
    all_to_all x1, starting transfers between devices, on_device(): lax.all_to_all(blocks, 'fsdp', split_axis=0, concat_axis=0, tiled=True)  5.61 us
    pallas_call x1, Pallas kernels, code_and_decode(): pl.pallas_call(code_kernel, out_shape=(half, half), in_specs=[pl.BlockSpe...  3.69 us
    all_to_all x1, waiting for transfers between devices, on_device(): lax.all_to_all(blocks, 'fsdp', split_axis=0, concat_axis=0, tiled=True)  2.78 us
    pallas_call x1, Pallas kernels, prepare(): pl.pallas_call(prepare_kernel, out_shape=jax.ShapeDtypeStruct((shards, ro...  2.21 us
  transfers between devices with their start and end apart: 13, of which 7 were waited for; matrix products, arithmetic and copies ran while one was open for 4% of the time, Pallas kernels for 16%

profile of v17, /device:TPU:0, one launch (start us, length us, event | category | flops | bytes accessed | tf_op | source)
XLA Modules:
  0.0 85.0 jit_solution(6923275142353484499)
XLA Ops:
  0.6 4.1 %collective-permute-start.2 = (bf16[128,1024]{1,0:T(8,128)(2,1)}, bf16[128,1024]{1,0:T(8,128)(2,1)S(1)}, u32[]{:S(2)}, u32[]{:S(2)}) collective-permute-start(bf16[128,1024]{1,0:T(8,128)(2,1)} %bitcast.20), channel_id=1, source_target_pairs={{0,4},{1,5},{2,6},{3,7},{4,0},{5,1},{6,2},{7,3},{8,12},{9,13},{10,... | collective-permute-start | bytes 786440 | tf_op jit(solution)/shard_map/ppermute | solution.py:24
  4.7 1.6 %collective-permute-start.1 = (bf16[128,1024]{1,0:T(8,128)(2,1)}, bf16[128,1024]{1,0:T(8,128)(2,1)S(1)}, u32[]{:S(2)}, u32[]{:S(2)}) collective-permute-start(bf16[128,1024]{1,0:T(8,128)(2,1)} %bitcast.21), channel_id=1, source_target_pairs={{0,2},{1,3},{2,0},{3,1},{4,6},{5,7},{6,4},{7,5},{8,10},{9,11},{10,... | collective-permute-start | bytes 786440 | tf_op jit(solution)/shard_map/ppermute | solution.py:24
  6.3 1.5 %collective-permute-start = (bf16[128,1024]{1,0:T(8,128)(2,1)}, bf16[128,1024]{1,0:T(8,128)(2,1)S(1)}, u32[]{:S(2)}, u32[]{:S(2)}) collective-permute-start(bf16[128,1024]{1,0:T(8,128)(2,1)} %bitcast.22), channel_id=1, source_target_pairs={{0,1},{1,0},{2,3},{3,2},{4,5},{5,4},{6,7},{7,6},{8,9},{9,8},{10,11... | collective-permute-start | bytes 786440 | tf_op jit(solution)/shard_map/ppermute | solution.py:24
  7.8 0.7 reshape.20
  8.6 1.6 %copy-done.2 = bf16[1,128,8192]{2,1,0:T(8,128)(2,1)S(1)} copy-done((bf16[1,128,8192]{2,1,0:T(8,128)(2,1)S(1)}, bf16[1,128,8192]{2,1,0:T(8,128)(2,1)}, u32[]{:S(2)}) %copy-start.2) | copy-done | bytes 2097176
  10.1 2.2 %prepare.1 = bf16[8,1024,128]{2,1,0:T(8,128)(2,1)} custom-call(bf16[128,8192]{1,0:T(8,128)(2,1)S(1)} %bitcast.17, f32[1,8192]{1,0:T(1,128)S(1)} %bitcast.18), custom_call_target="tpu_custom_call" | custom-call | flops 5242880 | bytes 4194304 | tf_op jit(solution)/shard_map/prepare/pallas_call | solution.py:58
  12.4 4.6 %collective-permute-done.2.refs_4_ = bf16[128,1024]{1,0:T(8,128)(2,1)S(1)} collective-permute-done((bf16[128,1024]{1,0:T(8,128)(2,1)}, bf16[128,1024]{1,0:T(8,128)(2,1)S(1)}, u32[]{:S(2)}, u32[]{:S(2)}) %collective-permute-start.2) | collective-permute-done | bytes 262176 | tf_op jit(solution)/shard_map/ppermute | solution.py:24
  17.0 0.2 collective-permute-done.1.refs_2_
  17.2 0.8 copy-done.12
  17.9 5.6 %all-to-all-start = ((bf16[8,1024,128]{2,1,0:T(8,128)(2,1)}), bf16[8,1024,128]{2,1,0:T(8,128)(2,1)}, u32[]{:S(2)}, u32[]{:S(2)}) async-start(bf16[8,1024,128]{2,1,0:T(8,128)(2,1)} %prepare.1), calls=%async_computation | async-start | bytes 4194304 | tf_op jit(solution)/shard_map/all_to_all | solution.py:285
  23.6 1.6 %copy-done.3 = bf16[1024,1024]{1,0:T(8,128)(2,1)S(1)} copy-done((bf16[1024,1024]{1,0:T(8,128)(2,1)S(1)}, bf16[1024,1024]{1,0:T(8,128)(2,1)}, u32[]{:S(2)}) %copy-start.3) | copy-done | bytes 2097176
  25.1 3.7 %code_and_decode.1 = (bf16[2,1024,256]{2,1,0:T(8,128)(2,1)S(1)}, bf16[2,1024,256]{2,1,0:T(8,128)(2,1)S(1)}) custom-call(s32[1]{0:T(128)} %bitcast.own_ref, bf16[1024,1024]{1,0:T(8,128)(2,1)S(1)} %copy-done.3, bf16[1024,1024]{1,0:T(8,128)(2,1)S(1)} %bitcast.16), custom_call_target="tpu_custom_call" | custom-call | flops 20971520 | bytes 6291456 | tf_op jit(solution)/shard_map/code_and_decode/pallas_call | solution.py:128
  28.8 0.1 collective-permute-start.6
  28.9 2.6 %collective-permute-done.6 = bf16[2,1024,256]{2,1,0:T(8,128)(2,1)S(1)} collective-permute-done((bf16[2,1024,256]{2,1,0:T(8,128)(2,1)S(1)}, bf16[2,1024,256]{2,1,0:T(8,128)(2,1)S(1)}, u32[]{:S(2)}, u32[]{:S(2)}) %collective-permute-start.6) | collective-permute-done | bytes 1048608 | tf_op jit(solution)/shard_map/ppermute | solution.py:24
  31.6 0.2 convert_add_fusion
  31.9 1.6 %collective-permute-start.7 = (bf16[1,1024,256]{2,1,0:T(8,128)(2,1)S(1)}, bf16[1,1024,256]{2,1,0:T(8,128)(2,1)S(1)}, u32[]{:S(2)}, u32[]{:S(2)}) collective-permute-start(bf16[1,1024,256]{2,1,0:T(8,128)(2,1)S(1)} %slice.23), channel_id=1, source_target_pairs={{0,16},{8,24},{16,0},{24,8},{1,17},{9,25},{17,1},{25,9},{2,18},{10... | collective-permute-start | bytes 1572872 | tf_op jit(solution)/shard_map/ppermute | solution.py:24
  33.4 12.5 %collective-permute-done.7 = bf16[1,1024,256]{2,1,0:T(8,128)(2,1)S(1)} collective-permute-done((bf16[1,1024,256]{2,1,0:T(8,128)(2,1)S(1)}, bf16[1,1024,256]{2,1,0:T(8,128)(2,1)S(1)}, u32[]{:S(2)}, u32[]{:S(2)}) %collective-permute-start.7) | collective-permute-done | bytes 524320 | tf_op jit(solution)/shard_map/ppermute | solution.py:24
  45.9 1.7 %fusion.2 = (bf16[1024,256]{1,0:T(8,128)(2,1)S(1)}, f32[1024,256]{1,0:T(8,128)}, f32[1024,256]{1,0:T(8,128)}) fusion(f32[1024,256]{1,0:T(8,128)S(1)} %copy-done.6, bf16[1,1024,256]{2,1,0:T(8,128)(2,1)S(1)} %collective-permute-done.7, f32[2,1024,256]{2,1,0:T(8,128)S(1)} %convert_add_fusion, f32[1024,256]{1,0:T(8,128)S(1)} %copy-done.7), kind=kLoop, calls=%fused_computation.8 | loop fusion | flops 2621440 | bytes 6291456 | tf_op jit(solution)/shard_map/convert_element_type | solution.py:297
  47.6 1.5 %collective-permute-start.9 = (bf16[1024,256]{1,0:T(8,128)(2,1)S(1)}, bf16[1024,256]{1,0:T(8,128)(2,1)S(1)}, u32[]{:S(2)}, u32[]{:S(2)}) collective-permute-start(bf16[1024,256]{1,0:T(8,128)(2,1)S(1)} %get-tuple-element.19.refs_7_), channel_id=1, source_target_pairs={{0,16},{8,24},{16,0},{24,8},{1,17},{9,25},{17,1},{25,9},{2,18},{10... | collective-permute-start | bytes 1572872 | tf_op jit(solution)/shard_map/ppermute | solution.py:24
  49.1 2.0 %collective-permute-start.4 = (bf16[128,1024]{1,0:T(8,128)(2,1)S(1)}, bf16[128,1024]{1,0:T(8,128)(2,1)S(1)}, u32[]{:S(2)}, u32[]{:S(2)}) collective-permute-start(bf16[128,1024]{1,0:T(8,128)(2,1)S(1)} %collective-permute-done.2.refs_4_), channel_id=1, source_target_pairs={{0,1},{1,0},{2,3},{3,2},{4,5},{5,4},{6,7},{7,6},{8,9},{9,8},{10,11... | collective-permute-start | bytes 786440 | tf_op jit(solution)/shard_map/ppermute | solution.py:24
  51.1 1.5 %collective-permute-start.5 = (bf16[128,1024]{1,0:T(8,128)(2,1)S(1)}, bf16[128,1024]{1,0:T(8,128)(2,1)S(1)}, u32[]{:S(2)}, u32[]{:S(2)}) collective-permute-start(bf16[128,1024]{1,0:T(8,128)(2,1)S(1)} %collective-permute-done.2.refs_4_), channel_id=1, source_target_pairs={{0,2},{1,3},{2,0},{3,1},{4,6},{5,7},{6,4},{7,5},{8,10},{9,11},{10,... | collective-permute-start | bytes 786440 | tf_op jit(solution)/shard_map/ppermute | solution.py:24
  52.5 0.6 collective-permute-start.3
  53.1 11.3 %collective-permute-done.5.refs_6_ = bf16[128,1024]{1,0:T(8,128)(2,1)S(1)} collective-permute-done((bf16[128,1024]{1,0:T(8,128)(2,1)S(1)}, bf16[128,1024]{1,0:T(8,128)(2,1)S(1)}, u32[]{:S(2)}, u32[]{:S(2)}) %collective-permute-start.5) | collective-permute-done | bytes 262176 | tf_op jit(solution)/shard_map/ppermute | solution.py:24
  64.5 3.0 %collective-permute-done.3.refs_3_ = bf16[128,1024]{1,0:T(8,128)(2,1)S(1)} collective-permute-done((bf16[128,1024]{1,0:T(8,128)(2,1)S(1)}, bf16[128,1024]{1,0:T(8,128)(2,1)S(1)}, u32[]{:S(2)}, u32[]{:S(2)}) %collective-permute-start.3) | collective-permute-done | bytes 262176 | tf_op jit(solution)/shard_map/ppermute | solution.py:24
  67.4 0.7 copy-done.15
  68.2 0.5 collective-permute-start.10
  68.7 0.7 pad_add_fusion.place_ref
  69.3 2.8 %all-to-all-done.tokens_ref = bf16[8,1024,128]{2,1,0:T(8,128)(2,1)} async-done(((bf16[8,1024,128]{2,1,0:T(8,128)(2,1)}), bf16[8,1024,128]{2,1,0:T(8,128)(2,1)}, u32[]{:S(2)}, u32[]{:S(2)}) %all-to-all-start) | async-done | bytes 2097184 | tf_op jit(solution)/shard_map/all_to_all | solution.py:285
  72.2 7.7 %accumulate.1 = (f32[1024,1024]{1,0:T(8,128)}, bf16[1024,128]{1,0:T(8,128)(2,1)}) custom-call(s32[2]{0:T(128)} %pad_add_fusion.place_ref, bf16[8,1024,128]{2,1,0:T(8,128)(2,1)} %all-to-all-done.tokens_ref, bf16[1024,1024]{1,0:T(8,128)(2,1)} %bitcast.15, bf16[128,1024]{1,0:T(8,128)(2,1)} %bitcast.23, bf16[128,1024]{1,0:T(8,128)(2,1)} %copy-done.12, ...), custom_call_target="tpu_custom_call" | custom-call | flops 1879048192 | bytes 12582912 | tf_op jit(solution)/shard_map/accumulate/pallas_call | solution.py:196
  79.9 2.2 %copy-done.1 = f32[1024,1024]{1,0:T(8,128)S(1)} copy-done((f32[1024,1024]{1,0:T(8,128)S(1)}, f32[1024,1024]{1,0:T(8,128)}, u32[]{:S(2)}) %copy-start.1) | copy-done | bytes 4194328
  82.1 0.9 %copy-done.4 = bf16[1024,128]{1,0:T(8,128)(2,1)S(1)} copy-done((bf16[1024,128]{1,0:T(8,128)(2,1)S(1)}, bf16[1024,128]{1,0:T(8,128)(2,1)}, u32[]{:S(2)}) %copy-start.4) | copy-done | bytes 262168
  83.0 2.0 %finish.1 = bf16[1024,1024]{1,0:T(8,128)(2,1)} custom-call(s32[1]{0:T(128)} %bitcast.own_ref, bf16[1024,128]{1,0:T(8,128)(2,1)S(1)} %copy-done.4, bf16[128,1024]{1,0:T(8,128)(2,1)S(1)} %collective-permute-done.10.cotangent_ref, f32[1024,1024]{1,0:T(8,128)S(1)} %copy-done.1, bf16[1024,256]{1,0:T(8,128)(2,1)S(1)} %collective-permute-done.11.piece_ref), custom_call_target="tpu_custom_call" | custom-call | flops 268435456 | bytes 7864320 | tf_op jit(solution)/shard_map/finish/pallas_call | solution.py:245
  (35 shorter events, 0.1 us)
Async XLA Ops:
  0.6 16.3 %collective-permute-start.2 = (bf16[128,1024]{1,0:T(8,128)(2,1)}, bf16[128,1024]{1,0:T(8,128)(2,1)S(1)}, u32[]{:S(2)}, u32[]{:S(2)}) collective-permute-start(bf16[128,1024]{1,0:T(8,128)(2,1)} %bitcast.20), channel_id=1, source_target_pairs={{0,4},{1,5},{2,6},{3,7},{4,0},{5,1},{6,2},{7,3},{8,12},{9,13},{10,... | collective-permute-start | bytes 786440 | tf_op jit(solution)/shard_map/ppermute | solution.py:24
  4.7 12.4 %collective-permute-start.1 = (bf16[128,1024]{1,0:T(8,128)(2,1)}, bf16[128,1024]{1,0:T(8,128)(2,1)S(1)}, u32[]{:S(2)}, u32[]{:S(2)}) collective-permute-start(bf16[128,1024]{1,0:T(8,128)(2,1)} %bitcast.21), channel_id=1, source_target_pairs={{0,2},{1,3},{2,0},{3,1},{4,6},{5,7},{6,4},{7,5},{8,10},{9,11},{10,... | collective-permute-start | bytes 786440 | tf_op jit(solution)/shard_map/ppermute | solution.py:24
  6.3 10.9 %collective-permute-start = (bf16[128,1024]{1,0:T(8,128)(2,1)}, bf16[128,1024]{1,0:T(8,128)(2,1)S(1)}, u32[]{:S(2)}, u32[]{:S(2)}) collective-permute-start(bf16[128,1024]{1,0:T(8,128)(2,1)} %bitcast.22), channel_id=1, source_target_pairs={{0,1},{1,0},{2,3},{3,2},{4,5},{5,4},{6,7},{7,6},{8,9},{9,8},{10,11... | collective-permute-start | bytes 786440 | tf_op jit(solution)/shard_map/ppermute | solution.py:24
  8.5 1.6 %copy-start.2 = (bf16[1,128,8192]{2,1,0:T(8,128)(2,1)S(1)}, bf16[1,128,8192]{2,1,0:T(8,128)(2,1)}, u32[]{:S(2)}) copy-start(bf16[1,128,8192]{2,1,0:T(8,128)(2,1)} %param.7) | copy-start | bytes 6291460
  17.0 34.1 %copy-start.10 = (bf16[128,1024]{1,0:T(8,128)(2,1)}, bf16[128,1024]{1,0:T(8,128)(2,1)S(1)}, u32[]{:S(2)}) copy-start(bf16[128,1024]{1,0:T(8,128)(2,1)S(1)} %collective-permute-done.2.refs_4_) | copy-start | bytes 786436
  17.2 35.4 %copy-start.11 = (bf16[128,1024]{1,0:T(8,128)(2,1)}, bf16[128,1024]{1,0:T(8,128)(2,1)S(1)}, u32[]{:S(2)}) copy-start(bf16[128,1024]{1,0:T(8,128)(2,1)S(1)} %collective-permute-done.1.refs_2_) | copy-start | bytes 786436
  17.2 0.8 copy-start.12
  17.2 6.4 %copy-start = (bf16[1,1024,1024]{2,1,0:T(8,128)(2,1)S(1)}, bf16[1,1024,1024]{2,1,0:T(8,128)(2,1)}, u32[]{:S(2)}) copy-start(bf16[1,1024,1024]{2,1,0:T(8,128)(2,1)} %param.10) | copy-start | bytes 6291460
  17.9 54.2 %all-to-all-start = ((bf16[8,1024,128]{2,1,0:T(8,128)(2,1)}), bf16[8,1024,128]{2,1,0:T(8,128)(2,1)}, u32[]{:S(2)}, u32[]{:S(2)}) async-start(bf16[8,1024,128]{2,1,0:T(8,128)(2,1)} %prepare.1), calls=%async_computation | async-start | bytes 4194304 | tf_op jit(solution)/shard_map/all_to_all | solution.py:285
  23.6 1.6 %copy-start.3 = (bf16[1024,1024]{1,0:T(8,128)(2,1)S(1)}, bf16[1024,1024]{1,0:T(8,128)(2,1)}, u32[]{:S(2)}) copy-start(bf16[1024,1024]{1,0:T(8,128)(2,1)} %shared_ref) | copy-start | bytes 6291460
  28.8 2.7 %collective-permute-start.6 = (bf16[2,1024,256]{2,1,0:T(8,128)(2,1)S(1)}, bf16[2,1024,256]{2,1,0:T(8,128)(2,1)S(1)}, u32[]{:S(2)}, u32[]{:S(2)}) collective-permute-start(bf16[2,1024,256]{2,1,0:T(8,128)(2,1)S(1)} %get-tuple-element.15), channel_id=1, source_target_pairs={{0,8},{8,0},{16,24},{24,16},{1,9},{9,1},{17,25},{25,17},{2,10},{10... | collective-permute-start | bytes 3145736 | tf_op jit(solution)/shard_map/ppermute | solution.py:24
  31.6 14.3 %copy-start.6 = (f32[1024,256]{1,0:T(8,128)S(1)}, f32[1024,256]{1,0:T(8,128)}, u32[]{:S(2)}) copy-start(f32[1024,256]{1,0:T(8,128)} %param.12) | copy-start | bytes 3145732
  31.6 14.3 %copy-start.7 = (f32[1024,256]{1,0:T(8,128)S(1)}, f32[1024,256]{1,0:T(8,128)}, u32[]{:S(2)}) copy-start(f32[1024,256]{1,0:T(8,128)} %param.13) | copy-start | bytes 3145732
  31.9 14.0 %collective-permute-start.7 = (bf16[1,1024,256]{2,1,0:T(8,128)(2,1)S(1)}, bf16[1,1024,256]{2,1,0:T(8,128)(2,1)S(1)}, u32[]{:S(2)}, u32[]{:S(2)}) collective-permute-start(bf16[1,1024,256]{2,1,0:T(8,128)(2,1)S(1)} %slice.23), channel_id=1, source_target_pairs={{0,16},{8,24},{16,0},{24,8},{1,17},{9,25},{17,1},{25,9},{2,18},{10... | collective-permute-start | bytes 1572872 | tf_op jit(solution)/shard_map/ppermute | solution.py:24
  47.6 24.6 %copy-start.5 = (bf16[1024,256]{1,0:T(8,128)(2,1)}, bf16[1024,256]{1,0:T(8,128)(2,1)S(1)}, u32[]{:S(2)}) copy-start(bf16[1024,256]{1,0:T(8,128)(2,1)S(1)} %get-tuple-element.19.refs_7_) | copy-start | bytes 1572868
  47.6 19.9 %collective-permute-start.9 = (bf16[1024,256]{1,0:T(8,128)(2,1)S(1)}, bf16[1024,256]{1,0:T(8,128)(2,1)S(1)}, u32[]{:S(2)}, u32[]{:S(2)}) collective-permute-start(bf16[1024,256]{1,0:T(8,128)(2,1)S(1)} %get-tuple-element.19.refs_7_), channel_id=1, source_target_pairs={{0,16},{8,24},{16,0},{24,8},{1,17},{9,25},{17,1},{25,9},{2,18},{10... | collective-permute-start | bytes 1572872 | tf_op jit(solution)/shard_map/ppermute | solution.py:24
  49.1 15.4 %collective-permute-start.4 = (bf16[128,1024]{1,0:T(8,128)(2,1)S(1)}, bf16[128,1024]{1,0:T(8,128)(2,1)S(1)}, u32[]{:S(2)}, u32[]{:S(2)}) collective-permute-start(bf16[128,1024]{1,0:T(8,128)(2,1)S(1)} %collective-permute-done.2.refs_4_), channel_id=1, source_target_pairs={{0,1},{1,0},{2,3},{3,2},{4,5},{5,4},{6,7},{7,6},{8,9},{9,8},{10,11... | collective-permute-start | bytes 786440 | tf_op jit(solution)/shard_map/ppermute | solution.py:24
  51.1 13.4 %collective-permute-start.5 = (bf16[128,1024]{1,0:T(8,128)(2,1)S(1)}, bf16[128,1024]{1,0:T(8,128)(2,1)S(1)}, u32[]{:S(2)}, u32[]{:S(2)}) collective-permute-start(bf16[128,1024]{1,0:T(8,128)(2,1)S(1)} %collective-permute-done.2.refs_4_), channel_id=1, source_target_pairs={{0,2},{1,3},{2,0},{3,1},{4,6},{5,7},{6,4},{7,5},{8,10},{9,11},{10,... | collective-permute-start | bytes 786440 | tf_op jit(solution)/shard_map/ppermute | solution.py:24
  52.5 14.9 %collective-permute-start.3 = (bf16[128,1024]{1,0:T(8,128)(2,1)S(1)}, bf16[128,1024]{1,0:T(8,128)(2,1)S(1)}, u32[]{:S(2)}, u32[]{:S(2)}) collective-permute-start(bf16[128,1024]{1,0:T(8,128)(2,1)S(1)} %collective-permute-done.1.refs_2_), channel_id=1, source_target_pairs={{0,1},{1,0},{2,3},{3,2},{4,5},{5,4},{6,7},{7,6},{8,9},{9,8},{10,11... | collective-permute-start | bytes 786440 | tf_op jit(solution)/shard_map/ppermute | solution.py:24
  53.1 16.2 %collective-permute-start.8 = (bf16[1024,256]{1,0:T(8,128)(2,1)S(1)}, bf16[1024,256]{1,0:T(8,128)(2,1)S(1)}, u32[]{:S(2)}, u32[]{:S(2)}) collective-permute-start(bf16[1024,256]{1,0:T(8,128)(2,1)S(1)} %get-tuple-element.19.refs_7_), channel_id=1, source_target_pairs={{0,8},{8,0},{16,24},{24,16},{1,9},{9,1},{17,25},{25,17},{2,10},{10... | collective-permute-start | bytes 1572872 | tf_op jit(solution)/shard_map/ppermute | solution.py:24
  64.5 7.7 %copy-start.14 = (bf16[128,1024]{1,0:T(8,128)(2,1)}, bf16[128,1024]{1,0:T(8,128)(2,1)S(1)}, u32[]{:S(2)}) copy-start(bf16[128,1024]{1,0:T(8,128)(2,1)S(1)} %collective-permute-done.5.refs_6_) | copy-start | bytes 786436
  64.5 7.7 %copy-start.13 = (bf16[128,1024]{1,0:T(8,128)(2,1)}, bf16[128,1024]{1,0:T(8,128)(2,1)S(1)}, u32[]{:S(2)}) copy-start(bf16[128,1024]{1,0:T(8,128)(2,1)S(1)} %collective-permute-done.4.refs_5_) | copy-start | bytes 786436
  67.4 0.7 copy-start.15
  68.2 4.0 %copy-start.8 = (bf16[1024,256]{1,0:T(8,128)(2,1)}, bf16[1024,256]{1,0:T(8,128)(2,1)S(1)}, u32[]{:S(2)}) copy-start(bf16[1024,256]{1,0:T(8,128)(2,1)S(1)} %collective-permute-done.9.refs_9_) | copy-start | bytes 1572868
  68.2 11.7 %collective-permute-start.11 = (bf16[1024,256]{1,0:T(8,128)(2,1)S(1)}, bf16[1024,256]{1,0:T(8,128)(2,1)S(1)}, u32[]{:S(2)}, u32[]{:S(2)}) collective-permute-start(bf16[1024,256]{1,0:T(8,128)(2,1)S(1)} %collective-permute-done.9.refs_9_), channel_id=1, source_target_pairs={{0,8},{8,0},{16,24},{24,16},{1,9},{9,1},{17,25},{25,17},{2,10},{10... | collective-permute-start | bytes 1572872 | tf_op jit(solution)/shard_map/ppermute | solution.py:24
  68.2 11.7 %collective-permute-start.10 = (bf16[128,1024]{1,0:T(8,128)(2,1)S(1)}, bf16[128,1024]{1,0:T(8,128)(2,1)S(1)}, u32[]{:S(2)}, u32[]{:S(2)}) collective-permute-start(bf16[128,1024]{1,0:T(8,128)(2,1)S(1)} %collective-permute-done.5.refs_6_), channel_id=1, source_target_pairs={{0,1},{1,0},{2,3},{3,2},{4,5},{5,4},{6,7},{7,6},{8,9},{9,8},{10,11... | collective-permute-start | bytes 786440 | tf_op jit(solution)/shard_map/ppermute | solution.py:24
  69.3 2.8 %copy-start.9 = (bf16[1024,256]{1,0:T(8,128)(2,1)}, bf16[1024,256]{1,0:T(8,128)(2,1)S(1)}, u32[]{:S(2)}) copy-start(bf16[1024,256]{1,0:T(8,128)(2,1)S(1)} %collective-permute-done.8.refs_8_) | copy-start | bytes 1572868
  79.9 2.2 %copy-start.1 = (f32[1024,1024]{1,0:T(8,128)S(1)}, f32[1024,1024]{1,0:T(8,128)}, u32[]{:S(2)}) copy-start(f32[1024,1024]{1,0:T(8,128)} %get-tuple-element.17.total_ref) | copy-start | bytes 12582916
  82.1 0.9 %copy-start.4 = (bf16[1024,128]{1,0:T(8,128)(2,1)S(1)}, bf16[1024,128]{1,0:T(8,128)(2,1)}, u32[]{:S(2)}) copy-start(bf16[1024,128]{1,0:T(8,128)(2,1)} %get-tuple-element.16.tokens_ref) | copy-start | bytes 786436

commit v18 on v17

--- a/solution.py
+++ b/solution.py
@@ -142,11 +142,11 @@
     )(own.reshape(1), shared, weight)
 
 
-def accumulate_kernel(parts, groups, rate, place_ref, tokens_ref, weight_ref, *refs):
+def accumulate_kernel(parts, groups, rate, mine_ref, own_ref, tokens_ref, weight_ref, *refs):
     cotangent_refs, refs = refs[:parts], refs[parts:]
     piece_refs, refs = refs[: groups - 1], refs[groups - 1 :]
     total_ref, last_ref, tokens, cotangents, weight, pieces, token_sems, cotangent_sems, piece_sems, sems = refs
-    mine, own = place_ref[0], place_ref[1]
+    mine, own = mine_ref[0], own_ref[0]
     depth, width = cotangent_refs[0].shape
     share = pieces.shape[2]
     tile = max(share, 256)
@@ -196,7 +196,7 @@
     return pl.pallas_call(
         functools.partial(accumulate_kernel, parts, groups, rate),
         out_shape=(jax.ShapeDtypeStruct((rows, width), jnp.float32), jax.ShapeDtypeStruct((rows, depth), jnp.bfloat16)),
-        in_specs=[pl.BlockSpec(memory_space=pltpu.SMEM)]
+        in_specs=[pl.BlockSpec(memory_space=pltpu.SMEM)] * 2
         + [pl.BlockSpec(memory_space=pltpu.HBM)] * (1 + parts + groups),
         out_specs=(pl.BlockSpec(memory_space=pltpu.VMEM),) * 2,
         scratch_shapes=[
@@ -209,14 +209,14 @@
             pltpu.SemaphoreType.DMA((groups,)),
             pltpu.SemaphoreType.DMA((2,)),
         ],
-        compiler_params=pltpu.CompilerParams(vmem_limit_bytes=58 * 2**20),
+        compiler_params=pltpu.CompilerParams(vmem_limit_bytes=43392 * 2**10),
         cost_estimate=pl.CostEstimate(
             flops=2 * depth * parts * rows * width,
             bytes_accessed=2 * depth * shards * (rows + width) + 8 * rows * width,
             transcendentals=0,
         ),
         name="accumulate",
-    )(jnp.stack([mine, own]), tokens, weight, *cotangents, *pieces)
+    )(mine.reshape(1), own.reshape(1), tokens, weight, *cotangents, *pieces)
 
 
 def finish_kernel(groups, rate, own_ref, tokens_ref, cotangent_ref, total_ref, piece_ref, out_ref, outs, sems):

time: 85.4 us -> 86.2 us (level)
  local copies, waits for them, and re-layouts: 7.87 us -> 10.8 us
  Pallas kernels: 15.6 us -> 14 us
    unnamed x32 -> x36, local copies, waits for them, and re-layouts: 7.82 us -> 10.8 us
    pallas_call x1, Pallas kernels: 7.72 us -> 5.01 us  [accumulate(): pl.pallas_call(functools.partial(accumulate_kernel, parts, groups, rate),...]
    pallas_call x1, Pallas kernels: 1.95 us -> 3.1 us  [finish(): pl.pallas_call(functools.partial(finish_kernel, width // share, rate), ou...]
  transfers between devices with their start and end apart: 13 -> 13, of which waited for: 7 -> 7; matrix products, arithmetic and copies ran while one was open for 4% -> 3% of each run, Pallas kernels for 16% -> 13%
where the time goes in v18:
time: 86.2 us; the launch traced here: 85.7 us
  waiting for transfers between devices  36.8 us (43%)
  starting transfers between devices  20.7 us (24%)
  Pallas kernels  14 us (16%)
  local copies, waits for them, and re-layouts  10.8 us (13%)
  other arithmetic  2.65 us (3%)
    ppermute x12, waiting for transfers between devices, swap(): return lax.ppermute(value, axis, [(i, i ^ mask) for i in range(size)])  33.5 us
    ppermute x12, starting transfers between devices, swap(): return lax.ppermute(value, axis, [(i, i ^ mask) for i in range(size)])  15 us
    unnamed x36, local copies, waits for them, and re-layouts  10.8 us
    all_to_all x1, starting transfers between devices, on_device(): lax.all_to_all(blocks, 'fsdp', split_axis=0, concat_axis=0, tiled=True)  5.71 us
    pallas_call x1, Pallas kernels, accumulate(): pl.pallas_call(functools.partial(accumulate_kernel, parts, groups, rate),...  5.01 us
    pallas_call x1, Pallas kernels, code_and_decode(): pl.pallas_call(code_kernel, out_shape=(half, half), in_specs=[pl.BlockSpe...  3.69 us
    all_to_all x1, waiting for transfers between devices, on_device(): lax.all_to_all(blocks, 'fsdp', split_axis=0, concat_axis=0, tiled=True)  3.3 us
    pallas_call x1, Pallas kernels, finish(): pl.pallas_call(functools.partial(finish_kernel, width // share, rate), ou...  3.1 us
  transfers between devices with their start and end apart: 13, of which 7 were waited for; matrix products, arithmetic and copies ran while one was open for 3% of the time, Pallas kernels for 13%

profile of v18, /device:TPU:0, one launch (start us, length us, event | category | flops | bytes accessed | tf_op | source)
XLA Modules:
  0.0 85.7 jit_solution(10408420514513517792)
XLA Ops:
  0.6 4.1 %collective-permute-start.2 = (bf16[128,1024]{1,0:T(8,128)(2,1)}, bf16[128,1024]{1,0:T(8,128)(2,1)S(1)}, u32[]{:S(2)}, u32[]{:S(2)}) collective-permute-start(bf16[128,1024]{1,0:T(8,128)(2,1)} %bitcast.18), channel_id=1, source_target_pairs={{0,4},{1,5},{2,6},{3,7},{4,0},{5,1},{6,2},{7,3},{8,12},{9,13},{10,... | collective-permute-start | bytes 786440 | tf_op jit(solution)/shard_map/ppermute | solution.py:24
  4.7 1.6 %collective-permute-start.1 = (bf16[128,1024]{1,0:T(8,128)(2,1)}, bf16[128,1024]{1,0:T(8,128)(2,1)S(1)}, u32[]{:S(2)}, u32[]{:S(2)}) collective-permute-start(bf16[128,1024]{1,0:T(8,128)(2,1)} %bitcast.19), channel_id=1, source_target_pairs={{0,2},{1,3},{2,0},{3,1},{4,6},{5,7},{6,4},{7,5},{8,10},{9,11},{10,... | collective-permute-start | bytes 786440 | tf_op jit(solution)/shard_map/ppermute | solution.py:24
  6.3 1.5 %collective-permute-start = (bf16[128,1024]{1,0:T(8,128)(2,1)}, bf16[128,1024]{1,0:T(8,128)(2,1)S(1)}, u32[]{:S(2)}, u32[]{:S(2)}) collective-permute-start(bf16[128,1024]{1,0:T(8,128)(2,1)} %bitcast.20), channel_id=1, source_target_pairs={{0,1},{1,0},{2,3},{3,2},{4,5},{5,4},{6,7},{7,6},{8,9},{9,8},{10,11... | collective-permute-start | bytes 786440 | tf_op jit(solution)/shard_map/ppermute | solution.py:24
  7.8 0.7 reshape.25
  8.6 1.6 %copy-done.1 = bf16[1,128,8192]{2,1,0:T(8,128)(2,1)S(1)} copy-done((bf16[1,128,8192]{2,1,0:T(8,128)(2,1)S(1)}, bf16[1,128,8192]{2,1,0:T(8,128)(2,1)}, u32[]{:S(2)}) %copy-start.1) | copy-done | bytes 2097176
  10.1 2.2 %prepare.1 = bf16[8,1024,128]{2,1,0:T(8,128)(2,1)} custom-call(bf16[128,8192]{1,0:T(8,128)(2,1)S(1)} %bitcast.17, f32[1,8192]{1,0:T(1,128)S(1)} %bitcast.22), custom_call_target="tpu_custom_call" | custom-call | flops 5242880 | bytes 4194304 | tf_op jit(solution)/shard_map/prepare/pallas_call | solution.py:58
  12.4 4.6 %collective-permute-done.2.refs_4_ = bf16[128,1024]{1,0:T(8,128)(2,1)S(1)} collective-permute-done((bf16[128,1024]{1,0:T(8,128)(2,1)}, bf16[128,1024]{1,0:T(8,128)(2,1)S(1)}, u32[]{:S(2)}, u32[]{:S(2)}) %collective-permute-start.2) | collective-permute-done | bytes 262176 | tf_op jit(solution)/shard_map/ppermute | solution.py:24
  17.9 0.7 copy-done.10
  18.6 5.7 %all-to-all-start = ((bf16[8,1024,128]{2,1,0:T(8,128)(2,1)}), bf16[8,1024,128]{2,1,0:T(8,128)(2,1)}, u32[]{:S(2)}, u32[]{:S(2)}) async-start(bf16[8,1024,128]{2,1,0:T(8,128)(2,1)} %prepare.1), calls=%async_computation | async-start | bytes 4194304 | tf_op jit(solution)/shard_map/all_to_all | solution.py:285
  24.3 1.6 %copy-done.2 = bf16[1024,1024]{1,0:T(8,128)(2,1)S(1)} copy-done((bf16[1024,1024]{1,0:T(8,128)(2,1)S(1)}, bf16[1024,1024]{1,0:T(8,128)(2,1)}, u32[]{:S(2)}) %copy-start.2) | copy-done | bytes 2097176
  25.9 3.7 %code_and_decode.1 = (bf16[2,1024,256]{2,1,0:T(8,128)(2,1)S(1)}, bf16[2,1024,256]{2,1,0:T(8,128)(2,1)S(1)}) custom-call(s32[1]{0:T(128)} %bitcast.own_ref, bf16[1024,1024]{1,0:T(8,128)(2,1)S(1)} %copy-done.2, bf16[1024,1024]{1,0:T(8,128)(2,1)S(1)} %bitcast.15), custom_call_target="tpu_custom_call" | custom-call | flops 20971520 | bytes 6291456 | tf_op jit(solution)/shard_map/code_and_decode/pallas_call | solution.py:128
  29.6 2.6 %collective-permute-done.6 = bf16[2,1024,256]{2,1,0:T(8,128)(2,1)S(1)} collective-permute-done((bf16[2,1024,256]{2,1,0:T(8,128)(2,1)S(1)}, bf16[2,1024,256]{2,1,0:T(8,128)(2,1)S(1)}, u32[]{:S(2)}, u32[]{:S(2)}) %collective-permute-start.6) | collective-permute-done | bytes 1048608 | tf_op jit(solution)/shard_map/ppermute | solution.py:24
  32.6 1.6 %collective-permute-start.7 = (bf16[1,1024,256]{2,1,0:T(8,128)(2,1)S(1)}, bf16[1,1024,256]{2,1,0:T(8,128)(2,1)S(1)}, u32[]{:S(2)}, u32[]{:S(2)}) collective-permute-start(bf16[1,1024,256]{2,1,0:T(8,128)(2,1)S(1)} %slice.23), channel_id=1, source_target_pairs={{0,16},{8,24},{16,0},{24,8},{1,17},{9,25},{17,1},{25,9},{2,18},{10... | collective-permute-start | bytes 1572872 | tf_op jit(solution)/shard_map/ppermute | solution.py:24
  34.2 12.5 %collective-permute-done.7 = bf16[1,1024,256]{2,1,0:T(8,128)(2,1)S(1)} collective-permute-done((bf16[1,1024,256]{2,1,0:T(8,128)(2,1)S(1)}, bf16[1,1024,256]{2,1,0:T(8,128)(2,1)S(1)}, u32[]{:S(2)}, u32[]{:S(2)}) %collective-permute-start.7) | collective-permute-done | bytes 524320 | tf_op jit(solution)/shard_map/ppermute | solution.py:24
  46.7 1.7 %fusion.2 = (bf16[1024,256]{1,0:T(8,128)(2,1)S(1)}, f32[1024,256]{1,0:T(8,128)}, f32[1024,256]{1,0:T(8,128)}) fusion(f32[1024,256]{1,0:T(8,128)S(1)} %copy-done.16, bf16[1,1024,256]{2,1,0:T(8,128)(2,1)S(1)} %collective-permute-done.7, f32[2,1024,256]{2,1,0:T(8,128)S(1)} %convert_add_fusion, f32[1024,256]{1,0:T(8,128)S(1)} %copy-done.17), kind=kLoop, calls=%fused_computation.7 | loop fusion | flops 2621440 | bytes 6291456 | tf_op jit(solution)/shard_map/convert_element_type | solution.py:297
  48.4 1.5 %collective-permute-start.9 = (bf16[1024,256]{1,0:T(8,128)(2,1)S(1)}, bf16[1024,256]{1,0:T(8,128)(2,1)S(1)}, u32[]{:S(2)}, u32[]{:S(2)}) collective-permute-start(bf16[1024,256]{1,0:T(8,128)(2,1)S(1)} %get-tuple-element.19.refs_7_), channel_id=1, source_target_pairs={{0,16},{8,24},{16,0},{24,8},{1,17},{9,25},{17,1},{25,9},{2,18},{10... | collective-permute-start | bytes 1572872 | tf_op jit(solution)/shard_map/ppermute | solution.py:24
  49.9 2.0 %collective-permute-start.4 = (bf16[128,1024]{1,0:T(8,128)(2,1)S(1)}, bf16[128,1024]{1,0:T(8,128)(2,1)S(1)}, u32[]{:S(2)}, u32[]{:S(2)}) collective-permute-start(bf16[128,1024]{1,0:T(8,128)(2,1)S(1)} %copy-done.5), channel_id=1, source_target_pairs={{0,1},{1,0},{2,3},{3,2},{4,5},{5,4},{6,7},{7,6},{8,9},{9,8},{10,11... | collective-permute-start | bytes 786440 | tf_op jit(solution)/shard_map/ppermute | solution.py:24
  51.9 1.5 %collective-permute-start.5 = (bf16[128,1024]{1,0:T(8,128)(2,1)S(1)}, bf16[128,1024]{1,0:T(8,128)(2,1)}, u32[]{:S(2)}, u32[]{:S(2)}) collective-permute-start(bf16[128,1024]{1,0:T(8,128)(2,1)S(1)} %copy-done.5), channel_id=1, source_target_pairs={{0,2},{1,3},{2,0},{3,1},{4,6},{5,7},{6,4},{7,5},{8,10},{9,11},{10,... | collective-permute-start | bytes 786440 | tf_op jit(solution)/shard_map/ppermute | solution.py:24
  53.3 0.6 collective-permute-start.3
  53.9 11.3 %collective-permute-done.5.refs_6_ = bf16[128,1024]{1,0:T(8,128)(2,1)} collective-permute-done((bf16[128,1024]{1,0:T(8,128)(2,1)S(1)}, bf16[128,1024]{1,0:T(8,128)(2,1)}, u32[]{:S(2)}, u32[]{:S(2)}) %collective-permute-start.5) | collective-permute-done | bytes 262176 | tf_op jit(solution)/shard_map/ppermute | solution.py:24
  65.2 0.7 copy-done.12
  65.9 2.3 %collective-permute-done.3.refs_3_ = bf16[128,1024]{1,0:T(8,128)(2,1)S(1)} collective-permute-done((bf16[128,1024]{1,0:T(8,128)(2,1)S(1)}, bf16[128,1024]{1,0:T(8,128)(2,1)S(1)}, u32[]{:S(2)}, u32[]{:S(2)}) %collective-permute-start.3) | collective-permute-done | bytes 262176 | tf_op jit(solution)/shard_map/ppermute | solution.py:24
  68.2 0.7 copy-done.14
  68.9 0.6 collective-permute-start.10
  69.5 3.3 %all-to-all-done.tokens_ref = bf16[8,1024,128]{2,1,0:T(8,128)(2,1)} async-done(((bf16[8,1024,128]{2,1,0:T(8,128)(2,1)}), bf16[8,1024,128]{2,1,0:T(8,128)(2,1)}, u32[]{:S(2)}, u32[]{:S(2)}) %all-to-all-start) | async-done | bytes 2097184 | tf_op jit(solution)/shard_map/all_to_all | solution.py:285
  72.8 0.9 %copy-done.6 = bf16[128,1024]{1,0:T(8,128)(2,1)S(1)} copy-done((bf16[128,1024]{1,0:T(8,128)(2,1)S(1)}, bf16[128,1024]{1,0:T(8,128)(2,1)}, u32[]{:S(2)}) %copy-start.6) | copy-done | bytes 262168
  73.8 0.9 %copy-done.9 = bf16[128,1024]{1,0:T(8,128)(2,1)S(1)} copy-done((bf16[128,1024]{1,0:T(8,128)(2,1)S(1)}, bf16[128,1024]{1,0:T(8,128)(2,1)}, u32[]{:S(2)}) %copy-start.9) | copy-done | bytes 262168
  74.7 0.9 %copy-done.11 = bf16[128,1024]{1,0:T(8,128)(2,1)S(1)} copy-done((bf16[128,1024]{1,0:T(8,128)(2,1)S(1)}, bf16[128,1024]{1,0:T(8,128)(2,1)}, u32[]{:S(2)}) %copy-start.11) | copy-done | bytes 262168
  75.7 0.9 %copy-done.13 = bf16[128,1024]{1,0:T(8,128)(2,1)S(1)} copy-done((bf16[128,1024]{1,0:T(8,128)(2,1)S(1)}, bf16[128,1024]{1,0:T(8,128)(2,1)}, u32[]{:S(2)}) %copy-start.13) | copy-done | bytes 262168
  76.6 0.9 %copy-done.15 = bf16[128,1024]{1,0:T(8,128)(2,1)S(1)} copy-done((bf16[128,1024]{1,0:T(8,128)(2,1)S(1)}, bf16[128,1024]{1,0:T(8,128)(2,1)}, u32[]{:S(2)}) %copy-start.15) | copy-done | bytes 262168
  77.6 5.0 %accumulate.1 = (f32[1024,1024]{1,0:T(8,128)S(1)}, bf16[1024,128]{1,0:T(8,128)(2,1)S(1)}) custom-call(s32[1]{0:T(128)} %bitcast.1.mine_ref, s32[1]{0:T(128)} %bitcast.own_ref, bf16[8,1024,128]{2,1,0:T(8,128)(2,1)} %all-to-all-done.tokens_ref, bf16[1024,1024]{1,0:T(8,128)(2,1)S(1)} %bitcast.16, bf16[128,1024]{1,0:T(8,128)(2,1)S(1)} %bitcast.21, ...), custom_call_target="tpu_custom_call" | custom-call | flops 1879048192 | bytes 12582912 | tf_op jit(solution)/shard_map/accumulate/pallas_call | solution.py:196
  82.6 3.1 %finish.1 = bf16[1024,1024]{1,0:T(8,128)(2,1)} custom-call(s32[1]{0:T(128)} %bitcast.own_ref, bf16[1024,128]{1,0:T(8,128)(2,1)S(1)} %get-tuple-element.16.tokens_ref, bf16[128,1024]{1,0:T(8,128)(2,1)} %collective-permute-done.10.cotangent_ref, f32[1024,1024]{1,0:T(8,128)S(1)} %get-tuple-element.17.total_ref, bf16[1024,256]{1,0:T(8,128)(2,1)} %collective-permute-done.11.piece_ref), custom_call_target="tpu_custom_call" | custom-call | flops 268435456 | bytes 7864320 | tf_op jit(solution)/shard_map/finish/pallas_call | solution.py:245
  (38 shorter events, 1.3 us)
Async XLA Ops:
  0.6 16.3 %collective-permute-start.2 = (bf16[128,1024]{1,0:T(8,128)(2,1)}, bf16[128,1024]{1,0:T(8,128)(2,1)S(1)}, u32[]{:S(2)}, u32[]{:S(2)}) collective-permute-start(bf16[128,1024]{1,0:T(8,128)(2,1)} %bitcast.18), channel_id=1, source_target_pairs={{0,4},{1,5},{2,6},{3,7},{4,0},{5,1},{6,2},{7,3},{8,12},{9,13},{10,... | collective-permute-start | bytes 786440 | tf_op jit(solution)/shard_map/ppermute | solution.py:24
  4.7 12.4 %collective-permute-start.1 = (bf16[128,1024]{1,0:T(8,128)(2,1)}, bf16[128,1024]{1,0:T(8,128)(2,1)S(1)}, u32[]{:S(2)}, u32[]{:S(2)}) collective-permute-start(bf16[128,1024]{1,0:T(8,128)(2,1)} %bitcast.19), channel_id=1, source_target_pairs={{0,2},{1,3},{2,0},{3,1},{4,6},{5,7},{6,4},{7,5},{8,10},{9,11},{10,... | collective-permute-start | bytes 786440 | tf_op jit(solution)/shard_map/ppermute | solution.py:24
  6.3 10.9 %collective-permute-start = (bf16[128,1024]{1,0:T(8,128)(2,1)}, bf16[128,1024]{1,0:T(8,128)(2,1)S(1)}, u32[]{:S(2)}, u32[]{:S(2)}) collective-permute-start(bf16[128,1024]{1,0:T(8,128)(2,1)} %bitcast.20), channel_id=1, source_target_pairs={{0,1},{1,0},{2,3},{3,2},{4,5},{5,4},{6,7},{7,6},{8,9},{9,8},{10,11... | collective-permute-start | bytes 786440 | tf_op jit(solution)/shard_map/ppermute | solution.py:24
  8.5 1.6 %copy-start.1 = (bf16[1,128,8192]{2,1,0:T(8,128)(2,1)S(1)}, bf16[1,128,8192]{2,1,0:T(8,128)(2,1)}, u32[]{:S(2)}) copy-start(bf16[1,128,8192]{2,1,0:T(8,128)(2,1)} %param.7) | copy-start | bytes 6291460
  17.0 0.7 copy-start.4
  17.2 0.7 copy-start.7
  17.9 0.7 copy-start.10
  18.6 5.7 %copy-start = (bf16[1,1024,1024]{2,1,0:T(8,128)(2,1)S(1)}, bf16[1,1024,1024]{2,1,0:T(8,128)(2,1)}, u32[]{:S(2)}) copy-start(bf16[1,1024,1024]{2,1,0:T(8,128)(2,1)} %param.10) | copy-start | bytes 6291460
  18.6 54.3 %all-to-all-start = ((bf16[8,1024,128]{2,1,0:T(8,128)(2,1)}), bf16[8,1024,128]{2,1,0:T(8,128)(2,1)}, u32[]{:S(2)}, u32[]{:S(2)}) async-start(bf16[8,1024,128]{2,1,0:T(8,128)(2,1)} %prepare.1), calls=%async_computation | async-start | bytes 4194304 | tf_op jit(solution)/shard_map/all_to_all | solution.py:285
  24.3 1.6 %copy-start.2 = (bf16[1024,1024]{1,0:T(8,128)(2,1)S(1)}, bf16[1024,1024]{1,0:T(8,128)(2,1)}, u32[]{:S(2)}) copy-start(bf16[1024,1024]{1,0:T(8,128)(2,1)} %shared_ref) | copy-start | bytes 6291460
  29.6 2.7 %collective-permute-start.6 = (bf16[2,1024,256]{2,1,0:T(8,128)(2,1)S(1)}, bf16[2,1024,256]{2,1,0:T(8,128)(2,1)S(1)}, u32[]{:S(2)}, u32[]{:S(2)}) collective-permute-start(bf16[2,1024,256]{2,1,0:T(8,128)(2,1)S(1)} %get-tuple-element.15), channel_id=1, source_target_pairs={{0,8},{8,0},{16,24},{24,16},{1,9},{9,1},{17,25},{25,17},{2,10},{10... | collective-permute-start | bytes 3145736 | tf_op jit(solution)/shard_map/ppermute | solution.py:24
  32.3 14.4 %copy-start.16 = (f32[1024,256]{1,0:T(8,128)S(1)}, f32[1024,256]{1,0:T(8,128)}, u32[]{:S(2)}) copy-start(f32[1024,256]{1,0:T(8,128)} %param.12) | copy-start | bytes 3145732
  32.3 14.4 %copy-start.17 = (f32[1024,256]{1,0:T(8,128)S(1)}, f32[1024,256]{1,0:T(8,128)}, u32[]{:S(2)}) copy-start(f32[1024,256]{1,0:T(8,128)} %param.13) | copy-start | bytes 3145732
  32.6 17.3 %copy-start.5 = (bf16[128,1024]{1,0:T(8,128)(2,1)S(1)}, bf16[128,1024]{1,0:T(8,128)(2,1)}, u32[]{:S(2)}) copy-start(bf16[128,1024]{1,0:T(8,128)(2,1)} %copy-done.4) | copy-start | bytes 786436
  32.6 20.7 %copy-start.8 = (bf16[128,1024]{1,0:T(8,128)(2,1)S(1)}, bf16[128,1024]{1,0:T(8,128)(2,1)}, u32[]{:S(2)}) copy-start(bf16[128,1024]{1,0:T(8,128)(2,1)} %copy-done.7) | copy-start | bytes 786436
  32.6 40.2 %copy-start.3 = (bf16[1,128,1024]{2,1,0:T(8,128)(2,1)S(1)}, bf16[1,128,1024]{2,1,0:T(8,128)(2,1)}, u32[]{:S(2)}) copy-start(bf16[1,128,1024]{2,1,0:T(8,128)(2,1)} %param.9) | copy-start | bytes 786436
  32.6 14.0 %collective-permute-start.7 = (bf16[1,1024,256]{2,1,0:T(8,128)(2,1)S(1)}, bf16[1,1024,256]{2,1,0:T(8,128)(2,1)S(1)}, u32[]{:S(2)}, u32[]{:S(2)}) collective-permute-start(bf16[1,1024,256]{2,1,0:T(8,128)(2,1)S(1)} %slice.23), channel_id=1, source_target_pairs={{0,16},{8,24},{16,0},{24,8},{1,17},{9,25},{17,1},{25,9},{2,18},{10... | collective-permute-start | bytes 1572872 | tf_op jit(solution)/shard_map/ppermute | solution.py:24
  48.4 20.5 %collective-permute-start.9 = (bf16[1024,256]{1,0:T(8,128)(2,1)S(1)}, bf16[1024,256]{1,0:T(8,128)(2,1)S(1)}, u32[]{:S(2)}, u32[]{:S(2)}) collective-permute-start(bf16[1024,256]{1,0:T(8,128)(2,1)S(1)} %get-tuple-element.19.refs_7_), channel_id=1, source_target_pairs={{0,16},{8,24},{16,0},{24,8},{1,17},{9,25},{17,1},{25,9},{2,18},{10... | collective-permute-start | bytes 1572872 | tf_op jit(solution)/shard_map/ppermute | solution.py:24
  49.9 15.3 %collective-permute-start.4 = (bf16[128,1024]{1,0:T(8,128)(2,1)S(1)}, bf16[128,1024]{1,0:T(8,128)(2,1)S(1)}, u32[]{:S(2)}, u32[]{:S(2)}) collective-permute-start(bf16[128,1024]{1,0:T(8,128)(2,1)S(1)} %copy-done.5), channel_id=1, source_target_pairs={{0,1},{1,0},{2,3},{3,2},{4,5},{5,4},{6,7},{7,6},{8,9},{9,8},{10,11... | collective-permute-start | bytes 786440 | tf_op jit(solution)/shard_map/ppermute | solution.py:24
  51.9 13.3 %collective-permute-start.5 = (bf16[128,1024]{1,0:T(8,128)(2,1)S(1)}, bf16[128,1024]{1,0:T(8,128)(2,1)}, u32[]{:S(2)}, u32[]{:S(2)}) collective-permute-start(bf16[128,1024]{1,0:T(8,128)(2,1)S(1)} %copy-done.5), channel_id=1, source_target_pairs={{0,2},{1,3},{2,0},{3,1},{4,6},{5,7},{6,4},{7,5},{8,10},{9,11},{10,... | collective-permute-start | bytes 786440 | tf_op jit(solution)/shard_map/ppermute | solution.py:24
  53.3 14.9 %collective-permute-start.3 = (bf16[128,1024]{1,0:T(8,128)(2,1)S(1)}, bf16[128,1024]{1,0:T(8,128)(2,1)S(1)}, u32[]{:S(2)}, u32[]{:S(2)}) collective-permute-start(bf16[128,1024]{1,0:T(8,128)(2,1)S(1)} %copy-done.8), channel_id=1, source_target_pairs={{0,1},{1,0},{2,3},{3,2},{4,5},{5,4},{6,7},{7,6},{8,9},{9,8},{10,11... | collective-permute-start | bytes 786440 | tf_op jit(solution)/shard_map/ppermute | solution.py:24
  53.9 15.6 %collective-permute-start.8 = (bf16[1024,256]{1,0:T(8,128)(2,1)S(1)}, bf16[1024,256]{1,0:T(8,128)(2,1)}, u32[]{:S(2)}, u32[]{:S(2)}) collective-permute-start(bf16[1024,256]{1,0:T(8,128)(2,1)S(1)} %get-tuple-element.19.refs_7_), channel_id=1, source_target_pairs={{0,8},{8,0},{16,24},{24,16},{1,9},{9,1},{17,25},{25,17},{2,10},{10... | collective-permute-start | bytes 1572872 | tf_op jit(solution)/shard_map/ppermute | solution.py:24
  65.2 0.7 copy-start.12
  68.2 0.7 copy-start.14
  68.9 13.7 %collective-permute-start.11 = (bf16[1024,256]{1,0:T(8,128)(2,1)S(1)}, bf16[1024,256]{1,0:T(8,128)(2,1)}, u32[]{:S(2)}, u32[]{:S(2)}) collective-permute-start(bf16[1024,256]{1,0:T(8,128)(2,1)S(1)} %collective-permute-done.9.refs_9_), channel_id=1, source_target_pairs={{0,8},{8,0},{16,24},{24,16},{1,9},{9,1},{17,25},{25,17},{2,10},{10... | collective-permute-start | bytes 1572872 | tf_op jit(solution)/shard_map/ppermute | solution.py:24
  68.9 13.7 %collective-permute-start.10 = (bf16[128,1024]{1,0:T(8,128)(2,1)}, bf16[128,1024]{1,0:T(8,128)(2,1)}, u32[]{:S(2)}, u32[]{:S(2)}) collective-permute-start(bf16[128,1024]{1,0:T(8,128)(2,1)} %collective-permute-done.5.refs_6_), channel_id=1, source_target_pairs={{0,1},{1,0},{2,3},{3,2},{4,5},{5,4},{6,7},{7,6},{8,9},{9,8},{10,11... | collective-permute-start | bytes 786440 | tf_op jit(solution)/shard_map/ppermute | solution.py:24
  72.8 1.0 %copy-start.6 = (bf16[128,1024]{1,0:T(8,128)(2,1)S(1)}, bf16[128,1024]{1,0:T(8,128)(2,1)}, u32[]{:S(2)}) copy-start(bf16[128,1024]{1,0:T(8,128)(2,1)} %copy-done.4) | copy-start | bytes 786436
  73.8 0.9 %copy-start.9 = (bf16[128,1024]{1,0:T(8,128)(2,1)S(1)}, bf16[128,1024]{1,0:T(8,128)(2,1)}, u32[]{:S(2)}) copy-start(bf16[128,1024]{1,0:T(8,128)(2,1)} %copy-done.7) | copy-start | bytes 786436
  74.7 0.9 %copy-start.11 = (bf16[128,1024]{1,0:T(8,128)(2,1)S(1)}, bf16[128,1024]{1,0:T(8,128)(2,1)}, u32[]{:S(2)}) copy-start(bf16[128,1024]{1,0:T(8,128)(2,1)} %copy-done.10) | copy-start | bytes 786436
  75.7 0.9 %copy-start.13 = (bf16[128,1024]{1,0:T(8,128)(2,1)S(1)}, bf16[128,1024]{1,0:T(8,128)(2,1)}, u32[]{:S(2)}) copy-start(bf16[128,1024]{1,0:T(8,128)(2,1)} %copy-done.12) | copy-start | bytes 786436
  76.6 0.9 %copy-start.15 = (bf16[128,1024]{1,0:T(8,128)(2,1)S(1)}, bf16[128,1024]{1,0:T(8,128)(2,1)}, u32[]{:S(2)}) copy-start(bf16[128,1024]{1,0:T(8,128)(2,1)} %copy-done.14) | copy-start | bytes 786436

commit v19 on v18

--- a/solution.py
+++ b/solution.py
@@ -209,7 +209,7 @@
             pltpu.SemaphoreType.DMA((groups,)),
             pltpu.SemaphoreType.DMA((2,)),
         ],
-        compiler_params=pltpu.CompilerParams(vmem_limit_bytes=43392 * 2**10),
+        compiler_params=pltpu.CompilerParams(vmem_limit_bytes=58880 * 2**10),
         cost_estimate=pl.CostEstimate(
             flops=2 * depth * parts * rows * width,
             bytes_accessed=2 * depth * shards * (rows + width) + 8 * rows * width,

time: 86.2 us -> 84.7 us (0.983)
  local copies, waits for them, and re-layouts: 10.8 us -> 7.87 us
  waiting for transfers between devices: 36.8 us -> 37.7 us
  Pallas kernels: 14 us -> 14.9 us
    unnamed x36 -> x32, local copies, waits for them, and re-layouts: 10.8 us -> 7.82 us
    pallas_call x1, Pallas kernels: 5.01 us -> 7.05 us  [accumulate(): pl.pallas_call(functools.partial(accumulate_kernel, parts, groups, rate),...]
    pallas_call x1, Pallas kernels: 3.1 us -> 1.95 us  [finish(): pl.pallas_call(functools.partial(finish_kernel, width // share, rate), ou...]
  transfers between devices with their start and end apart: 13 -> 13, of which waited for: 7 -> 7; matrix products, arithmetic and copies ran while one was open for 3% -> 3% of each run, Pallas kernels for 13% -> 15%
where the time goes in v19:
time: 84.7 us; the launch traced here: 84.3 us
  waiting for transfers between devices  37.7 us (45%)
  starting transfers between devices  20.5 us (24%)
  Pallas kernels  14.9 us (18%)
  local copies, waits for them, and re-layouts  7.87 us (9%)
  other arithmetic  2.6 us (3%)
    ppermute x12, waiting for transfers between devices, swap(): return lax.ppermute(value, axis, [(i, i ^ mask) for i in range(size)])  34.3 us
    ppermute x12, starting transfers between devices, swap(): return lax.ppermute(value, axis, [(i, i ^ mask) for i in range(size)])  14.9 us
    unnamed x32, local copies, waits for them, and re-layouts  7.82 us
    pallas_call x1, Pallas kernels, accumulate(): pl.pallas_call(functools.partial(accumulate_kernel, parts, groups, rate),...  7.05 us
    all_to_all x1, starting transfers between devices, on_device(): lax.all_to_all(blocks, 'fsdp', split_axis=0, concat_axis=0, tiled=True)  5.61 us
    pallas_call x1, Pallas kernels, code_and_decode(): pl.pallas_call(code_kernel, out_shape=(half, half), in_specs=[pl.BlockSpe...  3.69 us
    all_to_all x1, waiting for transfers between devices, on_device(): lax.all_to_all(blocks, 'fsdp', split_axis=0, concat_axis=0, tiled=True)  3.44 us
    pallas_call x1, Pallas kernels, prepare(): pl.pallas_call(prepare_kernel, out_shape=jax.ShapeDtypeStruct((shards, ro...  2.21 us
  transfers between devices with their start and end apart: 13, of which 7 were waited for; matrix products, arithmetic and copies ran while one was open for 3% of the time, Pallas kernels for 15%

profile of v19, /device:TPU:0, one launch (start us, length us, event | category | flops | bytes accessed | tf_op | source)
XLA Modules:
  0.0 84.3 jit_solution(2490964186665329309)
XLA Ops:
  0.6 4.1 %collective-permute-start.2 = (bf16[128,1024]{1,0:T(8,128)(2,1)}, bf16[128,1024]{1,0:T(8,128)(2,1)S(1)}, u32[]{:S(2)}, u32[]{:S(2)}) collective-permute-start(bf16[128,1024]{1,0:T(8,128)(2,1)} %bitcast.20), channel_id=1, source_target_pairs={{0,4},{1,5},{2,6},{3,7},{4,0},{5,1},{6,2},{7,3},{8,12},{9,13},{10,... | collective-permute-start | bytes 786440 | tf_op jit(solution)/shard_map/ppermute | solution.py:24
  4.7 1.6 %collective-permute-start.1 = (bf16[128,1024]{1,0:T(8,128)(2,1)}, bf16[128,1024]{1,0:T(8,128)(2,1)S(1)}, u32[]{:S(2)}, u32[]{:S(2)}) collective-permute-start(bf16[128,1024]{1,0:T(8,128)(2,1)} %bitcast.21), channel_id=1, source_target_pairs={{0,2},{1,3},{2,0},{3,1},{4,6},{5,7},{6,4},{7,5},{8,10},{9,11},{10,... | collective-permute-start | bytes 786440 | tf_op jit(solution)/shard_map/ppermute | solution.py:24
  6.3 1.5 %collective-permute-start = (bf16[128,1024]{1,0:T(8,128)(2,1)}, bf16[128,1024]{1,0:T(8,128)(2,1)S(1)}, u32[]{:S(2)}, u32[]{:S(2)}) collective-permute-start(bf16[128,1024]{1,0:T(8,128)(2,1)} %bitcast.22), channel_id=1, source_target_pairs={{0,1},{1,0},{2,3},{3,2},{4,5},{5,4},{6,7},{7,6},{8,9},{9,8},{10,11... | collective-permute-start | bytes 786440 | tf_op jit(solution)/shard_map/ppermute | solution.py:24
  7.8 0.7 reshape.25
  8.6 1.6 %copy-done.2 = bf16[1,128,8192]{2,1,0:T(8,128)(2,1)S(1)} copy-done((bf16[1,128,8192]{2,1,0:T(8,128)(2,1)S(1)}, bf16[1,128,8192]{2,1,0:T(8,128)(2,1)}, u32[]{:S(2)}) %copy-start.2) | copy-done | bytes 2097176
  10.1 2.2 %prepare.1 = bf16[8,1024,128]{2,1,0:T(8,128)(2,1)} custom-call(bf16[128,8192]{1,0:T(8,128)(2,1)S(1)} %bitcast.17, f32[1,8192]{1,0:T(1,128)S(1)} %bitcast.18), custom_call_target="tpu_custom_call" | custom-call | flops 5242880 | bytes 4194304 | tf_op jit(solution)/shard_map/prepare/pallas_call | solution.py:58
  12.4 4.6 %collective-permute-done.2.refs_4_ = bf16[128,1024]{1,0:T(8,128)(2,1)S(1)} collective-permute-done((bf16[128,1024]{1,0:T(8,128)(2,1)}, bf16[128,1024]{1,0:T(8,128)(2,1)S(1)}, u32[]{:S(2)}, u32[]{:S(2)}) %collective-permute-start.2) | collective-permute-done | bytes 262176 | tf_op jit(solution)/shard_map/ppermute | solution.py:24
  17.0 0.2 collective-permute-done.1.refs_2_
  17.2 0.8 copy-done.12
  17.9 5.6 %all-to-all-start = ((bf16[8,1024,128]{2,1,0:T(8,128)(2,1)}), bf16[8,1024,128]{2,1,0:T(8,128)(2,1)}, u32[]{:S(2)}, u32[]{:S(2)}) async-start(bf16[8,1024,128]{2,1,0:T(8,128)(2,1)} %prepare.1), calls=%async_computation | async-start | bytes 4194304 | tf_op jit(solution)/shard_map/all_to_all | solution.py:285
  23.6 1.6 %copy-done.3 = bf16[1024,1024]{1,0:T(8,128)(2,1)S(1)} copy-done((bf16[1024,1024]{1,0:T(8,128)(2,1)S(1)}, bf16[1024,1024]{1,0:T(8,128)(2,1)}, u32[]{:S(2)}) %copy-start.3) | copy-done | bytes 2097176
  25.1 3.7 %code_and_decode.1 = (bf16[2,1024,256]{2,1,0:T(8,128)(2,1)S(1)}, bf16[2,1024,256]{2,1,0:T(8,128)(2,1)S(1)}) custom-call(s32[1]{0:T(128)} %bitcast.own_ref, bf16[1024,1024]{1,0:T(8,128)(2,1)S(1)} %copy-done.3, bf16[1024,1024]{1,0:T(8,128)(2,1)S(1)} %bitcast.16), custom_call_target="tpu_custom_call" | custom-call | flops 20971520 | bytes 6291456 | tf_op jit(solution)/shard_map/code_and_decode/pallas_call | solution.py:128
  28.8 0.1 collective-permute-start.6
  28.9 2.6 %collective-permute-done.6 = bf16[2,1024,256]{2,1,0:T(8,128)(2,1)S(1)} collective-permute-done((bf16[2,1024,256]{2,1,0:T(8,128)(2,1)S(1)}, bf16[2,1024,256]{2,1,0:T(8,128)(2,1)S(1)}, u32[]{:S(2)}, u32[]{:S(2)}) %collective-permute-start.6) | collective-permute-done | bytes 1048608 | tf_op jit(solution)/shard_map/ppermute | solution.py:24
  31.6 0.2 convert_add_fusion
  31.8 0.1 slice.23
  31.9 1.6 %collective-permute-start.7 = (bf16[1,1024,256]{2,1,0:T(8,128)(2,1)S(1)}, bf16[1,1024,256]{2,1,0:T(8,128)(2,1)S(1)}, u32[]{:S(2)}, u32[]{:S(2)}) collective-permute-start(bf16[1,1024,256]{2,1,0:T(8,128)(2,1)S(1)} %slice.23), channel_id=1, source_target_pairs={{0,16},{8,24},{16,0},{24,8},{1,17},{9,25},{17,1},{25,9},{2,18},{10... | collective-permute-start | bytes 1572872 | tf_op jit(solution)/shard_map/ppermute | solution.py:24
  33.4 12.5 %collective-permute-done.7 = bf16[1,1024,256]{2,1,0:T(8,128)(2,1)S(1)} collective-permute-done((bf16[1,1024,256]{2,1,0:T(8,128)(2,1)S(1)}, bf16[1,1024,256]{2,1,0:T(8,128)(2,1)S(1)}, u32[]{:S(2)}, u32[]{:S(2)}) %collective-permute-start.7) | collective-permute-done | bytes 524320 | tf_op jit(solution)/shard_map/ppermute | solution.py:24
  45.9 1.7 %fusion.2 = (bf16[1024,256]{1,0:T(8,128)(2,1)S(1)}, f32[1024,256]{1,0:T(8,128)}, f32[1024,256]{1,0:T(8,128)}) fusion(f32[1024,256]{1,0:T(8,128)S(1)} %copy-done.6, bf16[1,1024,256]{2,1,0:T(8,128)(2,1)S(1)} %collective-permute-done.7, f32[2,1024,256]{2,1,0:T(8,128)S(1)} %convert_add_fusion, f32[1024,256]{1,0:T(8,128)S(1)} %copy-done.7), kind=kLoop, calls=%fused_computation.7 | loop fusion | flops 2621440 | bytes 6291456 | tf_op jit(solution)/shard_map/convert_element_type | solution.py:297
  47.6 1.5 %collective-permute-start.9 = (bf16[1024,256]{1,0:T(8,128)(2,1)S(1)}, bf16[1024,256]{1,0:T(8,128)(2,1)S(1)}, u32[]{:S(2)}, u32[]{:S(2)}) collective-permute-start(bf16[1024,256]{1,0:T(8,128)(2,1)S(1)} %get-tuple-element.19.refs_7_), channel_id=1, source_target_pairs={{0,16},{8,24},{16,0},{24,8},{1,17},{9,25},{17,1},{25,9},{2,18},{10... | collective-permute-start | bytes 1572872 | tf_op jit(solution)/shard_map/ppermute | solution.py:24
  49.1 2.0 %collective-permute-start.4 = (bf16[128,1024]{1,0:T(8,128)(2,1)S(1)}, bf16[128,1024]{1,0:T(8,128)(2,1)S(1)}, u32[]{:S(2)}, u32[]{:S(2)}) collective-permute-start(bf16[128,1024]{1,0:T(8,128)(2,1)S(1)} %collective-permute-done.2.refs_4_), channel_id=1, source_target_pairs={{0,1},{1,0},{2,3},{3,2},{4,5},{5,4},{6,7},{7,6},{8,9},{9,8},{10,11... | collective-permute-start | bytes 786440 | tf_op jit(solution)/shard_map/ppermute | solution.py:24
  51.1 1.5 %collective-permute-start.5 = (bf16[128,1024]{1,0:T(8,128)(2,1)S(1)}, bf16[128,1024]{1,0:T(8,128)(2,1)S(1)}, u32[]{:S(2)}, u32[]{:S(2)}) collective-permute-start(bf16[128,1024]{1,0:T(8,128)(2,1)S(1)} %collective-permute-done.2.refs_4_), channel_id=1, source_target_pairs={{0,2},{1,3},{2,0},{3,1},{4,6},{5,7},{6,4},{7,5},{8,10},{9,11},{10,... | collective-permute-start | bytes 786440 | tf_op jit(solution)/shard_map/ppermute | solution.py:24
  52.5 0.6 collective-permute-start.3
  53.1 11.3 %collective-permute-done.5.refs_6_ = bf16[128,1024]{1,0:T(8,128)(2,1)S(1)} collective-permute-done((bf16[128,1024]{1,0:T(8,128)(2,1)S(1)}, bf16[128,1024]{1,0:T(8,128)(2,1)S(1)}, u32[]{:S(2)}, u32[]{:S(2)}) %collective-permute-start.5) | collective-permute-done | bytes 262176 | tf_op jit(solution)/shard_map/ppermute | solution.py:24
  64.5 3.0 %collective-permute-done.3.refs_3_ = bf16[128,1024]{1,0:T(8,128)(2,1)S(1)} collective-permute-done((bf16[128,1024]{1,0:T(8,128)(2,1)S(1)}, bf16[128,1024]{1,0:T(8,128)(2,1)S(1)}, u32[]{:S(2)}, u32[]{:S(2)}) %collective-permute-start.3) | collective-permute-done | bytes 262176 | tf_op jit(solution)/shard_map/ppermute | solution.py:24
  67.4 0.7 copy-done.15
  68.2 0.5 collective-permute-start.10
  68.7 3.4 %all-to-all-done.tokens_ref = bf16[8,1024,128]{2,1,0:T(8,128)(2,1)} async-done(((bf16[8,1024,128]{2,1,0:T(8,128)(2,1)}), bf16[8,1024,128]{2,1,0:T(8,128)(2,1)}, u32[]{:S(2)}, u32[]{:S(2)}) %all-to-all-start) | async-done | bytes 2097184 | tf_op jit(solution)/shard_map/all_to_all | solution.py:285
  72.2 7.0 %accumulate.1 = (f32[1024,1024]{1,0:T(8,128)}, bf16[1024,128]{1,0:T(8,128)(2,1)}) custom-call(s32[1]{0:T(128)} %bitcast.1.mine_ref, s32[1]{0:T(128)} %bitcast.own_ref, bf16[8,1024,128]{2,1,0:T(8,128)(2,1)} %all-to-all-done.tokens_ref, bf16[1024,1024]{1,0:T(8,128)(2,1)} %bitcast.15, bf16[128,1024]{1,0:T(8,128)(2,1)} %bitcast.23, ...), custom_call_target="tpu_custom_call" | custom-call | flops 1879048192 | bytes 12582912 | tf_op jit(solution)/shard_map/accumulate/pallas_call | solution.py:196
  79.2 2.2 %copy-done.1 = f32[1024,1024]{1,0:T(8,128)S(1)} copy-done((f32[1024,1024]{1,0:T(8,128)S(1)}, f32[1024,1024]{1,0:T(8,128)}, u32[]{:S(2)}) %copy-start.1) | copy-done | bytes 4194328
  81.4 0.9 %copy-done.4 = bf16[1024,128]{1,0:T(8,128)(2,1)S(1)} copy-done((bf16[1024,128]{1,0:T(8,128)(2,1)S(1)}, bf16[1024,128]{1,0:T(8,128)(2,1)}, u32[]{:S(2)}) %copy-start.4) | copy-done | bytes 262168
  82.4 1.9 %finish.1 = bf16[1024,1024]{1,0:T(8,128)(2,1)} custom-call(s32[1]{0:T(128)} %bitcast.own_ref, bf16[1024,128]{1,0:T(8,128)(2,1)S(1)} %copy-done.4, bf16[128,1024]{1,0:T(8,128)(2,1)S(1)} %collective-permute-done.10.cotangent_ref, f32[1024,1024]{1,0:T(8,128)S(1)} %copy-done.1, bf16[1024,256]{1,0:T(8,128)(2,1)S(1)} %collective-permute-done.11.piece_ref), custom_call_target="tpu_custom_call" | custom-call | flops 268435456 | bytes 7864320 | tf_op jit(solution)/shard_map/finish/pallas_call | solution.py:245
  (34 shorter events, 0.1 us)
Async XLA Ops:
  0.6 16.3 %collective-permute-start.2 = (bf16[128,1024]{1,0:T(8,128)(2,1)}, bf16[128,1024]{1,0:T(8,128)(2,1)S(1)}, u32[]{:S(2)}, u32[]{:S(2)}) collective-permute-start(bf16[128,1024]{1,0:T(8,128)(2,1)} %bitcast.20), channel_id=1, source_target_pairs={{0,4},{1,5},{2,6},{3,7},{4,0},{5,1},{6,2},{7,3},{8,12},{9,13},{10,... | collective-permute-start | bytes 786440 | tf_op jit(solution)/shard_map/ppermute | solution.py:24
  4.7 12.4 %collective-permute-start.1 = (bf16[128,1024]{1,0:T(8,128)(2,1)}, bf16[128,1024]{1,0:T(8,128)(2,1)S(1)}, u32[]{:S(2)}, u32[]{:S(2)}) collective-permute-start(bf16[128,1024]{1,0:T(8,128)(2,1)} %bitcast.21), channel_id=1, source_target_pairs={{0,2},{1,3},{2,0},{3,1},{4,6},{5,7},{6,4},{7,5},{8,10},{9,11},{10,... | collective-permute-start | bytes 786440 | tf_op jit(solution)/shard_map/ppermute | solution.py:24
  6.3 10.9 %collective-permute-start = (bf16[128,1024]{1,0:T(8,128)(2,1)}, bf16[128,1024]{1,0:T(8,128)(2,1)S(1)}, u32[]{:S(2)}, u32[]{:S(2)}) collective-permute-start(bf16[128,1024]{1,0:T(8,128)(2,1)} %bitcast.22), channel_id=1, source_target_pairs={{0,1},{1,0},{2,3},{3,2},{4,5},{5,4},{6,7},{7,6},{8,9},{9,8},{10,11... | collective-permute-start | bytes 786440 | tf_op jit(solution)/shard_map/ppermute | solution.py:24
  8.5 1.6 %copy-start.2 = (bf16[1,128,8192]{2,1,0:T(8,128)(2,1)S(1)}, bf16[1,128,8192]{2,1,0:T(8,128)(2,1)}, u32[]{:S(2)}) copy-start(bf16[1,128,8192]{2,1,0:T(8,128)(2,1)} %param.7) | copy-start | bytes 6291460
  17.0 34.1 %copy-start.10 = (bf16[128,1024]{1,0:T(8,128)(2,1)}, bf16[128,1024]{1,0:T(8,128)(2,1)S(1)}, u32[]{:S(2)}) copy-start(bf16[128,1024]{1,0:T(8,128)(2,1)S(1)} %collective-permute-done.2.refs_4_) | copy-start | bytes 786436
  17.2 35.4 %copy-start.11 = (bf16[128,1024]{1,0:T(8,128)(2,1)}, bf16[128,1024]{1,0:T(8,128)(2,1)S(1)}, u32[]{:S(2)}) copy-start(bf16[128,1024]{1,0:T(8,128)(2,1)S(1)} %collective-permute-done.1.refs_2_) | copy-start | bytes 786436
  17.2 0.8 copy-start.12
  17.2 6.4 %copy-start = (bf16[1,1024,1024]{2,1,0:T(8,128)(2,1)S(1)}, bf16[1,1024,1024]{2,1,0:T(8,128)(2,1)}, u32[]{:S(2)}) copy-start(bf16[1,1024,1024]{2,1,0:T(8,128)(2,1)} %param.10) | copy-start | bytes 6291460
  17.9 54.2 %all-to-all-start = ((bf16[8,1024,128]{2,1,0:T(8,128)(2,1)}), bf16[8,1024,128]{2,1,0:T(8,128)(2,1)}, u32[]{:S(2)}, u32[]{:S(2)}) async-start(bf16[8,1024,128]{2,1,0:T(8,128)(2,1)} %prepare.1), calls=%async_computation | async-start | bytes 4194304 | tf_op jit(solution)/shard_map/all_to_all | solution.py:285
  23.6 1.6 %copy-start.3 = (bf16[1024,1024]{1,0:T(8,128)(2,1)S(1)}, bf16[1024,1024]{1,0:T(8,128)(2,1)}, u32[]{:S(2)}) copy-start(bf16[1024,1024]{1,0:T(8,128)(2,1)} %shared_ref) | copy-start | bytes 6291460
  28.8 2.7 %collective-permute-start.6 = (bf16[2,1024,256]{2,1,0:T(8,128)(2,1)S(1)}, bf16[2,1024,256]{2,1,0:T(8,128)(2,1)S(1)}, u32[]{:S(2)}, u32[]{:S(2)}) collective-permute-start(bf16[2,1024,256]{2,1,0:T(8,128)(2,1)S(1)} %get-tuple-element.15), channel_id=1, source_target_pairs={{0,8},{8,0},{16,24},{24,16},{1,9},{9,1},{17,25},{25,17},{2,10},{10... | collective-permute-start | bytes 3145736 | tf_op jit(solution)/shard_map/ppermute | solution.py:24
  31.6 14.3 %copy-start.6 = (f32[1024,256]{1,0:T(8,128)S(1)}, f32[1024,256]{1,0:T(8,128)}, u32[]{:S(2)}) copy-start(f32[1024,256]{1,0:T(8,128)} %param.12) | copy-start | bytes 3145732
  31.6 14.3 %copy-start.7 = (f32[1024,256]{1,0:T(8,128)S(1)}, f32[1024,256]{1,0:T(8,128)}, u32[]{:S(2)}) copy-start(f32[1024,256]{1,0:T(8,128)} %param.13) | copy-start | bytes 3145732
  31.9 14.0 %collective-permute-start.7 = (bf16[1,1024,256]{2,1,0:T(8,128)(2,1)S(1)}, bf16[1,1024,256]{2,1,0:T(8,128)(2,1)S(1)}, u32[]{:S(2)}, u32[]{:S(2)}) collective-permute-start(bf16[1,1024,256]{2,1,0:T(8,128)(2,1)S(1)} %slice.23), channel_id=1, source_target_pairs={{0,16},{8,24},{16,0},{24,8},{1,17},{9,25},{17,1},{25,9},{2,18},{10... | collective-permute-start | bytes 1572872 | tf_op jit(solution)/shard_map/ppermute | solution.py:24
  47.6 24.6 %copy-start.5 = (bf16[1024,256]{1,0:T(8,128)(2,1)}, bf16[1024,256]{1,0:T(8,128)(2,1)S(1)}, u32[]{:S(2)}) copy-start(bf16[1024,256]{1,0:T(8,128)(2,1)S(1)} %get-tuple-element.19.refs_7_) | copy-start | bytes 1572868
  47.6 19.9 %collective-permute-start.9 = (bf16[1024,256]{1,0:T(8,128)(2,1)S(1)}, bf16[1024,256]{1,0:T(8,128)(2,1)S(1)}, u32[]{:S(2)}, u32[]{:S(2)}) collective-permute-start(bf16[1024,256]{1,0:T(8,128)(2,1)S(1)} %get-tuple-element.19.refs_7_), channel_id=1, source_target_pairs={{0,16},{8,24},{16,0},{24,8},{1,17},{9,25},{17,1},{25,9},{2,18},{10... | collective-permute-start | bytes 1572872 | tf_op jit(solution)/shard_map/ppermute | solution.py:24
  49.1 15.4 %collective-permute-start.4 = (bf16[128,1024]{1,0:T(8,128)(2,1)S(1)}, bf16[128,1024]{1,0:T(8,128)(2,1)S(1)}, u32[]{:S(2)}, u32[]{:S(2)}) collective-permute-start(bf16[128,1024]{1,0:T(8,128)(2,1)S(1)} %collective-permute-done.2.refs_4_), channel_id=1, source_target_pairs={{0,1},{1,0},{2,3},{3,2},{4,5},{5,4},{6,7},{7,6},{8,9},{9,8},{10,11... | collective-permute-start | bytes 786440 | tf_op jit(solution)/shard_map/ppermute | solution.py:24
  51.1 13.4 %collective-permute-start.5 = (bf16[128,1024]{1,0:T(8,128)(2,1)S(1)}, bf16[128,1024]{1,0:T(8,128)(2,1)S(1)}, u32[]{:S(2)}, u32[]{:S(2)}) collective-permute-start(bf16[128,1024]{1,0:T(8,128)(2,1)S(1)} %collective-permute-done.2.refs_4_), channel_id=1, source_target_pairs={{0,2},{1,3},{2,0},{3,1},{4,6},{5,7},{6,4},{7,5},{8,10},{9,11},{10,... | collective-permute-start | bytes 786440 | tf_op jit(solution)/shard_map/ppermute | solution.py:24
  52.5 14.9 %collective-permute-start.3 = (bf16[128,1024]{1,0:T(8,128)(2,1)S(1)}, bf16[128,1024]{1,0:T(8,128)(2,1)S(1)}, u32[]{:S(2)}, u32[]{:S(2)}) collective-permute-start(bf16[128,1024]{1,0:T(8,128)(2,1)S(1)} %collective-permute-done.1.refs_2_), channel_id=1, source_target_pairs={{0,1},{1,0},{2,3},{3,2},{4,5},{5,4},{6,7},{7,6},{8,9},{9,8},{10,11... | collective-permute-start | bytes 786440 | tf_op jit(solution)/shard_map/ppermute | solution.py:24
  53.1 15.6 %collective-permute-start.8 = (bf16[1024,256]{1,0:T(8,128)(2,1)S(1)}, bf16[1024,256]{1,0:T(8,128)(2,1)S(1)}, u32[]{:S(2)}, u32[]{:S(2)}) collective-permute-start(bf16[1024,256]{1,0:T(8,128)(2,1)S(1)} %get-tuple-element.19.refs_7_), channel_id=1, source_target_pairs={{0,8},{8,0},{16,24},{24,16},{1,9},{9,1},{17,25},{25,17},{2,10},{10... | collective-permute-start | bytes 1572872 | tf_op jit(solution)/shard_map/ppermute | solution.py:24
  64.5 7.7 %copy-start.14 = (bf16[128,1024]{1,0:T(8,128)(2,1)}, bf16[128,1024]{1,0:T(8,128)(2,1)S(1)}, u32[]{:S(2)}) copy-start(bf16[128,1024]{1,0:T(8,128)(2,1)S(1)} %collective-permute-done.5.refs_6_) | copy-start | bytes 786436
  64.5 7.7 %copy-start.13 = (bf16[128,1024]{1,0:T(8,128)(2,1)}, bf16[128,1024]{1,0:T(8,128)(2,1)S(1)}, u32[]{:S(2)}) copy-start(bf16[128,1024]{1,0:T(8,128)(2,1)S(1)} %collective-permute-done.4.refs_5_) | copy-start | bytes 786436
  67.4 0.7 copy-start.15
  68.2 4.0 %copy-start.8 = (bf16[1024,256]{1,0:T(8,128)(2,1)}, bf16[1024,256]{1,0:T(8,128)(2,1)S(1)}, u32[]{:S(2)}) copy-start(bf16[1024,256]{1,0:T(8,128)(2,1)S(1)} %collective-permute-done.9.refs_9_) | copy-start | bytes 1572868
  68.2 11.1 %collective-permute-start.11 = (bf16[1024,256]{1,0:T(8,128)(2,1)S(1)}, bf16[1024,256]{1,0:T(8,128)(2,1)S(1)}, u32[]{:S(2)}, u32[]{:S(2)}) collective-permute-start(bf16[1024,256]{1,0:T(8,128)(2,1)S(1)} %collective-permute-done.9.refs_9_), channel_id=1, source_target_pairs={{0,8},{8,0},{16,24},{24,16},{1,9},{9,1},{17,25},{25,17},{2,10},{10... | collective-permute-start | bytes 1572872 | tf_op jit(solution)/shard_map/ppermute | solution.py:24
  68.2 11.0 %collective-permute-start.10 = (bf16[128,1024]{1,0:T(8,128)(2,1)S(1)}, bf16[128,1024]{1,0:T(8,128)(2,1)S(1)}, u32[]{:S(2)}, u32[]{:S(2)}) collective-permute-start(bf16[128,1024]{1,0:T(8,128)(2,1)S(1)} %collective-permute-done.5.refs_6_), channel_id=1, source_target_pairs={{0,1},{1,0},{2,3},{3,2},{4,5},{5,4},{6,7},{7,6},{8,9},{9,8},{10,11... | collective-permute-start | bytes 786440 | tf_op jit(solution)/shard_map/ppermute | solution.py:24
  68.7 3.5 %copy-start.9 = (bf16[1024,256]{1,0:T(8,128)(2,1)}, bf16[1024,256]{1,0:T(8,128)(2,1)S(1)}, u32[]{:S(2)}) copy-start(bf16[1024,256]{1,0:T(8,128)(2,1)S(1)} %collective-permute-done.8.refs_8_) | copy-start | bytes 1572868
  79.2 2.2 %copy-start.1 = (f32[1024,1024]{1,0:T(8,128)S(1)}, f32[1024,1024]{1,0:T(8,128)}, u32[]{:S(2)}) copy-start(f32[1024,1024]{1,0:T(8,128)} %get-tuple-element.17.total_ref) | copy-start | bytes 12582916
  81.4 0.9 %copy-start.4 = (bf16[1024,128]{1,0:T(8,128)(2,1)S(1)}, bf16[1024,128]{1,0:T(8,128)(2,1)}, u32[]{:S(2)}) copy-start(bf16[1024,128]{1,0:T(8,128)(2,1)} %get-tuple-element.16.tokens_ref) | copy-start | bytes 786436

commit v20 on v8

--- a/solution.py
+++ b/solution.py
@@ -142,73 +142,97 @@
     )(own.reshape(1), shared, weight)
 
 
-def mix_kernel(shards, groups, rate, place_ref, *refs):
-    tokens_ref, refs = refs[0], refs[1:]
+def mix_kernel(shards, groups, rate, mine_ref, own_ref, tokens_ref, weight_ref, *refs):
     cotangent_refs, refs = refs[:shards], refs[shards:]
     piece_refs, refs = refs[:groups], refs[groups:]
-    weight_ref, out_ref, cotangents, pieces, outs, out_sems = refs
-    mine, own = place_ref[0], place_ref[1]
+    out_ref, tokens, cotangents, weight, pieces, totals, outs, token_sems, cotangent_sems, piece_sems, weight_sem, out_sems = refs
+    mine, own = mine_ref[0], own_ref[0]
     depth, width = cotangent_refs[0].shape
     share = pieces.shape[2]
-    tile = outs.shape[2]
+    steps, _, tile = outs.shape
+
+    loads, rest = [], []
     for k, ref in enumerate(cotangent_refs):
-        cotangents[mine ^ k] = ref[...]
+        loads.append(pltpu.make_async_copy(tokens_ref.at[mine ^ k], tokens.at[k], token_sems.at[k]))
+        loads.append(pltpu.make_async_copy(ref, cotangents.at[pl.ds(k * depth, depth)], cotangent_sems.at[k]))
+    rest.append(pltpu.make_async_copy(weight_ref, weight, weight_sem))
     for k, ref in enumerate(piece_refs):
-        pieces[own ^ k] = ref[...]
-    left = jnp.concatenate([tokens_ref[k] for k in range(shards)], axis=1)
+        rest.append(pltpu.make_async_copy(ref, pieces.at[own ^ k], piece_sems.at[k]))
+    for load in loads + rest:
+        load.start()
     stores = []
-    for step in range(width // tile):
-        columns = slice(step * tile, (step + 1) * tile)
-        right = jnp.concatenate([cotangents[k, :, columns] for k in range(shards)], axis=0)
-        total = jnp.dot(left, right, preferred_element_type=jnp.float32)
-        for group in range(step * tile // share, (step + 1) * tile // share):
-            place = slice(group * share, (group + 1) * share)
-            part = slice(group * share - step * tile, (group + 1) * share - step * tile)
-            mixed = weight_ref[:, place].astype(jnp.float32) + pieces[group].astype(jnp.float32)
-            outs[step, :, part] = (mix_weight * mixed - rate * total[:, part]).astype(jnp.bfloat16)
-        stores.append(pltpu.make_async_copy(outs.at[step], out_ref.at[:, pl.ds(step * tile, tile)], out_sems.at[step]))
-        stores[-1].start()
+    some = 2
+    for first in range(0, shards, some):
+        end = first + some
+        for load in loads[2 * first : 2 * end]:
+            load.wait()
+        if end == shards:
+            for load in rest:
+                load.wait()
+        left = jnp.concatenate([tokens[k] for k in range(first, end)], axis=1)
+        for step in range(steps):
+            columns = slice(step * tile, (step + 1) * tile)
+            right = cotangents[first * depth : end * depth, columns]
+            total = jnp.dot(left, right, preferred_element_type=jnp.float32)
+            if first:
+                total = totals[step] + total
+            if end < shards:
+                totals[step] = total
+                continue
+            for group in range(step * tile // share, (step + 1) * tile // share):
+                place = slice(group * share, (group + 1) * share)
+                part = slice(group * share - step * tile, (group + 1) * share - step * tile)
+                mixed = weight[:, place].astype(jnp.float32) + pieces[group].astype(jnp.float32)
+                outs[step, :, part] = (mix_weight * mixed - rate * total[:, part]).astype(jnp.bfloat16)
+            place = pl.ds(step * tile, tile)
+            stores.append(pltpu.make_async_copy(outs.at[step], out_ref.at[:, place], out_sems.at[step]))
+            stores[step].start()
     for store in stores:
         store.wait()
 
 
-def mix(mine, own, tokens, cotangents, pieces, weight, rate):
+def mix(mine, own, tokens, cotangents, weight, pieces, rate):
     shards, rows, depth = tokens.shape
+    groups = len(pieces)
     width = weight.shape[1]
-    groups = len(pieces)
     share = width // groups
     tile = max(share, 256)
+    remote = pl.BlockSpec(memory_space=pltpu.HBM)
     return pl.pallas_call(
         functools.partial(mix_kernel, shards, groups, rate),
         out_shape=jax.ShapeDtypeStruct((rows, width), jnp.bfloat16),
-        in_specs=[pl.BlockSpec(memory_space=pltpu.SMEM)]
-        + [pl.BlockSpec(memory_space=pltpu.VMEM)] * (2 + shards + groups),
-        out_specs=pl.BlockSpec(memory_space=pltpu.HBM),
+        in_specs=[pl.BlockSpec(memory_space=pltpu.SMEM)] * 2 + [remote] * (2 + shards + groups),
+        out_specs=remote,
         scratch_shapes=[
-            pltpu.VMEM((shards, depth, width), jnp.bfloat16),
+            pltpu.VMEM((shards, rows, depth), jnp.bfloat16),
+            pltpu.VMEM((shards * depth, width), jnp.bfloat16),
+            pltpu.VMEM((rows, width), jnp.bfloat16),
             pltpu.VMEM((groups, rows, share), jnp.bfloat16),
+            pltpu.VMEM((width // tile, rows, tile), jnp.float32),
             pltpu.VMEM((width // tile, rows, tile), jnp.bfloat16),
+            pltpu.SemaphoreType.DMA((shards,)),
+            pltpu.SemaphoreType.DMA((shards,)),
+            pltpu.SemaphoreType.DMA((groups,)),
+            pltpu.SemaphoreType.DMA,
             pltpu.SemaphoreType.DMA((width // tile,)),
         ],
-        compiler_params=pltpu.CompilerParams(vmem_limit_bytes=24 * 2**20),
+        compiler_params=pltpu.CompilerParams(vmem_limit_bytes=58 * 2**20),
         cost_estimate=pl.CostEstimate(
             flops=2 * depth * shards * rows * width,
             bytes_accessed=2 * depth * shards * (rows + width) + 6 * rows * width,
             transcendentals=0,
         ),
         name="mix",
-    )(jnp.stack([mine, own]), tokens, *cotangents, *pieces, weight)
+    )(mine.reshape(1), own.reshape(1), tokens, weight, *cotangents, *pieces)
 
 
 def gather(piece, axis, size, after=()):
     pieces = {0: piece}
     bit = size // 2
     while bit:
-        if bit == 1 and after:
-            (*held, _) = lax.optimization_barrier((*(pieces[k] for k in sorted(pieces)[1:]), after))
-            pieces.update(zip(sorted(pieces)[1:], held))
         for k in sorted(pieces):
-            pieces[k ^ bit] = swap(pieces[k], axis, bit)
+            value = lax.optimization_barrier((pieces[k], *after))[0] if k and bit == 1 else pieces[k]
+            pieces[k ^ bit] = swap(value, axis, bit)
         bit //= 2
     return [pieces[k] for k in range(size)]
 
@@ -236,15 +260,14 @@
     while bit < groups:
         sent = swap(total[1::2].astype(jnp.bfloat16), "replica", bit)
         bit *= 2
-        if bit >= groups:
-            *_, sent = lax.optimization_barrier((*cotangents[: shards // 2 + 2], sent))
         total = total[0::2] + sent.astype(jnp.float32)
     average = total[0] / groups
     momentum_next = outer_beta * momentum + average
     master_next = master - outer_rate * (average + outer_beta * momentum_next)
-    pieces = gather(master_next.astype(jnp.bfloat16), "replica", groups, after=cotangents)
-
-    layer_next = mix(mine, own, columns, cotangents, pieces, weight, (1.0 - mix_weight) * inner_rate)
+    pieces = gather(master_next.astype(jnp.bfloat16), "replica", groups, after=(cotangents[shards // 2 - 1], cotangents[shards // 2 + 1]))
+
+    rate = (1.0 - mix_weight) * inner_rate
+    layer_next = mix(mine, own, columns, cotangents, weight, pieces, rate)
     return (layer_next[None], master_next, momentum_next)
 
 

time: 91.5 us -> 85 us (0.929)
  the two profiles are of different devices: /device:TPU:0 before, /device:TPU:10 now
where the time goes in v20:
time: 85 us; the launch traced here: 84.7 us
  waiting for transfers between devices  50.4 us (59%)
  starting transfers between devices  14.2 us (17%)
  Pallas kernels  11.7 us (14%)
  local copies, waits for them, and re-layouts  5.01 us (6%)
  other arithmetic  2.6 us (3%)
    ppermute x12, waiting for transfers between devices, swap(): return lax.ppermute(value, axis, [(i, i ^ mask) for i in range(size)])  50.4 us
    ppermute x12, starting transfers between devices, swap(): return lax.ppermute(value, axis, [(i, i ^ mask) for i in range(size)])  8.08 us
    all_to_all x1, starting transfers between devices, on_device(): lax.all_to_all(blocks, 'fsdp', split_axis=0, concat_axis=0, tiled=True)  6.14 us
    pallas_call x1, Pallas kernels, mix(): pl.pallas_call(functools.partial(mix_kernel, shards, groups, rate), out_s...  5.81 us
    unnamed x32, local copies, waits for them, and re-layouts  4.95 us
    pallas_call x1, Pallas kernels, code_and_decode(): pl.pallas_call(code_kernel, out_shape=(half, half), in_specs=[pl.BlockSpe...  3.69 us
    pallas_call x1, Pallas kernels, prepare(): pl.pallas_call(prepare_kernel, out_shape=jax.ShapeDtypeStruct((shards, ro...  2.21 us
  transfers between devices with their start and end apart: 13, of which 7 were waited for; matrix products, arithmetic and copies ran while one was open for 3% of the time, Pallas kernels for 7%

profile of v20, /device:TPU:10, one launch (start us, length us, event | category | flops | bytes accessed | tf_op | source)
XLA Modules:
  0.0 84.7 jit_solution(90826384362392260)
XLA Ops:
  0.6 2.7 %collective-permute-start.2 = (bf16[128,1024]{1,0:T(8,128)(2,1)}, bf16[128,1024]{1,0:T(8,128)(2,1)S(1)}, u32[]{:S(2)}, u32[]{:S(2)}) collective-permute-start(bf16[128,1024]{1,0:T(8,128)(2,1)} %bitcast.20), channel_id=1, source_target_pairs={{0,4},{1,5},{2,6},{3,7},{4,0},{5,1},{6,2},{7,3},{8,12},{9,13},{10,... | collective-permute-start | bytes 786440 | tf_op jit(solution)/shard_map/ppermute | solution.py:24
  3.3 0.4 collective-permute-start.1
  3.7 1.5 %collective-permute-start = (bf16[128,1024]{1,0:T(8,128)(2,1)}, bf16[128,1024]{1,0:T(8,128)(2,1)S(1)}, u32[]{:S(2)}, u32[]{:S(2)}) collective-permute-start(bf16[128,1024]{1,0:T(8,128)(2,1)} %bitcast.22), channel_id=1, source_target_pairs={{0,1},{1,0},{2,3},{3,2},{4,5},{5,4},{6,7},{7,6},{8,9},{9,8},{10,11... | collective-permute-start | bytes 786440 | tf_op jit(solution)/shard_map/ppermute | solution.py:24
  5.3 0.7 reshape.24
  6.0 1.6 %copy-done.1 = bf16[1,128,8192]{2,1,0:T(8,128)(2,1)S(1)} copy-done((bf16[1,128,8192]{2,1,0:T(8,128)(2,1)S(1)}, bf16[1,128,8192]{2,1,0:T(8,128)(2,1)}, u32[]{:S(2)}) %copy-start.1) | copy-done | bytes 2097176
  7.6 2.2 %prepare.1 = bf16[8,1024,128]{2,1,0:T(8,128)(2,1)} custom-call(bf16[128,8192]{1,0:T(8,128)(2,1)S(1)} %bitcast.17, f32[1,8192]{1,0:T(1,128)S(1)} %bitcast.18), custom_call_target="tpu_custom_call" | custom-call | flops 5242880 | bytes 4194304 | tf_op jit(solution)/shard_map/prepare/pallas_call | solution.py:58
  9.8 4.9 %collective-permute-done.2.refs_4_ = bf16[128,1024]{1,0:T(8,128)(2,1)S(1)} collective-permute-done((bf16[128,1024]{1,0:T(8,128)(2,1)}, bf16[128,1024]{1,0:T(8,128)(2,1)S(1)}, u32[]{:S(2)}, u32[]{:S(2)}) %collective-permute-start.2) | collective-permute-done | bytes 262176 | tf_op jit(solution)/shard_map/ppermute | solution.py:24
  14.7 1.0 %collective-permute-done.1.refs_2_ = bf16[128,1024]{1,0:T(8,128)(2,1)S(1)} collective-permute-done((bf16[128,1024]{1,0:T(8,128)(2,1)}, bf16[128,1024]{1,0:T(8,128)(2,1)S(1)}, u32[]{:S(2)}, u32[]{:S(2)}) %collective-permute-start.1) | collective-permute-done | bytes 262176 | tf_op jit(solution)/shard_map/ppermute | solution.py:24
  15.6 0.7 copy-done.11
  16.4 6.1 %all-to-all-start = ((bf16[8,1024,128]{2,1,0:T(8,128)(2,1)}), bf16[8,1024,128]{2,1,0:T(8,128)(2,1)}, u32[]{:S(2)}, u32[]{:S(2)}) async-start(bf16[8,1024,128]{2,1,0:T(8,128)(2,1)} %prepare.1), calls=%async_computation | async-start | bytes 4194304 | tf_op jit(solution)/shard_map/all_to_all | solution.py:255
  22.5 1.6 %copy-done.2 = bf16[1024,1024]{1,0:T(8,128)(2,1)S(1)} copy-done((bf16[1024,1024]{1,0:T(8,128)(2,1)S(1)}, bf16[1024,1024]{1,0:T(8,128)(2,1)}, u32[]{:S(2)}) %copy-start.2) | copy-done | bytes 2097176
  24.1 3.7 %code_and_decode.1 = (bf16[2,1024,256]{2,1,0:T(8,128)(2,1)S(1)}, bf16[2,1024,256]{2,1,0:T(8,128)(2,1)S(1)}) custom-call(s32[1]{0:T(128)} %bitcast.1.own_ref, bf16[1024,1024]{1,0:T(8,128)(2,1)S(1)} %copy-done.2, bf16[1024,1024]{1,0:T(8,128)(2,1)S(1)} %bitcast.16), custom_call_target="tpu_custom_call" | custom-call | flops 20971520 | bytes 6291456 | tf_op jit(solution)/shard_map/code_and_decode/pallas_call | solution.py:128
  27.8 0.1 collective-permute-start.7
  27.9 2.6 %collective-permute-done.7 = bf16[2,1024,256]{2,1,0:T(8,128)(2,1)S(1)} collective-permute-done((bf16[2,1024,256]{2,1,0:T(8,128)(2,1)S(1)}, bf16[2,1024,256]{2,1,0:T(8,128)(2,1)S(1)}, u32[]{:S(2)}, u32[]{:S(2)}) %collective-permute-start.7) | collective-permute-done | bytes 1048608 | tf_op jit(solution)/shard_map/ppermute | solution.py:24
  30.5 0.2 convert_add_fusion
  30.8 0.1 slice.23
  30.8 0.6 collective-permute-start.8
  31.4 13.4 %collective-permute-done.8 = bf16[1,1024,256]{2,1,0:T(8,128)(2,1)S(1)} collective-permute-done((bf16[1,1024,256]{2,1,0:T(8,128)(2,1)S(1)}, bf16[1,1024,256]{2,1,0:T(8,128)(2,1)S(1)}, u32[]{:S(2)}, u32[]{:S(2)}) %collective-permute-start.8) | collective-permute-done | bytes 524320 | tf_op jit(solution)/shard_map/ppermute | solution.py:24
  44.9 1.7 %fusion.2 = (bf16[1024,256]{1,0:T(8,128)(2,1)S(1)}, f32[1024,256]{1,0:T(8,128)}, f32[1024,256]{1,0:T(8,128)}) fusion(f32[1024,256]{1,0:T(8,128)S(1)} %copy-done.4, bf16[1,1024,256]{2,1,0:T(8,128)(2,1)S(1)} %collective-permute-done.8, f32[2,1024,256]{2,1,0:T(8,128)S(1)} %convert_add_fusion, f32[1024,256]{1,0:T(8,128)S(1)} %copy-done.5), kind=kLoop, calls=%fused_computation.7 | loop fusion | flops 2621440 | bytes 6291456 | tf_op jit(solution)/shard_map/convert_element_type | solution.py:267
  46.5 0.5 collective-permute-start.10
  47.1 1.5 %collective-permute-start.4 = (bf16[128,1024]{1,0:T(8,128)(2,1)S(1)}, bf16[128,1024]{1,0:T(8,128)(2,1)S(1)}, u32[]{:S(2)}, u32[]{:S(2)}) collective-permute-start(bf16[128,1024]{1,0:T(8,128)(2,1)S(1)} %collective-permute-done.2.refs_4_), channel_id=1, source_target_pairs={{0,1},{1,0},{2,3},{3,2},{4,5},{5,4},{6,7},{7,6},{8,9},{9,8},{10,11... | collective-permute-start | bytes 786440 | tf_op jit(solution)/shard_map/ppermute | solution.py:24
  48.5 0.6 collective-permute-start.3
  49.1 0.1 collective-permute-start.5
  49.2 9.8 %collective-permute-done.4.refs_5_ = bf16[128,1024]{1,0:T(8,128)(2,1)S(1)} collective-permute-done((bf16[128,1024]{1,0:T(8,128)(2,1)S(1)}, bf16[128,1024]{1,0:T(8,128)(2,1)S(1)}, u32[]{:S(2)}, u32[]{:S(2)}) %collective-permute-start.4) | collective-permute-done | bytes 262176 | tf_op jit(solution)/shard_map/ppermute | solution.py:24
  59.0 10.0 %collective-permute-done.3.refs_3_ = bf16[128,1024]{1,0:T(8,128)(2,1)S(1)} collective-permute-done((bf16[128,1024]{1,0:T(8,128)(2,1)S(1)}, bf16[128,1024]{1,0:T(8,128)(2,1)S(1)}, u32[]{:S(2)}, u32[]{:S(2)}) %collective-permute-start.3) | collective-permute-done | bytes 262176 | tf_op jit(solution)/shard_map/ppermute | solution.py:24
  69.0 0.1 collective-permute-start.11
  69.1 0.1 collective-permute-start.6
  69.2 8.6 %collective-permute-done.6.refs_7_ = bf16[128,1024]{1,0:T(8,128)(2,1)S(1)} collective-permute-done((bf16[128,1024]{1,0:T(8,128)(2,1)S(1)}, bf16[128,1024]{1,0:T(8,128)(2,1)S(1)}, u32[]{:S(2)}, u32[]{:S(2)}) %collective-permute-start.6) | collective-permute-done | bytes 262176 | tf_op jit(solution)/shard_map/ppermute | solution.py:24
  77.9 0.6 copy-done.15
  78.5 0.2 copy-done.7
  78.7 0.2 copy-done.8
  78.9 5.8 %mix.1 = bf16[1024,1024]{1,0:T(8,128)(2,1)} custom-call(s32[1]{0:T(128)} %bitcast.mine_ref, s32[1]{0:T(128)} %bitcast.1.own_ref, bf16[8,1024,128]{2,1,0:T(8,128)(2,1)} %all-to-all-done.tokens_ref, bf16[1024,1024]{1,0:T(8,128)(2,1)} %bitcast.15, bf16[128,1024]{1,0:T(8,128)(2,1)} %bitcast.23, bf16[128,1024]{1,0:T(8,128)(2,1)} %copy-done.11, ...), custom_call_target="tpu_custom_call" | custom-call | flops 2147483648 | bytes 10485760 | tf_op jit(solution)/shard_map/mix/pallas_call | solution.py:201
  (33 shorter events, 0.1 us)
Async XLA Ops:
  0.6 14.0 %collective-permute-start.2 = (bf16[128,1024]{1,0:T(8,128)(2,1)}, bf16[128,1024]{1,0:T(8,128)(2,1)S(1)}, u32[]{:S(2)}, u32[]{:S(2)}) collective-permute-start(bf16[128,1024]{1,0:T(8,128)(2,1)} %bitcast.20), channel_id=1, source_target_pairs={{0,4},{1,5},{2,6},{3,7},{4,0},{5,1},{6,2},{7,3},{8,12},{9,13},{10,... | collective-permute-start | bytes 786440 | tf_op jit(solution)/shard_map/ppermute | solution.py:24
  3.3 12.3 %collective-permute-start.1 = (bf16[128,1024]{1,0:T(8,128)(2,1)}, bf16[128,1024]{1,0:T(8,128)(2,1)S(1)}, u32[]{:S(2)}, u32[]{:S(2)}) collective-permute-start(bf16[128,1024]{1,0:T(8,128)(2,1)} %bitcast.21), channel_id=1, source_target_pairs={{0,2},{1,3},{2,0},{3,1},{4,6},{5,7},{6,4},{7,5},{8,10},{9,11},{10,... | collective-permute-start | bytes 786440 | tf_op jit(solution)/shard_map/ppermute | solution.py:24
  3.7 11.9 %collective-permute-start = (bf16[128,1024]{1,0:T(8,128)(2,1)}, bf16[128,1024]{1,0:T(8,128)(2,1)S(1)}, u32[]{:S(2)}, u32[]{:S(2)}) collective-permute-start(bf16[128,1024]{1,0:T(8,128)(2,1)} %bitcast.22), channel_id=1, source_target_pairs={{0,1},{1,0},{2,3},{3,2},{4,5},{5,4},{6,7},{7,6},{8,9},{9,8},{10,11... | collective-permute-start | bytes 786440 | tf_op jit(solution)/shard_map/ppermute | solution.py:24
  6.0 1.6 %copy-start.1 = (bf16[1,128,8192]{2,1,0:T(8,128)(2,1)S(1)}, bf16[1,128,8192]{2,1,0:T(8,128)(2,1)}, u32[]{:S(2)}) copy-start(bf16[1,128,8192]{2,1,0:T(8,128)(2,1)} %param.7) | copy-start | bytes 6291460
  14.7 34.4 %copy-start.9 = (bf16[128,1024]{1,0:T(8,128)(2,1)}, bf16[128,1024]{1,0:T(8,128)(2,1)S(1)}, u32[]{:S(2)}) copy-start(bf16[128,1024]{1,0:T(8,128)(2,1)S(1)} %collective-permute-done.2.refs_4_) | copy-start | bytes 786436
  15.6 32.9 %copy-start.10 = (bf16[128,1024]{1,0:T(8,128)(2,1)}, bf16[128,1024]{1,0:T(8,128)(2,1)S(1)}, u32[]{:S(2)}) copy-start(bf16[128,1024]{1,0:T(8,128)(2,1)S(1)} %collective-permute-done.1.refs_2_) | copy-start | bytes 786436
  15.6 0.8 copy-start.11
  15.6 6.9 %copy-start = (bf16[1,1024,1024]{2,1,0:T(8,128)(2,1)S(1)}, bf16[1,1024,1024]{2,1,0:T(8,128)(2,1)}, u32[]{:S(2)}) copy-start(bf16[1,1024,1024]{2,1,0:T(8,128)(2,1)} %param.10) | copy-start | bytes 6291460
  16.4 61.5 %all-to-all-start = ((bf16[8,1024,128]{2,1,0:T(8,128)(2,1)}), bf16[8,1024,128]{2,1,0:T(8,128)(2,1)}, u32[]{:S(2)}, u32[]{:S(2)}) async-start(bf16[8,1024,128]{2,1,0:T(8,128)(2,1)} %prepare.1), calls=%async_computation | async-start | bytes 4194304 | tf_op jit(solution)/shard_map/all_to_all | solution.py:255
  22.5 1.6 %copy-start.2 = (bf16[1024,1024]{1,0:T(8,128)(2,1)S(1)}, bf16[1024,1024]{1,0:T(8,128)(2,1)}, u32[]{:S(2)}) copy-start(bf16[1024,1024]{1,0:T(8,128)(2,1)} %shared_ref) | copy-start | bytes 6291460
  27.8 2.7 %collective-permute-start.7 = (bf16[2,1024,256]{2,1,0:T(8,128)(2,1)S(1)}, bf16[2,1024,256]{2,1,0:T(8,128)(2,1)S(1)}, u32[]{:S(2)}, u32[]{:S(2)}) collective-permute-start(bf16[2,1024,256]{2,1,0:T(8,128)(2,1)S(1)} %get-tuple-element.13), channel_id=1, source_target_pairs={{0,8},{8,0},{16,24},{24,16},{1,9},{9,1},{17,25},{25,17},{2,10},{10... | collective-permute-start | bytes 3145736 | tf_op jit(solution)/shard_map/ppermute | solution.py:24
  30.5 14.3 %copy-start.4 = (f32[1024,256]{1,0:T(8,128)S(1)}, f32[1024,256]{1,0:T(8,128)}, u32[]{:S(2)}) copy-start(f32[1024,256]{1,0:T(8,128)} %param.12) | copy-start | bytes 3145732
  30.5 14.3 %copy-start.5 = (f32[1024,256]{1,0:T(8,128)S(1)}, f32[1024,256]{1,0:T(8,128)}, u32[]{:S(2)}) copy-start(f32[1024,256]{1,0:T(8,128)} %param.13) | copy-start | bytes 3145732
  30.8 14.0 %collective-permute-start.8 = (bf16[1,1024,256]{2,1,0:T(8,128)(2,1)S(1)}, bf16[1,1024,256]{2,1,0:T(8,128)(2,1)S(1)}, u32[]{:S(2)}, u32[]{:S(2)}) collective-permute-start(bf16[1,1024,256]{2,1,0:T(8,128)(2,1)S(1)} %slice.23), channel_id=1, source_target_pairs={{0,16},{8,24},{16,0},{24,8},{1,17},{9,25},{17,1},{25,9},{2,18},{10... | collective-permute-start | bytes 1572872 | tf_op jit(solution)/shard_map/ppermute | solution.py:24
  46.5 31.3 %copy-start.3 = (bf16[1024,256]{1,0:T(8,128)(2,1)}, bf16[1024,256]{1,0:T(8,128)(2,1)S(1)}, u32[]{:S(2)}) copy-start(bf16[1024,256]{1,0:T(8,128)(2,1)S(1)} %get-tuple-element.15.refs_8_) | copy-start | bytes 1572868
  46.5 22.5 %collective-permute-start.10 = (bf16[1024,256]{1,0:T(8,128)(2,1)S(1)}, bf16[1024,256]{1,0:T(8,128)(2,1)S(1)}, u32[]{:S(2)}, u32[]{:S(2)}) collective-permute-start(bf16[1024,256]{1,0:T(8,128)(2,1)S(1)} %get-tuple-element.15.refs_8_), channel_id=1, source_target_pairs={{0,16},{8,24},{16,0},{24,8},{1,17},{9,25},{17,1},{25,9},{2,18},{10... | collective-permute-start | bytes 1572872 | tf_op jit(solution)/shard_map/ppermute | solution.py:24
  47.1 11.9 %collective-permute-start.4 = (bf16[128,1024]{1,0:T(8,128)(2,1)S(1)}, bf16[128,1024]{1,0:T(8,128)(2,1)S(1)}, u32[]{:S(2)}, u32[]{:S(2)}) collective-permute-start(bf16[128,1024]{1,0:T(8,128)(2,1)S(1)} %collective-permute-done.2.refs_4_), channel_id=1, source_target_pairs={{0,1},{1,0},{2,3},{3,2},{4,5},{5,4},{6,7},{7,6},{8,9},{9,8},{10,11... | collective-permute-start | bytes 786440 | tf_op jit(solution)/shard_map/ppermute | solution.py:24
  48.5 20.5 %collective-permute-start.3 = (bf16[128,1024]{1,0:T(8,128)(2,1)S(1)}, bf16[128,1024]{1,0:T(8,128)(2,1)S(1)}, u32[]{:S(2)}, u32[]{:S(2)}) collective-permute-start(bf16[128,1024]{1,0:T(8,128)(2,1)S(1)} %collective-permute-done.1.refs_2_), channel_id=1, source_target_pairs={{0,1},{1,0},{2,3},{3,2},{4,5},{5,4},{6,7},{7,6},{8,9},{9,8},{10,11... | collective-permute-start | bytes 786440 | tf_op jit(solution)/shard_map/ppermute | solution.py:24
  49.1 20.0 %collective-permute-start.5 = (bf16[128,1024]{1,0:T(8,128)(2,1)S(1)}, bf16[128,1024]{1,0:T(8,128)(2,1)S(1)}, u32[]{:S(2)}, u32[]{:S(2)}) collective-permute-start(bf16[128,1024]{1,0:T(8,128)(2,1)S(1)} %collective-permute-done.2.refs_4_), channel_id=1, source_target_pairs={{0,2},{1,3},{2,0},{3,1},{4,6},{5,7},{6,4},{7,5},{8,10},{9,11},{10,... | collective-permute-start | bytes 786440 | tf_op jit(solution)/shard_map/ppermute | solution.py:24
  49.2 28.7 %collective-permute-start.9 = (bf16[1024,256]{1,0:T(8,128)(2,1)S(1)}, bf16[1024,256]{1,0:T(8,128)(2,1)S(1)}, u32[]{:S(2)}, u32[]{:S(2)}) collective-permute-start(bf16[1024,256]{1,0:T(8,128)(2,1)S(1)} %get-tuple-element.15.refs_8_), channel_id=1, source_target_pairs={{0,8},{8,0},{16,24},{24,16},{1,9},{9,1},{17,25},{25,17},{2,10},{10... | collective-permute-start | bytes 1572872 | tf_op jit(solution)/shard_map/ppermute | solution.py:24
  59.0 18.9 %copy-start.12 = (bf16[128,1024]{1,0:T(8,128)(2,1)}, bf16[128,1024]{1,0:T(8,128)(2,1)S(1)}, u32[]{:S(2)}) copy-start(bf16[128,1024]{1,0:T(8,128)(2,1)S(1)} %collective-permute-done.4.refs_5_) | copy-start | bytes 786436
  69.0 8.9 %copy-start.13 = (bf16[128,1024]{1,0:T(8,128)(2,1)}, bf16[128,1024]{1,0:T(8,128)(2,1)S(1)}, u32[]{:S(2)}) copy-start(bf16[128,1024]{1,0:T(8,128)(2,1)S(1)} %collective-permute-done.3.refs_3_) | copy-start | bytes 786436
  69.0 8.9 %copy-start.6 = (bf16[1024,256]{1,0:T(8,128)(2,1)}, bf16[1024,256]{1,0:T(8,128)(2,1)S(1)}, u32[]{:S(2)}) copy-start(bf16[1024,256]{1,0:T(8,128)(2,1)S(1)} %collective-permute-done.10.refs_10_) | copy-start | bytes 1572868
  69.0 8.8 %collective-permute-start.11 = (bf16[1024,256]{1,0:T(8,128)(2,1)S(1)}, bf16[1024,256]{1,0:T(8,128)(2,1)S(1)}, u32[]{:S(2)}, u32[]{:S(2)}) collective-permute-start(bf16[1024,256]{1,0:T(8,128)(2,1)S(1)} %collective-permute-done.10.refs_10_), channel_id=1, source_target_pairs={{0,8},{8,0},{16,24},{24,16},{1,9},{9,1},{17,25},{25,17},{2,10},{10... | collective-permute-start | bytes 1572872 | tf_op jit(solution)/shard_map/ppermute | solution.py:24
  69.1 8.8 %copy-start.14 = (bf16[128,1024]{1,0:T(8,128)(2,1)}, bf16[128,1024]{1,0:T(8,128)(2,1)S(1)}, u32[]{:S(2)}) copy-start(bf16[128,1024]{1,0:T(8,128)(2,1)S(1)} %collective-permute-done.5.refs_6_) | copy-start | bytes 786436
  69.1 8.7 %collective-permute-start.6 = (bf16[128,1024]{1,0:T(8,128)(2,1)S(1)}, bf16[128,1024]{1,0:T(8,128)(2,1)S(1)}, u32[]{:S(2)}, u32[]{:S(2)}) collective-permute-start(bf16[128,1024]{1,0:T(8,128)(2,1)S(1)} %collective-permute-done.5.refs_6_), channel_id=1, source_target_pairs={{0,1},{1,0},{2,3},{3,2},{4,5},{5,4},{6,7},{7,6},{8,9},{9,8},{10,11... | collective-permute-start | bytes 786440 | tf_op jit(solution)/shard_map/ppermute | solution.py:24
  77.8 0.7 copy-start.15
  77.8 0.9 %copy-start.7 = (bf16[1024,256]{1,0:T(8,128)(2,1)}, bf16[1024,256]{1,0:T(8,128)(2,1)S(1)}, u32[]{:S(2)}) copy-start(bf16[1024,256]{1,0:T(8,128)(2,1)S(1)} %collective-permute-done.9.refs_9_) | copy-start | bytes 1572868
  77.8 1.1 %copy-start.8 = (bf16[1024,256]{1,0:T(8,128)(2,1)}, bf16[1024,256]{1,0:T(8,128)(2,1)S(1)}, u32[]{:S(2)}) copy-start(bf16[1024,256]{1,0:T(8,128)(2,1)S(1)} %collective-permute-done.11.refs_11_) | copy-start | bytes 1572868

commit v21 on v20

--- a/solution.py
+++ b/solution.py
@@ -226,6 +226,25 @@
     )(mine.reshape(1), own.reshape(1), tokens, weight, *cotangents, *pieces)
 
 
+def hand_on_kernel(value_ref, out_ref, sem):
+    copy = pltpu.make_async_copy(value_ref, out_ref, sem)
+    copy.start()
+    copy.wait()
+
+
+def hand_on(value):
+    return pl.pallas_call(
+        hand_on_kernel,
+        out_shape=jax.ShapeDtypeStruct(value.shape, value.dtype),
+        in_specs=[pl.BlockSpec(memory_space=pltpu.VMEM)],
+        out_specs=pl.BlockSpec(memory_space=pltpu.HBM),
+        scratch_shapes=[pltpu.SemaphoreType.DMA],
+        compiler_params=pltpu.CompilerParams(vmem_limit_bytes=16 * 2**20),
+        cost_estimate=pl.CostEstimate(flops=0, bytes_accessed=48 * value.size, transcendentals=0),
+        name="hand_on",
+    )(value)
+
+
 def gather(piece, axis, size, after=()):
     pieces = {0: piece}
     bit = size // 2
@@ -267,7 +286,7 @@
     pieces = gather(master_next.astype(jnp.bfloat16), "replica", groups, after=(cotangents[shards // 2 - 1], cotangents[shards // 2 + 1]))
 
     rate = (1.0 - mix_weight) * inner_rate
-    layer_next = mix(mine, own, columns, cotangents, weight, pieces, rate)
+    layer_next = mix(mine, own, columns, cotangents[:-1] + [hand_on(cotangents[-1])], weight, pieces, rate)
     return (layer_next[None], master_next, momentum_next)
 
 

time: 85 us -> 85.9 us (1.011)
    unnamed x32 -> x30, local copies, waits for them, and re-layouts: 4.95 us -> 5.56 us
where the time goes in v21:
time: 85.9 us; the launch traced here: 85.6 us
  waiting for transfers between devices  50.6 us (59%)
  starting transfers between devices  14.2 us (17%)
  Pallas kernels  11.7 us (14%)
  local copies, waits for them, and re-layouts  5.62 us (7%)
  other arithmetic  2.6 us (3%)
    ppermute x12, waiting for transfers between devices, swap(): return lax.ppermute(value, axis, [(i, i ^ mask) for i in range(size)])  50.6 us
    ppermute x12, starting transfers between devices, swap(): return lax.ppermute(value, axis, [(i, i ^ mask) for i in range(size)])  8.07 us
    all_to_all x1, starting transfers between devices, on_device(): lax.all_to_all(blocks, 'fsdp', split_axis=0, concat_axis=0, tiled=True)  6.14 us
    pallas_call x1, Pallas kernels, mix(): pl.pallas_call(functools.partial(mix_kernel, shards, groups, rate), out_s...  5.82 us
    unnamed x30, local copies, waits for them, and re-layouts  5.56 us
    pallas_call x1, Pallas kernels, code_and_decode(): pl.pallas_call(code_kernel, out_shape=(half, half), in_specs=[pl.BlockSpe...  3.69 us
    pallas_call x1, Pallas kernels, prepare(): pl.pallas_call(prepare_kernel, out_shape=jax.ShapeDtypeStruct((shards, ro...  2.21 us
  transfers between devices with their start and end apart: 13, of which 7 were waited for; matrix products, arithmetic and copies ran while one was open for 3% of the time, Pallas kernels for 7%

profile of v21, /device:TPU:10, one launch (start us, length us, event | category | flops | bytes accessed | tf_op | source)
XLA Modules:
  0.0 85.6 jit_solution(14858233672881811100)
XLA Ops:
  0.6 2.7 %collective-permute-start.2 = (bf16[128,1024]{1,0:T(8,128)(2,1)}, bf16[128,1024]{1,0:T(8,128)(2,1)S(1)}, u32[]{:S(2)}, u32[]{:S(2)}) collective-permute-start(bf16[128,1024]{1,0:T(8,128)(2,1)} %bitcast.20), channel_id=1, source_target_pairs={{0,4},{1,5},{2,6},{3,7},{4,0},{5,1},{6,2},{7,3},{8,12},{9,13},{10,... | collective-permute-start | bytes 786440 | tf_op jit(solution)/shard_map/ppermute | solution.py:24
  3.3 0.4 collective-permute-start.1
  3.7 1.5 %collective-permute-start = (bf16[128,1024]{1,0:T(8,128)(2,1)}, bf16[128,1024]{1,0:T(8,128)(2,1)S(1)}, u32[]{:S(2)}, u32[]{:S(2)}) collective-permute-start(bf16[128,1024]{1,0:T(8,128)(2,1)} %bitcast.22), channel_id=1, source_target_pairs={{0,1},{1,0},{2,3},{3,2},{4,5},{5,4},{6,7},{7,6},{8,9},{9,8},{10,11... | collective-permute-start | bytes 786440 | tf_op jit(solution)/shard_map/ppermute | solution.py:24
  5.3 0.7 reshape.24
  6.0 1.6 %copy-done.1 = bf16[1,128,8192]{2,1,0:T(8,128)(2,1)S(1)} copy-done((bf16[1,128,8192]{2,1,0:T(8,128)(2,1)S(1)}, bf16[1,128,8192]{2,1,0:T(8,128)(2,1)}, u32[]{:S(2)}) %copy-start.1) | copy-done | bytes 2097176
  7.6 2.2 %prepare.1 = bf16[8,1024,128]{2,1,0:T(8,128)(2,1)} custom-call(bf16[128,8192]{1,0:T(8,128)(2,1)S(1)} %bitcast.17, f32[1,8192]{1,0:T(1,128)S(1)} %bitcast.18), custom_call_target="tpu_custom_call" | custom-call | flops 5242880 | bytes 4194304 | tf_op jit(solution)/shard_map/prepare/pallas_call | solution.py:58
  9.8 4.9 %collective-permute-done.2.refs_4_ = bf16[128,1024]{1,0:T(8,128)(2,1)S(1)} collective-permute-done((bf16[128,1024]{1,0:T(8,128)(2,1)}, bf16[128,1024]{1,0:T(8,128)(2,1)S(1)}, u32[]{:S(2)}, u32[]{:S(2)}) %collective-permute-start.2) | collective-permute-done | bytes 262176 | tf_op jit(solution)/shard_map/ppermute | solution.py:24
  14.7 1.0 %collective-permute-done.1.refs_2_ = bf16[128,1024]{1,0:T(8,128)(2,1)S(1)} collective-permute-done((bf16[128,1024]{1,0:T(8,128)(2,1)}, bf16[128,1024]{1,0:T(8,128)(2,1)S(1)}, u32[]{:S(2)}, u32[]{:S(2)}) %collective-permute-start.1) | collective-permute-done | bytes 262176 | tf_op jit(solution)/shard_map/ppermute | solution.py:24
  15.6 0.7 copy-done.12
  16.4 6.1 %all-to-all-start = ((bf16[8,1024,128]{2,1,0:T(8,128)(2,1)}), bf16[8,1024,128]{2,1,0:T(8,128)(2,1)}, u32[]{:S(2)}, u32[]{:S(2)}) async-start(bf16[8,1024,128]{2,1,0:T(8,128)(2,1)} %prepare.1), calls=%async_computation | async-start | bytes 4194304 | tf_op jit(solution)/shard_map/all_to_all | solution.py:274
  22.5 1.6 %copy-done.2 = bf16[1024,1024]{1,0:T(8,128)(2,1)S(1)} copy-done((bf16[1024,1024]{1,0:T(8,128)(2,1)S(1)}, bf16[1024,1024]{1,0:T(8,128)(2,1)}, u32[]{:S(2)}) %copy-start.2) | copy-done | bytes 2097176
  24.1 3.7 %code_and_decode.1 = (bf16[2,1024,256]{2,1,0:T(8,128)(2,1)S(1)}, bf16[2,1024,256]{2,1,0:T(8,128)(2,1)S(1)}) custom-call(s32[1]{0:T(128)} %bitcast.1.own_ref, bf16[1024,1024]{1,0:T(8,128)(2,1)S(1)} %copy-done.2, bf16[1024,1024]{1,0:T(8,128)(2,1)S(1)} %bitcast.16), custom_call_target="tpu_custom_call" | custom-call | flops 20971520 | bytes 6291456 | tf_op jit(solution)/shard_map/code_and_decode/pallas_call | solution.py:128
  27.8 0.1 collective-permute-start.7
  27.9 2.6 %collective-permute-done.7 = bf16[2,1024,256]{2,1,0:T(8,128)(2,1)S(1)} collective-permute-done((bf16[2,1024,256]{2,1,0:T(8,128)(2,1)S(1)}, bf16[2,1024,256]{2,1,0:T(8,128)(2,1)S(1)}, u32[]{:S(2)}, u32[]{:S(2)}) %collective-permute-start.7) | collective-permute-done | bytes 1048608 | tf_op jit(solution)/shard_map/ppermute | solution.py:24
  30.5 0.2 convert_add_fusion
  30.8 0.1 slice.23
  30.8 0.6 collective-permute-start.8
  31.4 13.4 %collective-permute-done.8 = bf16[1,1024,256]{2,1,0:T(8,128)(2,1)S(1)} collective-permute-done((bf16[1,1024,256]{2,1,0:T(8,128)(2,1)S(1)}, bf16[1,1024,256]{2,1,0:T(8,128)(2,1)S(1)}, u32[]{:S(2)}, u32[]{:S(2)}) %collective-permute-start.8) | collective-permute-done | bytes 524320 | tf_op jit(solution)/shard_map/ppermute | solution.py:24
  44.9 1.7 %fusion.2 = (bf16[1024,256]{1,0:T(8,128)(2,1)S(1)}, f32[1024,256]{1,0:T(8,128)}, f32[1024,256]{1,0:T(8,128)}) fusion(f32[1024,256]{1,0:T(8,128)S(1)} %copy-done.5, bf16[1,1024,256]{2,1,0:T(8,128)(2,1)S(1)} %collective-permute-done.8, f32[2,1024,256]{2,1,0:T(8,128)S(1)} %convert_add_fusion, f32[1024,256]{1,0:T(8,128)S(1)} %copy-done.6), kind=kLoop, calls=%fused_computation.7 | loop fusion | flops 2621440 | bytes 6291456 | tf_op jit(solution)/shard_map/convert_element_type | solution.py:286
  46.5 0.5 collective-permute-start.10
  47.1 1.5 %collective-permute-start.4 = (bf16[128,1024]{1,0:T(8,128)(2,1)S(1)}, bf16[128,1024]{1,0:T(8,128)(2,1)S(1)}, u32[]{:S(2)}, u32[]{:S(2)}) collective-permute-start(bf16[128,1024]{1,0:T(8,128)(2,1)S(1)} %collective-permute-done.2.refs_4_), channel_id=1, source_target_pairs={{0,1},{1,0},{2,3},{3,2},{4,5},{5,4},{6,7},{7,6},{8,9},{9,8},{10,11... | collective-permute-start | bytes 786440 | tf_op jit(solution)/shard_map/ppermute | solution.py:24
  48.5 0.6 collective-permute-start.3
  49.1 0.1 collective-permute-start.5
  49.2 9.8 %collective-permute-done.4.refs_5_ = bf16[128,1024]{1,0:T(8,128)(2,1)S(1)} collective-permute-done((bf16[128,1024]{1,0:T(8,128)(2,1)S(1)}, bf16[128,1024]{1,0:T(8,128)(2,1)S(1)}, u32[]{:S(2)}, u32[]{:S(2)}) %collective-permute-start.4) | collective-permute-done | bytes 262176 | tf_op jit(solution)/shard_map/ppermute | solution.py:24
  59.0 10.0 %collective-permute-done.3.refs_3_ = bf16[128,1024]{1,0:T(8,128)(2,1)S(1)} collective-permute-done((bf16[128,1024]{1,0:T(8,128)(2,1)S(1)}, bf16[128,1024]{1,0:T(8,128)(2,1)S(1)}, u32[]{:S(2)}, u32[]{:S(2)}) %collective-permute-start.3) | collective-permute-done | bytes 262176 | tf_op jit(solution)/shard_map/ppermute | solution.py:24
  69.0 0.1 collective-permute-start.11
  69.1 0.1 collective-permute-start.6
  69.2 8.8 %collective-permute-done.6.value_ref = bf16[128,1024]{1,0:T(8,128)(2,1)S(1)} collective-permute-done((bf16[128,1024]{1,0:T(8,128)(2,1)}, bf16[128,1024]{1,0:T(8,128)(2,1)S(1)}, u32[]{:S(2)}, u32[]{:S(2)}) %collective-permute-start.6) | collective-permute-done | bytes 262176 | tf_op jit(solution)/shard_map/ppermute | solution.py:24
  78.1 0.7 copy-done.3
  78.9 0.7 copy-done.8
  79.6 0.2 copy-done.9
  79.8 5.8 %mix.1 = bf16[1024,1024]{1,0:T(8,128)(2,1)} custom-call(s32[1]{0:T(128)} %bitcast.mine_ref, s32[1]{0:T(128)} %bitcast.1.own_ref, bf16[8,1024,128]{2,1,0:T(8,128)(2,1)} %all-to-all-done.tokens_ref, bf16[1024,1024]{1,0:T(8,128)(2,1)} %bitcast.15, bf16[128,1024]{1,0:T(8,128)(2,1)} %bitcast.23, bf16[128,1024]{1,0:T(8,128)(2,1)} %copy-done.12, ...), custom_call_target="tpu_custom_call" | custom-call | flops 2147483648 | bytes 10485760 | tf_op jit(solution)/shard_map/mix/pallas_call | solution.py:201
  (32 shorter events, 0.1 us)
Async XLA Ops:
  0.6 14.0 %collective-permute-start.2 = (bf16[128,1024]{1,0:T(8,128)(2,1)}, bf16[128,1024]{1,0:T(8,128)(2,1)S(1)}, u32[]{:S(2)}, u32[]{:S(2)}) collective-permute-start(bf16[128,1024]{1,0:T(8,128)(2,1)} %bitcast.20), channel_id=1, source_target_pairs={{0,4},{1,5},{2,6},{3,7},{4,0},{5,1},{6,2},{7,3},{8,12},{9,13},{10,... | collective-permute-start | bytes 786440 | tf_op jit(solution)/shard_map/ppermute | solution.py:24
  3.3 12.3 %collective-permute-start.1 = (bf16[128,1024]{1,0:T(8,128)(2,1)}, bf16[128,1024]{1,0:T(8,128)(2,1)S(1)}, u32[]{:S(2)}, u32[]{:S(2)}) collective-permute-start(bf16[128,1024]{1,0:T(8,128)(2,1)} %bitcast.21), channel_id=1, source_target_pairs={{0,2},{1,3},{2,0},{3,1},{4,6},{5,7},{6,4},{7,5},{8,10},{9,11},{10,... | collective-permute-start | bytes 786440 | tf_op jit(solution)/shard_map/ppermute | solution.py:24
  3.7 11.9 %collective-permute-start = (bf16[128,1024]{1,0:T(8,128)(2,1)}, bf16[128,1024]{1,0:T(8,128)(2,1)S(1)}, u32[]{:S(2)}, u32[]{:S(2)}) collective-permute-start(bf16[128,1024]{1,0:T(8,128)(2,1)} %bitcast.22), channel_id=1, source_target_pairs={{0,1},{1,0},{2,3},{3,2},{4,5},{5,4},{6,7},{7,6},{8,9},{9,8},{10,11... | collective-permute-start | bytes 786440 | tf_op jit(solution)/shard_map/ppermute | solution.py:24
  6.0 1.6 %copy-start.1 = (bf16[1,128,8192]{2,1,0:T(8,128)(2,1)S(1)}, bf16[1,128,8192]{2,1,0:T(8,128)(2,1)}, u32[]{:S(2)}) copy-start(bf16[1,128,8192]{2,1,0:T(8,128)(2,1)} %param.7) | copy-start | bytes 6291460
  14.7 34.4 %copy-start.10 = (bf16[128,1024]{1,0:T(8,128)(2,1)}, bf16[128,1024]{1,0:T(8,128)(2,1)S(1)}, u32[]{:S(2)}) copy-start(bf16[128,1024]{1,0:T(8,128)(2,1)S(1)} %collective-permute-done.2.refs_4_) | copy-start | bytes 786436
  15.6 32.9 %copy-start.11 = (bf16[128,1024]{1,0:T(8,128)(2,1)}, bf16[128,1024]{1,0:T(8,128)(2,1)S(1)}, u32[]{:S(2)}) copy-start(bf16[128,1024]{1,0:T(8,128)(2,1)S(1)} %collective-permute-done.1.refs_2_) | copy-start | bytes 786436
  15.6 0.8 copy-start.12
  15.6 6.9 %copy-start = (bf16[1,1024,1024]{2,1,0:T(8,128)(2,1)S(1)}, bf16[1,1024,1024]{2,1,0:T(8,128)(2,1)}, u32[]{:S(2)}) copy-start(bf16[1,1024,1024]{2,1,0:T(8,128)(2,1)} %param.10) | copy-start | bytes 6291460
  16.4 62.4 %all-to-all-start = ((bf16[8,1024,128]{2,1,0:T(8,128)(2,1)}), bf16[8,1024,128]{2,1,0:T(8,128)(2,1)}, u32[]{:S(2)}, u32[]{:S(2)}) async-start(bf16[8,1024,128]{2,1,0:T(8,128)(2,1)} %prepare.1), calls=%async_computation | async-start | bytes 4194304 | tf_op jit(solution)/shard_map/all_to_all | solution.py:274
  22.5 1.6 %copy-start.2 = (bf16[1024,1024]{1,0:T(8,128)(2,1)S(1)}, bf16[1024,1024]{1,0:T(8,128)(2,1)}, u32[]{:S(2)}) copy-start(bf16[1024,1024]{1,0:T(8,128)(2,1)} %shared_ref) | copy-start | bytes 6291460
  27.8 2.7 %collective-permute-start.7 = (bf16[2,1024,256]{2,1,0:T(8,128)(2,1)S(1)}, bf16[2,1024,256]{2,1,0:T(8,128)(2,1)S(1)}, u32[]{:S(2)}, u32[]{:S(2)}) collective-permute-start(bf16[2,1024,256]{2,1,0:T(8,128)(2,1)S(1)} %get-tuple-element.13), channel_id=1, source_target_pairs={{0,8},{8,0},{16,24},{24,16},{1,9},{9,1},{17,25},{25,17},{2,10},{10... | collective-permute-start | bytes 3145736 | tf_op jit(solution)/shard_map/ppermute | solution.py:24
  30.5 14.3 %copy-start.5 = (f32[1024,256]{1,0:T(8,128)S(1)}, f32[1024,256]{1,0:T(8,128)}, u32[]{:S(2)}) copy-start(f32[1024,256]{1,0:T(8,128)} %param.12) | copy-start | bytes 3145732
  30.5 14.3 %copy-start.6 = (f32[1024,256]{1,0:T(8,128)S(1)}, f32[1024,256]{1,0:T(8,128)}, u32[]{:S(2)}) copy-start(f32[1024,256]{1,0:T(8,128)} %param.13) | copy-start | bytes 3145732
  30.8 14.0 %collective-permute-start.8 = (bf16[1,1024,256]{2,1,0:T(8,128)(2,1)S(1)}, bf16[1,1024,256]{2,1,0:T(8,128)(2,1)S(1)}, u32[]{:S(2)}, u32[]{:S(2)}) collective-permute-start(bf16[1,1024,256]{2,1,0:T(8,128)(2,1)S(1)} %slice.23), channel_id=1, source_target_pairs={{0,16},{8,24},{16,0},{24,8},{1,17},{9,25},{17,1},{25,9},{2,18},{10... | collective-permute-start | bytes 1572872 | tf_op jit(solution)/shard_map/ppermute | solution.py:24
  46.5 32.3 %copy-start.4 = (bf16[1024,256]{1,0:T(8,128)(2,1)}, bf16[1024,256]{1,0:T(8,128)(2,1)S(1)}, u32[]{:S(2)}) copy-start(bf16[1024,256]{1,0:T(8,128)(2,1)S(1)} %get-tuple-element.15.refs_8_) | copy-start | bytes 1572868
  46.5 22.5 %collective-permute-start.10 = (bf16[1024,256]{1,0:T(8,128)(2,1)S(1)}, bf16[1024,256]{1,0:T(8,128)(2,1)S(1)}, u32[]{:S(2)}, u32[]{:S(2)}) collective-permute-start(bf16[1024,256]{1,0:T(8,128)(2,1)S(1)} %get-tuple-element.15.refs_8_), channel_id=1, source_target_pairs={{0,16},{8,24},{16,0},{24,8},{1,17},{9,25},{17,1},{25,9},{2,18},{10... | collective-permute-start | bytes 1572872 | tf_op jit(solution)/shard_map/ppermute | solution.py:24
  47.1 11.9 %collective-permute-start.4 = (bf16[128,1024]{1,0:T(8,128)(2,1)S(1)}, bf16[128,1024]{1,0:T(8,128)(2,1)S(1)}, u32[]{:S(2)}, u32[]{:S(2)}) collective-permute-start(bf16[128,1024]{1,0:T(8,128)(2,1)S(1)} %collective-permute-done.2.refs_4_), channel_id=1, source_target_pairs={{0,1},{1,0},{2,3},{3,2},{4,5},{5,4},{6,7},{7,6},{8,9},{9,8},{10,11... | collective-permute-start | bytes 786440 | tf_op jit(solution)/shard_map/ppermute | solution.py:24
  48.5 20.5 %collective-permute-start.3 = (bf16[128,1024]{1,0:T(8,128)(2,1)S(1)}, bf16[128,1024]{1,0:T(8,128)(2,1)S(1)}, u32[]{:S(2)}, u32[]{:S(2)}) collective-permute-start(bf16[128,1024]{1,0:T(8,128)(2,1)S(1)} %collective-permute-done.1.refs_2_), channel_id=1, source_target_pairs={{0,1},{1,0},{2,3},{3,2},{4,5},{5,4},{6,7},{7,6},{8,9},{9,8},{10,11... | collective-permute-start | bytes 786440 | tf_op jit(solution)/shard_map/ppermute | solution.py:24
  49.1 20.0 %collective-permute-start.5 = (bf16[128,1024]{1,0:T(8,128)(2,1)S(1)}, bf16[128,1024]{1,0:T(8,128)(2,1)}, u32[]{:S(2)}, u32[]{:S(2)}) collective-permute-start(bf16[128,1024]{1,0:T(8,128)(2,1)S(1)} %collective-permute-done.2.refs_4_), channel_id=1, source_target_pairs={{0,2},{1,3},{2,0},{3,1},{4,6},{5,7},{6,4},{7,5},{8,10},{9,11},{10,... | collective-permute-start | bytes 786440 | tf_op jit(solution)/shard_map/ppermute | solution.py:24
  49.2 29.6 %collective-permute-start.9 = (bf16[1024,256]{1,0:T(8,128)(2,1)S(1)}, bf16[1024,256]{1,0:T(8,128)(2,1)S(1)}, u32[]{:S(2)}, u32[]{:S(2)}) collective-permute-start(bf16[1024,256]{1,0:T(8,128)(2,1)S(1)} %get-tuple-element.15.refs_8_), channel_id=1, source_target_pairs={{0,8},{8,0},{16,24},{24,16},{1,9},{9,1},{17,25},{25,17},{2,10},{10... | collective-permute-start | bytes 1572872 | tf_op jit(solution)/shard_map/ppermute | solution.py:24
  59.0 19.9 %copy-start.13 = (bf16[128,1024]{1,0:T(8,128)(2,1)}, bf16[128,1024]{1,0:T(8,128)(2,1)S(1)}, u32[]{:S(2)}) copy-start(bf16[128,1024]{1,0:T(8,128)(2,1)S(1)} %collective-permute-done.4.refs_5_) | copy-start | bytes 786436
  69.0 9.8 %copy-start.14 = (bf16[128,1024]{1,0:T(8,128)(2,1)}, bf16[128,1024]{1,0:T(8,128)(2,1)S(1)}, u32[]{:S(2)}) copy-start(bf16[128,1024]{1,0:T(8,128)(2,1)S(1)} %collective-permute-done.3.refs_3_) | copy-start | bytes 786436
  69.0 9.8 %copy-start.7 = (bf16[1024,256]{1,0:T(8,128)(2,1)}, bf16[1024,256]{1,0:T(8,128)(2,1)S(1)}, u32[]{:S(2)}) copy-start(bf16[1024,256]{1,0:T(8,128)(2,1)S(1)} %collective-permute-done.10.refs_10_) | copy-start | bytes 1572868
  69.0 9.8 %collective-permute-start.11 = (bf16[1024,256]{1,0:T(8,128)(2,1)S(1)}, bf16[1024,256]{1,0:T(8,128)(2,1)S(1)}, u32[]{:S(2)}, u32[]{:S(2)}) collective-permute-start(bf16[1024,256]{1,0:T(8,128)(2,1)S(1)} %collective-permute-done.10.refs_10_), channel_id=1, source_target_pairs={{0,8},{8,0},{16,24},{24,16},{1,9},{9,1},{17,25},{25,17},{2,10},{10... | collective-permute-start | bytes 1572872 | tf_op jit(solution)/shard_map/ppermute | solution.py:24
  69.1 8.9 %collective-permute-start.6 = (bf16[128,1024]{1,0:T(8,128)(2,1)}, bf16[128,1024]{1,0:T(8,128)(2,1)S(1)}, u32[]{:S(2)}, u32[]{:S(2)}) collective-permute-start(bf16[128,1024]{1,0:T(8,128)(2,1)} %collective-permute-done.5.refs_6_), channel_id=1, source_target_pairs={{0,1},{1,0},{2,3},{3,2},{4,5},{5,4},{6,7},{7,6},{8,9},{9,8},{10,11... | collective-permute-start | bytes 786440 | tf_op jit(solution)/shard_map/ppermute | solution.py:24
  78.1 0.7 copy-start.3
  78.8 0.8 copy-start.8
  78.8 1.0 %copy-start.9 = (bf16[1024,256]{1,0:T(8,128)(2,1)}, bf16[1024,256]{1,0:T(8,128)(2,1)S(1)}, u32[]{:S(2)}) copy-start(bf16[1024,256]{1,0:T(8,128)(2,1)S(1)} %collective-permute-done.11.refs_11_) | copy-start | bytes 1572868

commit v22 on v19

--- a/solution.py
+++ b/solution.py
@@ -209,7 +209,7 @@
             pltpu.SemaphoreType.DMA((groups,)),
             pltpu.SemaphoreType.DMA((2,)),
         ],
-        compiler_params=pltpu.CompilerParams(vmem_limit_bytes=58880 * 2**10),
+        compiler_params=pltpu.CompilerParams(vmem_limit_bytes=54 * 2**20),
         cost_estimate=pl.CostEstimate(
             flops=2 * depth * parts * rows * width,
             bytes_accessed=2 * depth * shards * (rows + width) + 8 * rows * width,

time: 84.7 us -> 84.7 us (level)
  no operation moved by 1% of the time
where the time goes in v22:
time: 84.7 us; the launch traced here: 84.3 us
  waiting for transfers between devices  37.7 us (45%)
  starting transfers between devices  20.5 us (24%)
  Pallas kernels  14.9 us (18%)
  local copies, waits for them, and re-layouts  7.87 us (9%)
  other arithmetic  2.6 us (3%)
    ppermute x12, waiting for transfers between devices, swap(): return lax.ppermute(value, axis, [(i, i ^ mask) for i in range(size)])  34.3 us
    ppermute x12, starting transfers between devices, swap(): return lax.ppermute(value, axis, [(i, i ^ mask) for i in range(size)])  14.9 us
    unnamed x32, local copies, waits for them, and re-layouts  7.82 us
    pallas_call x1, Pallas kernels, accumulate(): pl.pallas_call(functools.partial(accumulate_kernel, parts, groups, rate),...  7.05 us
    all_to_all x1, starting transfers between devices, on_device(): lax.all_to_all(blocks, 'fsdp', split_axis=0, concat_axis=0, tiled=True)  5.61 us
    pallas_call x1, Pallas kernels, code_and_decode(): pl.pallas_call(code_kernel, out_shape=(half, half), in_specs=[pl.BlockSpe...  3.69 us
    all_to_all x1, waiting for transfers between devices, on_device(): lax.all_to_all(blocks, 'fsdp', split_axis=0, concat_axis=0, tiled=True)  3.44 us
    pallas_call x1, Pallas kernels, prepare(): pl.pallas_call(prepare_kernel, out_shape=jax.ShapeDtypeStruct((shards, ro...  2.21 us
  transfers between devices with their start and end apart: 13, of which 7 were waited for; matrix products, arithmetic and copies ran while one was open for 3% of the time, Pallas kernels for 15%

profile of v22, /device:TPU:0, one launch (start us, length us, event | category | flops | bytes accessed | tf_op | source)
XLA Modules:
  0.0 84.3 jit_solution(2490964186665329309)
XLA Ops:
  0.6 4.1 %collective-permute-start.2 = (bf16[128,1024]{1,0:T(8,128)(2,1)}, bf16[128,1024]{1,0:T(8,128)(2,1)S(1)}, u32[]{:S(2)}, u32[]{:S(2)}) collective-permute-start(bf16[128,1024]{1,0:T(8,128)(2,1)} %bitcast.20), channel_id=1, source_target_pairs={{0,4},{1,5},{2,6},{3,7},{4,0},{5,1},{6,2},{7,3},{8,12},{9,13},{10,... | collective-permute-start | bytes 786440 | tf_op jit(solution)/shard_map/ppermute | solution.py:24
  4.7 1.6 %collective-permute-start.1 = (bf16[128,1024]{1,0:T(8,128)(2,1)}, bf16[128,1024]{1,0:T(8,128)(2,1)S(1)}, u32[]{:S(2)}, u32[]{:S(2)}) collective-permute-start(bf16[128,1024]{1,0:T(8,128)(2,1)} %bitcast.21), channel_id=1, source_target_pairs={{0,2},{1,3},{2,0},{3,1},{4,6},{5,7},{6,4},{7,5},{8,10},{9,11},{10,... | collective-permute-start | bytes 786440 | tf_op jit(solution)/shard_map/ppermute | solution.py:24
  6.3 1.5 %collective-permute-start = (bf16[128,1024]{1,0:T(8,128)(2,1)}, bf16[128,1024]{1,0:T(8,128)(2,1)S(1)}, u32[]{:S(2)}, u32[]{:S(2)}) collective-permute-start(bf16[128,1024]{1,0:T(8,128)(2,1)} %bitcast.22), channel_id=1, source_target_pairs={{0,1},{1,0},{2,3},{3,2},{4,5},{5,4},{6,7},{7,6},{8,9},{9,8},{10,11... | collective-permute-start | bytes 786440 | tf_op jit(solution)/shard_map/ppermute | solution.py:24
  7.8 0.7 reshape.25
  8.6 1.6 %copy-done.2 = bf16[1,128,8192]{2,1,0:T(8,128)(2,1)S(1)} copy-done((bf16[1,128,8192]{2,1,0:T(8,128)(2,1)S(1)}, bf16[1,128,8192]{2,1,0:T(8,128)(2,1)}, u32[]{:S(2)}) %copy-start.2) | copy-done | bytes 2097176
  10.1 2.2 %prepare.1 = bf16[8,1024,128]{2,1,0:T(8,128)(2,1)} custom-call(bf16[128,8192]{1,0:T(8,128)(2,1)S(1)} %bitcast.17, f32[1,8192]{1,0:T(1,128)S(1)} %bitcast.18), custom_call_target="tpu_custom_call" | custom-call | flops 5242880 | bytes 4194304 | tf_op jit(solution)/shard_map/prepare/pallas_call | solution.py:58
  12.4 4.6 %collective-permute-done.2.refs_4_ = bf16[128,1024]{1,0:T(8,128)(2,1)S(1)} collective-permute-done((bf16[128,1024]{1,0:T(8,128)(2,1)}, bf16[128,1024]{1,0:T(8,128)(2,1)S(1)}, u32[]{:S(2)}, u32[]{:S(2)}) %collective-permute-start.2) | collective-permute-done | bytes 262176 | tf_op jit(solution)/shard_map/ppermute | solution.py:24
  17.0 0.2 collective-permute-done.1.refs_2_
  17.2 0.8 copy-done.12
  17.9 5.6 %all-to-all-start = ((bf16[8,1024,128]{2,1,0:T(8,128)(2,1)}), bf16[8,1024,128]{2,1,0:T(8,128)(2,1)}, u32[]{:S(2)}, u32[]{:S(2)}) async-start(bf16[8,1024,128]{2,1,0:T(8,128)(2,1)} %prepare.1), calls=%async_computation | async-start | bytes 4194304 | tf_op jit(solution)/shard_map/all_to_all | solution.py:285
  23.6 1.6 %copy-done.3 = bf16[1024,1024]{1,0:T(8,128)(2,1)S(1)} copy-done((bf16[1024,1024]{1,0:T(8,128)(2,1)S(1)}, bf16[1024,1024]{1,0:T(8,128)(2,1)}, u32[]{:S(2)}) %copy-start.3) | copy-done | bytes 2097176
  25.1 3.7 %code_and_decode.1 = (bf16[2,1024,256]{2,1,0:T(8,128)(2,1)S(1)}, bf16[2,1024,256]{2,1,0:T(8,128)(2,1)S(1)}) custom-call(s32[1]{0:T(128)} %bitcast.own_ref, bf16[1024,1024]{1,0:T(8,128)(2,1)S(1)} %copy-done.3, bf16[1024,1024]{1,0:T(8,128)(2,1)S(1)} %bitcast.16), custom_call_target="tpu_custom_call" | custom-call | flops 20971520 | bytes 6291456 | tf_op jit(solution)/shard_map/code_and_decode/pallas_call | solution.py:128
  28.8 0.1 collective-permute-start.6
  28.9 2.6 %collective-permute-done.6 = bf16[2,1024,256]{2,1,0:T(8,128)(2,1)S(1)} collective-permute-done((bf16[2,1024,256]{2,1,0:T(8,128)(2,1)S(1)}, bf16[2,1024,256]{2,1,0:T(8,128)(2,1)S(1)}, u32[]{:S(2)}, u32[]{:S(2)}) %collective-permute-start.6) | collective-permute-done | bytes 1048608 | tf_op jit(solution)/shard_map/ppermute | solution.py:24
  31.6 0.2 convert_add_fusion
  31.8 0.1 slice.23
  31.9 1.6 %collective-permute-start.7 = (bf16[1,1024,256]{2,1,0:T(8,128)(2,1)S(1)}, bf16[1,1024,256]{2,1,0:T(8,128)(2,1)S(1)}, u32[]{:S(2)}, u32[]{:S(2)}) collective-permute-start(bf16[1,1024,256]{2,1,0:T(8,128)(2,1)S(1)} %slice.23), channel_id=1, source_target_pairs={{0,16},{8,24},{16,0},{24,8},{1,17},{9,25},{17,1},{25,9},{2,18},{10... | collective-permute-start | bytes 1572872 | tf_op jit(solution)/shard_map/ppermute | solution.py:24
  33.4 12.5 %collective-permute-done.7 = bf16[1,1024,256]{2,1,0:T(8,128)(2,1)S(1)} collective-permute-done((bf16[1,1024,256]{2,1,0:T(8,128)(2,1)S(1)}, bf16[1,1024,256]{2,1,0:T(8,128)(2,1)S(1)}, u32[]{:S(2)}, u32[]{:S(2)}) %collective-permute-start.7) | collective-permute-done | bytes 524320 | tf_op jit(solution)/shard_map/ppermute | solution.py:24
  45.9 1.7 %fusion.2 = (bf16[1024,256]{1,0:T(8,128)(2,1)S(1)}, f32[1024,256]{1,0:T(8,128)}, f32[1024,256]{1,0:T(8,128)}) fusion(f32[1024,256]{1,0:T(8,128)S(1)} %copy-done.6, bf16[1,1024,256]{2,1,0:T(8,128)(2,1)S(1)} %collective-permute-done.7, f32[2,1024,256]{2,1,0:T(8,128)S(1)} %convert_add_fusion, f32[1024,256]{1,0:T(8,128)S(1)} %copy-done.7), kind=kLoop, calls=%fused_computation.7 | loop fusion | flops 2621440 | bytes 6291456 | tf_op jit(solution)/shard_map/convert_element_type | solution.py:297
  47.6 1.5 %collective-permute-start.9 = (bf16[1024,256]{1,0:T(8,128)(2,1)S(1)}, bf16[1024,256]{1,0:T(8,128)(2,1)S(1)}, u32[]{:S(2)}, u32[]{:S(2)}) collective-permute-start(bf16[1024,256]{1,0:T(8,128)(2,1)S(1)} %get-tuple-element.19.refs_7_), channel_id=1, source_target_pairs={{0,16},{8,24},{16,0},{24,8},{1,17},{9,25},{17,1},{25,9},{2,18},{10... | collective-permute-start | bytes 1572872 | tf_op jit(solution)/shard_map/ppermute | solution.py:24
  49.1 2.0 %collective-permute-start.4 = (bf16[128,1024]{1,0:T(8,128)(2,1)S(1)}, bf16[128,1024]{1,0:T(8,128)(2,1)S(1)}, u32[]{:S(2)}, u32[]{:S(2)}) collective-permute-start(bf16[128,1024]{1,0:T(8,128)(2,1)S(1)} %collective-permute-done.2.refs_4_), channel_id=1, source_target_pairs={{0,1},{1,0},{2,3},{3,2},{4,5},{5,4},{6,7},{7,6},{8,9},{9,8},{10,11... | collective-permute-start | bytes 786440 | tf_op jit(solution)/shard_map/ppermute | solution.py:24
  51.1 1.5 %collective-permute-start.5 = (bf16[128,1024]{1,0:T(8,128)(2,1)S(1)}, bf16[128,1024]{1,0:T(8,128)(2,1)S(1)}, u32[]{:S(2)}, u32[]{:S(2)}) collective-permute-start(bf16[128,1024]{1,0:T(8,128)(2,1)S(1)} %collective-permute-done.2.refs_4_), channel_id=1, source_target_pairs={{0,2},{1,3},{2,0},{3,1},{4,6},{5,7},{6,4},{7,5},{8,10},{9,11},{10,... | collective-permute-start | bytes 786440 | tf_op jit(solution)/shard_map/ppermute | solution.py:24
  52.5 0.6 collective-permute-start.3
  53.1 11.3 %collective-permute-done.5.refs_6_ = bf16[128,1024]{1,0:T(8,128)(2,1)S(1)} collective-permute-done((bf16[128,1024]{1,0:T(8,128)(2,1)S(1)}, bf16[128,1024]{1,0:T(8,128)(2,1)S(1)}, u32[]{:S(2)}, u32[]{:S(2)}) %collective-permute-start.5) | collective-permute-done | bytes 262176 | tf_op jit(solution)/shard_map/ppermute | solution.py:24
  64.5 3.0 %collective-permute-done.3.refs_3_ = bf16[128,1024]{1,0:T(8,128)(2,1)S(1)} collective-permute-done((bf16[128,1024]{1,0:T(8,128)(2,1)S(1)}, bf16[128,1024]{1,0:T(8,128)(2,1)S(1)}, u32[]{:S(2)}, u32[]{:S(2)}) %collective-permute-start.3) | collective-permute-done | bytes 262176 | tf_op jit(solution)/shard_map/ppermute | solution.py:24
  67.4 0.7 copy-done.15
  68.2 0.5 collective-permute-start.10
  68.7 3.4 %all-to-all-done.tokens_ref = bf16[8,1024,128]{2,1,0:T(8,128)(2,1)} async-done(((bf16[8,1024,128]{2,1,0:T(8,128)(2,1)}), bf16[8,1024,128]{2,1,0:T(8,128)(2,1)}, u32[]{:S(2)}, u32[]{:S(2)}) %all-to-all-start) | async-done | bytes 2097184 | tf_op jit(solution)/shard_map/all_to_all | solution.py:285
  72.2 7.0 %accumulate.1 = (f32[1024,1024]{1,0:T(8,128)}, bf16[1024,128]{1,0:T(8,128)(2,1)}) custom-call(s32[1]{0:T(128)} %bitcast.1.mine_ref, s32[1]{0:T(128)} %bitcast.own_ref, bf16[8,1024,128]{2,1,0:T(8,128)(2,1)} %all-to-all-done.tokens_ref, bf16[1024,1024]{1,0:T(8,128)(2,1)} %bitcast.15, bf16[128,1024]{1,0:T(8,128)(2,1)} %bitcast.23, ...), custom_call_target="tpu_custom_call" | custom-call | flops 1879048192 | bytes 12582912 | tf_op jit(solution)/shard_map/accumulate/pallas_call | solution.py:196
  79.2 2.2 %copy-done.1 = f32[1024,1024]{1,0:T(8,128)S(1)} copy-done((f32[1024,1024]{1,0:T(8,128)S(1)}, f32[1024,1024]{1,0:T(8,128)}, u32[]{:S(2)}) %copy-start.1) | copy-done | bytes 4194328
  81.4 0.9 %copy-done.4 = bf16[1024,128]{1,0:T(8,128)(2,1)S(1)} copy-done((bf16[1024,128]{1,0:T(8,128)(2,1)S(1)}, bf16[1024,128]{1,0:T(8,128)(2,1)}, u32[]{:S(2)}) %copy-start.4) | copy-done | bytes 262168
  82.4 1.9 %finish.1 = bf16[1024,1024]{1,0:T(8,128)(2,1)} custom-call(s32[1]{0:T(128)} %bitcast.own_ref, bf16[1024,128]{1,0:T(8,128)(2,1)S(1)} %copy-done.4, bf16[128,1024]{1,0:T(8,128)(2,1)S(1)} %collective-permute-done.10.cotangent_ref, f32[1024,1024]{1,0:T(8,128)S(1)} %copy-done.1, bf16[1024,256]{1,0:T(8,128)(2,1)S(1)} %collective-permute-done.11.piece_ref), custom_call_target="tpu_custom_call" | custom-call | flops 268435456 | bytes 7864320 | tf_op jit(solution)/shard_map/finish/pallas_call | solution.py:245
  (34 shorter events, 0.1 us)
Async XLA Ops:
  0.6 16.3 %collective-permute-start.2 = (bf16[128,1024]{1,0:T(8,128)(2,1)}, bf16[128,1024]{1,0:T(8,128)(2,1)S(1)}, u32[]{:S(2)}, u32[]{:S(2)}) collective-permute-start(bf16[128,1024]{1,0:T(8,128)(2,1)} %bitcast.20), channel_id=1, source_target_pairs={{0,4},{1,5},{2,6},{3,7},{4,0},{5,1},{6,2},{7,3},{8,12},{9,13},{10,... | collective-permute-start | bytes 786440 | tf_op jit(solution)/shard_map/ppermute | solution.py:24
  4.7 12.4 %collective-permute-start.1 = (bf16[128,1024]{1,0:T(8,128)(2,1)}, bf16[128,1024]{1,0:T(8,128)(2,1)S(1)}, u32[]{:S(2)}, u32[]{:S(2)}) collective-permute-start(bf16[128,1024]{1,0:T(8,128)(2,1)} %bitcast.21), channel_id=1, source_target_pairs={{0,2},{1,3},{2,0},{3,1},{4,6},{5,7},{6,4},{7,5},{8,10},{9,11},{10,... | collective-permute-start | bytes 786440 | tf_op jit(solution)/shard_map/ppermute | solution.py:24
  6.3 10.9 %collective-permute-start = (bf16[128,1024]{1,0:T(8,128)(2,1)}, bf16[128,1024]{1,0:T(8,128)(2,1)S(1)}, u32[]{:S(2)}, u32[]{:S(2)}) collective-permute-start(bf16[128,1024]{1,0:T(8,128)(2,1)} %bitcast.22), channel_id=1, source_target_pairs={{0,1},{1,0},{2,3},{3,2},{4,5},{5,4},{6,7},{7,6},{8,9},{9,8},{10,11... | collective-permute-start | bytes 786440 | tf_op jit(solution)/shard_map/ppermute | solution.py:24
  8.5 1.6 %copy-start.2 = (bf16[1,128,8192]{2,1,0:T(8,128)(2,1)S(1)}, bf16[1,128,8192]{2,1,0:T(8,128)(2,1)}, u32[]{:S(2)}) copy-start(bf16[1,128,8192]{2,1,0:T(8,128)(2,1)} %param.7) | copy-start | bytes 6291460
  17.0 34.1 %copy-start.10 = (bf16[128,1024]{1,0:T(8,128)(2,1)}, bf16[128,1024]{1,0:T(8,128)(2,1)S(1)}, u32[]{:S(2)}) copy-start(bf16[128,1024]{1,0:T(8,128)(2,1)S(1)} %collective-permute-done.2.refs_4_) | copy-start | bytes 786436
  17.2 35.4 %copy-start.11 = (bf16[128,1024]{1,0:T(8,128)(2,1)}, bf16[128,1024]{1,0:T(8,128)(2,1)S(1)}, u32[]{:S(2)}) copy-start(bf16[128,1024]{1,0:T(8,128)(2,1)S(1)} %collective-permute-done.1.refs_2_) | copy-start | bytes 786436
  17.2 0.8 copy-start.12
  17.2 6.4 %copy-start = (bf16[1,1024,1024]{2,1,0:T(8,128)(2,1)S(1)}, bf16[1,1024,1024]{2,1,0:T(8,128)(2,1)}, u32[]{:S(2)}) copy-start(bf16[1,1024,1024]{2,1,0:T(8,128)(2,1)} %param.10) | copy-start | bytes 6291460
  17.9 54.2 %all-to-all-start = ((bf16[8,1024,128]{2,1,0:T(8,128)(2,1)}), bf16[8,1024,128]{2,1,0:T(8,128)(2,1)}, u32[]{:S(2)}, u32[]{:S(2)}) async-start(bf16[8,1024,128]{2,1,0:T(8,128)(2,1)} %prepare.1), calls=%async_computation | async-start | bytes 4194304 | tf_op jit(solution)/shard_map/all_to_all | solution.py:285
  23.6 1.6 %copy-start.3 = (bf16[1024,1024]{1,0:T(8,128)(2,1)S(1)}, bf16[1024,1024]{1,0:T(8,128)(2,1)}, u32[]{:S(2)}) copy-start(bf16[1024,1024]{1,0:T(8,128)(2,1)} %shared_ref) | copy-start | bytes 6291460
  28.8 2.7 %collective-permute-start.6 = (bf16[2,1024,256]{2,1,0:T(8,128)(2,1)S(1)}, bf16[2,1024,256]{2,1,0:T(8,128)(2,1)S(1)}, u32[]{:S(2)}, u32[]{:S(2)}) collective-permute-start(bf16[2,1024,256]{2,1,0:T(8,128)(2,1)S(1)} %get-tuple-element.15), channel_id=1, source_target_pairs={{0,8},{8,0},{16,24},{24,16},{1,9},{9,1},{17,25},{25,17},{2,10},{10... | collective-permute-start | bytes 3145736 | tf_op jit(solution)/shard_map/ppermute | solution.py:24
  31.6 14.3 %copy-start.6 = (f32[1024,256]{1,0:T(8,128)S(1)}, f32[1024,256]{1,0:T(8,128)}, u32[]{:S(2)}) copy-start(f32[1024,256]{1,0:T(8,128)} %param.12) | copy-start | bytes 3145732
  31.6 14.3 %copy-start.7 = (f32[1024,256]{1,0:T(8,128)S(1)}, f32[1024,256]{1,0:T(8,128)}, u32[]{:S(2)}) copy-start(f32[1024,256]{1,0:T(8,128)} %param.13) | copy-start | bytes 3145732
  31.9 14.0 %collective-permute-start.7 = (bf16[1,1024,256]{2,1,0:T(8,128)(2,1)S(1)}, bf16[1,1024,256]{2,1,0:T(8,128)(2,1)S(1)}, u32[]{:S(2)}, u32[]{:S(2)}) collective-permute-start(bf16[1,1024,256]{2,1,0:T(8,128)(2,1)S(1)} %slice.23), channel_id=1, source_target_pairs={{0,16},{8,24},{16,0},{24,8},{1,17},{9,25},{17,1},{25,9},{2,18},{10... | collective-permute-start | bytes 1572872 | tf_op jit(solution)/shard_map/ppermute | solution.py:24
  47.6 24.6 %copy-start.5 = (bf16[1024,256]{1,0:T(8,128)(2,1)}, bf16[1024,256]{1,0:T(8,128)(2,1)S(1)}, u32[]{:S(2)}) copy-start(bf16[1024,256]{1,0:T(8,128)(2,1)S(1)} %get-tuple-element.19.refs_7_) | copy-start | bytes 1572868
  47.6 19.9 %collective-permute-start.9 = (bf16[1024,256]{1,0:T(8,128)(2,1)S(1)}, bf16[1024,256]{1,0:T(8,128)(2,1)S(1)}, u32[]{:S(2)}, u32[]{:S(2)}) collective-permute-start(bf16[1024,256]{1,0:T(8,128)(2,1)S(1)} %get-tuple-element.19.refs_7_), channel_id=1, source_target_pairs={{0,16},{8,24},{16,0},{24,8},{1,17},{9,25},{17,1},{25,9},{2,18},{10... | collective-permute-start | bytes 1572872 | tf_op jit(solution)/shard_map/ppermute | solution.py:24
  49.1 15.4 %collective-permute-start.4 = (bf16[128,1024]{1,0:T(8,128)(2,1)S(1)}, bf16[128,1024]{1,0:T(8,128)(2,1)S(1)}, u32[]{:S(2)}, u32[]{:S(2)}) collective-permute-start(bf16[128,1024]{1,0:T(8,128)(2,1)S(1)} %collective-permute-done.2.refs_4_), channel_id=1, source_target_pairs={{0,1},{1,0},{2,3},{3,2},{4,5},{5,4},{6,7},{7,6},{8,9},{9,8},{10,11... | collective-permute-start | bytes 786440 | tf_op jit(solution)/shard_map/ppermute | solution.py:24
  51.1 13.4 %collective-permute-start.5 = (bf16[128,1024]{1,0:T(8,128)(2,1)S(1)}, bf16[128,1024]{1,0:T(8,128)(2,1)S(1)}, u32[]{:S(2)}, u32[]{:S(2)}) collective-permute-start(bf16[128,1024]{1,0:T(8,128)(2,1)S(1)} %collective-permute-done.2.refs_4_), channel_id=1, source_target_pairs={{0,2},{1,3},{2,0},{3,1},{4,6},{5,7},{6,4},{7,5},{8,10},{9,11},{10,... | collective-permute-start | bytes 786440 | tf_op jit(solution)/shard_map/ppermute | solution.py:24
  52.5 14.9 %collective-permute-start.3 = (bf16[128,1024]{1,0:T(8,128)(2,1)S(1)}, bf16[128,1024]{1,0:T(8,128)(2,1)S(1)}, u32[]{:S(2)}, u32[]{:S(2)}) collective-permute-start(bf16[128,1024]{1,0:T(8,128)(2,1)S(1)} %collective-permute-done.1.refs_2_), channel_id=1, source_target_pairs={{0,1},{1,0},{2,3},{3,2},{4,5},{5,4},{6,7},{7,6},{8,9},{9,8},{10,11... | collective-permute-start | bytes 786440 | tf_op jit(solution)/shard_map/ppermute | solution.py:24
  53.1 15.6 %collective-permute-start.8 = (bf16[1024,256]{1,0:T(8,128)(2,1)S(1)}, bf16[1024,256]{1,0:T(8,128)(2,1)S(1)}, u32[]{:S(2)}, u32[]{:S(2)}) collective-permute-start(bf16[1024,256]{1,0:T(8,128)(2,1)S(1)} %get-tuple-element.19.refs_7_), channel_id=1, source_target_pairs={{0,8},{8,0},{16,24},{24,16},{1,9},{9,1},{17,25},{25,17},{2,10},{10... | collective-permute-start | bytes 1572872 | tf_op jit(solution)/shard_map/ppermute | solution.py:24
  64.5 7.7 %copy-start.14 = (bf16[128,1024]{1,0:T(8,128)(2,1)}, bf16[128,1024]{1,0:T(8,128)(2,1)S(1)}, u32[]{:S(2)}) copy-start(bf16[128,1024]{1,0:T(8,128)(2,1)S(1)} %collective-permute-done.5.refs_6_) | copy-start | bytes 786436
  64.5 7.7 %copy-start.13 = (bf16[128,1024]{1,0:T(8,128)(2,1)}, bf16[128,1024]{1,0:T(8,128)(2,1)S(1)}, u32[]{:S(2)}) copy-start(bf16[128,1024]{1,0:T(8,128)(2,1)S(1)} %collective-permute-done.4.refs_5_) | copy-start | bytes 786436
  67.4 0.7 copy-start.15
  68.2 4.0 %copy-start.8 = (bf16[1024,256]{1,0:T(8,128)(2,1)}, bf16[1024,256]{1,0:T(8,128)(2,1)S(1)}, u32[]{:S(2)}) copy-start(bf16[1024,256]{1,0:T(8,128)(2,1)S(1)} %collective-permute-done.9.refs_9_) | copy-start | bytes 1572868
  68.2 11.1 %collective-permute-start.11 = (bf16[1024,256]{1,0:T(8,128)(2,1)S(1)}, bf16[1024,256]{1,0:T(8,128)(2,1)S(1)}, u32[]{:S(2)}, u32[]{:S(2)}) collective-permute-start(bf16[1024,256]{1,0:T(8,128)(2,1)S(1)} %collective-permute-done.9.refs_9_), channel_id=1, source_target_pairs={{0,8},{8,0},{16,24},{24,16},{1,9},{9,1},{17,25},{25,17},{2,10},{10... | collective-permute-start | bytes 1572872 | tf_op jit(solution)/shard_map/ppermute | solution.py:24
  68.2 11.0 %collective-permute-start.10 = (bf16[128,1024]{1,0:T(8,128)(2,1)S(1)}, bf16[128,1024]{1,0:T(8,128)(2,1)S(1)}, u32[]{:S(2)}, u32[]{:S(2)}) collective-permute-start(bf16[128,1024]{1,0:T(8,128)(2,1)S(1)} %collective-permute-done.5.refs_6_), channel_id=1, source_target_pairs={{0,1},{1,0},{2,3},{3,2},{4,5},{5,4},{6,7},{7,6},{8,9},{9,8},{10,11... | collective-permute-start | bytes 786440 | tf_op jit(solution)/shard_map/ppermute | solution.py:24
  68.7 3.5 %copy-start.9 = (bf16[1024,256]{1,0:T(8,128)(2,1)}, bf16[1024,256]{1,0:T(8,128)(2,1)S(1)}, u32[]{:S(2)}) copy-start(bf16[1024,256]{1,0:T(8,128)(2,1)S(1)} %collective-permute-done.8.refs_8_) | copy-start | bytes 1572868
  79.2 2.2 %copy-start.1 = (f32[1024,1024]{1,0:T(8,128)S(1)}, f32[1024,1024]{1,0:T(8,128)}, u32[]{:S(2)}) copy-start(f32[1024,1024]{1,0:T(8,128)} %get-tuple-element.17.total_ref) | copy-start | bytes 12582916
  81.4 0.9 %copy-start.4 = (bf16[1024,128]{1,0:T(8,128)(2,1)S(1)}, bf16[1024,128]{1,0:T(8,128)(2,1)}, u32[]{:S(2)}) copy-start(bf16[1024,128]{1,0:T(8,128)(2,1)} %get-tuple-element.16.tokens_ref) | copy-start | bytes 786436

commit v23 on v19

--- a/solution.py
+++ b/solution.py
@@ -145,7 +145,7 @@
 def accumulate_kernel(parts, groups, rate, mine_ref, own_ref, tokens_ref, weight_ref, *refs):
     cotangent_refs, refs = refs[:parts], refs[parts:]
     piece_refs, refs = refs[: groups - 1], refs[groups - 1 :]
-    total_ref, last_ref, tokens, cotangents, weight, pieces, token_sems, cotangent_sems, piece_sems, sems = refs
+    total_ref, tokens, cotangents, weight, pieces, totals, token_sems, cotangent_sems, piece_sems, weight_sem, sems = refs
     mine, own = mine_ref[0], own_ref[0]
     depth, width = cotangent_refs[0].shape
     share = pieces.shape[2]
@@ -155,13 +155,13 @@
     for k, ref in enumerate(cotangent_refs):
         loads.append(pltpu.make_async_copy(tokens_ref.at[mine ^ k], tokens.at[k], token_sems.at[k]))
         loads.append(pltpu.make_async_copy(ref, cotangents.at[pl.ds(k * depth, depth)], cotangent_sems.at[k]))
-    rest.append(pltpu.make_async_copy(weight_ref, weight, sems.at[0]))
+    rest.append(pltpu.make_async_copy(weight_ref, weight, weight_sem))
     for k, ref in enumerate(piece_refs):
         rest.append(pltpu.make_async_copy(ref, pieces.at[own ^ k], piece_sems.at[k]))
-    rest.append(pltpu.make_async_copy(tokens_ref.at[mine ^ parts], last_ref, sems.at[1]))
     for load in loads + rest:
         load.start()
     pieces[own ^ (groups - 1)] = jnp.zeros(pieces.shape[1:], pieces.dtype)
+    stores = []
     some = 2
     for first in range(0, parts, some):
         end = min(first + some, parts)
@@ -169,13 +169,13 @@
             load.wait()
         left = jnp.concatenate([tokens[k] for k in range(first, end)], axis=1)
         for start in range(0, width, tile):
-            columns = slice(start, start + tile)
+            columns = pl.ds(start, tile)
             right = cotangents[first * depth : end * depth, columns]
             total = jnp.dot(left, right, preferred_element_type=jnp.float32)
             if first:
-                total = total_ref[:, columns] + total
+                total = totals[:, columns] + total
             if end < parts:
-                total_ref[:, columns] = total
+                totals[:, columns] = total
                 continue
             if start == 0:
                 for load in rest:
@@ -185,7 +185,11 @@
                 part = slice(group * share - start, (group + 1) * share - start)
                 mixed = mix_weight * weight[:, place].astype(jnp.float32)
                 mixed = mixed + (1.0 - mix_weight) * pieces[group].astype(jnp.float32)
-                total_ref[:, place] = mixed - rate * total[:, part]
+                totals[:, place] = mixed - rate * total[:, part]
+            stores.append(pltpu.make_async_copy(totals.at[:, columns], total_ref.at[:, columns], sems.at[start // tile]))
+            stores[-1].start()
+    for store in stores:
+        store.wait()
 
 
 def accumulate(mine, own, tokens, cotangents, weight, pieces, rate):
@@ -195,19 +199,21 @@
     width = cotangents[0].shape[1]
     return pl.pallas_call(
         functools.partial(accumulate_kernel, parts, groups, rate),
-        out_shape=(jax.ShapeDtypeStruct((rows, width), jnp.float32), jax.ShapeDtypeStruct((rows, depth), jnp.bfloat16)),
+        out_shape=jax.ShapeDtypeStruct((rows, width), jnp.float32),
         in_specs=[pl.BlockSpec(memory_space=pltpu.SMEM)] * 2
         + [pl.BlockSpec(memory_space=pltpu.HBM)] * (1 + parts + groups),
-        out_specs=(pl.BlockSpec(memory_space=pltpu.VMEM),) * 2,
+        out_specs=pl.BlockSpec(memory_space=pltpu.HBM),
         scratch_shapes=[
             pltpu.VMEM((parts, rows, depth), jnp.bfloat16),
             pltpu.VMEM((parts * depth, width), jnp.bfloat16),
             pltpu.VMEM((rows, width), jnp.bfloat16),
             pltpu.VMEM((groups, rows, width // groups), jnp.bfloat16),
+            pltpu.VMEM((rows, width), jnp.float32),
             pltpu.SemaphoreType.DMA((parts,)),
             pltpu.SemaphoreType.DMA((parts,)),
             pltpu.SemaphoreType.DMA((groups,)),
-            pltpu.SemaphoreType.DMA((2,)),
+            pltpu.SemaphoreType.DMA,
+            pltpu.SemaphoreType.DMA((width // max(width // groups, 256),)),
         ],
         compiler_params=pltpu.CompilerParams(vmem_limit_bytes=58880 * 2**10),
         cost_estimate=pl.CostEstimate(
@@ -219,14 +225,24 @@
     )(mine.reshape(1), own.reshape(1), tokens, weight, *cotangents, *pieces)
 
 
-def finish_kernel(groups, rate, own_ref, tokens_ref, cotangent_ref, total_ref, piece_ref, out_ref, outs, sems):
+def finish_kernel(groups, rate, mine_ref, own_ref, tokens_ref, total_ref, cotangent_ref, piece_ref, out_ref, *refs):
+    outs, tokens, totals, sems, token_sem, total_sems = refs
     share = piece_ref.shape[1]
     steps, _, tile = outs.shape
+    last = tokens_ref.shape[0] - 1
+    loads = [pltpu.make_async_copy(tokens_ref.at[mine_ref[0] ^ last], tokens, token_sem)]
+    for step in range(steps):
+        place = pl.ds(step * tile, tile)
+        loads.append(pltpu.make_async_copy(total_ref.at[:, place], totals.at[:, place], total_sems.at[step]))
+    for load in loads:
+        load.start()
+    loads[0].wait()
     stores = []
     for step in range(steps):
         columns = slice(step * tile, (step + 1) * tile)
-        product = jnp.dot(tokens_ref[...], cotangent_ref[:, columns], preferred_element_type=jnp.float32)
-        total = total_ref[:, columns] - rate * product
+        loads[step + 1].wait()
+        product = jnp.dot(tokens[...], cotangent_ref[:, columns], preferred_element_type=jnp.float32)
+        total = totals[:, columns] - rate * product
         for group in range(step * tile // share, (step + 1) * tile // share):
             part = slice(group * share - step * tile, (group + 1) * share - step * tile)
             factor = jnp.where((own_ref[0] ^ (groups - 1)) == group, 1.0 - mix_weight, 0.0)
@@ -237,23 +253,32 @@
         store.wait()
 
 
-def finish(own, tokens, cotangent, total, piece, rate):
+def finish(mine, own, tokens, cotangent, total, piece, rate):
     rows, width = total.shape
-    depth = tokens.shape[1]
+    depth = tokens.shape[2]
     share = piece.shape[1]
     tile = max(share, 256)
     return pl.pallas_call(
         functools.partial(finish_kernel, width // share, rate),
         out_shape=jax.ShapeDtypeStruct((rows, width), jnp.bfloat16),
-        in_specs=[pl.BlockSpec(memory_space=pltpu.SMEM)] + [pl.BlockSpec(memory_space=pltpu.VMEM)] * 4,
+        in_specs=[pl.BlockSpec(memory_space=pltpu.SMEM)] * 2
+        + [pl.BlockSpec(memory_space=pltpu.HBM)] * 2
+        + [pl.BlockSpec(memory_space=pltpu.VMEM)] * 2,
         out_specs=pl.BlockSpec(memory_space=pltpu.HBM),
-        scratch_shapes=[pltpu.VMEM((width // tile, rows, tile), jnp.bfloat16), pltpu.SemaphoreType.DMA((width // tile,))],
-        compiler_params=pltpu.CompilerParams(vmem_limit_bytes=16 * 2**20),
+        scratch_shapes=[
+            pltpu.VMEM((width // tile, rows, tile), jnp.bfloat16),
+            pltpu.VMEM((rows, depth), jnp.bfloat16),
+            pltpu.VMEM((rows, width), jnp.float32),
+            pltpu.SemaphoreType.DMA((width // tile,)),
+            pltpu.SemaphoreType.DMA,
+            pltpu.SemaphoreType.DMA((width // tile,)),
+        ],
+        compiler_params=pltpu.CompilerParams(vmem_limit_bytes=46 * 2**20),
         cost_estimate=pl.CostEstimate(
             flops=2 * depth * rows * width, bytes_accessed=2 * depth * (rows + width) + 7 * rows * width, transcendentals=0
         ),
         name="finish",
-    )(own.reshape(1), tokens, cotangent, total, piece)
+    )(mine.reshape(1), own.reshape(1), tokens, total, cotangent, piece)
 
 
 def gather(piece, axis, size, after=()):
@@ -297,8 +322,8 @@
     pieces = gather(master_next.astype(jnp.bfloat16), "replica", groups, after=cotangents[:-1])
 
     rate = (1.0 - mix_weight) * inner_rate
-    total, last = accumulate(mine, own, columns, cotangents[:-1], weight, pieces[:-1], rate)
-    layer_next = finish(own, last, cotangents[-1], total, pieces[-1], rate)
+    total = accumulate(mine, own, columns, cotangents[:-1], weight, pieces[:-1], rate)
+    layer_next = finish(mine, own, columns, cotangents[-1], total, pieces[-1], rate)
     return (layer_next[None], master_next, momentum_next)
 
 

time: 84.7 us -> 86.8 us (1.025)
  waiting for transfers between devices: 37.7 us -> 33.5 us
  local copies, waits for them, and re-layouts: 7.87 us -> 11.9 us
  starting transfers between devices: 20.5 us -> 21.8 us
  Pallas kernels: 14.9 us -> 15.9 us
    unnamed x32 -> x28, local copies, waits for them, and re-layouts: 7.82 us -> 11.8 us
    all_to_all x1, waiting for transfers between devices: 3.44 us -> 1.27 us  [on_device(): lax.all_to_all(blocks, 'fsdp', split_axis=0, concat_axis=0, tiled=True)]
    ppermute x12, waiting for transfers between devices: 34.3 us -> 32.2 us  [swap(): return lax.ppermute(value, axis, [(i, i ^ mask) for i in range(size)])]
    pallas_call x1, Pallas kernels: 1.95 us -> 3.57 us  [finish(): pl.pallas_call(functools.partial(finish_kernel, width // share, rate), ou...]
    ppermute x12, starting transfers between devices: 14.9 us -> 16.3 us  [swap(): return lax.ppermute(value, axis, [(i, i ^ mask) for i in range(size)])]
  transfers between devices with their start and end apart: 13 -> 13, of which waited for: 7 -> 7; matrix products, arithmetic and copies ran while one was open for 3% -> 3% of each run, Pallas kernels for 15% -> 14%
where the time goes in v23:
time: 86.8 us; the launch traced here: 86.4 us
  waiting for transfers between devices  33.5 us (39%)
  starting transfers between devices  21.8 us (25%)
  Pallas kernels  15.9 us (18%)
  local copies, waits for them, and re-layouts  11.9 us (14%)
  other arithmetic  2.64 us (3%)
    ppermute x12, waiting for transfers between devices, swap(): return lax.ppermute(value, axis, [(i, i ^ mask) for i in range(size)])  32.2 us
    ppermute x12, starting transfers between devices, swap(): return lax.ppermute(value, axis, [(i, i ^ mask) for i in range(size)])  16.3 us
    unnamed x28, local copies, waits for them, and re-layouts  11.8 us
    pallas_call x1, Pallas kernels, accumulate(): pl.pallas_call(functools.partial(accumulate_kernel, parts, groups, rate),...  6.57 us
    all_to_all x1, starting transfers between devices, on_device(): lax.all_to_all(blocks, 'fsdp', split_axis=0, concat_axis=0, tiled=True)  5.49 us
    pallas_call x1, Pallas kernels, code_and_decode(): pl.pallas_call(code_kernel, out_shape=(half, half), in_specs=[pl.BlockSpe...  3.69 us
    pallas_call x1, Pallas kernels, finish(): pl.pallas_call(functools.partial(finish_kernel, width // share, rate), ou...  3.57 us
    pallas_call x1, Pallas kernels, prepare(): pl.pallas_call(prepare_kernel, out_shape=jax.ShapeDtypeStruct((shards, ro...  2.04 us
  transfers between devices with their start and end apart: 13, of which 7 were waited for; matrix products, arithmetic and copies ran while one was open for 3% of the time, Pallas kernels for 14%

profile of v23, /device:TPU:0, one launch (start us, length us, event | category | flops | bytes accessed | tf_op | source)
XLA Modules:
  0.0 86.4 jit_solution(16396106089593999310)
XLA Ops:
  0.6 4.1 %collective-permute-start.2 = (bf16[128,1024]{1,0:T(8,128)(2,1)}, bf16[128,1024]{1,0:T(8,128)(2,1)S(1)}, u32[]{:S(2)}, u32[]{:S(2)}) collective-permute-start(bf16[128,1024]{1,0:T(8,128)(2,1)} %bitcast.20), channel_id=1, source_target_pairs={{0,4},{1,5},{2,6},{3,7},{4,0},{5,1},{6,2},{7,3},{8,12},{9,13},{10,... | collective-permute-start | bytes 786440 | tf_op jit(solution)/shard_map/ppermute | solution.py:24
  4.7 1.6 %collective-permute-start.1 = (bf16[128,1024]{1,0:T(8,128)(2,1)}, bf16[128,1024]{1,0:T(8,128)(2,1)S(1)}, u32[]{:S(2)}, u32[]{:S(2)}) collective-permute-start(bf16[128,1024]{1,0:T(8,128)(2,1)} %bitcast.21), channel_id=1, source_target_pairs={{0,2},{1,3},{2,0},{3,1},{4,6},{5,7},{6,4},{7,5},{8,10},{9,11},{10,... | collective-permute-start | bytes 786440 | tf_op jit(solution)/shard_map/ppermute | solution.py:24
  6.3 1.5 %collective-permute-start = (bf16[128,1024]{1,0:T(8,128)(2,1)}, bf16[128,1024]{1,0:T(8,128)(2,1)}, u32[]{:S(2)}, u32[]{:S(2)}) collective-permute-start(bf16[128,1024]{1,0:T(8,128)(2,1)} %bitcast.22), channel_id=1, source_target_pairs={{0,1},{1,0},{2,3},{3,2},{4,5},{5,4},{6,7},{7,6},{8,9},{9,8},{10,11... | collective-permute-start | bytes 786440 | tf_op jit(solution)/shard_map/ppermute | solution.py:24
  7.8 0.7 reshape.26
  8.6 1.6 %copy-done.5 = bf16[1,128,8192]{2,1,0:T(8,128)(2,1)S(1)} copy-done((bf16[1,128,8192]{2,1,0:T(8,128)(2,1)S(1)}, bf16[1,128,8192]{2,1,0:T(8,128)(2,1)}, u32[]{:S(2)}) %copy-start.5) | copy-done | bytes 2097176
  10.1 2.0 %prepare.1 = bf16[8,1024,128]{2,1,0:T(8,128)(2,1)S(1)} custom-call(bf16[128,8192]{1,0:T(8,128)(2,1)S(1)} %bitcast.17, f32[1,8192]{1,0:T(1,128)S(1)} %bitcast.18), custom_call_target="tpu_custom_call" | custom-call | flops 5242880 | bytes 4194304 | tf_op jit(solution)/shard_map/prepare/pallas_call | solution.py:58
  12.2 1.3 %copy-done.3 = bf16[8,1024,128]{2,1,0:T(8,128)(2,1)} copy-done((bf16[8,1024,128]{2,1,0:T(8,128)(2,1)}, bf16[8,1024,128]{2,1,0:T(8,128)(2,1)S(1)}, u32[]{:S(2)}) %copy-start.3) | copy-done | bytes 2097176
  13.5 3.5 %collective-permute-done.2.refs_4_ = bf16[128,1024]{1,0:T(8,128)(2,1)S(1)} collective-permute-done((bf16[128,1024]{1,0:T(8,128)(2,1)}, bf16[128,1024]{1,0:T(8,128)(2,1)S(1)}, u32[]{:S(2)}, u32[]{:S(2)}) %collective-permute-start.2) | collective-permute-done | bytes 262176 | tf_op jit(solution)/shard_map/ppermute | solution.py:24
  17.0 0.2 collective-permute-done.1.refs_2_
  17.2 5.5 %all-to-all-start = ((bf16[8,1024,128]{2,1,0:T(8,128)(2,1)}), bf16[8,1024,128]{2,1,0:T(8,128)(2,1)S(1)}, u32[]{:S(2)}, u32[]{:S(2)}) async-start(bf16[8,1024,128]{2,1,0:T(8,128)(2,1)} %copy-done.3), calls=%async_computation | async-start | bytes 4194304 | tf_op jit(solution)/shard_map/all_to_all | solution.py:310
  22.7 1.6 %copy-done.4 = bf16[1,1024,1024]{2,1,0:T(8,128)(2,1)S(1)} copy-done((bf16[1,1024,1024]{2,1,0:T(8,128)(2,1)S(1)}, bf16[1,1024,1024]{2,1,0:T(8,128)(2,1)}, u32[]{:S(2)}) %copy-start.4) | copy-done | bytes 2097176
  24.3 1.6 %copy-done.6 = bf16[1024,1024]{1,0:T(8,128)(2,1)S(1)} copy-done((bf16[1024,1024]{1,0:T(8,128)(2,1)S(1)}, bf16[1024,1024]{1,0:T(8,128)(2,1)}, u32[]{:S(2)}) %copy-start.6) | copy-done | bytes 2097176
  25.8 3.7 %code_and_decode.1 = (bf16[2,1024,256]{2,1,0:T(8,128)(2,1)S(1)}, bf16[2,1024,256]{2,1,0:T(8,128)(2,1)S(1)}) custom-call(s32[1]{0:T(128)} %bitcast.1.own_ref, bf16[1024,1024]{1,0:T(8,128)(2,1)S(1)} %copy-done.6, bf16[1024,1024]{1,0:T(8,128)(2,1)S(1)} %bitcast.16), custom_call_target="tpu_custom_call" | custom-call | flops 20971520 | bytes 6291456 | tf_op jit(solution)/shard_map/code_and_decode/pallas_call | solution.py:128
  29.6 2.6 %collective-permute-done.6 = bf16[2,1024,256]{2,1,0:T(8,128)(2,1)S(1)} collective-permute-done((bf16[2,1024,256]{2,1,0:T(8,128)(2,1)S(1)}, bf16[2,1024,256]{2,1,0:T(8,128)(2,1)S(1)}, u32[]{:S(2)}, u32[]{:S(2)}) %collective-permute-start.6) | collective-permute-done | bytes 1048608 | tf_op jit(solution)/shard_map/ppermute | solution.py:24
  32.3 0.3 convert_add_fusion
  32.6 1.6 %collective-permute-start.7 = (bf16[1,1024,256]{2,1,0:T(8,128)(2,1)S(1)}, bf16[1,1024,256]{2,1,0:T(8,128)(2,1)S(1)}, u32[]{:S(2)}, u32[]{:S(2)}) collective-permute-start(bf16[1,1024,256]{2,1,0:T(8,128)(2,1)S(1)} %slice.23), channel_id=1, source_target_pairs={{0,16},{8,24},{16,0},{24,8},{1,17},{9,25},{17,1},{25,9},{2,18},{10... | collective-permute-start | bytes 1572872 | tf_op jit(solution)/shard_map/ppermute | solution.py:24
  34.2 12.5 %collective-permute-done.7 = bf16[1,1024,256]{2,1,0:T(8,128)(2,1)S(1)} collective-permute-done((bf16[1,1024,256]{2,1,0:T(8,128)(2,1)S(1)}, bf16[1,1024,256]{2,1,0:T(8,128)(2,1)S(1)}, u32[]{:S(2)}, u32[]{:S(2)}) %collective-permute-start.7) | collective-permute-done | bytes 524320 | tf_op jit(solution)/shard_map/ppermute | solution.py:24
  46.6 1.7 %fusion.2 = (bf16[1024,256]{1,0:T(8,128)(2,1)S(1)}, f32[1024,256]{1,0:T(8,128)}, f32[1024,256]{1,0:T(8,128)}) fusion(f32[1024,256]{1,0:T(8,128)S(1)} %copy-done.8, bf16[1,1024,256]{2,1,0:T(8,128)(2,1)S(1)} %collective-permute-done.7, f32[2,1024,256]{2,1,0:T(8,128)S(1)} %convert_add_fusion, f32[1024,256]{1,0:T(8,128)S(1)} %copy-done.9), kind=kLoop, calls=%fused_computation.7 | loop fusion | flops 2621440 | bytes 6291456 | tf_op jit(solution)/shard_map/convert_element_type | solution.py:322
  48.3 1.5 %collective-permute-start.9 = (bf16[1024,256]{1,0:T(8,128)(2,1)S(1)}, bf16[1024,256]{1,0:T(8,128)(2,1)}, u32[]{:S(2)}, u32[]{:S(2)}) collective-permute-start(bf16[1024,256]{1,0:T(8,128)(2,1)S(1)} %get-tuple-element.15.refs_7_), channel_id=1, source_target_pairs={{0,16},{8,24},{16,0},{24,8},{1,17},{9,25},{17,1},{25,9},{2,18},{10... | collective-permute-start | bytes 1572872 | tf_op jit(solution)/shard_map/ppermute | solution.py:24
  49.8 2.0 %collective-permute-start.4 = (bf16[128,1024]{1,0:T(8,128)(2,1)S(1)}, bf16[128,1024]{1,0:T(8,128)(2,1)S(1)}, u32[]{:S(2)}, u32[]{:S(2)}) collective-permute-start(bf16[128,1024]{1,0:T(8,128)(2,1)S(1)} %collective-permute-done.2.refs_4_), channel_id=1, source_target_pairs={{0,1},{1,0},{2,3},{3,2},{4,5},{5,4},{6,7},{7,6},{8,9},{9,8},{10,11... | collective-permute-start | bytes 786440 | tf_op jit(solution)/shard_map/ppermute | solution.py:24
  51.8 1.5 %collective-permute-start.5 = (bf16[128,1024]{1,0:T(8,128)(2,1)S(1)}, bf16[128,1024]{1,0:T(8,128)(2,1)}, u32[]{:S(2)}, u32[]{:S(2)}) collective-permute-start(bf16[128,1024]{1,0:T(8,128)(2,1)S(1)} %collective-permute-done.2.refs_4_), channel_id=1, source_target_pairs={{0,2},{1,3},{2,0},{3,1},{4,6},{5,7},{6,4},{7,5},{8,10},{9,11},{10,... | collective-permute-start | bytes 786440 | tf_op jit(solution)/shard_map/ppermute | solution.py:24
  53.3 0.6 collective-permute-start.3
  53.8 9.7 %collective-permute-done.5.refs_6_ = bf16[128,1024]{1,0:T(8,128)(2,1)} collective-permute-done((bf16[128,1024]{1,0:T(8,128)(2,1)S(1)}, bf16[128,1024]{1,0:T(8,128)(2,1)}, u32[]{:S(2)}, u32[]{:S(2)}) %collective-permute-start.5) | collective-permute-done | bytes 262176 | tf_op jit(solution)/shard_map/ppermute | solution.py:24
  63.5 3.8 %collective-permute-done.3.refs_3_ = bf16[128,1024]{1,0:T(8,128)(2,1)S(1)} collective-permute-done((bf16[128,1024]{1,0:T(8,128)(2,1)S(1)}, bf16[128,1024]{1,0:T(8,128)(2,1)S(1)}, u32[]{:S(2)}, u32[]{:S(2)}) %collective-permute-start.3) | collective-permute-done | bytes 262176 | tf_op jit(solution)/shard_map/ppermute | solution.py:24
  67.4 0.6 copy-done.13
  68.0 1.8 %collective-permute-start.10 = (bf16[128,1024]{1,0:T(8,128)(2,1)}, bf16[128,1024]{1,0:T(8,128)(2,1)S(1)}, u32[]{:S(2)}, u32[]{:S(2)}) collective-permute-start(bf16[128,1024]{1,0:T(8,128)(2,1)} %collective-permute-done.5.refs_6_), channel_id=1, source_target_pairs={{0,1},{1,0},{2,3},{3,2},{4,5},{5,4},{6,7},{7,6},{8,9},{9,8},{10,11... | collective-permute-start | bytes 786440 | tf_op jit(solution)/shard_map/ppermute | solution.py:24
  69.9 1.3 %all-to-all-done.tokens_ref = bf16[8,1024,128]{2,1,0:T(8,128)(2,1)S(1)} async-done(((bf16[8,1024,128]{2,1,0:T(8,128)(2,1)}), bf16[8,1024,128]{2,1,0:T(8,128)(2,1)S(1)}, u32[]{:S(2)}, u32[]{:S(2)}) %all-to-all-start) | async-done | bytes 2097184 | tf_op jit(solution)/shard_map/all_to_all | solution.py:310
  71.1 1.3 %copy-done = bf16[8,1024,128]{2,1,0:T(8,128)(2,1)} copy-done((bf16[8,1024,128]{2,1,0:T(8,128)(2,1)}, bf16[8,1024,128]{2,1,0:T(8,128)(2,1)S(1)}, u32[]{:S(2)}) %copy-start) | copy-done | bytes 2097176
  72.4 6.6 %accumulate.1.total_ref = f32[1024,1024]{1,0:T(8,128)} custom-call(s32[1]{0:T(128)} %bitcast.mine_ref, s32[1]{0:T(128)} %bitcast.1.own_ref, bf16[8,1024,128]{2,1,0:T(8,128)(2,1)} %copy-done, bf16[1024,1024]{1,0:T(8,128)(2,1)} %bitcast.15, bf16[128,1024]{1,0:T(8,128)(2,1)} %bitcast.23, bf16[128,1024]{1,0:T(8,128)(2,1)} %collective-permute-done.refs_1_, ...), custom_call_target="tpu_custom_call" | custom-call | flops 1879048192 | bytes 12582912 | tf_op jit(solution)/shard_map/accumulate/pallas_call | solution.py:200
  79.1 1.6 %copy-done.1 = bf16[8,1024,128]{2,1,0:T(8,128)(2,1)S(1)} copy-done((bf16[8,1024,128]{2,1,0:T(8,128)(2,1)S(1)}, bf16[8,1024,128]{2,1,0:T(8,128)(2,1)}, u32[]{:S(2)}) %copy-start.1) | copy-done | bytes 2097176
  80.6 2.2 %copy-done.2 = f32[1024,1024]{1,0:T(8,128)S(1)} copy-done((f32[1024,1024]{1,0:T(8,128)S(1)}, f32[1024,1024]{1,0:T(8,128)}, u32[]{:S(2)}) %copy-start.2) | copy-done | bytes 4194328
  82.8 3.6 %finish.1 = bf16[1024,1024]{1,0:T(8,128)(2,1)} custom-call(s32[1]{0:T(128)} %bitcast.mine_ref, s32[1]{0:T(128)} %bitcast.1.own_ref, bf16[8,1024,128]{2,1,0:T(8,128)(2,1)S(1)} %copy-done.1, f32[1024,1024]{1,0:T(8,128)S(1)} %copy-done.2, bf16[128,1024]{1,0:T(8,128)(2,1)S(1)} %collective-permute-done.10.cotangent_ref, ...), custom_call_target="tpu_custom_call" | custom-call | flops 268435456 | bytes 7864320 | tf_op jit(solution)/shard_map/finish/pallas_call | solution.py:261
  (30 shorter events, 0.3 us)
Async XLA Ops:
  0.6 16.3 %collective-permute-start.2 = (bf16[128,1024]{1,0:T(8,128)(2,1)}, bf16[128,1024]{1,0:T(8,128)(2,1)S(1)}, u32[]{:S(2)}, u32[]{:S(2)}) collective-permute-start(bf16[128,1024]{1,0:T(8,128)(2,1)} %bitcast.20), channel_id=1, source_target_pairs={{0,4},{1,5},{2,6},{3,7},{4,0},{5,1},{6,2},{7,3},{8,12},{9,13},{10,... | collective-permute-start | bytes 786440 | tf_op jit(solution)/shard_map/ppermute | solution.py:24
  4.7 12.4 %collective-permute-start.1 = (bf16[128,1024]{1,0:T(8,128)(2,1)}, bf16[128,1024]{1,0:T(8,128)(2,1)S(1)}, u32[]{:S(2)}, u32[]{:S(2)}) collective-permute-start(bf16[128,1024]{1,0:T(8,128)(2,1)} %bitcast.21), channel_id=1, source_target_pairs={{0,2},{1,3},{2,0},{3,1},{4,6},{5,7},{6,4},{7,5},{8,10},{9,11},{10,... | collective-permute-start | bytes 786440 | tf_op jit(solution)/shard_map/ppermute | solution.py:24
  6.3 10.9 %collective-permute-start = (bf16[128,1024]{1,0:T(8,128)(2,1)}, bf16[128,1024]{1,0:T(8,128)(2,1)}, u32[]{:S(2)}, u32[]{:S(2)}) collective-permute-start(bf16[128,1024]{1,0:T(8,128)(2,1)} %bitcast.22), channel_id=1, source_target_pairs={{0,1},{1,0},{2,3},{3,2},{4,5},{5,4},{6,7},{7,6},{8,9},{9,8},{10,11... | collective-permute-start | bytes 786440 | tf_op jit(solution)/shard_map/ppermute | solution.py:24
  8.5 1.6 %copy-start.5 = (bf16[1,128,8192]{2,1,0:T(8,128)(2,1)S(1)}, bf16[1,128,8192]{2,1,0:T(8,128)(2,1)}, u32[]{:S(2)}) copy-start(bf16[1,128,8192]{2,1,0:T(8,128)(2,1)} %param.7) | copy-start | bytes 6291460
  12.2 1.3 %copy-start.3 = (bf16[8,1024,128]{2,1,0:T(8,128)(2,1)}, bf16[8,1024,128]{2,1,0:T(8,128)(2,1)S(1)}, u32[]{:S(2)}) copy-start(bf16[8,1024,128]{2,1,0:T(8,128)(2,1)S(1)} %prepare.1) | copy-start | bytes 6291460
  17.0 34.8 %copy-start.10 = (bf16[128,1024]{1,0:T(8,128)(2,1)}, bf16[128,1024]{1,0:T(8,128)(2,1)S(1)}, u32[]{:S(2)}) copy-start(bf16[128,1024]{1,0:T(8,128)(2,1)S(1)} %collective-permute-done.2.refs_4_) | copy-start | bytes 786436
  17.2 36.1 %copy-start.11 = (bf16[128,1024]{1,0:T(8,128)(2,1)}, bf16[128,1024]{1,0:T(8,128)(2,1)S(1)}, u32[]{:S(2)}) copy-start(bf16[128,1024]{1,0:T(8,128)(2,1)S(1)} %collective-permute-done.1.refs_2_) | copy-start | bytes 786436
  17.2 54.0 %all-to-all-start = ((bf16[8,1024,128]{2,1,0:T(8,128)(2,1)}), bf16[8,1024,128]{2,1,0:T(8,128)(2,1)S(1)}, u32[]{:S(2)}, u32[]{:S(2)}) async-start(bf16[8,1024,128]{2,1,0:T(8,128)(2,1)} %copy-done.3), calls=%async_computation | async-start | bytes 4194304 | tf_op jit(solution)/shard_map/all_to_all | solution.py:310
  22.7 1.6 %copy-start.4 = (bf16[1,1024,1024]{2,1,0:T(8,128)(2,1)S(1)}, bf16[1,1024,1024]{2,1,0:T(8,128)(2,1)}, u32[]{:S(2)}) copy-start(bf16[1,1024,1024]{2,1,0:T(8,128)(2,1)} %param.10) | copy-start | bytes 6291460
  24.3 1.6 %copy-start.6 = (bf16[1024,1024]{1,0:T(8,128)(2,1)S(1)}, bf16[1024,1024]{1,0:T(8,128)(2,1)}, u32[]{:S(2)}) copy-start(bf16[1024,1024]{1,0:T(8,128)(2,1)} %shared_ref) | copy-start | bytes 6291460
  29.5 2.7 %collective-permute-start.6 = (bf16[2,1024,256]{2,1,0:T(8,128)(2,1)S(1)}, bf16[2,1024,256]{2,1,0:T(8,128)(2,1)S(1)}, u32[]{:S(2)}, u32[]{:S(2)}) collective-permute-start(bf16[2,1024,256]{2,1,0:T(8,128)(2,1)S(1)} %get-tuple-element.13), channel_id=1, source_target_pairs={{0,8},{8,0},{16,24},{24,16},{1,9},{9,1},{17,25},{25,17},{2,10},{10... | collective-permute-start | bytes 3145736 | tf_op jit(solution)/shard_map/ppermute | solution.py:24
  32.3 14.4 %copy-start.8 = (f32[1024,256]{1,0:T(8,128)S(1)}, f32[1024,256]{1,0:T(8,128)}, u32[]{:S(2)}) copy-start(f32[1024,256]{1,0:T(8,128)} %param.12) | copy-start | bytes 3145732
  32.3 14.4 %copy-start.9 = (f32[1024,256]{1,0:T(8,128)S(1)}, f32[1024,256]{1,0:T(8,128)}, u32[]{:S(2)}) copy-start(f32[1024,256]{1,0:T(8,128)} %param.13) | copy-start | bytes 3145732
  32.6 14.0 %collective-permute-start.7 = (bf16[1,1024,256]{2,1,0:T(8,128)(2,1)S(1)}, bf16[1,1024,256]{2,1,0:T(8,128)(2,1)S(1)}, u32[]{:S(2)}, u32[]{:S(2)}) collective-permute-start(bf16[1,1024,256]{2,1,0:T(8,128)(2,1)S(1)} %slice.23), channel_id=1, source_target_pairs={{0,16},{8,24},{16,0},{24,8},{1,17},{9,25},{17,1},{25,9},{2,18},{10... | collective-permute-start | bytes 1572872 | tf_op jit(solution)/shard_map/ppermute | solution.py:24
  48.3 22.8 %copy-start.7 = (bf16[1024,256]{1,0:T(8,128)(2,1)}, bf16[1024,256]{1,0:T(8,128)(2,1)S(1)}, u32[]{:S(2)}) copy-start(bf16[1024,256]{1,0:T(8,128)(2,1)S(1)} %get-tuple-element.15.refs_7_) | copy-start | bytes 1572868
  48.3 19.0 %collective-permute-start.9 = (bf16[1024,256]{1,0:T(8,128)(2,1)S(1)}, bf16[1024,256]{1,0:T(8,128)(2,1)}, u32[]{:S(2)}, u32[]{:S(2)}) collective-permute-start(bf16[1024,256]{1,0:T(8,128)(2,1)S(1)} %get-tuple-element.15.refs_7_), channel_id=1, source_target_pairs={{0,16},{8,24},{16,0},{24,8},{1,17},{9,25},{17,1},{25,9},{2,18},{10... | collective-permute-start | bytes 1572872 | tf_op jit(solution)/shard_map/ppermute | solution.py:24
  49.8 13.7 %collective-permute-start.4 = (bf16[128,1024]{1,0:T(8,128)(2,1)S(1)}, bf16[128,1024]{1,0:T(8,128)(2,1)S(1)}, u32[]{:S(2)}, u32[]{:S(2)}) collective-permute-start(bf16[128,1024]{1,0:T(8,128)(2,1)S(1)} %collective-permute-done.2.refs_4_), channel_id=1, source_target_pairs={{0,1},{1,0},{2,3},{3,2},{4,5},{5,4},{6,7},{7,6},{8,9},{9,8},{10,11... | collective-permute-start | bytes 786440 | tf_op jit(solution)/shard_map/ppermute | solution.py:24
  51.8 11.7 %collective-permute-start.5 = (bf16[128,1024]{1,0:T(8,128)(2,1)S(1)}, bf16[128,1024]{1,0:T(8,128)(2,1)}, u32[]{:S(2)}, u32[]{:S(2)}) collective-permute-start(bf16[128,1024]{1,0:T(8,128)(2,1)S(1)} %collective-permute-done.2.refs_4_), channel_id=1, source_target_pairs={{0,2},{1,3},{2,0},{3,1},{4,6},{5,7},{6,4},{7,5},{8,10},{9,11},{10,... | collective-permute-start | bytes 786440 | tf_op jit(solution)/shard_map/ppermute | solution.py:24
  53.3 14.0 %collective-permute-start.3 = (bf16[128,1024]{1,0:T(8,128)(2,1)S(1)}, bf16[128,1024]{1,0:T(8,128)(2,1)S(1)}, u32[]{:S(2)}, u32[]{:S(2)}) collective-permute-start(bf16[128,1024]{1,0:T(8,128)(2,1)S(1)} %collective-permute-done.1.refs_2_), channel_id=1, source_target_pairs={{0,1},{1,0},{2,3},{3,2},{4,5},{5,4},{6,7},{7,6},{8,9},{9,8},{10,11... | collective-permute-start | bytes 786440 | tf_op jit(solution)/shard_map/ppermute | solution.py:24
  53.8 16.0 %collective-permute-start.8 = (bf16[1024,256]{1,0:T(8,128)(2,1)S(1)}, bf16[1024,256]{1,0:T(8,128)(2,1)}, u32[]{:S(2)}, u32[]{:S(2)}) collective-permute-start(bf16[1024,256]{1,0:T(8,128)(2,1)S(1)} %get-tuple-element.15.refs_7_), channel_id=1, source_target_pairs={{0,8},{8,0},{16,24},{24,16},{1,9},{9,1},{17,25},{25,17},{2,10},{10... | collective-permute-start | bytes 1572872 | tf_op jit(solution)/shard_map/ppermute | solution.py:24
  63.5 3.8 %copy-start.12 = (bf16[128,1024]{1,0:T(8,128)(2,1)}, bf16[128,1024]{1,0:T(8,128)(2,1)S(1)}, u32[]{:S(2)}) copy-start(bf16[128,1024]{1,0:T(8,128)(2,1)S(1)} %collective-permute-done.4.refs_5_) | copy-start | bytes 786436
  67.3 0.7 copy-start.13
  67.3 11.7 %collective-permute-start.11 = (bf16[1024,256]{1,0:T(8,128)(2,1)}, bf16[1024,256]{1,0:T(8,128)(2,1)S(1)}, u32[]{:S(2)}, u32[]{:S(2)}) collective-permute-start(bf16[1024,256]{1,0:T(8,128)(2,1)} %collective-permute-done.9.refs_9_), channel_id=1, source_target_pairs={{0,8},{8,0},{16,24},{24,16},{1,9},{9,1},{17,25},{25,17},{2,10},{10... | collective-permute-start | bytes 1572872 | tf_op jit(solution)/shard_map/ppermute | solution.py:24
  68.0 11.0 %collective-permute-start.10 = (bf16[128,1024]{1,0:T(8,128)(2,1)}, bf16[128,1024]{1,0:T(8,128)(2,1)S(1)}, u32[]{:S(2)}, u32[]{:S(2)}) collective-permute-start(bf16[128,1024]{1,0:T(8,128)(2,1)} %collective-permute-done.5.refs_6_), channel_id=1, source_target_pairs={{0,1},{1,0},{2,3},{3,2},{4,5},{5,4},{6,7},{7,6},{8,9},{9,8},{10,11... | collective-permute-start | bytes 786440 | tf_op jit(solution)/shard_map/ppermute | solution.py:24
  71.1 1.3 %copy-start = (bf16[8,1024,128]{2,1,0:T(8,128)(2,1)}, bf16[8,1024,128]{2,1,0:T(8,128)(2,1)S(1)}, u32[]{:S(2)}) copy-start(bf16[8,1024,128]{2,1,0:T(8,128)(2,1)S(1)} %all-to-all-done.tokens_ref) | copy-start | bytes 6291460
  79.0 1.6 %copy-start.1 = (bf16[8,1024,128]{2,1,0:T(8,128)(2,1)S(1)}, bf16[8,1024,128]{2,1,0:T(8,128)(2,1)}, u32[]{:S(2)}) copy-start(bf16[8,1024,128]{2,1,0:T(8,128)(2,1)} %copy-done) | copy-start | bytes 6291460
  80.6 2.2 %copy-start.2 = (f32[1024,1024]{1,0:T(8,128)S(1)}, f32[1024,1024]{1,0:T(8,128)}, u32[]{:S(2)}) copy-start(f32[1024,1024]{1,0:T(8,128)} %accumulate.1.total_ref) | copy-start | bytes 12582916

commit v24 on v23

--- a/solution.py
+++ b/solution.py
@@ -273,7 +273,7 @@
             pltpu.SemaphoreType.DMA,
             pltpu.SemaphoreType.DMA((width // tile,)),
         ],
-        compiler_params=pltpu.CompilerParams(vmem_limit_bytes=46 * 2**20),
+        compiler_params=pltpu.CompilerParams(vmem_limit_bytes=58 * 2**20),
         cost_estimate=pl.CostEstimate(
             flops=2 * depth * rows * width, bytes_accessed=2 * depth * (rows + width) + 7 * rows * width, transcendentals=0
         ),

time: 86.8 us -> 86.2 us (level)
  local copies, waits for them, and re-layouts: 11.9 us -> 5.52 us
  waiting for transfers between devices: 33.5 us -> 38.3 us
  Pallas kernels: 15.9 us -> 18.1 us
  starting transfers between devices: 21.8 us -> 20.6 us
    unnamed x28 -> x32, local copies, waits for them, and re-layouts: 11.8 us -> 5.47 us
    all_to_all x1, waiting for transfers between devices: 1.27 us -> 4.02 us  [on_device(): lax.all_to_all(blocks, 'fsdp', split_axis=0, concat_axis=0, tiled=True)]
    ppermute x12, waiting for transfers between devices: 32.2 us -> 34.3 us  [swap(): return lax.ppermute(value, axis, [(i, i ^ mask) for i in range(size)])]
    pallas_call x1, Pallas kernels: 3.57 us -> 5.56 us  [finish(): pl.pallas_call(functools.partial(finish_kernel, width // share, rate), ou...]
    ppermute x12, starting transfers between devices: 16.3 us -> 15 us  [swap(): return lax.ppermute(value, axis, [(i, i ^ mask) for i in range(size)])]
  transfers between devices with their start and end apart: 13 -> 13, of which waited for: 7 -> 7; matrix products, arithmetic and copies ran while one was open for 3% -> 3% of each run, Pallas kernels for 14% -> 15%
where the time goes in v24:
time: 86.2 us; the launch traced here: 85.8 us
  waiting for transfers between devices  38.3 us (44%)
  starting transfers between devices  20.6 us (24%)
  Pallas kernels  18.1 us (21%)
  local copies, waits for them, and re-layouts  5.52 us (6%)
  other arithmetic  2.6 us (3%)
    ppermute x12, waiting for transfers between devices, swap(): return lax.ppermute(value, axis, [(i, i ^ mask) for i in range(size)])  34.3 us
    ppermute x12, starting transfers between devices, swap(): return lax.ppermute(value, axis, [(i, i ^ mask) for i in range(size)])  15 us
    pallas_call x1, Pallas kernels, accumulate(): pl.pallas_call(functools.partial(accumulate_kernel, parts, groups, rate),...  6.6 us
    all_to_all x1, starting transfers between devices, on_device(): lax.all_to_all(blocks, 'fsdp', split_axis=0, concat_axis=0, tiled=True)  5.61 us
    pallas_call x1, Pallas kernels, finish(): pl.pallas_call(functools.partial(finish_kernel, width // share, rate), ou...  5.56 us
    unnamed x32, local copies, waits for them, and re-layouts  5.47 us
    all_to_all x1, waiting for transfers between devices, on_device(): lax.all_to_all(blocks, 'fsdp', split_axis=0, concat_axis=0, tiled=True)  4.02 us
    pallas_call x1, Pallas kernels, code_and_decode(): pl.pallas_call(code_kernel, out_shape=(half, half), in_specs=[pl.BlockSpe...  3.69 us
  transfers between devices with their start and end apart: 13, of which 7 were waited for; matrix products, arithmetic and copies ran while one was open for 3% of the time, Pallas kernels for 15%

profile of v24, /device:TPU:0, one launch (start us, length us, event | category | flops | bytes accessed | tf_op | source)
XLA Modules:
  0.0 85.8 jit_solution(14355989391074760480)
XLA Ops:
  0.6 4.1 %collective-permute-start.2 = (bf16[128,1024]{1,0:T(8,128)(2,1)}, bf16[128,1024]{1,0:T(8,128)(2,1)S(1)}, u32[]{:S(2)}, u32[]{:S(2)}) collective-permute-start(bf16[128,1024]{1,0:T(8,128)(2,1)} %bitcast.20), channel_id=1, source_target_pairs={{0,4},{1,5},{2,6},{3,7},{4,0},{5,1},{6,2},{7,3},{8,12},{9,13},{10,... | collective-permute-start | bytes 786440 | tf_op jit(solution)/shard_map/ppermute | solution.py:24
  4.7 1.6 %collective-permute-start.1 = (bf16[128,1024]{1,0:T(8,128)(2,1)}, bf16[128,1024]{1,0:T(8,128)(2,1)S(1)}, u32[]{:S(2)}, u32[]{:S(2)}) collective-permute-start(bf16[128,1024]{1,0:T(8,128)(2,1)} %bitcast.21), channel_id=1, source_target_pairs={{0,2},{1,3},{2,0},{3,1},{4,6},{5,7},{6,4},{7,5},{8,10},{9,11},{10,... | collective-permute-start | bytes 786440 | tf_op jit(solution)/shard_map/ppermute | solution.py:24
  6.3 1.5 %collective-permute-start = (bf16[128,1024]{1,0:T(8,128)(2,1)}, bf16[128,1024]{1,0:T(8,128)(2,1)S(1)}, u32[]{:S(2)}, u32[]{:S(2)}) collective-permute-start(bf16[128,1024]{1,0:T(8,128)(2,1)} %bitcast.22), channel_id=1, source_target_pairs={{0,1},{1,0},{2,3},{3,2},{4,5},{5,4},{6,7},{7,6},{8,9},{9,8},{10,11... | collective-permute-start | bytes 786440 | tf_op jit(solution)/shard_map/ppermute | solution.py:24
  7.8 0.7 reshape.26
  8.6 1.6 %copy-done.1 = bf16[1,128,8192]{2,1,0:T(8,128)(2,1)S(1)} copy-done((bf16[1,128,8192]{2,1,0:T(8,128)(2,1)S(1)}, bf16[1,128,8192]{2,1,0:T(8,128)(2,1)}, u32[]{:S(2)}) %copy-start.1) | copy-done | bytes 2097176
  10.1 2.2 %prepare.1 = bf16[8,1024,128]{2,1,0:T(8,128)(2,1)} custom-call(bf16[128,8192]{1,0:T(8,128)(2,1)S(1)} %bitcast.17, f32[1,8192]{1,0:T(1,128)S(1)} %bitcast.18), custom_call_target="tpu_custom_call" | custom-call | flops 5242880 | bytes 4194304 | tf_op jit(solution)/shard_map/prepare/pallas_call | solution.py:58
  12.4 4.6 %collective-permute-done.2.refs_4_ = bf16[128,1024]{1,0:T(8,128)(2,1)S(1)} collective-permute-done((bf16[128,1024]{1,0:T(8,128)(2,1)}, bf16[128,1024]{1,0:T(8,128)(2,1)S(1)}, u32[]{:S(2)}, u32[]{:S(2)}) %collective-permute-start.2) | collective-permute-done | bytes 262176 | tf_op jit(solution)/shard_map/ppermute | solution.py:24
  17.0 0.2 collective-permute-done.1.refs_2_
  17.2 0.7 copy-done.11
  17.9 5.6 %all-to-all-start = ((bf16[8,1024,128]{2,1,0:T(8,128)(2,1)}), bf16[8,1024,128]{2,1,0:T(8,128)(2,1)}, u32[]{:S(2)}, u32[]{:S(2)}) async-start(bf16[8,1024,128]{2,1,0:T(8,128)(2,1)} %prepare.1), calls=%async_computation | async-start | bytes 4194304 | tf_op jit(solution)/shard_map/all_to_all | solution.py:310
  23.6 1.6 %copy-done.2 = bf16[1024,1024]{1,0:T(8,128)(2,1)S(1)} copy-done((bf16[1024,1024]{1,0:T(8,128)(2,1)S(1)}, bf16[1024,1024]{1,0:T(8,128)(2,1)}, u32[]{:S(2)}) %copy-start.2) | copy-done | bytes 2097176
  25.1 3.7 %code_and_decode.1 = (bf16[2,1024,256]{2,1,0:T(8,128)(2,1)S(1)}, bf16[2,1024,256]{2,1,0:T(8,128)(2,1)S(1)}) custom-call(s32[1]{0:T(128)} %bitcast.1.own_ref, bf16[1024,1024]{1,0:T(8,128)(2,1)S(1)} %copy-done.2, bf16[1024,1024]{1,0:T(8,128)(2,1)S(1)} %bitcast.16), custom_call_target="tpu_custom_call" | custom-call | flops 20971520 | bytes 6291456 | tf_op jit(solution)/shard_map/code_and_decode/pallas_call | solution.py:128
  28.8 0.1 collective-permute-start.6
  28.9 2.6 %collective-permute-done.6 = bf16[2,1024,256]{2,1,0:T(8,128)(2,1)S(1)} collective-permute-done((bf16[2,1024,256]{2,1,0:T(8,128)(2,1)S(1)}, bf16[2,1024,256]{2,1,0:T(8,128)(2,1)S(1)}, u32[]{:S(2)}, u32[]{:S(2)}) %collective-permute-start.6) | collective-permute-done | bytes 1048608 | tf_op jit(solution)/shard_map/ppermute | solution.py:24
  31.6 0.2 convert_add_fusion
  31.8 0.1 slice.23
  31.9 1.6 %collective-permute-start.7 = (bf16[1,1024,256]{2,1,0:T(8,128)(2,1)S(1)}, bf16[1,1024,256]{2,1,0:T(8,128)(2,1)S(1)}, u32[]{:S(2)}, u32[]{:S(2)}) collective-permute-start(bf16[1,1024,256]{2,1,0:T(8,128)(2,1)S(1)} %slice.23), channel_id=1, source_target_pairs={{0,16},{8,24},{16,0},{24,8},{1,17},{9,25},{17,1},{25,9},{2,18},{10... | collective-permute-start | bytes 1572872 | tf_op jit(solution)/shard_map/ppermute | solution.py:24
  33.4 12.5 %collective-permute-done.7 = bf16[1,1024,256]{2,1,0:T(8,128)(2,1)S(1)} collective-permute-done((bf16[1,1024,256]{2,1,0:T(8,128)(2,1)S(1)}, bf16[1,1024,256]{2,1,0:T(8,128)(2,1)S(1)}, u32[]{:S(2)}, u32[]{:S(2)}) %collective-permute-start.7) | collective-permute-done | bytes 524320 | tf_op jit(solution)/shard_map/ppermute | solution.py:24
  45.9 1.7 %fusion.2 = (bf16[1024,256]{1,0:T(8,128)(2,1)S(1)}, f32[1024,256]{1,0:T(8,128)}, f32[1024,256]{1,0:T(8,128)}) fusion(f32[1024,256]{1,0:T(8,128)S(1)} %copy-done.4, bf16[1,1024,256]{2,1,0:T(8,128)(2,1)S(1)} %collective-permute-done.7, f32[2,1024,256]{2,1,0:T(8,128)S(1)} %convert_add_fusion, f32[1024,256]{1,0:T(8,128)S(1)} %copy-done.5), kind=kLoop, calls=%fused_computation.7 | loop fusion | flops 2621440 | bytes 6291456 | tf_op jit(solution)/shard_map/convert_element_type | solution.py:322
  47.6 1.5 %collective-permute-start.9 = (bf16[1024,256]{1,0:T(8,128)(2,1)S(1)}, bf16[1024,256]{1,0:T(8,128)(2,1)S(1)}, u32[]{:S(2)}, u32[]{:S(2)}) collective-permute-start(bf16[1024,256]{1,0:T(8,128)(2,1)S(1)} %get-tuple-element.15.refs_7_), channel_id=1, source_target_pairs={{0,16},{8,24},{16,0},{24,8},{1,17},{9,25},{17,1},{25,9},{2,18},{10... | collective-permute-start | bytes 1572872 | tf_op jit(solution)/shard_map/ppermute | solution.py:24
  49.0 2.0 %collective-permute-start.4 = (bf16[128,1024]{1,0:T(8,128)(2,1)S(1)}, bf16[128,1024]{1,0:T(8,128)(2,1)S(1)}, u32[]{:S(2)}, u32[]{:S(2)}) collective-permute-start(bf16[128,1024]{1,0:T(8,128)(2,1)S(1)} %collective-permute-done.2.refs_4_), channel_id=1, source_target_pairs={{0,1},{1,0},{2,3},{3,2},{4,5},{5,4},{6,7},{7,6},{8,9},{9,8},{10,11... | collective-permute-start | bytes 786440 | tf_op jit(solution)/shard_map/ppermute | solution.py:24
  51.1 1.5 %collective-permute-start.5 = (bf16[128,1024]{1,0:T(8,128)(2,1)S(1)}, bf16[128,1024]{1,0:T(8,128)(2,1)S(1)}, u32[]{:S(2)}, u32[]{:S(2)}) collective-permute-start(bf16[128,1024]{1,0:T(8,128)(2,1)S(1)} %collective-permute-done.2.refs_4_), channel_id=1, source_target_pairs={{0,2},{1,3},{2,0},{3,1},{4,6},{5,7},{6,4},{7,5},{8,10},{9,11},{10,... | collective-permute-start | bytes 786440 | tf_op jit(solution)/shard_map/ppermute | solution.py:24
  52.5 0.6 collective-permute-start.3
  53.1 11.3 %collective-permute-done.5.refs_6_ = bf16[128,1024]{1,0:T(8,128)(2,1)S(1)} collective-permute-done((bf16[128,1024]{1,0:T(8,128)(2,1)S(1)}, bf16[128,1024]{1,0:T(8,128)(2,1)S(1)}, u32[]{:S(2)}, u32[]{:S(2)}) %collective-permute-start.5) | collective-permute-done | bytes 262176 | tf_op jit(solution)/shard_map/ppermute | solution.py:24
  64.5 3.0 %collective-permute-done.3.refs_3_ = bf16[128,1024]{1,0:T(8,128)(2,1)S(1)} collective-permute-done((bf16[128,1024]{1,0:T(8,128)(2,1)S(1)}, bf16[128,1024]{1,0:T(8,128)(2,1)S(1)}, u32[]{:S(2)}, u32[]{:S(2)}) %collective-permute-start.3) | collective-permute-done | bytes 262176 | tf_op jit(solution)/shard_map/ppermute | solution.py:24
  67.4 0.1 collective-permute-start.11
  67.5 0.6 collective-permute-start.10
  68.1 4.0 %all-to-all-done.tokens_ref = bf16[8,1024,128]{2,1,0:T(8,128)(2,1)} async-done(((bf16[8,1024,128]{2,1,0:T(8,128)(2,1)}), bf16[8,1024,128]{2,1,0:T(8,128)(2,1)}, u32[]{:S(2)}, u32[]{:S(2)}) %all-to-all-start) | async-done | bytes 2097184 | tf_op jit(solution)/shard_map/all_to_all | solution.py:310
  72.1 6.6 %accumulate.1.total_ref = f32[1024,1024]{1,0:T(8,128)} custom-call(s32[1]{0:T(128)} %bitcast.mine_ref, s32[1]{0:T(128)} %bitcast.1.own_ref, bf16[8,1024,128]{2,1,0:T(8,128)(2,1)} %all-to-all-done.tokens_ref, bf16[1024,1024]{1,0:T(8,128)(2,1)} %bitcast.15, bf16[128,1024]{1,0:T(8,128)(2,1)} %bitcast.23, bf16[128,1024]{1,0:T(8,128)(2,1)} %copy-done.11, ...), custom_call_target="tpu_custom_call" | custom-call | flops 1879048192 | bytes 12582912 | tf_op jit(solution)/shard_map/accumulate/pallas_call | solution.py:200
  78.8 0.7 copy-done.15
  79.5 0.8 copy-done.8
  80.3 5.6 %finish.1 = bf16[1024,1024]{1,0:T(8,128)(2,1)} custom-call(s32[1]{0:T(128)} %bitcast.mine_ref, s32[1]{0:T(128)} %bitcast.1.own_ref, bf16[8,1024,128]{2,1,0:T(8,128)(2,1)} %all-to-all-done.tokens_ref, f32[1024,1024]{1,0:T(8,128)} %accumulate.1.total_ref, bf16[128,1024]{1,0:T(8,128)(2,1)} %copy-done.15, bf16[1024,256]{1,0:T(8,128)(2,1)} %copy-done.8), custom_call_target="tpu_custom_call" | custom-call | flops 268435456 | bytes 7864320 | tf_op jit(solution)/shard_map/finish/pallas_call | solution.py:261
  (34 shorter events, 0.1 us)
Async XLA Ops:
  0.6 16.3 %collective-permute-start.2 = (bf16[128,1024]{1,0:T(8,128)(2,1)}, bf16[128,1024]{1,0:T(8,128)(2,1)S(1)}, u32[]{:S(2)}, u32[]{:S(2)}) collective-permute-start(bf16[128,1024]{1,0:T(8,128)(2,1)} %bitcast.20), channel_id=1, source_target_pairs={{0,4},{1,5},{2,6},{3,7},{4,0},{5,1},{6,2},{7,3},{8,12},{9,13},{10,... | collective-permute-start | bytes 786440 | tf_op jit(solution)/shard_map/ppermute | solution.py:24
  4.7 12.4 %collective-permute-start.1 = (bf16[128,1024]{1,0:T(8,128)(2,1)}, bf16[128,1024]{1,0:T(8,128)(2,1)S(1)}, u32[]{:S(2)}, u32[]{:S(2)}) collective-permute-start(bf16[128,1024]{1,0:T(8,128)(2,1)} %bitcast.21), channel_id=1, source_target_pairs={{0,2},{1,3},{2,0},{3,1},{4,6},{5,7},{6,4},{7,5},{8,10},{9,11},{10,... | collective-permute-start | bytes 786440 | tf_op jit(solution)/shard_map/ppermute | solution.py:24
  6.3 10.9 %collective-permute-start = (bf16[128,1024]{1,0:T(8,128)(2,1)}, bf16[128,1024]{1,0:T(8,128)(2,1)S(1)}, u32[]{:S(2)}, u32[]{:S(2)}) collective-permute-start(bf16[128,1024]{1,0:T(8,128)(2,1)} %bitcast.22), channel_id=1, source_target_pairs={{0,1},{1,0},{2,3},{3,2},{4,5},{5,4},{6,7},{7,6},{8,9},{9,8},{10,11... | collective-permute-start | bytes 786440 | tf_op jit(solution)/shard_map/ppermute | solution.py:24
  8.5 1.6 %copy-start.1 = (bf16[1,128,8192]{2,1,0:T(8,128)(2,1)S(1)}, bf16[1,128,8192]{2,1,0:T(8,128)(2,1)}, u32[]{:S(2)}) copy-start(bf16[1,128,8192]{2,1,0:T(8,128)(2,1)} %param.7) | copy-start | bytes 6291460
  17.0 34.1 %copy-start.9 = (bf16[128,1024]{1,0:T(8,128)(2,1)}, bf16[128,1024]{1,0:T(8,128)(2,1)S(1)}, u32[]{:S(2)}) copy-start(bf16[128,1024]{1,0:T(8,128)(2,1)S(1)} %collective-permute-done.2.refs_4_) | copy-start | bytes 786436
  17.2 35.4 %copy-start.10 = (bf16[128,1024]{1,0:T(8,128)(2,1)}, bf16[128,1024]{1,0:T(8,128)(2,1)S(1)}, u32[]{:S(2)}) copy-start(bf16[128,1024]{1,0:T(8,128)(2,1)S(1)} %collective-permute-done.1.refs_2_) | copy-start | bytes 786436
  17.2 0.8 copy-start.11
  17.2 6.4 %copy-start = (bf16[1,1024,1024]{2,1,0:T(8,128)(2,1)S(1)}, bf16[1,1024,1024]{2,1,0:T(8,128)(2,1)}, u32[]{:S(2)}) copy-start(bf16[1,1024,1024]{2,1,0:T(8,128)(2,1)} %param.10) | copy-start | bytes 6291460
  17.9 54.2 %all-to-all-start = ((bf16[8,1024,128]{2,1,0:T(8,128)(2,1)}), bf16[8,1024,128]{2,1,0:T(8,128)(2,1)}, u32[]{:S(2)}, u32[]{:S(2)}) async-start(bf16[8,1024,128]{2,1,0:T(8,128)(2,1)} %prepare.1), calls=%async_computation | async-start | bytes 4194304 | tf_op jit(solution)/shard_map/all_to_all | solution.py:310
  23.5 1.6 %copy-start.2 = (bf16[1024,1024]{1,0:T(8,128)(2,1)S(1)}, bf16[1024,1024]{1,0:T(8,128)(2,1)}, u32[]{:S(2)}) copy-start(bf16[1024,1024]{1,0:T(8,128)(2,1)} %shared_ref) | copy-start | bytes 6291460
  28.8 2.7 %collective-permute-start.6 = (bf16[2,1024,256]{2,1,0:T(8,128)(2,1)S(1)}, bf16[2,1024,256]{2,1,0:T(8,128)(2,1)S(1)}, u32[]{:S(2)}, u32[]{:S(2)}) collective-permute-start(bf16[2,1024,256]{2,1,0:T(8,128)(2,1)S(1)} %get-tuple-element.13), channel_id=1, source_target_pairs={{0,8},{8,0},{16,24},{24,16},{1,9},{9,1},{17,25},{25,17},{2,10},{10... | collective-permute-start | bytes 3145736 | tf_op jit(solution)/shard_map/ppermute | solution.py:24
  31.6 14.3 %copy-start.4 = (f32[1024,256]{1,0:T(8,128)S(1)}, f32[1024,256]{1,0:T(8,128)}, u32[]{:S(2)}) copy-start(f32[1024,256]{1,0:T(8,128)} %param.12) | copy-start | bytes 3145732
  31.6 14.3 %copy-start.5 = (f32[1024,256]{1,0:T(8,128)S(1)}, f32[1024,256]{1,0:T(8,128)}, u32[]{:S(2)}) copy-start(f32[1024,256]{1,0:T(8,128)} %param.13) | copy-start | bytes 3145732
  31.9 14.0 %collective-permute-start.7 = (bf16[1,1024,256]{2,1,0:T(8,128)(2,1)S(1)}, bf16[1,1024,256]{2,1,0:T(8,128)(2,1)S(1)}, u32[]{:S(2)}, u32[]{:S(2)}) collective-permute-start(bf16[1,1024,256]{2,1,0:T(8,128)(2,1)S(1)} %slice.23), channel_id=1, source_target_pairs={{0,16},{8,24},{16,0},{24,8},{1,17},{9,25},{17,1},{25,9},{2,18},{10... | collective-permute-start | bytes 1572872 | tf_op jit(solution)/shard_map/ppermute | solution.py:24
  47.5 24.6 %copy-start.3 = (bf16[1024,256]{1,0:T(8,128)(2,1)}, bf16[1024,256]{1,0:T(8,128)(2,1)S(1)}, u32[]{:S(2)}) copy-start(bf16[1024,256]{1,0:T(8,128)(2,1)S(1)} %get-tuple-element.15.refs_7_) | copy-start | bytes 1572868
  47.6 19.9 %collective-permute-start.9 = (bf16[1024,256]{1,0:T(8,128)(2,1)S(1)}, bf16[1024,256]{1,0:T(8,128)(2,1)S(1)}, u32[]{:S(2)}, u32[]{:S(2)}) collective-permute-start(bf16[1024,256]{1,0:T(8,128)(2,1)S(1)} %get-tuple-element.15.refs_7_), channel_id=1, source_target_pairs={{0,16},{8,24},{16,0},{24,8},{1,17},{9,25},{17,1},{25,9},{2,18},{10... | collective-permute-start | bytes 1572872 | tf_op jit(solution)/shard_map/ppermute | solution.py:24
  49.0 15.4 %collective-permute-start.4 = (bf16[128,1024]{1,0:T(8,128)(2,1)S(1)}, bf16[128,1024]{1,0:T(8,128)(2,1)S(1)}, u32[]{:S(2)}, u32[]{:S(2)}) collective-permute-start(bf16[128,1024]{1,0:T(8,128)(2,1)S(1)} %collective-permute-done.2.refs_4_), channel_id=1, source_target_pairs={{0,1},{1,0},{2,3},{3,2},{4,5},{5,4},{6,7},{7,6},{8,9},{9,8},{10,11... | collective-permute-start | bytes 786440 | tf_op jit(solution)/shard_map/ppermute | solution.py:24
  51.1 13.4 %collective-permute-start.5 = (bf16[128,1024]{1,0:T(8,128)(2,1)S(1)}, bf16[128,1024]{1,0:T(8,128)(2,1)S(1)}, u32[]{:S(2)}, u32[]{:S(2)}) collective-permute-start(bf16[128,1024]{1,0:T(8,128)(2,1)S(1)} %collective-permute-done.2.refs_4_), channel_id=1, source_target_pairs={{0,2},{1,3},{2,0},{3,1},{4,6},{5,7},{6,4},{7,5},{8,10},{9,11},{10,... | collective-permute-start | bytes 786440 | tf_op jit(solution)/shard_map/ppermute | solution.py:24
  52.5 14.9 %collective-permute-start.3 = (bf16[128,1024]{1,0:T(8,128)(2,1)S(1)}, bf16[128,1024]{1,0:T(8,128)(2,1)S(1)}, u32[]{:S(2)}, u32[]{:S(2)}) collective-permute-start(bf16[128,1024]{1,0:T(8,128)(2,1)S(1)} %collective-permute-done.1.refs_2_), channel_id=1, source_target_pairs={{0,1},{1,0},{2,3},{3,2},{4,5},{5,4},{6,7},{7,6},{8,9},{9,8},{10,11... | collective-permute-start | bytes 786440 | tf_op jit(solution)/shard_map/ppermute | solution.py:24
  53.1 15.0 %collective-permute-start.8 = (bf16[1024,256]{1,0:T(8,128)(2,1)S(1)}, bf16[1024,256]{1,0:T(8,128)(2,1)S(1)}, u32[]{:S(2)}, u32[]{:S(2)}) collective-permute-start(bf16[1024,256]{1,0:T(8,128)(2,1)S(1)} %get-tuple-element.15.refs_7_), channel_id=1, source_target_pairs={{0,8},{8,0},{16,24},{24,16},{1,9},{9,1},{17,25},{25,17},{2,10},{10... | collective-permute-start | bytes 1572872 | tf_op jit(solution)/shard_map/ppermute | solution.py:24
  64.4 7.7 %copy-start.13 = (bf16[128,1024]{1,0:T(8,128)(2,1)}, bf16[128,1024]{1,0:T(8,128)(2,1)S(1)}, u32[]{:S(2)}) copy-start(bf16[128,1024]{1,0:T(8,128)(2,1)S(1)} %collective-permute-done.5.refs_6_) | copy-start | bytes 786436
  64.5 7.7 %copy-start.12 = (bf16[128,1024]{1,0:T(8,128)(2,1)}, bf16[128,1024]{1,0:T(8,128)(2,1)S(1)}, u32[]{:S(2)}) copy-start(bf16[128,1024]{1,0:T(8,128)(2,1)S(1)} %collective-permute-done.4.refs_5_) | copy-start | bytes 786436
  67.4 4.7 %copy-start.14 = (bf16[128,1024]{1,0:T(8,128)(2,1)}, bf16[128,1024]{1,0:T(8,128)(2,1)S(1)}, u32[]{:S(2)}) copy-start(bf16[128,1024]{1,0:T(8,128)(2,1)S(1)} %collective-permute-done.3.refs_3_) | copy-start | bytes 786436
  67.4 4.7 %copy-start.6 = (bf16[1024,256]{1,0:T(8,128)(2,1)}, bf16[1024,256]{1,0:T(8,128)(2,1)S(1)}, u32[]{:S(2)}) copy-start(bf16[1024,256]{1,0:T(8,128)(2,1)S(1)} %collective-permute-done.9.refs_9_) | copy-start | bytes 1572868
  67.4 11.3 %collective-permute-start.11 = (bf16[1024,256]{1,0:T(8,128)(2,1)S(1)}, bf16[1024,256]{1,0:T(8,128)(2,1)S(1)}, u32[]{:S(2)}, u32[]{:S(2)}) collective-permute-start(bf16[1024,256]{1,0:T(8,128)(2,1)S(1)} %collective-permute-done.9.refs_9_), channel_id=1, source_target_pairs={{0,8},{8,0},{16,24},{24,16},{1,9},{9,1},{17,25},{25,17},{2,10},{10... | collective-permute-start | bytes 1572872 | tf_op jit(solution)/shard_map/ppermute | solution.py:24
  67.5 11.2 %collective-permute-start.10 = (bf16[128,1024]{1,0:T(8,128)(2,1)S(1)}, bf16[128,1024]{1,0:T(8,128)(2,1)S(1)}, u32[]{:S(2)}, u32[]{:S(2)}) collective-permute-start(bf16[128,1024]{1,0:T(8,128)(2,1)S(1)} %collective-permute-done.5.refs_6_), channel_id=1, source_target_pairs={{0,1},{1,0},{2,3},{3,2},{4,5},{5,4},{6,7},{7,6},{8,9},{9,8},{10,11... | collective-permute-start | bytes 786440 | tf_op jit(solution)/shard_map/ppermute | solution.py:24
  68.1 4.1 %copy-start.7 = (bf16[1024,256]{1,0:T(8,128)(2,1)}, bf16[1024,256]{1,0:T(8,128)(2,1)S(1)}, u32[]{:S(2)}) copy-start(bf16[1024,256]{1,0:T(8,128)(2,1)S(1)} %collective-permute-done.8.refs_8_) | copy-start | bytes 1572868
  78.8 0.7 copy-start.15
  79.5 0.8 copy-start.8
